TPU v7x, 32 devices: a whole 2x2x4 slice. The times are simulated.
32 devices in a mesh: row: 4 (over x, core), col: 4 (over z), mom: 2 (over y).
Axes of the slice: x: 2, y: 2, z: 4, core: 2. Of those that a mesh axis runs over, the one named last changes fastest.
Arguments:
- lesser: bfloat16 [4, 2, 1536, 1536], P('mom', None, 'row', 'col'), may hold values from -8 to 8
- greater: bfloat16 [4, 2, 1536, 1536], P('mom', None, 'col', 'row'), may hold values from -8 to 8
- triples: int32 [4, 8, 3], replicated, may hold values from 0 to 3
- diag_inverse: bfloat16 [4, 2, 1536, 384], P('mom', None, 'row'), may hold values from -0.21875 to 0.21875
- right_side: bfloat16 [4, 1536, 2, 1536], P('mom', 'row', None, 'col'), may hold values from -6 to 6
Outputs:
- sigma: bfloat16 [4, 2, 1536, 1536], P('mom', None, 'row', 'col')
- solution: bfloat16 [4, 1536, 2, 1536], P('mom', 'row', None, 'col')
Inputs may be any that keep to these rules, and one draw needn't show every extreme that they name: `triples`: each entry names a momentum point.
All inputs are finite; a program needn't handle non-finite values.
Results may differ from a plain program's by a relative error of at most 0.017.
Values may be sent and summed in bfloat16 or wider, within the bound.
No kernel may reach another device: no remote copies, remote signals or barrier semaphores. Data moves between devices by JAX's collectives and lax.ppermute only.
A program may use at most 128 MiB of HBM per device.

v0:
```python
import math

import jax
import jax.numpy as jnp
from jax import lax
from jax.sharding import PartitionSpec as P


def broadcast(value, axis, source):
    kept = jnp.where(lax.axis_index(axis) == source, value, 0).astype(value.dtype)
    return lax.psum(kept, axis)


def complex_mul(left_real, left_imag, right_real, right_imag):
    return (
        left_real * right_real - left_imag * right_imag,
        left_real * right_imag + left_imag * right_real,
    )


def complex_product(left_tiles, right_rows):
    count = left_tiles.shape[0]
    height = left_tiles.shape[2]
    inner = left_tiles.shape[3]
    breadth = right_rows.shape[3]
    stacked = left_tiles.reshape(count, 2 * height, inner)
    spread = right_rows.reshape(count, inner, 2 * breadth)
    product = jnp.einsum("kab,kbc->kac", stacked, spread, preferred_element_type=jnp.float32)
    product = product.reshape(count, 2, height, 2, breadth)
    out_real = product[:, 0, :, 0] - product[:, 1, :, 1]
    out_imag = product[:, 0, :, 1] + product[:, 1, :, 0]
    return jnp.stack([out_real, out_imag], axis=2)


def on_device(lesser, greater, triples, diag_inverse, right_side):
    local_count = lesser.shape[0]
    lesser_all, greater_all = (
        lax.all_gather(lesser, "mom", axis=0, tiled=True),
        lax.all_gather(greater, "mom", axis=0, tiled=True),
    )
    partner_all = jnp.swapaxes(greater_all, 2, 3)
    first_moment = lax.axis_index("mom") * local_count
    pair_count = triples.shape[1]
    inv_pairs = 1.0 / pair_count

    def select_tile(stacked_tiles, which):
        return lax.dynamic_index_in_dim(stacked_tiles, which, 0, keepdims=False).astype(jnp.float32)

    sigma_parts = []
    for local_moment in range(local_count):
        table_rows = lax.dynamic_index_in_dim(
            triples, first_moment + local_moment, 0, keepdims=False
        )

        def add_term(pair_index, carry):
            sum_real, sum_imag = carry
            first_tile = select_tile(lesser_all, table_rows[pair_index, 0])
            second_tile = select_tile(lesser_all, table_rows[pair_index, 1])
            third_tile = select_tile(partner_all, table_rows[pair_index, 2])
            prod_real, prod_imag = complex_mul(
                first_tile[0], first_tile[1], second_tile[0], second_tile[1]
            )
            full_real, full_imag = complex_mul(prod_real, prod_imag, third_tile[0], third_tile[1])
            return (sum_real + full_real, sum_imag + full_imag)

        zero_tile = jnp.zeros(lesser.shape[2:], jnp.float32)
        sum_real, sum_imag = lax.fori_loop(0, pair_count, add_term, (zero_tile, zero_tile))
        sigma_parts.append(jnp.stack([sum_real, sum_imag]) * inv_pairs)
    sigma = jnp.stack(sigma_parts).astype(jnp.bfloat16)
    row_index = lax.axis_index("row")
    n_rows = lax.axis_size("row")
    tile_side = lesser.shape[2]
    weight = 1.0 / math.sqrt(tile_side * n_rows)
    kernel_rows = lax.all_gather(sigma, "col", axis=3, tiled=True)

    def solve_rows(pending):
        return complex_product(diag_inverse, pending.astype(jnp.bfloat16)).astype(jnp.bfloat16)

    def empty_rows(pending):
        return jnp.zeros(right_side.shape, jnp.bfloat16)

    def sweep(step_index, carry):
        pending, solved = carry
        is_owner = row_index == step_index
        candidate = lax.cond(is_owner, solve_rows, empty_rows, pending)
        solved = jnp.where(is_owner, candidate, solved)
        shared = broadcast(candidate, "row", step_index)
        kernel_tile = lax.dynamic_slice_in_dim(kernel_rows, step_index * tile_side, tile_side, 3)
        update = complex_product(kernel_tile, shared)
        pending = pending + jnp.where(row_index > step_index, weight * update, 0.0)
        return (pending, solved)

    start_pending = right_side.astype(jnp.float32)
    start_solved = jnp.zeros(right_side.shape, jnp.bfloat16)
    pending, solved = lax.fori_loop(0, n_rows - 1, sweep, (start_pending, start_solved))
    is_last = row_index == n_rows - 1
    last_rows = lax.cond(is_last, solve_rows, empty_rows, pending)
    solved = jnp.where(is_last, last_rows, solved)
    return (sigma, solved)


def solution(mesh):
    placed = (
        P("mom", None, "row", "col"),
        P("mom", None, "col", "row"),
        P(),
        P("mom", None, "row", None),
        P("mom", "row", None, "col"),
    )
    return jax.shard_map(
        on_device,
        mesh=mesh,
        in_specs=placed,
        out_specs=(P("mom", None, "row", "col"), P("mom", "row", None, "col")),
        check_vma=False,
    )
```

profile of v0, /device:TPU:3, one launch (start us, length us, event | category | flops | bytes accessed | tf_op | source)
XLA Modules:
  0.0 650.4 jit_solution(171456273349878052)
XLA Ops:
  8.8 38.1 %all-gather.6.cloned.1.call-done = bf16[4,2,384,384]{3,2,1,0:T(8,128)(2,1)} async-done(((bf16[2,2,384,384]{3,2,1,0:T(8,128)(2,1)}), bf16[4,2,384,384]{3,2,1,0:T(8,128)(2,1)}) %all-gather.6.cloned.1.call-update) | async-done | bytes 2359312 | tf_op jit(solution)/shard_map/all_gather | solution.py:39
  46.9 4.3 copy.40
  51.2 33.4 %all-gather.4.cloned.1.call-done = bf16[4,2,384,384]{3,2,1,0:T(8,128)(2,1)} async-done(((bf16[2,2,384,384]{3,2,1,0:T(8,128)(2,1)}), bf16[4,2,384,384]{3,2,1,0:T(8,128)(2,1)}) %all-gather.4.cloned.1.call-update) | async-done | bytes 2359312 | tf_op jit(solution)/shard_map/all_gather | solution.py:38
  84.5 92.0 %while.50 = (s32[]{:T(128)}, f32[384,384]{1,0:T(8,128)}, f32[384,384]{1,0:T(8,128)}, s32[8,3]{0,1:T(4,128)S(1)}, bf16[4,2,384,384]{3,2,1,0:T(8,128)(2,1)}, /*ind...) while((s32[]{:T(128)}, f32[384,384]{1,0:T(8,128)}, f32[384,384]{1,0:T(8,128)}, ...), condition=%wide.region_1.2_spmd.clone, body=%wide.region_0.1_spmd.clone.sunk | while | flops 3244044 | bytes 19464492 | solution.py:67
  103.2 2.2 bitcast_add_fusion.8
  113.2 1.8 dynamic-slice_convert_fusion.8
  115.0 2.2 bitcast_add_fusion.8
  126.6 2.2 bitcast_add_fusion.8
  138.2 2.2 bitcast_add_fusion.8
  148.1 1.7 dynamic-slice_convert_fusion.8
  149.9 2.2 bitcast_add_fusion.8
  161.5 2.2 bitcast_add_fusion.8
  173.1 2.2 bitcast_add_fusion.8
  176.6 91.5 %while.51 = (s32[]{:T(128)}, f32[384,384]{1,0:T(8,128)}, f32[384,384]{1,0:T(8,128)}, s32[8,3]{0,1:T(4,128)S(1)}, bf16[4,2,384,384]{3,2,1,0:T(8,128)(2,1)}, /*ind...) while((s32[]{:T(128)}, f32[384,384]{1,0:T(8,128)}, f32[384,384]{1,0:T(8,128)}, ...), condition=%wide.region_3.4_spmd.clone, body=%wide.region_2.3_spmd.clone.sunk | while | flops 3244044 | bytes 19464492 | solution.py:67
  195.3 2.2 bitcast_add_fusion.10
  206.8 2.2 bitcast_add_fusion.10
  218.4 2.2 bitcast_add_fusion.10
  230.0 2.2 bitcast_add_fusion.10
  241.6 2.2 bitcast_add_fusion.10
  253.1 2.2 bitcast_add_fusion.10
  264.7 2.2 bitcast_add_fusion.10
  273.0 87.5 %all-gather.8.cloned.1.call-done = bf16[2,2,384,1536]{3,2,1,0:T(8,128)(2,1)} async-done(((bf16[2,2,384,384]{3,2,1,0:T(8,128)(2,1)}), bf16[2,2,384,1536]{3,2,1,0:T(8,128)(2,1)}) %all-gather.8.cloned.1.call-update) | async-done | bytes 4718608 | tf_op jit(solution)/shard_map/all_gather | solution.py:74
  360.6 254.1 %while.52 = (s32[]{:T(128)}, f32[2,384,2,384]{3,2,1,0:T(2,128)S(1)}, bf16[2,384,2,384]{3,1,0,2:T(8,128)(2,1)}, s32[]{:T(128)}, bf16[2,2,384,1536]{3,2,1,0:T(8,12...) while((s32[]{:T(128)}, ...), condition=%wide.region_8.9_spmd.clone, body=%wide.region_4.8_spmd.clone.sunk | while | flops 1819607040 | bytes 87294248 | solution.py:95
  364.6 56.7 %all-reduce.2.cloned.1.call-done = bf16[2,384,768]{2,1,0:T(8,128)(2,1)} async-done(((bf16[2,384,768]{2,1,0:T(8,128)(2,1)}), bf16[2,384,768]{2,1,0:T(8,128)(2,1)}) %all-reduce.2.cloned.1.call-update) | async-done | bytes 1179664 | tf_op jit(solution)/shard_map/while/body/eval_jaxpr/psum | solution.py:11
  421.3 4.8 fusion.32
  426.1 6.7 %reshape.316 = f32[2,2,384,2,384]{4,3,2,1,0:T(2,128)} reshape(f32[2,768,768]{2,1,0:T(8,128)} %fusion.32) | data formatting | bytes 9437184 | tf_op jit(solution)/shard_map/while/body/eval_jaxpr/reshape | solution.py:29
  432.8 6.1 fusion.33
  438.9 3.5 fusion.34
  442.6 2.6 select_select_fusion.2
  447.8 59.1 %all-reduce.2.cloned.1.call-done = bf16[2,384,768]{2,1,0:T(8,128)(2,1)} async-done(((bf16[2,384,768]{2,1,0:T(8,128)(2,1)}), bf16[2,384,768]{2,1,0:T(8,128)(2,1)}) %all-reduce.2.cloned.1.call-update) | async-done | bytes 1179664 | tf_op jit(solution)/shard_map/while/body/eval_jaxpr/psum | solution.py:11
  506.9 4.8 fusion.32
  511.7 6.7 %reshape.316 = f32[2,2,384,2,384]{4,3,2,1,0:T(2,128)} reshape(f32[2,768,768]{2,1,0:T(8,128)} %fusion.32) | data formatting | bytes 9437184 | tf_op jit(solution)/shard_map/while/body/eval_jaxpr/reshape | solution.py:29
  518.4 6.1 fusion.33
  524.5 3.5 fusion.34
  528.3 2.6 select_select_fusion.2
  533.4 60.0 %all-reduce.2.cloned.1.call-done = bf16[2,384,768]{2,1,0:T(8,128)(2,1)} async-done(((bf16[2,384,768]{2,1,0:T(8,128)(2,1)}), bf16[2,384,768]{2,1,0:T(8,128)(2,1)}) %all-reduce.2.cloned.1.call-update) | async-done | bytes 1179664 | tf_op jit(solution)/shard_map/while/body/eval_jaxpr/psum | solution.py:11
  593.5 4.8 fusion.32
  598.3 6.7 %reshape.316 = f32[2,2,384,2,384]{4,3,2,1,0:T(2,128)} reshape(f32[2,768,768]{2,1,0:T(8,128)} %fusion.32) | data formatting | bytes 9437184 | tf_op jit(solution)/shard_map/while/body/eval_jaxpr/reshape | solution.py:29
  605.0 6.1 fusion.33
  611.1 3.5 fusion.34
  614.7 25.1 %conditional.2 = (bf16[2,384,2,384]{3,2,1,0:T(2,128)(2,1)}) conditional(s32[]{:T(128)} %convert_element_type.81, () %tuple.72, (bf16[2,2,384,384]{3,2,1,0:T(8,128)(2,1)}, f32[2,384,2,384]{3,2,1,0:T(2,128)S(1)}) %tuple.184), branch_computations={%region_9.10_spmd, %region_10.11_spmd} | conditional | flops 908328960 | bytes 47185956 | solution.py:97
  614.9 1.9 convert_element_type.78
  616.8 3.2 reshape.302
  620.0 3.5 fusion.18
  623.5 6.7 %reshape.303 = f32[2,2,384,2,384]{4,3,2,1,0:T(2,128)} reshape(f32[2,768,768]{2,1,0:T(8,128)} %fusion.18) | data formatting | bytes 9437184 | tf_op jit(solution)/shard_map/cond/branch_1_fun/reshape | solution.py:29
  630.2 6.7 %fusion.15 = (f32[2,1,384,1,384]{4,3,2,1,0:T(1,128)S(1)}, f32[2,1,384,1,384]{4,3,2,1,0:T(1,128)S(1)}, f32[2,1,384,1,384]{4,3,2,1,0:T(1,128)S(1)}, f32[2,1,384,1,384]{4,3,2,1,0:T(1,128)S(1)}) fusion(f32[2,2,384,2,384]{4,3,2,1,0:T(2,128)} %reshape.303), kind=kLoop, calls=%fused_computation.55 | loop fusion | bytes 9437184 | tf_op jit(solution)/shard_map/cond/branch_1_fun/slice | solution.py:30
  637.5 2.3 copy.45
  639.7 3.8 broadcast_select_fusion
  (162 shorter events, 72.6 us)
Async XLA Ops:
  7.2 1.6 copy-start.9
  7.2 39.7 %all-gather.6.cloned.1.call-start = ((), (), s32[]{:S(2)}) async-start(), calls=%async_computation.1 | async-start | bytes 3538944 | tf_op jit(solution)/shard_map/all_gather | solution.py:39
  7.9 76.6 %all-gather.4.cloned.1.call-start = ((), (), s32[]{:S(2)}) async-start(), calls=%async_computation | async-start | bytes 3538944 | tf_op jit(solution)/shard_map/all_gather | solution.py:38
  8.7 351.9 %all-gather.8.cloned.1.call-start = ((), (), s32[]{:S(2)}) async-start(), calls=%async_computation.2 | async-start | bytes 5898240 | tf_op jit(solution)/shard_map/all_gather | solution.py:74
  92.7 1.1 copy-start.6
  94.2 0.8 copy-start.7
  103.2 2.2 copy-start.6
  105.8 0.8 copy-start.7
  114.9 2.2 copy-start.6
  117.6 0.8 copy-start.7
  126.6 2.2 copy-start.6
  129.2 0.8 copy-start.7
  138.2 2.2 copy-start.6
  140.8 0.8 copy-start.7
  149.9 2.2 copy-start.6
  152.5 0.8 copy-start.7
  161.5 2.2 copy-start.6
  164.1 0.8 copy-start.7
  173.1 2.2 copy-start.6
  175.7 0.8 copy-start.7
  184.8 1.1 copy-start.3
  186.2 0.8 copy-start.4
  195.2 2.2 copy-start.3
  197.8 0.8 copy-start.4
  206.8 2.2 copy-start.3
  209.4 0.8 copy-start.4
  218.4 2.2 copy-start.3
  221.0 0.8 copy-start.4
  230.0 2.2 copy-start.3
  232.6 0.8 copy-start.4
  241.6 2.2 copy-start.3
  244.1 0.8 copy-start.4
  253.1 2.2 copy-start.3
  255.7 0.8 copy-start.4
  264.7 2.2 copy-start.3
  267.3 0.8 copy-start.4
  268.1 1.4 copy-start.2
  268.1 1.6 copy-start.5
  270.9 1.3 copy-start.8
  360.6 60.7 %all-reduce.2.cloned.1.call-start = ((), (), s32[]{:S(2)}) async-start(), calls=%async_computation.3 | async-start | bytes 2359296 | tf_op jit(solution)/shard_map/while/body/eval_jaxpr/psum | solution.py:11
  442.5 64.5 %all-reduce.2.cloned.1.call-start = ((), (), s32[]{:S(2)}) async-start(), calls=%async_computation.3 | async-start | bytes 2359296 | tf_op jit(solution)/shard_map/while/body/eval_jaxpr/psum | solution.py:11
  528.1 65.4 %all-reduce.2.cloned.1.call-start = ((), (), s32[]{:S(2)}) async-start(), calls=%async_computation.3 | async-start | bytes 2359296 | tf_op jit(solution)/shard_map/while/body/eval_jaxpr/psum | solution.py:11
  614.6 25.1 %copy-start.1 = (bf16[2,384,2,384]{3,1,0,2:T(8,128)(2,1)S(1)}, bf16[2,384,2,384]{3,1,0,2:T(8,128)(2,1)}, u32[]{:S(2)}) copy-start(bf16[2,384,2,384]{3,1,0,2:T(8,128)(2,1)} %get-tuple-element.407) | copy-start | bytes 3538948
  616.8 3.2 copy-start
Sparse Core Ops, SparseCore 0:
  9.6 37.2 all-gather.5
  48.4 36.0 all-gather.3
  271.1 89.4 all-gather.7
  363.5 57.7 all-reduce.1
  446.5 60.3 all-reduce.1
  532.2 61.2 all-reduce.1
where the time goes:
time: 654 us; the launch traced here: 650 us
  waiting for transfers between devices  336 us (51%)
  other arithmetic  111 us (17%)
  loops' own time  94.2 us (14%)
  local copies, waits for them, and re-layouts  76.6 us (12%)
  matrix products  18 us (3%)
  between operations  14.2 us (2%)
    psum x3, waiting for transfers between devices, broadcast(): return lax.psum(kept, axis)  176 us
    another operation x2, loops' own time, on_device(): lax.fori_loop(0, pair_count, add_term, (zero_tile, zero_tile))  93.7 us
    all_gather x1, waiting for transfers between devices, on_device(): kernel_rows = lax.all_gather(sigma, 'col', axis=3, tiled=True)  87.5 us
    add x32, other arithmetic, add_term(): return (sum_real + full_real, sum_imag + full_imag)  39 us
    all_gather x1, waiting for transfers between devices, on_device(): lax.all_gather(greater, 'mom', axis=0, tiled=True)  38.1 us
    all_gather x1, waiting for transfers between devices, on_device(): lax.all_gather(lesser, 'mom', axis=0, tiled=True)  33.4 us
    convert_element_type x16, other arithmetic, select_tile(): lax.dynamic_index_in_dim(stacked_tiles, which, 0, keepdims=False)  26.9 us
    reshape x4, local copies, waits for them, and re-layouts, complex_product(): product = product.reshape(count, 2, height, 2, breadth)  26.8 us
  transfers between devices with their start and end apart: 6, of which 6 were waited for; matrix products, arithmetic and copies ran while one was open for 1% of the time, Pallas kernels for 0%

commit v1 on v0

v1 whole, which is shorter than its diff:
```python
import functools
import itertools
import math

import jax
import jax.numpy as jnp
from jax import lax
from jax.experimental import pallas as pl
from jax.experimental.pallas import tpu as pltpu
from jax.sharding import PartitionSpec as P

AXES = ("row", "col", "mom")
VMEM_BYTES = 56 * 1024 * 1024


class Plan:
    def __init__(self, mesh, moments, side):
        self.rows = mesh.shape["row"]
        self.cols = mesh.shape["col"]
        self.moms = mesh.shape["mom"]
        self.moments = moments
        self.side = side
        self.groups = self.rows // moments
        self.half = side // self.moms
        self.part = 2 * self.half // self.groups
        self.dpart = 2 * side // self.groups
        self.width = side // self.groups
        self.tiles = self.rows * (self.rows - 1) // 2

    def tile(self, row, col):
        return row * (row - 1) // 2 + col

    def send(self, value, target):
        pairs = []
        index = lambda r, c, m: (r * self.cols + c) * self.moms + m
        for place in itertools.product(range(self.rows), range(self.cols), range(self.moms)):
            goal = target(*place)
            if goal is not None:
                pairs.append((index(*place), index(*goal)))
        return lax.ppermute(value, AXES, pairs)


def hbm(count):
    return [pl.BlockSpec(memory_space=pl.ANY)] * count


def smem():
    return pl.BlockSpec(memory_space=pltpu.SMEM)


def run_copies(copies):
    for copy in copies:
        copy.start()
    for copy in copies:
        copy.wait()


def sigma_kernel(plan, pair_count, place, triples, *refs):
    moms, moments, groups = plan.moms, plan.moments, plan.groups
    half, part, side = plan.half, plan.part, plan.side
    lesser_in, partner_in = refs[:moms], refs[moms : 2 * moms]
    outs = refs[2 * moms : 2 * moms + moms * plan.rows]
    lesser, partner, result, sems = refs[2 * moms + moms * plan.rows :]
    r, y = place[0], place[2]
    copies = []
    for which, (sources, target) in enumerate(((lesser_in, lesser), (partner_in, partner))):
        for q in range(moms):
            owner = y ^ q
            source = sources[q]
            if q == 0:
                source = source.at[:, :, pl.ds(pl.multiple_of(y * half, half), half), :]
            copies.append(
                pltpu.make_async_copy(
                    source, target.at[pl.ds(owner * moments, moments)], sems.at[which * moms + q]
                )
            )
    run_copies(copies)
    scale = 1.0 / pair_count
    lanes = 128 if side % 128 == 0 else side
    for q in reversed(range(moms)):
        for base in range(0, plan.rows, groups):
            moment = (y ^ q) * moments + (r ^ base) // groups
            table = [[triples[moment, m, n] for n in range(3)] for m in range(pair_count)]

            def block(index, _, table=table):
                row = pl.multiple_of(index * 16, 16)
                for lane in range(0, side, lanes):
                    at = (pl.ds(row, 16), pl.ds(lane, lanes))
                    total_re = total_im = None
                    for a, b, c in table:
                        a_re = lesser[(a, 0) + at].astype(jnp.float32)
                        a_im = lesser[(a, 1) + at].astype(jnp.float32)
                        b_re = lesser[(b, 0) + at].astype(jnp.float32)
                        b_im = lesser[(b, 1) + at].astype(jnp.float32)
                        c_re = partner[(c, 0) + at].astype(jnp.float32)
                        c_im = partner[(c, 1) + at].astype(jnp.float32)
                        p_re = a_re * b_re - a_im * b_im
                        p_im = a_re * b_im + a_im * b_re
                        f_re = p_re * c_re - p_im * c_im
                        f_im = p_re * c_im + p_im * c_re
                        total_re = f_re if total_re is None else total_re + f_re
                        total_im = f_im if total_im is None else total_im + f_im
                    result[(0,) + at] = (total_re * scale).astype(jnp.bfloat16)
                    result[(1,) + at] = (total_im * scale).astype(jnp.bfloat16)
                return 0

            lax.fori_loop(0, half // 16, block, 0)
            for t in range(groups):
                g = (r % groups) ^ t
                start = pl.multiple_of(lax.rem(g * part, half), 16)
                outs[q * plan.rows + base + t][...] = result[g * part // half, pl.ds(start, part), :]


def gather_kernel(plan, sources, place, *refs):
    ins, out, sems = refs[:-2], refs[-2], refs[-1]
    for col in range(plan.cols):

        @pl.when(place[1] == col)
        def _(col=col):
            run_copies(
                [
                    pltpu.make_async_copy(ins[sources[col][t]], out.at[t], sems.at[t])
                    for t in range(plan.tiles)
                ]
            )


def place_kernel(plan, place, *refs):
    ins, out, sems = refs[:-2], refs[-2], refs[-1]
    r, y = place[0], place[2]
    copies = []
    for q in range(plan.moms):
        for s in range(plan.rows):
            g = (r ^ s) % plan.groups
            row = (y ^ q) * plan.half + lax.rem(g * plan.part, plan.half)
            index = q * plan.rows + s
            copies.append(
                pltpu.make_async_copy(
                    ins[index],
                    out.at[
                        (r ^ s) // plan.groups,
                        g * plan.part // plan.half,
                        pl.ds(pl.multiple_of(row, 16), plan.part),
                        :,
                    ],
                    sems.at[index],
                )
            )
    run_copies(copies)


def solve_kernel(plan, place, *refs):
    rows, moms, groups, side = plan.rows, plan.moms, plan.groups, plan.side
    refs = list(refs)
    take = lambda count: [refs.pop(0) for _ in range(count)]
    sig_in, diag_in, right_in, outs = take(moms * groups), take(groups), take(rows), take(rows)
    sig, diag, right, solved, turned, sems = refs
    r, y = place[0], place[2]
    copies = []

    def copy(source, target):
        copies.append(pltpu.make_async_copy(source, target, sems.at[len(copies)]))

    for t in range(groups):
        g = (r % groups) ^ t
        for s in range(rows):
            row = pl.multiple_of(lax.rem(g * plan.dpart, side), 16)
            copy(
                diag_in[t].at[s],
                diag.at[r ^ t ^ s, g * plan.dpart // side, pl.ds(row, plan.dpart), :],
            )
        for q in range(moms):
            row = (y ^ q) * plan.half + lax.rem(g * plan.part, plan.half)
            copy(
                sig_in[q * groups + t],
                sig.at[:, g * plan.part // plan.half, pl.ds(pl.multiple_of(row, 16), plan.part), :],
            )
    for s in range(rows):
        copy(right_in[s], right.at[r ^ s])
    run_copies(copies)

    weight = 1.0 / math.sqrt(side * rows)
    width = plan.width

    def turn(value):
        return jnp.concatenate([-value[:, width:], value[:, :width]], axis=1)

    def dot(left, value):
        return jnp.dot(left, value, preferred_element_type=jnp.float32)

    for row in range(rows):
        pending = right[row].astype(jnp.float32)
        if row > 0:
            update = None
            for col in range(row):
                t = plan.tile(row, col)
                term = dot(sig[t, 0], solved[col]) + dot(sig[t, 1], turned[col])
                update = term if update is None else update + term
            pending = pending + weight * update
        value = dot(diag[row, 0], pending.astype(jnp.bfloat16)) + dot(
            diag[row, 1], turn(pending).astype(jnp.bfloat16)
        )
        solved[row] = value.astype(jnp.bfloat16)
        turned[row] = turn(value).astype(jnp.bfloat16)
    copies = [
        pltpu.make_async_copy(solved.at[r ^ s], outs[s], sems.at[s]) for s in range(rows)
    ]
    run_copies(copies)


def on_device(mesh, lesser, greater, triples, diag_inverse, right_side):
    moments, _, side, _ = lesser.shape
    plan = Plan(mesh, moments, side)
    rows, cols, moms, groups = plan.rows, plan.cols, plan.moms, plan.groups
    half, part, width = plan.half, plan.part, plan.width
    pair_count = triples.shape[1]
    r, z, y = (lax.axis_index(axis) for axis in AXES)
    place = jnp.stack([r, z, y]).astype(jnp.int32)
    bf16 = jnp.bfloat16
    params = pltpu.CompilerParams(vmem_limit_bytes=VMEM_BYTES)
    dma = lambda count: pltpu.SemaphoreType.DMA((count,))

    def exchange_mom(value, q):
        return plan.send(value, lambda a, b, c: (a, b, c ^ q))

    def exchange_row(value, s):
        return plan.send(value, lambda a, b, c: (a ^ s, b, c))

    def half_of(value, q):
        return lax.dynamic_slice_in_dim(value, (y ^ q) * half, half, 2)

    lesser_all = [lesser] + [exchange_mom(half_of(lesser, q), q) for q in range(1, moms)]
    partner = jnp.swapaxes(greater, 2, 3)
    partner_all = [partner] + [exchange_mom(half_of(partner, q), q) for q in range(1, moms)]

    flat_diag = diag_inverse.reshape(moments * 2 * side, side)
    diag_parts = [
        lax.dynamic_slice_in_dim(flat_diag, (r ^ s) * plan.dpart, plan.dpart, 0) for s in range(rows)
    ]
    diag_parts = [diag_parts[0]] + [exchange_row(diag_parts[s], s) for s in range(1, rows)]
    diag_own = jnp.stack(diag_parts)
    diag_all = [diag_own] + [exchange_row(diag_own, t) for t in range(1, groups)]

    right = right_side.reshape(moments, side, 2, groups, width).transpose(0, 3, 1, 2, 4)
    right = right.reshape(rows, side, 2 * width)
    right_parts = [lax.dynamic_index_in_dim(right, r ^ s, 0, keepdims=False) for s in range(rows)]
    right_all = [right_parts[0]] + [exchange_row(right_parts[s], s) for s in range(1, rows)]

    slots = pl.pallas_call(
        functools.partial(sigma_kernel, plan, pair_count),
        out_shape=[jax.ShapeDtypeStruct((part, side), bf16)] * (moms * rows),
        in_specs=[smem(), smem()] + hbm(2 * moms),
        scratch_shapes=[
            pltpu.VMEM((moms * moments, 2, half, side), bf16),
            pltpu.VMEM((moms * moments, 2, half, side), bf16),
            pltpu.VMEM((2, half, side), bf16),
            dma(2 * moms),
        ],
        compiler_params=params,
        name="self_energy",
    )(place, triples, *lesser_all, *partner_all)

    chunks = [slots[:rows]]
    for q in range(1, moms):
        chunks.append([exchange_mom(slot, q) for slot in slots[q * rows : (q + 1) * rows]])

    sigma = pl.pallas_call(
        functools.partial(place_kernel, plan),
        out_shape=jax.ShapeDtypeStruct(lesser.shape, bf16),
        in_specs=[smem()] + hbm(moms * rows),
        out_specs=pl.BlockSpec(memory_space=pl.ANY),
        scratch_shapes=[dma(moms * rows)],
        compiler_params=params,
        name="place_sigma",
    )(place, *[slot for chunk in chunks for slot in chunk])

    def spread(chunk):
        came = [chunk[0]] + [
            plan.send(chunk[s], lambda a, b, c: (a ^ s, b, c) if a > b else None)
            for s in range(1, rows)
        ]
        own = {}
        for i in range(1, rows):
            own[i] = lax.select_n(r ^ jnp.minimum(z + i, rows - 1), *came)
        buffers, found = [], {}

        def keep(value, pairs):
            for key in pairs:
                found[key] = len(buffers)
            buffers.append(value)

        for i in range(1, rows):
            keep(own[i], [(j, i, j) for j in range(cols) if j + i < rows])
        last = cols - 1
        relay = []
        for step in range(1, cols):
            for i in range(1, rows):
                up = [
                    j
                    for j in range(cols)
                    if j + i < rows and j + step < cols and (j + step < last or step == 1)
                ]
                if up:
                    value = plan.send(own[i], lambda a, b, c: (a, b + step, c) if b in up else None)
                    keep(value, [(j, i, j + step) for j in up])
                    if last - 1 - step in up:
                        relay.append((last - 1 - step, i, value))
        for j, i, value in relay:
            value = plan.send(value, lambda a, b, c: (a, last, c) if b == last - 1 else None)
            keep(value, [(j, i, last)])
        for step in range(1, cols):
            for i in range(1, rows):
                down = [j for j in range(cols) if j + i < rows and j - step >= 0]
                if down:
                    value = plan.send(own[i], lambda a, b, c: (a, b - step, c) if b in down else None)
                    keep(value, [(j, i, j - step) for j in down])
        sources = [
            [found[(j, i - j, c)] for i in range(rows) for j in range(i)] for c in range(cols)
        ]
        lower = pl.pallas_call(
            functools.partial(gather_kernel, plan, sources),
            out_shape=jax.ShapeDtypeStruct((plan.tiles, part, side), bf16),
            in_specs=[smem()] + hbm(len(buffers)),
            out_specs=pl.BlockSpec(memory_space=pl.ANY),
            scratch_shapes=[dma(plan.tiles)],
            compiler_params=params,
            name="collect_lower",
        )(place, *buffers)
        return [lower] + [exchange_row(lower, t) for t in range(1, groups)]

    sigma_all = [part_of for chunk in chunks for part_of in spread(chunk)]

    solved = pl.pallas_call(
        functools.partial(solve_kernel, plan),
        out_shape=[jax.ShapeDtypeStruct((side, 2 * width), bf16)] * rows,
        in_specs=[smem()] + hbm(moms * groups + groups + rows),
        out_specs=hbm(rows),
        scratch_shapes=[
            pltpu.VMEM((plan.tiles, 2, side, side), bf16),
            pltpu.VMEM((rows, 2, side, side), bf16),
            pltpu.VMEM((rows, side, 2 * width), bf16),
            pltpu.VMEM((rows, side, 2 * width), bf16),
            pltpu.VMEM((rows, side, 2 * width), bf16),
            dma(groups * (rows + moms) + rows),
        ],
        compiler_params=params,
        name="substitution",
    )(place, *sigma_all, *diag_all, *right_all)

    back = [solved[0]] + [exchange_row(solved[s], s) for s in range(1, rows)]
    pieces = jnp.stack([lax.select_n(r ^ s, *back) for s in range(rows)])
    pieces = pieces.reshape(moments, groups, side, 2, width).transpose(0, 2, 3, 1, 4)
    return sigma, pieces.reshape(moments, side, 2, side)


def solution(mesh):
    placed = (
        P("mom", None, "row", "col"),
        P("mom", None, "col", "row"),
        P(),
        P("mom", None, "row", None),
        P("mom", "row", None, "col"),
    )
    return jax.shard_map(
        functools.partial(on_device, mesh),
        mesh=mesh,
        in_specs=placed,
        out_specs=(P("mom", None, "row", "col"), P("mom", "row", None, "col")),
        check_vma=False,
    )
```

time: 654 us -> 263 us (0.40)
  the two profiles are of different devices: /device:TPU:3 before, /device:TPU:25 now
where the time goes in v1:
time: 263 us; the launch traced here: 260 us
  Pallas kernels  116 us (44%)
  waiting for transfers between devices  63.9 us (24%)
  starting transfers between devices  60.8 us (23%)
  local copies, waits for them, and re-layouts  14.9 us (6%)
    ppermute x52, waiting for transfers between devices, send(): return lax.ppermute(value, AXES, pairs)  63.9 us
    ppermute x52, starting transfers between devices, send(): return lax.ppermute(value, AXES, pairs)  60.8 us
    pallas_call x2, Pallas kernels, spread(): pl.pallas_call(functools.partial(gather_kernel, plan, sources), out_shape...  57.3 us
    pallas_call x1, Pallas kernels, on_device(): pl.pallas_call(functools.partial(place_kernel, plan), out_shape=jax.Shape...  37.7 us
    pallas_call x1, Pallas kernels, on_device(): pl.pallas_call(functools.partial(sigma_kernel, plan, pair_count), out_sha...  11.7 us
    unnamed x102, local copies, waits for them, and re-layouts  10.3 us
    pallas_call x1, Pallas kernels, on_device(): pl.pallas_call(functools.partial(solve_kernel, plan), out_shape=[jax.Shap...  9.68 us
  transfers between devices with their start and end apart: 52, of which 11 were waited for; matrix products, arithmetic and copies ran while one was open for 3% of the time, Pallas kernels for 41%

profile of v1, /device:TPU:25, one launch (start us, length us, event | category | flops | bytes accessed | tf_op | source)
XLA Modules:
  0.0 260.2 jit_solution(17266387223437444324)
XLA Ops:
  0.6 1.7 copy.12
  2.4 0.9 dynamic-slice_bitcast_fusion
  3.3 1.2 collective-permute-start.1
  4.5 0.9 constant_dynamic-slice_fusion.7
  5.4 1.0 collective-permute-start
  6.5 1.0 collective-permute-start.42
  7.5 1.2 collective-permute-start.43
  10.1 7.7 %collective-permute-done.1.refs_3_ = bf16[2,2,192,384]{3,2,1,0:T(8,128)(2,1)} collective-permute-done((bf16[2,2,192,384]{3,2,1,0:T(8,128)(2,1)}, bf16[2,2,192,384]{3,2,1,0:T(8,128)(2,1)}, u32[]{:S(2)}, u32[]{:S(2)}) %collective-permute-start.1) | collective-permute-done | bytes 589856 | tf_op jit(solution)/shard_map/ppermute | solution.py:40
  17.8 12.5 %collective-permute-done.refs_1_ = bf16[2,2,192,384]{3,2,1,0:T(8,128)(2,1)S(1)} collective-permute-done((bf16[2,2,192,384]{3,2,1,0:T(8,128)(2,1)}, bf16[2,2,192,384]{3,2,1,0:T(8,128)(2,1)S(1)}, u32[]{:S(2)}, u32[]{:S(2)}) %collective-permute-start) | collective-permute-done | bytes 589856 | tf_op jit(solution)/shard_map/ppermute | solution.py:40
  30.3 0.8 copy-done.12
  31.2 11.7 %self_energy.1 = (bf16[192,384]{1,0:T(8,128)(2,1)}, bf16[192,384]{1,0:T(8,128)(2,1)}, bf16[192,384]{1,0:T(8,128)(2,1)}, bf16[192,384]{1,0:T(8,128)(2,1)}, bf16[1...) custom-call(s32[3]{0:T(128)} %pad_add_fusion.place, ...), custom_call_target="tpu_custom_call" | custom-call | tf_op jit(solution)/shard_map/self_energy/pallas_call | solution.py:249
  42.9 1.3 collective-permute-start.3
  46.2 3.0 %collective-permute-start.44 = (bf16[384,384]{1,0:T(8,128)(2,1)S(1)}, bf16[384,384]{1,0:T(8,128)(2,1)S(1)}, u32[]{:S(2)}, u32[]{:S(2)}) collective-permute-start(bf16[384,384]{1,0:T(8,128)(2,1)S(1)} %get-tuple-element.37), channel_id=1, source_target_pairs={{0,24},{1,25},{2,26},{3,27},{4,28},{5,29},{6,30},{7,31},{8,16},{9,... | collective-permute-start | bytes 884744 | tf_op jit(solution)/shard_map/ppermute | solution.py:40
  49.4 1.2 collective-permute-start.5
  51.6 1.0 select_select_fusion.3
  52.6 1.6 collective-permute-done.4.refs_6_
  54.8 2.5 collective-permute-done.5.refs_7_
  58.0 1.3 collective-permute-start.9
  59.3 1.2 collective-permute-done.2.refs_4_
  66.8 1.3 collective-permute-start.27
  70.9 17.8 %collective-permute-done.27.refs_3_ = bf16[192,384]{1,0:T(8,128)(2,1)S(1)} collective-permute-done((bf16[192,384]{1,0:T(8,128)(2,1)S(1)}, bf16[192,384]{1,0:T(8,128)(2,1)S(1)}, u32[]{:S(2)}, u32[]{:S(2)}) %collective-permute-start.27) | collective-permute-done | bytes 147488 | tf_op jit(solution)/shard_map/ppermute | solution.py:40
  91.4 1.3 collective-permute-start.15
  92.8 1.3 collective-permute-start.16
  94.5 1.3 collective-permute-start.17
  95.8 1.3 collective-permute-start.18
  97.1 1.3 collective-permute-start.19
  98.4 7.5 %collective-permute-done.15.refs_9_ = bf16[192,384]{1,0:T(8,128)(2,1)S(1)} collective-permute-done((bf16[192,384]{1,0:T(8,128)(2,1)S(1)}, bf16[192,384]{1,0:T(8,128)(2,1)S(1)}, u32[]{:S(2)}, u32[]{:S(2)}) %collective-permute-start.15) | collective-permute-done | bytes 147488 | tf_op jit(solution)/shard_map/ppermute | solution.py:40
  105.9 1.3 collective-permute-start.33
  107.5 8.7 %collective-permute-start.45 = (bf16[4,384,384]{2,1,0:T(8,128)(2,1)S(1)}, bf16[4,384,384]{2,1,0:T(8,128)(2,1)}, u32[]{:S(2)}, u32[]{:S(2)}) collective-permute-start(bf16[4,384,384]{2,1,0:T(8,128)(2,1)S(1)} %pad_maximum_fusion.refs_4_), channel_id=1, source_target_pairs={{0,8},{1,9},{2,10},{3,11},{4,12},{5,13},{6,14},{7,15},{8,0},{9,1},... | collective-permute-start | bytes 3538952 | tf_op jit(solution)/shard_map/ppermute | solution.py:40
  116.2 1.3 collective-permute-start.34
  117.5 1.3 collective-permute-start.35
  118.9 1.3 collective-permute-start.36
  120.2 1.5 collective-permute-start.37
  121.7 28.7 %collect_lower.2.refs_0_ = bf16[6,192,384]{2,1,0:T(8,128)(2,1)} custom-call(s32[3]{0:T(128)} %pad_add_fusion.place, bf16[192,384]{1,0:T(8,128)(2,1)} %copy-done.8, bf16[192,384]{1,0:T(8,128)(2,1)} %copy-done.7, bf16[192,384]{1,0:T(8,128)(2,1)} %copy-done.6, bf16[192,384]{1,0:T(8,128)(2,1)} %copy-done.20, bf16[192,384]{1,0:T(8,128)(2,1)} %copy-done.22, ...), custom_call_target="tpu_custom_call" | custom-call | tf_op jit(solution)/shard_map/collect_lower/pallas_call | solution.py:320
  150.5 6.6 %collective-permute-start.23 = (bf16[6,192,384]{2,1,0:T(8,128)(2,1)}, bf16[6,192,384]{2,1,0:T(8,128)(2,1)}, u32[]{:S(2)}, u32[]{:S(2)}) collective-permute-start(bf16[6,192,384]{2,1,0:T(8,128)(2,1)} %collect_lower.2.refs_0_), channel_id=1, source_target_pairs={{0,8},{1,9},{2,10},{3,11},{4,12},{5,13},{6,14},{7,15},{8,0},{9,1},... | collective-permute-start | bytes 2654216 | tf_op jit(solution)/shard_map/ppermute | solution.py:40
  158.5 28.7 %collect_lower.3.refs_2_ = bf16[6,192,384]{2,1,0:T(8,128)(2,1)} custom-call(s32[3]{0:T(128)} %pad_add_fusion.place, bf16[192,384]{1,0:T(8,128)(2,1)} %copy-done.11, bf16[192,384]{1,0:T(8,128)(2,1)} %copy-done.10, bf16[192,384]{1,0:T(8,128)(2,1)} %copy-done.9, bf16[192,384]{1,0:T(8,128)(2,1)} %copy-done.26, bf16[192,384]{1,0:T(8,128)(2,1)} %copy-done.27, ...), custom_call_target="tpu_custom_call" | custom-call | tf_op jit(solution)/shard_map/collect_lower/pallas_call | solution.py:320
  187.3 2.0 copy.15
  190.5 1.0 collective-permute-start.47
  191.7 0.9 collective-permute-start.48
  192.7 0.9 copy.17
  193.6 5.6 %collective-permute-done.47.refs_8_ = bf16[384,384]{1,0:T(8,128)(2,1)S(1)} collective-permute-done((bf16[384,384]{1,0:T(8,128)(2,1)S(1)}, bf16[384,384]{1,0:T(8,128)(2,1)S(1)}, u32[]{:S(2)}, u32[]{:S(2)}) %collective-permute-start.47) | collective-permute-done | bytes 294944 | tf_op jit(solution)/shard_map/ppermute | solution.py:40
  199.2 6.5 %collective-permute-done.48.refs_9_ = bf16[384,384]{1,0:T(8,128)(2,1)S(1)} collective-permute-done((bf16[384,384]{1,0:T(8,128)(2,1)S(1)}, bf16[384,384]{1,0:T(8,128)(2,1)S(1)}, u32[]{:S(2)}, u32[]{:S(2)}) %collective-permute-start.48) | collective-permute-done | bytes 294944 | tf_op jit(solution)/shard_map/ppermute | solution.py:40
  206.3 9.7 %substitution.1 = (bf16[384,384]{1,0:T(8,128)(2,1)}, bf16[384,384]{1,0:T(8,128)(2,1)}, bf16[384,384]{1,0:T(8,128)(2,1)}, bf16[384,384]{1,0:T(8,128)(2,1)}) custom-call(s32[3]{0:T(128)} %pad_add_fusion.place, bf16[6,192,384]{2,1,0:T(8,128)(2,1)} %collect_lower.2.refs_0_, bf16[6,192,384]{2,1,0:T(8,128)(2,1)} %collective-permute-done.23.refs_1_, ...), custom_call_target="tpu_custom_call" | custom-call | tf_op jit(solution)/shard_map/substitution/pallas_call | solution.py:333
  216.3 0.9 collective-permute-start.50
  217.2 1.0 collective-permute-start.51
  218.2 37.7 %place_sigma.1 = bf16[2,2,384,384]{3,2,1,0:T(8,128)(2,1)} custom-call(s32[3]{0:T(128)} %pad_add_fusion.place, bf16[192,384]{1,0:T(8,128)(2,1)} %get-tuple-element.14.refs_0_, bf16[192,384]{1,0:T(8,128)(2,1)} %get-tuple-element.15.refs_1_, bf16[192,384]{1,0:T(8,128)(2,1)} %get-tuple-element.16.refs_2_, bf16[192,384]{1,0:T(8,128)(2,1)} %get-tuple-element.17.refs_3_, ...), custom_call_target="tpu_custom_call" | custom-call | tf_op jit(solution)/shard_map/place_sigma/pallas_call | solution.py:267
  256.4 0.8 copy.21
  257.3 2.8 %copy.23 = bf16[2,384,2,384]{3,2,1,0:T(2,128)(2,1)} copy(bf16[2,384,2,384]{1,3,2,0:T(8,128)(2,1)S(1)} %bitcast.34) | data formatting | bytes 2359296
  (180 shorter events, 22.4 us)
Async XLA Ops:
  3.3 14.5 %collective-permute-start.1 = (bf16[2,2,192,384]{3,2,1,0:T(8,128)(2,1)}, bf16[2,2,192,384]{3,2,1,0:T(8,128)(2,1)}, u32[]{:S(2)}, u32[]{:S(2)}) collective-permute-start(bf16[2,2,192,384]{3,2,1,0:T(8,128)(2,1)} %dynamic-slice_bitcast_fusion), channel_id=1, source_target_pairs={{0,1},{1,0},{2,3},{3,2},{4,5},{5,4},{6,7},{7,6},{8,9},{9,8},{10,11... | collective-permute-start | bytes 1769480 | tf_op jit(solution)/shard_map/ppermute | solution.py:40
  5.4 24.9 %collective-permute-start = (bf16[2,2,192,384]{3,2,1,0:T(8,128)(2,1)}, bf16[2,2,192,384]{3,2,1,0:T(8,128)(2,1)S(1)}, u32[]{:S(2)}, u32[]{:S(2)}) collective-permute-start(bf16[2,2,192,384]{3,2,1,0:T(8,128)(2,1)} %constant_dynamic-slice_fusion.7), channel_id=1, source_target_pairs={{0,1},{1,0},{2,3},{3,2},{4,5},{5,4},{6,7},{7,6},{8,9},{9,8},{10,11... | collective-permute-start | bytes 1769480 | tf_op jit(solution)/shard_map/ppermute | solution.py:40
  6.5 39.0 %collective-permute-start.42 = (bf16[384,384]{1,0:T(8,128)(2,1)S(1)}, bf16[384,384]{1,0:T(8,128)(2,1)S(1)}, u32[]{:S(2)}, u32[]{:S(2)}) collective-permute-start(bf16[384,384]{1,0:T(8,128)(2,1)S(1)} %get-tuple-element.39), channel_id=1, source_target_pairs={{0,8},{1,9},{2,10},{3,11},{4,12},{5,13},{6,14},{7,15},{8,0},{9,1},... | collective-permute-start | bytes 884744 | tf_op jit(solution)/shard_map/ppermute | solution.py:40
  7.5 38.6 %collective-permute-start.43 = (bf16[384,384]{1,0:T(8,128)(2,1)S(1)}, bf16[384,384]{1,0:T(8,128)(2,1)S(1)}, u32[]{:S(2)}, u32[]{:S(2)}) collective-permute-start(bf16[384,384]{1,0:T(8,128)(2,1)S(1)} %get-tuple-element.38), channel_id=1, source_target_pairs={{0,16},{1,17},{2,18},{3,19},{4,20},{5,21},{6,22},{7,23},{8,24},{9,... | collective-permute-start | bytes 884744 | tf_op jit(solution)/shard_map/ppermute | solution.py:40
  42.9 6.3 %collective-permute-start.3 = (bf16[192,384]{1,0:T(8,128)(2,1)}, bf16[192,384]{1,0:T(8,128)(2,1)S(1)}, u32[]{:S(2)}, u32[]{:S(2)}) collective-permute-start(bf16[192,384]{1,0:T(8,128)(2,1)} %get-tuple-element.19), channel_id=1, source_target_pairs={{0,1},{1,0},{2,3},{3,2},{4,5},{5,4},{6,7},{7,6},{8,9},{9,8},{10,11... | collective-permute-start | bytes 442376 | tf_op jit(solution)/shard_map/ppermute | solution.py:40
  44.2 5.3 %collective-permute-start.6 = (bf16[192,384]{1,0:T(8,128)(2,1)}, bf16[192,384]{1,0:T(8,128)(2,1)S(1)}, u32[]{:S(2)}, u32[]{:S(2)}) collective-permute-start(bf16[192,384]{1,0:T(8,128)(2,1)} %get-tuple-element.15.refs_1_), channel_id=1, source_target_pairs={{8,0},{9,1},{16,24},{17,25},{18,26},{19,27},{24,16},{25,17},{26,18... | collective-permute-start | bytes 442376 | tf_op jit(solution)/shard_map/ppermute | solution.py:40
  44.8 5.8 %collective-permute-start.7 = (bf16[192,384]{1,0:T(8,128)(2,1)}, bf16[192,384]{1,0:T(8,128)(2,1)S(1)}, u32[]{:S(2)}, u32[]{:S(2)}) collective-permute-start(bf16[192,384]{1,0:T(8,128)(2,1)} %get-tuple-element.16.refs_2_), channel_id=1, source_target_pairs={{8,24},{9,25},{16,0},{17,1},{18,2},{19,3},{24,8},{25,9},{26,10},{2... | collective-permute-start | bytes 442376 | tf_op jit(solution)/shard_map/ppermute | solution.py:40
  45.5 5.4 %collective-permute-start.8 = (bf16[192,384]{1,0:T(8,128)(2,1)}, bf16[192,384]{1,0:T(8,128)(2,1)S(1)}, u32[]{:S(2)}, u32[]{:S(2)}) collective-permute-start(bf16[192,384]{1,0:T(8,128)(2,1)} %get-tuple-element.17.refs_3_), channel_id=1, source_target_pairs={{8,16},{9,17},{16,8},{17,9},{18,10},{19,11},{24,0},{25,1},{26,2},{... | collective-permute-start | bytes 442376 | tf_op jit(solution)/shard_map/ppermute | solution.py:40
  46.2 11.8 %collective-permute-start.44 = (bf16[384,384]{1,0:T(8,128)(2,1)S(1)}, bf16[384,384]{1,0:T(8,128)(2,1)S(1)}, u32[]{:S(2)}, u32[]{:S(2)}) collective-permute-start(bf16[384,384]{1,0:T(8,128)(2,1)S(1)} %get-tuple-element.37), channel_id=1, source_target_pairs={{0,24},{1,25},{2,26},{3,27},{4,28},{5,29},{6,30},{7,31},{8,16},{9,... | collective-permute-start | bytes 884744 | tf_op jit(solution)/shard_map/ppermute | solution.py:40
  49.2 5.0 %collective-permute-start.4 = (bf16[192,384]{1,0:T(8,128)(2,1)}, bf16[192,384]{1,0:T(8,128)(2,1)S(1)}, u32[]{:S(2)}, u32[]{:S(2)}) collective-permute-start(bf16[192,384]{1,0:T(8,128)(2,1)} %get-tuple-element.20), channel_id=1, source_target_pairs={{0,1},{1,0},{2,3},{3,2},{4,5},{5,4},{6,7},{7,6},{8,9},{9,8},{10,11... | collective-permute-start | bytes 442376 | tf_op jit(solution)/shard_map/ppermute | solution.py:40
  49.4 7.9 %collective-permute-start.5 = (bf16[192,384]{1,0:T(8,128)(2,1)}, bf16[192,384]{1,0:T(8,128)(2,1)S(1)}, u32[]{:S(2)}, u32[]{:S(2)}) collective-permute-start(bf16[192,384]{1,0:T(8,128)(2,1)} %get-tuple-element.21), channel_id=1, source_target_pairs={{0,1},{1,0},{2,3},{3,2},{4,5},{5,4},{6,7},{7,6},{8,9},{9,8},{10,11... | collective-permute-start | bytes 442376 | tf_op jit(solution)/shard_map/ppermute | solution.py:40
  50.7 9.8 %collective-permute-start.2 = (bf16[192,384]{1,0:T(8,128)(2,1)}, bf16[192,384]{1,0:T(8,128)(2,1)S(1)}, u32[]{:S(2)}, u32[]{:S(2)}) collective-permute-start(bf16[192,384]{1,0:T(8,128)(2,1)} %get-tuple-element.18), channel_id=1, source_target_pairs={{0,1},{1,0},{2,3},{3,2},{4,5},{5,4},{6,7},{7,6},{8,9},{9,8},{10,11... | collective-permute-start | bytes 442376 | tf_op jit(solution)/shard_map/ppermute | solution.py:40
  50.9 10.3 %collective-permute-start.24 = (bf16[192,384]{1,0:T(8,128)(2,1)S(1)}, bf16[192,384]{1,0:T(8,128)(2,1)S(1)}, u32[]{:S(2)}, u32[]{:S(2)}) collective-permute-start(bf16[192,384]{1,0:T(8,128)(2,1)S(1)} %collective-permute-done.3.refs_5_), channel_id=1, source_target_pairs={{8,0},{9,1},{16,24},{17,25},{18,26},{19,27},{24,16},{25,17},{26,18... | collective-permute-start | bytes 442376 | tf_op jit(solution)/shard_map/ppermute | solution.py:40
  54.2 7.7 %collective-permute-start.25 = (bf16[192,384]{1,0:T(8,128)(2,1)S(1)}, bf16[192,384]{1,0:T(8,128)(2,1)S(1)}, u32[]{:S(2)}, u32[]{:S(2)}) collective-permute-start(bf16[192,384]{1,0:T(8,128)(2,1)S(1)} %collective-permute-done.4.refs_6_), channel_id=1, source_target_pairs={{8,24},{9,25},{16,0},{17,1},{18,2},{19,3},{24,8},{25,9},{26,10},{2... | collective-permute-start | bytes 442376 | tf_op jit(solution)/shard_map/ppermute | solution.py:40
  57.3 5.2 %collective-permute-start.26 = (bf16[192,384]{1,0:T(8,128)(2,1)S(1)}, bf16[192,384]{1,0:T(8,128)(2,1)S(1)}, u32[]{:S(2)}, u32[]{:S(2)}) collective-permute-start(bf16[192,384]{1,0:T(8,128)(2,1)S(1)} %collective-permute-done.5.refs_7_), channel_id=1, source_target_pairs={{8,16},{9,17},{16,8},{17,9},{18,10},{19,11},{24,0},{25,1},{26,2},{... | collective-permute-start | bytes 442376 | tf_op jit(solution)/shard_map/ppermute | solution.py:40
  58.0 5.9 %collective-permute-start.9 = (bf16[192,384]{1,0:T(8,128)(2,1)S(1)}, bf16[192,384]{1,0:T(8,128)(2,1)S(1)}, u32[]{:S(2)}, u32[]{:S(2)}) collective-permute-start(bf16[192,384]{1,0:T(8,128)(2,1)S(1)} %get-tuple-element.45.refs_0_), channel_id=1, source_target_pairs={{0,2},{1,3},{2,4},{3,5},{4,6},{5,7},{8,10},{9,11},{10,12},{11,13},... | collective-permute-start | bytes 442376 | tf_op jit(solution)/shard_map/ppermute | solution.py:40
  60.5 4.9 %collective-permute-start.12 = (bf16[192,384]{1,0:T(8,128)(2,1)S(1)}, bf16[192,384]{1,0:T(8,128)(2,1)S(1)}, u32[]{:S(2)}, u32[]{:S(2)}) collective-permute-start(bf16[192,384]{1,0:T(8,128)(2,1)S(1)} %get-tuple-element.45.refs_0_), channel_id=1, source_target_pairs={{0,4},{1,5},{8,12},{9,13},{16,20},{17,21},{24,28},{25,29}} | collective-permute-start | bytes 442376 | tf_op jit(solution)/shard_map/ppermute | solution.py:40
  61.9 4.2 %collective-permute-start.13 = (bf16[192,384]{1,0:T(8,128)(2,1)S(1)}, bf16[192,384]{1,0:T(8,128)(2,1)S(1)}, u32[]{:S(2)}, u32[]{:S(2)}) collective-permute-start(bf16[192,384]{1,0:T(8,128)(2,1)S(1)} %get-tuple-element.44.refs_1_), channel_id=1, source_target_pairs={{0,4},{1,5},{8,12},{9,13},{16,20},{17,21},{24,28},{25,29}} | collective-permute-start | bytes 442376 | tf_op jit(solution)/shard_map/ppermute | solution.py:40
  62.5 4.2 %collective-permute-start.14 = (bf16[192,384]{1,0:T(8,128)(2,1)S(1)}, bf16[192,384]{1,0:T(8,128)(2,1)S(1)}, u32[]{:S(2)}, u32[]{:S(2)}) collective-permute-start(bf16[192,384]{1,0:T(8,128)(2,1)S(1)} %get-tuple-element.43.refs_2_), channel_id=1, source_target_pairs={{0,4},{1,5},{8,12},{9,13},{16,20},{17,21},{24,28},{25,29}} | collective-permute-start | bytes 442376 | tf_op jit(solution)/shard_map/ppermute | solution.py:40
  63.9 4.2 %collective-permute-start.11 = (bf16[192,384]{1,0:T(8,128)(2,1)S(1)}, bf16[192,384]{1,0:T(8,128)(2,1)S(1)}, u32[]{:S(2)}, u32[]{:S(2)}) collective-permute-start(bf16[192,384]{1,0:T(8,128)(2,1)S(1)} %get-tuple-element.43.refs_2_), channel_id=1, source_target_pairs={{0,2},{1,3},{8,10},{9,11},{16,18},{17,19},{24,26},{25,27}} | collective-permute-start | bytes 442376 | tf_op jit(solution)/shard_map/ppermute | solution.py:40
  64.7 4.1 %collective-permute-start.20 = (bf16[192,384]{1,0:T(8,128)(2,1)S(1)}, bf16[192,384]{1,0:T(8,128)(2,1)S(1)}, u32[]{:S(2)}, u32[]{:S(2)}) collective-permute-start(bf16[192,384]{1,0:T(8,128)(2,1)S(1)} %get-tuple-element.45.refs_0_), channel_id=1, source_target_pairs={{2,0},{3,1},{4,2},{5,3},{10,8},{11,9},{12,10},{13,11},{18,16},{19,... | collective-permute-start | bytes 442376 | tf_op jit(solution)/shard_map/ppermute | solution.py:40
  65.4 4.1 %collective-permute-start.21 = (bf16[192,384]{1,0:T(8,128)(2,1)S(1)}, bf16[192,384]{1,0:T(8,128)(2,1)S(1)}, u32[]{:S(2)}, u32[]{:S(2)}) collective-permute-start(bf16[192,384]{1,0:T(8,128)(2,1)S(1)} %get-tuple-element.44.refs_1_), channel_id=1, source_target_pairs={{2,0},{3,1},{10,8},{11,9},{18,16},{19,17},{26,24},{27,25}} | collective-permute-start | bytes 442376 | tf_op jit(solution)/shard_map/ppermute | solution.py:40
  66.8 21.9 %collective-permute-start.27 = (bf16[192,384]{1,0:T(8,128)(2,1)S(1)}, bf16[192,384]{1,0:T(8,128)(2,1)S(1)}, u32[]{:S(2)}, u32[]{:S(2)}) collective-permute-start(bf16[192,384]{1,0:T(8,128)(2,1)S(1)} %get-tuple-element.42.refs_0_), channel_id=1, source_target_pairs={{0,2},{1,3},{2,4},{3,5},{4,6},{5,7},{8,10},{9,11},{10,12},{11,13},... | collective-permute-start | bytes 442376 | tf_op jit(solution)/shard_map/ppermute | solution.py:40
  68.1 21.2 %collective-permute-start.28 = (bf16[192,384]{1,0:T(8,128)(2,1)S(1)}, bf16[192,384]{1,0:T(8,128)(2,1)S(1)}, u32[]{:S(2)}, u32[]{:S(2)}) collective-permute-start(bf16[192,384]{1,0:T(8,128)(2,1)S(1)} %get-tuple-element.41.refs_1_), channel_id=1, source_target_pairs={{0,2},{1,3},{2,4},{3,5},{8,10},{9,11},{10,12},{11,13},{16,18},{17,... | collective-permute-start | bytes 442376 | tf_op jit(solution)/shard_map/ppermute | solution.py:40
  68.8 21.2 %collective-permute-start.30 = (bf16[192,384]{1,0:T(8,128)(2,1)S(1)}, bf16[192,384]{1,0:T(8,128)(2,1)S(1)}, u32[]{:S(2)}, u32[]{:S(2)}) collective-permute-start(bf16[192,384]{1,0:T(8,128)(2,1)S(1)} %get-tuple-element.42.refs_0_), channel_id=1, source_target_pairs={{0,4},{1,5},{8,12},{9,13},{16,20},{17,21},{24,28},{25,29}} | collective-permute-start | bytes 442376 | tf_op jit(solution)/shard_map/ppermute | solution.py:40
  69.5 21.2 %collective-permute-start.31 = (bf16[192,384]{1,0:T(8,128)(2,1)S(1)}, bf16[192,384]{1,0:T(8,128)(2,1)S(1)}, u32[]{:S(2)}, u32[]{:S(2)}) collective-permute-start(bf16[192,384]{1,0:T(8,128)(2,1)S(1)} %get-tuple-element.41.refs_1_), channel_id=1, source_target_pairs={{0,4},{1,5},{8,12},{9,13},{16,20},{17,21},{24,28},{25,29}} | collective-permute-start | bytes 442376 | tf_op jit(solution)/shard_map/ppermute | solution.py:40
  70.2 21.2 %collective-permute-start.32 = (bf16[192,384]{1,0:T(8,128)(2,1)S(1)}, bf16[192,384]{1,0:T(8,128)(2,1)S(1)}, u32[]{:S(2)}, u32[]{:S(2)}) collective-permute-start(bf16[192,384]{1,0:T(8,128)(2,1)S(1)} %get-tuple-element.40.refs_2_), channel_id=1, source_target_pairs={{0,4},{1,5},{8,12},{9,13},{16,20},{17,21},{24,28},{25,29}} | collective-permute-start | bytes 442376 | tf_op jit(solution)/shard_map/ppermute | solution.py:40
  89.4 5.1 %collective-permute-start.38 = (bf16[192,384]{1,0:T(8,128)(2,1)S(1)}, bf16[192,384]{1,0:T(8,128)(2,1)S(1)}, u32[]{:S(2)}, u32[]{:S(2)}) collective-permute-start(bf16[192,384]{1,0:T(8,128)(2,1)S(1)} %get-tuple-element.42.refs_0_), channel_id=1, source_target_pairs={{2,0},{3,1},{4,2},{5,3},{10,8},{11,9},{12,10},{13,11},{18,16},{19,... | collective-permute-start | bytes 442376 | tf_op jit(solution)/shard_map/ppermute | solution.py:40
  90.0 5.7 %collective-permute-start.39 = (bf16[192,384]{1,0:T(8,128)(2,1)S(1)}, bf16[192,384]{1,0:T(8,128)(2,1)S(1)}, u32[]{:S(2)}, u32[]{:S(2)}) collective-permute-start(bf16[192,384]{1,0:T(8,128)(2,1)S(1)} %get-tuple-element.41.refs_1_), channel_id=1, source_target_pairs={{2,0},{3,1},{10,8},{11,9},{18,16},{19,17},{26,24},{27,25}} | collective-permute-start | bytes 442376 | tf_op jit(solution)/shard_map/ppermute | solution.py:40
  90.7 6.3 %collective-permute-start.40 = (bf16[192,384]{1,0:T(8,128)(2,1)S(1)}, bf16[192,384]{1,0:T(8,128)(2,1)S(1)}, u32[]{:S(2)}, u32[]{:S(2)}) collective-permute-start(bf16[192,384]{1,0:T(8,128)(2,1)S(1)} %get-tuple-element.42.refs_0_), channel_id=1, source_target_pairs={{4,0},{5,1},{12,8},{13,9},{20,16},{21,17},{28,24},{29,25}} | collective-permute-start | bytes 442376 | tf_op jit(solution)/shard_map/ppermute | solution.py:40
  91.4 14.5 %collective-permute-start.15 = (bf16[192,384]{1,0:T(8,128)(2,1)S(1)}, bf16[192,384]{1,0:T(8,128)(2,1)S(1)}, u32[]{:S(2)}, u32[]{:S(2)}) collective-permute-start(bf16[192,384]{1,0:T(8,128)(2,1)S(1)} %collective-permute-done.9.refs_3_), channel_id=1, source_target_pairs={{4,6},{5,7},{12,14},{13,15},{20,22},{21,23},{28,30},{29,31}} | collective-permute-start | bytes 442376 | tf_op jit(solution)/shard_map/ppermute | solution.py:40
  92.8 14.7 %collective-permute-start.16 = (bf16[192,384]{1,0:T(8,128)(2,1)S(1)}, bf16[192,384]{1,0:T(8,128)(2,1)S(1)}, u32[]{:S(2)}, u32[]{:S(2)}) collective-permute-start(bf16[192,384]{1,0:T(8,128)(2,1)S(1)} %collective-permute-done.10.refs_4_), channel_id=1, source_target_pairs={{4,6},{5,7},{12,14},{13,15},{20,22},{21,23},{28,30},{29,31}} | collective-permute-start | bytes 442376 | tf_op jit(solution)/shard_map/ppermute | solution.py:40
  94.5 21.7 %collective-permute-start.17 = (bf16[192,384]{1,0:T(8,128)(2,1)S(1)}, bf16[192,384]{1,0:T(8,128)(2,1)S(1)}, u32[]{:S(2)}, u32[]{:S(2)}) collective-permute-start(bf16[192,384]{1,0:T(8,128)(2,1)S(1)} %collective-permute-done.12.refs_6_), channel_id=1, source_target_pairs={{4,6},{5,7},{12,14},{13,15},{20,22},{21,23},{28,30},{29,31}} | collective-permute-start | bytes 442376 | tf_op jit(solution)/shard_map/ppermute | solution.py:40
  95.8 21.7 %collective-permute-start.18 = (bf16[192,384]{1,0:T(8,128)(2,1)S(1)}, bf16[192,384]{1,0:T(8,128)(2,1)S(1)}, u32[]{:S(2)}, u32[]{:S(2)}) collective-permute-start(bf16[192,384]{1,0:T(8,128)(2,1)S(1)} %collective-permute-done.13.refs_7_), channel_id=1, source_target_pairs={{4,6},{5,7},{12,14},{13,15},{20,22},{21,23},{28,30},{29,31}} | collective-permute-start | bytes 442376 | tf_op jit(solution)/shard_map/ppermute | solution.py:40
  97.1 21.7 %collective-permute-start.19 = (bf16[192,384]{1,0:T(8,128)(2,1)S(1)}, bf16[192,384]{1,0:T(8,128)(2,1)S(1)}, u32[]{:S(2)}, u32[]{:S(2)}) collective-permute-start(bf16[192,384]{1,0:T(8,128)(2,1)S(1)} %collective-permute-done.14.refs_8_), channel_id=1, source_target_pairs={{4,6},{5,7},{12,14},{13,15},{20,22},{21,23},{28,30},{29,31}} | collective-permute-start | bytes 442376 | tf_op jit(solution)/shard_map/ppermute | solution.py:40
  105.9 14.2 %collective-permute-start.33 = (bf16[192,384]{1,0:T(8,128)(2,1)S(1)}, bf16[192,384]{1,0:T(8,128)(2,1)S(1)}, u32[]{:S(2)}, u32[]{:S(2)}) collective-permute-start(bf16[192,384]{1,0:T(8,128)(2,1)S(1)} %collective-permute-done.27.refs_3_), channel_id=1, source_target_pairs={{4,6},{5,7},{12,14},{13,15},{20,22},{21,23},{28,30},{29,31}} | collective-permute-start | bytes 442376 | tf_op jit(solution)/shard_map/ppermute | solution.py:40
  107.5 98.1 %collective-permute-start.45 = (bf16[4,384,384]{2,1,0:T(8,128)(2,1)S(1)}, bf16[4,384,384]{2,1,0:T(8,128)(2,1)}, u32[]{:S(2)}, u32[]{:S(2)}) collective-permute-start(bf16[4,384,384]{2,1,0:T(8,128)(2,1)S(1)} %pad_maximum_fusion.refs_4_), channel_id=1, source_target_pairs={{0,8},{1,9},{2,10},{3,11},{4,12},{5,13},{6,14},{7,15},{8,0},{9,1},... | collective-permute-start | bytes 3538952 | tf_op jit(solution)/shard_map/ppermute | solution.py:40
  116.2 34.3 %collective-permute-start.34 = (bf16[192,384]{1,0:T(8,128)(2,1)S(1)}, bf16[192,384]{1,0:T(8,128)(2,1)S(1)}, u32[]{:S(2)}, u32[]{:S(2)}) collective-permute-start(bf16[192,384]{1,0:T(8,128)(2,1)S(1)} %collective-permute-done.28.refs_4_), channel_id=1, source_target_pairs={{4,6},{5,7},{12,14},{13,15},{20,22},{21,23},{28,30},{29,31}} | collective-permute-start | bytes 442376 | tf_op jit(solution)/shard_map/ppermute | solution.py:40
  117.5 39.6 %collective-permute-start.35 = (bf16[192,384]{1,0:T(8,128)(2,1)S(1)}, bf16[192,384]{1,0:T(8,128)(2,1)S(1)}, u32[]{:S(2)}, u32[]{:S(2)}) collective-permute-start(bf16[192,384]{1,0:T(8,128)(2,1)S(1)} %collective-permute-done.30.refs_6_), channel_id=1, source_target_pairs={{4,6},{5,7},{12,14},{13,15},{20,22},{21,23},{28,30},{29,31}} | collective-permute-start | bytes 442376 | tf_op jit(solution)/shard_map/ppermute | solution.py:40
  118.9 38.3 %collective-permute-start.36 = (bf16[192,384]{1,0:T(8,128)(2,1)S(1)}, bf16[192,384]{1,0:T(8,128)(2,1)S(1)}, u32[]{:S(2)}, u32[]{:S(2)}) collective-permute-start(bf16[192,384]{1,0:T(8,128)(2,1)S(1)} %collective-permute-done.31.refs_7_), channel_id=1, source_target_pairs={{4,6},{5,7},{12,14},{13,15},{20,22},{21,23},{28,30},{29,31}} | collective-permute-start | bytes 442376 | tf_op jit(solution)/shard_map/ppermute | solution.py:40
  120.2 36.9 %collective-permute-start.37 = (bf16[192,384]{1,0:T(8,128)(2,1)S(1)}, bf16[192,384]{1,0:T(8,128)(2,1)S(1)}, u32[]{:S(2)}, u32[]{:S(2)}) collective-permute-start(bf16[192,384]{1,0:T(8,128)(2,1)S(1)} %collective-permute-done.32.refs_8_), channel_id=1, source_target_pairs={{4,6},{5,7},{12,14},{13,15},{20,22},{21,23},{28,30},{29,31}} | collective-permute-start | bytes 442376 | tf_op jit(solution)/shard_map/ppermute | solution.py:40
  150.5 55.2 %collective-permute-start.23 = (bf16[6,192,384]{2,1,0:T(8,128)(2,1)}, bf16[6,192,384]{2,1,0:T(8,128)(2,1)}, u32[]{:S(2)}, u32[]{:S(2)}) collective-permute-start(bf16[6,192,384]{2,1,0:T(8,128)(2,1)} %collect_lower.2.refs_0_), channel_id=1, source_target_pairs={{0,8},{1,9},{2,10},{3,11},{4,12},{5,13},{6,14},{7,15},{8,0},{9,1},... | collective-permute-start | bytes 2654216 | tf_op jit(solution)/shard_map/ppermute | solution.py:40
  187.2 18.5 %collective-permute-start.41 = (bf16[6,192,384]{2,1,0:T(8,128)(2,1)}, bf16[6,192,384]{2,1,0:T(8,128)(2,1)}, u32[]{:S(2)}, u32[]{:S(2)}) collective-permute-start(bf16[6,192,384]{2,1,0:T(8,128)(2,1)} %collect_lower.3.refs_2_), channel_id=1, source_target_pairs={{0,8},{1,9},{2,10},{3,11},{4,12},{5,13},{6,14},{7,15},{8,0},{9,1},... | collective-permute-start | bytes 2654216 | tf_op jit(solution)/shard_map/ppermute | solution.py:40
  190.5 8.7 %collective-permute-start.47 = (bf16[384,384]{1,0:T(8,128)(2,1)S(1)}, bf16[384,384]{1,0:T(8,128)(2,1)S(1)}, u32[]{:S(2)}, u32[]{:S(2)}) collective-permute-start(bf16[384,384]{1,0:T(8,128)(2,1)S(1)} %bitcast.42), channel_id=1, source_target_pairs={{0,16},{1,17},{2,18},{3,19},{4,20},{5,21},{6,22},{7,23},{8,24},{9,... | collective-permute-start | bytes 884744 | tf_op jit(solution)/shard_map/ppermute | solution.py:40
  191.7 13.9 %collective-permute-start.48 = (bf16[384,384]{1,0:T(8,128)(2,1)S(1)}, bf16[384,384]{1,0:T(8,128)(2,1)S(1)}, u32[]{:S(2)}, u32[]{:S(2)}) collective-permute-start(bf16[384,384]{1,0:T(8,128)(2,1)S(1)} %bitcast.43), channel_id=1, source_target_pairs={{0,24},{1,25},{2,26},{3,27},{4,28},{5,29},{6,30},{7,31},{8,16},{9,... | collective-permute-start | bytes 884744 | tf_op jit(solution)/shard_map/ppermute | solution.py:40
  216.0 39.9 %collective-permute-start.49 = (bf16[384,384]{1,0:T(8,128)(2,1)}, bf16[384,384]{1,0:T(8,128)(2,1)S(1)}, u32[]{:S(2)}, u32[]{:S(2)}) collective-permute-start(bf16[384,384]{1,0:T(8,128)(2,1)} %get-tuple-element.23), channel_id=1, source_target_pairs={{0,8},{1,9},{2,10},{3,11},{4,12},{5,13},{6,14},{7,15},{8,0},{9,1},... | collective-permute-start | bytes 884744 | tf_op jit(solution)/shard_map/ppermute | solution.py:40
  216.3 39.6 %collective-permute-start.50 = (bf16[384,384]{1,0:T(8,128)(2,1)}, bf16[384,384]{1,0:T(8,128)(2,1)S(1)}, u32[]{:S(2)}, u32[]{:S(2)}) collective-permute-start(bf16[384,384]{1,0:T(8,128)(2,1)} %get-tuple-element.24), channel_id=1, source_target_pairs={{0,16},{1,17},{2,18},{3,19},{4,20},{5,21},{6,22},{7,23},{8,24},{9,... | collective-permute-start | bytes 884744 | tf_op jit(solution)/shard_map/ppermute | solution.py:40
  217.2 38.8 %collective-permute-start.51 = (bf16[384,384]{1,0:T(8,128)(2,1)}, bf16[384,384]{1,0:T(8,128)(2,1)S(1)}, u32[]{:S(2)}, u32[]{:S(2)}) collective-permute-start(bf16[384,384]{1,0:T(8,128)(2,1)} %get-tuple-element.25), channel_id=1, source_target_pairs={{0,24},{1,25},{2,26},{3,27},{4,28},{5,29},{6,30},{7,31},{8,16},{9,... | collective-permute-start | bytes 884744 | tf_op jit(solution)/shard_map/ppermute | solution.py:40
  (53 other events, 1235.6 us)

commit v2 on v1

v2 whole, which is shorter than its diff:
```python
import functools
import itertools
import math

import jax
import jax.numpy as jnp
from jax import lax
from jax.experimental import pallas as pl
from jax.experimental.pallas import tpu as pltpu
from jax.sharding import PartitionSpec as P

AXES = ("row", "col", "mom")
VMEM_BYTES = 56 * 1024 * 1024


class Plan:
    def __init__(self, mesh, moments, side):
        self.rows = mesh.shape["row"]
        self.cols = mesh.shape["col"]
        self.moms = mesh.shape["mom"]
        self.moments = moments
        self.side = side
        self.groups = self.rows // moments
        self.half = side // self.moms
        self.width = side // self.groups
        self.keys = [
            (b, j)
            for b in reversed(range(moments))
            for j in range(self.cols - 1)
            if (b + 1) * self.groups - 1 > j
        ]

    def send(self, value, target):
        pairs = []
        index = lambda r, c, m: (r * self.cols + c) * self.moms + m
        for place in itertools.product(range(self.rows), range(self.cols), range(self.moms)):
            goal = target(*place)
            if goal is not None:
                pairs.append((index(*place), index(*goal)))
        return lax.ppermute(value, AXES, pairs)

    def direct(self):
        last = self.cols - 1
        wanted = [
            (key, key[1], to)
            for key in self.keys
            for to in range(self.cols)
            if to != key[1] and (to < last or key[1] == last - 1)
        ]
        first = lambda send: (send[0][0] < self.moments - 1, send[2] != last - 1, abs(send[1] - send[2]))
        steps = []
        for key, source, to in sorted(wanted, key=first):
            for step in steps:
                if source not in step and to not in [goal for _, goal in step.values()]:
                    break
            else:
                step = {}
                steps.append(step)
            step[source] = (key, to)
        return steps


def hbm(count):
    return [pl.BlockSpec(memory_space=pl.ANY)] * count


def smem():
    return pl.BlockSpec(memory_space=pltpu.SMEM)


def run_copies(copies):
    for copy in copies:
        copy.start()
    for copy in copies:
        copy.wait()


def sigma_kernel(plan, pair_count, extra, place, triples, *refs):
    moms, moments, groups = plan.moms, plan.moments, plan.groups
    half, side = plan.half, plan.side
    lesser_in, partner_in = refs[:moms], refs[moms : 2 * moms]
    outs = refs[2 * moms + extra : 2 * moms + extra + moms * moments]
    lesser, partner, sems = refs[2 * moms + extra + moms * moments :]
    x, y = place[0] // groups, place[2]
    copies = []
    for which, (sources, target) in enumerate(((lesser_in, lesser), (partner_in, partner))):
        for q in range(moms):
            source = sources[q]
            if q == 0:
                source = source.at[:, :, pl.ds(pl.multiple_of(y * half, half), half), :]
            copies.append(
                pltpu.make_async_copy(
                    source, target.at[pl.ds((y ^ q) * moments, moments)], sems.at[which * moms + q]
                )
            )
    run_copies(copies)
    scale = 1.0 / pair_count
    lanes = 128 if side % 128 == 0 else side
    for q in reversed(range(moms)):
        for b in range(moments):
            moment = (y ^ q) * moments + (x ^ b)
            table = [[triples[moment, m, n] for n in range(3)] for m in range(pair_count)]
            out = outs[q * moments + b]

            def block(index, _, table=table, out=out):
                row = pl.multiple_of(index * 16, 16)
                for lane in range(0, side, lanes):
                    at = (pl.ds(row, 16), pl.ds(lane, lanes))
                    total_re = total_im = None
                    for a, b, c in table:
                        a_re, a_im = lesser[(a, 0) + at], lesser[(a, 1) + at]
                        b_re, b_im = lesser[(b, 0) + at], lesser[(b, 1) + at]
                        c_re, c_im = partner[(c, 0) + at], partner[(c, 1) + at]
                        p_re = a_re * b_re - a_im * b_im
                        p_im = a_re * b_im + a_im * b_re
                        f_re = (p_re * c_re - p_im * c_im).astype(jnp.float32)
                        f_im = (p_re * c_im + p_im * c_re).astype(jnp.float32)
                        total_re = f_re if total_re is None else total_re + f_re
                        total_im = f_im if total_im is None else total_im + f_im
                    out[(0,) + at] = (total_re * scale).astype(jnp.bfloat16)
                    out[(1,) + at] = (total_im * scale).astype(jnp.bfloat16)
                return 0

            lax.fori_loop(0, half // 16, block, 0)


def gather_kernel(plan, sources, place, *refs):
    ins, out, sems = refs[:-2], refs[-2], refs[-1]
    for col in range(plan.cols):

        @pl.when(place[1] == col)
        def _(col=col):
            run_copies(
                [
                    pltpu.make_async_copy(ins[index], out.at[k], sems.at[k])
                    for k, index in enumerate(sources[col])
                ]
            )


def place_kernel(plan, place, *refs):
    ins, out, sems = refs[:-2], refs[-2], refs[-1]
    x, y = place[0] // plan.groups, place[2]
    copies = []
    for q in range(plan.moms):
        rows = pl.ds(pl.multiple_of((y ^ q) * plan.half, plan.half), plan.half)
        for b in range(plan.moments):
            index = q * plan.moments + b
            copies.append(pltpu.make_async_copy(ins[index], out.at[x ^ b, :, rows, :], sems.at[index]))
    run_copies(copies)


def solve_kernel(plan, place, *refs):
    rows, moms, groups, side = plan.rows, plan.moms, plan.groups, plan.side
    moments, half, width = plan.moments, plan.half, plan.width
    refs = list(refs)
    take = lambda count: [refs.pop(0) for _ in range(count)]
    sig_in, diag_in, right_in = take(moms * groups), take(moments * groups), take(rows)
    outs = take(rows)
    sig, diag, right, solved, sems = refs
    r, y = place[0], place[2]
    count = [0]

    def copy(source, target):
        made = pltpu.make_async_copy(source, target, sems.at[count[0]])
        count[0] += 1
        made.start()
        return made

    stages = [[] for _ in range(moments)]
    for s in range(rows):
        stages[0].append(copy(right_in[s], right.at[r ^ s]))
    for b in range(moments):
        for t in range(groups):
            for p in range(2):
                stages[0].append(
                    copy(
                        diag_in[b * groups + t].at[p],
                        diag.at[r ^ (b * groups) ^ t, :, pl.ds(p * side, side)],
                    )
                )
    for k, (b, j) in reversed(list(enumerate(plan.keys))):
        for t in range(groups):
            tile_row = b * groups + ((r % groups) ^ t)
            for q in range(moms):
                at = pl.ds(pl.multiple_of((y ^ q) * half, half), half)
                for p in range(2):
                    stages[b].append(
                        copy(
                            sig_in[q * groups + t].at[k, p],
                            sig.at[tile_row, at, pl.ds((2 * j + p) * side, side)],
                        )
                    )

    weight = 1.0 / math.sqrt(side * rows)

    def turn(value):
        return jnp.concatenate([-value[:, width:], value[:, :width]], axis=1)

    for row in range(rows):
        if row % groups == 0:
            for made in stages[row // groups]:
                made.wait()
        pending = right[row].astype(jnp.float32)
        if row > 0:
            depth = 2 * side * row
            pending = pending + weight * jnp.dot(
                sig[row, :, :depth], solved[:depth, :], preferred_element_type=jnp.float32
            )
        both = jnp.concatenate([pending, turn(pending)], axis=0).astype(jnp.bfloat16)
        value = jnp.dot(diag[row], both, preferred_element_type=jnp.float32)
        solved[pl.ds(2 * row * side, side), :] = value.astype(jnp.bfloat16)
        solved[pl.ds((2 * row + 1) * side, side), :] = turn(value).astype(jnp.bfloat16)
    copies = []
    for s in range(rows):
        at = pl.ds(pl.multiple_of(2 * (r ^ s) * side, side), side)
        copies.append(pltpu.make_async_copy(solved.at[at, :], outs[s], sems.at[s]))
    run_copies(copies)


def on_device(mesh, lesser, greater, triples, diag_inverse, right_side):
    moments, _, side, _ = lesser.shape
    plan = Plan(mesh, moments, side)
    rows, cols, moms, groups = plan.rows, plan.cols, plan.moms, plan.groups
    half, width = plan.half, plan.width
    pair_count = triples.shape[1]
    r, z, y = (lax.axis_index(axis) for axis in AXES)
    x = r // groups
    place = jnp.stack([r, z, y]).astype(jnp.int32)
    bf16 = jnp.bfloat16
    params = pltpu.CompilerParams(vmem_limit_bytes=VMEM_BYTES)
    dma = lambda count: pltpu.SemaphoreType.DMA((count,))

    def exchange_mom(value, q):
        return plan.send(value, lambda a, b, c: (a, b, c ^ q))

    def exchange_row(value, s):
        return plan.send(value, lambda a, b, c: (a ^ s, b, c))

    def half_of(value, q):
        return lax.dynamic_slice_in_dim(value, (y ^ q) * half, half, 2)

    lesser_all = [lesser] + [exchange_mom(half_of(lesser, q), q) for q in range(1, moms)]
    partner = jnp.swapaxes(greater, 2, 3)
    partner_all = [partner] + [exchange_mom(half_of(partner, q), q) for q in range(1, moms)]

    diag_all = [lax.dynamic_index_in_dim(diag_inverse, x ^ b, 0, keepdims=False) for b in range(moments)]
    diag_all = diag_all[:1] + [exchange_row(diag_all[b], b * groups) for b in range(1, moments)]

    right = right_side.reshape(moments, side, 2, groups, width).transpose(0, 3, 1, 2, 4)
    right = right.reshape(rows, side, 2 * width)
    right_all = [lax.dynamic_index_in_dim(right, r ^ s, 0, keepdims=False) for s in range(rows)]
    right_all = right_all[:1] + [exchange_row(right_all[s], s) for s in range(1, rows)]

    early = diag_all + right_all
    slots = pl.pallas_call(
        functools.partial(sigma_kernel, plan, pair_count, len(early)),
        out_shape=[jax.ShapeDtypeStruct((2, half, side), bf16)] * (moms * moments),
        in_specs=[smem(), smem()] + hbm(2 * moms + len(early)),
        scratch_shapes=[
            pltpu.VMEM((moms * moments, 2, half, side), bf16),
            pltpu.VMEM((moms * moments, 2, half, side), bf16),
            dma(2 * moms),
        ],
        compiler_params=params,
        name="self_energy",
    )(place, triples, *lesser_all, *partner_all, *early)

    diag_all = [
        value if t == 0 else exchange_row(value, t) for value in diag_all for t in range(groups)
    ]
    chunks = [slots[:moments]]
    for q in range(1, moms):
        chunks.append([exchange_mom(slot, q) for slot in slots[q * moments : (q + 1) * moments]])

    sigma = pl.pallas_call(
        functools.partial(place_kernel, plan),
        out_shape=jax.ShapeDtypeStruct(lesser.shape, bf16),
        in_specs=[smem()] + hbm(moms * moments),
        scratch_shapes=[dma(moms * moments)],
        compiler_params=params,
        name="place_sigma",
    )(place, *[slot for chunk in chunks for slot in chunk])

    def spread(chunk):
        came = [chunk[0]] + [
            plan.send(chunk[b], lambda a, c, m: (a ^ (b * groups), c, m) if a > c else None)
            for b in range(1, moments)
        ]
        own = [lax.select_n(x ^ b, *came) for b in range(moments)]
        buffers, found = list(own), {}
        for b, j in plan.keys:
            found[(b, j, j)] = b
        last = cols - 1

        def valid(key, a):
            return key[0] * groups + a % groups > key[1]

        for step in plan.direct():
            blocks = sorted({key[0] for key, _ in step.values()})
            value = own[blocks[0]]
            for b in blocks[1:]:
                for source, (key, _) in step.items():
                    if key[0] == b:
                        value = jnp.where(z == source, own[b], value)
            goal = lambda a, c, m: (
                (a, step[c][1], m) if c in step and valid(step[c][0], a) else None
            )
            for key, to in step.values():
                found[key + (to,)] = len(buffers)
            buffers.append(plan.send(value, goal))
        for key in sorted(plan.keys, key=lambda key: found.get(key + (last - 1,), 0)):
            if key[1] < last - 1:
                value = buffers[found[key + (last - 1,)]]
                goal = lambda a, c, m: (a, last, m) if c == last - 1 and valid(key, a) else None
                found[key + (last,)] = len(buffers)
                buffers.append(plan.send(value, goal))
        sources = [[found[key + (c,)] for key in plan.keys] for c in range(cols)]
        lower = pl.pallas_call(
            functools.partial(gather_kernel, plan, sources),
            out_shape=jax.ShapeDtypeStruct((len(plan.keys), 2, half, side), bf16),
            in_specs=[smem()] + hbm(len(buffers)),
            scratch_shapes=[dma(len(plan.keys))],
            compiler_params=params,
            name="collect_lower",
        )(place, *buffers)
        return [lower] + [exchange_row(lower, t) for t in range(1, groups)]

    sigma_all = [part_of for chunk in chunks for part_of in spread(chunk)]

    solved = pl.pallas_call(
        functools.partial(solve_kernel, plan),
        out_shape=[jax.ShapeDtypeStruct((side, 2 * width), bf16)] * rows,
        in_specs=[smem()] + hbm(moms * groups + rows + rows),
        out_specs=hbm(rows),
        scratch_shapes=[
            pltpu.VMEM((rows, side, 2 * side * (cols - 1)), bf16),
            pltpu.VMEM((rows, side, 2 * side), bf16),
            pltpu.VMEM((rows, side, 2 * width), bf16),
            pltpu.VMEM((rows * 2 * side, 2 * width), bf16),
            dma(rows + 2 * rows + len(plan.keys) * groups * moms * 2),
        ],
        compiler_params=params,
        name="substitution",
    )(place, *sigma_all, *diag_all, *right_all)

    back = [solved[0]] + [exchange_row(solved[s], s) for s in range(1, rows)]
    pieces = jnp.stack([lax.select_n(r ^ s, *back) for s in range(rows)])
    pieces = pieces.reshape(moments, groups, side, 2, width).transpose(0, 2, 3, 1, 4)
    return sigma, pieces.reshape(moments, side, 2, side)


def solution(mesh):
    placed = (
        P("mom", None, "row", "col"),
        P("mom", None, "col", "row"),
        P(),
        P("mom", None, "row", None),
        P("mom", "row", None, "col"),
    )
    return jax.shard_map(
        functools.partial(on_device, mesh),
        mesh=mesh,
        in_specs=placed,
        out_specs=(P("mom", None, "row", "col"), P("mom", "row", None, "col")),
        check_vma=False,
    )
```

time: 263 us -> 157 us (0.60)
  Pallas kernels: 116 us -> 28.1 us
  starting transfers between devices: 60.8 us -> 27 us
  waiting for transfers between devices: 63.9 us -> 76 us
  local copies, waits for them, and re-layouts: 14.9 us -> 21.5 us
    pallas_call x2, Pallas kernels: 57.3 us -> 5.98 us  [spread(): pl.pallas_call(functools.partial(gather_kernel, plan, sources), out_shape...]
    pallas_call x1, Pallas kernels: 37.7 us -> 3.08 us  [on_device(): pl.pallas_call(functools.partial(place_kernel, plan), out_shape=jax.Shape...]
    ppermute x52 -> x31, starting transfers between devices: 60.8 us -> 27 us  [send(): return lax.ppermute(value, AXES, pairs)]
    ppermute x52 -> x31, waiting for transfers between devices: 63.9 us -> 76 us  [send(): return lax.ppermute(value, AXES, pairs)]
    dynamic_slice x5, local copies, waits for them, and re-layouts: 1.68 us -> 5.08 us  [on_device(): lax.dynamic_index_in_dim(right, r ^ s, 0, keepdims=False)]
    unnamed x102 -> x78, local copies, waits for them, and re-layouts: 10.3 us -> 12.5 us
  transfers between devices with their start and end apart: 52 -> 31, of which waited for: 11 -> 17; matrix products, arithmetic and copies ran while one was open for 3% -> 6% of each run, Pallas kernels for 41% -> 6%
where the time goes in v2:
time: 157 us; the launch traced here: 156 us
  waiting for transfers between devices  76 us (48%)
  Pallas kernels  28.1 us (18%)
  starting transfers between devices  27 us (17%)
  local copies, waits for them, and re-layouts  21.5 us (14%)
  other arithmetic  2.17 us (1%)
    ppermute x31, waiting for transfers between devices, send(): return lax.ppermute(value, AXES, pairs)  76 us
    ppermute x31, starting transfers between devices, send(): return lax.ppermute(value, AXES, pairs)  27 us
    unnamed x78, local copies, waits for them, and re-layouts  12.5 us
    pallas_call x1, Pallas kernels, on_device(): pl.pallas_call(functools.partial(sigma_kernel, plan, pair_count, len(earl...  10.6 us
    pallas_call x1, Pallas kernels, on_device(): pl.pallas_call(functools.partial(solve_kernel, plan), out_shape=[jax.Shap...  8.49 us
    pallas_call x2, Pallas kernels, spread(): pl.pallas_call(functools.partial(gather_kernel, plan, sources), out_shape...  5.98 us
    dynamic_slice x5, local copies, waits for them, and re-layouts, on_device(): lax.dynamic_index_in_dim(right, r ^ s, 0, keepdims=False)  5.08 us
  transfers between devices with their start and end apart: 31, of which 17 were waited for; matrix products, arithmetic and copies ran while one was open for 6% of the time, Pallas kernels for 6%

profile of v2, /device:TPU:25, one launch (start us, length us, event | category | flops | bytes accessed | tf_op | source)
XLA Modules:
  0.0 156.1 jit_solution(14602612340995638011)
XLA Ops:
  0.6 3.6 %copy.14 = bf16[2,384,2,384]{1,3,2,0:T(8,128)(2,1)S(1)} copy(bf16[2,384,2,384]{3,2,1,0:T(2,128)(2,1)} %param.9) | data formatting | bytes 2359296 | tf_op args[4]
  4.4 0.9 constant_dynamic-slice_fusion
  5.3 0.9 copy.17
  6.9 1.1 dynamic-slice_bitcast_fusion
  8.1 1.2 collective-permute-start.2
  10.1 0.9 dynamic-slice_bitcast_fusion.2
  11.0 1.2 collective-permute-start.1
  12.2 0.9 constant_dynamic-slice_fusion.4
  13.1 1.0 collective-permute-start
  14.1 1.2 copy.18
  15.9 1.2 copy.19
  17.1 1.7 %collective-permute-start.5 = (bf16[384,384]{1,0:T(8,128)(2,1)S(1)}, bf16[384,384]{1,0:T(8,128)(2,1)S(1)}, u32[]{:S(2)}, u32[]{:S(2)}) collective-permute-start(bf16[384,384]{1,0:T(8,128)(2,1)S(1)} %bitcast.38), channel_id=1, source_target_pairs={{0,24},{1,25},{2,26},{3,27},{4,28},{5,29},{6,30},{7,31},{8,16},{9,... | collective-permute-start | bytes 884744 | tf_op jit(solution)/shard_map/ppermute | solution.py:40
  18.8 0.9 copy.16
  21.0 8.5 %collective-permute-done.4.refs_8_.refs_10_ = bf16[384,384]{1,0:T(8,128)(2,1)S(1)} collective-permute-done((bf16[384,384]{1,0:T(8,128)(2,1)S(1)}, bf16[384,384]{1,0:T(8,128)(2,1)S(1)}, u32[]{:S(2)}, u32[]{:S(2)}) %collective-permute-start.4) | collective-permute-done | bytes 294944 | tf_op jit(solution)/shard_map/ppermute | solution.py:40
  29.5 6.7 %collective-permute-done.5.refs_9_.refs_11_ = bf16[384,384]{1,0:T(8,128)(2,1)S(1)} collective-permute-done((bf16[384,384]{1,0:T(8,128)(2,1)S(1)}, bf16[384,384]{1,0:T(8,128)(2,1)S(1)}, u32[]{:S(2)}, u32[]{:S(2)}) %collective-permute-start.5) | collective-permute-done | bytes 294944 | tf_op jit(solution)/shard_map/ppermute | solution.py:40
  36.3 2.2 %collective-permute-done.refs_1_ = bf16[2,2,192,384]{3,2,1,0:T(8,128)(2,1)S(1)} collective-permute-done((bf16[2,2,192,384]{3,2,1,0:T(8,128)(2,1)}, bf16[2,2,192,384]{3,2,1,0:T(8,128)(2,1)S(1)}, u32[]{:S(2)}, u32[]{:S(2)}) %collective-permute-start) | collective-permute-done | bytes 589856 | tf_op jit(solution)/shard_map/ppermute | solution.py:40
  39.3 10.6 %self_energy.1 = (bf16[2,192,384]{2,1,0:T(8,128)(2,1)}, bf16[2,192,384]{2,1,0:T(8,128)(2,1)}, bf16[2,192,384]{2,1,0:T(8,128)(2,1)}, bf16[2,192,384]{2,1,0:T(8,128)(2,1)}) custom-call(s32[3]{0:T(128)} %pad_add_fusion.place, s32[4,8,3]{2,1,0:T(8,128)} %copy.20.triples, bf16[2,2,384,384]{3,2,1,0:T(8,128)(2,1)} %refs_0_.1, bf16[2,2,192,384]{3,2,1,0:T(8,128)(2,1)} %copy-done.17, ...), custom_call_target="tpu_custom_call" | custom-call | tf_op jit(solution)/shard_map/self_energy/pallas_call | solution.py:256
  49.8 1.3 collective-permute-start.7
  52.1 5.4 %collective-permute-done.7.refs_3_ = bf16[2,192,384]{2,1,0:T(8,128)(2,1)S(1)} collective-permute-done((bf16[2,192,384]{2,1,0:T(8,128)(2,1)}, bf16[2,192,384]{2,1,0:T(8,128)(2,1)S(1)}, u32[]{:S(2)}, u32[]{:S(2)}) %collective-permute-start.7) | collective-permute-done | bytes 294944 | tf_op jit(solution)/shard_map/ppermute | solution.py:40
  58.2 1.0 broadcast_select_fusion.1
  59.3 1.3 collective-permute-start.9
  61.9 1.9 %collective-permute-done.6.refs_2_ = bf16[2,192,384]{2,1,0:T(8,128)(2,1)S(1)} collective-permute-done((bf16[2,192,384]{2,1,0:T(8,128)(2,1)}, bf16[2,192,384]{2,1,0:T(8,128)(2,1)S(1)}, u32[]{:S(2)}, u32[]{:S(2)}) %collective-permute-start.6) | collective-permute-done | bytes 294944 | tf_op jit(solution)/shard_map/ppermute | solution.py:40
  64.6 1.3 collective-permute-start.18
  65.9 0.8 collective-permute-done.9.refs_2_
  68.1 1.3 collective-permute-start.13
  69.5 1.3 collective-permute-start.14
  70.8 4.9 %collective-permute-done.18.refs_2_ = bf16[2,192,384]{2,1,0:T(8,128)(2,1)S(1)} collective-permute-done((bf16[2,192,384]{2,1,0:T(8,128)(2,1)S(1)}, bf16[2,192,384]{2,1,0:T(8,128)(2,1)S(1)}, u32[]{:S(2)}, u32[]{:S(2)}) %collective-permute-start.18) | collective-permute-done | bytes 294944 | tf_op jit(solution)/shard_map/ppermute | solution.py:40
  76.4 1.3 collective-permute-start.15
  77.7 1.3 collective-permute-start.22
  79.0 10.5 %collective-permute-done.13.refs_6_ = bf16[2,192,384]{2,1,0:T(8,128)(2,1)S(1)} collective-permute-done((bf16[2,192,384]{2,1,0:T(8,128)(2,1)S(1)}, bf16[2,192,384]{2,1,0:T(8,128)(2,1)S(1)}, u32[]{:S(2)}, u32[]{:S(2)}) %collective-permute-start.13) | collective-permute-done | bytes 294944 | tf_op jit(solution)/shard_map/ppermute | solution.py:40
  89.5 1.3 collective-permute-start.23
  90.8 5.0 %collective-permute-done.14.refs_7_ = bf16[2,192,384]{2,1,0:T(8,128)(2,1)S(1)} collective-permute-done((bf16[2,192,384]{2,1,0:T(8,128)(2,1)S(1)}, bf16[2,192,384]{2,1,0:T(8,128)(2,1)S(1)}, u32[]{:S(2)}, u32[]{:S(2)}) %collective-permute-start.14) | collective-permute-done | bytes 294944 | tf_op jit(solution)/shard_map/ppermute | solution.py:40
  95.9 1.3 collective-permute-start.24
  97.1 9.2 %collective-permute-done.15.refs_8_ = bf16[2,192,384]{2,1,0:T(8,128)(2,1)S(1)} collective-permute-done((bf16[2,192,384]{2,1,0:T(8,128)(2,1)S(1)}, bf16[2,192,384]{2,1,0:T(8,128)(2,1)S(1)}, u32[]{:S(2)}, u32[]{:S(2)}) %collective-permute-start.15) | collective-permute-done | bytes 294944 | tf_op jit(solution)/shard_map/ppermute | solution.py:40
  107.1 3.0 %collect_lower.2.refs_0_ = bf16[4,2,192,384]{3,2,1,0:T(8,128)(2,1)} custom-call(s32[3]{0:T(128)} %pad_add_fusion.place, bf16[2,192,384]{2,1,0:T(8,128)(2,1)} %copy-done.10, bf16[2,192,384]{2,1,0:T(8,128)(2,1)} %copy-done.9, bf16[2,192,384]{2,1,0:T(8,128)(2,1)} %copy-done.21, bf16[2,192,384]{2,1,0:T(8,128)(2,1)} %copy-done.22, ...), custom_call_target="tpu_custom_call" | custom-call | tf_op jit(solution)/shard_map/collect_lower/pallas_call | solution.py:319
  110.5 3.2 %collective-permute-done.23.refs_7_ = bf16[2,192,384]{2,1,0:T(8,128)(2,1)S(1)} collective-permute-done((bf16[2,192,384]{2,1,0:T(8,128)(2,1)S(1)}, bf16[2,192,384]{2,1,0:T(8,128)(2,1)S(1)}, u32[]{:S(2)}, u32[]{:S(2)}) %collective-permute-start.23) | collective-permute-done | bytes 294944 | tf_op jit(solution)/shard_map/ppermute | solution.py:40
  113.6 3.2 %collective-permute-done.24.refs_8_ = bf16[2,192,384]{2,1,0:T(8,128)(2,1)S(1)} collective-permute-done((bf16[2,192,384]{2,1,0:T(8,128)(2,1)S(1)}, bf16[2,192,384]{2,1,0:T(8,128)(2,1)S(1)}, u32[]{:S(2)}, u32[]{:S(2)}) %collective-permute-start.24) | collective-permute-done | bytes 294944 | tf_op jit(solution)/shard_map/ppermute | solution.py:40
  117.5 3.0 %collect_lower.3.refs_2_ = bf16[4,2,192,384]{3,2,1,0:T(8,128)(2,1)} custom-call(s32[3]{0:T(128)} %pad_add_fusion.place, bf16[2,192,384]{2,1,0:T(8,128)(2,1)} %copy-done.12, bf16[2,192,384]{2,1,0:T(8,128)(2,1)} %copy-done.11, bf16[2,192,384]{2,1,0:T(8,128)(2,1)} %copy-done.24, bf16[2,192,384]{2,1,0:T(8,128)(2,1)} %copy-done.25, ...), custom_call_target="tpu_custom_call" | custom-call | tf_op jit(solution)/shard_map/collect_lower/pallas_call | solution.py:319
  121.2 3.1 %collective-permute-done.26.refs_5_ = bf16[2,384,384]{2,1,0:T(8,128)(2,1)S(1)} collective-permute-done((bf16[2,384,384]{2,1,0:T(8,128)(2,1)S(1)}, bf16[2,384,384]{2,1,0:T(8,128)(2,1)S(1)}, u32[]{:S(2)}, u32[]{:S(2)}) %collective-permute-start.26) | collective-permute-done | bytes 589856 | tf_op jit(solution)/shard_map/ppermute | solution.py:40
  124.3 0.8 collective-permute-done.27.refs_7_
  125.2 0.8 copy-done.19
  126.3 1.0 copy-done.16
  127.4 8.5 %substitution.1 = (bf16[384,384]{1,0:T(8,128)(2,1)}, bf16[384,384]{1,0:T(8,128)(2,1)}, bf16[384,384]{1,0:T(8,128)(2,1)}, bf16[384,384]{1,0:T(8,128)(2,1)}) custom-call(s32[3]{0:T(128)} %pad_add_fusion.place, bf16[4,2,192,384]{3,2,1,0:T(8,128)(2,1)} %collect_lower.2.refs_0_, bf16[4,2,192,384]{3,2,1,0:T(8,128)(2,1)} %copy-done.15, ...), custom_call_target="tpu_custom_call" | custom-call | tf_op jit(solution)/shard_map/substitution/pallas_call | solution.py:331
  136.1 2.0 %collective-permute-start.29 = (bf16[384,384]{1,0:T(8,128)(2,1)}, bf16[384,384]{1,0:T(8,128)(2,1)S(1)}, u32[]{:S(2)}, u32[]{:S(2)}) collective-permute-start(bf16[384,384]{1,0:T(8,128)(2,1)} %get-tuple-element.16), channel_id=1, source_target_pairs={{0,16},{1,17},{2,18},{3,19},{4,20},{5,21},{6,22},{7,23},{8,24},{9,... | collective-permute-start | bytes 884744 | tf_op jit(solution)/shard_map/ppermute | solution.py:40
  138.4 3.1 %place_sigma.1 = bf16[2,2,384,384]{3,2,1,0:T(8,128)(2,1)} custom-call(s32[3]{0:T(128)} %pad_add_fusion.place, bf16[2,192,384]{2,1,0:T(8,128)(2,1)} %get-tuple-element.10.refs_0_, bf16[2,192,384]{2,1,0:T(8,128)(2,1)} %get-tuple-element.11.refs_1_, bf16[2,192,384]{2,1,0:T(8,128)(2,1)} %copy-done.8, bf16[2,192,384]{2,1,0:T(8,128)(2,1)} %copy-done.20), custom_call_target="tpu_custom_call" | custom-call | tf_op jit(solution)/shard_map/place_sigma/pallas_call | solution.py:276
  141.5 3.9 %collective-permute-done.29 = bf16[384,384]{1,0:T(8,128)(2,1)S(1)} collective-permute-done((bf16[384,384]{1,0:T(8,128)(2,1)}, bf16[384,384]{1,0:T(8,128)(2,1)S(1)}, u32[]{:S(2)}, u32[]{:S(2)}) %collective-permute-start.29) | collective-permute-done | bytes 294944 | tf_op jit(solution)/shard_map/ppermute | solution.py:40
  145.4 6.5 %collective-permute-done.30 = bf16[384,384]{1,0:T(8,128)(2,1)S(1)} collective-permute-done((bf16[384,384]{1,0:T(8,128)(2,1)}, bf16[384,384]{1,0:T(8,128)(2,1)S(1)}, u32[]{:S(2)}, u32[]{:S(2)}) %collective-permute-start.30) | collective-permute-done | bytes 294944 | tf_op jit(solution)/shard_map/ppermute | solution.py:40
  153.2 2.8 %copy.23 = bf16[2,384,2,384]{3,2,1,0:T(2,128)(2,1)} copy(bf16[2,384,2,384]{1,3,2,0:T(8,128)(2,1)S(1)} %bitcast.32) | data formatting | bytes 2359296
  (113 shorter events, 14.8 us)
Async XLA Ops:
  6.2 10.8 %collective-permute-start.3 = (bf16[384,384]{1,0:T(8,128)(2,1)}, bf16[384,384]{1,0:T(8,128)(2,1)S(1)}, u32[]{:S(2)}, u32[]{:S(2)}) collective-permute-start(bf16[384,384]{1,0:T(8,128)(2,1)} %bitcast.11), channel_id=1, source_target_pairs={{0,8},{1,9},{2,10},{3,11},{4,12},{5,13},{6,14},{7,15},{8,0},{9,1},... | collective-permute-start | bytes 884744 | tf_op jit(solution)/shard_map/ppermute | solution.py:40
  8.1 28.2 %collective-permute-start.2 = (bf16[2,384,384]{2,1,0:T(8,128)(2,1)}, bf16[2,384,384]{2,1,0:T(8,128)(2,1)S(1)}, u32[]{:S(2)}, u32[]{:S(2)}) collective-permute-start(bf16[2,384,384]{2,1,0:T(8,128)(2,1)} %get-tuple-element.34), channel_id=1, source_target_pairs={{0,16},{1,17},{2,18},{3,19},{4,20},{5,21},{6,22},{7,23},{8,24},{9,... | collective-permute-start | bytes 1769480 | tf_op jit(solution)/shard_map/ppermute | solution.py:40
  11.0 25.3 %collective-permute-start.1 = (bf16[2,2,192,384]{3,2,1,0:T(8,128)(2,1)}, bf16[2,2,192,384]{3,2,1,0:T(8,128)(2,1)}, u32[]{:S(2)}, u32[]{:S(2)}) collective-permute-start(bf16[2,2,192,384]{3,2,1,0:T(8,128)(2,1)} %dynamic-slice_bitcast_fusion.2), channel_id=1, source_target_pairs={{0,1},{1,0},{2,3},{3,2},{4,5},{5,4},{6,7},{7,6},{8,9},{9,8},{10,11... | collective-permute-start | bytes 1769480 | tf_op jit(solution)/shard_map/ppermute | solution.py:40
  13.1 25.4 %collective-permute-start = (bf16[2,2,192,384]{3,2,1,0:T(8,128)(2,1)}, bf16[2,2,192,384]{3,2,1,0:T(8,128)(2,1)S(1)}, u32[]{:S(2)}, u32[]{:S(2)}) collective-permute-start(bf16[2,2,192,384]{3,2,1,0:T(8,128)(2,1)} %constant_dynamic-slice_fusion.4), channel_id=1, source_target_pairs={{0,1},{1,0},{2,3},{3,2},{4,5},{5,4},{6,7},{7,6},{8,9},{9,8},{10,11... | collective-permute-start | bytes 1769480 | tf_op jit(solution)/shard_map/ppermute | solution.py:40
  15.3 14.3 %collective-permute-start.4 = (bf16[384,384]{1,0:T(8,128)(2,1)S(1)}, bf16[384,384]{1,0:T(8,128)(2,1)S(1)}, u32[]{:S(2)}, u32[]{:S(2)}) collective-permute-start(bf16[384,384]{1,0:T(8,128)(2,1)S(1)} %bitcast.37), channel_id=1, source_target_pairs={{0,16},{1,17},{2,18},{3,19},{4,20},{5,21},{6,22},{7,23},{8,24},{9,... | collective-permute-start | bytes 884744 | tf_op jit(solution)/shard_map/ppermute | solution.py:40
  17.1 21.4 %copy-start.5 = (bf16[384,384]{1,0:T(8,128)(2,1)}, bf16[384,384]{1,0:T(8,128)(2,1)S(1)}, u32[]{:S(2)}) copy-start(bf16[384,384]{1,0:T(8,128)(2,1)S(1)} %collective-permute-done.3.refs_7_.refs_9_) | copy-start | bytes 884740
  17.1 19.2 %collective-permute-start.5 = (bf16[384,384]{1,0:T(8,128)(2,1)S(1)}, bf16[384,384]{1,0:T(8,128)(2,1)S(1)}, u32[]{:S(2)}, u32[]{:S(2)}) collective-permute-start(bf16[384,384]{1,0:T(8,128)(2,1)S(1)} %bitcast.38), channel_id=1, source_target_pairs={{0,24},{1,25},{2,26},{3,27},{4,28},{5,29},{6,30},{7,31},{8,16},{9,... | collective-permute-start | bytes 884744 | tf_op jit(solution)/shard_map/ppermute | solution.py:40
  49.8 7.7 %collective-permute-start.7 = (bf16[2,192,384]{2,1,0:T(8,128)(2,1)}, bf16[2,192,384]{2,1,0:T(8,128)(2,1)S(1)}, u32[]{:S(2)}, u32[]{:S(2)}) collective-permute-start(bf16[2,192,384]{2,1,0:T(8,128)(2,1)} %get-tuple-element.13), channel_id=1, source_target_pairs={{0,1},{1,0},{2,3},{3,2},{4,5},{5,4},{6,7},{7,6},{8,9},{9,8},{10,11... | collective-permute-start | bytes 884744 | tf_op jit(solution)/shard_map/ppermute | solution.py:40
  51.1 7.1 %collective-permute-start.8 = (bf16[2,192,384]{2,1,0:T(8,128)(2,1)}, bf16[2,192,384]{2,1,0:T(8,128)(2,1)S(1)}, u32[]{:S(2)}, u32[]{:S(2)}) collective-permute-start(bf16[2,192,384]{2,1,0:T(8,128)(2,1)} %get-tuple-element.11.refs_1_), channel_id=1, source_target_pairs={{8,24},{9,25},{16,0},{17,1},{18,2},{19,3},{24,8},{25,9},{26,10},{2... | collective-permute-start | bytes 884744 | tf_op jit(solution)/shard_map/ppermute | solution.py:40
  51.8 12.0 %collective-permute-start.6 = (bf16[2,192,384]{2,1,0:T(8,128)(2,1)}, bf16[2,192,384]{2,1,0:T(8,128)(2,1)S(1)}, u32[]{:S(2)}, u32[]{:S(2)}) collective-permute-start(bf16[2,192,384]{2,1,0:T(8,128)(2,1)} %get-tuple-element.12), channel_id=1, source_target_pairs={{0,1},{1,0},{2,3},{3,2},{4,5},{5,4},{6,7},{7,6},{8,9},{9,8},{10,11... | collective-permute-start | bytes 884744 | tf_op jit(solution)/shard_map/ppermute | solution.py:40
  57.5 7.0 %collective-permute-start.17 = (bf16[2,192,384]{2,1,0:T(8,128)(2,1)S(1)}, bf16[2,192,384]{2,1,0:T(8,128)(2,1)S(1)}, u32[]{:S(2)}, u32[]{:S(2)}) collective-permute-start(bf16[2,192,384]{2,1,0:T(8,128)(2,1)S(1)} %collective-permute-done.7.refs_3_), channel_id=1, source_target_pairs={{8,24},{9,25},{16,0},{17,1},{18,2},{19,3},{24,8},{25,9},{26,10},{2... | collective-permute-start | bytes 884744 | tf_op jit(solution)/shard_map/ppermute | solution.py:40
  59.2 47.1 %copy-start.9 = (bf16[2,192,384]{2,1,0:T(8,128)(2,1)}, bf16[2,192,384]{2,1,0:T(8,128)(2,1)S(1)}, u32[]{:S(2)}) copy-start(bf16[2,192,384]{2,1,0:T(8,128)(2,1)S(1)} %get-tuple-element.24.refs_1_) | copy-start | bytes 884740
  59.3 47.1 %copy-start.10 = (bf16[2,192,384]{2,1,0:T(8,128)(2,1)}, bf16[2,192,384]{2,1,0:T(8,128)(2,1)S(1)}, u32[]{:S(2)}) copy-start(bf16[2,192,384]{2,1,0:T(8,128)(2,1)S(1)} %get-tuple-element.25.refs_0_) | copy-start | bytes 884740
  59.3 7.5 %collective-permute-start.9 = (bf16[2,192,384]{2,1,0:T(8,128)(2,1)S(1)}, bf16[2,192,384]{2,1,0:T(8,128)(2,1)S(1)}, u32[]{:S(2)}, u32[]{:S(2)}) collective-permute-start(bf16[2,192,384]{2,1,0:T(8,128)(2,1)S(1)} %get-tuple-element.24.refs_1_), channel_id=1, source_target_pairs={{0,2},{1,3},{2,4},{3,5},{8,10},{9,11},{10,12},{11,13},{12,14},{13,... | collective-permute-start | bytes 884744 | tf_op jit(solution)/shard_map/ppermute | solution.py:40
  60.6 6.8 %collective-permute-start.10 = (bf16[2,192,384]{2,1,0:T(8,128)(2,1)S(1)}, bf16[2,192,384]{2,1,0:T(8,128)(2,1)S(1)}, u32[]{:S(2)}, u32[]{:S(2)}) collective-permute-start(bf16[2,192,384]{2,1,0:T(8,128)(2,1)S(1)} %get-tuple-element.24.refs_1_), channel_id=1, source_target_pairs={{0,4},{1,5},{2,0},{3,1},{8,12},{9,13},{10,8},{11,9},{12,10},{13,11... | collective-permute-start | bytes 884744 | tf_op jit(solution)/shard_map/ppermute | solution.py:40
  61.3 6.9 %collective-permute-start.11 = (bf16[2,192,384]{2,1,0:T(8,128)(2,1)S(1)}, bf16[2,192,384]{2,1,0:T(8,128)(2,1)S(1)}, u32[]{:S(2)}, u32[]{:S(2)}) collective-permute-start(bf16[2,192,384]{2,1,0:T(8,128)(2,1)S(1)} %get-tuple-element.23), channel_id=1, source_target_pairs={{8,12},{9,13},{12,8},{13,9},{24,28},{25,29},{28,24},{29,25}} | collective-permute-start | bytes 884744 | tf_op jit(solution)/shard_map/ppermute | solution.py:40
  63.8 46.3 %copy-start.8 = (bf16[2,192,384]{2,1,0:T(8,128)(2,1)}, bf16[2,192,384]{2,1,0:T(8,128)(2,1)S(1)}, u32[]{:S(2)}) copy-start(bf16[2,192,384]{2,1,0:T(8,128)(2,1)S(1)} %collective-permute-done.6.refs_2_) | copy-start | bytes 884740
  63.8 5.6 %collective-permute-start.12 = (bf16[2,192,384]{2,1,0:T(8,128)(2,1)S(1)}, bf16[2,192,384]{2,1,0:T(8,128)(2,1)S(1)}, u32[]{:S(2)}, u32[]{:S(2)}) collective-permute-start(bf16[2,192,384]{2,1,0:T(8,128)(2,1)S(1)} %get-tuple-element.25.refs_0_), channel_id=1, source_target_pairs={{8,10},{9,11},{24,26},{25,27}} | collective-permute-start | bytes 884744 | tf_op jit(solution)/shard_map/ppermute | solution.py:40
  64.6 45.5 %copy-start.11 = (bf16[2,192,384]{2,1,0:T(8,128)(2,1)}, bf16[2,192,384]{2,1,0:T(8,128)(2,1)S(1)}, u32[]{:S(2)}) copy-start(bf16[2,192,384]{2,1,0:T(8,128)(2,1)S(1)} %get-tuple-element.21.refs_1_) | copy-start | bytes 884740
  64.6 45.5 %copy-start.12 = (bf16[2,192,384]{2,1,0:T(8,128)(2,1)}, bf16[2,192,384]{2,1,0:T(8,128)(2,1)S(1)}, u32[]{:S(2)}) copy-start(bf16[2,192,384]{2,1,0:T(8,128)(2,1)S(1)} %get-tuple-element.22.refs_0_) | copy-start | bytes 884740
  64.6 11.1 %collective-permute-start.18 = (bf16[2,192,384]{2,1,0:T(8,128)(2,1)S(1)}, bf16[2,192,384]{2,1,0:T(8,128)(2,1)S(1)}, u32[]{:S(2)}, u32[]{:S(2)}) collective-permute-start(bf16[2,192,384]{2,1,0:T(8,128)(2,1)S(1)} %get-tuple-element.21.refs_1_), channel_id=1, source_target_pairs={{0,2},{1,3},{2,4},{3,5},{8,10},{9,11},{10,12},{11,13},{12,14},{13,... | collective-permute-start | bytes 884744 | tf_op jit(solution)/shard_map/ppermute | solution.py:40
  66.7 39.6 %copy-start.21 = (bf16[2,192,384]{2,1,0:T(8,128)(2,1)}, bf16[2,192,384]{2,1,0:T(8,128)(2,1)S(1)}, u32[]{:S(2)}) copy-start(bf16[2,192,384]{2,1,0:T(8,128)(2,1)S(1)} %collective-permute-done.9.refs_2_) | copy-start | bytes 884740
  66.7 9.7 %collective-permute-start.19 = (bf16[2,192,384]{2,1,0:T(8,128)(2,1)S(1)}, bf16[2,192,384]{2,1,0:T(8,128)(2,1)S(1)}, u32[]{:S(2)}, u32[]{:S(2)}) collective-permute-start(bf16[2,192,384]{2,1,0:T(8,128)(2,1)S(1)} %get-tuple-element.21.refs_1_), channel_id=1, source_target_pairs={{0,4},{1,5},{2,0},{3,1},{8,12},{9,13},{10,8},{11,9},{12,10},{13,11... | collective-permute-start | bytes 884744 | tf_op jit(solution)/shard_map/ppermute | solution.py:40
  67.4 38.9 %copy-start.22 = (bf16[2,192,384]{2,1,0:T(8,128)(2,1)}, bf16[2,192,384]{2,1,0:T(8,128)(2,1)S(1)}, u32[]{:S(2)}) copy-start(bf16[2,192,384]{2,1,0:T(8,128)(2,1)S(1)} %collective-permute-done.10.refs_3_) | copy-start | bytes 884740
  67.4 10.3 %collective-permute-start.20 = (bf16[2,192,384]{2,1,0:T(8,128)(2,1)S(1)}, bf16[2,192,384]{2,1,0:T(8,128)(2,1)S(1)}, u32[]{:S(2)}, u32[]{:S(2)}) collective-permute-start(bf16[2,192,384]{2,1,0:T(8,128)(2,1)S(1)} %get-tuple-element.20), channel_id=1, source_target_pairs={{8,12},{9,13},{12,8},{13,9},{24,28},{25,29},{28,24},{29,25}} | collective-permute-start | bytes 884744 | tf_op jit(solution)/shard_map/ppermute | solution.py:40
  68.1 38.2 %copy-start.23 = (bf16[2,192,384]{2,1,0:T(8,128)(2,1)}, bf16[2,192,384]{2,1,0:T(8,128)(2,1)S(1)}, u32[]{:S(2)}) copy-start(bf16[2,192,384]{2,1,0:T(8,128)(2,1)S(1)} %collective-permute-done.11.refs_4_) | copy-start | bytes 884740
  68.1 21.4 %collective-permute-start.13 = (bf16[2,192,384]{2,1,0:T(8,128)(2,1)S(1)}, bf16[2,192,384]{2,1,0:T(8,128)(2,1)S(1)}, u32[]{:S(2)}, u32[]{:S(2)}) collective-permute-start(bf16[2,192,384]{2,1,0:T(8,128)(2,1)S(1)} %collective-permute-done.9.refs_2_), channel_id=1, source_target_pairs={{4,6},{5,7},{12,14},{13,15},{20,22},{21,23},{28,30},{29,31}} | collective-permute-start | bytes 884744 | tf_op jit(solution)/shard_map/ppermute | solution.py:40
  69.5 36.9 %copy-start.26 = (bf16[2,192,384]{2,1,0:T(8,128)(2,1)}, bf16[2,192,384]{2,1,0:T(8,128)(2,1)S(1)}, u32[]{:S(2)}) copy-start(bf16[2,192,384]{2,1,0:T(8,128)(2,1)S(1)} %collective-permute-done.12.refs_5_) | copy-start | bytes 884740
  69.5 26.4 %collective-permute-start.14 = (bf16[2,192,384]{2,1,0:T(8,128)(2,1)S(1)}, bf16[2,192,384]{2,1,0:T(8,128)(2,1)S(1)}, u32[]{:S(2)}, u32[]{:S(2)}) collective-permute-start(bf16[2,192,384]{2,1,0:T(8,128)(2,1)S(1)} %collective-permute-done.10.refs_3_), channel_id=1, source_target_pairs={{4,6},{5,7},{12,14},{13,15},{20,22},{21,23},{28,30},{29,31}} | collective-permute-start | bytes 884744 | tf_op jit(solution)/shard_map/ppermute | solution.py:40
  75.7 34.4 %copy-start.24 = (bf16[2,192,384]{2,1,0:T(8,128)(2,1)}, bf16[2,192,384]{2,1,0:T(8,128)(2,1)S(1)}, u32[]{:S(2)}) copy-start(bf16[2,192,384]{2,1,0:T(8,128)(2,1)S(1)} %collective-permute-done.18.refs_2_) | copy-start | bytes 884740
  75.7 34.6 %collective-permute-start.21 = (bf16[2,192,384]{2,1,0:T(8,128)(2,1)S(1)}, bf16[2,192,384]{2,1,0:T(8,128)(2,1)S(1)}, u32[]{:S(2)}, u32[]{:S(2)}) collective-permute-start(bf16[2,192,384]{2,1,0:T(8,128)(2,1)S(1)} %get-tuple-element.22.refs_0_), channel_id=1, source_target_pairs={{8,10},{9,11},{24,26},{25,27}} | collective-permute-start | bytes 884744 | tf_op jit(solution)/shard_map/ppermute | solution.py:40
  76.4 33.7 %copy-start.25 = (bf16[2,192,384]{2,1,0:T(8,128)(2,1)}, bf16[2,192,384]{2,1,0:T(8,128)(2,1)S(1)}, u32[]{:S(2)}) copy-start(bf16[2,192,384]{2,1,0:T(8,128)(2,1)S(1)} %collective-permute-done.19.refs_3_) | copy-start | bytes 884740
  76.4 29.9 %collective-permute-start.15 = (bf16[2,192,384]{2,1,0:T(8,128)(2,1)S(1)}, bf16[2,192,384]{2,1,0:T(8,128)(2,1)S(1)}, u32[]{:S(2)}, u32[]{:S(2)}) collective-permute-start(bf16[2,192,384]{2,1,0:T(8,128)(2,1)S(1)} %collective-permute-done.11.refs_4_), channel_id=1, source_target_pairs={{12,14},{13,15},{28,30},{29,31}} | collective-permute-start | bytes 884744 | tf_op jit(solution)/shard_map/ppermute | solution.py:40
  77.7 32.4 %copy-start.27 = (bf16[2,192,384]{2,1,0:T(8,128)(2,1)}, bf16[2,192,384]{2,1,0:T(8,128)(2,1)S(1)}, u32[]{:S(2)}) copy-start(bf16[2,192,384]{2,1,0:T(8,128)(2,1)S(1)} %collective-permute-done.20.refs_4_) | copy-start | bytes 884740
  77.7 32.7 %collective-permute-start.22 = (bf16[2,192,384]{2,1,0:T(8,128)(2,1)S(1)}, bf16[2,192,384]{2,1,0:T(8,128)(2,1)S(1)}, u32[]{:S(2)}, u32[]{:S(2)}) collective-permute-start(bf16[2,192,384]{2,1,0:T(8,128)(2,1)S(1)} %collective-permute-done.18.refs_2_), channel_id=1, source_target_pairs={{4,6},{5,7},{12,14},{13,15},{20,22},{21,23},{28,30},{29,31}} | collective-permute-start | bytes 884744 | tf_op jit(solution)/shard_map/ppermute | solution.py:40
  89.5 16.8 %copy-start.29 = (bf16[2,192,384]{2,1,0:T(8,128)(2,1)}, bf16[2,192,384]{2,1,0:T(8,128)(2,1)S(1)}, u32[]{:S(2)}) copy-start(bf16[2,192,384]{2,1,0:T(8,128)(2,1)S(1)} %collective-permute-done.13.refs_6_) | copy-start | bytes 884740
  89.5 24.1 %collective-permute-start.23 = (bf16[2,192,384]{2,1,0:T(8,128)(2,1)S(1)}, bf16[2,192,384]{2,1,0:T(8,128)(2,1)S(1)}, u32[]{:S(2)}, u32[]{:S(2)}) collective-permute-start(bf16[2,192,384]{2,1,0:T(8,128)(2,1)S(1)} %collective-permute-done.19.refs_3_), channel_id=1, source_target_pairs={{4,6},{5,7},{12,14},{13,15},{20,22},{21,23},{28,30},{29,31}} | collective-permute-start | bytes 884744 | tf_op jit(solution)/shard_map/ppermute | solution.py:40
  95.9 10.5 %copy-start.31 = (bf16[2,192,384]{2,1,0:T(8,128)(2,1)}, bf16[2,192,384]{2,1,0:T(8,128)(2,1)S(1)}, u32[]{:S(2)}) copy-start(bf16[2,192,384]{2,1,0:T(8,128)(2,1)S(1)} %collective-permute-done.14.refs_7_) | copy-start | bytes 884740
  95.9 20.9 %collective-permute-start.24 = (bf16[2,192,384]{2,1,0:T(8,128)(2,1)S(1)}, bf16[2,192,384]{2,1,0:T(8,128)(2,1)S(1)}, u32[]{:S(2)}, u32[]{:S(2)}) collective-permute-start(bf16[2,192,384]{2,1,0:T(8,128)(2,1)S(1)} %collective-permute-done.20.refs_4_), channel_id=1, source_target_pairs={{12,14},{13,15},{28,30},{29,31}} | collective-permute-start | bytes 884744 | tf_op jit(solution)/shard_map/ppermute | solution.py:40
  110.2 10.9 %copy-start.4 = (bf16[2,384,384]{2,1,0:T(8,128)(2,1)S(1)}, bf16[2,384,384]{2,1,0:T(8,128)(2,1)}, u32[]{:S(2)}) copy-start(bf16[2,384,384]{2,1,0:T(8,128)(2,1)} %copy-done.3) | copy-start | bytes 1769476
  110.2 15.0 %collective-permute-start.16 = (bf16[4,2,192,384]{3,2,1,0:T(8,128)(2,1)}, bf16[4,2,192,384]{3,2,1,0:T(8,128)(2,1)S(1)}, u32[]{:S(2)}, u32[]{:S(2)}) collective-permute-start(bf16[4,2,192,384]{3,2,1,0:T(8,128)(2,1)} %collect_lower.2.refs_0_), channel_id=1, source_target_pairs={{0,8},{1,9},{2,10},{3,11},{4,12},{5,13},{6,14},{7,15},{8,0},{9,1},... | collective-permute-start | bytes 3538952 | tf_op jit(solution)/shard_map/ppermute | solution.py:40
  120.5 4.6 %collective-permute-start.25 = (bf16[4,2,192,384]{3,2,1,0:T(8,128)(2,1)}, bf16[4,2,192,384]{3,2,1,0:T(8,128)(2,1)S(1)}, u32[]{:S(2)}, u32[]{:S(2)}) collective-permute-start(bf16[4,2,192,384]{3,2,1,0:T(8,128)(2,1)} %collect_lower.3.refs_2_), channel_id=1, source_target_pairs={{0,8},{1,9},{2,10},{3,11},{4,12},{5,13},{6,14},{7,15},{8,0},{9,1},... | collective-permute-start | bytes 3538952 | tf_op jit(solution)/shard_map/ppermute | solution.py:40
  120.6 3.7 %collective-permute-start.26 = (bf16[2,384,384]{2,1,0:T(8,128)(2,1)S(1)}, bf16[2,384,384]{2,1,0:T(8,128)(2,1)S(1)}, u32[]{:S(2)}, u32[]{:S(2)}) collective-permute-start(bf16[2,384,384]{2,1,0:T(8,128)(2,1)S(1)} %copy-done.1), channel_id=1, source_target_pairs={{0,8},{1,9},{2,10},{3,11},{4,12},{5,13},{6,14},{7,15},{8,0},{9,1},... | collective-permute-start | bytes 1769480 | tf_op jit(solution)/shard_map/ppermute | solution.py:40
  121.1 4.0 %collective-permute-start.27 = (bf16[2,384,384]{2,1,0:T(8,128)(2,1)S(1)}, bf16[2,384,384]{2,1,0:T(8,128)(2,1)S(1)}, u32[]{:S(2)}, u32[]{:S(2)}) collective-permute-start(bf16[2,384,384]{2,1,0:T(8,128)(2,1)S(1)} %copy-done.4), channel_id=1, source_target_pairs={{0,8},{1,9},{2,10},{3,11},{4,12},{5,13},{6,14},{7,15},{8,0},{9,1},... | collective-permute-start | bytes 1769480 | tf_op jit(solution)/shard_map/ppermute | solution.py:40
  135.9 5.6 %collective-permute-start.28 = (bf16[384,384]{1,0:T(8,128)(2,1)}, bf16[384,384]{1,0:T(8,128)(2,1)S(1)}, u32[]{:S(2)}, u32[]{:S(2)}) collective-permute-start(bf16[384,384]{1,0:T(8,128)(2,1)} %get-tuple-element.15), channel_id=1, source_target_pairs={{0,8},{1,9},{2,10},{3,11},{4,12},{5,13},{6,14},{7,15},{8,0},{9,1},... | collective-permute-start | bytes 884744 | tf_op jit(solution)/shard_map/ppermute | solution.py:40
  136.1 9.3 %collective-permute-start.29 = (bf16[384,384]{1,0:T(8,128)(2,1)}, bf16[384,384]{1,0:T(8,128)(2,1)S(1)}, u32[]{:S(2)}, u32[]{:S(2)}) collective-permute-start(bf16[384,384]{1,0:T(8,128)(2,1)} %get-tuple-element.16), channel_id=1, source_target_pairs={{0,16},{1,17},{2,18},{3,19},{4,20},{5,21},{6,22},{7,23},{8,24},{9,... | collective-permute-start | bytes 884744 | tf_op jit(solution)/shard_map/ppermute | solution.py:40
  138.1 13.8 %collective-permute-start.30 = (bf16[384,384]{1,0:T(8,128)(2,1)}, bf16[384,384]{1,0:T(8,128)(2,1)S(1)}, u32[]{:S(2)}, u32[]{:S(2)}) collective-permute-start(bf16[384,384]{1,0:T(8,128)(2,1)} %get-tuple-element.17), channel_id=1, source_target_pairs={{0,24},{1,25},{2,26},{3,27},{4,28},{5,29},{6,30},{7,31},{8,16},{9,... | collective-permute-start | bytes 884744 | tf_op jit(solution)/shard_map/ppermute | solution.py:40
  138.4 13.5 %copy-start.35 = (bf16[384,384]{1,0:T(8,128)(2,1)S(1)}, bf16[384,384]{1,0:T(8,128)(2,1)}, u32[]{:S(2)}) copy-start(bf16[384,384]{1,0:T(8,128)(2,1)} %get-tuple-element.14) | copy-start | bytes 884740
  (20 other events, 69.8 us)

commit v3 on v2

v3 whole, which is shorter than its diff:
```python
import functools
import itertools
import math

import jax
import jax.numpy as jnp
from jax import lax
from jax.experimental import pallas as pl
from jax.experimental.pallas import tpu as pltpu
from jax.sharding import PartitionSpec as P

AXES = ("row", "col", "mom")
VMEM_BYTES = 56 * 1024 * 1024


class Plan:
    def __init__(self, mesh, moments, side):
        self.rows = mesh.shape["row"]
        self.cols = mesh.shape["col"]
        self.moms = mesh.shape["mom"]
        self.moments = moments
        self.side = side
        self.groups = self.rows // moments
        self.half = side // self.moms
        self.width = side // self.groups
        self.keys = [
            (b, j)
            for b in range(moments)
            for j in range(self.cols - 1)
            if (b + 1) * self.groups - 1 > j
        ]

    def send(self, value, target):
        pairs = []
        index = lambda r, c, m: (r * self.cols + c) * self.moms + m
        for place in itertools.product(range(self.rows), range(self.cols), range(self.moms)):
            goal = target(*place)
            if goal is not None:
                pairs.append((index(*place), index(*goal)))
        return lax.ppermute(value, AXES, pairs)

    def direct(self, wanted):
        hub = self.cols - 2
        steps = []
        for key, source, to in sorted(wanted, key=lambda s: (s[2] != hub, abs(s[1] - s[2]))):
            for step in steps:
                if source not in step and to not in [goal for _, goal in step.values()]:
                    break
            else:
                step = {}
                steps.append(step)
            step[source] = (key, to)
        return steps


def hbm(count):
    return [pl.BlockSpec(memory_space=pl.ANY)] * count


def smem():
    return pl.BlockSpec(memory_space=pltpu.SMEM)


def run_copies(copies):
    for copy in copies:
        copy.start()
    for copy in copies:
        copy.wait()


def sigma_kernel(plan, pair_count, place, triples, *refs):
    moms, moments, groups = plan.moms, plan.moments, plan.groups
    half, side = plan.half, plan.side
    lesser_in, partner_in = refs[:moms], refs[moms : 2 * moms]
    outs = refs[2 * moms : 2 * moms + moms * moments]
    lesser, partner, sems = refs[2 * moms + moms * moments :]
    x, y = place[0] // groups, place[2]
    copies = []
    for which, (sources, target) in enumerate(((lesser_in, lesser), (partner_in, partner))):
        for q in range(moms):
            source = sources[q]
            if q == 0:
                source = source.at[:, :, pl.ds(pl.multiple_of(y * half, half), half), :]
            copies.append(
                pltpu.make_async_copy(
                    source, target.at[pl.ds((y ^ q) * moments, moments)], sems.at[which * moms + q]
                )
            )
    run_copies(copies)
    scale = 1.0 / pair_count
    lanes = 128 if side % 128 == 0 else side
    for q in reversed(range(moms)):
        for b in range(moments):
            moment = (y ^ q) * moments + (x ^ b)
            table = [[triples[moment, m, n] for n in range(3)] for m in range(pair_count)]
            out = outs[q * moments + b]

            def block(index, _, table=table, out=out):
                row = pl.multiple_of(index * 16, 16)
                for lane in range(0, side, lanes):
                    at = (pl.ds(row, 16), pl.ds(lane, lanes))
                    total_re = total_im = None
                    for a, b, c in table:
                        a_re, a_im = lesser[(a, 0) + at], lesser[(a, 1) + at]
                        b_re, b_im = lesser[(b, 0) + at], lesser[(b, 1) + at]
                        c_re, c_im = partner[(c, 0) + at], partner[(c, 1) + at]
                        p_re = a_re * b_re - a_im * b_im
                        p_im = a_re * b_im + a_im * b_re
                        f_re = (p_re * c_re - p_im * c_im).astype(jnp.float32)
                        f_im = (p_re * c_im + p_im * c_re).astype(jnp.float32)
                        total_re = f_re if total_re is None else total_re + f_re
                        total_im = f_im if total_im is None else total_im + f_im
                    out[(0,) + at] = (total_re * scale).astype(jnp.bfloat16)
                    out[(1,) + at] = (total_im * scale).astype(jnp.bfloat16)
                return 0

            lax.fori_loop(0, half // 16, block, 0)


def place_kernel(plan, place, *refs):
    ins, out, sems = refs[:-2], refs[-2], refs[-1]
    x, y = place[0] // plan.groups, place[2]
    copies = []
    for q in range(plan.moms):
        rows = pl.ds(pl.multiple_of((y ^ q) * plan.half, plan.half), plan.half)
        for b in range(plan.moments):
            index = q * plan.moments + b
            copies.append(pltpu.make_async_copy(ins[index], out.at[x ^ b, :, rows, :], sems.at[index]))
    run_copies(copies)


def solve_kernel(plan, block, place, *refs):
    rows, moms, groups, side = plan.rows, plan.moms, plan.groups, plan.side
    half, width = plan.half, plan.width
    keys = [j for b, j in plan.keys if b == block]
    final = block == plan.moments - 1
    refs = list(refs)
    take = lambda count: [refs.pop(0) for _ in range(count)]
    sig_in, diag_in, right_in = take(moms * groups * len(keys)), take(groups), take(rows)
    before = take(1 if block else 0)
    outs = take(rows if final else 1)
    sig, diag, right, solved, sems = refs
    r, y = place[0], place[2]
    copies = []

    def copy(source, target):
        copies.append(pltpu.make_async_copy(source, target, sems.at[len(copies)]))
        copies[-1].start()

    base = block * groups
    done = 2 * side * base
    for t in range(groups):
        local = (r % groups) ^ t
        for k, j in enumerate(keys):
            for q in range(moms):
                at = pl.ds(pl.multiple_of((y ^ q) * half, half), half)
                for p in range(2):
                    copy(
                        sig_in[(q * groups + t) * len(keys) + k].at[p],
                        sig.at[local, at, pl.ds((2 * j + p) * side, side)],
                    )
        for p in range(2):
            copy(diag_in[t].at[p], diag.at[local, :, pl.ds(p * side, side)])
    for s in range(rows):
        copy(right_in[s], right.at[r ^ s])
    if block:
        copy(before[0], solved.at[pl.ds(0, done), :])
    for made in copies:
        made.wait()

    weight = 1.0 / math.sqrt(side * rows)

    def turn(value):
        return jnp.concatenate([-value[:, width:], value[:, :width]], axis=1)

    for row in range(base, base + groups):
        pending = right[row].astype(jnp.float32)
        if row > 0:
            depth = 2 * side * row
            pending = pending + weight * jnp.dot(
                sig[row - base, :, :depth], solved[:depth, :], preferred_element_type=jnp.float32
            )
        both = jnp.concatenate([pending, turn(pending)], axis=0).astype(jnp.bfloat16)
        value = jnp.dot(diag[row - base], both, preferred_element_type=jnp.float32)
        solved[pl.ds(2 * row * side, side), :] = value.astype(jnp.bfloat16)
        solved[pl.ds((2 * row + 1) * side, side), :] = turn(value).astype(jnp.bfloat16)
    if final:
        copies = []
        for s in range(rows):
            at = pl.ds(pl.multiple_of(2 * (r ^ s) * side, side), side)
            copies.append(pltpu.make_async_copy(solved.at[at, :], outs[s], sems.at[s]))
        run_copies(copies)
    else:
        run_copies([pltpu.make_async_copy(solved, outs[0], sems.at[0])])


def on_device(mesh, lesser, greater, triples, diag_inverse, right_side):
    moments, _, side, _ = lesser.shape
    plan = Plan(mesh, moments, side)
    rows, cols, moms, groups = plan.rows, plan.cols, plan.moms, plan.groups
    half, width = plan.half, plan.width
    pair_count = triples.shape[1]
    r, z, y = (lax.axis_index(axis) for axis in AXES)
    x = r // groups
    place = jnp.stack([r, z, y]).astype(jnp.int32)
    bf16 = jnp.bfloat16
    params = pltpu.CompilerParams(vmem_limit_bytes=VMEM_BYTES)
    dma = lambda count: pltpu.SemaphoreType.DMA((count,))

    def exchange_mom(value, q):
        return plan.send(value, lambda a, b, c: (a, b, c ^ q))

    def exchange_row(value, s):
        return plan.send(value, lambda a, b, c: (a ^ s, b, c))

    def half_of(value, q):
        return lax.dynamic_slice_in_dim(value, (y ^ q) * half, half, 2)

    halves = [half_of(lesser, q) for q in range(1, moms)]
    halves, diag_inverse = lax.optimization_barrier((halves, diag_inverse))
    lesser_all = [lesser] + [exchange_mom(halves[q - 1], q) for q in range(1, moms)]
    partner = jnp.swapaxes(greater, 2, 3)
    partner_all = [partner] + [exchange_mom(half_of(partner, q), q) for q in range(1, moms)]

    came = [lax.dynamic_index_in_dim(diag_inverse, x ^ b, 0, keepdims=False) for b in range(moments)]
    came = came[:1] + [exchange_row(came[b], b * groups) for b in range(1, moments)]
    diag = [lax.select_n(x ^ b, *came) for b in range(moments)]

    right = right_side.reshape(moments, side, 2, groups, width).transpose(0, 3, 1, 2, 4)
    right = right.reshape(rows, side, 2 * width)
    right_all = [lax.dynamic_index_in_dim(right, r ^ s, 0, keepdims=False) for s in range(rows)]
    lesser_all, partner_all, right_all, diag = lax.optimization_barrier(
        (lesser_all, partner_all, right_all, diag)
    )

    slots = pl.pallas_call(
        functools.partial(sigma_kernel, plan, pair_count),
        out_shape=[jax.ShapeDtypeStruct((2, half, side), bf16)] * (moms * moments),
        in_specs=[smem(), smem()] + hbm(2 * moms),
        scratch_shapes=[
            pltpu.VMEM((moms * moments, 2, half, side), bf16),
            pltpu.VMEM((moms * moments, 2, half, side), bf16),
            dma(2 * moms),
        ],
        compiler_params=params,
        name="self_energy",
    )(place, triples, *lesser_all, *partner_all)

    own, whole = [], list(slots[:moments])
    for q in range(moms):
        mine = slots[q * moments : (q + 1) * moments]
        came = [mine[0] if q == 0 else exchange_mom(mine[0], q)]
        for b in range(1, moments):
            came.append(
                plan.send(mine[b], lambda a, c, m: (a ^ (b * groups), c, m ^ q) if a > c else None)
            )
        own.append([lax.select_n(x ^ b, *came) for b in range(moments)])
        if q > 0:
            whole += came[:1] + [exchange_mom(mine[b], q) for b in range(1, moments)]

    sigma = pl.pallas_call(
        functools.partial(place_kernel, plan),
        out_shape=jax.ShapeDtypeStruct(lesser.shape, bf16),
        in_specs=[smem()] + hbm(moms * moments),
        scratch_shapes=[dma(moms * moments)],
        compiler_params=params,
        name="place_sigma",
    )(place, *whole)

    last, top = cols - 1, moments - 1
    found = {}

    def valid(key, a):
        return key[0] * groups + a % groups > key[1]

    def spread(step, values):
        chosen = None
        for source, (key, _) in step.items():
            value = values[key[0]]
            if chosen is None:
                chosen, used = value, value
            elif value is not used:
                chosen = jnp.where(z == source, value, chosen)
        goal = lambda a, c, m: ((a, step[c][1], m) if c in step and valid(step[c][0], a) else None)
        return plan.send(chosen, goal)

    def relay(value, key):
        goal = lambda a, c, m: (a, last, m) if c == last - 1 and valid(key, a) else None
        return plan.send(value, goal)

    sends = [
        (key, key[1], to)
        for key in plan.keys
        for to in range(cols)
        if to != key[1] and (to < last or key[1] == last - 1)
    ]
    split = [send for send in sends if send[0][0] == top and send[2] >= send[1] - 1]
    joint = [send for send in sends if send not in split]
    for key in plan.keys:
        found[key, key[1]] = [own[q][key[0]] for q in range(moms)]
    previous = None
    for q in range(moms):
        values = own[q]
        if previous is not None:
            values, _, right_all = lax.optimization_barrier((values, previous, right_all))
        previous = []
        for step in plan.direct(split):
            value = spread(step, values)
            previous.append(value)
            for key, to in step.values():
                found.setdefault((key, to), []).append(value)
        for key in plan.keys:
            if key[0] == top and key[1] < last - 1:
                value = found[key, last - 1][q]
                if q > 0:
                    value, _ = lax.optimization_barrier((value, found[key, last][q - 1]))
                found.setdefault((key, last), []).append(relay(value, key))
    values = [jnp.stack([own[q][b] for q in range(moms)]) for b in range(moments)]
    for step in plan.direct(joint):
        value = spread(step, values)
        for key, to in step.values():
            found[key, to] = [value[q] for q in range(moms)]
            if key[0] < top and to == last - 1 and key[1] < last - 1:
                value_last = relay(value, key)
                found[key, last] = [value_last[q] for q in range(moms)]

    right_all = right_all[:1] + [exchange_row(right_all[s], s) for s in range(1, rows)]
    before = []
    for block in range(moments):
        keys = [key for key in plan.keys if key[0] == block]
        tiles = [
            [lax.select_n(z, *[found[key, c][q] for c in range(cols)]) for key in keys]
            for q in range(moms)
        ]
        sig_all = [
            value if t == 0 else exchange_row(value, t)
            for q in range(moms)
            for t in range(groups)
            for value in tiles[q]
        ]
        diag_all = [diag[block] if t == 0 else exchange_row(diag[block], t) for t in range(groups)]
        final = block == top
        shape = (side, 2 * width) if final else ((block + 1) * groups * 2 * side, 2 * width)
        count = rows if final else 1
        depth = max(j for _, j in keys) + 1
        before = pl.pallas_call(
            functools.partial(solve_kernel, plan, block),
            out_shape=[jax.ShapeDtypeStruct(shape, bf16)] * count,
            in_specs=[smem()] + hbm(len(sig_all) + groups + rows + (1 if block else 0)),
            out_specs=hbm(count),
            scratch_shapes=[
                pltpu.VMEM((groups, side, 2 * side * depth), bf16),
                pltpu.VMEM((groups, side, 2 * side), bf16),
                pltpu.VMEM((rows, side, 2 * width), bf16),
                pltpu.VMEM(((block + 1) * groups * 2 * side, 2 * width), bf16),
                dma(2 * len(sig_all) + 2 * groups + rows + 1),
            ],
            compiler_params=params,
            name="substitution",
        )(place, *sig_all, *diag_all, *right_all, *before)

    back = [before[0]] + [exchange_row(before[s], s) for s in range(1, rows)]
    pieces = jnp.stack([lax.select_n(r ^ s, *back) for s in range(rows)])
    pieces = pieces.reshape(moments, groups, side, 2, width).transpose(0, 2, 3, 1, 4)
    return sigma, pieces.reshape(moments, side, 2, side)


def solution(mesh):
    placed = (
        P("mom", None, "row", "col"),
        P("mom", None, "col", "row"),
        P(),
        P("mom", None, "row", None),
        P("mom", "row", None, "col"),
    )
    return jax.shard_map(
        functools.partial(on_device, mesh),
        mesh=mesh,
        in_specs=placed,
        out_specs=(P("mom", None, "row", "col"), P("mom", "row", None, "col")),
        check_vma=False,
    )
```

time: 157 us -> 175 us (1.11)
  waiting for transfers between devices: 76 us -> 93.1 us
  other arithmetic: 2.17 us -> 7.07 us
  local copies, waits for them, and re-layouts: 21.5 us -> 17.7 us
    ppermute x31 -> x34, waiting for transfers between devices: 76 us -> 93.1 us  [send(): return lax.ppermute(value, AXES, pairs)]
    unnamed x78 -> x84, local copies, waits for them, and re-layouts: 12.5 us -> 9.05 us
    select_n x2 -> x4, other arithmetic: 1.14 us -> 4.12 us  [the longest x2 2.88 us: on_device(): lax.select_n(z, *[found[key, c][q] for c in range(cols)])]
    another operation x0 -> x2, other arithmetic: none -> 1.98 us  [on_device(): jnp.stack([own[q][b] for q in range(moms)])]
    ppermute x31 -> x34, starting transfers between devices: 27 us -> 28.6 us  [send(): return lax.ppermute(value, AXES, pairs)]
    pallas_call x4 -> x3, Pallas kernels: 25 us -> 23.6 us  [the longest x2 13.1 us: on_device(): pl.pallas_call(functools.partial(solve_kernel, plan, block), out_shape=[j...]
  transfers between devices with their start and end apart: 31 -> 34, of which waited for: 17 -> 14; matrix products, arithmetic and copies ran while one was open for 6% -> 8% of each run, Pallas kernels for 6% -> 9%
where the time goes in v3:
time: 175 us; the launch traced here: 174 us
  waiting for transfers between devices  93.1 us (53%)
  starting transfers between devices  28.6 us (16%)
  Pallas kernels  26.5 us (15%)
  local copies, waits for them, and re-layouts  17.7 us (10%)
  other arithmetic  7.07 us (4%)
    ppermute x34, waiting for transfers between devices, send(): return lax.ppermute(value, AXES, pairs)  93.1 us
    ppermute x34, starting transfers between devices, send(): return lax.ppermute(value, AXES, pairs)  28.6 us
    pallas_call x2, Pallas kernels, on_device(): pl.pallas_call(functools.partial(solve_kernel, plan, block), out_shape=[j...  13.1 us
    pallas_call x1, Pallas kernels, on_device(): pl.pallas_call(functools.partial(sigma_kernel, plan, pair_count), out_sha...  10.5 us
    unnamed x84, local copies, waits for them, and re-layouts  9.05 us
    dynamic_slice x5, local copies, waits for them, and re-layouts, on_device(): lax.dynamic_index_in_dim(right, r ^ s, 0, keepdims=False)  3.73 us
  transfers between devices with their start and end apart: 34, of which 14 were waited for; matrix products, arithmetic and copies ran while one was open for 8% of the time, Pallas kernels for 9%

profile of v3, /device:TPU:25, one launch (start us, length us, event | category | flops | bytes accessed | tf_op | source)
XLA Modules:
  0.0 174.3 jit_solution(11413559554662807758)
XLA Ops:
  0.7 2.1 %constant_dynamic-slice_fusion.4 = bf16[2,2,192,384]{3,2,1,0:T(8,128)(2,1)} fusion(bf16[2,2,384,384]{3,2,1,0:T(8,128)(2,1)} %refs_0_, s32[]{:T(128)S(6)} %select_n.319), kind=kLoop, calls=%fused_computation.38 | loop fusion | bytes 1179652 | tf_op jit(solution)/shard_map/dynamic_slice | solution.py:217
  2.8 0.9 dynamic-slice_bitcast_fusion
  3.7 1.2 collective-permute-start.2
  5.7 0.9 dynamic-slice_bitcast_fusion.1
  6.6 1.2 collective-permute-start.1
  8.0 2.0 %copy.14 = bf16[2,384,2,384]{1,3,2,0:T(8,128)(2,1)S(1)} copy(bf16[2,384,2,384]{3,2,1,0:T(2,128)(2,1)S(1)} %copy-done.17) | data formatting | bytes 2359296 | tf_op args[4]
  10.3 0.9 copy.18
  11.2 0.9 copy.19
  12.1 0.9 copy.16
  13.0 0.9 copy.17
  15.2 3.0 %collective-permute-done.2 = bf16[2,384,384]{2,1,0:T(8,128)(2,1)} collective-permute-done((bf16[2,384,384]{2,1,0:T(8,128)(2,1)}, bf16[2,384,384]{2,1,0:T(8,128)(2,1)}, u32[]{:S(2)}, u32[]{:S(2)}) %collective-permute-start.2) | collective-permute-done | bytes 589856 | tf_op jit(solution)/shard_map/ppermute | solution.py:40
  18.2 1.2 bitcast_select_fusion
  19.4 1.4 collective-permute-done.1.refs_3_
  20.8 12.6 %collective-permute-done.refs_1_ = bf16[2,2,192,384]{3,2,1,0:T(8,128)(2,1)} collective-permute-done((bf16[2,2,192,384]{3,2,1,0:T(8,128)(2,1)}, bf16[2,2,192,384]{3,2,1,0:T(8,128)(2,1)}, u32[]{:S(2)}, u32[]{:S(2)}) %collective-permute-start) | collective-permute-done | bytes 589856 | tf_op jit(solution)/shard_map/ppermute | solution.py:40
  33.4 10.5 %self_energy.1 = (bf16[2,192,384]{2,1,0:T(8,128)(2,1)}, bf16[2,192,384]{2,1,0:T(8,128)(2,1)}, bf16[2,192,384]{2,1,0:T(8,128)(2,1)}, bf16[2,192,384]{2,1,0:T(8,128)(2,1)}) custom-call(s32[3]{0:T(128)} %pad_add_fusion.place, s32[4,8,3]{2,1,0:T(8,128)} %copy.20.triples, bf16[2,2,384,384]{3,2,1,0:T(8,128)(2,1)} %refs_0_, ...), custom_call_target="tpu_custom_call" | custom-call | tf_op jit(solution)/shard_map/self_energy/pallas_call | solution.py:236
  45.3 1.3 collective-permute-start.3
  46.6 1.0 fusion.6
  47.7 4.6 %collective-permute-done.3.refs_2_ = bf16[2,192,384]{2,1,0:T(8,128)(2,1)S(1)} collective-permute-done((bf16[2,192,384]{2,1,0:T(8,128)(2,1)}, bf16[2,192,384]{2,1,0:T(8,128)(2,1)S(1)}, u32[]{:S(2)}, u32[]{:S(2)}) %collective-permute-start.3) | collective-permute-done | bytes 294944 | tf_op jit(solution)/shard_map/ppermute | solution.py:40
  52.3 1.0 pad_maximum_fusion.1
  54.7 1.3 collective-permute-start.6
  56.0 1.3 collective-permute-start.8
  57.3 18.0 %collective-permute-done.6 = bf16[2,192,384]{2,1,0:T(8,128)(2,1)S(1)} collective-permute-done((bf16[2,192,384]{2,1,0:T(8,128)(2,1)S(1)}, bf16[2,192,384]{2,1,0:T(8,128)(2,1)S(1)}, u32[]{:S(2)}, u32[]{:S(2)}) %collective-permute-start.6) | collective-permute-done | bytes 294944 | tf_op jit(solution)/shard_map/ppermute | solution.py:40
  75.3 1.4 collective-permute-start.16
  76.7 1.3 collective-permute-start.9
  78.0 1.3 collective-permute-start.15
  79.3 1.5 collective-permute-start.26
  80.8 8.8 %collective-permute-done.8 = bf16[2,192,384]{2,1,0:T(8,128)(2,1)S(1)} collective-permute-done((bf16[2,192,384]{2,1,0:T(8,128)(2,1)S(1)}, bf16[2,192,384]{2,1,0:T(8,128)(2,1)S(1)}, u32[]{:S(2)}, u32[]{:S(2)}) %collective-permute-start.8) | collective-permute-done | bytes 294944 | tf_op jit(solution)/shard_map/ppermute | solution.py:40
  89.6 1.3 collective-permute-start.27
  90.9 1.3 collective-permute-start.17
  92.2 5.8 %collective-permute-done.9 = bf16[2,192,384]{2,1,0:T(8,128)(2,1)S(1)} collective-permute-done((bf16[2,192,384]{2,1,0:T(8,128)(2,1)S(1)}, bf16[2,192,384]{2,1,0:T(8,128)(2,1)S(1)}, u32[]{:S(2)}, u32[]{:S(2)}) %collective-permute-start.9) | collective-permute-done | bytes 294944 | tf_op jit(solution)/shard_map/ppermute | solution.py:40
  98.0 3.1 %collective-permute-done.15 = bf16[2,192,384]{2,1,0:T(8,128)(2,1)} collective-permute-done((bf16[2,192,384]{2,1,0:T(8,128)(2,1)S(1)}, bf16[2,192,384]{2,1,0:T(8,128)(2,1)}, u32[]{:S(2)}, u32[]{:S(2)}) %collective-permute-start.15) | collective-permute-done | bytes 294944 | tf_op jit(solution)/shard_map/ppermute | solution.py:40
  101.1 1.3 collective-permute-start.18
  102.6 14.4 %collective-permute-done.17 = bf16[2,192,384]{2,1,0:T(8,128)(2,1)} collective-permute-done((bf16[2,192,384]{2,1,0:T(8,128)(2,1)}, bf16[2,192,384]{2,1,0:T(8,128)(2,1)}, u32[]{:S(2)}, u32[]{:S(2)}) %collective-permute-start.17) | collective-permute-done | bytes 294944 | tf_op jit(solution)/shard_map/ppermute | solution.py:40
  116.9 3.2 %collective-permute-done.18 = bf16[2,192,384]{2,1,0:T(8,128)(2,1)} collective-permute-done((bf16[2,192,384]{2,1,0:T(8,128)(2,1)}, bf16[2,192,384]{2,1,0:T(8,128)(2,1)}, u32[]{:S(2)}, u32[]{:S(2)}) %collective-permute-start.18) | collective-permute-done | bytes 294944 | tf_op jit(solution)/shard_map/ppermute | solution.py:40
  120.1 1.4 select_select_fusion
  121.6 2.1 %collective-permute-start.25 = (bf16[384,384]{1,0:T(8,128)(2,1)S(1)}, bf16[384,384]{1,0:T(8,128)(2,1)S(1)}, u32[]{:S(2)}, u32[]{:S(2)}) collective-permute-start(bf16[384,384]{1,0:T(8,128)(2,1)S(1)} %bitcast.82), channel_id=1, source_target_pairs={{0,24},{1,25},{2,26},{3,27},{4,28},{5,29},{6,30},{7,31},{8,16},{9,... | collective-permute-start | bytes 884744 | tf_op jit(solution)/shard_map/ppermute | solution.py:40
  123.8 1.5 fusion.1
  126.0 3.6 %collective-permute-done.24.refs_8_.refs_16_ = bf16[384,384]{1,0:T(8,128)(2,1)S(1)} collective-permute-done((bf16[384,384]{1,0:T(8,128)(2,1)S(1)}, bf16[384,384]{1,0:T(8,128)(2,1)S(1)}, u32[]{:S(2)}, u32[]{:S(2)}) %collective-permute-start.24) | collective-permute-done | bytes 294944 | tf_op jit(solution)/shard_map/ppermute | solution.py:40
  129.7 2.3 %collective-permute-start.20 = (bf16[2,192,384]{2,1,0:T(8,128)(2,1)S(1)}, bf16[2,192,384]{2,1,0:T(8,128)(2,1)S(1)}, u32[]{:S(2)}, u32[]{:S(2)}) collective-permute-start(bf16[2,192,384]{2,1,0:T(8,128)(2,1)S(1)} %get-tuple-element.71.refs_7_), channel_id=1, source_target_pairs={{0,8},{1,9},{2,10},{3,11},{4,12},{5,13},{6,14},{7,15},{8,0},{9,1},... | collective-permute-start | bytes 884744 | tf_op jit(solution)/shard_map/ppermute | solution.py:40
  132.0 4.7 %collective-permute-done.25.refs_9_.refs_17_ = bf16[384,384]{1,0:T(8,128)(2,1)S(1)} collective-permute-done((bf16[384,384]{1,0:T(8,128)(2,1)S(1)}, bf16[384,384]{1,0:T(8,128)(2,1)S(1)}, u32[]{:S(2)}, u32[]{:S(2)}) %collective-permute-start.25) | collective-permute-done | bytes 294944 | tf_op jit(solution)/shard_map/ppermute | solution.py:40
  138.1 5.3 %substitution.2.refs_18_ = bf16[1536,384]{1,0:T(8,128)(2,1)} custom-call(s32[3]{0:T(128)} %pad_add_fusion.place, bf16[2,192,384]{2,1,0:T(8,128)(2,1)} %copy-done.14, bf16[2,192,384]{2,1,0:T(8,128)(2,1)} %copy-done.33, bf16[2,192,384]{2,1,0:T(8,128)(2,1)} %copy-done.13, bf16[2,192,384]{2,1,0:T(8,128)(2,1)} %copy-done.34, bf16[2,384,384]{2,1,0:T(8,128)(2,1)} %copy-done.3, ...), custom_call_target="tpu_custom_call" | custom-call | tf_op jit(solution)/shard_map/substitution/pallas_call | solution.py:346
  143.4 1.3 collective-permute-start.4
  146.4 7.8 %substitution.3 = (bf16[384,384]{1,0:T(8,128)(2,1)}, bf16[384,384]{1,0:T(8,128)(2,1)}, bf16[384,384]{1,0:T(8,128)(2,1)}, bf16[384,384]{1,0:T(8,128)(2,1)}) custom-call(s32[3]{0:T(128)} %pad_add_fusion.place, bf16[2,192,384]{2,1,0:T(8,128)(2,1)} %copy-done.7, bf16[2,192,384]{2,1,0:T(8,128)(2,1)} %copy-done.8, bf16[2,192,384]{2,1,0:T(8,128)(2,1)} %copy-done.9, ...), custom_call_target="tpu_custom_call" | custom-call | tf_op jit(solution)/shard_map/substitution/pallas_call | solution.py:346
  154.9 1.7 collective-permute-start.33
  157.3 2.9 %place_sigma.1 = bf16[2,2,384,384]{3,2,1,0:T(8,128)(2,1)} custom-call(s32[3]{0:T(128)} %pad_add_fusion.place, bf16[2,192,384]{2,1,0:T(8,128)(2,1)} %get-tuple-element.35.refs_0_, bf16[2,192,384]{2,1,0:T(8,128)(2,1)} %get-tuple-element.36.refs_1_, bf16[2,192,384]{2,1,0:T(8,128)(2,1)} %copy-done.15, bf16[2,192,384]{2,1,0:T(8,128)(2,1)} %copy-done.32), custom_call_target="tpu_custom_call" | custom-call | tf_op jit(solution)/shard_map/place_sigma/pallas_call | solution.py:261
  160.3 3.4 %collective-permute-done.32 = bf16[384,384]{1,0:T(8,128)(2,1)S(1)} collective-permute-done((bf16[384,384]{1,0:T(8,128)(2,1)}, bf16[384,384]{1,0:T(8,128)(2,1)S(1)}, u32[]{:S(2)}, u32[]{:S(2)}) %collective-permute-start.32) | collective-permute-done | bytes 294944 | tf_op jit(solution)/shard_map/ppermute | solution.py:40
  163.7 6.5 %collective-permute-done.33 = bf16[384,384]{1,0:T(8,128)(2,1)S(1)} collective-permute-done((bf16[384,384]{1,0:T(8,128)(2,1)}, bf16[384,384]{1,0:T(8,128)(2,1)S(1)}, u32[]{:S(2)}, u32[]{:S(2)}) %collective-permute-start.33) | collective-permute-done | bytes 294944 | tf_op jit(solution)/shard_map/ppermute | solution.py:40
  171.5 2.8 %copy.23 = bf16[2,384,2,384]{3,2,1,0:T(2,128)(2,1)} copy(bf16[2,384,2,384]{1,3,2,0:T(8,128)(2,1)S(1)} %bitcast.74) | data formatting | bytes 2359296
  (128 shorter events, 12.0 us)
Async XLA Ops:
  3.7 14.5 %collective-permute-start.2 = (bf16[2,384,384]{2,1,0:T(8,128)(2,1)}, bf16[2,384,384]{2,1,0:T(8,128)(2,1)}, u32[]{:S(2)}, u32[]{:S(2)}) collective-permute-start(bf16[2,384,384]{2,1,0:T(8,128)(2,1)} %dynamic-slice_bitcast_fusion), channel_id=1, source_target_pairs={{0,16},{1,17},{2,18},{3,19},{4,20},{5,21},{6,22},{7,23},{8,24},{9,... | collective-permute-start | bytes 1769480 | tf_op jit(solution)/shard_map/ppermute | solution.py:40
  6.6 14.2 %collective-permute-start.1 = (bf16[2,2,192,384]{3,2,1,0:T(8,128)(2,1)}, bf16[2,2,192,384]{3,2,1,0:T(8,128)(2,1)}, u32[]{:S(2)}, u32[]{:S(2)}) collective-permute-start(bf16[2,2,192,384]{3,2,1,0:T(8,128)(2,1)} %dynamic-slice_bitcast_fusion.1), channel_id=1, source_target_pairs={{0,1},{1,0},{2,3},{3,2},{4,5},{5,4},{6,7},{7,6},{8,9},{9,8},{10,11... | collective-permute-start | bytes 1769480 | tf_op jit(solution)/shard_map/ppermute | solution.py:40
  7.8 25.6 %collective-permute-start = (bf16[2,2,192,384]{3,2,1,0:T(8,128)(2,1)}, bf16[2,2,192,384]{3,2,1,0:T(8,128)(2,1)}, u32[]{:S(2)}, u32[]{:S(2)}) collective-permute-start(bf16[2,2,192,384]{3,2,1,0:T(8,128)(2,1)} %constant_dynamic-slice_fusion.4), channel_id=1, source_target_pairs={{0,1},{1,0},{2,3},{3,2},{4,5},{5,4},{6,7},{7,6},{8,9},{9,8},{10,11... | collective-permute-start | bytes 1769480 | tf_op jit(solution)/shard_map/ppermute | solution.py:40
  19.4 83.1 %copy-start.3 = (bf16[2,384,384]{2,1,0:T(8,128)(2,1)}, bf16[2,384,384]{2,1,0:T(8,128)(2,1)S(1)}, u32[]{:S(2)}) copy-start(bf16[2,384,384]{2,1,0:T(8,128)(2,1)S(1)} %get-tuple-element.51.refs_4_) | copy-start | bytes 1769476
  19.4 97.6 %copy-start.2 = (bf16[2,384,384]{2,1,0:T(8,128)(2,1)}, bf16[2,384,384]{2,1,0:T(8,128)(2,1)S(1)}, u32[]{:S(2)}) copy-start(bf16[2,384,384]{2,1,0:T(8,128)(2,1)S(1)} %get-tuple-element.46.refs_12_) | copy-start | bytes 1769476
  44.0 2.7 %collective-permute-start.5 = (bf16[2,192,384]{2,1,0:T(8,128)(2,1)}, bf16[2,192,384]{2,1,0:T(8,128)(2,1)S(1)}, u32[]{:S(2)}, u32[]{:S(2)}) collective-permute-start(bf16[2,192,384]{2,1,0:T(8,128)(2,1)} %get-tuple-element.36.refs_1_), channel_id=1, source_target_pairs={{8,24},{9,25},{16,0},{17,1},{18,2},{19,3},{24,8},{25,9},{26,10},{2... | collective-permute-start | bytes 884744 | tf_op jit(solution)/shard_map/ppermute | solution.py:40
  44.6 3.0 %collective-permute-start.10 = (bf16[2,192,384]{2,1,0:T(8,128)(2,1)}, bf16[2,192,384]{2,1,0:T(8,128)(2,1)S(1)}, u32[]{:S(2)}, u32[]{:S(2)}) collective-permute-start(bf16[2,192,384]{2,1,0:T(8,128)(2,1)} %get-tuple-element.38), channel_id=1, source_target_pairs={{8,25},{9,24},{16,1},{17,0},{18,3},{19,2},{24,9},{25,8},{26,11},{2... | collective-permute-start | bytes 884744 | tf_op jit(solution)/shard_map/ppermute | solution.py:40
  45.3 6.9 %collective-permute-start.3 = (bf16[2,192,384]{2,1,0:T(8,128)(2,1)}, bf16[2,192,384]{2,1,0:T(8,128)(2,1)S(1)}, u32[]{:S(2)}, u32[]{:S(2)}) collective-permute-start(bf16[2,192,384]{2,1,0:T(8,128)(2,1)} %get-tuple-element.37), channel_id=1, source_target_pairs={{0,1},{1,0},{2,3},{3,2},{4,5},{5,4},{6,7},{7,6},{8,9},{9,8},{10,11... | collective-permute-start | bytes 884744 | tf_op jit(solution)/shard_map/ppermute | solution.py:40
  53.3 26.0 %collective-permute-start.11 = (bf16[2,2,192,384]{3,2,1,0:T(8,128)(2,1)S(1)}, bf16[2,2,192,384]{3,2,1,0:T(8,128)(2,1)S(1)}, u32[]{:S(2)}, u32[]{:S(2)}) collective-permute-start(bf16[2,2,192,384]{3,2,1,0:T(8,128)(2,1)S(1)} %get-tuple-element.80), channel_id=1, source_target_pairs={{8,12},{9,13},{12,8},{13,9},{24,28},{25,29},{28,24},{29,25}} | collective-permute-start | bytes 1769480 | tf_op jit(solution)/shard_map/ppermute | solution.py:40
  54.0 2.0 %collective-permute-start.7 = (bf16[2,192,384]{2,1,0:T(8,128)(2,1)S(1)}, bf16[2,192,384]{2,1,0:T(8,128)(2,1)S(1)}, u32[]{:S(2)}, u32[]{:S(2)}) collective-permute-start(bf16[2,192,384]{2,1,0:T(8,128)(2,1)S(1)} %get-tuple-element.82), channel_id=1, source_target_pairs={{0,4},{1,5},{2,0},{3,1},{8,12},{9,13},{10,8},{11,9},{12,10},{13,11... | collective-permute-start | bytes 884744 | tf_op jit(solution)/shard_map/ppermute | solution.py:40
  54.7 20.7 %collective-permute-start.6 = (bf16[2,192,384]{2,1,0:T(8,128)(2,1)S(1)}, bf16[2,192,384]{2,1,0:T(8,128)(2,1)S(1)}, u32[]{:S(2)}, u32[]{:S(2)}) collective-permute-start(bf16[2,192,384]{2,1,0:T(8,128)(2,1)S(1)} %get-tuple-element.82), channel_id=1, source_target_pairs={{0,2},{1,3},{2,4},{3,5},{8,10},{9,11},{10,12},{11,13},{12,14},{13,... | collective-permute-start | bytes 884744 | tf_op jit(solution)/shard_map/ppermute | solution.py:40
  56.0 33.6 %collective-permute-start.8 = (bf16[2,192,384]{2,1,0:T(8,128)(2,1)S(1)}, bf16[2,192,384]{2,1,0:T(8,128)(2,1)S(1)}, u32[]{:S(2)}, u32[]{:S(2)}) collective-permute-start(bf16[2,192,384]{2,1,0:T(8,128)(2,1)S(1)} %collective-permute-done.7), channel_id=1, source_target_pairs={{4,6},{5,7},{12,14},{13,15},{20,22},{21,23},{28,30},{29,31}} | collective-permute-start | bytes 884744 | tf_op jit(solution)/shard_map/ppermute | solution.py:40
  75.3 15.6 %collective-permute-start.16 = (bf16[2,192,384]{2,1,0:T(8,128)(2,1)S(1)}, bf16[2,192,384]{2,1,0:T(8,128)(2,1)}, u32[]{:S(2)}, u32[]{:S(2)}) collective-permute-start(bf16[2,192,384]{2,1,0:T(8,128)(2,1)S(1)} %get-tuple-element.43), channel_id=1, source_target_pairs={{0,4},{1,5},{2,0},{3,1},{8,12},{9,13},{10,8},{11,9},{12,10},{13,11... | collective-permute-start | bytes 884744 | tf_op jit(solution)/shard_map/ppermute | solution.py:40
  76.7 21.3 %collective-permute-start.9 = (bf16[2,192,384]{2,1,0:T(8,128)(2,1)S(1)}, bf16[2,192,384]{2,1,0:T(8,128)(2,1)S(1)}, u32[]{:S(2)}, u32[]{:S(2)}) collective-permute-start(bf16[2,192,384]{2,1,0:T(8,128)(2,1)S(1)} %collective-permute-done.6), channel_id=1, source_target_pairs={{4,6},{5,7},{12,14},{13,15},{20,22},{21,23},{28,30},{29,31}} | collective-permute-start | bytes 884744 | tf_op jit(solution)/shard_map/ppermute | solution.py:40
  78.0 23.2 %collective-permute-start.15 = (bf16[2,192,384]{2,1,0:T(8,128)(2,1)S(1)}, bf16[2,192,384]{2,1,0:T(8,128)(2,1)}, u32[]{:S(2)}, u32[]{:S(2)}) collective-permute-start(bf16[2,192,384]{2,1,0:T(8,128)(2,1)S(1)} %get-tuple-element.43), channel_id=1, source_target_pairs={{0,2},{1,3},{2,4},{3,5},{8,10},{9,11},{10,12},{11,13},{12,14},{13,... | collective-permute-start | bytes 884744 | tf_op jit(solution)/shard_map/ppermute | solution.py:40
  79.3 42.2 %collective-permute-start.26 = (bf16[2,2,192,384]{3,2,1,0:T(8,128)(2,1)}, bf16[2,2,192,384]{3,2,1,0:T(8,128)(2,1)}, u32[]{:S(2)}, u32[]{:S(2)}) collective-permute-start(bf16[2,2,192,384]{3,2,1,0:T(8,128)(2,1)} %get-tuple-element.79), channel_id=1, source_target_pairs={{8,10},{9,11},{24,26},{25,27}} | collective-permute-start | bytes 1769480 | tf_op jit(solution)/shard_map/ppermute | solution.py:40
  89.6 32.0 %collective-permute-start.27 = (bf16[2,2,192,384]{3,2,1,0:T(8,128)(2,1)S(1)}, bf16[2,2,192,384]{3,2,1,0:T(8,128)(2,1)}, u32[]{:S(2)}, u32[]{:S(2)}) collective-permute-start(bf16[2,2,192,384]{3,2,1,0:T(8,128)(2,1)S(1)} %collective-permute-done.11), channel_id=1, source_target_pairs={{12,14},{13,15},{28,30},{29,31}} | collective-permute-start | bytes 1769480 | tf_op jit(solution)/shard_map/ppermute | solution.py:40
  90.9 26.1 %collective-permute-start.17 = (bf16[2,192,384]{2,1,0:T(8,128)(2,1)}, bf16[2,192,384]{2,1,0:T(8,128)(2,1)}, u32[]{:S(2)}, u32[]{:S(2)}) collective-permute-start(bf16[2,192,384]{2,1,0:T(8,128)(2,1)} %collective-permute-done.16), channel_id=1, source_target_pairs={{4,6},{5,7},{12,14},{13,15},{20,22},{21,23},{28,30},{29,31}} | collective-permute-start | bytes 884744 | tf_op jit(solution)/shard_map/ppermute | solution.py:40
  101.1 19.0 %collective-permute-start.18 = (bf16[2,192,384]{2,1,0:T(8,128)(2,1)}, bf16[2,192,384]{2,1,0:T(8,128)(2,1)}, u32[]{:S(2)}, u32[]{:S(2)}) collective-permute-start(bf16[2,192,384]{2,1,0:T(8,128)(2,1)} %collective-permute-done.15), channel_id=1, source_target_pairs={{4,6},{5,7},{12,14},{13,15},{20,22},{21,23},{28,30},{29,31}} | collective-permute-start | bytes 884744 | tf_op jit(solution)/shard_map/ppermute | solution.py:40
  102.5 19.1 %copy-start.36 = (bf16[1,384,384]{2,1,0:T(8,128)(2,1)S(1)}, bf16[1,384,384]{2,1,0:T(8,128)(2,1)}, u32[]{:S(2)}) copy-start(bf16[1,384,384]{2,1,0:T(8,128)(2,1)} %copy.18) | copy-start | bytes 884740
  102.5 19.2 %copy-start.35 = (bf16[1,384,384]{2,1,0:T(8,128)(2,1)S(1)}, bf16[1,384,384]{2,1,0:T(8,128)(2,1)}, u32[]{:S(2)}) copy-start(bf16[1,384,384]{2,1,0:T(8,128)(2,1)} %copy.19) | copy-start | bytes 884740
  102.5 21.3 %copy-start.1 = (bf16[2,192,384]{2,1,0:T(8,128)(2,1)S(1)}, bf16[2,192,384]{2,1,0:T(8,128)(2,1)}, u32[]{:S(2)}) copy-start(bf16[2,192,384]{2,1,0:T(8,128)(2,1)} %get-tuple-element.35.refs_0_) | copy-start | bytes 884740
  102.5 21.3 %copy-start.29 = (bf16[2,192,384]{2,1,0:T(8,128)(2,1)S(1)}, bf16[2,192,384]{2,1,0:T(8,128)(2,1)}, u32[]{:S(2)}) copy-start(bf16[2,192,384]{2,1,0:T(8,128)(2,1)} %copy-done.28) | copy-start | bytes 884740
  102.5 21.3 %copy-start.31 = (bf16[2,192,384]{2,1,0:T(8,128)(2,1)S(1)}, bf16[2,192,384]{2,1,0:T(8,128)(2,1)}, u32[]{:S(2)}) copy-start(bf16[2,192,384]{2,1,0:T(8,128)(2,1)} %copy-done.30) | copy-start | bytes 884740
  102.5 22.8 %collective-permute-start.30 = (bf16[2,384,384]{2,1,0:T(8,128)(2,1)S(1)}, bf16[2,384,384]{2,1,0:T(8,128)(2,1)S(1)}, u32[]{:S(2)}, u32[]{:S(2)}) collective-permute-start(bf16[2,384,384]{2,1,0:T(8,128)(2,1)S(1)} %get-tuple-element.51.refs_4_), channel_id=1, source_target_pairs={{0,8},{1,9},{2,10},{3,11},{4,12},{5,13},{6,14},{7,15},{8,0},{9,1},... | collective-permute-start | bytes 1769480 | tf_op jit(solution)/shard_map/ppermute | solution.py:40
  116.9 8.5 %collective-permute-start.22 = (bf16[2,384,384]{2,1,0:T(8,128)(2,1)S(1)}, bf16[2,384,384]{2,1,0:T(8,128)(2,1)S(1)}, u32[]{:S(2)}, u32[]{:S(2)}) collective-permute-start(bf16[2,384,384]{2,1,0:T(8,128)(2,1)S(1)} %get-tuple-element.46.refs_12_), channel_id=1, source_target_pairs={{0,8},{1,9},{2,10},{3,11},{4,12},{5,13},{6,14},{7,15},{8,0},{9,1},... | collective-permute-start | bytes 1769480 | tf_op jit(solution)/shard_map/ppermute | solution.py:40
  120.1 5.8 %collective-permute-start.23 = (bf16[384,384]{1,0:T(8,128)(2,1)}, bf16[384,384]{1,0:T(8,128)(2,1)S(1)}, u32[]{:S(2)}, u32[]{:S(2)}) collective-permute-start(bf16[384,384]{1,0:T(8,128)(2,1)} %bitcast.84), channel_id=1, source_target_pairs={{0,8},{1,9},{2,10},{3,11},{4,12},{5,13},{6,14},{7,15},{8,0},{9,1},... | collective-permute-start | bytes 884744 | tf_op jit(solution)/shard_map/ppermute | solution.py:40
  121.5 15.2 %copy-start.10 = (bf16[2,192,384]{2,1,0:T(8,128)(2,1)}, bf16[2,192,384]{2,1,0:T(8,128)(2,1)S(1)}, u32[]{:S(2)}) copy-start(bf16[2,192,384]{2,1,0:T(8,128)(2,1)S(1)} %get-tuple-element.70.refs_8_) | copy-start | bytes 884740
  121.5 8.1 %collective-permute-start.24 = (bf16[384,384]{1,0:T(8,128)(2,1)S(1)}, bf16[384,384]{1,0:T(8,128)(2,1)S(1)}, u32[]{:S(2)}, u32[]{:S(2)}) collective-permute-start(bf16[384,384]{1,0:T(8,128)(2,1)S(1)} %bitcast.83), channel_id=1, source_target_pairs={{0,16},{1,17},{2,18},{3,19},{4,20},{5,21},{6,22},{7,23},{8,24},{9,... | collective-permute-start | bytes 884744 | tf_op jit(solution)/shard_map/ppermute | solution.py:40
  121.6 15.0 %collective-permute-start.25 = (bf16[384,384]{1,0:T(8,128)(2,1)S(1)}, bf16[384,384]{1,0:T(8,128)(2,1)S(1)}, u32[]{:S(2)}, u32[]{:S(2)}) collective-permute-start(bf16[384,384]{1,0:T(8,128)(2,1)S(1)} %bitcast.82), channel_id=1, source_target_pairs={{0,24},{1,25},{2,26},{3,27},{4,28},{5,29},{6,30},{7,31},{8,16},{9,... | collective-permute-start | bytes 884744 | tf_op jit(solution)/shard_map/ppermute | solution.py:40
  125.3 12.4 %copy-start.13 = (bf16[2,192,384]{2,1,0:T(8,128)(2,1)}, bf16[2,192,384]{2,1,0:T(8,128)(2,1)S(1)}, u32[]{:S(2)}) copy-start(bf16[2,192,384]{2,1,0:T(8,128)(2,1)S(1)} %get-tuple-element.58.refs_2_) | copy-start | bytes 884740
  125.3 19.5 %copy-start.7 = (bf16[2,192,384]{2,1,0:T(8,128)(2,1)}, bf16[2,192,384]{2,1,0:T(8,128)(2,1)S(1)}, u32[]{:S(2)}) copy-start(bf16[2,192,384]{2,1,0:T(8,128)(2,1)S(1)} %get-tuple-element.76.refs_0_) | copy-start | bytes 884740
  125.3 19.5 %copy-start.8 = (bf16[2,192,384]{2,1,0:T(8,128)(2,1)}, bf16[2,192,384]{2,1,0:T(8,128)(2,1)S(1)}, u32[]{:S(2)}) copy-start(bf16[2,192,384]{2,1,0:T(8,128)(2,1)S(1)} %get-tuple-element.77.refs_1_) | copy-start | bytes 884740
  125.3 19.5 %copy-start.9 = (bf16[2,192,384]{2,1,0:T(8,128)(2,1)}, bf16[2,192,384]{2,1,0:T(8,128)(2,1)S(1)}, u32[]{:S(2)}) copy-start(bf16[2,192,384]{2,1,0:T(8,128)(2,1)S(1)} %get-tuple-element.78.refs_2_) | copy-start | bytes 884740
  125.3 11.3 %collective-permute-start.19 = (bf16[2,192,384]{2,1,0:T(8,128)(2,1)S(1)}, bf16[2,192,384]{2,1,0:T(8,128)(2,1)S(1)}, u32[]{:S(2)}, u32[]{:S(2)}) collective-permute-start(bf16[2,192,384]{2,1,0:T(8,128)(2,1)S(1)} %get-tuple-element.72.refs_6_), channel_id=1, source_target_pairs={{0,8},{1,9},{2,10},{3,11},{4,12},{5,13},{6,14},{7,15},{8,0},{9,1},... | collective-permute-start | bytes 884744 | tf_op jit(solution)/shard_map/ppermute | solution.py:40
  125.4 19.3 %copy-start.20 = (bf16[2,384,384]{2,1,0:T(8,128)(2,1)}, bf16[2,384,384]{2,1,0:T(8,128)(2,1)S(1)}, u32[]{:S(2)}) copy-start(bf16[2,384,384]{2,1,0:T(8,128)(2,1)S(1)} %collective-permute-done.22.refs_13_) | copy-start | bytes 1769476
  125.4 11.7 %collective-permute-start.28 = (bf16[2,192,384]{2,1,0:T(8,128)(2,1)S(1)}, bf16[2,192,384]{2,1,0:T(8,128)(2,1)S(1)}, u32[]{:S(2)}, u32[]{:S(2)}) collective-permute-start(bf16[2,192,384]{2,1,0:T(8,128)(2,1)S(1)} %get-tuple-element.59.refs_0_), channel_id=1, source_target_pairs={{0,8},{1,9},{2,10},{3,11},{4,12},{5,13},{6,14},{7,15},{8,0},{9,1},... | collective-permute-start | bytes 884744 | tf_op jit(solution)/shard_map/ppermute | solution.py:40
  125.9 11.3 %collective-permute-start.29 = (bf16[2,192,384]{2,1,0:T(8,128)(2,1)S(1)}, bf16[2,192,384]{2,1,0:T(8,128)(2,1)S(1)}, u32[]{:S(2)}, u32[]{:S(2)}) collective-permute-start(bf16[2,192,384]{2,1,0:T(8,128)(2,1)S(1)} %get-tuple-element.58.refs_2_), channel_id=1, source_target_pairs={{0,8},{1,9},{2,10},{3,11},{4,12},{5,13},{6,14},{7,15},{8,0},{9,1},... | collective-permute-start | bytes 884744 | tf_op jit(solution)/shard_map/ppermute | solution.py:40
  129.7 13.7 %collective-permute-start.20 = (bf16[2,192,384]{2,1,0:T(8,128)(2,1)S(1)}, bf16[2,192,384]{2,1,0:T(8,128)(2,1)S(1)}, u32[]{:S(2)}, u32[]{:S(2)}) collective-permute-start(bf16[2,192,384]{2,1,0:T(8,128)(2,1)S(1)} %get-tuple-element.71.refs_7_), channel_id=1, source_target_pairs={{0,8},{1,9},{2,10},{3,11},{4,12},{5,13},{6,14},{7,15},{8,0},{9,1},... | collective-permute-start | bytes 884744 | tf_op jit(solution)/shard_map/ppermute | solution.py:40
  136.7 8.0 %collective-permute-start.21 = (bf16[2,192,384]{2,1,0:T(8,128)(2,1)S(1)}, bf16[2,192,384]{2,1,0:T(8,128)(2,1)S(1)}, u32[]{:S(2)}, u32[]{:S(2)}) collective-permute-start(bf16[2,192,384]{2,1,0:T(8,128)(2,1)S(1)} %get-tuple-element.70.refs_8_), channel_id=1, source_target_pairs={{0,8},{1,9},{2,10},{3,11},{4,12},{5,13},{6,14},{7,15},{8,0},{9,1},... | collective-permute-start | bytes 884744 | tf_op jit(solution)/shard_map/ppermute | solution.py:40
  136.7 8.0 %collective-permute-start.12 = (bf16[2,192,384]{2,1,0:T(8,128)(2,1)S(1)}, bf16[2,192,384]{2,1,0:T(8,128)(2,1)S(1)}, u32[]{:S(2)}, u32[]{:S(2)}) collective-permute-start(bf16[2,192,384]{2,1,0:T(8,128)(2,1)S(1)} %get-tuple-element.76.refs_0_), channel_id=1, source_target_pairs={{0,8},{1,9},{2,10},{3,11},{4,12},{5,13},{6,14},{7,15},{8,0},{9,1},... | collective-permute-start | bytes 884744 | tf_op jit(solution)/shard_map/ppermute | solution.py:40
  137.2 7.5 %collective-permute-start.13 = (bf16[2,192,384]{2,1,0:T(8,128)(2,1)S(1)}, bf16[2,192,384]{2,1,0:T(8,128)(2,1)S(1)}, u32[]{:S(2)}, u32[]{:S(2)}) collective-permute-start(bf16[2,192,384]{2,1,0:T(8,128)(2,1)S(1)} %get-tuple-element.77.refs_1_), channel_id=1, source_target_pairs={{0,8},{1,9},{2,10},{3,11},{4,12},{5,13},{6,14},{7,15},{8,0},{9,1},... | collective-permute-start | bytes 884744 | tf_op jit(solution)/shard_map/ppermute | solution.py:40
  137.3 7.5 %collective-permute-start.14 = (bf16[2,192,384]{2,1,0:T(8,128)(2,1)S(1)}, bf16[2,192,384]{2,1,0:T(8,128)(2,1)S(1)}, u32[]{:S(2)}, u32[]{:S(2)}) collective-permute-start(bf16[2,192,384]{2,1,0:T(8,128)(2,1)S(1)} %get-tuple-element.78.refs_2_), channel_id=1, source_target_pairs={{0,8},{1,9},{2,10},{3,11},{4,12},{5,13},{6,14},{7,15},{8,0},{9,1},... | collective-permute-start | bytes 884744 | tf_op jit(solution)/shard_map/ppermute | solution.py:40
  143.4 13.2 %collective-permute-start.4 = (bf16[2,192,384]{2,1,0:T(8,128)(2,1)S(1)}, bf16[2,192,384]{2,1,0:T(8,128)(2,1)S(1)}, u32[]{:S(2)}, u32[]{:S(2)}) collective-permute-start(bf16[2,192,384]{2,1,0:T(8,128)(2,1)S(1)} %copy-done.39), channel_id=1, source_target_pairs={{0,1},{1,0},{2,3},{3,2},{4,5},{5,4},{6,7},{7,6},{8,9},{9,8},{10,11... | collective-permute-start | bytes 884744 | tf_op jit(solution)/shard_map/ppermute | solution.py:40
  154.1 6.1 %collective-permute-start.31 = (bf16[384,384]{1,0:T(8,128)(2,1)}, bf16[384,384]{1,0:T(8,128)(2,1)S(1)}, u32[]{:S(2)}, u32[]{:S(2)}) collective-permute-start(bf16[384,384]{1,0:T(8,128)(2,1)} %get-tuple-element.53), channel_id=1, source_target_pairs={{0,8},{1,9},{2,10},{3,11},{4,12},{5,13},{6,14},{7,15},{8,0},{9,1},... | collective-permute-start | bytes 884744 | tf_op jit(solution)/shard_map/ppermute | solution.py:40
  154.9 8.8 %collective-permute-start.32 = (bf16[384,384]{1,0:T(8,128)(2,1)}, bf16[384,384]{1,0:T(8,128)(2,1)S(1)}, u32[]{:S(2)}, u32[]{:S(2)}) collective-permute-start(bf16[384,384]{1,0:T(8,128)(2,1)} %get-tuple-element.54), channel_id=1, source_target_pairs={{0,16},{1,17},{2,18},{3,19},{4,20},{5,21},{6,22},{7,23},{8,24},{9,... | collective-permute-start | bytes 884744 | tf_op jit(solution)/shard_map/ppermute | solution.py:40
  154.9 15.3 %collective-permute-start.33 = (bf16[384,384]{1,0:T(8,128)(2,1)}, bf16[384,384]{1,0:T(8,128)(2,1)S(1)}, u32[]{:S(2)}, u32[]{:S(2)}) collective-permute-start(bf16[384,384]{1,0:T(8,128)(2,1)} %get-tuple-element.55), channel_id=1, source_target_pairs={{0,24},{1,25},{2,26},{3,27},{4,28},{5,29},{6,30},{7,31},{8,16},{9,... | collective-permute-start | bytes 884744 | tf_op jit(solution)/shard_map/ppermute | solution.py:40
  156.6 13.6 %copy-start.37 = (bf16[384,384]{1,0:T(8,128)(2,1)S(1)}, bf16[384,384]{1,0:T(8,128)(2,1)}, u32[]{:S(2)}) copy-start(bf16[384,384]{1,0:T(8,128)(2,1)} %get-tuple-element.52) | copy-start | bytes 884740
  (26 other events, 117.8 us)

commit v4 on v3

v4 whole, which is shorter than its diff:
```python
import functools
import itertools
import math

import jax
import jax.numpy as jnp
from jax import lax
from jax.experimental import pallas as pl
from jax.experimental.pallas import tpu as pltpu
from jax.sharding import PartitionSpec as P

AXES = ("row", "col", "mom")
VMEM_BYTES = 56 * 1024 * 1024


class Plan:
    def __init__(self, mesh, moments, side):
        self.rows = mesh.shape["row"]
        self.cols = mesh.shape["col"]
        self.moms = mesh.shape["mom"]
        self.moments = moments
        self.side = side
        self.groups = self.rows // moments
        self.half = side // self.moms
        self.width = side // self.groups
        self.keys = [
            (b, j)
            for b in range(moments)
            for j in range(self.cols - 1)
            if (b + 1) * self.groups - 1 > j
        ]

    def send(self, value, target):
        pairs = []
        index = lambda r, c, m: (r * self.cols + c) * self.moms + m
        for place in itertools.product(range(self.rows), range(self.cols), range(self.moms)):
            goal = target(*place)
            if goal is not None:
                pairs.append((index(*place), index(*goal)))
        return lax.ppermute(value, AXES, pairs)

    def direct(self, wanted):
        hub = self.cols - 2
        steps = []
        for key, source, to in sorted(wanted, key=lambda s: (s[2] != hub, abs(s[1] - s[2]))):
            for step in steps:
                if source not in step and to not in [goal for _, goal in step.values()]:
                    break
            else:
                step = {}
                steps.append(step)
            step[source] = (key, to)
        return steps


def hbm(count):
    return [pl.BlockSpec(memory_space=pl.ANY)] * count


def smem():
    return pl.BlockSpec(memory_space=pltpu.SMEM)


def run_copies(copies):
    for copy in copies:
        copy.start()
    for copy in copies:
        copy.wait()


def sigma_kernel(plan, pair_count, chunks, place, quads, thirds, *refs):
    moms, moments, groups = plan.moms, plan.moments, plan.groups
    half, side, count = plan.half, plan.side, plan.moms * plan.moments
    lesser_in, partner_in = refs[:moms], refs[moms : 2 * moms]
    outs = refs[2 * moms : 2 * moms + count]
    lesser, partner, pairs, third, held, in_sems, out_sems = refs[2 * moms + count :]
    x, y = place[0] // groups, place[2]
    height = half // chunks
    copies = [[] for _ in range(chunks)]
    for chunk in range(chunks):
        rows = pl.ds(chunk * height, height)
        for which, (sources, target) in enumerate(((lesser_in, lesser), (partner_in, partner))):
            for q in range(moms):
                source = sources[q].at[:, :, rows, :]
                if q == 0:
                    start = pl.multiple_of(y * half + chunk * height, 16)
                    source = sources[q].at[:, :, pl.ds(start, height), :]
                copy = pltpu.make_async_copy(
                    source,
                    target.at[pl.ds((y ^ q) * moments, moments), :, rows, :],
                    in_sems.at[(chunk * 2 + which) * moms + q],
                )
                copy.start()
                copies[chunk].append(copy)
    scale = 1.0 / pair_count
    lanes = 128 if side % 128 == 0 else side
    order = [(q, b) for q in reversed(range(moms)) for b in range(moments)]
    sent = []
    for chunk in range(chunks):
        for copy in copies[chunk]:
            copy.wait()

        def block(index, _, chunk=chunk):
            rows = pl.ds(pl.multiple_of(chunk * height + index * 16, 16), 16)
            for c in range(count):
                for p in range(2):
                    third[c, p] = partner[c, p, rows, :].astype(jnp.float32)
            n = 0
            for a in range(count):
                for b in range(a + 1):
                    for lane in range(0, side, lanes):
                        cols = pl.ds(lane, lanes)
                        a_re = lesser[a, 0, rows, cols].astype(jnp.float32)
                        a_im = lesser[a, 1, rows, cols].astype(jnp.float32)
                        b_re = lesser[b, 0, rows, cols].astype(jnp.float32)
                        b_im = lesser[b, 1, rows, cols].astype(jnp.float32)
                        pairs[n, 0, :, cols] = a_re * b_re - a_im * b_im
                        pairs[n, 1, :, cols] = a_re * b_im + a_im * b_re
                    n += 1
            for q, b in order:
                moment = (y ^ q) * moments + (x ^ b)
                for lane in range(0, side, lanes):
                    cols = pl.ds(lane, lanes)
                    total_re = total_im = None
                    for m in range(pair_count):
                        quad, c = quads[moment, m], thirds[moment, m]
                        p_re, p_im = pairs[quad, 0, :, cols], pairs[quad, 1, :, cols]
                        c_re, c_im = third[c, 0, :, cols], third[c, 1, :, cols]
                        f_re = p_re * c_re - p_im * c_im
                        f_im = p_re * c_im + p_im * c_re
                        total_re = f_re if total_re is None else total_re + f_re
                        total_im = f_im if total_im is None else total_im + f_im
                    held[q * moments + b, 0, rows, cols] = (total_re * scale).astype(jnp.bfloat16)
                    held[q * moments + b, 1, rows, cols] = (total_im * scale).astype(jnp.bfloat16)
            return 0

        lax.fori_loop(0, height // 16, block, 0)
        rows = pl.ds(chunk * height, height)
        for index in range(count):
            copy = pltpu.make_async_copy(
                held.at[index, :, rows, :], outs[index].at[:, rows, :], out_sems.at[chunk * count + index]
            )
            copy.start()
            sent.append(copy)
    for copy in sent:
        copy.wait()


def place_kernel(plan, place, *refs):
    ins, out, sems = refs[:-2], refs[-2], refs[-1]
    x, y = place[0] // plan.groups, place[2]
    copies = []
    for q in range(plan.moms):
        rows = pl.ds(pl.multiple_of((y ^ q) * plan.half, plan.half), plan.half)
        for b in range(plan.moments):
            index = q * plan.moments + b
            copies.append(pltpu.make_async_copy(ins[index], out.at[x ^ b, :, rows, :], sems.at[index]))
    run_copies(copies)


def solve_kernel(plan, place, *refs):
    rows, moms, groups, side = plan.rows, plan.moms, plan.groups, plan.side
    moments, half, width, keys = plan.moments, plan.half, plan.width, plan.keys
    top = moments - 1
    refs = list(refs)
    take = lambda count: [refs.pop(0) for _ in range(count)]
    sig_in = {}
    for key in keys:
        for t in range(groups):
            if key[0] == top:
                sig_in[key, t] = take(moms)
            else:
                (ref,) = take(1)
                sig_in[key, t] = [ref.at[q] for q in range(moms)]
    diag_in = {(b, t): take(1)[0] for b in range(moments) for t in range(groups)}
    right_in, outs = take(rows), take(rows)
    sig, diag, right, solved, right_sems, sems, out_sems = refs
    r, y = place[0], place[2]
    g = r % groups

    def tile_copies(row, t):
        made = []
        b = row // groups
        add = lambda source, target: made.append(
            pltpu.make_async_copy(source, target, sems.at[row, len(made)])
        )
        for p in range(2):
            add(diag_in[b, t].at[p], diag.at[row, :, pl.ds(p * side, side)])
        for key in keys:
            if key[0] == b and row > key[1]:
                for q in range(moms):
                    at = pl.ds(pl.multiple_of((y ^ q) * half, half), half)
                    for p in range(2):
                        lane = pl.ds((2 * key[1] + p) * side, side)
                        add(sig_in[key, t][q].at[p], sig.at[row, at, lane])
        return made

    for s in range(rows):
        pltpu.make_async_copy(right_in[s], right.at[r ^ s], right_sems.at[s]).start()
    for me in range(groups):

        @pl.when(g == me)
        def _(me=me):
            for row in range(rows):
                for copy in tile_copies(row, me ^ (row % groups)):
                    copy.start()

    for s in range(rows):
        pltpu.make_async_copy(right_in[s], right.at[r ^ s], right_sems.at[s]).wait()

    weight = 1.0 / math.sqrt(side * rows)

    def turn(value):
        return jnp.concatenate([-value[:, width:], value[:, :width]], axis=1)

    for row in range(rows):
        for copy in tile_copies(row, 0):
            copy.wait()
        pending = right[row].astype(jnp.float32)
        if row > 0:
            depth = 2 * side * row
            pending = pending + weight * jnp.dot(
                sig[row, :, :depth], solved[:depth, :], preferred_element_type=jnp.float32
            )
        both = jnp.concatenate([pending, turn(pending)], axis=0).astype(jnp.bfloat16)
        value = jnp.dot(diag[row], both, preferred_element_type=jnp.float32)
        solved[pl.ds(2 * row * side, side), :] = value.astype(jnp.bfloat16)
        solved[pl.ds((2 * row + 1) * side, side), :] = turn(value).astype(jnp.bfloat16)
        for s in range(rows):

            @pl.when((r ^ s) == row)
            def _(s=s, row=row):
                at = pl.ds(2 * row * side, side)
                pltpu.make_async_copy(solved.at[at, :], outs[s], out_sems.at[s]).start()

    for s in range(rows):
        pltpu.make_async_copy(solved.at[pl.ds(0, side), :], outs[s], out_sems.at[s]).wait()


def after(value, *others):
    return lax.optimization_barrier((value, others))[0]


def on_device(mesh, lesser, greater, triples, diag_inverse, right_side):
    moments, _, side, _ = lesser.shape
    plan = Plan(mesh, moments, side)
    rows, cols, moms, groups = plan.rows, plan.cols, plan.moms, plan.groups
    half, width = plan.half, plan.width
    pair_count = triples.shape[1]
    count = moms * moments
    r, z, y = (lax.axis_index(axis) for axis in AXES)
    x = r // groups
    place = jnp.stack([r, z, y]).astype(jnp.int32)
    bf16, f32 = jnp.bfloat16, jnp.float32
    params = pltpu.CompilerParams(vmem_limit_bytes=VMEM_BYTES)
    dma = lambda *shape: pltpu.SemaphoreType.DMA(shape)

    def exchange_mom(value, q):
        return plan.send(value, lambda a, b, c: (a, b, c ^ q))

    def exchange_row(value, s):
        return plan.send(value, lambda a, b, c: (a ^ s, b, c))

    def half_of(value, q):
        return lax.dynamic_slice_in_dim(value, (y ^ q) * half, half, 2)

    halves = [half_of(lesser, q) for q in range(1, moms)]
    greater, diag_inverse, right_side = after((greater, diag_inverse, right_side), halves)
    lesser_all = [lesser] + [exchange_mom(halves[q - 1], q) for q in range(1, moms)]
    partner = jnp.swapaxes(greater, 2, 3)
    halves = [half_of(partner, q) for q in range(1, moms)]
    diag_inverse, right_side = after((diag_inverse, right_side), halves)
    partner_all = [partner] + [exchange_mom(halves[q - 1], q) for q in range(1, moms)]

    came = [lax.dynamic_index_in_dim(diag_inverse, x ^ b, 0, keepdims=False) for b in range(moments)]
    came = came[:1] + [exchange_row(came[b], b * groups) for b in range(1, moments)]
    diag = [lax.select_n(x ^ b, *came) for b in range(moments)]

    right = right_side.reshape(moments, side, 2, groups, width).transpose(0, 3, 1, 2, 4)
    right = right.reshape(rows, side, 2 * width)
    right_all = [lax.dynamic_index_in_dim(right, r ^ s, 0, keepdims=False) for s in range(rows)]
    lesser_all, partner_all, right_all, diag = lax.optimization_barrier(
        (lesser_all, partner_all, right_all, diag)
    )

    high = jnp.maximum(triples[..., 0], triples[..., 1])
    low = jnp.minimum(triples[..., 0], triples[..., 1])
    quads, thirds = high * (high + 1) // 2 + low, triples[..., 2]
    chunks = 4 if half % 64 == 0 else 1
    slots = pl.pallas_call(
        functools.partial(sigma_kernel, plan, pair_count, chunks),
        out_shape=[jax.ShapeDtypeStruct((2, half, side), bf16)] * count,
        in_specs=[smem()] * 3 + hbm(2 * moms),
        out_specs=hbm(count),
        scratch_shapes=[
            pltpu.VMEM((count, 2, half, side), bf16),
            pltpu.VMEM((count, 2, half, side), bf16),
            pltpu.VMEM((count * (count + 1) // 2, 2, 16, side), f32),
            pltpu.VMEM((count, 2, 16, side), f32),
            pltpu.VMEM((count, 2, half, side), bf16),
            dma(chunks * 2 * moms),
            dma(chunks * count),
        ],
        compiler_params=params,
        name="self_energy",
    )(place, quads, thirds, *lesser_all, *partner_all)

    def own_tiles(q):
        mine = slots[q * moments : (q + 1) * moments]
        came = []
        for b in range(1, moments):
            came.append(
                plan.send(mine[b], lambda a, c, m: (a ^ (b * groups), c, m ^ q) if a > c else None)
            )
        return [mine[0] if q == 0 else exchange_mom(mine[0], q)] + came

    def by_block(came):
        return [lax.select_n(x ^ b, *came) for b in range(moments)]

    came = [own_tiles(q) for q in range(moms)]
    last, top = cols - 1, moments - 1

    def valid(key, a):
        return key[0] * groups + a % groups > key[1]

    def spread(step, values):
        chosen = used = None
        for source, (key, _) in step.items():
            value = values[key[0]]
            if chosen is None:
                chosen = used = value
            elif value is not used:
                chosen = jnp.where(z == source, value, chosen)
        goal = lambda a, c, m: ((a, step[c][1], m) if c in step and valid(step[c][0], a) else None)
        return plan.send(chosen, goal)

    def relay(value, key):
        goal = lambda a, c, m: (a, last, m) if c == last - 1 and valid(key, a) else None
        return plan.send(value, goal)

    sends = [
        (key, key[1], to)
        for key in plan.keys
        for to in range(cols)
        if to != key[1] and (to < last or key[1] == last - 1)
    ]
    split = [send for send in sends if send[0][0] == top and send[2] >= send[1] - 1]
    joint = [send for send in sends if send not in split]
    found = {}
    own, whole = [], None
    log = []

    def issue(make, value):
        if len(log) > 2:
            value = after(value, log[-3])
        log.append(make(value))
        return log[-1]

    extra = []

    def fill():
        if extra:
            extra.pop(0)()

    right_came = [right_all[0]] + [None] * (rows - 1)

    def right_step(s):
        def run():
            right_came[s] = issue(lambda v: exchange_row(v, s), right_all[s])

        return run

    diag_came = {}

    def diag_step(b, t):
        def run():
            diag_came[b, t] = issue(lambda v: exchange_row(v, t), diag[b])

        return run

    extra += [right_step(s) for s in reversed(range(1, rows))]
    extra += [diag_step(b, t) for b in range(moments) for t in range(1, groups)]

    for q in range(moms):
        own.append(by_block(came[q]))
        for key in plan.keys:
            if key[0] == top:
                found.setdefault((key, key[1]), []).append(own[q][top])
    joint_values = [jnp.stack([own[k][b] for k in range(moms)]) for b in range(moments)]
    for key in plan.keys:
        if key[0] < top:
            found[key, key[1]] = joint_values[key[0]]

    def split_step(q, step):
        def run():
            value = issue(lambda v: spread(step, v), own[q])
            for key, to in step.values():
                found.setdefault((key, to), []).append(value)

        return run

    def split_relay(q, key):
        def run():
            value = found[key, last - 1][q]
            if q + 1 < moms:
                value = after(value, came[q + 1])
            value = issue(lambda v: relay(v, key), value)
            found.setdefault((key, last), []).append(value)
            fill()

        return run

    def joint_step(step):
        def run():
            value = issue(lambda v: spread(step, v), joint_values)
            for key, to in step.values():
                found[key, to] = [value[k] for k in range(moms)] if key[0] == top else value

        return run

    def joint_relay(key):
        def run():
            found[key, last] = issue(lambda v: relay(v, key), found[key, last - 1])

        return run

    relays = sorted([key for key in plan.keys if key[1] < last - 1], key=lambda key: -key[1])
    schedule, waiting = [], []
    for q in range(moms):
        for n, step in enumerate(plan.direct(split)):
            if waiting:
                schedule.append(waiting.pop(0))
            schedule.append(split_step(q, step))
        schedule += waiting
        waiting = [split_relay(q, key) for key in relays if key[0] == top]
    steps = [joint_step(step) for step in plan.direct(joint)]
    schedule = schedule[:-1] + steps[:1] + schedule[-1:]
    low_relays = [joint_relay(key) for key in relays if key[0] < top]
    schedule += waiting[:1] + (steps[1:] + low_relays if cols > 4 else low_relays)
    schedule += waiting[1:] + (steps[1:] if cols <= 4 else [])
    for run in schedule:
        run()
    while extra:
        fill()

    whole = [slots[b] for b in range(moments)]
    for q in range(1, moms):
        whole.append(came[q][0])
        for b in range(1, moments):
            whole.append(exchange_mom(after(slots[q * moments + b], log[-1]), q))
    sigma = pl.pallas_call(
        functools.partial(place_kernel, plan),
        out_shape=jax.ShapeDtypeStruct(lesser.shape, bf16),
        in_specs=[smem()] + hbm(count),
        scratch_shapes=[dma(count)],
        compiler_params=params,
        name="place_sigma",
    )(place, *whole)

    sig_all = []
    for key in plan.keys:
        if key[0] == top:
            mine = [lax.select_n(z, *[found[key, c][q] for c in range(cols)]) for q in range(moms)]
        else:
            mine = [lax.select_n(z, *[found[key, c] for c in range(cols)])]
        for t in range(groups):
            sig_all += mine if t == 0 else [exchange_row(value, t) for value in mine]
    diag_all = [
        diag[b] if t == 0 else diag_came[b, t] for b in range(moments) for t in range(groups)
    ]
    most = 2 + 4 * moms * (cols - 1)
    solved = pl.pallas_call(
        functools.partial(solve_kernel, plan),
        out_shape=[jax.ShapeDtypeStruct((side, 2 * width), bf16)] * rows,
        in_specs=[smem()] + hbm(len(sig_all) + len(diag_all) + rows),
        out_specs=hbm(rows),
        scratch_shapes=[
            pltpu.VMEM((rows, side, 2 * side * (cols - 1)), bf16),
            pltpu.VMEM((rows, side, 2 * side), bf16),
            pltpu.VMEM((rows, side, 2 * width), bf16),
            pltpu.VMEM((rows * 2 * side, 2 * width), bf16),
            dma(rows),
            dma(rows, most),
            dma(rows),
        ],
        compiler_params=params,
        name="substitution",
    )(place, *sig_all, *diag_all, *right_came)

    back = [solved[0]] + [exchange_row(solved[s], s) for s in range(1, rows)]
    pieces = jnp.stack([lax.select_n(r ^ s, *back) for s in range(rows)])
    pieces = pieces.reshape(moments, groups, side, 2, width).transpose(0, 2, 3, 1, 4)
    return sigma, pieces.reshape(moments, side, 2, side)


def solution(mesh):
    placed = (
        P("mom", None, "row", "col"),
        P("mom", None, "col", "row"),
        P(),
        P("mom", None, "row", None),
        P("mom", "row", None, "col"),
    )
    return jax.shard_map(
        functools.partial(on_device, mesh),
        mesh=mesh,
        in_specs=placed,
        out_specs=(P("mom", None, "row", "col"), P("mom", "row", None, "col")),
        check_vma=False,
    )
```

time: 175 us -> 158 us (0.903)
  waiting for transfers between devices: 93.1 us -> 75.9 us
  Pallas kernels: 26.5 us -> 17.4 us
  starting transfers between devices: 28.6 us -> 37 us
    ppermute x34 -> x33, waiting for transfers between devices: 93.1 us -> 75.9 us  [send(): return lax.ppermute(value, AXES, pairs)]
    pallas_call x3 -> x2, Pallas kernels: 23.6 us -> 14.4 us  [the longest x1 8.19 us: on_device(): pl.pallas_call(functools.partial(solve_kernel, plan), out_shape=[jax.Shap...]
    ppermute x34 -> x33, starting transfers between devices: 28.6 us -> 37 us  [send(): return lax.ppermute(value, AXES, pairs)]
    unnamed x84 -> x67, local copies, waits for them, and re-layouts: 9.05 us -> 6.22 us
    optimization_barrier x0 -> x2, local copies, waits for them, and re-layouts: none -> 2.75 us  [after(): return lax.optimization_barrier((value, others))[0]]
  transfers between devices with their start and end apart: 34 -> 33, of which waited for: 14 -> 13; matrix products, arithmetic and copies ran while one was open for 8% -> 10% of each run, Pallas kernels for 9% -> 7%
where the time goes in v4:
time: 158 us; the launch traced here: 157 us
  waiting for transfers between devices  75.9 us (48%)
  starting transfers between devices  37 us (23%)
  local copies, waits for them, and re-layouts  18.2 us (12%)
  Pallas kernels  17.4 us (11%)
  other arithmetic  7.08 us (4%)
    ppermute x33, waiting for transfers between devices, send(): return lax.ppermute(value, AXES, pairs)  75.9 us
    ppermute x33, starting transfers between devices, send(): return lax.ppermute(value, AXES, pairs)  37 us
    pallas_call x1, Pallas kernels, on_device(): pl.pallas_call(functools.partial(solve_kernel, plan), out_shape=[jax.Shap...  8.19 us
    pallas_call x1, Pallas kernels, on_device(): pl.pallas_call(functools.partial(sigma_kernel, plan, pair_count, chunks),...  6.25 us
    unnamed x67, local copies, waits for them, and re-layouts  6.22 us
    dynamic_slice x5, local copies, waits for them, and re-layouts, on_device(): lax.dynamic_index_in_dim(right, r ^ s, 0, keepdims=False)  3.77 us
  transfers between devices with their start and end apart: 33, of which 13 were waited for; matrix products, arithmetic and copies ran while one was open for 10% of the time, Pallas kernels for 7%

profile of v4, /device:TPU:25, one launch (start us, length us, event | category | flops | bytes accessed | tf_op | source)
XLA Modules:
  0.0 156.9 jit_solution(5964255614262301008)
XLA Ops:
  0.6 2.0 %constant_dynamic-slice_fusion.4 = bf16[2,2,192,384]{3,2,1,0:T(8,128)(2,1)} fusion(bf16[2,2,384,384]{3,2,1,0:T(8,128)(2,1)} %refs_0_, s32[]{:T(128)S(6)} %select_n.316), kind=kLoop, calls=%fused_computation.39 | loop fusion | bytes 1179652 | tf_op jit(solution)/shard_map/dynamic_slice | solution.py:265
  2.7 1.2 collective-permute-start
  4.7 0.9 dynamic-slice_bitcast_fusion.1
  5.9 0.9 dynamic-slice_bitcast_fusion
  6.8 1.2 collective-permute-start.2
  8.0 2.0 %copy.13 = bf16[2,384,2,384]{1,3,2,0:T(8,128)(2,1)S(1)} copy(bf16[2,384,2,384]{3,2,1,0:T(2,128)(2,1)S(1)} %copy-done.12) | data formatting | bytes 2359296 | tf_op jit(solution)/shard_map/optimization_barrier | solution.py:241
  10.3 0.9 copy.15
  11.2 0.9 copy.16
  12.1 0.9 copy.17
  13.1 0.9 copy.18
  15.7 5.0 %collective-permute-done.2 = bf16[2,384,384]{2,1,0:T(8,128)(2,1)} collective-permute-done((bf16[2,384,384]{2,1,0:T(8,128)(2,1)}, bf16[2,384,384]{2,1,0:T(8,128)(2,1)}, u32[]{:S(2)}, u32[]{:S(2)}) %collective-permute-start.2) | collective-permute-done | bytes 589856 | tf_op jit(solution)/shard_map/ppermute | solution.py:40
  20.7 1.2 bitcast_select_fusion
  21.9 7.9 %collective-permute-done.1.refs_3_ = bf16[2,2,192,384]{3,2,1,0:T(8,128)(2,1)} collective-permute-done((bf16[2,2,192,384]{3,2,1,0:T(8,128)(2,1)}, bf16[2,2,192,384]{3,2,1,0:T(8,128)(2,1)}, u32[]{:S(2)}, u32[]{:S(2)}) %collective-permute-start.1) | collective-permute-done | bytes 589856 | tf_op jit(solution)/shard_map/ppermute | solution.py:40
  29.8 6.2 %self_energy.1 = (bf16[2,192,384]{2,1,0:T(8,128)(2,1)}, bf16[2,192,384]{2,1,0:T(8,128)(2,1)}, bf16[2,192,384]{2,1,0:T(8,128)(2,1)}, bf16[2,192,384]{2,1,0:T(8,128)(2,1)}) custom-call(s32[3]{0:T(128)} %pad_add_fusion.place, s32[4,8]{1,0:T(4,128)} %fusion.5.quads, s32[4,8]{1,0:T(4,128)} %slice_bitcast_fusion.2.thirds, bf16[2,2,384,384]{3,2,1,0:T(8,128)(2,1)} %refs_0_, ...), custom_call_target="tpu_custom_call" | custom-call | tf_op jit(solution)/shard_map/self_energy/pallas_call | solution.py:290
  36.8 1.3 collective-permute-start.3
  38.8 1.0 select_bitcast_fusion.4
  39.8 1.3 collective-permute-start.7
  41.1 1.4 collective-permute-start.6
  42.5 1.5 collective-permute-done.3.refs_2_
  44.1 7.3 %collective-permute-done.7 = bf16[2,192,384]{2,1,0:T(8,128)(2,1)} collective-permute-done((bf16[2,192,384]{2,1,0:T(8,128)(2,1)S(1)}, bf16[2,192,384]{2,1,0:T(8,128)(2,1)}, u32[]{:S(2)}, u32[]{:S(2)}) %collective-permute-start.7) | collective-permute-done | bytes 294944 | tf_op jit(solution)/shard_map/ppermute | solution.py:40
  51.4 1.3 collective-permute-start.8
  52.7 1.3 collective-permute-start.11
  54.2 5.0 %collective-permute-done.8 = bf16[2,192,384]{2,1,0:T(8,128)(2,1)} collective-permute-done((bf16[2,192,384]{2,1,0:T(8,128)(2,1)}, bf16[2,192,384]{2,1,0:T(8,128)(2,1)}, u32[]{:S(2)}, u32[]{:S(2)}) %collective-permute-start.8) | collective-permute-done | bytes 294944 | tf_op jit(solution)/shard_map/ppermute | solution.py:40
  59.2 1.3 collective-permute-start.9
  60.4 4.9 %collective-permute-done.11 = bf16[2,192,384]{2,1,0:T(8,128)(2,1)} collective-permute-done((bf16[2,192,384]{2,1,0:T(8,128)(2,1)S(1)}, bf16[2,192,384]{2,1,0:T(8,128)(2,1)}, u32[]{:S(2)}, u32[]{:S(2)}) %collective-permute-start.11) | collective-permute-done | bytes 294944 | tf_op jit(solution)/shard_map/ppermute | solution.py:40
  66.2 5.9 %collective-permute-start.12 = (bf16[384,384]{1,0:T(8,128)(2,1)S(1)}, bf16[384,384]{1,0:T(8,128)(2,1)S(1)}, u32[]{:S(2)}, u32[]{:S(2)}) collective-permute-start(bf16[384,384]{1,0:T(8,128)(2,1)S(1)} %bitcast.68), channel_id=1, source_target_pairs={{0,24},{1,25},{2,26},{3,27},{4,28},{5,29},{6,30},{7,31},{8,16},{9,... | collective-permute-start | bytes 884744 | tf_op jit(solution)/shard_map/ppermute | solution.py:40
  72.0 1.4 collective-permute-start.10
  73.4 4.7 %collective-permute-done.12.refs_21_ = bf16[384,384]{1,0:T(8,128)(2,1)S(1)} collective-permute-done((bf16[384,384]{1,0:T(8,128)(2,1)S(1)}, bf16[384,384]{1,0:T(8,128)(2,1)S(1)}, u32[]{:S(2)}, u32[]{:S(2)}) %collective-permute-start.12) | collective-permute-done | bytes 294944 | tf_op jit(solution)/shard_map/ppermute | solution.py:40
  78.1 2.6 %collective-permute-start.13 = (bf16[384,384]{1,0:T(8,128)(2,1)S(1)}, bf16[384,384]{1,0:T(8,128)(2,1)S(1)}, u32[]{:S(2)}, u32[]{:S(2)}) collective-permute-start(bf16[384,384]{1,0:T(8,128)(2,1)S(1)} %bitcast.67), channel_id=1, source_target_pairs={{0,16},{1,17},{2,18},{3,19},{4,20},{5,21},{6,22},{7,23},{8,24},{9,... | collective-permute-start | bytes 884744 | tf_op jit(solution)/shard_map/ppermute | solution.py:40
  80.8 1.3 collective-permute-start.19
  82.1 5.3 %collective-permute-done.13.refs_20_ = bf16[384,384]{1,0:T(8,128)(2,1)S(1)} collective-permute-done((bf16[384,384]{1,0:T(8,128)(2,1)S(1)}, bf16[384,384]{1,0:T(8,128)(2,1)S(1)}, u32[]{:S(2)}, u32[]{:S(2)}) %collective-permute-start.13) | collective-permute-done | bytes 294944 | tf_op jit(solution)/shard_map/ppermute | solution.py:40
  87.3 1.3 collective-permute-start.14
  88.6 18.4 %collective-permute-done.14 = bf16[2,192,384]{2,1,0:T(8,128)(2,1)} collective-permute-done((bf16[2,192,384]{2,1,0:T(8,128)(2,1)}, bf16[2,192,384]{2,1,0:T(8,128)(2,1)}, u32[]{:S(2)}, u32[]{:S(2)}) %collective-permute-start.14) | collective-permute-done | bytes 294944 | tf_op jit(solution)/shard_map/ppermute | solution.py:40
  107.0 1.3 collective-permute-start.15
  109.2 1.5 collective-permute-start.20
  110.6 1.0 collective-permute-start.28
  111.6 5.1 %collective-permute-done.15 = bf16[2,192,384]{2,1,0:T(8,128)(2,1)} collective-permute-done((bf16[2,192,384]{2,1,0:T(8,128)(2,1)}, bf16[2,192,384]{2,1,0:T(8,128)(2,1)}, u32[]{:S(2)}, u32[]{:S(2)}) %collective-permute-start.15) | collective-permute-done | bytes 294944 | tf_op jit(solution)/shard_map/ppermute | solution.py:40
  116.8 1.9 %collective-permute-start.16 = (bf16[2,384,384]{2,1,0:T(8,128)(2,1)S(1)}, bf16[2,384,384]{2,1,0:T(8,128)(2,1)S(1)}, u32[]{:S(2)}, u32[]{:S(2)}) collective-permute-start(bf16[2,384,384]{2,1,0:T(8,128)(2,1)S(1)} %get-tuple-element.67.refs_16_), channel_id=1, source_target_pairs={{0,8},{1,9},{2,10},{3,11},{4,12},{5,13},{6,14},{7,15},{8,0},{9,1},... | collective-permute-start | bytes 1769480 | tf_op jit(solution)/shard_map/ppermute | solution.py:40
  118.7 1.9 %fusion.1 = (bf16[2,192,384]{2,1,0:T(8,128)(2,1)S(1)}, bf16[2,192,384]{2,1,0:T(8,128)(2,1)S(1)}, bf16[2,192,384]{2,1,0:T(8,128)(2,1)S(1)}, bf16[2,192,384]{2,1,0...) fusion(bf16[2,192,384]{2,1,0:T(8,128)(2,1)} %collective-permute-done.10, ...), kind=kLoop, calls=%fused_computation.11 | loop fusion | flops 2654208 | bytes 5308419 | tf_op jit(solution)/shard_map/select_n | solution.py:463
  121.7 1.2 select_select_fusion.refs_0_
  124.3 1.2 collective-permute-done.25.refs_9_
  125.5 1.2 collective-permute-start.17
  128.6 8.2 %substitution.1 = (bf16[384,384]{1,0:T(8,128)(2,1)}, bf16[384,384]{1,0:T(8,128)(2,1)}, bf16[384,384]{1,0:T(8,128)(2,1)}, bf16[384,384]{1,0:T(8,128)(2,1)}) custom-call(s32[3]{0:T(128)} %pad_add_fusion.place, bf16[2,2,192,384]{3,2,1,0:T(8,128)(2,1)} %copy-done.3, bf16[2,2,192,384]{3,2,1,0:T(8,128)(2,1)} %copy-done.16, bf16[2,192,384]{2,1,0:T(8,128)(2,1)} %copy-done.7, ...), custom_call_target="tpu_custom_call" | custom-call | tf_op jit(solution)/shard_map/substitution/pallas_call | solution.py:472
  136.8 2.1 %collective-permute-start.31 = (bf16[384,384]{1,0:T(8,128)(2,1)}, bf16[384,384]{1,0:T(8,128)(2,1)S(1)}, u32[]{:S(2)}, u32[]{:S(2)}) collective-permute-start(bf16[384,384]{1,0:T(8,128)(2,1)} %get-tuple-element.80), channel_id=1, source_target_pairs={{0,16},{1,17},{2,18},{3,19},{4,20},{5,21},{6,22},{7,23},{8,24},{9,... | collective-permute-start | bytes 884744 | tf_op jit(solution)/shard_map/ppermute | solution.py:40
  140.3 2.9 %place_sigma.1 = bf16[2,2,384,384]{3,2,1,0:T(8,128)(2,1)} custom-call(s32[3]{0:T(128)} %pad_add_fusion.place, bf16[2,192,384]{2,1,0:T(8,128)(2,1)} %get-tuple-element.51.refs_0_, bf16[2,192,384]{2,1,0:T(8,128)(2,1)} %get-tuple-element.52.refs_1_, bf16[2,192,384]{2,1,0:T(8,128)(2,1)} %copy-done.10, bf16[2,192,384]{2,1,0:T(8,128)(2,1)} %copy-done.25), custom_call_target="tpu_custom_call" | custom-call | tf_op jit(solution)/shard_map/place_sigma/pallas_call | solution.py:451
  143.3 2.8 %collective-permute-done.31 = bf16[384,384]{1,0:T(8,128)(2,1)S(1)} collective-permute-done((bf16[384,384]{1,0:T(8,128)(2,1)}, bf16[384,384]{1,0:T(8,128)(2,1)S(1)}, u32[]{:S(2)}, u32[]{:S(2)}) %collective-permute-start.31) | collective-permute-done | bytes 294944 | tf_op jit(solution)/shard_map/ppermute | solution.py:40
  146.1 6.6 %collective-permute-done.32 = bf16[384,384]{1,0:T(8,128)(2,1)S(1)} collective-permute-done((bf16[384,384]{1,0:T(8,128)(2,1)}, bf16[384,384]{1,0:T(8,128)(2,1)S(1)}, u32[]{:S(2)}, u32[]{:S(2)}) %collective-permute-start.32) | collective-permute-done | bytes 294944 | tf_op jit(solution)/shard_map/ppermute | solution.py:40
  154.0 2.8 %copy.21 = bf16[2,384,2,384]{3,2,1,0:T(2,128)(2,1)} copy(bf16[2,384,2,384]{1,3,2,0:T(8,128)(2,1)S(1)} %bitcast.58) | data formatting | bytes 2359296
  (113 shorter events, 13.1 us)
Async XLA Ops:
  0.6 3.3 %copy-start.11 = (bf16[2,2,384,384]{3,2,1,0:T(8,128)(2,1)S(1)}, bf16[2,2,384,384]{3,2,1,0:T(8,128)(2,1)}, u32[]{:S(2)}) copy-start(bf16[2,2,384,384]{3,2,1,0:T(8,128)(2,1)} %param.6) | copy-start | bytes 3538948
  2.7 19.2 %collective-permute-start = (bf16[2,2,192,384]{3,2,1,0:T(8,128)(2,1)}, bf16[2,2,192,384]{3,2,1,0:T(8,128)(2,1)}, u32[]{:S(2)}, u32[]{:S(2)}) collective-permute-start(bf16[2,2,192,384]{3,2,1,0:T(8,128)(2,1)} %constant_dynamic-slice_fusion.4), channel_id=1, source_target_pairs={{0,1},{1,0},{2,3},{3,2},{4,5},{5,4},{6,7},{7,6},{8,9},{9,8},{10,11... | collective-permute-start | bytes 1769480 | tf_op jit(solution)/shard_map/ppermute | solution.py:40
  4.7 3.3 %copy-start.12 = (bf16[2,384,2,384]{3,2,1,0:T(2,128)(2,1)S(1)}, bf16[2,384,2,384]{3,2,1,0:T(2,128)(2,1)}, u32[]{:S(2)}) copy-start(bf16[2,384,2,384]{3,2,1,0:T(2,128)(2,1)} %param.9) | copy-start | bytes 3538948
  5.6 24.2 %collective-permute-start.1 = (bf16[2,2,192,384]{3,2,1,0:T(8,128)(2,1)}, bf16[2,2,192,384]{3,2,1,0:T(8,128)(2,1)}, u32[]{:S(2)}, u32[]{:S(2)}) collective-permute-start(bf16[2,2,192,384]{3,2,1,0:T(8,128)(2,1)} %dynamic-slice_bitcast_fusion.1), channel_id=1, source_target_pairs={{0,1},{1,0},{2,3},{3,2},{4,5},{5,4},{6,7},{7,6},{8,9},{9,8},{10,11... | collective-permute-start | bytes 1769480 | tf_op jit(solution)/shard_map/ppermute | solution.py:40
  6.8 13.9 %collective-permute-start.2 = (bf16[2,384,384]{2,1,0:T(8,128)(2,1)}, bf16[2,384,384]{2,1,0:T(8,128)(2,1)}, u32[]{:S(2)}, u32[]{:S(2)}) collective-permute-start(bf16[2,384,384]{2,1,0:T(8,128)(2,1)} %dynamic-slice_bitcast_fusion), channel_id=1, source_target_pairs={{0,16},{1,17},{2,18},{3,19},{4,20},{5,21},{6,22},{7,23},{8,24},{9,... | collective-permute-start | bytes 1769480 | tf_op jit(solution)/shard_map/ppermute | solution.py:40
  10.3 3.7 %copy-start.32 = (s32[4,8,3]{1,0,2:T(4,128)S(1)}, s32[4,8,3]{1,0,2:T(4,128)}, u32[]{:S(2)}) copy-start(s32[4,8,3]{1,0,2:T(4,128)} %param.7) | copy-start | bytes 1156
  21.9 94.9 %copy-start.1 = (bf16[2,384,384]{2,1,0:T(8,128)(2,1)}, bf16[2,384,384]{2,1,0:T(8,128)(2,1)S(1)}, u32[]{:S(2)}) copy-start(bf16[2,384,384]{2,1,0:T(8,128)(2,1)S(1)} %get-tuple-element.67.refs_16_) | copy-start | bytes 1769476
  21.9 99.4 %copy-start.2 = (bf16[2,384,384]{2,1,0:T(8,128)(2,1)}, bf16[2,384,384]{2,1,0:T(8,128)(2,1)S(1)}, u32[]{:S(2)}) copy-start(bf16[2,384,384]{2,1,0:T(8,128)(2,1)S(1)} %get-tuple-element.76.refs_14_) | copy-start | bytes 1769476
  36.1 2.7 %collective-permute-start.5 = (bf16[2,192,384]{2,1,0:T(8,128)(2,1)}, bf16[2,192,384]{2,1,0:T(8,128)(2,1)S(1)}, u32[]{:S(2)}, u32[]{:S(2)}) collective-permute-start(bf16[2,192,384]{2,1,0:T(8,128)(2,1)} %get-tuple-element.52.refs_1_), channel_id=1, source_target_pairs={{8,24},{9,25},{16,0},{17,1},{18,2},{19,3},{24,8},{25,9},{26,10},{2... | collective-permute-start | bytes 884744 | tf_op jit(solution)/shard_map/ppermute | solution.py:40
  36.8 7.2 %collective-permute-start.3 = (bf16[2,192,384]{2,1,0:T(8,128)(2,1)}, bf16[2,192,384]{2,1,0:T(8,128)(2,1)S(1)}, u32[]{:S(2)}, u32[]{:S(2)}) collective-permute-start(bf16[2,192,384]{2,1,0:T(8,128)(2,1)} %get-tuple-element.53), channel_id=1, source_target_pairs={{0,1},{1,0},{2,3},{3,2},{4,5},{5,4},{6,7},{7,6},{8,9},{9,8},{10,11... | collective-permute-start | bytes 884744 | tf_op jit(solution)/shard_map/ppermute | solution.py:40
  38.1 5.9 %collective-permute-start.4 = (bf16[2,192,384]{2,1,0:T(8,128)(2,1)}, bf16[2,192,384]{2,1,0:T(8,128)(2,1)S(1)}, u32[]{:S(2)}, u32[]{:S(2)}) collective-permute-start(bf16[2,192,384]{2,1,0:T(8,128)(2,1)} %get-tuple-element.68), channel_id=1, source_target_pairs={{8,25},{9,24},{16,1},{17,0},{18,3},{19,2},{24,9},{25,8},{26,11},{2... | collective-permute-start | bytes 884744 | tf_op jit(solution)/shard_map/ppermute | solution.py:40
  39.8 11.6 %collective-permute-start.7 = (bf16[2,192,384]{2,1,0:T(8,128)(2,1)S(1)}, bf16[2,192,384]{2,1,0:T(8,128)(2,1)}, u32[]{:S(2)}, u32[]{:S(2)}) collective-permute-start(bf16[2,192,384]{2,1,0:T(8,128)(2,1)S(1)} %get-tuple-element.104), channel_id=1, source_target_pairs={{0,2},{1,3},{2,4},{3,5},{8,10},{9,11},{10,12},{11,13},{12,14},{13,... | collective-permute-start | bytes 884744 | tf_op jit(solution)/shard_map/ppermute | solution.py:40
  41.1 11.6 %collective-permute-start.6 = (bf16[2,192,384]{2,1,0:T(8,128)(2,1)S(1)}, bf16[2,192,384]{2,1,0:T(8,128)(2,1)}, u32[]{:S(2)}, u32[]{:S(2)}) collective-permute-start(bf16[2,192,384]{2,1,0:T(8,128)(2,1)S(1)} %get-tuple-element.104), channel_id=1, source_target_pairs={{0,4},{1,5},{2,0},{3,1},{8,12},{9,13},{10,8},{11,9},{12,10},{13,11... | collective-permute-start | bytes 884744 | tf_op jit(solution)/shard_map/ppermute | solution.py:40
  44.0 8.7 %copy-start.10 = (bf16[2,192,384]{2,1,0:T(8,128)(2,1)}, bf16[2,192,384]{2,1,0:T(8,128)(2,1)S(1)}, u32[]{:S(2)}) copy-start(bf16[2,192,384]{2,1,0:T(8,128)(2,1)S(1)} %collective-permute-done.3.refs_2_) | copy-start | bytes 884740
  51.4 7.8 %collective-permute-start.8 = (bf16[2,192,384]{2,1,0:T(8,128)(2,1)}, bf16[2,192,384]{2,1,0:T(8,128)(2,1)}, u32[]{:S(2)}, u32[]{:S(2)}) collective-permute-start(bf16[2,192,384]{2,1,0:T(8,128)(2,1)} %collective-permute-done.7), channel_id=1, source_target_pairs={{4,6},{5,7},{12,14},{13,15},{20,22},{21,23},{28,30},{29,31}} | collective-permute-start | bytes 884744 | tf_op jit(solution)/shard_map/ppermute | solution.py:40
  52.7 12.7 %collective-permute-start.11 = (bf16[2,192,384]{2,1,0:T(8,128)(2,1)S(1)}, bf16[2,192,384]{2,1,0:T(8,128)(2,1)}, u32[]{:S(2)}, u32[]{:S(2)}) collective-permute-start(bf16[2,192,384]{2,1,0:T(8,128)(2,1)S(1)} %get-tuple-element.60), channel_id=1, source_target_pairs={{0,2},{1,3},{2,4},{3,5},{8,10},{9,11},{10,12},{11,13},{12,14},{13,... | collective-permute-start | bytes 884744 | tf_op jit(solution)/shard_map/ppermute | solution.py:40
  54.1 12.0 %copy-start.30 = (bf16[1,384,384]{2,1,0:T(8,128)(2,1)S(1)}, bf16[1,384,384]{2,1,0:T(8,128)(2,1)}, u32[]{:S(2)}) copy-start(bf16[1,384,384]{2,1,0:T(8,128)(2,1)} %copy.18) | copy-start | bytes 884740
  54.2 24.0 %copy-start.29 = (bf16[1,384,384]{2,1,0:T(8,128)(2,1)S(1)}, bf16[1,384,384]{2,1,0:T(8,128)(2,1)}, u32[]{:S(2)}) copy-start(bf16[1,384,384]{2,1,0:T(8,128)(2,1)} %copy.17) | copy-start | bytes 884740
  59.2 12.9 %collective-permute-start.9 = (bf16[2,192,384]{2,1,0:T(8,128)(2,1)}, bf16[2,192,384]{2,1,0:T(8,128)(2,1)}, u32[]{:S(2)}, u32[]{:S(2)}) collective-permute-start(bf16[2,192,384]{2,1,0:T(8,128)(2,1)} %collective-permute-done.6), channel_id=1, source_target_pairs={{4,6},{5,7},{12,14},{13,15},{20,22},{21,23},{28,30},{29,31}} | collective-permute-start | bytes 884744 | tf_op jit(solution)/shard_map/ppermute | solution.py:40
  65.5 15.3 %collective-permute-start.18 = (bf16[2,2,192,384]{3,2,1,0:T(8,128)(2,1)S(1)}, bf16[2,2,192,384]{3,2,1,0:T(8,128)(2,1)S(1)}, u32[]{:S(2)}, u32[]{:S(2)}) collective-permute-start(bf16[2,2,192,384]{3,2,1,0:T(8,128)(2,1)S(1)} %broadcast_select_fusion), channel_id=1, source_target_pairs={{8,12},{9,13},{12,8},{13,9},{24,28},{25,29},{28,24},{29,25}} | collective-permute-start | bytes 1769480 | tf_op jit(solution)/shard_map/ppermute | solution.py:40
  66.2 12.0 %collective-permute-start.12 = (bf16[384,384]{1,0:T(8,128)(2,1)S(1)}, bf16[384,384]{1,0:T(8,128)(2,1)S(1)}, u32[]{:S(2)}, u32[]{:S(2)}) collective-permute-start(bf16[384,384]{1,0:T(8,128)(2,1)S(1)} %bitcast.68), channel_id=1, source_target_pairs={{0,24},{1,25},{2,26},{3,27},{4,28},{5,29},{6,30},{7,31},{8,16},{9,... | collective-permute-start | bytes 884744 | tf_op jit(solution)/shard_map/ppermute | solution.py:40
  72.0 8.7 %collective-permute-start.10 = (bf16[2,192,384]{2,1,0:T(8,128)(2,1)S(1)}, bf16[2,192,384]{2,1,0:T(8,128)(2,1)}, u32[]{:S(2)}, u32[]{:S(2)}) collective-permute-start(bf16[2,192,384]{2,1,0:T(8,128)(2,1)S(1)} %get-tuple-element.60), channel_id=1, source_target_pairs={{0,4},{1,5},{2,0},{3,1},{8,12},{9,13},{10,8},{11,9},{12,10},{13,11... | collective-permute-start | bytes 884744 | tf_op jit(solution)/shard_map/ppermute | solution.py:40
  78.1 9.2 %collective-permute-start.13 = (bf16[384,384]{1,0:T(8,128)(2,1)S(1)}, bf16[384,384]{1,0:T(8,128)(2,1)S(1)}, u32[]{:S(2)}, u32[]{:S(2)}) collective-permute-start(bf16[384,384]{1,0:T(8,128)(2,1)S(1)} %bitcast.67), channel_id=1, source_target_pairs={{0,16},{1,17},{2,18},{3,19},{4,20},{5,21},{6,22},{7,23},{8,24},{9,... | collective-permute-start | bytes 884744 | tf_op jit(solution)/shard_map/ppermute | solution.py:40
  80.8 27.6 %collective-permute-start.19 = (bf16[2,2,192,384]{3,2,1,0:T(8,128)(2,1)S(1)}, bf16[2,2,192,384]{3,2,1,0:T(8,128)(2,1)S(1)}, u32[]{:S(2)}, u32[]{:S(2)}) collective-permute-start(bf16[2,2,192,384]{3,2,1,0:T(8,128)(2,1)S(1)} %collective-permute-done.18), channel_id=1, source_target_pairs={{12,14},{13,15},{28,30},{29,31}} | collective-permute-start | bytes 1769480 | tf_op jit(solution)/shard_map/ppermute | solution.py:40
  87.3 21.0 %copy-start.20 = (bf16[384,384]{1,0:T(8,128)(2,1)}, bf16[384,384]{1,0:T(8,128)(2,1)S(1)}, u32[]{:S(2)}) copy-start(bf16[384,384]{1,0:T(8,128)(2,1)S(1)} %collective-permute-done.13.refs_20_) | copy-start | bytes 884740
  87.3 19.7 %collective-permute-start.14 = (bf16[2,192,384]{2,1,0:T(8,128)(2,1)}, bf16[2,192,384]{2,1,0:T(8,128)(2,1)}, u32[]{:S(2)}, u32[]{:S(2)}) collective-permute-start(bf16[2,192,384]{2,1,0:T(8,128)(2,1)} %collective-permute-done.11), channel_id=1, source_target_pairs={{4,6},{5,7},{12,14},{13,15},{20,22},{21,23},{28,30},{29,31}} | collective-permute-start | bytes 884744 | tf_op jit(solution)/shard_map/ppermute | solution.py:40
  107.0 9.7 %collective-permute-start.15 = (bf16[2,192,384]{2,1,0:T(8,128)(2,1)}, bf16[2,192,384]{2,1,0:T(8,128)(2,1)}, u32[]{:S(2)}, u32[]{:S(2)}) collective-permute-start(bf16[2,192,384]{2,1,0:T(8,128)(2,1)} %collective-permute-done.10), channel_id=1, source_target_pairs={{4,6},{5,7},{12,14},{13,15},{20,22},{21,23},{28,30},{29,31}} | collective-permute-start | bytes 884744 | tf_op jit(solution)/shard_map/ppermute | solution.py:40
  109.2 12.1 %collective-permute-start.20 = (bf16[2,2,192,384]{3,2,1,0:T(8,128)(2,1)S(1)}, bf16[2,2,192,384]{3,2,1,0:T(8,128)(2,1)}, u32[]{:S(2)}, u32[]{:S(2)}) collective-permute-start(bf16[2,2,192,384]{3,2,1,0:T(8,128)(2,1)S(1)} %get-tuple-element.72), channel_id=1, source_target_pairs={{8,10},{9,11},{24,26},{25,27}} | collective-permute-start | bytes 1769480 | tf_op jit(solution)/shard_map/ppermute | solution.py:40
  110.6 11.1 %copy-start.18 = (bf16[2,2,192,384]{3,2,1,0:T(8,128)(2,1)S(1)}, bf16[2,2,192,384]{3,2,1,0:T(8,128)(2,1)}, u32[]{:S(2)}) copy-start(bf16[2,2,192,384]{3,2,1,0:T(8,128)(2,1)} %copy-done.17) | copy-start | bytes 1769476
  110.6 10.5 %collective-permute-start.28 = (bf16[384,384]{1,0:T(8,128)(2,1)}, bf16[384,384]{1,0:T(8,128)(2,1)S(1)}, u32[]{:S(2)}, u32[]{:S(2)}) collective-permute-start(bf16[384,384]{1,0:T(8,128)(2,1)} %bitcast.66), channel_id=1, source_target_pairs={{0,8},{1,9},{2,10},{3,11},{4,12},{5,13},{6,14},{7,15},{8,0},{9,1},... | collective-permute-start | bytes 884744 | tf_op jit(solution)/shard_map/ppermute | solution.py:40
  116.8 7.0 %collective-permute-start.16 = (bf16[2,384,384]{2,1,0:T(8,128)(2,1)S(1)}, bf16[2,384,384]{2,1,0:T(8,128)(2,1)S(1)}, u32[]{:S(2)}, u32[]{:S(2)}) collective-permute-start(bf16[2,384,384]{2,1,0:T(8,128)(2,1)S(1)} %get-tuple-element.67.refs_16_), channel_id=1, source_target_pairs={{0,8},{1,9},{2,10},{3,11},{4,12},{5,13},{6,14},{7,15},{8,0},{9,1},... | collective-permute-start | bytes 1769480 | tf_op jit(solution)/shard_map/ppermute | solution.py:40
  120.6 3.2 %copy-start.4 = (bf16[2,192,384]{2,1,0:T(8,128)(2,1)}, bf16[2,192,384]{2,1,0:T(8,128)(2,1)S(1)}, u32[]{:S(2)}) copy-start(bf16[2,192,384]{2,1,0:T(8,128)(2,1)S(1)} %get-tuple-element.94.refs_11_) | copy-start | bytes 884740
  120.6 2.4 %collective-permute-start.22 = (bf16[2,192,384]{2,1,0:T(8,128)(2,1)S(1)}, bf16[2,192,384]{2,1,0:T(8,128)(2,1)S(1)}, u32[]{:S(2)}, u32[]{:S(2)}) collective-permute-start(bf16[2,192,384]{2,1,0:T(8,128)(2,1)S(1)} %get-tuple-element.100.refs_2_), channel_id=1, source_target_pairs={{0,8},{1,9},{2,10},{3,11},{4,12},{5,13},{6,14},{7,15},{8,0},{9,1},... | collective-permute-start | bytes 884744 | tf_op jit(solution)/shard_map/ppermute | solution.py:40
  120.7 2.4 %collective-permute-start.23 = (bf16[2,192,384]{2,1,0:T(8,128)(2,1)S(1)}, bf16[2,192,384]{2,1,0:T(8,128)(2,1)S(1)}, u32[]{:S(2)}, u32[]{:S(2)}) collective-permute-start(bf16[2,192,384]{2,1,0:T(8,128)(2,1)S(1)} %get-tuple-element.96.refs_3_), channel_id=1, source_target_pairs={{0,8},{1,9},{2,10},{3,11},{4,12},{5,13},{6,14},{7,15},{8,0},{9,1},... | collective-permute-start | bytes 884744 | tf_op jit(solution)/shard_map/ppermute | solution.py:40
  121.2 2.4 %collective-permute-start.24 = (bf16[2,192,384]{2,1,0:T(8,128)(2,1)S(1)}, bf16[2,192,384]{2,1,0:T(8,128)(2,1)S(1)}, u32[]{:S(2)}, u32[]{:S(2)}) collective-permute-start(bf16[2,192,384]{2,1,0:T(8,128)(2,1)S(1)} %get-tuple-element.101.refs_6_), channel_id=1, source_target_pairs={{0,8},{1,9},{2,10},{3,11},{4,12},{5,13},{6,14},{7,15},{8,0},{9,1},... | collective-permute-start | bytes 884744 | tf_op jit(solution)/shard_map/ppermute | solution.py:40
  121.3 5.5 %collective-permute-start.29 = (bf16[2,384,384]{2,1,0:T(8,128)(2,1)S(1)}, bf16[2,384,384]{2,1,0:T(8,128)(2,1)S(1)}, u32[]{:S(2)}, u32[]{:S(2)}) collective-permute-start(bf16[2,384,384]{2,1,0:T(8,128)(2,1)S(1)} %get-tuple-element.76.refs_14_), channel_id=1, source_target_pairs={{0,8},{1,9},{2,10},{3,11},{4,12},{5,13},{6,14},{7,15},{8,0},{9,1},... | collective-permute-start | bytes 1769480 | tf_op jit(solution)/shard_map/ppermute | solution.py:40
  122.9 3.8 %copy-start.3 = (bf16[2,2,192,384]{3,2,1,0:T(8,128)(2,1)}, bf16[2,2,192,384]{3,2,1,0:T(8,128)(2,1)S(1)}, u32[]{:S(2)}) copy-start(bf16[2,2,192,384]{3,2,1,0:T(8,128)(2,1)S(1)} %select_select_fusion.refs_0_) | copy-start | bytes 1769476
  123.0 3.8 %copy-start.22 = (bf16[2,192,384]{2,1,0:T(8,128)(2,1)}, bf16[2,192,384]{2,1,0:T(8,128)(2,1)S(1)}, u32[]{:S(2)}) copy-start(bf16[2,192,384]{2,1,0:T(8,128)(2,1)S(1)} %collective-permute-done.22.refs_4_) | copy-start | bytes 884740
  123.0 3.8 %collective-permute-start.21 = (bf16[2,2,192,384]{3,2,1,0:T(8,128)(2,1)S(1)}, bf16[2,2,192,384]{3,2,1,0:T(8,128)(2,1)S(1)}, u32[]{:S(2)}, u32[]{:S(2)}) collective-permute-start(bf16[2,2,192,384]{3,2,1,0:T(8,128)(2,1)S(1)} %select_select_fusion.refs_0_), channel_id=1, source_target_pairs={{0,8},{1,9},{2,10},{3,11},{4,12},{5,13},{6,14},{7,15},{8,0},{9,1},... | collective-permute-start | bytes 1769480 | tf_op jit(solution)/shard_map/ppermute | solution.py:40
  123.1 3.7 %copy-start.23 = (bf16[2,192,384]{2,1,0:T(8,128)(2,1)}, bf16[2,192,384]{2,1,0:T(8,128)(2,1)S(1)}, u32[]{:S(2)}) copy-start(bf16[2,192,384]{2,1,0:T(8,128)(2,1)S(1)} %collective-permute-done.23.refs_5_) | copy-start | bytes 884740
  123.1 2.3 %collective-permute-start.25 = (bf16[2,192,384]{2,1,0:T(8,128)(2,1)S(1)}, bf16[2,192,384]{2,1,0:T(8,128)(2,1)S(1)}, u32[]{:S(2)}, u32[]{:S(2)}) collective-permute-start(bf16[2,192,384]{2,1,0:T(8,128)(2,1)S(1)} %get-tuple-element.95.refs_7_), channel_id=1, source_target_pairs={{0,8},{1,9},{2,10},{3,11},{4,12},{5,13},{6,14},{7,15},{8,0},{9,1},... | collective-permute-start | bytes 884744 | tf_op jit(solution)/shard_map/ppermute | solution.py:40
  123.6 3.1 %collective-permute-start.26 = (bf16[2,192,384]{2,1,0:T(8,128)(2,1)S(1)}, bf16[2,192,384]{2,1,0:T(8,128)(2,1)S(1)}, u32[]{:S(2)}, u32[]{:S(2)}) collective-permute-start(bf16[2,192,384]{2,1,0:T(8,128)(2,1)S(1)} %get-tuple-element.102.refs_10_), channel_id=1, source_target_pairs={{0,8},{1,9},{2,10},{3,11},{4,12},{5,13},{6,14},{7,15},{8,0},{9,1},... | collective-permute-start | bytes 884744 | tf_op jit(solution)/shard_map/ppermute | solution.py:40
  123.8 2.9 %collective-permute-start.27 = (bf16[2,192,384]{2,1,0:T(8,128)(2,1)S(1)}, bf16[2,192,384]{2,1,0:T(8,128)(2,1)S(1)}, u32[]{:S(2)}, u32[]{:S(2)}) collective-permute-start(bf16[2,192,384]{2,1,0:T(8,128)(2,1)S(1)} %get-tuple-element.94.refs_11_), channel_id=1, source_target_pairs={{0,8},{1,9},{2,10},{3,11},{4,12},{5,13},{6,14},{7,15},{8,0},{9,1},... | collective-permute-start | bytes 884744 | tf_op jit(solution)/shard_map/ppermute | solution.py:40
  125.5 14.1 %collective-permute-start.17 = (bf16[2,192,384]{2,1,0:T(8,128)(2,1)}, bf16[2,192,384]{2,1,0:T(8,128)(2,1)S(1)}, u32[]{:S(2)}, u32[]{:S(2)}) collective-permute-start(bf16[2,192,384]{2,1,0:T(8,128)(2,1)} %get-tuple-element.68), channel_id=1, source_target_pairs={{0,1},{1,0},{2,3},{3,2},{4,5},{5,4},{6,7},{7,6},{8,9},{9,8},{10,11... | collective-permute-start | bytes 884744 | tf_op jit(solution)/shard_map/ppermute | solution.py:40
  136.8 9.4 %collective-permute-start.31 = (bf16[384,384]{1,0:T(8,128)(2,1)}, bf16[384,384]{1,0:T(8,128)(2,1)S(1)}, u32[]{:S(2)}, u32[]{:S(2)}) collective-permute-start(bf16[384,384]{1,0:T(8,128)(2,1)} %get-tuple-element.80), channel_id=1, source_target_pairs={{0,16},{1,17},{2,18},{3,19},{4,20},{5,21},{6,22},{7,23},{8,24},{9,... | collective-permute-start | bytes 884744 | tf_op jit(solution)/shard_map/ppermute | solution.py:40
  138.9 13.8 %collective-permute-start.32 = (bf16[384,384]{1,0:T(8,128)(2,1)}, bf16[384,384]{1,0:T(8,128)(2,1)S(1)}, u32[]{:S(2)}, u32[]{:S(2)}) collective-permute-start(bf16[384,384]{1,0:T(8,128)(2,1)} %get-tuple-element.81), channel_id=1, source_target_pairs={{0,24},{1,25},{2,26},{3,27},{4,28},{5,29},{6,30},{7,31},{8,16},{9,... | collective-permute-start | bytes 884744 | tf_op jit(solution)/shard_map/ppermute | solution.py:40
  139.3 13.4 %collective-permute-start.30 = (bf16[384,384]{1,0:T(8,128)(2,1)}, bf16[384,384]{1,0:T(8,128)(2,1)S(1)}, u32[]{:S(2)}, u32[]{:S(2)}) collective-permute-start(bf16[384,384]{1,0:T(8,128)(2,1)} %get-tuple-element.79), channel_id=1, source_target_pairs={{0,8},{1,9},{2,10},{3,11},{4,12},{5,13},{6,14},{7,15},{8,0},{9,1},... | collective-permute-start | bytes 884744 | tf_op jit(solution)/shard_map/ppermute | solution.py:40
  139.6 13.1 %copy-start.31 = (bf16[384,384]{1,0:T(8,128)(2,1)S(1)}, bf16[384,384]{1,0:T(8,128)(2,1)}, u32[]{:S(2)}) copy-start(bf16[384,384]{1,0:T(8,128)(2,1)} %get-tuple-element.78) | copy-start | bytes 884740
  (18 other events, 33.5 us)

commit v5 on v4

--- a/solution.py
+++ b/solution.py
@@ -168,10 +168,11 @@
     for key in keys:
         for t in range(groups):
             if key[0] == top:
-                sig_in[key, t] = take(moms)
+                sig_in[key, t] = take(1)
             else:
                 (ref,) = take(1)
                 sig_in[key, t] = [ref.at[q] for q in range(moms)]
+    gathered = [None] + take(moms - 1)
     diag_in = {(b, t): take(1)[0] for b in range(moments) for t in range(groups)}
     right_in, outs = take(rows), take(rows)
     sig, diag, right, solved, right_sems, sems, out_sems = refs
@@ -190,9 +191,13 @@
             if key[0] == b and row > key[1]:
                 for q in range(moms):
                     at = pl.ds(pl.multiple_of((y ^ q) * half, half), half)
+                    if b == top and q > 0:
+                        source = gathered[q].at[(row % groups) * plan.cols + key[1]]
+                    else:
+                        source = sig_in[key, t][q]
                     for p in range(2):
                         lane = pl.ds((2 * key[1] + p) * side, side)
-                        add(sig_in[key, t][q].at[p], sig.at[row, at, lane])
+                        add(source.at[p], sig.at[row, at, lane])
         return made
 
     for s in range(rows):
@@ -279,8 +284,13 @@
     right = right_side.reshape(moments, side, 2, groups, width).transpose(0, 3, 1, 2, 4)
     right = right.reshape(rows, side, 2 * width)
     right_all = [lax.dynamic_index_in_dim(right, r ^ s, 0, keepdims=False) for s in range(rows)]
-    lesser_all, partner_all, right_all, diag = lax.optimization_barrier(
-        (lesser_all, partner_all, right_all, diag)
+    right_all = after(right_all, lesser_all[1:])
+    right_came = right_all[:1] + [exchange_row(right_all[s], s) for s in range(1, rows)]
+    diag_all = [
+        diag[b] if t == 0 else exchange_row(diag[b], t) for b in range(moments) for t in range(groups)
+    ]
+    lesser_all, partner_all, right_came, diag_all = lax.optimization_barrier(
+        (lesser_all, partner_all, right_came, diag_all)
     )
 
     high = jnp.maximum(triples[..., 0], triples[..., 1])
@@ -356,57 +366,35 @@
         log.append(make(value))
         return log[-1]
 
-    extra = []
-
-    def fill():
-        if extra:
-            extra.pop(0)()
-
-    right_came = [right_all[0]] + [None] * (rows - 1)
-
-    def right_step(s):
-        def run():
-            right_came[s] = issue(lambda v: exchange_row(v, s), right_all[s])
-
-        return run
-
-    diag_came = {}
-
-    def diag_step(b, t):
-        def run():
-            diag_came[b, t] = issue(lambda v: exchange_row(v, t), diag[b])
-
-        return run
-
-    extra += [right_step(s) for s in reversed(range(1, rows))]
-    extra += [diag_step(b, t) for b in range(moments) for t in range(1, groups)]
-
     for q in range(moms):
         own.append(by_block(came[q]))
-        for key in plan.keys:
-            if key[0] == top:
-                found.setdefault((key, key[1]), []).append(own[q][top])
+    members = [
+        [(b * groups + g) * cols + c for g in range(groups) for c in range(cols)]
+        for b in range(moments)
+    ]
+    gathered = [
+        lax.all_gather(own[q][top], AXES[:2], axis_index_groups=members) for q in range(1, moms)
+    ]
+    for key in plan.keys:
+        if key[0] == top:
+            found[key, key[1]] = own[0][top]
     joint_values = [jnp.stack([own[k][b] for k in range(moms)]) for b in range(moments)]
     for key in plan.keys:
         if key[0] < top:
             found[key, key[1]] = joint_values[key[0]]
 
-    def split_step(q, step):
+    def split_step(step):
         def run():
-            value = issue(lambda v: spread(step, v), own[q])
+            value = issue(lambda v: spread(step, v), own[0])
             for key, to in step.values():
-                found.setdefault((key, to), []).append(value)
+                found[key, to] = value
 
         return run
 
-    def split_relay(q, key):
+    def split_relay(key):
         def run():
-            value = found[key, last - 1][q]
-            if q + 1 < moms:
-                value = after(value, came[q + 1])
-            value = issue(lambda v: relay(v, key), value)
-            found.setdefault((key, last), []).append(value)
-            fill()
+            value = after(found[key, last - 1], came[1:])
+            found[key, last] = issue(lambda v: relay(v, key), value)
 
         return run
 
@@ -414,7 +402,7 @@
         def run():
             value = issue(lambda v: spread(step, v), joint_values)
             for key, to in step.values():
-                found[key, to] = [value[k] for k in range(moms)] if key[0] == top else value
+                found[key, to] = value[0] if key[0] == top else value
 
         return run
 
@@ -425,23 +413,12 @@
         return run
 
     relays = sorted([key for key in plan.keys if key[1] < last - 1], key=lambda key: -key[1])
-    schedule, waiting = [], []
-    for q in range(moms):
-        for n, step in enumerate(plan.direct(split)):
-            if waiting:
-                schedule.append(waiting.pop(0))
-            schedule.append(split_step(q, step))
-        schedule += waiting
-        waiting = [split_relay(q, key) for key in relays if key[0] == top]
-    steps = [joint_step(step) for step in plan.direct(joint)]
-    schedule = schedule[:-1] + steps[:1] + schedule[-1:]
-    low_relays = [joint_relay(key) for key in relays if key[0] < top]
-    schedule += waiting[:1] + (steps[1:] + low_relays if cols > 4 else low_relays)
-    schedule += waiting[1:] + (steps[1:] if cols <= 4 else [])
+    schedule = [split_step(step) for step in plan.direct(split)]
+    schedule += [split_relay(key) for key in relays if key[0] == top]
+    schedule += [joint_step(step) for step in plan.direct(joint)]
+    schedule += [joint_relay(key) for key in relays if key[0] < top]
     for run in schedule:
         run()
-    while extra:
-        fill()
 
     whole = [slots[b] for b in range(moments)]
     for q in range(1, moms):
@@ -459,15 +436,10 @@
 
     sig_all = []
     for key in plan.keys:
-        if key[0] == top:
-            mine = [lax.select_n(z, *[found[key, c][q] for c in range(cols)]) for q in range(moms)]
-        else:
-            mine = [lax.select_n(z, *[found[key, c] for c in range(cols)])]
+        mine = lax.select_n(z, *[found[key, c] for c in range(cols)])
         for t in range(groups):
-            sig_all += mine if t == 0 else [exchange_row(value, t) for value in mine]
-    diag_all = [
-        diag[b] if t == 0 else diag_came[b, t] for b in range(moments) for t in range(groups)
-    ]
+            sig_all.append(mine if t == 0 else exchange_row(mine, t))
+    sig_all += gathered
     most = 2 + 4 * moms * (cols - 1)
     solved = pl.pallas_call(
         functools.partial(solve_kernel, plan),

time: 158 us -> 175 us (1.11)
  waiting for transfers between devices: 75.9 us -> 98.6 us
  starting transfers between devices: 37 us -> 22.8 us
  between operations: 1.24 us -> 14.6 us
  other arithmetic: 7.08 us -> 4.35 us
  local copies, waits for them, and re-layouts: 18.2 us -> 16.3 us
    ppermute x33 -> x26, waiting for transfers between devices: 75.9 us -> 98.5 us  [send(): return lax.ppermute(value, AXES, pairs)]
    ppermute x33 -> x26, starting transfers between devices: 37 us -> 22.7 us  [send(): return lax.ppermute(value, AXES, pairs)]
    select_n x2, other arithmetic: 3.07 us -> 0.28 us  [on_device(): mine = lax.select_n(z, *[found[key, c] for c in range(cols)])]
    dynamic_slice x5, local copies, waits for them, and re-layouts: 3.77 us -> 1.67 us  [on_device(): lax.dynamic_index_in_dim(right, r ^ s, 0, keepdims=False)]
    unnamed x67 -> x63, local copies, waits for them, and re-layouts: 6.22 us -> 6.45 us
  transfers between devices with their start and end apart: 33 -> 27, of which waited for: 13 -> 11; matrix products, arithmetic and copies ran while one was open for 10% -> 4% of each run, Pallas kernels for 7% -> 6%
where the time goes in v5:
time: 175 us; the launch traced here: 174 us
  waiting for transfers between devices  98.6 us (56%)
  starting transfers between devices  22.8 us (13%)
  Pallas kernels  17.4 us (10%)
  local copies, waits for them, and re-layouts  16.3 us (9%)
  between operations  14.6 us (8%)
  other arithmetic  4.35 us (2%)
    ppermute x26, waiting for transfers between devices, send(): return lax.ppermute(value, AXES, pairs)  98.5 us
    ppermute x26, starting transfers between devices, send(): return lax.ppermute(value, AXES, pairs)  22.7 us
    pallas_call x1, Pallas kernels, on_device(): pl.pallas_call(functools.partial(solve_kernel, plan), out_shape=[jax.Shap...  8.21 us
    unnamed x63, local copies, waits for them, and re-layouts  6.45 us
    pallas_call x1, Pallas kernels, on_device(): pl.pallas_call(functools.partial(sigma_kernel, plan, pair_count, chunks),...  6.24 us
  transfers between devices with their start and end apart: 27, of which 11 were waited for; matrix products, arithmetic and copies ran while one was open for 4% of the time, Pallas kernels for 6%

profile of v5, /device:TPU:25, one launch (start us, length us, event | category | flops | bytes accessed | tf_op | source)
XLA Modules:
  0.0 174.0 jit_solution(11506222739273446625)
XLA Ops:
  7.2 2.0 %constant_dynamic-slice_fusion.4 = bf16[2,2,192,384]{3,2,1,0:T(8,128)(2,1)} fusion(bf16[2,2,384,384]{3,2,1,0:T(8,128)(2,1)} %refs_0_, s32[]{:T(128)S(6)} %select_n.271), kind=kLoop, calls=%fused_computation.34 | loop fusion | bytes 1179652 | tf_op jit(solution)/shard_map/dynamic_slice | solution.py:270
  9.3 0.8 copy.22
  10.1 0.9 dynamic-slice_bitcast_fusion.1
  11.0 0.9 dynamic-slice_bitcast_fusion
  11.9 1.2 collective-permute-start.5
  13.1 1.2 collective-permute-start
  14.6 2.0 %copy.24 = bf16[2,384,2,384]{1,3,2,0:T(8,128)(2,1)S(1)} copy(bf16[2,384,2,384]{3,2,1,0:T(2,128)(2,1)S(1)} %copy-done.11) | data formatting | bytes 2359296 | tf_op jit(solution)/shard_map/optimization_barrier | solution.py:246
  16.7 9.7 %collective-permute-done.5 = bf16[2,384,384]{2,1,0:T(8,128)(2,1)} collective-permute-done((bf16[2,384,384]{2,1,0:T(8,128)(2,1)}, bf16[2,384,384]{2,1,0:T(8,128)(2,1)}, u32[]{:S(2)}, u32[]{:S(2)}) %collective-permute-start.5) | collective-permute-done | bytes 589856 | tf_op jit(solution)/shard_map/ppermute | solution.py:40
  26.4 1.4 bitcast_select_fusion
  27.8 1.6 collective-permute-start.6
  29.6 0.9 copy.26
  31.2 0.6 fusion.3.quads
  31.8 0.8 collective-permute-start.2
  32.6 1.2 collective-permute-start.3
  33.8 6.2 %collective-permute-done.1.refs_3_ = bf16[2,2,192,384]{3,2,1,0:T(8,128)(2,1)} collective-permute-done((bf16[2,2,192,384]{3,2,1,0:T(8,128)(2,1)}, bf16[2,2,192,384]{3,2,1,0:T(8,128)(2,1)}, u32[]{:S(2)}, u32[]{:S(2)}) %collective-permute-start.1) | collective-permute-done | bytes 589856 | tf_op jit(solution)/shard_map/ppermute | solution.py:40
  39.9 2.0 %collective-permute-start.4 = (bf16[384,384]{1,0:T(8,128)(2,1)S(1)}, bf16[384,384]{1,0:T(8,128)(2,1)S(1)}, u32[]{:S(2)}, u32[]{:S(2)}) collective-permute-start(bf16[384,384]{1,0:T(8,128)(2,1)S(1)} %bitcast.61), channel_id=1, source_target_pairs={{0,24},{1,25},{2,26},{3,27},{4,28},{5,29},{6,30},{7,31},{8,16},{9,... | collective-permute-start | bytes 884744 | tf_op jit(solution)/shard_map/ppermute | solution.py:40
  41.9 0.6 pad_add_fusion.place
  42.5 0.6 slice_bitcast_fusion.1.thirds
  43.1 5.8 %collective-permute-done.4.refs_16_ = bf16[384,384]{1,0:T(8,128)(2,1)S(1)} collective-permute-done((bf16[384,384]{1,0:T(8,128)(2,1)S(1)}, bf16[384,384]{1,0:T(8,128)(2,1)S(1)}, u32[]{:S(2)}, u32[]{:S(2)}) %collective-permute-start.4) | collective-permute-done | bytes 294944 | tf_op jit(solution)/shard_map/ppermute | solution.py:40
  48.9 0.7 copy-done.17
  49.6 6.2 %self_energy.1 = (bf16[2,192,384]{2,1,0:T(8,128)(2,1)}, bf16[2,192,384]{2,1,0:T(8,128)(2,1)}, bf16[2,192,384]{2,1,0:T(8,128)(2,1)}, bf16[2,192,384]{2,1,0:T(8,128)(2,1)}) custom-call(s32[3]{0:T(128)} %pad_add_fusion.place, s32[4,8]{1,0:T(4,128)} %fusion.3.quads, s32[4,8]{1,0:T(4,128)} %slice_bitcast_fusion.1.thirds, bf16[2,2,384,384]{3,2,1,0:T(8,128)(2,1)} %refs_0_, ...), custom_call_target="tpu_custom_call" | custom-call | tf_op jit(solution)/shard_map/self_energy/pallas_call | solution.py:300
  55.9 1.3 collective-permute-start.8
  57.2 0.7 collective-permute-start.10
  57.9 5.5 %collective-permute-done.8.refs_2_ = bf16[2,192,384]{2,1,0:T(8,128)(2,1)S(1)} collective-permute-done((bf16[2,192,384]{2,1,0:T(8,128)(2,1)}, bf16[2,192,384]{2,1,0:T(8,128)(2,1)S(1)}, u32[]{:S(2)}, u32[]{:S(2)}) %collective-permute-start.8) | collective-permute-done | bytes 294944 | tf_op jit(solution)/shard_map/ppermute | solution.py:40
  63.4 0.9 broadcast_select_fusion.1
  64.3 0.8 collective-permute-start.9
  65.2 0.7 collective-permute-start.11
  65.9 1.3 collective-permute-start.13
  67.4 0.7 collective-permute-start.12
  68.1 24.7 %collective-permute-done.13 = bf16[2,192,384]{2,1,0:T(8,128)(2,1)S(1)} collective-permute-done((bf16[2,192,384]{2,1,0:T(8,128)(2,1)S(1)}, bf16[2,192,384]{2,1,0:T(8,128)(2,1)S(1)}, u32[]{:S(2)}, u32[]{:S(2)}) %collective-permute-start.13) | collective-permute-done | bytes 294944 | tf_op jit(solution)/shard_map/ppermute | solution.py:40
  92.8 1.3 collective-permute-start.17
  94.1 1.3 collective-permute-start.14
  95.4 21.9 %collective-permute-done.17 = bf16[2,192,384]{2,1,0:T(8,128)(2,1)S(1)} collective-permute-done((bf16[2,192,384]{2,1,0:T(8,128)(2,1)S(1)}, bf16[2,192,384]{2,1,0:T(8,128)(2,1)S(1)}, u32[]{:S(2)}, u32[]{:S(2)}) %collective-permute-start.17) | collective-permute-done | bytes 294944 | tf_op jit(solution)/shard_map/ppermute | solution.py:40
  117.4 0.7 collective-permute-start.18
  118.1 5.6 %collective-permute-done.14 = bf16[2,192,384]{2,1,0:T(8,128)(2,1)S(1)} collective-permute-done((bf16[2,192,384]{2,1,0:T(8,128)(2,1)S(1)}, bf16[2,192,384]{2,1,0:T(8,128)(2,1)S(1)}, u32[]{:S(2)}, u32[]{:S(2)}) %collective-permute-start.14) | collective-permute-done | bytes 294944 | tf_op jit(solution)/shard_map/ppermute | solution.py:40
  123.7 0.7 copy-done.27
  124.4 1.3 collective-permute-start.15
  125.8 9.3 %collective-permute-done.15 = bf16[2,2,192,384]{3,2,1,0:T(8,128)(2,1)S(1)} collective-permute-done((bf16[2,2,192,384]{3,2,1,0:T(8,128)(2,1)S(1)}, bf16[2,2,192,384]{3,2,1,0:T(8,128)(2,1)S(1)}, u32[]{:S(2)}, u32[]{:S(2)}) %collective-permute-start.15) | collective-permute-done | bytes 589856 | tf_op jit(solution)/shard_map/ppermute | solution.py:40
  136.6 1.5 collective-permute-start.16
  139.4 8.2 %substitution.1 = (bf16[384,384]{1,0:T(8,128)(2,1)}, bf16[384,384]{1,0:T(8,128)(2,1)}, bf16[384,384]{1,0:T(8,128)(2,1)}, bf16[384,384]{1,0:T(8,128)(2,1)}) custom-call(s32[3]{0:T(128)} %pad_add_fusion.place, bf16[2,2,192,384]{3,2,1,0:T(8,128)(2,1)} %copy-done.4, bf16[2,2,192,384]{3,2,1,0:T(8,128)(2,1)} %copy-done.13, bf16[2,192,384]{2,1,0:T(8,128)(2,1)} %copy-done.9, ...), custom_call_target="tpu_custom_call" | custom-call | tf_op jit(solution)/shard_map/substitution/pallas_call | solution.py:444
  147.6 1.2 collective-permute-start.24
  148.9 0.9 collective-permute-start.25
  149.9 0.7 copy-done.18
  150.6 2.9 %place_sigma.1 = bf16[2,2,384,384]{3,2,1,0:T(8,128)(2,1)} custom-call(s32[3]{0:T(128)} %pad_add_fusion.place, bf16[2,192,384]{2,1,0:T(8,128)(2,1)} %get-tuple-element.52.refs_0_, bf16[2,192,384]{2,1,0:T(8,128)(2,1)} %get-tuple-element.53.refs_1_, bf16[2,192,384]{2,1,0:T(8,128)(2,1)} %copy-done.6, bf16[2,192,384]{2,1,0:T(8,128)(2,1)} %copy-done.18), custom_call_target="tpu_custom_call" | custom-call | tf_op jit(solution)/shard_map/place_sigma/pallas_call | solution.py:428
  153.6 2.5 %collective-permute-done.24 = bf16[384,384]{1,0:T(8,128)(2,1)S(1)} collective-permute-done((bf16[384,384]{1,0:T(8,128)(2,1)}, bf16[384,384]{1,0:T(8,128)(2,1)S(1)}, u32[]{:S(2)}, u32[]{:S(2)}) %collective-permute-start.24) | collective-permute-done | bytes 294944 | tf_op jit(solution)/shard_map/ppermute | solution.py:40
  156.1 6.9 %collective-permute-done.25 = bf16[384,384]{1,0:T(8,128)(2,1)S(1)} collective-permute-done((bf16[384,384]{1,0:T(8,128)(2,1)}, bf16[384,384]{1,0:T(8,128)(2,1)S(1)}, u32[]{:S(2)}, u32[]{:S(2)}) %collective-permute-start.25) | collective-permute-done | bytes 294944 | tf_op jit(solution)/shard_map/ppermute | solution.py:40
  163.4 0.8 copy.30
  164.3 2.8 %copy.32 = bf16[2,384,2,384]{3,2,1,0:T(2,128)(2,1)} copy(bf16[2,384,2,384]{1,3,2,0:T(8,128)(2,1)S(1)} %bitcast.54) | data formatting | bytes 2359296
  (98 shorter events, 5.1 us)
Async XLA Ops:
  7.2 2.1 %copy-start.10 = (bf16[2,2,384,384]{3,2,1,0:T(8,128)(2,1)S(1)}, bf16[2,2,384,384]{3,2,1,0:T(8,128)(2,1)}, u32[]{:S(2)}) copy-start(bf16[2,2,384,384]{3,2,1,0:T(8,128)(2,1)} %param.6) | copy-start | bytes 3538948
  7.2 131.4 %all-gather.3.cloned.1.call-start = ((), (), s32[]{:S(2)}) async-start(), calls=%async_computation | async-start | bytes 2654208 | tf_op jit(solution)/shard_map/all_gather | solution.py:376
  9.3 1.7 copy-start.12
  10.1 1.8 %copy-start = (bf16[2,2,384,384]{2,3,1,0:T(8,128)(2,1)}, bf16[2,2,384,384]{2,3,1,0:T(8,128)(2,1)S(1)}, u32[]{:S(2)}) copy-start(bf16[2,2,384,384]{2,3,1,0:T(8,128)(2,1)S(1)} %copy.22) | copy-start | bytes 3538948
  10.1 4.5 %copy-start.11 = (bf16[2,384,2,384]{3,2,1,0:T(2,128)(2,1)S(1)}, bf16[2,384,2,384]{3,2,1,0:T(2,128)(2,1)}, u32[]{:S(2)}) copy-start(bf16[2,384,2,384]{3,2,1,0:T(2,128)(2,1)} %param.9) | copy-start | bytes 3538948
  11.9 14.5 %collective-permute-start.5 = (bf16[2,384,384]{2,1,0:T(8,128)(2,1)}, bf16[2,384,384]{2,1,0:T(8,128)(2,1)}, u32[]{:S(2)}, u32[]{:S(2)}) collective-permute-start(bf16[2,384,384]{2,1,0:T(8,128)(2,1)} %dynamic-slice_bitcast_fusion), channel_id=1, source_target_pairs={{0,16},{1,17},{2,18},{3,19},{4,20},{5,21},{6,22},{7,23},{8,24},{9,... | collective-permute-start | bytes 1769480 | tf_op jit(solution)/shard_map/ppermute | solution.py:40
  13.1 18.7 %collective-permute-start = (bf16[2,2,192,384]{3,2,1,0:T(8,128)(2,1)}, bf16[2,2,192,384]{3,2,1,0:T(8,128)(2,1)}, u32[]{:S(2)}, u32[]{:S(2)}) collective-permute-start(bf16[2,2,192,384]{3,2,1,0:T(8,128)(2,1)} %constant_dynamic-slice_fusion.4), channel_id=1, source_target_pairs={{0,1},{1,0},{2,3},{3,2},{4,5},{5,4},{6,7},{7,6},{8,9},{9,8},{10,11... | collective-permute-start | bytes 1769480 | tf_op jit(solution)/shard_map/ppermute | solution.py:40
  14.3 25.6 %collective-permute-start.1 = (bf16[2,2,192,384]{3,2,1,0:T(8,128)(2,1)}, bf16[2,2,192,384]{3,2,1,0:T(8,128)(2,1)}, u32[]{:S(2)}, u32[]{:S(2)}) collective-permute-start(bf16[2,2,192,384]{3,2,1,0:T(8,128)(2,1)} %dynamic-slice_bitcast_fusion.1), channel_id=1, source_target_pairs={{0,1},{1,0},{2,3},{3,2},{4,5},{5,4},{6,7},{7,6},{8,9},{9,8},{10,11... | collective-permute-start | bytes 1769480 | tf_op jit(solution)/shard_map/ppermute | solution.py:40
  27.8 1.8 %copy-start.2 = (bf16[2,384,384]{2,1,0:T(8,128)(2,1)}, bf16[2,384,384]{2,1,0:T(8,128)(2,1)S(1)}, u32[]{:S(2)}) copy-start(bf16[2,384,384]{2,1,0:T(8,128)(2,1)S(1)} %get-tuple-element.66.refs_11_) | copy-start | bytes 1769476
  27.8 1.8 %copy-start.3 = (bf16[2,384,384]{2,1,0:T(8,128)(2,1)}, bf16[2,384,384]{2,1,0:T(8,128)(2,1)S(1)}, u32[]{:S(2)}) copy-start(bf16[2,384,384]{2,1,0:T(8,128)(2,1)S(1)} %get-tuple-element.64.refs_9_) | copy-start | bytes 1769476
  27.8 21.1 %collective-permute-start.6 = (bf16[2,384,384]{2,1,0:T(8,128)(2,1)S(1)}, bf16[2,384,384]{2,1,0:T(8,128)(2,1)}, u32[]{:S(2)}, u32[]{:S(2)}) collective-permute-start(bf16[2,384,384]{2,1,0:T(8,128)(2,1)S(1)} %get-tuple-element.64.refs_9_), channel_id=1, source_target_pairs={{0,8},{1,9},{2,10},{3,11},{4,12},{5,13},{6,14},{7,15},{8,0},{9,1},... | collective-permute-start | bytes 1769480 | tf_op jit(solution)/shard_map/ppermute | solution.py:40
  29.4 19.5 %collective-permute-start.7 = (bf16[2,384,384]{2,1,0:T(8,128)(2,1)S(1)}, bf16[2,384,384]{2,1,0:T(8,128)(2,1)}, u32[]{:S(2)}, u32[]{:S(2)}) collective-permute-start(bf16[2,384,384]{2,1,0:T(8,128)(2,1)S(1)} %get-tuple-element.66.refs_11_), channel_id=1, source_target_pairs={{0,8},{1,9},{2,10},{3,11},{4,12},{5,13},{6,14},{7,15},{8,0},{9,1},... | collective-permute-start | bytes 1769480 | tf_op jit(solution)/shard_map/ppermute | solution.py:40
  31.8 11.3 %collective-permute-start.2 = (bf16[384,384]{1,0:T(8,128)(2,1)S(1)}, bf16[384,384]{1,0:T(8,128)(2,1)S(1)}, u32[]{:S(2)}, u32[]{:S(2)}) collective-permute-start(bf16[384,384]{1,0:T(8,128)(2,1)S(1)} %bitcast.63), channel_id=1, source_target_pairs={{0,8},{1,9},{2,10},{3,11},{4,12},{5,13},{6,14},{7,15},{8,0},{9,1},... | collective-permute-start | bytes 884744 | tf_op jit(solution)/shard_map/ppermute | solution.py:40
  32.6 10.6 %collective-permute-start.3 = (bf16[384,384]{1,0:T(8,128)(2,1)S(1)}, bf16[384,384]{1,0:T(8,128)(2,1)S(1)}, u32[]{:S(2)}, u32[]{:S(2)}) collective-permute-start(bf16[384,384]{1,0:T(8,128)(2,1)S(1)} %bitcast.62), channel_id=1, source_target_pairs={{0,16},{1,17},{2,18},{3,19},{4,20},{5,21},{6,22},{7,23},{8,24},{9,... | collective-permute-start | bytes 884744 | tf_op jit(solution)/shard_map/ppermute | solution.py:40
  39.9 9.0 %collective-permute-start.4 = (bf16[384,384]{1,0:T(8,128)(2,1)S(1)}, bf16[384,384]{1,0:T(8,128)(2,1)S(1)}, u32[]{:S(2)}, u32[]{:S(2)}) collective-permute-start(bf16[384,384]{1,0:T(8,128)(2,1)S(1)} %bitcast.61), channel_id=1, source_target_pairs={{0,24},{1,25},{2,26},{3,27},{4,28},{5,29},{6,30},{7,31},{8,16},{9,... | collective-permute-start | bytes 884744 | tf_op jit(solution)/shard_map/ppermute | solution.py:40
  43.1 5.8 %copy-start.15 = (bf16[384,384]{1,0:T(8,128)(2,1)}, bf16[384,384]{1,0:T(8,128)(2,1)S(1)}, u32[]{:S(2)}) copy-start(bf16[384,384]{1,0:T(8,128)(2,1)S(1)} %collective-permute-done.2.refs_14_) | copy-start | bytes 884740
  43.1 5.8 %copy-start.16 = (bf16[384,384]{1,0:T(8,128)(2,1)}, bf16[384,384]{1,0:T(8,128)(2,1)S(1)}, u32[]{:S(2)}) copy-start(bf16[384,384]{1,0:T(8,128)(2,1)S(1)} %collective-permute-done.3.refs_15_) | copy-start | bytes 884740
  55.9 8.4 %copy-start.14 = (bf16[2,192,384]{2,1,0:T(8,128)(2,1)S(1)}, bf16[2,192,384]{2,1,0:T(8,128)(2,1)}, u32[]{:S(2)}) copy-start(bf16[2,192,384]{2,1,0:T(8,128)(2,1)} %get-tuple-element.53.refs_1_) | copy-start | bytes 884740
  55.9 9.2 %copy-start.5 = (bf16[2,192,384]{2,1,0:T(8,128)(2,1)S(1)}, bf16[2,192,384]{2,1,0:T(8,128)(2,1)}, u32[]{:S(2)}) copy-start(bf16[2,192,384]{2,1,0:T(8,128)(2,1)} %get-tuple-element.52.refs_0_) | copy-start | bytes 884740
  55.9 7.5 %collective-permute-start.8 = (bf16[2,192,384]{2,1,0:T(8,128)(2,1)}, bf16[2,192,384]{2,1,0:T(8,128)(2,1)S(1)}, u32[]{:S(2)}, u32[]{:S(2)}) collective-permute-start(bf16[2,192,384]{2,1,0:T(8,128)(2,1)} %get-tuple-element.54), channel_id=1, source_target_pairs={{0,1},{1,0},{2,3},{3,2},{4,5},{5,4},{6,7},{7,6},{8,9},{9,8},{10,11... | collective-permute-start | bytes 884744 | tf_op jit(solution)/shard_map/ppermute | solution.py:40
  57.2 6.2 %collective-permute-start.10 = (bf16[2,192,384]{2,1,0:T(8,128)(2,1)}, bf16[2,192,384]{2,1,0:T(8,128)(2,1)S(1)}, u32[]{:S(2)}, u32[]{:S(2)}) collective-permute-start(bf16[2,192,384]{2,1,0:T(8,128)(2,1)} %get-tuple-element.61), channel_id=1, source_target_pairs={{8,25},{9,24},{16,1},{17,0},{18,3},{19,2},{24,9},{25,8},{26,11},{2... | collective-permute-start | bytes 884744 | tf_op jit(solution)/shard_map/ppermute | solution.py:40
  63.4 1.8 %copy-start.6 = (bf16[2,192,384]{2,1,0:T(8,128)(2,1)}, bf16[2,192,384]{2,1,0:T(8,128)(2,1)S(1)}, u32[]{:S(2)}) copy-start(bf16[2,192,384]{2,1,0:T(8,128)(2,1)S(1)} %collective-permute-done.8.refs_2_) | copy-start | bytes 884740
  64.2 3.0 %copy-start.1 = (bf16[2,192,384]{2,1,0:T(8,128)(2,1)S(1)}, bf16[2,192,384]{2,1,0:T(8,128)(2,1)}, u32[]{:S(2)}) copy-start(bf16[2,192,384]{2,1,0:T(8,128)(2,1)} %get-tuple-element.95) | copy-start | bytes 884740
  64.3 0.8 collective-permute-start.9
  65.2 2.1 %collective-permute-start.11 = (bf16[2,192,384]{2,1,0:T(8,128)(2,1)S(1)}, bf16[2,192,384]{2,1,0:T(8,128)(2,1)S(1)}, u32[]{:S(2)}, u32[]{:S(2)}) collective-permute-start(bf16[2,192,384]{2,1,0:T(8,128)(2,1)S(1)} %get-tuple-element.93), channel_id=1, source_target_pairs={{0,4},{1,5},{2,0},{3,1},{8,12},{9,13},{10,8},{11,9},{12,10},{13,11... | collective-permute-start | bytes 884744 | tf_op jit(solution)/shard_map/ppermute | solution.py:40
  65.9 26.9 %collective-permute-start.13 = (bf16[2,192,384]{2,1,0:T(8,128)(2,1)S(1)}, bf16[2,192,384]{2,1,0:T(8,128)(2,1)S(1)}, u32[]{:S(2)}, u32[]{:S(2)}) collective-permute-start(bf16[2,192,384]{2,1,0:T(8,128)(2,1)S(1)} %get-tuple-element.93), channel_id=1, source_target_pairs={{0,2},{1,3},{2,4},{3,5},{8,10},{9,11},{10,12},{11,13},{12,14},{13,... | collective-permute-start | bytes 884744 | tf_op jit(solution)/shard_map/ppermute | solution.py:40
  67.3 56.3 %copy-start.23 = (bf16[2,192,384]{2,1,0:T(8,128)(2,1)}, bf16[2,192,384]{2,1,0:T(8,128)(2,1)S(1)}, u32[]{:S(2)}) copy-start(bf16[2,192,384]{2,1,0:T(8,128)(2,1)S(1)} %collective-permute-done.11) | copy-start | bytes 884740
  67.4 57.0 %collective-permute-start.12 = (bf16[2,2,192,384]{3,2,1,0:T(8,128)(2,1)S(1)}, bf16[2,2,192,384]{3,2,1,0:T(8,128)(2,1)S(1)}, u32[]{:S(2)}, u32[]{:S(2)}) collective-permute-start(bf16[2,2,192,384]{3,2,1,0:T(8,128)(2,1)S(1)} %broadcast_select_fusion), channel_id=1, source_target_pairs={{8,12},{9,13},{12,8},{13,9},{24,28},{25,29},{28,24},{29,25}} | collective-permute-start | bytes 1769480 | tf_op jit(solution)/shard_map/ppermute | solution.py:40
  92.8 2.6 %copy-start.25 = (bf16[2,192,384]{2,1,0:T(8,128)(2,1)}, bf16[2,192,384]{2,1,0:T(8,128)(2,1)S(1)}, u32[]{:S(2)}) copy-start(bf16[2,192,384]{2,1,0:T(8,128)(2,1)S(1)} %collective-permute-done.13) | copy-start | bytes 884740
  92.8 24.5 %collective-permute-start.17 = (bf16[2,192,384]{2,1,0:T(8,128)(2,1)S(1)}, bf16[2,192,384]{2,1,0:T(8,128)(2,1)S(1)}, u32[]{:S(2)}, u32[]{:S(2)}) collective-permute-start(bf16[2,192,384]{2,1,0:T(8,128)(2,1)S(1)} %collective-permute-done.13), channel_id=1, source_target_pairs={{4,6},{5,7},{12,14},{13,15},{20,22},{21,23},{28,30},{29,31}} | collective-permute-start | bytes 884744 | tf_op jit(solution)/shard_map/ppermute | solution.py:40
  94.1 29.6 %collective-permute-start.14 = (bf16[2,192,384]{2,1,0:T(8,128)(2,1)S(1)}, bf16[2,192,384]{2,1,0:T(8,128)(2,1)S(1)}, u32[]{:S(2)}, u32[]{:S(2)}) collective-permute-start(bf16[2,192,384]{2,1,0:T(8,128)(2,1)S(1)} %collective-permute-done.11), channel_id=1, source_target_pairs={{4,6},{5,7},{12,14},{13,15},{20,22},{21,23},{28,30},{29,31}} | collective-permute-start | bytes 884744 | tf_op jit(solution)/shard_map/ppermute | solution.py:40
  117.4 8.4 %collective-permute-start.18 = (bf16[2,2,192,384]{3,2,1,0:T(8,128)(2,1)S(1)}, bf16[2,2,192,384]{3,2,1,0:T(8,128)(2,1)S(1)}, u32[]{:S(2)}, u32[]{:S(2)}) collective-permute-start(bf16[2,2,192,384]{3,2,1,0:T(8,128)(2,1)S(1)} %get-tuple-element.63), channel_id=1, source_target_pairs={{8,10},{9,11},{24,26},{25,27}} | collective-permute-start | bytes 1769480 | tf_op jit(solution)/shard_map/ppermute | solution.py:40
  124.4 10.6 %collective-permute-start.15 = (bf16[2,2,192,384]{3,2,1,0:T(8,128)(2,1)S(1)}, bf16[2,2,192,384]{3,2,1,0:T(8,128)(2,1)S(1)}, u32[]{:S(2)}, u32[]{:S(2)}) collective-permute-start(bf16[2,2,192,384]{3,2,1,0:T(8,128)(2,1)S(1)} %collective-permute-done.12), channel_id=1, source_target_pairs={{12,14},{13,15},{28,30},{29,31}} | collective-permute-start | bytes 1769480 | tf_op jit(solution)/shard_map/ppermute | solution.py:40
  125.7 9.6 %copy-start.24 = (bf16[2,192,384]{2,1,0:T(8,128)(2,1)S(1)}, bf16[2,192,384]{2,1,0:T(8,128)(2,1)}, u32[]{:S(2)}) copy-start(bf16[2,192,384]{2,1,0:T(8,128)(2,1)} %copy-done.23) | copy-start | bytes 884740
  125.7 9.5 %copy-start.26 = (bf16[2,192,384]{2,1,0:T(8,128)(2,1)S(1)}, bf16[2,192,384]{2,1,0:T(8,128)(2,1)}, u32[]{:S(2)}) copy-start(bf16[2,192,384]{2,1,0:T(8,128)(2,1)} %copy-done.25) | copy-start | bytes 884740
  125.7 9.5 %copy-start.28 = (bf16[2,192,384]{2,1,0:T(8,128)(2,1)S(1)}, bf16[2,192,384]{2,1,0:T(8,128)(2,1)}, u32[]{:S(2)}) copy-start(bf16[2,192,384]{2,1,0:T(8,128)(2,1)} %copy-done.27) | copy-start | bytes 884740
  135.2 3.3 %collective-permute-start.19 = (bf16[2,2,192,384]{3,2,1,0:T(8,128)(2,1)S(1)}, bf16[2,2,192,384]{3,2,1,0:T(8,128)(2,1)S(1)}, u32[]{:S(2)}, u32[]{:S(2)}) collective-permute-start(bf16[2,2,192,384]{3,2,1,0:T(8,128)(2,1)S(1)} %select_select_fusion.refs_0_), channel_id=1, source_target_pairs={{0,8},{1,9},{2,10},{3,11},{4,12},{5,13},{6,14},{7,15},{8,0},{9,1},... | collective-permute-start | bytes 1769480 | tf_op jit(solution)/shard_map/ppermute | solution.py:40
  136.0 2.6 %copy-start.7 = (bf16[2,192,384]{2,1,0:T(8,128)(2,1)}, bf16[2,192,384]{2,1,0:T(8,128)(2,1)S(1)}, u32[]{:S(2)}) copy-start(bf16[2,192,384]{2,1,0:T(8,128)(2,1)S(1)} %get-tuple-element.90.refs_6_) | copy-start | bytes 884740
  136.0 2.6 %copy-start.8 = (bf16[2,192,384]{2,1,0:T(8,128)(2,1)}, bf16[2,192,384]{2,1,0:T(8,128)(2,1)S(1)}, u32[]{:S(2)}) copy-start(bf16[2,192,384]{2,1,0:T(8,128)(2,1)S(1)} %get-tuple-element.91.refs_4_) | copy-start | bytes 884740
  136.0 2.6 %copy-start.9 = (bf16[2,192,384]{2,1,0:T(8,128)(2,1)}, bf16[2,192,384]{2,1,0:T(8,128)(2,1)S(1)}, u32[]{:S(2)}) copy-start(bf16[2,192,384]{2,1,0:T(8,128)(2,1)S(1)} %get-tuple-element.92.refs_2_) | copy-start | bytes 884740
  136.0 2.1 %collective-permute-start.20 = (bf16[2,192,384]{2,1,0:T(8,128)(2,1)S(1)}, bf16[2,192,384]{2,1,0:T(8,128)(2,1)S(1)}, u32[]{:S(2)}, u32[]{:S(2)}) collective-permute-start(bf16[2,192,384]{2,1,0:T(8,128)(2,1)S(1)} %get-tuple-element.92.refs_2_), channel_id=1, source_target_pairs={{0,8},{1,9},{2,10},{3,11},{4,12},{5,13},{6,14},{7,15},{8,0},{9,1},... | collective-permute-start | bytes 884744 | tf_op jit(solution)/shard_map/ppermute | solution.py:40
  136.0 2.1 %collective-permute-start.21 = (bf16[2,192,384]{2,1,0:T(8,128)(2,1)S(1)}, bf16[2,192,384]{2,1,0:T(8,128)(2,1)S(1)}, u32[]{:S(2)}, u32[]{:S(2)}) collective-permute-start(bf16[2,192,384]{2,1,0:T(8,128)(2,1)S(1)} %get-tuple-element.91.refs_4_), channel_id=1, source_target_pairs={{0,8},{1,9},{2,10},{3,11},{4,12},{5,13},{6,14},{7,15},{8,0},{9,1},... | collective-permute-start | bytes 884744 | tf_op jit(solution)/shard_map/ppermute | solution.py:40
  136.5 2.0 %collective-permute-start.22 = (bf16[2,192,384]{2,1,0:T(8,128)(2,1)S(1)}, bf16[2,192,384]{2,1,0:T(8,128)(2,1)S(1)}, u32[]{:S(2)}, u32[]{:S(2)}) collective-permute-start(bf16[2,192,384]{2,1,0:T(8,128)(2,1)S(1)} %get-tuple-element.90.refs_6_), channel_id=1, source_target_pairs={{0,8},{1,9},{2,10},{3,11},{4,12},{5,13},{6,14},{7,15},{8,0},{9,1},... | collective-permute-start | bytes 884744 | tf_op jit(solution)/shard_map/ppermute | solution.py:40
  136.6 13.3 %collective-permute-start.16 = (bf16[2,192,384]{2,1,0:T(8,128)(2,1)S(1)}, bf16[2,192,384]{2,1,0:T(8,128)(2,1)S(1)}, u32[]{:S(2)}, u32[]{:S(2)}) collective-permute-start(bf16[2,192,384]{2,1,0:T(8,128)(2,1)S(1)} %copy-done.30), channel_id=1, source_target_pairs={{0,1},{1,0},{2,3},{3,2},{4,5},{5,4},{6,7},{7,6},{8,9},{9,8},{10,11... | collective-permute-start | bytes 884744 | tf_op jit(solution)/shard_map/ppermute | solution.py:40
  147.6 8.4 %collective-permute-start.24 = (bf16[384,384]{1,0:T(8,128)(2,1)}, bf16[384,384]{1,0:T(8,128)(2,1)S(1)}, u32[]{:S(2)}, u32[]{:S(2)}) collective-permute-start(bf16[384,384]{1,0:T(8,128)(2,1)} %get-tuple-element.74), channel_id=1, source_target_pairs={{0,16},{1,17},{2,18},{3,19},{4,20},{5,21},{6,22},{7,23},{8,24},{9,... | collective-permute-start | bytes 884744 | tf_op jit(solution)/shard_map/ppermute | solution.py:40
  148.9 14.1 %collective-permute-start.25 = (bf16[384,384]{1,0:T(8,128)(2,1)}, bf16[384,384]{1,0:T(8,128)(2,1)S(1)}, u32[]{:S(2)}, u32[]{:S(2)}) collective-permute-start(bf16[384,384]{1,0:T(8,128)(2,1)} %get-tuple-element.75), channel_id=1, source_target_pairs={{0,24},{1,25},{2,26},{3,27},{4,28},{5,29},{6,30},{7,31},{8,16},{9,... | collective-permute-start | bytes 884744 | tf_op jit(solution)/shard_map/ppermute | solution.py:40
  149.8 13.2 %collective-permute-start.23 = (bf16[384,384]{1,0:T(8,128)(2,1)}, bf16[384,384]{1,0:T(8,128)(2,1)S(1)}, u32[]{:S(2)}, u32[]{:S(2)}) collective-permute-start(bf16[384,384]{1,0:T(8,128)(2,1)} %get-tuple-element.73), channel_id=1, source_target_pairs={{0,8},{1,9},{2,10},{3,11},{4,12},{5,13},{6,14},{7,15},{8,0},{9,1},... | collective-permute-start | bytes 884744 | tf_op jit(solution)/shard_map/ppermute | solution.py:40
  149.9 13.1 %copy-start.22 = (bf16[384,384]{1,0:T(8,128)(2,1)S(1)}, bf16[384,384]{1,0:T(8,128)(2,1)}, u32[]{:S(2)}) copy-start(bf16[384,384]{1,0:T(8,128)(2,1)} %get-tuple-element.72) | copy-start | bytes 884740
  (10 other events, 9.1 us)
Sparse Core Ops, SparseCore 0:
  64.4 50.3 all-gather.2

commit v6 on v5

--- a/solution.py
+++ b/solution.py
@@ -158,60 +158,30 @@
     run_copies(copies)
 
 
-def solve_kernel(plan, place, *refs):
+def solve_kernel(plan, sources, place, diag, right, *refs):
     rows, moms, groups, side = plan.rows, plan.moms, plan.groups, plan.side
     moments, half, width, keys = plan.moments, plan.half, plan.width, plan.keys
     top = moments - 1
-    refs = list(refs)
-    take = lambda count: [refs.pop(0) for _ in range(count)]
-    sig_in = {}
-    for key in keys:
-        for t in range(groups):
-            if key[0] == top:
-                sig_in[key, t] = take(1)
-            else:
-                (ref,) = take(1)
-                sig_in[key, t] = [ref.at[q] for q in range(moms)]
-    gathered = [None] + take(moms - 1)
-    diag_in = {(b, t): take(1)[0] for b in range(moments) for t in range(groups)}
-    right_in, outs = take(rows), take(rows)
-    sig, diag, right, solved, right_sems, sems, out_sems = refs
+    sig_in, outs = refs[: -rows - 4], refs[-rows - 4 : -4]
+    sig, solved, sems, out_sems = refs[-4:]
     r, y = place[0], place[2]
     g = r % groups
-
-    def tile_copies(row, t):
-        made = []
-        b = row // groups
-        add = lambda source, target: made.append(
-            pltpu.make_async_copy(source, target, sems.at[row, len(made)])
-        )
-        for p in range(2):
-            add(diag_in[b, t].at[p], diag.at[row, :, pl.ds(p * side, side)])
-        for key in keys:
-            if key[0] == b and row > key[1]:
-                for q in range(moms):
-                    at = pl.ds(pl.multiple_of((y ^ q) * half, half), half)
-                    if b == top and q > 0:
-                        source = gathered[q].at[(row % groups) * plan.cols + key[1]]
-                    else:
-                        source = sig_in[key, t][q]
-                    for p in range(2):
-                        lane = pl.ds((2 * key[1] + p) * side, side)
-                        add(source.at[p], sig.at[row, at, lane])
-        return made
-
-    for s in range(rows):
-        pltpu.make_async_copy(right_in[s], right.at[r ^ s], right_sems.at[s]).start()
-    for me in range(groups):
-
-        @pl.when(g == me)
-        def _(me=me):
-            for row in range(rows):
-                for copy in tile_copies(row, me ^ (row % groups)):
-                    copy.start()
-
-    for s in range(rows):
-        pltpu.make_async_copy(right_in[s], right.at[r ^ s], right_sems.at[s]).wait()
+    for key in sorted(keys, key=lambda key: key[0]):
+        for col in range(plan.cols):
+
+            @pl.when(place[1] == col)
+            def _(key=key, col=col):
+                for t in range(groups):
+                    row = key[0] * groups + (g ^ t)
+                    for q in range(moms):
+                        index, part = sources[key, col, q, t]
+                        ref = sig_in[index] if part is None else sig_in[index].at[part]
+                        at = pl.ds(pl.multiple_of((y ^ q) * half, half), half)
+                        for p in range(2):
+                            lane = pl.ds((2 * key[1] + p) * side, side)
+                            pltpu.make_async_copy(
+                                ref.at[p], sig.at[row, at, lane], sems.at[key[0]]
+                            ).start()
 
     weight = 1.0 / math.sqrt(side * rows)
 
@@ -219,16 +189,27 @@
         return jnp.concatenate([-value[:, width:], value[:, :width]], axis=1)
 
     for row in range(rows):
-        for copy in tile_copies(row, 0):
-            copy.wait()
-        pending = right[row].astype(jnp.float32)
+        if row == max(1, row // groups * groups):
+            for key in keys:
+                if key[0] == row // groups:
+                    for t in range(groups * moms * 2):
+                        pltpu.make_async_copy(
+                            sig.at[0, pl.ds(0, half), pl.ds(0, side)],
+                            sig.at[0, pl.ds(0, half), pl.ds(0, side)],
+                            sems.at[key[0]],
+                        ).wait()
+        pending = right[r ^ row].astype(jnp.float32)
         if row > 0:
             depth = 2 * side * row
             pending = pending + weight * jnp.dot(
                 sig[row, :, :depth], solved[:depth, :], preferred_element_type=jnp.float32
             )
         both = jnp.concatenate([pending, turn(pending)], axis=0).astype(jnp.bfloat16)
-        value = jnp.dot(diag[row], both, preferred_element_type=jnp.float32)
+        value = jnp.dot(
+            diag[(row // groups) * groups + (g ^ (row % groups))],
+            both,
+            preferred_element_type=jnp.float32,
+        )
         solved[pl.ds(2 * row * side, side), :] = value.astype(jnp.bfloat16)
         solved[pl.ds((2 * row + 1) * side, side), :] = turn(value).astype(jnp.bfloat16)
         for s in range(rows):
@@ -285,12 +266,13 @@
     right = right.reshape(rows, side, 2 * width)
     right_all = [lax.dynamic_index_in_dim(right, r ^ s, 0, keepdims=False) for s in range(rows)]
     right_all = after(right_all, lesser_all[1:])
-    right_came = right_all[:1] + [exchange_row(right_all[s], s) for s in range(1, rows)]
-    diag_all = [
-        diag[b] if t == 0 else exchange_row(diag[b], t) for b in range(moments) for t in range(groups)
-    ]
-    lesser_all, partner_all, right_came, diag_all = lax.optimization_barrier(
-        (lesser_all, partner_all, right_came, diag_all)
+    right_came = jnp.stack(right_all[:1] + [exchange_row(right_all[s], s) for s in range(1, rows)])
+    diag = [jnp.concatenate([value[0], value[1]], axis=1) for value in diag]
+    diag_came = jnp.stack(
+        [diag[b] if t == 0 else exchange_row(diag[b], t) for b in range(moments) for t in range(groups)]
+    )
+    lesser_all, partner_all, right_came, diag_came = lax.optimization_barrier(
+        (lesser_all, partner_all, right_came, diag_came)
     )
 
     high = jnp.maximum(triples[..., 0], triples[..., 1])
@@ -358,73 +340,102 @@
     joint = [send for send in sends if send not in split]
     found = {}
     own, whole = [], None
-    log = []
-
-    def issue(make, value):
-        if len(log) > 2:
-            value = after(value, log[-3])
-        log.append(make(value))
-        return log[-1]
+    buffers = []
+
+    def number(value):
+        for index, held in enumerate(buffers):
+            if held is value:
+                return index
+        buffers.append(value)
+        return len(buffers) - 1
 
     for q in range(moms):
         own.append(by_block(came[q]))
-    members = [
-        [(b * groups + g) * cols + c for g in range(groups) for c in range(cols)]
-        for b in range(moments)
-    ]
-    gathered = [
-        lax.all_gather(own[q][top], AXES[:2], axis_index_groups=members) for q in range(1, moms)
-    ]
-    for key in plan.keys:
-        if key[0] == top:
-            found[key, key[1]] = own[0][top]
+        for key in plan.keys:
+            if key[0] == top:
+                found[key, key[1], q] = (own[q][top], None)
     joint_values = [jnp.stack([own[k][b] for k in range(moms)]) for b in range(moments)]
     for key in plan.keys:
         if key[0] < top:
-            found[key, key[1]] = joint_values[key[0]]
-
-    def split_step(step):
-        def run():
-            value = issue(lambda v: spread(step, v), own[0])
-            for key, to in step.values():
-                found[key, to] = value
-
-        return run
-
-    def split_relay(key):
-        def run():
-            value = after(found[key, last - 1], came[1:])
-            found[key, last] = issue(lambda v: relay(v, key), value)
-
-        return run
-
-    def joint_step(step):
-        def run():
-            value = issue(lambda v: spread(step, v), joint_values)
-            for key, to in step.values():
-                found[key, to] = value[0] if key[0] == top else value
-
-        return run
-
-    def joint_relay(key):
-        def run():
-            found[key, last] = issue(lambda v: relay(v, key), found[key, last - 1])
-
-        return run
+            for q in range(moms):
+                found[key, key[1], q] = (joint_values[key[0]], q)
+
+    steps = plan.direct(split)
+    sent, relayed = {}, [[] for _ in range(moms)]
+
+    def split_step(q, n):
+        value = own[q]
+        if q > 0:
+            value = after(value, sent[q - 1, n], relayed[q - 1][:n])
+        sent[q, n] = value = spread(steps[n], value)
+        for key, to in steps[n].values():
+            found[key, to, q] = (value, None)
+
+    def split_relay(q, key):
+        value = found[key, last - 1, q][0]
+        if q + 1 < moms:
+            value = after(value, came[q + 1])
+        if q > 0:
+            value = after(value, found[key, last, q - 1][0])
+        value = relay(value, key)
+        found[key, last, q] = (value, None)
+        relayed[q].append(value)
 
     relays = sorted([key for key in plan.keys if key[1] < last - 1], key=lambda key: -key[1])
-    schedule = [split_step(step) for step in plan.direct(split)]
-    schedule += [split_relay(key) for key in relays if key[0] == top]
-    schedule += [joint_step(step) for step in plan.direct(joint)]
-    schedule += [joint_relay(key) for key in relays if key[0] < top]
-    for run in schedule:
-        run()
+    for q in range(moms):
+        for n in range(len(steps)):
+            split_step(q, n)
+        for key in relays:
+            if key[0] == top:
+                split_relay(q, key)
+    for n, step in enumerate(plan.direct(joint)):
+        behind = sent[moms - 1, min(n, len(steps) - 1)]
+        value = spread(step, after(joint_values, behind, relayed[0]))
+        for key, to in step.values():
+            for q in range(moms):
+                found[key, to, q] = (value, q)
+    for key in relays:
+        if key[0] < top:
+            value = relay(found[key, last - 1, 0][0], key)
+            for q in range(moms):
+                found[key, last, q] = (value, q)
+
+    sources = {}
+    for (key, col, q), (value, part) in found.items():
+        sources[key, col, q, 0] = (number(value), part)
+    swapped = {}
+    for (key, col, q), (value, part) in found.items():
+        for t in range(1, groups):
+            index = number(value)
+            if (index, t) not in swapped:
+                swapped[index, t] = exchange_row(value, t)
+            sources[key, col, q, t] = ((index, t), part)
+    place_of = {name: len(buffers) + n for n, name in enumerate(swapped)}
+    for name, (index, part) in sources.items():
+        if name[3] > 0:
+            sources[name] = (place_of[index], part)
+    sig_all = buffers + list(swapped.values())
+
+    solved = pl.pallas_call(
+        functools.partial(solve_kernel, plan, sources),
+        out_shape=[jax.ShapeDtypeStruct((side, 2 * width), bf16)] * rows,
+        in_specs=[smem()] + [pl.BlockSpec(memory_space=pltpu.VMEM)] * 2 + hbm(len(sig_all)),
+        out_specs=hbm(rows),
+        scratch_shapes=[
+            pltpu.VMEM((rows, side, 2 * side * (cols - 1)), bf16),
+            pltpu.VMEM((rows * 2 * side, 2 * width), bf16),
+            dma(moments),
+            dma(rows),
+        ],
+        compiler_params=params,
+        name="substitution",
+    )(place, diag_came, right_came, *sig_all)
 
     whole = [slots[b] for b in range(moments)]
     for q in range(1, moms):
         whole.append(came[q][0])
         for b in range(1, moments):
-            whole.append(exchange_mom(after(slots[q * moments + b], log[-1]), q))
+            whole.append(exchange_mom(after(slots[q * moments + b], solved), q))
     sigma = pl.pallas_call(
         functools.partial(place_kernel, plan),
         out_shape=jax.ShapeDtypeStruct(lesser.shape, bf16),
@@ -434,32 +445,8 @@
         name="place_sigma",
     )(place, *whole)
 
-    sig_all = []
-    for key in plan.keys:
-        mine = lax.select_n(z, *[found[key, c] for c in range(cols)])
-        for t in range(groups):
-            sig_all.append(mine if t == 0 else exchange_row(mine, t))
-    sig_all += gathered
-    most = 2 + 4 * moms * (cols - 1)
-    solved = pl.pallas_call(
-        functools.partial(solve_kernel, plan),
-        out_shape=[jax.ShapeDtypeStruct((side, 2 * width), bf16)] * rows,
-        in_specs=[smem()] + hbm(len(sig_all) + len(diag_all) + rows),
-        out_specs=hbm(rows),
-        scratch_shapes=[
-            pltpu.VMEM((rows, side, 2 * side * (cols - 1)), bf16),
-            pltpu.VMEM((rows, side, 2 * side), bf16),
-            pltpu.VMEM((rows, side, 2 * width), bf16),
-            pltpu.VMEM((rows * 2 * side, 2 * width), bf16),
-            dma(rows),
-            dma(rows, most),
-            dma(rows),
-        ],
-        compiler_params=params,
-        name="substitution",
-    )(place, *sig_all, *diag_all, *right_came)
-
     back = [solved[0]] + [exchange_row(solved[s], s) for s in range(1, rows)]
+    back = after(back, sigma)
     pieces = jnp.stack([lax.select_n(r ^ s, *back) for s in range(rows)])
     pieces = pieces.reshape(moments, groups, side, 2, width).transpose(0, 2, 3, 1, 4)
     return sigma, pieces.reshape(moments, side, 2, side)

time: 175 us -> 163 us (0.931)
  between operations: 14.6 us -> 1.33 us
  waiting for transfers between devices: 98.6 us -> 88.2 us
  starting transfers between devices: 22.8 us -> 30.4 us
  other arithmetic: 4.35 us -> 7.91 us
    ppermute x26 -> x40, waiting for transfers between devices: 98.5 us -> 88.2 us  [send(): return lax.ppermute(value, AXES, pairs)]
    ppermute x26 -> x40, starting transfers between devices: 22.7 us -> 30.4 us  [send(): return lax.ppermute(value, AXES, pairs)]
    another operation x0 -> x4, other arithmetic: none -> 3.88 us  [the longest x3 2.68 us: on_device(): jnp.stack([diag[b] if t == 0 else exchange_row(diag[b], t) for b in range...]
    unnamed x63 -> x73, local copies, waits for them, and re-layouts: 6.45 us -> 5.86 us
  transfers between devices with their start and end apart: 27 -> 40, of which waited for: 11 -> 16; matrix products, arithmetic and copies ran while one was open for 4% -> 8% of each run, Pallas kernels for 6% -> 2%
where the time goes in v6:
time: 163 us
  waiting for transfers between devices  88.2 us (54%)
  starting transfers between devices  30.4 us (19%)
  Pallas kernels  17.4 us (11%)
  local copies, waits for them, and re-layouts  17.2 us (11%)
  other arithmetic  7.91 us (5%)
    ppermute x40, waiting for transfers between devices, send(): return lax.ppermute(value, AXES, pairs)  88.2 us
    ppermute x40, starting transfers between devices, send(): return lax.ppermute(value, AXES, pairs)  30.4 us
    pallas_call x1, Pallas kernels, on_device(): pl.pallas_call(functools.partial(solve_kernel, plan, sources), out_shape=...  8.18 us
    pallas_call x1, Pallas kernels, on_device(): pl.pallas_call(functools.partial(sigma_kernel, plan, pair_count, chunks),...  6.29 us
    unnamed x73, local copies, waits for them, and re-layouts  5.86 us
  transfers between devices with their start and end apart: 40, of which 16 were waited for; matrix products, arithmetic and copies ran while one was open for 8% of the time, Pallas kernels for 2%

profile of v6, /device:TPU:25, one launch (start us, length us, event | category | flops | bytes accessed | tf_op | source)
XLA Modules:
  0.0 162.5 jit_solution(12073431550734293594)
XLA Ops:
  0.7 2.0 %constant_dynamic-slice_fusion.4 = bf16[2,2,192,384]{3,2,1,0:T(8,128)(2,1)} fusion(bf16[2,2,384,384]{3,2,1,0:T(8,128)(2,1)} %refs_0_, s32[]{:T(128)S(6)} %select_n.193), kind=kLoop, calls=%fused_computation.36 | loop fusion | bytes 1179652 | tf_op jit(solution)/shard_map/dynamic_slice | solution.py:251
  3.5 0.9 dynamic-slice_bitcast_fusion.1
  4.4 0.9 dynamic-slice_bitcast_fusion
  5.3 1.2 collective-permute-start.5
  6.5 1.2 collective-permute-start
  8.0 2.0 %copy.13 = bf16[2,384,2,384]{1,3,2,0:T(8,128)(2,1)S(1)} copy(bf16[2,384,2,384]{3,2,1,0:T(2,128)(2,1)S(1)} %copy-done.6) | data formatting | bytes 2359296 | tf_op jit(solution)/shard_map/optimization_barrier | solution.py:227
  10.5 0.9 copy.16
  11.4 0.9 copy.17
  12.3 0.9 copy.18
  13.2 6.6 %collective-permute-done.5 = bf16[2,384,384]{2,1,0:T(8,128)(2,1)} collective-permute-done((bf16[2,384,384]{2,1,0:T(8,128)(2,1)}, bf16[2,384,384]{2,1,0:T(8,128)(2,1)}, u32[]{:S(2)}, u32[]{:S(2)}) %collective-permute-start.5) | collective-permute-done | bytes 589856 | tf_op jit(solution)/shard_map/ppermute | solution.py:40
  19.8 1.2 bitcast_select_fusion.1
  21.2 1.6 collective-permute-start.6
  22.9 1.2 collective-permute-start.2
  24.1 0.9 fusion.3
  26.1 1.6 collective-permute-start.4
  28.9 5.1 %collective-permute-done.3 = bf16[384,384]{1,0:T(8,128)(2,1)S(1)} collective-permute-done((bf16[384,384]{1,0:T(8,128)(2,1)}, bf16[384,384]{1,0:T(8,128)(2,1)S(1)}, u32[]{:S(2)}, u32[]{:S(2)}) %collective-permute-start.3) | collective-permute-done | bytes 294944 | tf_op jit(solution)/shard_map/ppermute | solution.py:40
  33.9 6.9 %collective-permute-done.4 = bf16[384,384]{1,0:T(8,128)(2,1)S(1)} collective-permute-done((bf16[384,384]{1,0:T(8,128)(2,1)}, bf16[384,384]{1,0:T(8,128)(2,1)S(1)}, u32[]{:S(2)}, u32[]{:S(2)}) %collective-permute-start.4) | collective-permute-done | bytes 294944 | tf_op jit(solution)/shard_map/ppermute | solution.py:40
  40.8 1.2 pad_maximum_fusion.1.right
  42.0 1.7 %pad_maximum_fusion.diag = bf16[4,384,768]{2,1,0:T(8,128)(2,1)} fusion(bf16[1,384,768]{2,1,0:T(8,128)(2,1)S(1)} %bitcast.71, bf16[1,384,768]{2,1,0:T(8,128)(2,1)S(1)} %get-tuple-element.96, bf16[1,384,768]{2,1,0:T(8,128)(2,1)S(1)} %bitcast.70, bf16[1,384,768]{2,1,0:T(8,128)(2,1)S(1)} %get-tuple-element.92), kind=kLoop, calls=%fused_computation | loop fusion | flops 3538944 | bytes 4718592 | tf_op jit(solution)/shard_map/stack | solution.py:271
  43.7 6.3 %self_energy.1 = (bf16[2,192,384]{2,1,0:T(8,128)(2,1)}, bf16[2,192,384]{2,1,0:T(8,128)(2,1)}, bf16[2,192,384]{2,1,0:T(8,128)(2,1)}, bf16[2,192,384]{2,1,0:T(8,128)(2,1)}) custom-call(s32[3]{0:T(128)} %pad_add_fusion.place, s32[4,8]{1,0:T(4,128)} %fusion.1.quads, s32[4,8]{1,0:T(4,128)} %slice_bitcast_fusion.4.thirds, bf16[2,2,384,384]{3,2,1,0:T(8,128)(2,1)} %refs_0_, ...), custom_call_target="tpu_custom_call" | custom-call | tf_op jit(solution)/shard_map/self_energy/pallas_call | solution.py:282
  51.4 1.3 collective-permute-start.8
  52.7 1.0 select_bitcast_fusion.4
  53.7 1.3 collective-permute-start.11
  55.7 4.8 %collective-permute-done.8.refs_2_ = bf16[2,192,384]{2,1,0:T(8,128)(2,1)S(1)} collective-permute-done((bf16[2,192,384]{2,1,0:T(8,128)(2,1)}, bf16[2,192,384]{2,1,0:T(8,128)(2,1)S(1)}, u32[]{:S(2)}, u32[]{:S(2)}) %collective-permute-start.8) | collective-permute-done | bytes 294944 | tf_op jit(solution)/shard_map/ppermute | solution.py:40
  60.6 4.6 %collective-permute-done.11.refs_3_ = bf16[2,192,384]{2,1,0:T(8,128)(2,1)S(1)} collective-permute-done((bf16[2,192,384]{2,1,0:T(8,128)(2,1)S(1)}, bf16[2,192,384]{2,1,0:T(8,128)(2,1)S(1)}, u32[]{:S(2)}, u32[]{:S(2)}) %collective-permute-start.11) | collective-permute-done | bytes 294944 | tf_op jit(solution)/shard_map/ppermute | solution.py:40
  65.2 1.3 collective-permute-start.13
  66.5 1.3 collective-permute-start.14
  67.8 1.3 collective-permute-start.15
  69.4 8.7 %collective-permute-done.13.refs_5_ = bf16[2,192,384]{2,1,0:T(8,128)(2,1)S(1)} collective-permute-done((bf16[2,192,384]{2,1,0:T(8,128)(2,1)S(1)}, bf16[2,192,384]{2,1,0:T(8,128)(2,1)S(1)}, u32[]{:S(2)}, u32[]{:S(2)}) %collective-permute-start.13) | collective-permute-done | bytes 294944 | tf_op jit(solution)/shard_map/ppermute | solution.py:40
  78.1 6.9 %collective-permute-done.14.refs_6_ = bf16[2,192,384]{2,1,0:T(8,128)(2,1)S(1)} collective-permute-done((bf16[2,192,384]{2,1,0:T(8,128)(2,1)S(1)}, bf16[2,192,384]{2,1,0:T(8,128)(2,1)S(1)}, u32[]{:S(2)}, u32[]{:S(2)}) %collective-permute-start.14) | collective-permute-done | bytes 294944 | tf_op jit(solution)/shard_map/ppermute | solution.py:40
  85.0 4.8 %collective-permute-done.15.refs_7_ = bf16[2,192,384]{2,1,0:T(8,128)(2,1)S(1)} collective-permute-done((bf16[2,192,384]{2,1,0:T(8,128)(2,1)S(1)}, bf16[2,192,384]{2,1,0:T(8,128)(2,1)S(1)}, u32[]{:S(2)}, u32[]{:S(2)}) %collective-permute-start.15) | collective-permute-done | bytes 294944 | tf_op jit(solution)/shard_map/ppermute | solution.py:40
  92.4 1.3 collective-permute-done.22.refs_14_
  93.7 1.3 collective-permute-start.17
  95.7 1.3 collective-permute-start.21
  97.6 17.8 %collective-permute-done.17.refs_9_ = bf16[2,192,384]{2,1,0:T(8,128)(2,1)S(1)} collective-permute-done((bf16[2,192,384]{2,1,0:T(8,128)(2,1)S(1)}, bf16[2,192,384]{2,1,0:T(8,128)(2,1)S(1)}, u32[]{:S(2)}, u32[]{:S(2)}) %collective-permute-start.17) | collective-permute-done | bytes 294944 | tf_op jit(solution)/shard_map/ppermute | solution.py:40
  115.5 1.6 collective-permute-start.27
  117.1 1.5 collective-permute-start.18
  119.3 3.3 %collective-permute-done.21.refs_13_ = bf16[2,2,192,384]{3,2,1,0:T(8,128)(2,1)S(1)} collective-permute-done((bf16[2,2,192,384]{3,2,1,0:T(8,128)(2,1)S(1)}, bf16[2,2,192,384]{3,2,1,0:T(8,128)(2,1)S(1)}, u32[]{:S(2)}, u32[]{:S(2)}) %collective-permute-start.21) | collective-permute-done | bytes 589856 | tf_op jit(solution)/shard_map/ppermute | solution.py:40
  122.6 6.0 %collective-permute-done.18.refs_10_ = bf16[2,192,384]{2,1,0:T(8,128)(2,1)S(1)} collective-permute-done((bf16[2,192,384]{2,1,0:T(8,128)(2,1)S(1)}, bf16[2,192,384]{2,1,0:T(8,128)(2,1)S(1)}, u32[]{:S(2)}, u32[]{:S(2)}) %collective-permute-start.18) | collective-permute-done | bytes 294944 | tf_op jit(solution)/shard_map/ppermute | solution.py:40
  129.1 1.1 collective-permute-done.30.refs_22_
  132.1 0.8 copy-done.14
  133.0 8.2 %substitution.1 = (bf16[384,384]{1,0:T(8,128)(2,1)}, bf16[384,384]{1,0:T(8,128)(2,1)}, bf16[384,384]{1,0:T(8,128)(2,1)}, bf16[384,384]{1,0:T(8,128)(2,1)}) custom-call(s32[3]{0:T(128)} %pad_add_fusion.place, bf16[4,384,768]{2,1,0:T(8,128)(2,1)} %pad_maximum_fusion.diag, bf16[4,384,384]{2,1,0:T(8,128)(2,1)} %pad_maximum_fusion.1.right, ...), custom_call_target="tpu_custom_call" | custom-call | tf_op jit(solution)/shard_map/substitution/pallas_call | solution.py:419
  141.2 1.3 collective-permute-start.36
  143.1 1.6 %collective-permute-start.39 = (bf16[384,384]{1,0:T(8,128)(2,1)}, bf16[384,384]{1,0:T(8,128)(2,1)S(1)}, u32[]{:S(2)}, u32[]{:S(2)}) collective-permute-start(bf16[384,384]{1,0:T(8,128)(2,1)} %get-tuple-element.70), channel_id=1, source_target_pairs={{0,24},{1,25},{2,26},{3,27},{4,28},{5,29},{6,30},{7,31},{8,16},{9,... | collective-permute-start | bytes 884744 | tf_op jit(solution)/shard_map/ppermute | solution.py:40
  144.7 4.9 %collective-permute-done.36.refs_3_ = bf16[2,192,384]{2,1,0:T(8,128)(2,1)S(1)} collective-permute-done((bf16[2,192,384]{2,1,0:T(8,128)(2,1)}, bf16[2,192,384]{2,1,0:T(8,128)(2,1)S(1)}, u32[]{:S(2)}, u32[]{:S(2)}) %collective-permute-start.36) | collective-permute-done | bytes 294944 | tf_op jit(solution)/shard_map/ppermute | solution.py:40
  150.3 2.9 %place_sigma.1 = bf16[2,2,384,384]{3,2,1,0:T(8,128)(2,1)} custom-call(s32[3]{0:T(128)} %pad_add_fusion.place, bf16[2,192,384]{2,1,0:T(8,128)(2,1)} %get-tuple-element.52.refs_0_, bf16[2,192,384]{2,1,0:T(8,128)(2,1)} %get-tuple-element.53.refs_1_, bf16[2,192,384]{2,1,0:T(8,128)(2,1)} %copy-done.4, bf16[2,192,384]{2,1,0:T(8,128)(2,1)} %copy-done.33), custom_call_target="tpu_custom_call" | custom-call | tf_op jit(solution)/shard_map/place_sigma/pallas_call | solution.py:439
  153.3 5.0 %collective-permute-done.39 = bf16[384,384]{1,0:T(8,128)(2,1)S(1)} collective-permute-done((bf16[384,384]{1,0:T(8,128)(2,1)}, bf16[384,384]{1,0:T(8,128)(2,1)S(1)}, u32[]{:S(2)}, u32[]{:S(2)}) %collective-permute-start.39) | collective-permute-done | bytes 294944 | tf_op jit(solution)/shard_map/ppermute | solution.py:40
  159.7 2.8 %copy.21 = bf16[2,384,2,384]{3,2,1,0:T(2,128)(2,1)} copy(bf16[2,384,2,384]{1,3,2,0:T(8,128)(2,1)S(1)} %bitcast.64) | data formatting | bytes 2359296
  (137 shorter events, 16.0 us)
Async XLA Ops:
  5.3 14.5 %collective-permute-start.5 = (bf16[2,384,384]{2,1,0:T(8,128)(2,1)}, bf16[2,384,384]{2,1,0:T(8,128)(2,1)}, u32[]{:S(2)}, u32[]{:S(2)}) collective-permute-start(bf16[2,384,384]{2,1,0:T(8,128)(2,1)} %dynamic-slice_bitcast_fusion), channel_id=1, source_target_pairs={{0,16},{1,17},{2,18},{3,19},{4,20},{5,21},{6,22},{7,23},{8,24},{9,... | collective-permute-start | bytes 1769480 | tf_op jit(solution)/shard_map/ppermute | solution.py:40
  6.5 16.3 %collective-permute-start = (bf16[2,2,192,384]{3,2,1,0:T(8,128)(2,1)}, bf16[2,2,192,384]{3,2,1,0:T(8,128)(2,1)}, u32[]{:S(2)}, u32[]{:S(2)}) collective-permute-start(bf16[2,2,192,384]{3,2,1,0:T(8,128)(2,1)} %constant_dynamic-slice_fusion.4), channel_id=1, source_target_pairs={{0,1},{1,0},{2,3},{3,2},{4,5},{5,4},{6,7},{7,6},{8,9},{9,8},{10,11... | collective-permute-start | bytes 1769480 | tf_op jit(solution)/shard_map/ppermute | solution.py:40
  7.8 35.9 %collective-permute-start.1 = (bf16[2,2,192,384]{3,2,1,0:T(8,128)(2,1)}, bf16[2,2,192,384]{3,2,1,0:T(8,128)(2,1)}, u32[]{:S(2)}, u32[]{:S(2)}) collective-permute-start(bf16[2,2,192,384]{3,2,1,0:T(8,128)(2,1)} %dynamic-slice_bitcast_fusion.1), channel_id=1, source_target_pairs={{0,1},{1,0},{2,3},{3,2},{4,5},{5,4},{6,7},{7,6},{8,9},{9,8},{10,11... | collective-permute-start | bytes 1769480 | tf_op jit(solution)/shard_map/ppermute | solution.py:40
  21.2 20.8 %collective-permute-start.6 = (bf16[384,768]{1,0:T(8,128)(2,1)S(1)}, bf16[384,768]{1,0:T(8,128)(2,1)S(1)}, u32[]{:S(2)}, u32[]{:S(2)}) collective-permute-start(bf16[384,768]{1,0:T(8,128)(2,1)S(1)} %get-tuple-element.93), channel_id=1, source_target_pairs={{0,8},{1,9},{2,10},{3,11},{4,12},{5,13},{6,14},{7,15},{8,0},{9,1},... | collective-permute-start | bytes 1769480 | tf_op jit(solution)/shard_map/ppermute | solution.py:40
  22.9 3.2 %collective-permute-start.2 = (bf16[384,384]{1,0:T(8,128)(2,1)}, bf16[384,384]{1,0:T(8,128)(2,1)S(1)}, u32[]{:S(2)}, u32[]{:S(2)}) collective-permute-start(bf16[384,384]{1,0:T(8,128)(2,1)} %bitcast.12), channel_id=1, source_target_pairs={{0,8},{1,9},{2,10},{3,11},{4,12},{5,13},{6,14},{7,15},{8,0},{9,1},... | collective-permute-start | bytes 884744 | tf_op jit(solution)/shard_map/ppermute | solution.py:40
  25.0 17.1 %collective-permute-start.7 = (bf16[384,768]{1,0:T(8,128)(2,1)}, bf16[384,768]{1,0:T(8,128)(2,1)S(1)}, u32[]{:S(2)}, u32[]{:S(2)}) collective-permute-start(bf16[384,768]{1,0:T(8,128)(2,1)} %get-tuple-element.97), channel_id=1, source_target_pairs={{0,8},{1,9},{2,10},{3,11},{4,12},{5,13},{6,14},{7,15},{8,0},{9,1},... | collective-permute-start | bytes 1769480 | tf_op jit(solution)/shard_map/ppermute | solution.py:40
  25.6 8.4 %collective-permute-start.3 = (bf16[384,384]{1,0:T(8,128)(2,1)}, bf16[384,384]{1,0:T(8,128)(2,1)S(1)}, u32[]{:S(2)}, u32[]{:S(2)}) collective-permute-start(bf16[384,384]{1,0:T(8,128)(2,1)} %bitcast.76), channel_id=1, source_target_pairs={{0,16},{1,17},{2,18},{3,19},{4,20},{5,21},{6,22},{7,23},{8,24},{9,... | collective-permute-start | bytes 884744 | tf_op jit(solution)/shard_map/ppermute | solution.py:40
  26.1 14.7 %collective-permute-start.4 = (bf16[384,384]{1,0:T(8,128)(2,1)}, bf16[384,384]{1,0:T(8,128)(2,1)S(1)}, u32[]{:S(2)}, u32[]{:S(2)}) collective-permute-start(bf16[384,384]{1,0:T(8,128)(2,1)} %bitcast.75), channel_id=1, source_target_pairs={{0,24},{1,25},{2,26},{3,27},{4,28},{5,29},{6,30},{7,31},{8,16},{9,... | collective-permute-start | bytes 884744 | tf_op jit(solution)/shard_map/ppermute | solution.py:40
  50.0 2.7 %collective-permute-start.9 = (bf16[2,192,384]{2,1,0:T(8,128)(2,1)}, bf16[2,192,384]{2,1,0:T(8,128)(2,1)S(1)}, u32[]{:S(2)}, u32[]{:S(2)}) collective-permute-start(bf16[2,192,384]{2,1,0:T(8,128)(2,1)} %get-tuple-element.53.refs_1_), channel_id=1, source_target_pairs={{8,24},{9,25},{16,0},{17,1},{18,2},{19,3},{24,8},{25,9},{26,10},{2... | collective-permute-start | bytes 884744 | tf_op jit(solution)/shard_map/ppermute | solution.py:40
  50.7 5.0 %collective-permute-start.10 = (bf16[2,192,384]{2,1,0:T(8,128)(2,1)}, bf16[2,192,384]{2,1,0:T(8,128)(2,1)S(1)}, u32[]{:S(2)}, u32[]{:S(2)}) collective-permute-start(bf16[2,192,384]{2,1,0:T(8,128)(2,1)} %get-tuple-element.71), channel_id=1, source_target_pairs={{8,25},{9,24},{16,1},{17,0},{18,3},{19,2},{24,9},{25,8},{26,11},{2... | collective-permute-start | bytes 884744 | tf_op jit(solution)/shard_map/ppermute | solution.py:40
  51.4 9.1 %collective-permute-start.8 = (bf16[2,192,384]{2,1,0:T(8,128)(2,1)}, bf16[2,192,384]{2,1,0:T(8,128)(2,1)S(1)}, u32[]{:S(2)}, u32[]{:S(2)}) collective-permute-start(bf16[2,192,384]{2,1,0:T(8,128)(2,1)} %get-tuple-element.54), channel_id=1, source_target_pairs={{0,1},{1,0},{2,3},{3,2},{4,5},{5,4},{6,7},{7,6},{8,9},{9,8},{10,11... | collective-permute-start | bytes 884744 | tf_op jit(solution)/shard_map/ppermute | solution.py:40
  53.7 37.6 %copy-start.2 = (bf16[2,192,384]{2,1,0:T(8,128)(2,1)}, bf16[2,192,384]{2,1,0:T(8,128)(2,1)S(1)}, u32[]{:S(2)}) copy-start(bf16[2,192,384]{2,1,0:T(8,128)(2,1)S(1)} %get-tuple-element.89.refs_0_) | copy-start | bytes 884740
  53.7 11.5 %collective-permute-start.11 = (bf16[2,192,384]{2,1,0:T(8,128)(2,1)S(1)}, bf16[2,192,384]{2,1,0:T(8,128)(2,1)S(1)}, u32[]{:S(2)}, u32[]{:S(2)}) collective-permute-start(bf16[2,192,384]{2,1,0:T(8,128)(2,1)S(1)} %get-tuple-element.89.refs_0_), channel_id=1, source_target_pairs={{0,2},{1,3},{2,4},{3,5},{8,10},{9,11},{10,12},{11,13},{12,14},{13,... | collective-permute-start | bytes 884744 | tf_op jit(solution)/shard_map/ppermute | solution.py:40
  55.0 11.5 %collective-permute-start.12 = (bf16[2,192,384]{2,1,0:T(8,128)(2,1)S(1)}, bf16[2,192,384]{2,1,0:T(8,128)(2,1)S(1)}, u32[]{:S(2)}, u32[]{:S(2)}) collective-permute-start(bf16[2,192,384]{2,1,0:T(8,128)(2,1)S(1)} %get-tuple-element.89.refs_0_), channel_id=1, source_target_pairs={{0,4},{1,5},{2,0},{3,1},{8,12},{9,13},{10,8},{11,9},{12,10},{13,11... | collective-permute-start | bytes 884744 | tf_op jit(solution)/shard_map/ppermute | solution.py:40
  65.2 12.8 %collective-permute-start.13 = (bf16[2,192,384]{2,1,0:T(8,128)(2,1)S(1)}, bf16[2,192,384]{2,1,0:T(8,128)(2,1)S(1)}, u32[]{:S(2)}, u32[]{:S(2)}) collective-permute-start(bf16[2,192,384]{2,1,0:T(8,128)(2,1)S(1)} %collective-permute-done.11.refs_3_), channel_id=1, source_target_pairs={{4,6},{5,7},{12,14},{13,15},{20,22},{21,23},{28,30},{29,31}} | collective-permute-start | bytes 884744 | tf_op jit(solution)/shard_map/ppermute | solution.py:40
  66.5 18.5 %collective-permute-start.14 = (bf16[2,192,384]{2,1,0:T(8,128)(2,1)S(1)}, bf16[2,192,384]{2,1,0:T(8,128)(2,1)S(1)}, u32[]{:S(2)}, u32[]{:S(2)}) collective-permute-start(bf16[2,192,384]{2,1,0:T(8,128)(2,1)S(1)} %collective-permute-done.12.refs_4_), channel_id=1, source_target_pairs={{4,6},{5,7},{12,14},{13,15},{20,22},{21,23},{28,30},{29,31}} | collective-permute-start | bytes 884744 | tf_op jit(solution)/shard_map/ppermute | solution.py:40
  67.8 21.9 %collective-permute-start.15 = (bf16[2,192,384]{2,1,0:T(8,128)(2,1)S(1)}, bf16[2,192,384]{2,1,0:T(8,128)(2,1)S(1)}, u32[]{:S(2)}, u32[]{:S(2)}) collective-permute-start(bf16[2,192,384]{2,1,0:T(8,128)(2,1)S(1)} %get-tuple-element.61.refs_1_), channel_id=1, source_target_pairs={{0,2},{1,3},{2,4},{3,5},{8,10},{9,11},{10,12},{11,13},{12,14},{13,... | collective-permute-start | bytes 884744 | tf_op jit(solution)/shard_map/ppermute | solution.py:40
  69.1 22.7 %collective-permute-start.23 = (bf16[2,192,384]{2,1,0:T(8,128)(2,1)S(1)}, bf16[2,192,384]{2,1,0:T(8,128)(2,1)S(1)}, u32[]{:S(2)}, u32[]{:S(2)}) collective-permute-start(bf16[2,192,384]{2,1,0:T(8,128)(2,1)S(1)} %get-tuple-element.61.refs_1_), channel_id=1, source_target_pairs={{0,8},{1,9},{2,10},{3,11},{4,12},{5,13},{6,14},{7,15},{8,0},{9,1},... | collective-permute-start | bytes 884744 | tf_op jit(solution)/shard_map/ppermute | solution.py:40
  69.4 62.0 %copy-start.1 = (bf16[2,2,192,384]{3,2,1,0:T(8,128)(2,1)}, bf16[2,2,192,384]{3,2,1,0:T(8,128)(2,1)S(1)}, u32[]{:S(2)}) copy-start(bf16[2,2,192,384]{3,2,1,0:T(8,128)(2,1)S(1)} %pad_maximum_fusion.5.refs_2_) | copy-start | bytes 1769476
  78.1 53.3 %copy-start.17 = (bf16[2,192,384]{2,1,0:T(8,128)(2,1)}, bf16[2,192,384]{2,1,0:T(8,128)(2,1)S(1)}, u32[]{:S(2)}) copy-start(bf16[2,192,384]{2,1,0:T(8,128)(2,1)S(1)} %collective-permute-done.13.refs_5_) | copy-start | bytes 884740
  85.0 46.4 %copy-start.18 = (bf16[2,192,384]{2,1,0:T(8,128)(2,1)}, bf16[2,192,384]{2,1,0:T(8,128)(2,1)S(1)}, u32[]{:S(2)}) copy-start(bf16[2,192,384]{2,1,0:T(8,128)(2,1)S(1)} %collective-permute-done.14.refs_6_) | copy-start | bytes 884740
  89.7 41.6 %copy-start.19 = (bf16[2,192,384]{2,1,0:T(8,128)(2,1)}, bf16[2,192,384]{2,1,0:T(8,128)(2,1)S(1)}, u32[]{:S(2)}) copy-start(bf16[2,192,384]{2,1,0:T(8,128)(2,1)S(1)} %collective-permute-done.15.refs_7_) | copy-start | bytes 884740
  89.8 5.9 %collective-permute-start.19 = (bf16[2,2,192,384]{3,2,1,0:T(8,128)(2,1)S(1)}, bf16[2,2,192,384]{3,2,1,0:T(8,128)(2,1)S(1)}, u32[]{:S(2)}, u32[]{:S(2)}) collective-permute-start(bf16[2,2,192,384]{3,2,1,0:T(8,128)(2,1)S(1)} %broadcast_select_fusion), channel_id=1, source_target_pairs={{8,12},{9,13},{12,8},{13,9},{24,28},{25,29},{28,24},{29,25}} | collective-permute-start | bytes 1769480 | tf_op jit(solution)/shard_map/ppermute | solution.py:40
  90.5 1.4 collective-permute-start.16
  91.2 5.9 %collective-permute-start.24 = (bf16[2,2,192,384]{3,2,1,0:T(8,128)(2,1)S(1)}, bf16[2,2,192,384]{3,2,1,0:T(8,128)(2,1)S(1)}, u32[]{:S(2)}, u32[]{:S(2)}) collective-permute-start(bf16[2,2,192,384]{3,2,1,0:T(8,128)(2,1)S(1)} %pad_maximum_fusion.5.refs_2_), channel_id=1, source_target_pairs={{0,8},{1,9},{2,10},{3,11},{4,12},{5,13},{6,14},{7,15},{8,0},{9,1},... | collective-permute-start | bytes 1769480 | tf_op jit(solution)/shard_map/ppermute | solution.py:40
  91.3 2.4 %collective-permute-start.22 = (bf16[2,192,384]{2,1,0:T(8,128)(2,1)S(1)}, bf16[2,192,384]{2,1,0:T(8,128)(2,1)S(1)}, u32[]{:S(2)}, u32[]{:S(2)}) collective-permute-start(bf16[2,192,384]{2,1,0:T(8,128)(2,1)S(1)} %get-tuple-element.89.refs_0_), channel_id=1, source_target_pairs={{0,8},{1,9},{2,10},{3,11},{4,12},{5,13},{6,14},{7,15},{8,0},{9,1},... | collective-permute-start | bytes 884744 | tf_op jit(solution)/shard_map/ppermute | solution.py:40
  91.8 39.5 %copy-start.20 = (bf16[2,192,384]{2,1,0:T(8,128)(2,1)}, bf16[2,192,384]{2,1,0:T(8,128)(2,1)S(1)}, u32[]{:S(2)}) copy-start(bf16[2,192,384]{2,1,0:T(8,128)(2,1)S(1)} %collective-permute-done.23.refs_15_) | copy-start | bytes 884740
  91.8 3.2 %collective-permute-start.25 = (bf16[2,192,384]{2,1,0:T(8,128)(2,1)S(1)}, bf16[2,192,384]{2,1,0:T(8,128)(2,1)S(1)}, u32[]{:S(2)}, u32[]{:S(2)}) collective-permute-start(bf16[2,192,384]{2,1,0:T(8,128)(2,1)S(1)} %collective-permute-done.11.refs_3_), channel_id=1, source_target_pairs={{0,8},{1,9},{2,10},{3,11},{4,12},{5,13},{6,14},{7,15},{8,0},{9,1},... | collective-permute-start | bytes 884744 | tf_op jit(solution)/shard_map/ppermute | solution.py:40
  92.0 39.4 %copy-start.21 = (bf16[2,192,384]{2,1,0:T(8,128)(2,1)}, bf16[2,192,384]{2,1,0:T(8,128)(2,1)S(1)}, u32[]{:S(2)}) copy-start(bf16[2,192,384]{2,1,0:T(8,128)(2,1)S(1)} %collective-permute-done.16.refs_8_) | copy-start | bytes 884740
  92.0 5.1 %collective-permute-start.26 = (bf16[2,192,384]{2,1,0:T(8,128)(2,1)S(1)}, bf16[2,192,384]{2,1,0:T(8,128)(2,1)S(1)}, u32[]{:S(2)}, u32[]{:S(2)}) collective-permute-start(bf16[2,192,384]{2,1,0:T(8,128)(2,1)S(1)} %collective-permute-done.12.refs_4_), channel_id=1, source_target_pairs={{0,8},{1,9},{2,10},{3,11},{4,12},{5,13},{6,14},{7,15},{8,0},{9,1},... | collective-permute-start | bytes 884744 | tf_op jit(solution)/shard_map/ppermute | solution.py:40
  93.7 37.7 %copy-start.22 = (bf16[2,192,384]{2,1,0:T(8,128)(2,1)}, bf16[2,192,384]{2,1,0:T(8,128)(2,1)S(1)}, u32[]{:S(2)}) copy-start(bf16[2,192,384]{2,1,0:T(8,128)(2,1)S(1)} %collective-permute-done.22.refs_14_) | copy-start | bytes 884740
  93.7 21.8 %collective-permute-start.17 = (bf16[2,192,384]{2,1,0:T(8,128)(2,1)S(1)}, bf16[2,192,384]{2,1,0:T(8,128)(2,1)S(1)}, u32[]{:S(2)}, u32[]{:S(2)}) collective-permute-start(bf16[2,192,384]{2,1,0:T(8,128)(2,1)S(1)} %collective-permute-done.15.refs_7_), channel_id=1, source_target_pairs={{4,6},{5,7},{12,14},{13,15},{20,22},{21,23},{28,30},{29,31}} | collective-permute-start | bytes 884744 | tf_op jit(solution)/shard_map/ppermute | solution.py:40
  95.0 24.2 %collective-permute-start.20 = (bf16[2,2,192,384]{3,2,1,0:T(8,128)(2,1)S(1)}, bf16[2,2,192,384]{3,2,1,0:T(8,128)(2,1)S(1)}, u32[]{:S(2)}, u32[]{:S(2)}) collective-permute-start(bf16[2,2,192,384]{3,2,1,0:T(8,128)(2,1)S(1)} %pad_maximum_fusion.5.refs_2_), channel_id=1, source_target_pairs={{8,10},{9,11},{24,26},{25,27}} | collective-permute-start | bytes 1769480 | tf_op jit(solution)/shard_map/ppermute | solution.py:40
  95.7 26.8 %collective-permute-start.21 = (bf16[2,2,192,384]{3,2,1,0:T(8,128)(2,1)S(1)}, bf16[2,2,192,384]{3,2,1,0:T(8,128)(2,1)S(1)}, u32[]{:S(2)}, u32[]{:S(2)}) collective-permute-start(bf16[2,2,192,384]{3,2,1,0:T(8,128)(2,1)S(1)} %collective-permute-done.19.refs_11_), channel_id=1, source_target_pairs={{12,14},{13,15},{28,30},{29,31}} | collective-permute-start | bytes 1769480 | tf_op jit(solution)/shard_map/ppermute | solution.py:40
  97.1 20.0 %collective-permute-start.29 = (bf16[2,192,384]{2,1,0:T(8,128)(2,1)S(1)}, bf16[2,192,384]{2,1,0:T(8,128)(2,1)S(1)}, u32[]{:S(2)}, u32[]{:S(2)}) collective-permute-start(bf16[2,192,384]{2,1,0:T(8,128)(2,1)S(1)} %collective-permute-done.15.refs_7_), channel_id=1, source_target_pairs={{0,8},{1,9},{2,10},{3,11},{4,12},{5,13},{6,14},{7,15},{8,0},{9,1},... | collective-permute-start | bytes 884744 | tf_op jit(solution)/shard_map/ppermute | solution.py:40
  97.2 21.4 %collective-permute-start.28 = (bf16[2,192,384]{2,1,0:T(8,128)(2,1)S(1)}, bf16[2,192,384]{2,1,0:T(8,128)(2,1)S(1)}, u32[]{:S(2)}, u32[]{:S(2)}) collective-permute-start(bf16[2,192,384]{2,1,0:T(8,128)(2,1)S(1)} %collective-permute-done.14.refs_6_), channel_id=1, source_target_pairs={{0,8},{1,9},{2,10},{3,11},{4,12},{5,13},{6,14},{7,15},{8,0},{9,1},... | collective-permute-start | bytes 884744 | tf_op jit(solution)/shard_map/ppermute | solution.py:40
  115.5 3.2 %collective-permute-start.27 = (bf16[2,192,384]{2,1,0:T(8,128)(2,1)S(1)}, bf16[2,192,384]{2,1,0:T(8,128)(2,1)S(1)}, u32[]{:S(2)}, u32[]{:S(2)}) collective-permute-start(bf16[2,192,384]{2,1,0:T(8,128)(2,1)S(1)} %collective-permute-done.13.refs_5_), channel_id=1, source_target_pairs={{0,8},{1,9},{2,10},{3,11},{4,12},{5,13},{6,14},{7,15},{8,0},{9,1},... | collective-permute-start | bytes 884744 | tf_op jit(solution)/shard_map/ppermute | solution.py:40
  117.1 11.5 %collective-permute-start.18 = (bf16[2,192,384]{2,1,0:T(8,128)(2,1)S(1)}, bf16[2,192,384]{2,1,0:T(8,128)(2,1)S(1)}, u32[]{:S(2)}, u32[]{:S(2)}) collective-permute-start(bf16[2,192,384]{2,1,0:T(8,128)(2,1)S(1)} %collective-permute-done.16.refs_8_), channel_id=1, source_target_pairs={{4,6},{5,7},{12,14},{13,15},{20,22},{21,23},{28,30},{29,31}} | collective-permute-start | bytes 884744 | tf_op jit(solution)/shard_map/ppermute | solution.py:40
  118.6 10.4 %collective-permute-start.31 = (bf16[2,192,384]{2,1,0:T(8,128)(2,1)S(1)}, bf16[2,192,384]{2,1,0:T(8,128)(2,1)S(1)}, u32[]{:S(2)}, u32[]{:S(2)}) collective-permute-start(bf16[2,192,384]{2,1,0:T(8,128)(2,1)S(1)} %collective-permute-done.17.refs_9_), channel_id=1, source_target_pairs={{0,8},{1,9},{2,10},{3,11},{4,12},{5,13},{6,14},{7,15},{8,0},{9,1},... | collective-permute-start | bytes 884744 | tf_op jit(solution)/shard_map/ppermute | solution.py:40
  118.7 11.9 %collective-permute-start.33 = (bf16[2,2,192,384]{3,2,1,0:T(8,128)(2,1)S(1)}, bf16[2,2,192,384]{3,2,1,0:T(8,128)(2,1)S(1)}, u32[]{:S(2)}, u32[]{:S(2)}) collective-permute-start(bf16[2,2,192,384]{3,2,1,0:T(8,128)(2,1)S(1)} %collective-permute-done.19.refs_11_), channel_id=1, source_target_pairs={{0,8},{1,9},{2,10},{3,11},{4,12},{5,13},{6,14},{7,15},{8,0},{9,1},... | collective-permute-start | bytes 1769480 | tf_op jit(solution)/shard_map/ppermute | solution.py:40
  119.2 11.4 %collective-permute-start.34 = (bf16[2,2,192,384]{3,2,1,0:T(8,128)(2,1)S(1)}, bf16[2,2,192,384]{3,2,1,0:T(8,128)(2,1)S(1)}, u32[]{:S(2)}, u32[]{:S(2)}) collective-permute-start(bf16[2,2,192,384]{3,2,1,0:T(8,128)(2,1)S(1)} %collective-permute-done.20.refs_12_), channel_id=1, source_target_pairs={{0,8},{1,9},{2,10},{3,11},{4,12},{5,13},{6,14},{7,15},{8,0},{9,1},... | collective-permute-start | bytes 1769480 | tf_op jit(solution)/shard_map/ppermute | solution.py:40
  122.6 8.7 %collective-permute-start.35 = (bf16[2,2,192,384]{3,2,1,0:T(8,128)(2,1)S(1)}, bf16[2,2,192,384]{3,2,1,0:T(8,128)(2,1)S(1)}, u32[]{:S(2)}, u32[]{:S(2)}) collective-permute-start(bf16[2,2,192,384]{3,2,1,0:T(8,128)(2,1)S(1)} %collective-permute-done.21.refs_13_), channel_id=1, source_target_pairs={{0,8},{1,9},{2,10},{3,11},{4,12},{5,13},{6,14},{7,15},{8,0},{9,1},... | collective-permute-start | bytes 1769480 | tf_op jit(solution)/shard_map/ppermute | solution.py:40
  128.6 1.6 collective-permute-start.30
  129.0 1.6 collective-permute-start.32
  141.2 8.5 %collective-permute-start.36 = (bf16[2,192,384]{2,1,0:T(8,128)(2,1)}, bf16[2,192,384]{2,1,0:T(8,128)(2,1)S(1)}, u32[]{:S(2)}, u32[]{:S(2)}) collective-permute-start(bf16[2,192,384]{2,1,0:T(8,128)(2,1)} %get-tuple-element.71), channel_id=1, source_target_pairs={{0,1},{1,0},{2,3},{3,2},{4,5},{5,4},{6,7},{7,6},{8,9},{9,8},{10,11... | collective-permute-start | bytes 884744 | tf_op jit(solution)/shard_map/ppermute | solution.py:40
  142.5 10.9 %collective-permute-start.37 = (bf16[384,384]{1,0:T(8,128)(2,1)}, bf16[384,384]{1,0:T(8,128)(2,1)S(1)}, u32[]{:S(2)}, u32[]{:S(2)}) collective-permute-start(bf16[384,384]{1,0:T(8,128)(2,1)} %get-tuple-element.68), channel_id=1, source_target_pairs={{0,8},{1,9},{2,10},{3,11},{4,12},{5,13},{6,14},{7,15},{8,0},{9,1},... | collective-permute-start | bytes 884744 | tf_op jit(solution)/shard_map/ppermute | solution.py:40
  143.1 10.2 %collective-permute-start.38 = (bf16[384,384]{1,0:T(8,128)(2,1)}, bf16[384,384]{1,0:T(8,128)(2,1)S(1)}, u32[]{:S(2)}, u32[]{:S(2)}) collective-permute-start(bf16[384,384]{1,0:T(8,128)(2,1)} %get-tuple-element.69), channel_id=1, source_target_pairs={{0,16},{1,17},{2,18},{3,19},{4,20},{5,21},{6,22},{7,23},{8,24},{9,... | collective-permute-start | bytes 884744 | tf_op jit(solution)/shard_map/ppermute | solution.py:40
  143.1 15.3 %collective-permute-start.39 = (bf16[384,384]{1,0:T(8,128)(2,1)}, bf16[384,384]{1,0:T(8,128)(2,1)S(1)}, u32[]{:S(2)}, u32[]{:S(2)}) collective-permute-start(bf16[384,384]{1,0:T(8,128)(2,1)} %get-tuple-element.70), channel_id=1, source_target_pairs={{0,24},{1,25},{2,26},{3,27},{4,28},{5,29},{6,30},{7,31},{8,16},{9,... | collective-permute-start | bytes 884744 | tf_op jit(solution)/shard_map/ppermute | solution.py:40
  (28 other events, 344.4 us)

commit v7 on v6

--- a/solution.py
+++ b/solution.py
@@ -39,18 +39,19 @@
                 pairs.append((index(*place), index(*goal)))
         return lax.ppermute(value, AXES, pairs)
 
-    def direct(self, wanted):
-        hub = self.cols - 2
-        steps = []
-        for key, source, to in sorted(wanted, key=lambda s: (s[2] != hub, abs(s[1] - s[2]))):
-            for step in steps:
-                if source not in step and to not in [goal for _, goal in step.values()]:
-                    break
-            else:
-                step = {}
-                steps.append(step)
-            step[source] = (key, to)
-        return steps
+    def ring(self, step):
+        own = {
+            col: [key for key in reversed(self.keys) if key[1] == col] for col in range(self.cols)
+        }
+        sends = {}
+        order = range(self.cols) if step > 0 else reversed(range(self.cols))
+        queue = []
+        for col in order:
+            queue = [(key, None) for key in own[col]] + [(key, n) for n, (key, _) in enumerate(queue)]
+            if 0 <= col + step < self.cols:
+                for n, item in enumerate(queue):
+                    sends[col, n] = item
+        return sends
 
 
 def hbm(count):
@@ -174,8 +175,7 @@
                 for t in range(groups):
                     row = key[0] * groups + (g ^ t)
                     for q in range(moms):
-                        index, part = sources[key, col, q, t]
-                        ref = sig_in[index] if part is None else sig_in[index].at[part]
+                        ref = sig_in[sources[key, col, q, t]]
                         at = pl.ds(pl.multiple_of((y ^ q) * half, half), half)
                         for p in range(2):
                             lane = pl.ds((2 * key[1] + p) * side, side)
@@ -265,15 +265,14 @@
     right = right_side.reshape(moments, side, 2, groups, width).transpose(0, 3, 1, 2, 4)
     right = right.reshape(rows, side, 2 * width)
     right_all = [lax.dynamic_index_in_dim(right, r ^ s, 0, keepdims=False) for s in range(rows)]
-    right_all = after(right_all, lesser_all[1:])
-    right_came = jnp.stack(right_all[:1] + [exchange_row(right_all[s], s) for s in range(1, rows)])
     diag = [jnp.concatenate([value[0], value[1]], axis=1) for value in diag]
-    diag_came = jnp.stack(
-        [diag[b] if t == 0 else exchange_row(diag[b], t) for b in range(moments) for t in range(groups)]
+    diag_all = [
+        diag[b] if t == 0 else exchange_row(diag[b], t) for b in range(moments) for t in range(groups)
+    ]
+    lesser_all, partner_all, right_all, diag_all = lax.optimization_barrier(
+        (lesser_all, partner_all, right_all, diag_all)
     )
-    lesser_all, partner_all, right_came, diag_came = lax.optimization_barrier(
-        (lesser_all, partner_all, right_came, diag_came)
-    )
+    diag_came = jnp.stack(diag_all)
 
     high = jnp.maximum(triples[..., 0], triples[..., 1])
     low = jnp.minimum(triples[..., 0], triples[..., 1])
@@ -297,124 +296,87 @@
         name="self_energy",
     )(place, quads, thirds, *lesser_all, *partner_all)
 
+    came = []
+
     def own_tiles(q):
         mine = slots[q * moments : (q + 1) * moments]
-        came = []
+        if came:
+            mine = mine[:1] + after(mine[1:], came[-1][1:])
+        got = []
         for b in range(1, moments):
-            came.append(
+            got.append(
                 plan.send(mine[b], lambda a, c, m: (a ^ (b * groups), c, m ^ q) if a > c else None)
             )
-        return [mine[0] if q == 0 else exchange_mom(mine[0], q)] + came
+        came.append([mine[0] if q == 0 else exchange_mom(mine[0], q)] + got)
 
     def by_block(came):
         return [lax.select_n(x ^ b, *came) for b in range(moments)]
 
-    came = [own_tiles(q) for q in range(moms)]
-    last, top = cols - 1, moments - 1
+    for q in range(moms):
+        own_tiles(q)
+    right_all = after(right_all, came[-1])
+    right_all = right_all[:1] + [exchange_row(right_all[s], s) for s in range(1, rows)]
+    right_came = jnp.stack(right_all)
 
     def valid(key, a):
         return key[0] * groups + a % groups > key[1]
 
-    def spread(step, values):
+    found = {}
+    own = []
+    for q in range(moms):
+        own.append(by_block(came[q]))
+        for key in plan.keys:
+            found[key, key[1], q] = own[q][key[0]]
+
+    def shift(q, direction, number, got, *behind):
+        sends = {col: item for (col, n), item in plan.ring(direction).items() if n == number}
         chosen = used = None
-        for source, (key, _) in step.items():
-            value = values[key[0]]
+        for col, (key, step) in sends.items():
+            value = own[q][key[0]] if step is None else got[step]
             if chosen is None:
                 chosen = used = value
             elif value is not used:
-                chosen = jnp.where(z == source, value, chosen)
-        goal = lambda a, c, m: ((a, step[c][1], m) if c in step and valid(step[c][0], a) else None)
-        return plan.send(chosen, goal)
-
-    def relay(value, key):
-        goal = lambda a, c, m: (a, last, m) if c == last - 1 and valid(key, a) else None
-        return plan.send(value, goal)
-
-    sends = [
-        (key, key[1], to)
-        for key in plan.keys
-        for to in range(cols)
-        if to != key[1] and (to < last or key[1] == last - 1)
-    ]
-    split = [send for send in sends if send[0][0] == top and send[2] >= send[1] - 1]
-    joint = [send for send in sends if send not in split]
-    found = {}
-    own, whole = [], None
+                chosen = jnp.where(z == col, value, chosen)
+        goal = lambda a, c, m: (
+            (a, c + direction, m) if c in sends and valid(sends[c][0], a) else None
+        )
+        value = plan.send(after(chosen, behind), goal)
+        got.append(value)
+        for col, (key, _) in sends.items():
+            found[key, col + direction, q] = value
+
+    right_got, left_got = [[] for _ in range(moms)], [[] for _ in range(moms)]
+    right_steps = max(n for _, n in plan.ring(1)) + 1
+    left_steps = max(n for _, n in plan.ring(-1)) + 1
+    for number in range(right_steps):
+        for q in range(moms):
+            behind = []
+            if q > 0:
+                behind.append(right_got[q - 1][number])
+            if number == 1 and q + 1 < moms:
+                behind.append(came[q + 1])
+            if number + 1 == right_steps and q + 1 == moms:
+                behind += [right_came, diag_came]
+            shift(q, 1, number, right_got[q], *behind)
+    for number in range(left_steps):
+        for q in range(moms):
+            shift(q, -1, number, left_got[q], right_got[q][min(number, right_steps - 1)])
+
     buffers = []
 
-    def number(value):
+    def number_of(value):
         for index, held in enumerate(buffers):
             if held is value:
                 return index
         buffers.append(value)
         return len(buffers) - 1
 
-    for q in range(moms):
-        own.append(by_block(came[q]))
-        for key in plan.keys:
-            if key[0] == top:
-                found[key, key[1], q] = (own[q][top], None)
-    joint_values = [jnp.stack([own[k][b] for k in range(moms)]) for b in range(moments)]
-    for key in plan.keys:
-        if key[0] < top:
-            for q in range(moms):
-                found[key, key[1], q] = (joint_values[key[0]], q)
-
-    steps = plan.direct(split)
-    sent, relayed = {}, [[] for _ in range(moms)]
-
-    def split_step(q, n):
-        value = own[q]
-        if q > 0:
-            value = after(value, sent[q - 1, n], relayed[q - 1][:n])
-        sent[q, n] = value = spread(steps[n], value)
-        for key, to in steps[n].values():
-            found[key, to, q] = (value, None)
-
-    def split_relay(q, key):
-        value = found[key, last - 1, q][0]
-        if q + 1 < moms:
-            value = after(value, came[q + 1])
-        if q > 0:
-            value = after(value, found[key, last, q - 1][0])
-        value = relay(value, key)
-        found[key, last, q] = (value, None)
-        relayed[q].append(value)
-
-    relays = sorted([key for key in plan.keys if key[1] < last - 1], key=lambda key: -key[1])
-    for q in range(moms):
-        for n in range(len(steps)):
-            split_step(q, n)
-        for key in relays:
-            if key[0] == top:
-                split_relay(q, key)
-    for n, step in enumerate(plan.direct(joint)):
-        behind = sent[moms - 1, min(n, len(steps) - 1)]
-        value = spread(step, after(joint_values, behind, relayed[0]))
-        for key, to in step.values():
-            for q in range(moms):
-                found[key, to, q] = (value, q)
-    for key in relays:
-        if key[0] < top:
-            value = relay(found[key, last - 1, 0][0], key)
-            for q in range(moms):
-                found[key, last, q] = (value, q)
-
-    sources = {}
-    for (key, col, q), (value, part) in found.items():
-        sources[key, col, q, 0] = (number(value), part)
-    swapped = {}
-    for (key, col, q), (value, part) in found.items():
-        for t in range(1, groups):
-            index = number(value)
-            if (index, t) not in swapped:
-                swapped[index, t] = exchange_row(value, t)
-            sources[key, col, q, t] = ((index, t), part)
-    place_of = {name: len(buffers) + n for n, name in enumerate(swapped)}
-    for name, (index, part) in sources.items():
-        if name[3] > 0:
-            sources[name] = (place_of[index], part)
-    sig_all = buffers + list(swapped.values())
+    sources = {name + (0,): number_of(value) for name, value in found.items()}
+    sig_all = list(buffers)
+    for t in range(1, groups):
+        for name, value in found.items():
+            sources[name + (t,)] = len(sig_all) + number_of(value)
+        sig_all += [exchange_row(value, t) for value in buffers]
 
     solved = pl.pallas_call(
         functools.partial(solve_kernel, plan, sources),

time: 163 us -> 155 us (0.951)
  waiting for transfers between devices: 88.2 us -> 69.3 us
  starting transfers between devices: 30.4 us -> 42.4 us
    ppermute x40 -> x43, waiting for transfers between devices: 88.2 us -> 69.3 us  [send(): return lax.ppermute(value, AXES, pairs)]
    ppermute x40 -> x43, starting transfers between devices: 30.4 us -> 42.4 us  [send(): return lax.ppermute(value, AXES, pairs)]
    unnamed x73 -> x91, local copies, waits for them, and re-layouts: 5.86 us -> 4.44 us
    another operation x7 -> x2, other arithmetic: 5.04 us -> 4.24 us  [the longest x1 3.04 us: on_device(): diag_came = jnp.stack(diag_all)]
  transfers between devices with their start and end apart: 40 -> 43, of which waited for: 16 -> 13; matrix products, arithmetic and copies ran while one was open for 8% -> 8% of each run, Pallas kernels for 2% -> 2%
where the time goes in v7:
time: 155 us; the launch traced here: 154 us
  waiting for transfers between devices  69.3 us (45%)
  starting transfers between devices  42.4 us (27%)
  Pallas kernels  17.4 us (11%)
  local copies, waits for them, and re-layouts  15.8 us (10%)
  other arithmetic  7.33 us (5%)
    ppermute x43, waiting for transfers between devices, send(): return lax.ppermute(value, AXES, pairs)  69.3 us
    ppermute x43, starting transfers between devices, send(): return lax.ppermute(value, AXES, pairs)  42.4 us
    pallas_call x1, Pallas kernels, on_device(): pl.pallas_call(functools.partial(solve_kernel, plan, sources), out_shape=...  8.18 us
    pallas_call x1, Pallas kernels, on_device(): pl.pallas_call(functools.partial(sigma_kernel, plan, pair_count, chunks),...  6.24 us
    unnamed x91, local copies, waits for them, and re-layouts  4.44 us
  transfers between devices with their start and end apart: 43, of which 13 were waited for; matrix products, arithmetic and copies ran while one was open for 8% of the time, Pallas kernels for 2%

profile of v7, /device:TPU:25, one launch (start us, length us, event | category | flops | bytes accessed | tf_op | source)
XLA Modules:
  0.0 153.6 jit_solution(17987744939945502856)
XLA Ops:
  0.7 2.0 %constant_dynamic-slice_fusion.4 = bf16[2,2,192,384]{3,2,1,0:T(8,128)(2,1)} fusion(bf16[2,2,384,384]{3,2,1,0:T(8,128)(2,1)} %refs_0_, s32[]{:T(128)S(6)} %select_n.207), kind=kLoop, calls=%fused_computation.35 | loop fusion | bytes 1179652 | tf_op jit(solution)/shard_map/dynamic_slice | solution.py:251
  2.7 0.8 copy.11
  3.5 0.9 dynamic-slice_bitcast_fusion.1
  4.4 0.9 dynamic-slice_bitcast_fusion
  5.3 1.2 collective-permute-start.2
  6.5 1.2 collective-permute-start.1
  8.0 2.0 %copy.13 = bf16[2,384,2,384]{1,3,2,0:T(8,128)(2,1)S(1)} copy(bf16[2,384,2,384]{3,2,1,0:T(2,128)(2,1)S(1)} %copy-done.10) | data formatting | bytes 2359296 | tf_op jit(solution)/shard_map/optimization_barrier | solution.py:227
  10.1 9.7 %collective-permute-done.2 = bf16[2,384,384]{2,1,0:T(8,128)(2,1)} collective-permute-done((bf16[2,384,384]{2,1,0:T(8,128)(2,1)}, bf16[2,384,384]{2,1,0:T(8,128)(2,1)}, u32[]{:S(2)}, u32[]{:S(2)}) %collective-permute-start.2) | collective-permute-done | bytes 589856 | tf_op jit(solution)/shard_map/ppermute | solution.py:40
  19.8 1.2 bitcast_select_fusion
  21.2 1.6 %collective-permute-start.4 = (bf16[384,768]{1,0:T(8,128)(2,1)S(1)}, bf16[384,768]{1,0:T(8,128)(2,1)}, u32[]{:S(2)}, u32[]{:S(2)}) collective-permute-start(bf16[384,768]{1,0:T(8,128)(2,1)S(1)} %pad_maximum_fusion.4), channel_id=1, source_target_pairs={{0,8},{1,9},{2,10},{3,11},{4,12},{5,13},{6,14},{7,15},{8,0},{9,1},... | collective-permute-start | bytes 1769480 | tf_op jit(solution)/shard_map/ppermute | solution.py:40
  23.3 0.9 copy.16
  24.2 0.9 copy.17
  25.1 0.9 copy.18
  27.8 5.6 %collective-permute-done.refs_1_ = bf16[2,2,192,384]{3,2,1,0:T(8,128)(2,1)} collective-permute-done((bf16[2,2,192,384]{3,2,1,0:T(8,128)(2,1)}, bf16[2,2,192,384]{3,2,1,0:T(8,128)(2,1)}, u32[]{:S(2)}, u32[]{:S(2)}) %collective-permute-start) | collective-permute-done | bytes 589856 | tf_op jit(solution)/shard_map/ppermute | solution.py:40
  33.4 6.2 %self_energy.1 = (bf16[2,192,384]{2,1,0:T(8,128)(2,1)}, bf16[2,192,384]{2,1,0:T(8,128)(2,1)}, bf16[2,192,384]{2,1,0:T(8,128)(2,1)}, bf16[2,192,384]{2,1,0:T(8,128)(2,1)}) custom-call(s32[3]{0:T(128)} %pad_add_fusion.place, s32[4,8]{1,0:T(4,128)} %fusion.1.quads, s32[4,8]{1,0:T(4,128)} %slice_bitcast_fusion.4.thirds, bf16[2,2,384,384]{3,2,1,0:T(8,128)(2,1)} %refs_0_, ...), custom_call_target="tpu_custom_call" | custom-call | tf_op jit(solution)/shard_map/self_energy/pallas_call | solution.py:281
  39.6 0.8 collective-permute-start.6
  40.4 1.3 collective-permute-start.5
  42.5 1.3 collective-permute-start.11
  43.8 3.6 %collective-permute-done.5.refs_2_ = bf16[2,192,384]{2,1,0:T(8,128)(2,1)S(1)} collective-permute-done((bf16[2,192,384]{2,1,0:T(8,128)(2,1)}, bf16[2,192,384]{2,1,0:T(8,128)(2,1)S(1)}, u32[]{:S(2)}, u32[]{:S(2)}) %collective-permute-start.5) | collective-permute-done | bytes 294944 | tf_op jit(solution)/shard_map/ppermute | solution.py:40
  47.4 7.8 %collective-permute-done.11.refs_4_ = bf16[2,192,384]{2,1,0:T(8,128)(2,1)S(1)} collective-permute-done((bf16[2,192,384]{2,1,0:T(8,128)(2,1)S(1)}, bf16[2,192,384]{2,1,0:T(8,128)(2,1)S(1)}, u32[]{:S(2)}, u32[]{:S(2)}) %collective-permute-start.11) | collective-permute-done | bytes 294944 | tf_op jit(solution)/shard_map/ppermute | solution.py:40
  55.3 1.3 collective-permute-start.12
  56.6 1.3 collective-permute-start.13
  58.0 5.6 %collective-permute-done.12.refs_5_ = bf16[2,192,384]{2,1,0:T(8,128)(2,1)S(1)} collective-permute-done((bf16[2,192,384]{2,1,0:T(8,128)(2,1)S(1)}, bf16[2,192,384]{2,1,0:T(8,128)(2,1)S(1)}, u32[]{:S(2)}, u32[]{:S(2)}) %collective-permute-start.12) | collective-permute-done | bytes 294944 | tf_op jit(solution)/shard_map/ppermute | solution.py:40
  63.7 5.1 %collective-permute-done.13.refs_6_ = bf16[2,192,384]{2,1,0:T(8,128)(2,1)S(1)} collective-permute-done((bf16[2,192,384]{2,1,0:T(8,128)(2,1)S(1)}, bf16[2,192,384]{2,1,0:T(8,128)(2,1)S(1)}, u32[]{:S(2)}, u32[]{:S(2)}) %collective-permute-start.13) | collective-permute-done | bytes 294944 | tf_op jit(solution)/shard_map/ppermute | solution.py:40
  68.9 1.3 collective-permute-start.14
  70.2 1.3 collective-permute-start.15
  72.2 1.9 %collective-permute-start.8 = (bf16[384,384]{1,0:T(8,128)(2,1)S(1)}, bf16[384,384]{1,0:T(8,128)(2,1)S(1)}, u32[]{:S(2)}, u32[]{:S(2)}) collective-permute-start(bf16[384,384]{1,0:T(8,128)(2,1)S(1)} %bitcast.67), channel_id=1, source_target_pairs={{0,8},{1,9},{2,10},{3,11},{4,12},{5,13},{6,14},{7,15},{8,0},{9,1},... | collective-permute-start | bytes 884744 | tf_op jit(solution)/shard_map/ppermute | solution.py:40
  74.0 3.8 %collective-permute-start.9 = (bf16[384,384]{1,0:T(8,128)(2,1)S(1)}, bf16[384,384]{1,0:T(8,128)(2,1)S(1)}, u32[]{:S(2)}, u32[]{:S(2)}) collective-permute-start(bf16[384,384]{1,0:T(8,128)(2,1)S(1)} %bitcast.66), channel_id=1, source_target_pairs={{0,16},{1,17},{2,18},{3,19},{4,20},{5,21},{6,22},{7,23},{8,24},{9,... | collective-permute-start | bytes 884744 | tf_op jit(solution)/shard_map/ppermute | solution.py:40
  77.8 10.0 %collective-permute-start.10 = (bf16[384,384]{1,0:T(8,128)(2,1)S(1)}, bf16[384,384]{1,0:T(8,128)(2,1)S(1)}, u32[]{:S(2)}, u32[]{:S(2)}) collective-permute-start(bf16[384,384]{1,0:T(8,128)(2,1)S(1)} %bitcast.65), channel_id=1, source_target_pairs={{0,24},{1,25},{2,26},{3,27},{4,28},{5,29},{6,30},{7,31},{8,16},{9,... | collective-permute-start | bytes 884744 | tf_op jit(solution)/shard_map/ppermute | solution.py:40
  89.1 4.0 %collective-permute-done.10 = bf16[384,384]{1,0:T(8,128)(2,1)S(1)} collective-permute-done((bf16[384,384]{1,0:T(8,128)(2,1)S(1)}, bf16[384,384]{1,0:T(8,128)(2,1)S(1)}, u32[]{:S(2)}, u32[]{:S(2)}) %collective-permute-start.10) | collective-permute-done | bytes 294944 | tf_op jit(solution)/shard_map/ppermute | solution.py:40
  93.1 1.3 collective-permute-start.16
  94.4 1.3 collective-permute-start.17
  97.0 9.1 %collective-permute-done.16.refs_9_ = bf16[2,192,384]{2,1,0:T(8,128)(2,1)S(1)} collective-permute-done((bf16[2,192,384]{2,1,0:T(8,128)(2,1)S(1)}, bf16[2,192,384]{2,1,0:T(8,128)(2,1)S(1)}, u32[]{:S(2)}, u32[]{:S(2)}) %collective-permute-start.16) | collective-permute-done | bytes 294944 | tf_op jit(solution)/shard_map/ppermute | solution.py:40
  106.5 2.5 %collective-permute-done.17.refs_10_ = bf16[2,192,384]{2,1,0:T(8,128)(2,1)S(1)} collective-permute-done((bf16[2,192,384]{2,1,0:T(8,128)(2,1)S(1)}, bf16[2,192,384]{2,1,0:T(8,128)(2,1)S(1)}, u32[]{:S(2)}, u32[]{:S(2)}) %collective-permute-start.17) | collective-permute-done | bytes 294944 | tf_op jit(solution)/shard_map/ppermute | solution.py:40
  109.0 3.0 %pad_maximum_fusion.diag = bf16[4,384,768]{2,1,0:T(8,128)(2,1)} fusion(bf16[1,384,768]{2,1,0:T(8,128)(2,1)} %bitcast.24, bf16[1,384,768]{2,1,0:T(8,128)(2,1)S(1)} %bitcast.60, bf16[1,384,768]{2,1,0:T(8,128)(2,1)} %bitcast.22, bf16[1,384,768]{2,1,0:T(8,128)(2,1)S(1)} %bitcast.61), kind=kLoop, calls=%fused_computation | loop fusion | flops 3538944 | bytes 4718592 | tf_op jit(solution)/shard_map/stack | solution.py:275
  112.1 1.2 pad_maximum_fusion.1.right
  113.3 0.8 collective-permute-start.22
  115.3 1.5 collective-permute-start.18
  118.0 4.7 %collective-permute-done.18.refs_11_ = bf16[2,192,384]{2,1,0:T(8,128)(2,1)S(1)} collective-permute-done((bf16[2,192,384]{2,1,0:T(8,128)(2,1)S(1)}, bf16[2,192,384]{2,1,0:T(8,128)(2,1)S(1)}, u32[]{:S(2)}, u32[]{:S(2)}) %collective-permute-start.18) | collective-permute-done | bytes 294944 | tf_op jit(solution)/shard_map/ppermute | solution.py:40
  122.8 1.5 collective-permute-done.34.refs_27_
  125.2 8.2 %substitution.1 = (bf16[384,384]{1,0:T(8,128)(2,1)}, bf16[384,384]{1,0:T(8,128)(2,1)}, bf16[384,384]{1,0:T(8,128)(2,1)}, bf16[384,384]{1,0:T(8,128)(2,1)}) custom-call(s32[3]{0:T(128)} %pad_add_fusion.place, bf16[4,384,768]{2,1,0:T(8,128)(2,1)} %pad_maximum_fusion.diag, bf16[4,384,384]{2,1,0:T(8,128)(2,1)} %pad_maximum_fusion.1.right, ...), custom_call_target="tpu_custom_call" | custom-call | tf_op jit(solution)/shard_map/substitution/pallas_call | solution.py:381
  134.1 1.6 %collective-permute-start.41 = (bf16[384,384]{1,0:T(8,128)(2,1)}, bf16[384,384]{1,0:T(8,128)(2,1)S(1)}, u32[]{:S(2)}, u32[]{:S(2)}) collective-permute-start(bf16[384,384]{1,0:T(8,128)(2,1)} %get-tuple-element.83), channel_id=1, source_target_pairs={{0,16},{1,17},{2,18},{3,19},{4,20},{5,21},{6,22},{7,23},{8,24},{9,... | collective-permute-start | bytes 884744 | tf_op jit(solution)/shard_map/ppermute | solution.py:40
  135.8 6.1 %collective-permute-done.39.refs_3_ = bf16[2,192,384]{2,1,0:T(8,128)(2,1)S(1)} collective-permute-done((bf16[2,192,384]{2,1,0:T(8,128)(2,1)S(1)}, bf16[2,192,384]{2,1,0:T(8,128)(2,1)S(1)}, u32[]{:S(2)}, u32[]{:S(2)}) %collective-permute-start.39) | collective-permute-done | bytes 294944 | tf_op jit(solution)/shard_map/ppermute | solution.py:40
  141.9 0.7 copy-done.38
  142.6 2.9 %place_sigma.1 = bf16[2,2,384,384]{3,2,1,0:T(8,128)(2,1)} custom-call(s32[3]{0:T(128)} %pad_add_fusion.place, bf16[2,192,384]{2,1,0:T(8,128)(2,1)} %get-tuple-element.55.refs_0_, bf16[2,192,384]{2,1,0:T(8,128)(2,1)} %get-tuple-element.56.refs_1_, bf16[2,192,384]{2,1,0:T(8,128)(2,1)} %copy-done.2, bf16[2,192,384]{2,1,0:T(8,128)(2,1)} %copy-done.38), custom_call_target="tpu_custom_call" | custom-call | tf_op jit(solution)/shard_map/place_sigma/pallas_call | solution.py:401
  145.6 3.9 %collective-permute-done.42 = bf16[384,384]{1,0:T(8,128)(2,1)S(1)} collective-permute-done((bf16[384,384]{1,0:T(8,128)(2,1)}, bf16[384,384]{1,0:T(8,128)(2,1)S(1)}, u32[]{:S(2)}, u32[]{:S(2)}) %collective-permute-start.42) | collective-permute-done | bytes 294944 | tf_op jit(solution)/shard_map/ppermute | solution.py:40
  149.9 0.8 copy.19
  150.8 2.8 %copy.21 = bf16[2,384,2,384]{3,2,1,0:T(2,128)(2,1)} copy(bf16[2,384,2,384]{1,3,2,0:T(8,128)(2,1)S(1)} %bitcast.57) | data formatting | bytes 2359296
  (160 shorter events, 11.9 us)
Async XLA Ops:
  5.3 14.5 %collective-permute-start.2 = (bf16[2,384,384]{2,1,0:T(8,128)(2,1)}, bf16[2,384,384]{2,1,0:T(8,128)(2,1)}, u32[]{:S(2)}, u32[]{:S(2)}) collective-permute-start(bf16[2,384,384]{2,1,0:T(8,128)(2,1)} %dynamic-slice_bitcast_fusion), channel_id=1, source_target_pairs={{0,16},{1,17},{2,18},{3,19},{4,20},{5,21},{6,22},{7,23},{8,24},{9,... | collective-permute-start | bytes 1769480 | tf_op jit(solution)/shard_map/ppermute | solution.py:40
  6.5 21.3 %collective-permute-start.1 = (bf16[2,2,192,384]{3,2,1,0:T(8,128)(2,1)}, bf16[2,2,192,384]{3,2,1,0:T(8,128)(2,1)}, u32[]{:S(2)}, u32[]{:S(2)}) collective-permute-start(bf16[2,2,192,384]{3,2,1,0:T(8,128)(2,1)} %dynamic-slice_bitcast_fusion.1), channel_id=1, source_target_pairs={{0,1},{1,0},{2,3},{3,2},{4,5},{5,4},{6,7},{7,6},{8,9},{9,8},{10,11... | collective-permute-start | bytes 1769480 | tf_op jit(solution)/shard_map/ppermute | solution.py:40
  7.8 25.6 %collective-permute-start = (bf16[2,2,192,384]{3,2,1,0:T(8,128)(2,1)}, bf16[2,2,192,384]{3,2,1,0:T(8,128)(2,1)}, u32[]{:S(2)}, u32[]{:S(2)}) collective-permute-start(bf16[2,2,192,384]{3,2,1,0:T(8,128)(2,1)} %constant_dynamic-slice_fusion.4), channel_id=1, source_target_pairs={{0,1},{1,0},{2,3},{3,2},{4,5},{5,4},{6,7},{7,6},{8,9},{9,8},{10,11... | collective-permute-start | bytes 1769480 | tf_op jit(solution)/shard_map/ppermute | solution.py:40
  21.2 12.2 %collective-permute-start.4 = (bf16[384,768]{1,0:T(8,128)(2,1)S(1)}, bf16[384,768]{1,0:T(8,128)(2,1)}, u32[]{:S(2)}, u32[]{:S(2)}) collective-permute-start(bf16[384,768]{1,0:T(8,128)(2,1)S(1)} %pad_maximum_fusion.4), channel_id=1, source_target_pairs={{0,8},{1,9},{2,10},{3,11},{4,12},{5,13},{6,14},{7,15},{8,0},{9,1},... | collective-permute-start | bytes 1769480 | tf_op jit(solution)/shard_map/ppermute | solution.py:40
  22.8 10.5 %collective-permute-start.3 = (bf16[384,768]{1,0:T(8,128)(2,1)S(1)}, bf16[384,768]{1,0:T(8,128)(2,1)}, u32[]{:S(2)}, u32[]{:S(2)}) collective-permute-start(bf16[384,768]{1,0:T(8,128)(2,1)S(1)} %pad_maximum_fusion.3), channel_id=1, source_target_pairs={{0,8},{1,9},{2,10},{3,11},{4,12},{5,13},{6,14},{7,15},{8,0},{9,1},... | collective-permute-start | bytes 1769480 | tf_op jit(solution)/shard_map/ppermute | solution.py:40
  39.6 2.1 %collective-permute-start.6 = (bf16[2,192,384]{2,1,0:T(8,128)(2,1)}, bf16[2,192,384]{2,1,0:T(8,128)(2,1)S(1)}, u32[]{:S(2)}, u32[]{:S(2)}) collective-permute-start(bf16[2,192,384]{2,1,0:T(8,128)(2,1)} %get-tuple-element.56.refs_1_), channel_id=1, source_target_pairs={{8,24},{9,25},{16,0},{17,1},{18,2},{19,3},{24,8},{25,9},{26,10},{2... | collective-permute-start | bytes 884744 | tf_op jit(solution)/shard_map/ppermute | solution.py:40
  40.4 6.9 %collective-permute-start.5 = (bf16[2,192,384]{2,1,0:T(8,128)(2,1)}, bf16[2,192,384]{2,1,0:T(8,128)(2,1)S(1)}, u32[]{:S(2)}, u32[]{:S(2)}) collective-permute-start(bf16[2,192,384]{2,1,0:T(8,128)(2,1)} %get-tuple-element.57), channel_id=1, source_target_pairs={{0,1},{1,0},{2,3},{3,2},{4,5},{5,4},{6,7},{7,6},{8,9},{9,8},{10,11... | collective-permute-start | bytes 884744 | tf_op jit(solution)/shard_map/ppermute | solution.py:40
  41.7 5.6 %collective-permute-start.7 = (bf16[2,192,384]{2,1,0:T(8,128)(2,1)}, bf16[2,192,384]{2,1,0:T(8,128)(2,1)S(1)}, u32[]{:S(2)}, u32[]{:S(2)}) collective-permute-start(bf16[2,192,384]{2,1,0:T(8,128)(2,1)} %get-tuple-element.85), channel_id=1, source_target_pairs={{8,25},{9,24},{16,1},{17,0},{18,3},{19,2},{24,9},{25,8},{26,11},{2... | collective-permute-start | bytes 884744 | tf_op jit(solution)/shard_map/ppermute | solution.py:40
  42.5 12.8 %collective-permute-start.11 = (bf16[2,192,384]{2,1,0:T(8,128)(2,1)S(1)}, bf16[2,192,384]{2,1,0:T(8,128)(2,1)S(1)}, u32[]{:S(2)}, u32[]{:S(2)}) collective-permute-start(bf16[2,192,384]{2,1,0:T(8,128)(2,1)S(1)} %broadcast_select_fusion.1.refs_1_), channel_id=1, source_target_pairs={{0,2},{1,3},{2,4},{3,5},{8,10},{9,11},{10,12},{11,13},{12,14},{13,... | collective-permute-start | bytes 884744 | tf_op jit(solution)/shard_map/ppermute | solution.py:40
  47.4 41.0 %copy-start.4 = (bf16[2,192,384]{2,1,0:T(8,128)(2,1)}, bf16[2,192,384]{2,1,0:T(8,128)(2,1)S(1)}, u32[]{:S(2)}) copy-start(bf16[2,192,384]{2,1,0:T(8,128)(2,1)S(1)} %broadcast_select_fusion.refs_3_) | copy-start | bytes 884740
  55.3 8.4 %collective-permute-start.12 = (bf16[2,192,384]{2,1,0:T(8,128)(2,1)S(1)}, bf16[2,192,384]{2,1,0:T(8,128)(2,1)S(1)}, u32[]{:S(2)}, u32[]{:S(2)}) collective-permute-start(bf16[2,192,384]{2,1,0:T(8,128)(2,1)S(1)} %broadcast_select_fusion.refs_3_), channel_id=1, source_target_pairs={{0,2},{1,3},{2,4},{3,5},{8,10},{9,11},{10,12},{11,13},{12,14},{13,... | collective-permute-start | bytes 884744 | tf_op jit(solution)/shard_map/ppermute | solution.py:40
  56.6 55.4 %copy-start.7 = (bf16[2,192,384]{2,1,0:T(8,128)(2,1)}, bf16[2,192,384]{2,1,0:T(8,128)(2,1)S(1)}, u32[]{:S(2)}) copy-start(bf16[2,192,384]{2,1,0:T(8,128)(2,1)S(1)} %get-tuple-element.95.refs_0_) | copy-start | bytes 884740
  56.6 12.2 %collective-permute-start.13 = (bf16[2,192,384]{2,1,0:T(8,128)(2,1)S(1)}, bf16[2,192,384]{2,1,0:T(8,128)(2,1)S(1)}, u32[]{:S(2)}, u32[]{:S(2)}) collective-permute-start(bf16[2,192,384]{2,1,0:T(8,128)(2,1)S(1)} %get-tuple-element.73), channel_id=1, source_target_pairs={{2,4},{3,5},{4,6},{5,7},{8,10},{9,11},{10,12},{11,13},{12,14},{13,... | collective-permute-start | bytes 884744 | tf_op jit(solution)/shard_map/ppermute | solution.py:40
  58.0 16.1 %collective-permute-start.24 = (bf16[2,192,384]{2,1,0:T(8,128)(2,1)S(1)}, bf16[2,192,384]{2,1,0:T(8,128)(2,1)S(1)}, u32[]{:S(2)}, u32[]{:S(2)}) collective-permute-start(bf16[2,192,384]{2,1,0:T(8,128)(2,1)S(1)} %broadcast_select_fusion.1.refs_1_), channel_id=1, source_target_pairs={{0,8},{1,9},{2,10},{3,11},{4,12},{5,13},{6,14},{7,15},{8,0},{9,1},... | collective-permute-start | bytes 884744 | tf_op jit(solution)/shard_map/ppermute | solution.py:40
  63.7 48.4 %copy-start.6 = (bf16[2,192,384]{2,1,0:T(8,128)(2,1)}, bf16[2,192,384]{2,1,0:T(8,128)(2,1)S(1)}, u32[]{:S(2)}) copy-start(bf16[2,192,384]{2,1,0:T(8,128)(2,1)S(1)} %collective-permute-done.12.refs_5_) | copy-start | bytes 884740
  63.7 48.3 %copy-start.8 = (bf16[2,192,384]{2,1,0:T(8,128)(2,1)}, bf16[2,192,384]{2,1,0:T(8,128)(2,1)S(1)}, u32[]{:S(2)}) copy-start(bf16[2,192,384]{2,1,0:T(8,128)(2,1)S(1)} %get-tuple-element.93.refs_2_) | copy-start | bytes 884740
  68.9 43.2 %copy-start.12 = (bf16[2,192,384]{2,1,0:T(8,128)(2,1)}, bf16[2,192,384]{2,1,0:T(8,128)(2,1)S(1)}, u32[]{:S(2)}) copy-start(bf16[2,192,384]{2,1,0:T(8,128)(2,1)S(1)} %collective-permute-done.13.refs_6_) | copy-start | bytes 884740
  68.9 9.0 %collective-permute-start.14 = (bf16[2,192,384]{2,1,0:T(8,128)(2,1)S(1)}, bf16[2,192,384]{2,1,0:T(8,128)(2,1)S(1)}, u32[]{:S(2)}, u32[]{:S(2)}) collective-permute-start(bf16[2,192,384]{2,1,0:T(8,128)(2,1)S(1)} %get-tuple-element.74), channel_id=1, source_target_pairs={{2,4},{3,5},{4,6},{5,7},{8,10},{9,11},{10,12},{11,13},{12,14},{13,... | collective-permute-start | bytes 884744 | tf_op jit(solution)/shard_map/ppermute | solution.py:40
  70.2 17.6 %collective-permute-start.15 = (bf16[2,192,384]{2,1,0:T(8,128)(2,1)S(1)}, bf16[2,192,384]{2,1,0:T(8,128)(2,1)S(1)}, u32[]{:S(2)}, u32[]{:S(2)}) collective-permute-start(bf16[2,192,384]{2,1,0:T(8,128)(2,1)S(1)} %collective-permute-done.13.refs_6_), channel_id=1, source_target_pairs={{4,6},{5,7},{10,12},{11,13},{12,14},{13,15},{20,22},{21,23},{26,28... | collective-permute-start | bytes 884744 | tf_op jit(solution)/shard_map/ppermute | solution.py:40
  71.5 16.3 %collective-permute-start.19 = (bf16[2,192,384]{2,1,0:T(8,128)(2,1)S(1)}, bf16[2,192,384]{2,1,0:T(8,128)(2,1)S(1)}, u32[]{:S(2)}, u32[]{:S(2)}) collective-permute-start(bf16[2,192,384]{2,1,0:T(8,128)(2,1)S(1)} %broadcast_select_fusion.1.refs_1_), channel_id=1, source_target_pairs={{2,0},{3,1},{10,8},{11,9},{12,10},{13,11},{18,16},{19,17},{26,24},... | collective-permute-start | bytes 884744 | tf_op jit(solution)/shard_map/ppermute | solution.py:40
  72.2 16.2 %collective-permute-start.8 = (bf16[384,384]{1,0:T(8,128)(2,1)S(1)}, bf16[384,384]{1,0:T(8,128)(2,1)S(1)}, u32[]{:S(2)}, u32[]{:S(2)}) collective-permute-start(bf16[384,384]{1,0:T(8,128)(2,1)S(1)} %bitcast.67), channel_id=1, source_target_pairs={{0,8},{1,9},{2,10},{3,11},{4,12},{5,13},{6,14},{7,15},{8,0},{9,1},... | collective-permute-start | bytes 884744 | tf_op jit(solution)/shard_map/ppermute | solution.py:40
  74.0 14.4 %collective-permute-start.9 = (bf16[384,384]{1,0:T(8,128)(2,1)S(1)}, bf16[384,384]{1,0:T(8,128)(2,1)S(1)}, u32[]{:S(2)}, u32[]{:S(2)}) collective-permute-start(bf16[384,384]{1,0:T(8,128)(2,1)S(1)} %bitcast.66), channel_id=1, source_target_pairs={{0,16},{1,17},{2,18},{3,19},{4,20},{5,21},{6,22},{7,23},{8,24},{9,... | collective-permute-start | bytes 884744 | tf_op jit(solution)/shard_map/ppermute | solution.py:40
  77.8 15.3 %collective-permute-start.10 = (bf16[384,384]{1,0:T(8,128)(2,1)S(1)}, bf16[384,384]{1,0:T(8,128)(2,1)S(1)}, u32[]{:S(2)}, u32[]{:S(2)}) collective-permute-start(bf16[384,384]{1,0:T(8,128)(2,1)S(1)} %bitcast.65), channel_id=1, source_target_pairs={{0,24},{1,25},{2,26},{3,27},{4,28},{5,29},{6,30},{7,31},{8,16},{9,... | collective-permute-start | bytes 884744 | tf_op jit(solution)/shard_map/ppermute | solution.py:40
  87.8 6.6 %collective-permute-start.26 = (bf16[2,192,384]{2,1,0:T(8,128)(2,1)S(1)}, bf16[2,192,384]{2,1,0:T(8,128)(2,1)S(1)}, u32[]{:S(2)}, u32[]{:S(2)}) collective-permute-start(bf16[2,192,384]{2,1,0:T(8,128)(2,1)S(1)} %broadcast_select_fusion.refs_3_), channel_id=1, source_target_pairs={{0,8},{1,9},{2,10},{3,11},{4,12},{5,13},{6,14},{7,15},{8,0},{9,1},... | collective-permute-start | bytes 884744 | tf_op jit(solution)/shard_map/ppermute | solution.py:40
  87.8 7.9 %collective-permute-start.23 = (bf16[2,192,384]{2,1,0:T(8,128)(2,1)S(1)}, bf16[2,192,384]{2,1,0:T(8,128)(2,1)S(1)}, u32[]{:S(2)}, u32[]{:S(2)}) collective-permute-start(bf16[2,192,384]{2,1,0:T(8,128)(2,1)S(1)} %get-tuple-element.95.refs_0_), channel_id=1, source_target_pairs={{0,8},{1,9},{2,10},{3,11},{4,12},{5,13},{6,14},{7,15},{8,0},{9,1},... | collective-permute-start | bytes 884744 | tf_op jit(solution)/shard_map/ppermute | solution.py:40
  88.3 8.1 %collective-permute-start.27 = (bf16[2,192,384]{2,1,0:T(8,128)(2,1)S(1)}, bf16[2,192,384]{2,1,0:T(8,128)(2,1)S(1)}, u32[]{:S(2)}, u32[]{:S(2)}) collective-permute-start(bf16[2,192,384]{2,1,0:T(8,128)(2,1)S(1)} %collective-permute-done.11.refs_4_), channel_id=1, source_target_pairs={{0,8},{1,9},{2,10},{3,11},{4,12},{5,13},{6,14},{7,15},{8,0},{9,1},... | collective-permute-start | bytes 884744 | tf_op jit(solution)/shard_map/ppermute | solution.py:40
  88.4 8.1 %collective-permute-start.20 = (bf16[2,192,384]{2,1,0:T(8,128)(2,1)S(1)}, bf16[2,192,384]{2,1,0:T(8,128)(2,1)S(1)}, u32[]{:S(2)}, u32[]{:S(2)}) collective-permute-start(bf16[2,192,384]{2,1,0:T(8,128)(2,1)S(1)} %broadcast_select_fusion.refs_3_), channel_id=1, source_target_pairs={{2,0},{3,1},{10,8},{11,9},{12,10},{13,11},{18,16},{19,17},{26,24},... | collective-permute-start | bytes 884744 | tf_op jit(solution)/shard_map/ppermute | solution.py:40
  93.1 13.0 %collective-permute-start.16 = (bf16[2,192,384]{2,1,0:T(8,128)(2,1)S(1)}, bf16[2,192,384]{2,1,0:T(8,128)(2,1)S(1)}, u32[]{:S(2)}, u32[]{:S(2)}) collective-permute-start(bf16[2,192,384]{2,1,0:T(8,128)(2,1)S(1)} %collective-permute-done.14.refs_7_), channel_id=1, source_target_pairs={{4,6},{5,7},{10,12},{11,13},{12,14},{13,15},{20,22},{21,23},{26,28... | collective-permute-start | bytes 884744 | tf_op jit(solution)/shard_map/ppermute | solution.py:40
  94.4 14.6 %collective-permute-start.17 = (bf16[2,192,384]{2,1,0:T(8,128)(2,1)S(1)}, bf16[2,192,384]{2,1,0:T(8,128)(2,1)S(1)}, u32[]{:S(2)}, u32[]{:S(2)}) collective-permute-start(bf16[2,192,384]{2,1,0:T(8,128)(2,1)S(1)} %collective-permute-done.15.refs_8_), channel_id=1, source_target_pairs={{12,14},{13,15},{28,30},{29,31}} | collective-permute-start | bytes 884744 | tf_op jit(solution)/shard_map/ppermute | solution.py:40
  95.7 17.6 %collective-permute-start.21 = (bf16[2,192,384]{2,1,0:T(8,128)(2,1)S(1)}, bf16[2,192,384]{2,1,0:T(8,128)(2,1)S(1)}, u32[]{:S(2)}, u32[]{:S(2)}) collective-permute-start(bf16[2,192,384]{2,1,0:T(8,128)(2,1)S(1)} %collective-permute-done.19.refs_12_), channel_id=1, source_target_pairs={{10,8},{11,9},{26,24},{27,25}} | collective-permute-start | bytes 884744 | tf_op jit(solution)/shard_map/ppermute | solution.py:40
  96.4 18.4 %collective-permute-start.25 = (bf16[2,192,384]{2,1,0:T(8,128)(2,1)S(1)}, bf16[2,192,384]{2,1,0:T(8,128)(2,1)S(1)}, u32[]{:S(2)}, u32[]{:S(2)}) collective-permute-start(bf16[2,192,384]{2,1,0:T(8,128)(2,1)S(1)} %get-tuple-element.93.refs_2_), channel_id=1, source_target_pairs={{0,8},{1,9},{2,10},{3,11},{4,12},{5,13},{6,14},{7,15},{8,0},{9,1},... | collective-permute-start | bytes 884744 | tf_op jit(solution)/shard_map/ppermute | solution.py:40
  96.5 17.6 %collective-permute-start.35 = (bf16[2,192,384]{2,1,0:T(8,128)(2,1)S(1)}, bf16[2,192,384]{2,1,0:T(8,128)(2,1)S(1)}, u32[]{:S(2)}, u32[]{:S(2)}) collective-permute-start(bf16[2,192,384]{2,1,0:T(8,128)(2,1)S(1)} %collective-permute-done.19.refs_12_), channel_id=1, source_target_pairs={{0,8},{1,9},{2,10},{3,11},{4,12},{5,13},{6,14},{7,15},{8,0},{9,1},... | collective-permute-start | bytes 884744 | tf_op jit(solution)/shard_map/ppermute | solution.py:40
  106.1 8.5 %collective-permute-start.29 = (bf16[2,192,384]{2,1,0:T(8,128)(2,1)S(1)}, bf16[2,192,384]{2,1,0:T(8,128)(2,1)S(1)}, u32[]{:S(2)}, u32[]{:S(2)}) collective-permute-start(bf16[2,192,384]{2,1,0:T(8,128)(2,1)S(1)} %collective-permute-done.13.refs_6_), channel_id=1, source_target_pairs={{0,8},{1,9},{2,10},{3,11},{4,12},{5,13},{6,14},{7,15},{8,0},{9,1},... | collective-permute-start | bytes 884744 | tf_op jit(solution)/shard_map/ppermute | solution.py:40
  109.0 6.3 %collective-permute-start.28 = (bf16[2,192,384]{2,1,0:T(8,128)(2,1)S(1)}, bf16[2,192,384]{2,1,0:T(8,128)(2,1)S(1)}, u32[]{:S(2)}, u32[]{:S(2)}) collective-permute-start(bf16[2,192,384]{2,1,0:T(8,128)(2,1)S(1)} %collective-permute-done.12.refs_5_), channel_id=1, source_target_pairs={{0,8},{1,9},{2,10},{3,11},{4,12},{5,13},{6,14},{7,15},{8,0},{9,1},... | collective-permute-start | bytes 884744 | tf_op jit(solution)/shard_map/ppermute | solution.py:40
  113.3 3.4 %collective-permute-start.22 = (bf16[2,192,384]{2,1,0:T(8,128)(2,1)S(1)}, bf16[2,192,384]{2,1,0:T(8,128)(2,1)S(1)}, u32[]{:S(2)}, u32[]{:S(2)}) collective-permute-start(bf16[2,192,384]{2,1,0:T(8,128)(2,1)S(1)} %collective-permute-done.20.refs_13_), channel_id=1, source_target_pairs={{10,8},{11,9},{26,24},{27,25}} | collective-permute-start | bytes 884744 | tf_op jit(solution)/shard_map/ppermute | solution.py:40
  114.2 2.7 %collective-permute-start.37 = (bf16[2,192,384]{2,1,0:T(8,128)(2,1)S(1)}, bf16[2,192,384]{2,1,0:T(8,128)(2,1)S(1)}, u32[]{:S(2)}, u32[]{:S(2)}) collective-permute-start(bf16[2,192,384]{2,1,0:T(8,128)(2,1)S(1)} %collective-permute-done.21.refs_14_), channel_id=1, source_target_pairs={{0,8},{1,9},{2,10},{3,11},{4,12},{5,13},{6,14},{7,15},{8,0},{9,1},... | collective-permute-start | bytes 884744 | tf_op jit(solution)/shard_map/ppermute | solution.py:40
  114.6 2.8 %collective-permute-start.36 = (bf16[2,192,384]{2,1,0:T(8,128)(2,1)S(1)}, bf16[2,192,384]{2,1,0:T(8,128)(2,1)S(1)}, u32[]{:S(2)}, u32[]{:S(2)}) collective-permute-start(bf16[2,192,384]{2,1,0:T(8,128)(2,1)S(1)} %collective-permute-done.20.refs_13_), channel_id=1, source_target_pairs={{0,8},{1,9},{2,10},{3,11},{4,12},{5,13},{6,14},{7,15},{8,0},{9,1},... | collective-permute-start | bytes 884744 | tf_op jit(solution)/shard_map/ppermute | solution.py:40
  114.8 2.7 %collective-permute-start.30 = (bf16[2,192,384]{2,1,0:T(8,128)(2,1)S(1)}, bf16[2,192,384]{2,1,0:T(8,128)(2,1)S(1)}, u32[]{:S(2)}, u32[]{:S(2)}) collective-permute-start(bf16[2,192,384]{2,1,0:T(8,128)(2,1)S(1)} %collective-permute-done.14.refs_7_), channel_id=1, source_target_pairs={{0,8},{1,9},{2,10},{3,11},{4,12},{5,13},{6,14},{7,15},{8,0},{9,1},... | collective-permute-start | bytes 884744 | tf_op jit(solution)/shard_map/ppermute | solution.py:40
  115.3 7.5 %collective-permute-start.18 = (bf16[2,192,384]{2,1,0:T(8,128)(2,1)S(1)}, bf16[2,192,384]{2,1,0:T(8,128)(2,1)S(1)}, u32[]{:S(2)}, u32[]{:S(2)}) collective-permute-start(bf16[2,192,384]{2,1,0:T(8,128)(2,1)S(1)} %collective-permute-done.16.refs_9_), channel_id=1, source_target_pairs={{12,14},{13,15},{28,30},{29,31}} | collective-permute-start | bytes 884744 | tf_op jit(solution)/shard_map/ppermute | solution.py:40
  116.8 6.0 %collective-permute-start.31 = (bf16[2,192,384]{2,1,0:T(8,128)(2,1)S(1)}, bf16[2,192,384]{2,1,0:T(8,128)(2,1)S(1)}, u32[]{:S(2)}, u32[]{:S(2)}) collective-permute-start(bf16[2,192,384]{2,1,0:T(8,128)(2,1)S(1)} %collective-permute-done.15.refs_8_), channel_id=1, source_target_pairs={{0,8},{1,9},{2,10},{3,11},{4,12},{5,13},{6,14},{7,15},{8,0},{9,1},... | collective-permute-start | bytes 884744 | tf_op jit(solution)/shard_map/ppermute | solution.py:40
  116.9 5.9 %collective-permute-start.32 = (bf16[2,192,384]{2,1,0:T(8,128)(2,1)S(1)}, bf16[2,192,384]{2,1,0:T(8,128)(2,1)S(1)}, u32[]{:S(2)}, u32[]{:S(2)}) collective-permute-start(bf16[2,192,384]{2,1,0:T(8,128)(2,1)S(1)} %collective-permute-done.16.refs_9_), channel_id=1, source_target_pairs={{0,8},{1,9},{2,10},{3,11},{4,12},{5,13},{6,14},{7,15},{8,0},{9,1},... | collective-permute-start | bytes 884744 | tf_op jit(solution)/shard_map/ppermute | solution.py:40
  117.4 5.3 %collective-permute-start.38 = (bf16[2,192,384]{2,1,0:T(8,128)(2,1)S(1)}, bf16[2,192,384]{2,1,0:T(8,128)(2,1)S(1)}, u32[]{:S(2)}, u32[]{:S(2)}) collective-permute-start(bf16[2,192,384]{2,1,0:T(8,128)(2,1)S(1)} %collective-permute-done.22.refs_15_), channel_id=1, source_target_pairs={{0,8},{1,9},{2,10},{3,11},{4,12},{5,13},{6,14},{7,15},{8,0},{9,1},... | collective-permute-start | bytes 884744 | tf_op jit(solution)/shard_map/ppermute | solution.py:40
  117.5 5.3 %collective-permute-start.33 = (bf16[2,192,384]{2,1,0:T(8,128)(2,1)S(1)}, bf16[2,192,384]{2,1,0:T(8,128)(2,1)S(1)}, u32[]{:S(2)}, u32[]{:S(2)}) collective-permute-start(bf16[2,192,384]{2,1,0:T(8,128)(2,1)S(1)} %collective-permute-done.17.refs_10_), channel_id=1, source_target_pairs={{0,8},{1,9},{2,10},{3,11},{4,12},{5,13},{6,14},{7,15},{8,0},{9,1},... | collective-permute-start | bytes 884744 | tf_op jit(solution)/shard_map/ppermute | solution.py:40
  122.7 1.6 %collective-permute-start.34 = (bf16[2,192,384]{2,1,0:T(8,128)(2,1)S(1)}, bf16[2,192,384]{2,1,0:T(8,128)(2,1)S(1)}, u32[]{:S(2)}, u32[]{:S(2)}) collective-permute-start(bf16[2,192,384]{2,1,0:T(8,128)(2,1)S(1)} %collective-permute-done.18.refs_11_), channel_id=1, source_target_pairs={{0,8},{1,9},{2,10},{3,11},{4,12},{5,13},{6,14},{7,15},{8,0},{9,1},... | collective-permute-start | bytes 884744 | tf_op jit(solution)/shard_map/ppermute | solution.py:40
  133.4 8.5 %collective-permute-start.39 = (bf16[2,192,384]{2,1,0:T(8,128)(2,1)S(1)}, bf16[2,192,384]{2,1,0:T(8,128)(2,1)S(1)}, u32[]{:S(2)}, u32[]{:S(2)}) collective-permute-start(bf16[2,192,384]{2,1,0:T(8,128)(2,1)S(1)} %copy-done.44), channel_id=1, source_target_pairs={{0,1},{1,0},{2,3},{3,2},{4,5},{5,4},{6,7},{7,6},{8,9},{9,8},{10,11... | collective-permute-start | bytes 884744 | tf_op jit(solution)/shard_map/ppermute | solution.py:40
  133.6 11.9 %collective-permute-start.40 = (bf16[384,384]{1,0:T(8,128)(2,1)}, bf16[384,384]{1,0:T(8,128)(2,1)S(1)}, u32[]{:S(2)}, u32[]{:S(2)}) collective-permute-start(bf16[384,384]{1,0:T(8,128)(2,1)} %get-tuple-element.82), channel_id=1, source_target_pairs={{0,8},{1,9},{2,10},{3,11},{4,12},{5,13},{6,14},{7,15},{8,0},{9,1},... | collective-permute-start | bytes 884744 | tf_op jit(solution)/shard_map/ppermute | solution.py:40
  134.1 11.5 %collective-permute-start.41 = (bf16[384,384]{1,0:T(8,128)(2,1)}, bf16[384,384]{1,0:T(8,128)(2,1)S(1)}, u32[]{:S(2)}, u32[]{:S(2)}) collective-permute-start(bf16[384,384]{1,0:T(8,128)(2,1)} %get-tuple-element.83), channel_id=1, source_target_pairs={{0,16},{1,17},{2,18},{3,19},{4,20},{5,21},{6,22},{7,23},{8,24},{9,... | collective-permute-start | bytes 884744 | tf_op jit(solution)/shard_map/ppermute | solution.py:40
  135.7 13.8 %collective-permute-start.42 = (bf16[384,384]{1,0:T(8,128)(2,1)}, bf16[384,384]{1,0:T(8,128)(2,1)S(1)}, u32[]{:S(2)}, u32[]{:S(2)}) collective-permute-start(bf16[384,384]{1,0:T(8,128)(2,1)} %get-tuple-element.84), channel_id=1, source_target_pairs={{0,24},{1,25},{2,26},{3,27},{4,28},{5,29},{6,30},{7,31},{8,16},{9,... | collective-permute-start | bytes 884744 | tf_op jit(solution)/shard_map/ppermute | solution.py:40
  (40 other events, 527.9 us)

commit v8 on v7

--- a/solution.py
+++ b/solution.py
@@ -39,19 +39,47 @@
                 pairs.append((index(*place), index(*goal)))
         return lax.ppermute(value, AXES, pairs)
 
-    def ring(self, step):
-        own = {
-            col: [key for key in reversed(self.keys) if key[1] == col] for col in range(self.cols)
-        }
-        sends = {}
-        order = range(self.cols) if step > 0 else reversed(range(self.cols))
-        queue = []
-        for col in order:
-            queue = [(key, None) for key in own[col]] + [(key, n) for n, (key, _) in enumerate(queue)]
-            if 0 <= col + step < self.cols:
-                for n, item in enumerate(queue):
-                    sends[col, n] = item
+    def ring(self):
+        top, last = self.moments - 1, self.cols - 1
+        sends, queue = {}, []
+        for col in range(last):
+            queue = [((top, col), None)] + [(key, n) for n, (key, _) in enumerate(queue)]
+            for n, (key, step) in enumerate(queue):
+                sends[n, col] = (key, col + 1, step)
+        wanted = [
+            (key, to)
+            for key in self.keys
+            if key[0] < top
+            for to in range(self.cols)
+            if to not in (key[1], last)
+        ]
+        for key, to in wanted:
+            for n in range(1, last):
+                if (n, key[1]) in sends or (n, to - 1) in sends and sends[n, to - 1][1] == to:
+                    continue
+                if to not in [goal for (m, _), (_, goal, _) in sends.items() if m == n]:
+                    sends[n, key[1]] = (key, to, None)
+                    break
         return sends
+
+    def rest(self):
+        done = {(key, to) for key, to, _ in self.ring().values()}
+        wanted = [
+            (key, to)
+            for key in self.keys
+            for to in range(self.cols)
+            if to != key[1] and (key, to) not in done
+        ]
+        steps = []
+        for key, to in sorted(wanted, key=lambda item: (item[0][0], -item[1], -item[0][1])):
+            for step in steps:
+                if key[1] not in step and to not in [goal for _, goal in step.values()]:
+                    break
+            else:
+                step = {}
+                steps.append(step)
+            step[key[1]] = (key, to)
+        return steps
 
 
 def hbm(count):
@@ -175,7 +203,8 @@
                 for t in range(groups):
                     row = key[0] * groups + (g ^ t)
                     for q in range(moms):
-                        ref = sig_in[sources[key, col, q, t]]
+                        index, part = sources[key, col, q, t]
+                        ref = sig_in[index] if part is None else sig_in[index].at[part]
                         at = pl.ds(pl.multiple_of((y ^ q) * half, half), half)
                         for p in range(2):
                             lane = pl.ds((2 * key[1] + p) * side, side)
@@ -322,45 +351,56 @@
         return key[0] * groups + a % groups > key[1]
 
     found = {}
-    own = []
-    for q in range(moms):
-        own.append(by_block(came[q]))
-        for key in plan.keys:
-            found[key, key[1], q] = own[q][key[0]]
-
-    def shift(q, direction, number, got, *behind):
-        sends = {col: item for (col, n), item in plan.ring(direction).items() if n == number}
+    own = [by_block(came[q]) for q in range(moms)]
+    both = [jnp.stack([own[q][b] for q in range(moms)]) for b in range(moments)]
+    for key in plan.keys:
+        for q in range(moms):
+            found[key, key[1], q] = (both[key[0]], q)
+
+    def choose(values):
         chosen = used = None
-        for col, (key, step) in sends.items():
-            value = own[q][key[0]] if step is None else got[step]
+        for col, value in values.items():
             if chosen is None:
                 chosen = used = value
             elif value is not used:
                 chosen = jnp.where(z == col, value, chosen)
-        goal = lambda a, c, m: (
-            (a, c + direction, m) if c in sends and valid(sends[c][0], a) else None
-        )
-        value = plan.send(after(chosen, behind), goal)
-        got.append(value)
-        for col, (key, _) in sends.items():
-            found[key, col + direction, q] = value
-
-    right_got, left_got = [[] for _ in range(moms)], [[] for _ in range(moms)]
-    right_steps = max(n for _, n in plan.ring(1)) + 1
-    left_steps = max(n for _, n in plan.ring(-1)) + 1
-    for number in range(right_steps):
+        return chosen
+
+    def shift(values, goals):
+        goal = lambda a, c, m: (a, goals[c][1], m) if c in goals and valid(goals[c][0], a) else None
+        return plan.send(choose(values), goal)
+
+    ring, rest = plan.ring(), plan.rest()
+    got = [[] for _ in range(moms)]
+
+    def ring_step(q, number, *behind):
+        sends = {col: item for (n, col), item in ring.items() if n == number}
+        values = {
+            col: own[q][key[0]] if step is None else got[q][step]
+            for col, (key, _, step) in sends.items()
+        }
+        value = shift(after(values, behind), {col: item[:2] for col, item in sends.items()})
+        got[q].append(value)
+        for key, to, _ in sends.values():
+            found[key, to, q] = (value, None)
+
+    def rest_step(number, *behind):
+        step = rest[number]
+        value = shift(after({col: both[key[0]] for col, (key, _) in step.items()}, behind), step)
+        for key, to in step.values():
+            for q in range(moms):
+                found[key, to, q] = (value, q)
+
+    for number in range(cols - 1):
         for q in range(moms):
-            behind = []
-            if q > 0:
-                behind.append(right_got[q - 1][number])
+            behind = [got[p][number] for p in range(q)]
             if number == 1 and q + 1 < moms:
-                behind.append(came[q + 1])
-            if number + 1 == right_steps and q + 1 == moms:
-                behind += [right_came, diag_came]
-            shift(q, 1, number, right_got[q], *behind)
-    for number in range(left_steps):
-        for q in range(moms):
-            shift(q, -1, number, left_got[q], right_got[q][min(number, right_steps - 1)])
+                behind += [came[q + 1], diag_came]
+            if number == cols - 2 and q + 1 == moms:
+                behind.append(right_came)
+            ring_step(q, number, *behind)
+    for number in range(len(rest)):
+        rest_step(number, got[0][1], got[-1][0])
 
     buffers = []
 
@@ -371,11 +411,11 @@
         buffers.append(value)
         return len(buffers) - 1
 
-    sources = {name + (0,): number_of(value) for name, value in found.items()}
+    sources = {name + (0,): (number_of(value), part) for name, (value, part) in found.items()}
     sig_all = list(buffers)
     for t in range(1, groups):
-        for name, value in found.items():
-            sources[name + (t,)] = len(sig_all) + number_of(value)
+        for name, (value, part) in found.items():
+            sources[name + (t,)] = (len(sig_all) + number_of(value), part)
         sig_all += [exchange_row(value, t) for value in buffers]
 
     solved = pl.pallas_call(

time: 155 us -> 145 us (0.935)
  waiting for transfers between devices: 69.3 us -> 57.1 us
    ppermute x43 -> x33, waiting for transfers between devices: 69.3 us -> 57.1 us  [send(): return lax.ppermute(value, AXES, pairs)]
    dynamic_slice x5, local copies, waits for them, and re-layouts: 3.03 us -> 1 us  [on_device(): lax.dynamic_index_in_dim(right, r ^ s, 0, keepdims=False)]
    ppermute x43 -> x33, starting transfers between devices: 42.4 us -> 43.8 us  [send(): return lax.ppermute(value, AXES, pairs)]
    unnamed x91 -> x59, local copies, waits for them, and re-layouts: 4.44 us -> 5.32 us
  transfers between devices with their start and end apart: 43 -> 33, of which waited for: 13 -> 12; matrix products, arithmetic and copies ran while one was open for 8% -> 8% of each run, Pallas kernels for 2% -> 2%
where the time goes in v8:
time: 145 us; the launch traced here: 143 us
  waiting for transfers between devices  57.1 us (39%)
  starting transfers between devices  43.8 us (30%)
  Pallas kernels  17.6 us (12%)
  local copies, waits for them, and re-layouts  14.6 us (10%)
  other arithmetic  8.58 us (6%)
    ppermute x33, waiting for transfers between devices, send(): return lax.ppermute(value, AXES, pairs)  57.1 us
    ppermute x33, starting transfers between devices, send(): return lax.ppermute(value, AXES, pairs)  43.8 us
    pallas_call x1, Pallas kernels, on_device(): pl.pallas_call(functools.partial(solve_kernel, plan, sources), out_shape=...  8.36 us
    pallas_call x1, Pallas kernels, on_device(): pl.pallas_call(functools.partial(sigma_kernel, plan, pair_count, chunks),...  6.25 us
    unnamed x59, local copies, waits for them, and re-layouts  5.32 us
    another operation x1, other arithmetic, on_device(): diag_came = jnp.stack(diag_all)  2.95 us
    pallas_call x1, Pallas kernels, on_device(): pl.pallas_call(functools.partial(place_kernel, plan), out_shape=jax.Shape...  2.95 us
    dynamic_slice x2, local copies, waits for them, and re-layouts, half_of(): return lax.dynamic_slice_in_dim(value, (y ^ q) * half, half, 2)  2.94 us
  transfers between devices with their start and end apart: 33, of which 12 were waited for; matrix products, arithmetic and copies ran while one was open for 8% of the time, Pallas kernels for 2%

profile of v8, /device:TPU:25, one launch (start us, length us, event | category | flops | bytes accessed | tf_op | source)
XLA Modules:
  0.0 143.0 jit_solution(4999579452527840084)
XLA Ops:
  0.7 2.0 %constant_dynamic-slice_fusion.4 = bf16[2,2,192,384]{3,2,1,0:T(8,128)(2,1)} fusion(bf16[2,2,384,384]{3,2,1,0:T(8,128)(2,1)} %refs_0_, s32[]{:T(128)S(6)} %select_n.245), kind=kLoop, calls=%fused_computation.42 | loop fusion | bytes 1179652 | tf_op jit(solution)/shard_map/dynamic_slice | solution.py:280
  2.7 0.8 copy.11
  3.5 0.9 dynamic-slice_bitcast_fusion.1
  4.4 0.9 dynamic-slice_bitcast_fusion
  5.3 1.2 collective-permute-start.2
  6.5 1.2 collective-permute-start.1
  8.0 2.0 %copy.13 = bf16[2,384,2,384]{1,3,2,0:T(8,128)(2,1)S(1)} copy(bf16[2,384,2,384]{3,2,1,0:T(2,128)(2,1)S(1)} %copy-done.9) | data formatting | bytes 2359296 | tf_op jit(solution)/shard_map/optimization_barrier | solution.py:256
  10.1 9.7 %collective-permute-done.2 = bf16[2,384,384]{2,1,0:T(8,128)(2,1)} collective-permute-done((bf16[2,384,384]{2,1,0:T(8,128)(2,1)}, bf16[2,384,384]{2,1,0:T(8,128)(2,1)}, u32[]{:S(2)}, u32[]{:S(2)}) %collective-permute-start.2) | collective-permute-done | bytes 589856 | tf_op jit(solution)/shard_map/ppermute | solution.py:40
  19.8 1.2 bitcast_select_fusion
  21.2 1.6 %collective-permute-start.4 = (bf16[384,768]{1,0:T(8,128)(2,1)S(1)}, bf16[384,768]{1,0:T(8,128)(2,1)}, u32[]{:S(2)}, u32[]{:S(2)}) collective-permute-start(bf16[384,768]{1,0:T(8,128)(2,1)S(1)} %pad_maximum_fusion.4), channel_id=1, source_target_pairs={{0,8},{1,9},{2,10},{3,11},{4,12},{5,13},{6,14},{7,15},{8,0},{9,1},... | collective-permute-start | bytes 1769480 | tf_op jit(solution)/shard_map/ppermute | solution.py:40
  25.8 7.6 %collective-permute-done.refs_1_ = bf16[2,2,192,384]{3,2,1,0:T(8,128)(2,1)} collective-permute-done((bf16[2,2,192,384]{3,2,1,0:T(8,128)(2,1)}, bf16[2,2,192,384]{3,2,1,0:T(8,128)(2,1)}, u32[]{:S(2)}, u32[]{:S(2)}) %collective-permute-start) | collective-permute-done | bytes 589856 | tf_op jit(solution)/shard_map/ppermute | solution.py:40
  33.4 6.2 %self_energy.1 = (bf16[2,192,384]{2,1,0:T(8,128)(2,1)}, bf16[2,192,384]{2,1,0:T(8,128)(2,1)}, bf16[2,192,384]{2,1,0:T(8,128)(2,1)}, bf16[2,192,384]{2,1,0:T(8,128)(2,1)}) custom-call(s32[3]{0:T(128)} %pad_add_fusion.place, s32[4,8]{1,0:T(4,128)} %fusion.1.quads, s32[4,8]{1,0:T(4,128)} %slice_bitcast_fusion.4.thirds, bf16[2,2,384,384]{3,2,1,0:T(8,128)(2,1)} %refs_0_, ...), custom_call_target="tpu_custom_call" | custom-call | tf_op jit(solution)/shard_map/self_energy/pallas_call | solution.py:310
  39.6 0.8 collective-permute-start.6
  40.5 1.3 collective-permute-start.5
  41.8 1.0 broadcast_select_fusion.3
  42.8 1.3 collective-permute-start.11
  44.1 0.7 collective-permute-start.7
  44.8 3.0 %pad_maximum_fusion.diag = bf16[4,384,768]{2,1,0:T(8,128)(2,1)} fusion(bf16[1,384,768]{2,1,0:T(8,128)(2,1)} %bitcast.24, bf16[1,384,768]{2,1,0:T(8,128)(2,1)S(1)} %bitcast.68, bf16[1,384,768]{2,1,0:T(8,128)(2,1)} %bitcast.22, bf16[1,384,768]{2,1,0:T(8,128)(2,1)S(1)} %bitcast.69), kind=kLoop, calls=%fused_computation | loop fusion | flops 3538944 | bytes 4718592 | tf_op jit(solution)/shard_map/stack | solution.py:304
  47.8 7.2 %collective-permute-done.11.refs_2_ = bf16[2,192,384]{2,1,0:T(8,128)(2,1)S(1)} collective-permute-done((bf16[2,192,384]{2,1,0:T(8,128)(2,1)S(1)}, bf16[2,192,384]{2,1,0:T(8,128)(2,1)S(1)}, u32[]{:S(2)}, u32[]{:S(2)}) %collective-permute-start.11) | collective-permute-done | bytes 294944 | tf_op jit(solution)/shard_map/ppermute | solution.py:40
  55.0 1.3 collective-permute-start.13
  56.5 1.3 collective-permute-start.12
  57.9 2.0 %collective-permute-start.10 = (bf16[384,384]{1,0:T(8,128)(2,1)S(1)}, bf16[384,384]{1,0:T(8,128)(2,1)S(1)}, u32[]{:S(2)}, u32[]{:S(2)}) collective-permute-start(bf16[384,384]{1,0:T(8,128)(2,1)S(1)} %bitcast.73), channel_id=1, source_target_pairs={{0,24},{1,25},{2,26},{3,27},{4,28},{5,29},{6,30},{7,31},{8,16},{9,... | collective-permute-start | bytes 884744 | tf_op jit(solution)/shard_map/ppermute | solution.py:40
  60.1 7.4 %collective-permute-done.13.refs_4_ = bf16[2,192,384]{2,1,0:T(8,128)(2,1)S(1)} collective-permute-done((bf16[2,192,384]{2,1,0:T(8,128)(2,1)S(1)}, bf16[2,192,384]{2,1,0:T(8,128)(2,1)S(1)}, u32[]{:S(2)}, u32[]{:S(2)}) %collective-permute-start.13) | collective-permute-done | bytes 294944 | tf_op jit(solution)/shard_map/ppermute | solution.py:40
  67.6 2.8 %collective-permute-start.21 = (bf16[2,192,384]{2,1,0:T(8,128)(2,1)S(1)}, bf16[2,192,384]{2,1,0:T(8,128)(2,1)S(1)}, u32[]{:S(2)}, u32[]{:S(2)}) collective-permute-start(bf16[2,192,384]{2,1,0:T(8,128)(2,1)S(1)} %collective-permute-done.11.refs_2_), channel_id=1, source_target_pairs={{0,8},{1,9},{2,10},{3,11},{4,12},{5,13},{6,14},{7,15},{8,0},{9,1},... | collective-permute-start | bytes 884744 | tf_op jit(solution)/shard_map/ppermute | solution.py:40
  70.5 1.5 %collective-permute-done.12.refs_3_ = bf16[2,192,384]{2,1,0:T(8,128)(2,1)S(1)} collective-permute-done((bf16[2,192,384]{2,1,0:T(8,128)(2,1)S(1)}, bf16[2,192,384]{2,1,0:T(8,128)(2,1)S(1)}, u32[]{:S(2)}, u32[]{:S(2)}) %collective-permute-start.12) | collective-permute-done | bytes 294944 | tf_op jit(solution)/shard_map/ppermute | solution.py:40
  72.0 1.3 collective-permute-start.15
  73.3 1.3 collective-permute-start.14
  74.8 0.7 collective-permute-start.18
  75.5 1.3 collective-permute-start.17
  76.8 4.2 %collective-permute-done.15.refs_6_ = bf16[2,192,384]{2,1,0:T(8,128)(2,1)S(1)} collective-permute-done((bf16[2,192,384]{2,1,0:T(8,128)(2,1)S(1)}, bf16[2,192,384]{2,1,0:T(8,128)(2,1)S(1)}, u32[]{:S(2)}, u32[]{:S(2)}) %collective-permute-start.15) | collective-permute-done | bytes 294944 | tf_op jit(solution)/shard_map/ppermute | solution.py:40
  81.0 6.1 %collective-permute-start.20 = (bf16[2,2,192,384]{3,2,1,0:T(8,128)(2,1)S(1)}, bf16[2,2,192,384]{3,2,1,0:T(8,128)(2,1)S(1)}, u32[]{:S(2)}, u32[]{:S(2)}) collective-permute-start(bf16[2,2,192,384]{3,2,1,0:T(8,128)(2,1)S(1)} %pad_maximum_fusion.6.refs_1_), channel_id=1, source_target_pairs={{0,8},{1,9},{2,10},{3,11},{4,12},{5,13},{6,14},{7,15},{8,0},{9,1},... | collective-permute-start | bytes 1769480 | tf_op jit(solution)/shard_map/ppermute | solution.py:40
  87.4 9.5 %collective-permute-start.19 = (bf16[2,2,192,384]{3,2,1,0:T(8,128)(2,1)S(1)}, bf16[2,2,192,384]{3,2,1,0:T(8,128)(2,1)S(1)}, u32[]{:S(2)}, u32[]{:S(2)}) collective-permute-start(bf16[2,2,192,384]{3,2,1,0:T(8,128)(2,1)S(1)} %pad_maximum_fusion.5.refs_0_), channel_id=1, source_target_pairs={{0,8},{1,9},{2,10},{3,11},{4,12},{5,13},{6,14},{7,15},{8,0},{9,1},... | collective-permute-start | bytes 1769480 | tf_op jit(solution)/shard_map/ppermute | solution.py:40
  97.0 1.2 pad_maximum_fusion.1.right
  98.3 0.7 collective-permute-done.22.refs_13_
  99.0 1.5 %collective-permute-start.16 = (bf16[2,192,384]{2,1,0:T(8,128)(2,1)S(1)}, bf16[2,192,384]{2,1,0:T(8,128)(2,1)S(1)}, u32[]{:S(2)}, u32[]{:S(2)}) collective-permute-start(bf16[2,192,384]{2,1,0:T(8,128)(2,1)S(1)} %broadcast_select_fusion), channel_id=1, source_target_pairs={{4,6},{5,7},{8,12},{9,13},{12,14},{13,15},{20,22},{21,23},{24,28},... | collective-permute-start | bytes 884744 | tf_op jit(solution)/shard_map/ppermute | solution.py:40
  101.7 7.4 %collective-permute-done.16.refs_7_ = bf16[2,192,384]{2,1,0:T(8,128)(2,1)S(1)} collective-permute-done((bf16[2,192,384]{2,1,0:T(8,128)(2,1)S(1)}, bf16[2,192,384]{2,1,0:T(8,128)(2,1)S(1)}, u32[]{:S(2)}, u32[]{:S(2)}) %collective-permute-start.16) | collective-permute-done | bytes 294944 | tf_op jit(solution)/shard_map/ppermute | solution.py:40
  109.1 1.2 collective-permute-start.26
  110.3 1.2 collective-permute-done.26.refs_17_
  112.4 0.8 copy-done.16
  113.2 8.4 %substitution.1 = (bf16[384,384]{1,0:T(8,128)(2,1)}, bf16[384,384]{1,0:T(8,128)(2,1)}, bf16[384,384]{1,0:T(8,128)(2,1)}, bf16[384,384]{1,0:T(8,128)(2,1)}) custom-call(s32[3]{0:T(128)} %pad_add_fusion.place, bf16[4,384,768]{2,1,0:T(8,128)(2,1)} %pad_maximum_fusion.diag, bf16[4,384,384]{2,1,0:T(8,128)(2,1)} %pad_maximum_fusion.1.right, ...), custom_call_target="tpu_custom_call" | custom-call | tf_op jit(solution)/shard_map/substitution/pallas_call | solution.py:421
  121.6 1.3 collective-permute-start.29
  123.5 1.6 %collective-permute-start.32 = (bf16[384,384]{1,0:T(8,128)(2,1)}, bf16[384,384]{1,0:T(8,128)(2,1)S(1)}, u32[]{:S(2)}, u32[]{:S(2)}) collective-permute-start(bf16[384,384]{1,0:T(8,128)(2,1)} %get-tuple-element.106), channel_id=1, source_target_pairs={{0,24},{1,25},{2,26},{3,27},{4,28},{5,29},{6,30},{7,31},{8,16},{9,... | collective-permute-start | bytes 884744 | tf_op jit(solution)/shard_map/ppermute | solution.py:40
  125.2 4.7 %collective-permute-done.29.refs_3_ = bf16[2,192,384]{2,1,0:T(8,128)(2,1)S(1)} collective-permute-done((bf16[2,192,384]{2,1,0:T(8,128)(2,1)S(1)}, bf16[2,192,384]{2,1,0:T(8,128)(2,1)S(1)}, u32[]{:S(2)}, u32[]{:S(2)}) %collective-permute-start.29) | collective-permute-done | bytes 294944 | tf_op jit(solution)/shard_map/ppermute | solution.py:40
  129.9 0.7 copy-done.25
  130.6 2.9 %place_sigma.1 = bf16[2,2,384,384]{3,2,1,0:T(8,128)(2,1)} custom-call(s32[3]{0:T(128)} %pad_add_fusion.place, bf16[2,192,384]{2,1,0:T(8,128)(2,1)} %get-tuple-element.66.refs_0_, bf16[2,192,384]{2,1,0:T(8,128)(2,1)} %get-tuple-element.67.refs_1_, bf16[2,192,384]{2,1,0:T(8,128)(2,1)} %copy-done.5, bf16[2,192,384]{2,1,0:T(8,128)(2,1)} %copy-done.25), custom_call_target="tpu_custom_call" | custom-call | tf_op jit(solution)/shard_map/place_sigma/pallas_call | solution.py:441
  133.6 5.2 %collective-permute-done.32 = bf16[384,384]{1,0:T(8,128)(2,1)S(1)} collective-permute-done((bf16[384,384]{1,0:T(8,128)(2,1)}, bf16[384,384]{1,0:T(8,128)(2,1)S(1)}, u32[]{:S(2)}, u32[]{:S(2)}) %collective-permute-start.32) | collective-permute-done | bytes 294944 | tf_op jit(solution)/shard_map/ppermute | solution.py:40
  139.2 0.8 copy.19
  140.1 2.8 %copy.21 = bf16[2,384,2,384]{3,2,1,0:T(2,128)(2,1)} copy(bf16[2,384,2,384]{1,3,2,0:T(8,128)(2,1)S(1)} %bitcast.61) | data formatting | bytes 2359296
  (115 shorter events, 7.9 us)
Async XLA Ops:
  5.3 14.5 %collective-permute-start.2 = (bf16[2,384,384]{2,1,0:T(8,128)(2,1)}, bf16[2,384,384]{2,1,0:T(8,128)(2,1)}, u32[]{:S(2)}, u32[]{:S(2)}) collective-permute-start(bf16[2,384,384]{2,1,0:T(8,128)(2,1)} %dynamic-slice_bitcast_fusion), channel_id=1, source_target_pairs={{0,16},{1,17},{2,18},{3,19},{4,20},{5,21},{6,22},{7,23},{8,24},{9,... | collective-permute-start | bytes 1769480 | tf_op jit(solution)/shard_map/ppermute | solution.py:40
  6.5 19.2 %collective-permute-start.1 = (bf16[2,2,192,384]{3,2,1,0:T(8,128)(2,1)}, bf16[2,2,192,384]{3,2,1,0:T(8,128)(2,1)}, u32[]{:S(2)}, u32[]{:S(2)}) collective-permute-start(bf16[2,2,192,384]{3,2,1,0:T(8,128)(2,1)} %dynamic-slice_bitcast_fusion.1), channel_id=1, source_target_pairs={{0,1},{1,0},{2,3},{3,2},{4,5},{5,4},{6,7},{7,6},{8,9},{9,8},{10,11... | collective-permute-start | bytes 1769480 | tf_op jit(solution)/shard_map/ppermute | solution.py:40
  7.8 25.6 %collective-permute-start = (bf16[2,2,192,384]{3,2,1,0:T(8,128)(2,1)}, bf16[2,2,192,384]{3,2,1,0:T(8,128)(2,1)}, u32[]{:S(2)}, u32[]{:S(2)}) collective-permute-start(bf16[2,2,192,384]{3,2,1,0:T(8,128)(2,1)} %constant_dynamic-slice_fusion.4), channel_id=1, source_target_pairs={{0,1},{1,0},{2,3},{3,2},{4,5},{5,4},{6,7},{7,6},{8,9},{9,8},{10,11... | collective-permute-start | bytes 1769480 | tf_op jit(solution)/shard_map/ppermute | solution.py:40
  21.2 12.2 %collective-permute-start.4 = (bf16[384,768]{1,0:T(8,128)(2,1)S(1)}, bf16[384,768]{1,0:T(8,128)(2,1)}, u32[]{:S(2)}, u32[]{:S(2)}) collective-permute-start(bf16[384,768]{1,0:T(8,128)(2,1)S(1)} %pad_maximum_fusion.4), channel_id=1, source_target_pairs={{0,8},{1,9},{2,10},{3,11},{4,12},{5,13},{6,14},{7,15},{8,0},{9,1},... | collective-permute-start | bytes 1769480 | tf_op jit(solution)/shard_map/ppermute | solution.py:40
  22.9 10.5 %collective-permute-start.3 = (bf16[384,768]{1,0:T(8,128)(2,1)S(1)}, bf16[384,768]{1,0:T(8,128)(2,1)}, u32[]{:S(2)}, u32[]{:S(2)}) collective-permute-start(bf16[384,768]{1,0:T(8,128)(2,1)S(1)} %pad_maximum_fusion.3), channel_id=1, source_target_pairs={{0,8},{1,9},{2,10},{3,11},{4,12},{5,13},{6,14},{7,15},{8,0},{9,1},... | collective-permute-start | bytes 1769480 | tf_op jit(solution)/shard_map/ppermute | solution.py:40
  39.6 2.1 %collective-permute-start.6 = (bf16[2,192,384]{2,1,0:T(8,128)(2,1)}, bf16[2,192,384]{2,1,0:T(8,128)(2,1)S(1)}, u32[]{:S(2)}, u32[]{:S(2)}) collective-permute-start(bf16[2,192,384]{2,1,0:T(8,128)(2,1)} %get-tuple-element.67.refs_1_), channel_id=1, source_target_pairs={{8,24},{9,25},{16,0},{17,1},{18,2},{19,3},{24,8},{25,9},{26,10},{2... | collective-permute-start | bytes 884744 | tf_op jit(solution)/shard_map/ppermute | solution.py:40
  40.5 7.3 %collective-permute-start.5 = (bf16[2,192,384]{2,1,0:T(8,128)(2,1)}, bf16[2,192,384]{2,1,0:T(8,128)(2,1)S(1)}, u32[]{:S(2)}, u32[]{:S(2)}) collective-permute-start(bf16[2,192,384]{2,1,0:T(8,128)(2,1)} %get-tuple-element.68), channel_id=1, source_target_pairs={{0,1},{1,0},{2,3},{3,2},{4,5},{5,4},{6,7},{7,6},{8,9},{9,8},{10,11... | collective-permute-start | bytes 884744 | tf_op jit(solution)/shard_map/ppermute | solution.py:40
  42.8 12.2 %collective-permute-start.11 = (bf16[2,192,384]{2,1,0:T(8,128)(2,1)S(1)}, bf16[2,192,384]{2,1,0:T(8,128)(2,1)S(1)}, u32[]{:S(2)}, u32[]{:S(2)}) collective-permute-start(bf16[2,192,384]{2,1,0:T(8,128)(2,1)S(1)} %select_select_fusion.4), channel_id=1, source_target_pairs={{0,2},{1,3},{2,4},{3,5},{8,10},{9,11},{10,12},{11,13},{12,14},{13,... | collective-permute-start | bytes 884744 | tf_op jit(solution)/shard_map/ppermute | solution.py:40
  44.1 10.8 %collective-permute-start.7 = (bf16[2,192,384]{2,1,0:T(8,128)(2,1)S(1)}, bf16[2,192,384]{2,1,0:T(8,128)(2,1)S(1)}, u32[]{:S(2)}, u32[]{:S(2)}) collective-permute-start(bf16[2,192,384]{2,1,0:T(8,128)(2,1)S(1)} %copy-done.28), channel_id=1, source_target_pairs={{8,25},{9,24},{16,1},{17,0},{18,3},{19,2},{24,9},{25,8},{26,11},{2... | collective-permute-start | bytes 884744 | tf_op jit(solution)/shard_map/ppermute | solution.py:40
  47.8 8.7 %copy-start.5 = (bf16[2,192,384]{2,1,0:T(8,128)(2,1)}, bf16[2,192,384]{2,1,0:T(8,128)(2,1)S(1)}, u32[]{:S(2)}) copy-start(bf16[2,192,384]{2,1,0:T(8,128)(2,1)S(1)} %collective-permute-done.5.refs_2_) | copy-start | bytes 884740
  55.0 12.6 %copy-start.6 = (bf16[2,192,384]{2,1,0:T(8,128)(2,1)}, bf16[2,192,384]{2,1,0:T(8,128)(2,1)S(1)}, u32[]{:S(2)}) copy-start(bf16[2,192,384]{2,1,0:T(8,128)(2,1)S(1)} %collective-permute-done.11.refs_2_) | copy-start | bytes 884740
  55.0 12.5 %collective-permute-start.13 = (bf16[2,192,384]{2,1,0:T(8,128)(2,1)S(1)}, bf16[2,192,384]{2,1,0:T(8,128)(2,1)S(1)}, u32[]{:S(2)}, u32[]{:S(2)}) collective-permute-start(bf16[2,192,384]{2,1,0:T(8,128)(2,1)S(1)} %select_select_fusion.2), channel_id=1, source_target_pairs={{2,4},{3,5},{4,6},{5,7},{8,10},{9,11},{10,12},{11,13},{12,14},{13,... | collective-permute-start | bytes 884744 | tf_op jit(solution)/shard_map/ppermute | solution.py:40
  56.5 15.5 %collective-permute-start.12 = (bf16[2,192,384]{2,1,0:T(8,128)(2,1)S(1)}, bf16[2,192,384]{2,1,0:T(8,128)(2,1)S(1)}, u32[]{:S(2)}, u32[]{:S(2)}) collective-permute-start(bf16[2,192,384]{2,1,0:T(8,128)(2,1)S(1)} %select_select_fusion.3), channel_id=1, source_target_pairs={{0,2},{1,3},{2,4},{3,5},{8,10},{9,11},{10,12},{11,13},{12,14},{13,... | collective-permute-start | bytes 884744 | tf_op jit(solution)/shard_map/ppermute | solution.py:40
  57.8 15.5 %collective-permute-start.8 = (bf16[384,384]{1,0:T(8,128)(2,1)S(1)}, bf16[384,384]{1,0:T(8,128)(2,1)S(1)}, u32[]{:S(2)}, u32[]{:S(2)}) collective-permute-start(bf16[384,384]{1,0:T(8,128)(2,1)S(1)} %bitcast.75), channel_id=1, source_target_pairs={{0,8},{1,9},{2,10},{3,11},{4,12},{5,13},{6,14},{7,15},{8,0},{9,1},... | collective-permute-start | bytes 884744 | tf_op jit(solution)/shard_map/ppermute | solution.py:40
  57.8 16.8 %collective-permute-start.9 = (bf16[384,384]{1,0:T(8,128)(2,1)S(1)}, bf16[384,384]{1,0:T(8,128)(2,1)S(1)}, u32[]{:S(2)}, u32[]{:S(2)}) collective-permute-start(bf16[384,384]{1,0:T(8,128)(2,1)S(1)} %bitcast.74), channel_id=1, source_target_pairs={{0,16},{1,17},{2,18},{3,19},{4,20},{5,21},{6,22},{7,23},{8,24},{9,... | collective-permute-start | bytes 884744 | tf_op jit(solution)/shard_map/ppermute | solution.py:40
  57.9 16.9 %collective-permute-start.10 = (bf16[384,384]{1,0:T(8,128)(2,1)S(1)}, bf16[384,384]{1,0:T(8,128)(2,1)S(1)}, u32[]{:S(2)}, u32[]{:S(2)}) collective-permute-start(bf16[384,384]{1,0:T(8,128)(2,1)S(1)} %bitcast.73), channel_id=1, source_target_pairs={{0,24},{1,25},{2,26},{3,27},{4,28},{5,29},{6,30},{7,31},{8,16},{9,... | collective-permute-start | bytes 884744 | tf_op jit(solution)/shard_map/ppermute | solution.py:40
  60.0 21.0 %copy-start.1 = (bf16[2,2,192,384]{3,2,1,0:T(8,128)(2,1)}, bf16[2,2,192,384]{3,2,1,0:T(8,128)(2,1)S(1)}, u32[]{:S(2)}) copy-start(bf16[2,2,192,384]{3,2,1,0:T(8,128)(2,1)S(1)} %pad_maximum_fusion.6.refs_1_) | copy-start | bytes 1769476
  60.1 27.2 %copy-start.2 = (bf16[2,2,192,384]{3,2,1,0:T(8,128)(2,1)}, bf16[2,2,192,384]{3,2,1,0:T(8,128)(2,1)S(1)}, u32[]{:S(2)}) copy-start(bf16[2,2,192,384]{3,2,1,0:T(8,128)(2,1)S(1)} %pad_maximum_fusion.5.refs_0_) | copy-start | bytes 1769476
  67.6 7.2 %copy-start.3 = (bf16[2,192,384]{2,1,0:T(8,128)(2,1)}, bf16[2,192,384]{2,1,0:T(8,128)(2,1)S(1)}, u32[]{:S(2)}) copy-start(bf16[2,192,384]{2,1,0:T(8,128)(2,1)S(1)} %collective-permute-done.13.refs_4_) | copy-start | bytes 884740
  67.6 8.0 %collective-permute-start.21 = (bf16[2,192,384]{2,1,0:T(8,128)(2,1)S(1)}, bf16[2,192,384]{2,1,0:T(8,128)(2,1)S(1)}, u32[]{:S(2)}, u32[]{:S(2)}) collective-permute-start(bf16[2,192,384]{2,1,0:T(8,128)(2,1)S(1)} %collective-permute-done.11.refs_2_), channel_id=1, source_target_pairs={{0,8},{1,9},{2,10},{3,11},{4,12},{5,13},{6,14},{7,15},{8,0},{9,1},... | collective-permute-start | bytes 884744 | tf_op jit(solution)/shard_map/ppermute | solution.py:40
  72.0 25.0 %copy-start.7 = (bf16[2,192,384]{2,1,0:T(8,128)(2,1)}, bf16[2,192,384]{2,1,0:T(8,128)(2,1)S(1)}, u32[]{:S(2)}) copy-start(bf16[2,192,384]{2,1,0:T(8,128)(2,1)S(1)} %collective-permute-done.12.refs_3_) | copy-start | bytes 884740
  72.0 9.1 %collective-permute-start.15 = (bf16[2,192,384]{2,1,0:T(8,128)(2,1)S(1)}, bf16[2,192,384]{2,1,0:T(8,128)(2,1)S(1)}, u32[]{:S(2)}, u32[]{:S(2)}) collective-permute-start(bf16[2,192,384]{2,1,0:T(8,128)(2,1)S(1)} %broadcast_select_fusion.1), channel_id=1, source_target_pairs={{4,6},{5,7},{8,12},{9,13},{12,14},{13,15},{20,22},{21,23},{24,28},... | collective-permute-start | bytes 884744 | tf_op jit(solution)/shard_map/ppermute | solution.py:40
  73.3 14.0 %collective-permute-start.14 = (bf16[2,192,384]{2,1,0:T(8,128)(2,1)S(1)}, bf16[2,192,384]{2,1,0:T(8,128)(2,1)S(1)}, u32[]{:S(2)}, u32[]{:S(2)}) collective-permute-start(bf16[2,192,384]{2,1,0:T(8,128)(2,1)S(1)} %select_select_fusion.1), channel_id=1, source_target_pairs={{2,4},{3,5},{4,6},{5,7},{8,10},{9,11},{10,12},{11,13},{12,14},{13,... | collective-permute-start | bytes 884744 | tf_op jit(solution)/shard_map/ppermute | solution.py:40
  74.6 22.3 %collective-permute-start.23 = (bf16[2,192,384]{2,1,0:T(8,128)(2,1)S(1)}, bf16[2,192,384]{2,1,0:T(8,128)(2,1)S(1)}, u32[]{:S(2)}, u32[]{:S(2)}) collective-permute-start(bf16[2,192,384]{2,1,0:T(8,128)(2,1)S(1)} %collective-permute-done.13.refs_4_), channel_id=1, source_target_pairs={{0,8},{1,9},{2,10},{3,11},{4,12},{5,13},{6,14},{7,15},{8,0},{9,1},... | collective-permute-start | bytes 884744 | tf_op jit(solution)/shard_map/ppermute | solution.py:40
  74.8 25.6 %collective-permute-start.18 = (bf16[2,2,192,384]{3,2,1,0:T(8,128)(2,1)S(1)}, bf16[2,2,192,384]{3,2,1,0:T(8,128)(2,1)S(1)}, u32[]{:S(2)}, u32[]{:S(2)}) collective-permute-start(bf16[2,2,192,384]{3,2,1,0:T(8,128)(2,1)S(1)} %pad_maximum_fusion.6.refs_1_), channel_id=1, source_target_pairs={{12,8},{13,9},{28,24},{29,25}} | collective-permute-start | bytes 1769480 | tf_op jit(solution)/shard_map/ppermute | solution.py:40
  75.5 22.7 %copy-start.17 = (bf16[2,192,384]{2,1,0:T(8,128)(2,1)}, bf16[2,192,384]{2,1,0:T(8,128)(2,1)S(1)}, u32[]{:S(2)}) copy-start(bf16[2,192,384]{2,1,0:T(8,128)(2,1)S(1)} %collective-permute-done.21.refs_12_) | copy-start | bytes 884740
  75.5 25.4 %collective-permute-start.17 = (bf16[2,2,192,384]{3,2,1,0:T(8,128)(2,1)S(1)}, bf16[2,2,192,384]{3,2,1,0:T(8,128)(2,1)S(1)}, u32[]{:S(2)}, u32[]{:S(2)}) collective-permute-start(bf16[2,2,192,384]{3,2,1,0:T(8,128)(2,1)S(1)} %select_select_fusion), channel_id=1, source_target_pairs={{2,0},{3,1},{8,14},{9,15},{10,8},{11,9},{12,10},{13,11},{18,16},{1... | collective-permute-start | bytes 1769480 | tf_op jit(solution)/shard_map/ppermute | solution.py:40
  81.0 20.0 %copy-start.18 = (bf16[2,192,384]{2,1,0:T(8,128)(2,1)}, bf16[2,192,384]{2,1,0:T(8,128)(2,1)S(1)}, u32[]{:S(2)}) copy-start(bf16[2,192,384]{2,1,0:T(8,128)(2,1)S(1)} %collective-permute-done.15.refs_6_) | copy-start | bytes 884740
  81.0 20.0 %collective-permute-start.20 = (bf16[2,2,192,384]{3,2,1,0:T(8,128)(2,1)S(1)}, bf16[2,2,192,384]{3,2,1,0:T(8,128)(2,1)S(1)}, u32[]{:S(2)}, u32[]{:S(2)}) collective-permute-start(bf16[2,2,192,384]{3,2,1,0:T(8,128)(2,1)S(1)} %pad_maximum_fusion.6.refs_1_), channel_id=1, source_target_pairs={{0,8},{1,9},{2,10},{3,11},{4,12},{5,13},{6,14},{7,15},{8,0},{9,1},... | collective-permute-start | bytes 1769480 | tf_op jit(solution)/shard_map/ppermute | solution.py:40
  87.4 14.1 %copy-start.4 = (bf16[2,192,384]{2,1,0:T(8,128)(2,1)}, bf16[2,192,384]{2,1,0:T(8,128)(2,1)S(1)}, u32[]{:S(2)}) copy-start(bf16[2,192,384]{2,1,0:T(8,128)(2,1)S(1)} %collective-permute-done.14.refs_5_) | copy-start | bytes 884740
  87.4 14.1 %collective-permute-start.19 = (bf16[2,2,192,384]{3,2,1,0:T(8,128)(2,1)S(1)}, bf16[2,2,192,384]{3,2,1,0:T(8,128)(2,1)S(1)}, u32[]{:S(2)}, u32[]{:S(2)}) collective-permute-start(bf16[2,2,192,384]{3,2,1,0:T(8,128)(2,1)S(1)} %pad_maximum_fusion.5.refs_0_), channel_id=1, source_target_pairs={{0,8},{1,9},{2,10},{3,11},{4,12},{5,13},{6,14},{7,15},{8,0},{9,1},... | collective-permute-start | bytes 1769480 | tf_op jit(solution)/shard_map/ppermute | solution.py:40
  96.9 2.0 %collective-permute-start.22 = (bf16[2,192,384]{2,1,0:T(8,128)(2,1)S(1)}, bf16[2,192,384]{2,1,0:T(8,128)(2,1)S(1)}, u32[]{:S(2)}, u32[]{:S(2)}) collective-permute-start(bf16[2,192,384]{2,1,0:T(8,128)(2,1)S(1)} %collective-permute-done.12.refs_3_), channel_id=1, source_target_pairs={{0,8},{1,9},{2,10},{3,11},{4,12},{5,13},{6,14},{7,15},{8,0},{9,1},... | collective-permute-start | bytes 884744 | tf_op jit(solution)/shard_map/ppermute | solution.py:40
  99.0 12.5 %copy-start.20 = (bf16[2,192,384]{2,1,0:T(8,128)(2,1)}, bf16[2,192,384]{2,1,0:T(8,128)(2,1)S(1)}, u32[]{:S(2)}) copy-start(bf16[2,192,384]{2,1,0:T(8,128)(2,1)S(1)} %collective-permute-done.22.refs_13_) | copy-start | bytes 884740
  99.0 10.1 %collective-permute-start.16 = (bf16[2,192,384]{2,1,0:T(8,128)(2,1)S(1)}, bf16[2,192,384]{2,1,0:T(8,128)(2,1)S(1)}, u32[]{:S(2)}, u32[]{:S(2)}) collective-permute-start(bf16[2,192,384]{2,1,0:T(8,128)(2,1)S(1)} %broadcast_select_fusion), channel_id=1, source_target_pairs={{4,6},{5,7},{8,12},{9,13},{12,14},{13,15},{20,22},{21,23},{24,28},... | collective-permute-start | bytes 884744 | tf_op jit(solution)/shard_map/ppermute | solution.py:40
  100.4 11.1 %copy-start.11 = (bf16[2,2,192,384]{3,2,1,0:T(8,128)(2,1)}, bf16[2,2,192,384]{3,2,1,0:T(8,128)(2,1)S(1)}, u32[]{:S(2)}) copy-start(bf16[2,2,192,384]{3,2,1,0:T(8,128)(2,1)S(1)} %collective-permute-done.18.refs_9_) | copy-start | bytes 1769476
  100.5 11.0 %collective-permute-start.28 = (bf16[2,2,192,384]{3,2,1,0:T(8,128)(2,1)S(1)}, bf16[2,2,192,384]{3,2,1,0:T(8,128)(2,1)S(1)}, u32[]{:S(2)}, u32[]{:S(2)}) collective-permute-start(bf16[2,2,192,384]{3,2,1,0:T(8,128)(2,1)S(1)} %collective-permute-done.18.refs_9_), channel_id=1, source_target_pairs={{0,8},{1,9},{2,10},{3,11},{4,12},{5,13},{6,14},{7,15},{8,0},{9,1},... | collective-permute-start | bytes 1769480 | tf_op jit(solution)/shard_map/ppermute | solution.py:40
  100.9 10.6 %copy-start.12 = (bf16[2,2,192,384]{3,2,1,0:T(8,128)(2,1)}, bf16[2,2,192,384]{3,2,1,0:T(8,128)(2,1)S(1)}, u32[]{:S(2)}) copy-start(bf16[2,2,192,384]{3,2,1,0:T(8,128)(2,1)S(1)} %collective-permute-done.17.refs_8_) | copy-start | bytes 1769476
  100.9 10.6 %collective-permute-start.27 = (bf16[2,2,192,384]{3,2,1,0:T(8,128)(2,1)S(1)}, bf16[2,2,192,384]{3,2,1,0:T(8,128)(2,1)S(1)}, u32[]{:S(2)}, u32[]{:S(2)}) collective-permute-start(bf16[2,2,192,384]{3,2,1,0:T(8,128)(2,1)S(1)} %collective-permute-done.17.refs_8_), channel_id=1, source_target_pairs={{0,8},{1,9},{2,10},{3,11},{4,12},{5,13},{6,14},{7,15},{8,0},{9,1},... | collective-permute-start | bytes 1769480 | tf_op jit(solution)/shard_map/ppermute | solution.py:40
  101.0 10.5 %copy-start.13 = (bf16[2,2,192,384]{3,2,1,0:T(8,128)(2,1)}, bf16[2,2,192,384]{3,2,1,0:T(8,128)(2,1)S(1)}, u32[]{:S(2)}) copy-start(bf16[2,2,192,384]{3,2,1,0:T(8,128)(2,1)S(1)} %collective-permute-done.20.refs_11_) | copy-start | bytes 1769476
  101.0 9.2 %collective-permute-start.25 = (bf16[2,192,384]{2,1,0:T(8,128)(2,1)S(1)}, bf16[2,192,384]{2,1,0:T(8,128)(2,1)S(1)}, u32[]{:S(2)}, u32[]{:S(2)}) collective-permute-start(bf16[2,192,384]{2,1,0:T(8,128)(2,1)S(1)} %collective-permute-done.15.refs_6_), channel_id=1, source_target_pairs={{0,8},{1,9},{2,10},{3,11},{4,12},{5,13},{6,14},{7,15},{8,0},{9,1},... | collective-permute-start | bytes 884744 | tf_op jit(solution)/shard_map/ppermute | solution.py:40
  101.5 10.1 %copy-start.14 = (bf16[2,2,192,384]{3,2,1,0:T(8,128)(2,1)}, bf16[2,2,192,384]{3,2,1,0:T(8,128)(2,1)S(1)}, u32[]{:S(2)}) copy-start(bf16[2,2,192,384]{3,2,1,0:T(8,128)(2,1)S(1)} %collective-permute-done.19.refs_10_) | copy-start | bytes 1769476
  101.5 8.8 %collective-permute-start.24 = (bf16[2,192,384]{2,1,0:T(8,128)(2,1)S(1)}, bf16[2,192,384]{2,1,0:T(8,128)(2,1)S(1)}, u32[]{:S(2)}, u32[]{:S(2)}) collective-permute-start(bf16[2,192,384]{2,1,0:T(8,128)(2,1)S(1)} %collective-permute-done.14.refs_5_), channel_id=1, source_target_pairs={{0,8},{1,9},{2,10},{3,11},{4,12},{5,13},{6,14},{7,15},{8,0},{9,1},... | collective-permute-start | bytes 884744 | tf_op jit(solution)/shard_map/ppermute | solution.py:40
  109.1 2.4 %collective-permute-start.26 = (bf16[2,192,384]{2,1,0:T(8,128)(2,1)S(1)}, bf16[2,192,384]{2,1,0:T(8,128)(2,1)S(1)}, u32[]{:S(2)}, u32[]{:S(2)}) collective-permute-start(bf16[2,192,384]{2,1,0:T(8,128)(2,1)S(1)} %collective-permute-done.16.refs_7_), channel_id=1, source_target_pairs={{0,8},{1,9},{2,10},{3,11},{4,12},{5,13},{6,14},{7,15},{8,0},{9,1},... | collective-permute-start | bytes 884744 | tf_op jit(solution)/shard_map/ppermute | solution.py:40
  121.6 8.3 %collective-permute-start.29 = (bf16[2,192,384]{2,1,0:T(8,128)(2,1)S(1)}, bf16[2,192,384]{2,1,0:T(8,128)(2,1)S(1)}, u32[]{:S(2)}, u32[]{:S(2)}) collective-permute-start(bf16[2,192,384]{2,1,0:T(8,128)(2,1)S(1)} %copy-done.28), channel_id=1, source_target_pairs={{0,1},{1,0},{2,3},{3,2},{4,5},{5,4},{6,7},{7,6},{8,9},{9,8},{10,11... | collective-permute-start | bytes 884744 | tf_op jit(solution)/shard_map/ppermute | solution.py:40
  122.9 10.7 %collective-permute-start.30 = (bf16[384,384]{1,0:T(8,128)(2,1)}, bf16[384,384]{1,0:T(8,128)(2,1)S(1)}, u32[]{:S(2)}, u32[]{:S(2)}) collective-permute-start(bf16[384,384]{1,0:T(8,128)(2,1)} %get-tuple-element.104), channel_id=1, source_target_pairs={{0,8},{1,9},{2,10},{3,11},{4,12},{5,13},{6,14},{7,15},{8,0},{9,1},... | collective-permute-start | bytes 884744 | tf_op jit(solution)/shard_map/ppermute | solution.py:40
  123.5 10.1 %collective-permute-start.31 = (bf16[384,384]{1,0:T(8,128)(2,1)}, bf16[384,384]{1,0:T(8,128)(2,1)S(1)}, u32[]{:S(2)}, u32[]{:S(2)}) collective-permute-start(bf16[384,384]{1,0:T(8,128)(2,1)} %get-tuple-element.105), channel_id=1, source_target_pairs={{0,16},{1,17},{2,18},{3,19},{4,20},{5,21},{6,22},{7,23},{8,24},{9,... | collective-permute-start | bytes 884744 | tf_op jit(solution)/shard_map/ppermute | solution.py:40
  123.5 15.3 %collective-permute-start.32 = (bf16[384,384]{1,0:T(8,128)(2,1)}, bf16[384,384]{1,0:T(8,128)(2,1)S(1)}, u32[]{:S(2)}, u32[]{:S(2)}) collective-permute-start(bf16[384,384]{1,0:T(8,128)(2,1)} %get-tuple-element.106), channel_id=1, source_target_pairs={{0,24},{1,25},{2,26},{3,27},{4,28},{5,29},{6,30},{7,31},{8,16},{9,... | collective-permute-start | bytes 884744 | tf_op jit(solution)/shard_map/ppermute | solution.py:40
  125.2 13.6 %copy-start.26 = (bf16[384,384]{1,0:T(8,128)(2,1)S(1)}, bf16[384,384]{1,0:T(8,128)(2,1)}, u32[]{:S(2)}) copy-start(bf16[384,384]{1,0:T(8,128)(2,1)} %get-tuple-element.108) | copy-start | bytes 884740
  (14 other events, 25.7 us)

commit v9 on v8

--- a/solution.py
+++ b/solution.py
@@ -23,6 +23,13 @@
         self.groups = self.rows // moments
         self.half = side // self.moms
         self.width = side // self.groups
+        self.subs = 2 if self.half % 32 == 0 else 1
+        self.sub = self.half // self.subs
+        self.chunks = [(0, u * self.sub, self.sub) for u in range(self.subs)]
+        self.chunks += [(q, 0, self.half) for q in range(1, self.moms)]
+        self.starts = [0]
+        for _, _, height in self.chunks:
+            self.starts.append(self.starts[-1] + height)
         self.keys = [
             (b, j)
             for b in range(moments)
@@ -97,14 +104,16 @@
         copy.wait()
 
 
-def sigma_kernel(plan, pair_count, chunks, place, quads, thirds, *refs):
+def sigma_kernel(plan, pair_count, u, chunks, place, quads, thirds, *refs):
     moms, moments, groups = plan.moms, plan.moments, plan.groups
-    half, side, count = plan.half, plan.side, plan.moms * plan.moments
-    lesser_in, partner_in = refs[:moms], refs[moms : 2 * moms]
-    outs = refs[2 * moms : 2 * moms + count]
-    lesser, partner, pairs, third, held, in_sems, out_sems = refs[2 * moms + count :]
+    half, sub, side, count = plan.half, plan.sub, plan.side, plan.moms * plan.moments
+    refs = list(refs)
+    take = lambda number: [refs.pop(0) for _ in range(number)]
+    lesser_in, partner_in = take(moms), take(moms)
+    before, outs = take(count - moments if u else 0), take(count)
+    lesser, partner, pairs, third, held, in_sems, out_sems, before_sems = refs
     x, y = place[0] // groups, place[2]
-    height = half // chunks
+    height = sub // chunks
     copies = [[] for _ in range(chunks)]
     for chunk in range(chunks):
         rows = pl.ds(chunk * height, height)
@@ -112,7 +121,7 @@
             for q in range(moms):
                 source = sources[q].at[:, :, rows, :]
                 if q == 0:
-                    start = pl.multiple_of(y * half + chunk * height, 16)
+                    start = pl.multiple_of(y * half + u * sub + chunk * height, 16)
                     source = sources[q].at[:, :, pl.ds(start, height), :]
                 copy = pltpu.make_async_copy(
                     source,
@@ -121,6 +130,14 @@
                 )
                 copy.start()
                 copies[chunk].append(copy)
+    earlier = [
+        pltpu.make_async_copy(
+            before[n], held.at[moments + n, :, pl.ds(0, u * sub), :], before_sems.at[n]
+        )
+        for n in range(len(before))
+    ]
+    for copy in earlier:
+        copy.start()
     scale = 1.0 / pair_count
     lanes = 128 if side % 128 == 0 else side
     order = [(q, b) for q in reversed(range(moms)) for b in range(moments)]
@@ -130,7 +147,8 @@
             copy.wait()
 
         def block(index, _, chunk=chunk):
-            rows = pl.ds(pl.multiple_of(chunk * height + index * 16, 16), 16)
+            row = chunk * height + index * 16
+            rows = pl.ds(pl.multiple_of(row, 16), 16)
             for c in range(count):
                 for p in range(2):
                     third[c, p] = partner[c, p, rows, :].astype(jnp.float32)
@@ -148,6 +166,7 @@
                     n += 1
             for q, b in order:
                 moment = (y ^ q) * moments + (x ^ b)
+                to = rows if q == 0 else pl.ds(pl.multiple_of(u * sub + row, 16), 16)
                 for lane in range(0, side, lanes):
                     cols = pl.ds(lane, lanes)
                     total_re = total_im = None
@@ -159,18 +178,28 @@
                         f_im = p_re * c_im + p_im * c_re
                         total_re = f_re if total_re is None else total_re + f_re
                         total_im = f_im if total_im is None else total_im + f_im
-                    held[q * moments + b, 0, rows, cols] = (total_re * scale).astype(jnp.bfloat16)
-                    held[q * moments + b, 1, rows, cols] = (total_im * scale).astype(jnp.bfloat16)
+                    held[q * moments + b, 0, to, cols] = (total_re * scale).astype(jnp.bfloat16)
+                    held[q * moments + b, 1, to, cols] = (total_im * scale).astype(jnp.bfloat16)
             return 0
 
         lax.fori_loop(0, height // 16, block, 0)
-        rows = pl.ds(chunk * height, height)
         for index in range(count):
+            offset = chunk * height + (u * sub if index >= moments else 0)
+            rows = pl.ds(offset, height)
             copy = pltpu.make_async_copy(
                 held.at[index, :, rows, :], outs[index].at[:, rows, :], out_sems.at[chunk * count + index]
             )
             copy.start()
             sent.append(copy)
+    for copy in earlier:
+        copy.wait()
+    for n in range(len(before)):
+        rows = pl.ds(0, u * sub)
+        copy = pltpu.make_async_copy(
+            held.at[moments + n, :, rows, :], outs[moments + n].at[:, rows, :], before_sems.at[n]
+        )
+        copy.start()
+        sent.append(copy)
     for copy in sent:
         copy.wait()
 
@@ -179,10 +208,10 @@
     ins, out, sems = refs[:-2], refs[-2], refs[-1]
     x, y = place[0] // plan.groups, place[2]
     copies = []
-    for q in range(plan.moms):
-        rows = pl.ds(pl.multiple_of((y ^ q) * plan.half, plan.half), plan.half)
+    for k, (q, first, height) in enumerate(plan.chunks):
+        rows = pl.ds(pl.multiple_of((y ^ q) * plan.half + first, 16), height)
         for b in range(plan.moments):
-            index = q * plan.moments + b
+            index = k * plan.moments + b
             copies.append(pltpu.make_async_copy(ins[index], out.at[x ^ b, :, rows, :], sems.at[index]))
     run_copies(copies)
 
@@ -202,14 +231,15 @@
             def _(key=key, col=col):
                 for t in range(groups):
                     row = key[0] * groups + (g ^ t)
-                    for q in range(moms):
-                        index, part = sources[key, col, q, t]
-                        ref = sig_in[index] if part is None else sig_in[index].at[part]
-                        at = pl.ds(pl.multiple_of((y ^ q) * half, half), half)
+                    for k, (q, first, height) in enumerate(plan.chunks):
+                        index, start = sources[key, col, k, t]
+                        at = pl.ds(pl.multiple_of((y ^ q) * half + first, 16), height)
                         for p in range(2):
                             lane = pl.ds((2 * key[1] + p) * side, side)
                             pltpu.make_async_copy(
-                                ref.at[p], sig.at[row, at, lane], sems.at[key[0]]
+                                sig_in[index].at[p, pl.ds(start, height), :],
+                                sig.at[row, at, lane],
+                                sems.at[key[0]],
                             ).start()
 
     weight = 1.0 / math.sqrt(side * rows)
@@ -221,12 +251,9 @@
         if row == max(1, row // groups * groups):
             for key in keys:
                 if key[0] == row // groups:
-                    for t in range(groups * moms * 2):
-                        pltpu.make_async_copy(
-                            sig.at[0, pl.ds(0, half), pl.ds(0, side)],
-                            sig.at[0, pl.ds(0, half), pl.ds(0, side)],
-                            sems.at[key[0]],
-                        ).wait()
+                    for _ in range(groups * 2):
+                        tile = sig.at[0, :, pl.ds(0, side)]
+                        pltpu.make_async_copy(tile, tile, sems.at[key[0]]).wait()
         pending = right[r ^ row].astype(jnp.float32)
         if row > 0:
             depth = 2 * side * row
@@ -276,102 +303,119 @@
     def exchange_row(value, s):
         return plan.send(value, lambda a, b, c: (a ^ s, b, c))
 
-    def half_of(value, q):
-        return lax.dynamic_slice_in_dim(value, (y ^ q) * half, half, 2)
-
-    halves = [half_of(lesser, q) for q in range(1, moms)]
-    greater, diag_inverse, right_side = after((greater, diag_inverse, right_side), halves)
-    lesser_all = [lesser] + [exchange_mom(halves[q - 1], q) for q in range(1, moms)]
+    def by_block(came):
+        return [lax.select_n(x ^ b, *came) for b in range(moments)]
+
+    def part_of(value, q, u):
+        return lax.dynamic_slice_in_dim(value, (y ^ q) * half + u * plan.sub, plan.sub, 2)
+
+    parts = [part_of(lesser, q, 0) for q in range(1, moms)]
+    greater, diag_inverse, right_side = after((greater, diag_inverse, right_side), parts)
+    lesser_came = [[exchange_mom(parts[q - 1], q) for q in range(1, moms)]]
     partner = jnp.swapaxes(greater, 2, 3)
-    halves = [half_of(partner, q) for q in range(1, moms)]
-    diag_inverse, right_side = after((diag_inverse, right_side), halves)
-    partner_all = [partner] + [exchange_mom(halves[q - 1], q) for q in range(1, moms)]
-
-    came = [lax.dynamic_index_in_dim(diag_inverse, x ^ b, 0, keepdims=False) for b in range(moments)]
-    came = came[:1] + [exchange_row(came[b], b * groups) for b in range(1, moments)]
-    diag = [lax.select_n(x ^ b, *came) for b in range(moments)]
+    parts = [part_of(partner, q, 0) for q in range(1, moms)]
+    diag_inverse, right_side = after((diag_inverse, right_side), parts)
+    partner_came = [[exchange_mom(parts[q - 1], q) for q in range(1, moms)]]
+    for u in range(1, plan.subs):
+        parts = [(part_of(lesser, q, u), part_of(partner, q, u)) for q in range(1, moms)]
+        parts = after(parts, lesser_came[-1])
+        lesser_came.append([exchange_mom(parts[q - 1][0], q) for q in range(1, moms)])
+        partner_came.append([exchange_mom(parts[q - 1][1], q) for q in range(1, moms)])
+
+    mine = [lax.dynamic_index_in_dim(diag_inverse, x ^ b, 0, keepdims=False) for b in range(moments)]
+    diag = mine[:1] + [exchange_row(mine[b], b * groups) for b in range(1, moments)]
 
     right = right_side.reshape(moments, side, 2, groups, width).transpose(0, 3, 1, 2, 4)
     right = right.reshape(rows, side, 2 * width)
     right_all = [lax.dynamic_index_in_dim(right, r ^ s, 0, keepdims=False) for s in range(rows)]
+    high = jnp.maximum(triples[..., 0], triples[..., 1])
+    low = jnp.minimum(triples[..., 0], triples[..., 1])
+    quads, thirds = high * (high + 1) // 2 + low, triples[..., 2]
+    copies = 2 if plan.sub % 32 == 0 else 1
+    came = []
+    whole = []
+    rest_of = []
+
+    def self_energy(u, *behind):
+        height = (u + 1) * plan.sub
+        shapes = [(2, plan.sub, side)] * moments + [(2, height, side)] * (count - moments)
+        return pl.pallas_call(
+            functools.partial(sigma_kernel, plan, pair_count, u, copies),
+            out_shape=[jax.ShapeDtypeStruct(shape, bf16) for shape in shapes],
+            in_specs=[smem()] * 3 + hbm(2 * moms + len(rest_of)),
+            out_specs=hbm(count),
+            scratch_shapes=[
+                pltpu.VMEM((count, 2, plan.sub, side), bf16),
+                pltpu.VMEM((count, 2, plan.sub, side), bf16),
+                pltpu.VMEM((count * (count + 1) // 2, 2, 16, side), f32),
+                pltpu.VMEM((count, 2, 16, side), f32),
+                pltpu.VMEM((count, 2, height, side), bf16),
+                dma(copies * 2 * moms),
+                dma(copies * count),
+                dma(count),
+            ],
+            compiler_params=params,
+            name="self_energy",
+        )(
+            *after((place, quads, thirds), behind),
+            *([lesser] + lesser_came[u]),
+            *([partner] + partner_came[u]),
+            *rest_of,
+        )
+
+    def to_row(value, b, q):
+        goal = lambda a, c, m: (a ^ (b * groups), c, m ^ q) if a > c else None
+        return plan.send(value, goal)
+
+    for u in range(plan.subs):
+        slots = list(self_energy(u, right_all, diag))
+        came = [after(tiles, rest_of, slots) for tiles in came]
+        rest_of = slots[moments:]
+        came.append(slots[:1] + [to_row(slots[b], b, 0) for b in range(1, moments)])
+        whole += slots[:moments]
+    late = []
+    for q in range(1, moms):
+        mine = rest_of[(q - 1) * moments : q * moments]
+        came.append(
+            [exchange_mom(mine[0], q)] + [to_row(mine[b], b, q) for b in range(1, moments)]
+        )
+        late += [(came[-1][0], None)] + [(mine[b], q) for b in range(1, moments)]
+    right_all = after(right_all, came[-1])
+    right_all = right_all[:1] + [exchange_row(right_all[s], s) for s in range(1, rows)]
+    right_came = jnp.stack(right_all)
+    diag = after(by_block(diag), came[-1])
     diag = [jnp.concatenate([value[0], value[1]], axis=1) for value in diag]
     diag_all = [
         diag[b] if t == 0 else exchange_row(diag[b], t) for b in range(moments) for t in range(groups)
     ]
-    lesser_all, partner_all, right_all, diag_all = lax.optimization_barrier(
-        (lesser_all, partner_all, right_all, diag_all)
-    )
     diag_came = jnp.stack(diag_all)
-
-    high = jnp.maximum(triples[..., 0], triples[..., 1])
-    low = jnp.minimum(triples[..., 0], triples[..., 1])
-    quads, thirds = high * (high + 1) // 2 + low, triples[..., 2]
-    chunks = 4 if half % 64 == 0 else 1
-    slots = pl.pallas_call(
-        functools.partial(sigma_kernel, plan, pair_count, chunks),
-        out_shape=[jax.ShapeDtypeStruct((2, half, side), bf16)] * count,
-        in_specs=[smem()] * 3 + hbm(2 * moms),
-        out_specs=hbm(count),
-        scratch_shapes=[
-            pltpu.VMEM((count, 2, half, side), bf16),
-            pltpu.VMEM((count, 2, half, side), bf16),
-            pltpu.VMEM((count * (count + 1) // 2, 2, 16, side), f32),
-            pltpu.VMEM((count, 2, 16, side), f32),
-            pltpu.VMEM((count, 2, half, side), bf16),
-            dma(chunks * 2 * moms),
-            dma(chunks * count),
-        ],
-        compiler_params=params,
-        name="self_energy",
-    )(place, quads, thirds, *lesser_all, *partner_all)
-
-    came = []
-
-    def own_tiles(q):
-        mine = slots[q * moments : (q + 1) * moments]
-        if came:
-            mine = mine[:1] + after(mine[1:], came[-1][1:])
-        got = []
-        for b in range(1, moments):
-            got.append(
-                plan.send(mine[b], lambda a, c, m: (a ^ (b * groups), c, m ^ q) if a > c else None)
-            )
-        came.append([mine[0] if q == 0 else exchange_mom(mine[0], q)] + got)
-
-    def by_block(came):
-        return [lax.select_n(x ^ b, *came) for b in range(moments)]
-
-    for q in range(moms):
-        own_tiles(q)
-    right_all = after(right_all, came[-1])
-    right_all = right_all[:1] + [exchange_row(right_all[s], s) for s in range(1, rows)]
-    right_came = jnp.stack(right_all)
 
     def valid(key, a):
         return key[0] * groups + a % groups > key[1]
 
     found = {}
-    own = [by_block(came[q]) for q in range(moms)]
-    both = [jnp.stack([own[q][b] for q in range(moms)]) for b in range(moments)]
+    own = [by_block(tiles) for tiles in came]
+    both = [jnp.concatenate([tiles[b] for tiles in own], axis=1) for b in range(moments)]
     for key in plan.keys:
-        for q in range(moms):
-            found[key, key[1], q] = (both[key[0]], q)
-
-    def choose(values):
-        chosen = used = None
+        for k in range(len(plan.chunks)):
+            found[key, key[1], k] = (both[key[0]], plan.starts[k])
+
+    def choose(values, behind):
+        distinct = list({id(value): value for value in values.values()}.values())
+        number = {id(value): n for n, value in enumerate(distinct)}
+        distinct = after(distinct, behind)
+        chosen = distinct[0]
         for col, value in values.items():
-            if chosen is None:
-                chosen = used = value
-            elif value is not used:
-                chosen = jnp.where(z == col, value, chosen)
+            if number[id(value)]:
+                chosen = jnp.where(z == col, distinct[number[id(value)]], chosen)
         return chosen
 
-    def shift(values, goals):
+    def shift(values, goals, behind):
         goal = lambda a, c, m: (a, goals[c][1], m) if c in goals and valid(goals[c][0], a) else None
-        return plan.send(choose(values), goal)
+        return plan.send(choose(values, behind), goal)
 
     ring, rest = plan.ring(), plan.rest()
-    got = [[] for _ in range(moms)]
+    got = [[] for _ in plan.chunks]
 
     def ring_step(q, number, *behind):
         sends = {col: item for (n, col), item in ring.items() if n == number}
@@ -379,28 +423,26 @@
             col: own[q][key[0]] if step is None else got[q][step]
             for col, (key, _, step) in sends.items()
         }
-        value = shift(after(values, behind), {col: item[:2] for col, item in sends.items()})
+        value = shift(values, {col: item[:2] for col, item in sends.items()}, behind)
         got[q].append(value)
         for key, to, _ in sends.values():
-            found[key, to, q] = (value, None)
+            found[key, to, q] = (value, 0)
 
     def rest_step(number, *behind):
         step = rest[number]
-        value = shift(after({col: both[key[0]] for col, (key, _) in step.items()}, behind), step)
+        value = shift({col: both[key[0]] for col, (key, _) in step.items()}, step, behind)
         for key, to in step.values():
-            for q in range(moms):
-                found[key, to, q] = (value, q)
+            for k in range(len(plan.chunks)):
+                found[key, to, k] = (value, plan.starts[k])
 
     for number in range(cols - 1):
-        for q in range(moms):
-            behind = [got[p][number] for p in range(q)]
-            if number == 1 and q + 1 < moms:
-                behind += [came[q + 1], diag_came]
-            if number == cols - 2 and q + 1 == moms:
-                behind.append(right_came)
-            ring_step(q, number, *behind)
+        for k in range(len(plan.chunks)):
+            behind = [got[k - 1][number]] if k else []
+            if number == 1 and k + 1 < len(plan.chunks):
+                behind.append(came[k + 1])
+            ring_step(k, number, *behind)
     for number in range(len(rest)):
-        rest_step(number, got[0][1], got[-1][0])
+        rest_step(number, got[0][1], got[-1][0], right_all)
 
     buffers = []
 
@@ -433,16 +475,13 @@
         name="substitution",
     )(place, diag_came, right_came, *sig_all)
 
-    whole = [slots[b] for b in range(moments)]
-    for q in range(1, moms):
-        whole.append(came[q][0])
-        for b in range(1, moments):
-            whole.append(exchange_mom(after(slots[q * moments + b], solved), q))
+    for value, q in late:
+        whole.append(value if q is None else exchange_mom(after(value, solved), q))
     sigma = pl.pallas_call(
         functools.partial(place_kernel, plan),
         out_shape=jax.ShapeDtypeStruct(lesser.shape, bf16),
-        in_specs=[smem()] + hbm(count),
-        scratch_shapes=[dma(count)],
+        in_specs=[smem()] + hbm(len(whole)),
+        scratch_shapes=[dma(len(whole))],
         compiler_params=params,
         name="place_sigma",
     )(place, *whole)

time: 145 us -> 155 us (1.069)
  waiting for transfers between devices: 57.1 us -> 69.3 us
  starting transfers between devices: 43.8 us -> 39.6 us
  other arithmetic: 8.58 us -> 5.33 us
  local copies, waits for them, and re-layouts: 14.6 us -> 17.7 us
  Pallas kernels: 17.6 us -> 20.6 us
    ppermute x33 -> x42, waiting for transfers between devices: 57.1 us -> 69.3 us  [send(): return lax.ppermute(value, AXES, pairs)]
    ppermute x33 -> x42, starting transfers between devices: 43.8 us -> 39.6 us  [send(): return lax.ppermute(value, AXES, pairs)]
    pallas_call x1 -> x2, Pallas kernels: 6.25 us -> 9.18 us  [self_energy(): pl.pallas_call(functools.partial(sigma_kernel, plan, pair_count, u, copie...]
    dynamic_slice x5, local copies, waits for them, and re-layouts: 1 us -> 3.83 us  [on_device(): lax.dynamic_index_in_dim(right, r ^ s, 0, keepdims=False)]
    unnamed x59 -> x79, local copies, waits for them, and re-layouts: 5.32 us -> 5.61 us
  transfers between devices with their start and end apart: 33 -> 42, of which waited for: 12 -> 14; matrix products, arithmetic and copies ran while one was open for 8% -> 9% of each run, Pallas kernels for 2% -> 5%
where the time goes in v9:
time: 155 us; the launch traced here: 154 us
  waiting for transfers between devices  69.3 us (45%)
  starting transfers between devices  39.6 us (26%)
  Pallas kernels  20.6 us (13%)
  local copies, waits for them, and re-layouts  17.7 us (11%)
  other arithmetic  5.33 us (3%)
    ppermute x42, waiting for transfers between devices, send(): return lax.ppermute(value, AXES, pairs)  69.3 us
    ppermute x42, starting transfers between devices, send(): return lax.ppermute(value, AXES, pairs)  39.6 us
    pallas_call x2, Pallas kernels, self_energy(): pl.pallas_call(functools.partial(sigma_kernel, plan, pair_count, u, copie...  9.18 us
    pallas_call x1, Pallas kernels, on_device(): pl.pallas_call(functools.partial(solve_kernel, plan, sources), out_shape=...  8.35 us
    unnamed x79, local copies, waits for them, and re-layouts  5.61 us
    dynamic_slice x5, local copies, waits for them, and re-layouts, on_device(): lax.dynamic_index_in_dim(right, r ^ s, 0, keepdims=False)  3.83 us
  transfers between devices with their start and end apart: 42, of which 14 were waited for; matrix products, arithmetic and copies ran while one was open for 9% of the time, Pallas kernels for 5%

profile of v9, /device:TPU:25, one launch (start us, length us, event | category | flops | bytes accessed | tf_op | source)
XLA Modules:
  0.0 154.0 jit_solution(17156748496106267368)
XLA Ops:
  0.7 2.0 %constant_dynamic-slice_fusion = (bf16[2,2,96,384]{3,2,1,0:T(8,128)(2,1)}, bf16[2,2,96,384]{3,2,1,0:T(8,128)(2,1)}) fusion(bf16[2,2,384,384]{3,2,1,0:T(8,128)(2,1)} %refs_0_.3, s32[]{:T(128)S(6)} %select_n.257, s32[]{:T(128)S(6)} %select_n.249), kind=kLoop, calls=%fused_computation.39 | loop fusion | bytes 1179656 | tf_op jit(solution)/shard_map/dynamic_slice | solution.py:310
  2.7 1.2 collective-permute-start.1
  4.8 0.9 dynamic-slice_bitcast_fusion.2
  5.9 0.9 dynamic-slice_bitcast_fusion
  6.8 1.2 collective-permute-start
  8.6 2.0 %copy.13 = bf16[2,384,2,384]{1,3,2,0:T(8,128)(2,1)S(1)} copy(bf16[2,384,2,384]{3,2,1,0:T(2,128)(2,1)S(1)} %copy-done.7) | data formatting | bytes 2359296 | tf_op jit(solution)/shard_map/optimization_barrier | solution.py:283
  10.7 1.0 constant_dynamic-slice_fusion.1
  12.3 1.2 collective-permute-start.3
  14.3 1.3 copy.15
  15.6 1.2 copy.16
  17.2 3.3 %collective-permute-done = bf16[2,384,384]{2,1,0:T(8,128)(2,1)S(1)} collective-permute-done((bf16[2,384,384]{2,1,0:T(8,128)(2,1)}, bf16[2,384,384]{2,1,0:T(8,128)(2,1)S(1)}, u32[]{:S(2)}, u32[]{:S(2)}) %collective-permute-start) | collective-permute-done | bytes 589856 | tf_op jit(solution)/shard_map/ppermute | solution.py:47
  20.7 4.5 %self_energy.2 = (bf16[2,96,384]{2,1,0:T(8,128)(2,1)}, bf16[2,96,384]{2,1,0:T(8,128)(2,1)}, bf16[2,96,384]{2,1,0:T(8,128)(2,1)}, bf16[2,96,384]{2,1,0:T(8,128)(2,1)}) custom-call(s32[3]{0:T(128)} %pad_add_fusion.place, s32[4,8]{1,0:T(4,128)} %fusion.1.quads, s32[4,8]{1,0:T(4,128)} %slice_bitcast_fusion.4.thirds, bf16[2,2,384,384]{3,2,1,0:T(8,128)(2,1)} %refs_0_.3, ...), custom_call_target="tpu_custom_call" | custom-call | tf_op jit(solution)/shard_map/self_energy/pallas_call | solution.py:342
  25.2 4.7 %collective-permute-done.4.refs_3_ = bf16[2,2,96,384]{3,2,1,0:T(8,128)(2,1)} collective-permute-done((bf16[2,2,96,384]{3,2,1,0:T(8,128)(2,1)}, bf16[2,2,96,384]{3,2,1,0:T(8,128)(2,1)}, u32[]{:S(2)}, u32[]{:S(2)}) %collective-permute-start.4) | collective-permute-done | bytes 294944 | tf_op jit(solution)/shard_map/ppermute | solution.py:47
  29.8 4.7 %self_energy.3 = (bf16[2,96,384]{2,1,0:T(8,128)(2,1)}, bf16[2,96,384]{2,1,0:T(8,128)(2,1)}, bf16[2,192,384]{2,1,0:T(8,128)(2,1)}, bf16[2,192,384]{2,1,0:T(8,128)(2,1)}) custom-call(s32[3]{0:T(128)} %pad_add_fusion.place, s32[4,8]{1,0:T(4,128)} %fusion.1.quads, s32[4,8]{1,0:T(4,128)} %slice_bitcast_fusion.4.thirds, bf16[2,2,384,384]{3,2,1,0:T(8,128)(2,1)} %refs_0_.3, ...), custom_call_target="tpu_custom_call" | custom-call | tf_op jit(solution)/shard_map/self_energy/pallas_call | solution.py:342
  34.6 1.3 collective-permute-start.5
  37.2 0.8 collective-permute-start.12
  38.2 1.3 collective-permute-start.14
  39.6 2.2 %collective-permute-done.5.refs_4_ = bf16[2,192,384]{2,1,0:T(8,128)(2,1)S(1)} collective-permute-done((bf16[2,192,384]{2,1,0:T(8,128)(2,1)}, bf16[2,192,384]{2,1,0:T(8,128)(2,1)S(1)}, u32[]{:S(2)}, u32[]{:S(2)}) %collective-permute-start.5) | collective-permute-done | bytes 294944 | tf_op jit(solution)/shard_map/ppermute | solution.py:47
  41.8 3.6 %collective-permute-start.11 = (bf16[384,384]{1,0:T(8,128)(2,1)S(1)}, bf16[384,384]{1,0:T(8,128)(2,1)S(1)}, u32[]{:S(2)}, u32[]{:S(2)}) collective-permute-start(bf16[384,384]{1,0:T(8,128)(2,1)S(1)} %bitcast.72), channel_id=1, source_target_pairs={{0,24},{1,25},{2,26},{3,27},{4,28},{5,29},{6,30},{7,31},{8,16},{9,... | collective-permute-start | bytes 884744 | tf_op jit(solution)/shard_map/ppermute | solution.py:47
  45.8 6.1 %collective-permute-done.14.refs_2_ = bf16[2,96,384]{2,1,0:T(8,128)(2,1)S(1)} collective-permute-done((bf16[2,96,384]{2,1,0:T(8,128)(2,1)S(1)}, bf16[2,96,384]{2,1,0:T(8,128)(2,1)S(1)}, u32[]{:S(2)}, u32[]{:S(2)}) %collective-permute-start.14) | collective-permute-done | bytes 147488 | tf_op jit(solution)/shard_map/ppermute | solution.py:47
  51.9 1.3 collective-permute-start.15
  53.2 1.3 collective-permute-start.17
  54.9 5.3 %collective-permute-done.15.refs_3_ = bf16[2,96,384]{2,1,0:T(8,128)(2,1)S(1)} collective-permute-done((bf16[2,96,384]{2,1,0:T(8,128)(2,1)S(1)}, bf16[2,96,384]{2,1,0:T(8,128)(2,1)S(1)}, u32[]{:S(2)}, u32[]{:S(2)}) %collective-permute-start.15) | collective-permute-done | bytes 147488 | tf_op jit(solution)/shard_map/ppermute | solution.py:47
  60.2 2.0 %collective-permute-done.17.refs_5_ = bf16[2,96,384]{2,1,0:T(8,128)(2,1)S(1)} collective-permute-done((bf16[2,96,384]{2,1,0:T(8,128)(2,1)S(1)}, bf16[2,96,384]{2,1,0:T(8,128)(2,1)S(1)}, u32[]{:S(2)}, u32[]{:S(2)}) %collective-permute-start.17) | collective-permute-done | bytes 147488 | tf_op jit(solution)/shard_map/ppermute | solution.py:47
  62.2 1.3 collective-permute-start.18
  63.5 1.3 collective-permute-start.20
  64.9 3.5 %collective-permute-done.18.refs_6_ = bf16[2,96,384]{2,1,0:T(8,128)(2,1)S(1)} collective-permute-done((bf16[2,96,384]{2,1,0:T(8,128)(2,1)S(1)}, bf16[2,96,384]{2,1,0:T(8,128)(2,1)S(1)}, u32[]{:S(2)}, u32[]{:S(2)}) %collective-permute-start.18) | collective-permute-done | bytes 147488 | tf_op jit(solution)/shard_map/ppermute | solution.py:47
  68.4 1.3 collective-permute-start.16
  70.3 5.7 %collective-permute-start.27 = (bf16[2,96,384]{2,1,0:T(8,128)(2,1)S(1)}, bf16[2,96,384]{2,1,0:T(8,128)(2,1)S(1)}, u32[]{:S(2)}, u32[]{:S(2)}) collective-permute-start(bf16[2,96,384]{2,1,0:T(8,128)(2,1)S(1)} %collective-permute-done.14.refs_2_), channel_id=1, source_target_pairs={{0,8},{1,9},{2,10},{3,11},{4,12},{5,13},{6,14},{7,15},{8,0},{9,1},... | collective-permute-start | bytes 442376 | tf_op jit(solution)/shard_map/ppermute | solution.py:47
  76.1 1.3 collective-permute-done.16.refs_4_
  78.1 1.3 collective-permute-start.21
  80.5 9.5 %collective-permute-done.21.refs_9_ = bf16[2,96,384]{2,1,0:T(8,128)(2,1)S(1)} collective-permute-done((bf16[2,96,384]{2,1,0:T(8,128)(2,1)S(1)}, bf16[2,96,384]{2,1,0:T(8,128)(2,1)S(1)}, u32[]{:S(2)}, u32[]{:S(2)}) %collective-permute-start.21) | collective-permute-done | bytes 147488 | tf_op jit(solution)/shard_map/ppermute | solution.py:47
  90.4 1.3 collective-permute-start.19
  91.9 1.3 collective-permute-start.23
  94.0 13.1 %collective-permute-done.19.refs_7_ = bf16[2,192,384]{2,1,0:T(8,128)(2,1)S(1)} collective-permute-done((bf16[2,192,384]{2,1,0:T(8,128)(2,1)S(1)}, bf16[2,192,384]{2,1,0:T(8,128)(2,1)S(1)}, u32[]{:S(2)}, u32[]{:S(2)}) %collective-permute-start.19) | collective-permute-done | bytes 294944 | tf_op jit(solution)/shard_map/ppermute | solution.py:47
  107.1 0.9 collective-permute-start.26
  108.2 1.5 collective-permute-start.22
  110.8 7.9 %collective-permute-done.22.refs_10_ = bf16[2,192,384]{2,1,0:T(8,128)(2,1)S(1)} collective-permute-done((bf16[2,192,384]{2,1,0:T(8,128)(2,1)S(1)}, bf16[2,192,384]{2,1,0:T(8,128)(2,1)S(1)}, u32[]{:S(2)}, u32[]{:S(2)}) %collective-permute-start.22) | collective-permute-done | bytes 294944 | tf_op jit(solution)/shard_map/ppermute | solution.py:47
  119.5 1.2 pad_maximum_fusion.1.right
  120.7 1.7 %pad_maximum_fusion.diag = bf16[4,384,768]{2,1,0:T(8,128)(2,1)} fusion(bf16[1,384,768]{2,1,0:T(8,128)(2,1)S(1)} %bitcast.65, bf16[1,384,768]{2,1,0:T(8,128)(2,1)S(1)} %get-tuple-element.128, bf16[1,384,768]{2,1,0:T(8,128)(2,1)S(1)} %bitcast.66, bf16[1,384,768]{2,1,0:T(8,128)(2,1)S(1)} %get-tuple-element.124), kind=kLoop, calls=%fused_computation | loop fusion | flops 3538944 | bytes 4718592 | tf_op jit(solution)/shard_map/stack | solution.py:391
  123.6 0.8 copy-done.15
  124.4 8.3 %substitution.1 = (bf16[384,384]{1,0:T(8,128)(2,1)}, bf16[384,384]{1,0:T(8,128)(2,1)}, bf16[384,384]{1,0:T(8,128)(2,1)}, bf16[384,384]{1,0:T(8,128)(2,1)}) custom-call(s32[3]{0:T(128)} %pad_add_fusion.place, bf16[4,384,768]{2,1,0:T(8,128)(2,1)} %pad_maximum_fusion.diag, bf16[4,384,384]{2,1,0:T(8,128)(2,1)} %pad_maximum_fusion.1.right, ...), custom_call_target="tpu_custom_call" | custom-call | tf_op jit(solution)/shard_map/substitution/pallas_call | solution.py:463
  132.8 1.3 collective-permute-start.38
  134.3 1.7 %collective-permute-start.40 = (bf16[384,384]{1,0:T(8,128)(2,1)}, bf16[384,384]{1,0:T(8,128)(2,1)S(1)}, u32[]{:S(2)}, u32[]{:S(2)}) collective-permute-start(bf16[384,384]{1,0:T(8,128)(2,1)} %get-tuple-element.99), channel_id=1, source_target_pairs={{0,16},{1,17},{2,18},{3,19},{4,20},{5,21},{6,22},{7,23},{8,24},{9,... | collective-permute-start | bytes 884744 | tf_op jit(solution)/shard_map/ppermute | solution.py:47
  136.2 5.3 %collective-permute-done.38.refs_5_ = bf16[2,192,384]{2,1,0:T(8,128)(2,1)S(1)} collective-permute-done((bf16[2,192,384]{2,1,0:T(8,128)(2,1)S(1)}, bf16[2,192,384]{2,1,0:T(8,128)(2,1)S(1)}, u32[]{:S(2)}, u32[]{:S(2)}) %collective-permute-start.38) | collective-permute-done | bytes 294944 | tf_op jit(solution)/shard_map/ppermute | solution.py:47
  142.2 3.1 %place_sigma.1 = bf16[2,2,384,384]{3,2,1,0:T(8,128)(2,1)} custom-call(s32[3]{0:T(128)} %pad_add_fusion.place, bf16[2,96,384]{2,1,0:T(8,128)(2,1)} %get-tuple-element.78.refs_0_, bf16[2,96,384]{2,1,0:T(8,128)(2,1)} %get-tuple-element.63.refs_1_, bf16[2,96,384]{2,1,0:T(8,128)(2,1)} %get-tuple-element.68.refs_2_, ...), custom_call_target="tpu_custom_call" | custom-call | tf_op jit(solution)/shard_map/place_sigma/pallas_call | solution.py:480
  145.3 4.5 %collective-permute-done.41 = bf16[384,384]{1,0:T(8,128)(2,1)S(1)} collective-permute-done((bf16[384,384]{1,0:T(8,128)(2,1)}, bf16[384,384]{1,0:T(8,128)(2,1)S(1)}, u32[]{:S(2)}, u32[]{:S(2)}) %collective-permute-start.41) | collective-permute-done | bytes 294944 | tf_op jit(solution)/shard_map/ppermute | solution.py:47
  151.1 2.8 %copy.23 = bf16[2,384,2,384]{3,2,1,0:T(2,128)(2,1)} copy(bf16[2,384,2,384]{1,3,2,0:T(8,128)(2,1)S(1)} %bitcast.62) | data formatting | bytes 2359296
  (156 shorter events, 15.5 us)
Async XLA Ops:
  2.7 9.6 %collective-permute-start.1 = (bf16[2,2,96,384]{3,2,1,0:T(8,128)(2,1)}, bf16[2,2,96,384]{3,2,1,0:T(8,128)(2,1)}, u32[]{:S(2)}, u32[]{:S(2)}) collective-permute-start(bf16[2,2,96,384]{3,2,1,0:T(8,128)(2,1)} %get-tuple-element.117), channel_id=1, source_target_pairs={{0,1},{1,0},{2,3},{3,2},{4,5},{5,4},{6,7},{7,6},{8,9},{9,8},{10,11... | collective-permute-start | bytes 884744 | tf_op jit(solution)/shard_map/ppermute | solution.py:47
  5.7 15.0 %collective-permute-start.2 = (bf16[2,2,96,384]{3,2,1,0:T(8,128)(2,1)}, bf16[2,2,96,384]{3,2,1,0:T(8,128)(2,1)}, u32[]{:S(2)}, u32[]{:S(2)}) collective-permute-start(bf16[2,2,96,384]{3,2,1,0:T(8,128)(2,1)} %get-tuple-element.115), channel_id=1, source_target_pairs={{0,1},{1,0},{2,3},{3,2},{4,5},{5,4},{6,7},{7,6},{8,9},{9,8},{10,11... | collective-permute-start | bytes 884744 | tf_op jit(solution)/shard_map/ppermute | solution.py:47
  6.8 13.8 %collective-permute-start = (bf16[2,384,384]{2,1,0:T(8,128)(2,1)}, bf16[2,384,384]{2,1,0:T(8,128)(2,1)S(1)}, u32[]{:S(2)}, u32[]{:S(2)}) collective-permute-start(bf16[2,384,384]{2,1,0:T(8,128)(2,1)} %dynamic-slice_bitcast_fusion), channel_id=1, source_target_pairs={{0,16},{1,17},{2,18},{3,19},{4,20},{5,21},{6,22},{7,23},{8,24},{9,... | collective-permute-start | bytes 1769480 | tf_op jit(solution)/shard_map/ppermute | solution.py:47
  12.3 12.9 %collective-permute-start.3 = (bf16[2,2,96,384]{3,2,1,0:T(8,128)(2,1)}, bf16[2,2,96,384]{3,2,1,0:T(8,128)(2,1)S(1)}, u32[]{:S(2)}, u32[]{:S(2)}) collective-permute-start(bf16[2,2,96,384]{3,2,1,0:T(8,128)(2,1)} %get-tuple-element.64), channel_id=1, source_target_pairs={{0,1},{1,0},{2,3},{3,2},{4,5},{5,4},{6,7},{7,6},{8,9},{9,8},{10,11... | collective-permute-start | bytes 884744 | tf_op jit(solution)/shard_map/ppermute | solution.py:47
  13.5 16.3 %collective-permute-start.4 = (bf16[2,2,96,384]{3,2,1,0:T(8,128)(2,1)}, bf16[2,2,96,384]{3,2,1,0:T(8,128)(2,1)}, u32[]{:S(2)}, u32[]{:S(2)}) collective-permute-start(bf16[2,2,96,384]{3,2,1,0:T(8,128)(2,1)} %get-tuple-element.65), channel_id=1, source_target_pairs={{0,1},{1,0},{2,3},{3,2},{4,5},{5,4},{6,7},{7,6},{8,9},{9,8},{10,11... | collective-permute-start | bytes 884744 | tf_op jit(solution)/shard_map/ppermute | solution.py:47
  34.6 7.2 %collective-permute-start.5 = (bf16[2,192,384]{2,1,0:T(8,128)(2,1)}, bf16[2,192,384]{2,1,0:T(8,128)(2,1)S(1)}, u32[]{:S(2)}, u32[]{:S(2)}) collective-permute-start(bf16[2,192,384]{2,1,0:T(8,128)(2,1)} %get-tuple-element.70), channel_id=1, source_target_pairs={{0,1},{1,0},{2,3},{3,2},{4,5},{5,4},{6,7},{7,6},{8,9},{9,8},{10,11... | collective-permute-start | bytes 884744 | tf_op jit(solution)/shard_map/ppermute | solution.py:47
  35.9 5.9 %collective-permute-start.6 = (bf16[2,192,384]{2,1,0:T(8,128)(2,1)}, bf16[2,192,384]{2,1,0:T(8,128)(2,1)S(1)}, u32[]{:S(2)}, u32[]{:S(2)}) collective-permute-start(bf16[2,192,384]{2,1,0:T(8,128)(2,1)} %get-tuple-element.101), channel_id=1, source_target_pairs={{8,25},{9,24},{16,1},{17,0},{18,3},{19,2},{24,9},{25,8},{26,11},{2... | collective-permute-start | bytes 884744 | tf_op jit(solution)/shard_map/ppermute | solution.py:47
  36.6 3.0 %collective-permute-start.13 = (bf16[2,96,384]{2,1,0:T(8,128)(2,1)}, bf16[2,96,384]{2,1,0:T(8,128)(2,1)S(1)}, u32[]{:S(2)}, u32[]{:S(2)}) collective-permute-start(bf16[2,96,384]{2,1,0:T(8,128)(2,1)} %get-tuple-element.69.refs_3_), channel_id=1, source_target_pairs={{8,24},{9,25},{16,0},{17,1},{18,2},{19,3},{24,8},{25,9},{26,10},{2... | collective-permute-start | bytes 442376 | tf_op jit(solution)/shard_map/ppermute | solution.py:47
  37.2 0.9 collective-permute-start.12
  38.2 13.7 %collective-permute-start.14 = (bf16[2,96,384]{2,1,0:T(8,128)(2,1)S(1)}, bf16[2,96,384]{2,1,0:T(8,128)(2,1)S(1)}, u32[]{:S(2)}, u32[]{:S(2)}) collective-permute-start(bf16[2,96,384]{2,1,0:T(8,128)(2,1)S(1)} %get-tuple-element.132), channel_id=1, source_target_pairs={{0,2},{1,3},{2,4},{3,5},{8,10},{9,11},{10,12},{11,13},{12,14},{13,... | collective-permute-start | bytes 442376 | tf_op jit(solution)/shard_map/ppermute | solution.py:47
  41.8 36.2 %collective-permute-start.11 = (bf16[384,384]{1,0:T(8,128)(2,1)S(1)}, bf16[384,384]{1,0:T(8,128)(2,1)S(1)}, u32[]{:S(2)}, u32[]{:S(2)}) collective-permute-start(bf16[384,384]{1,0:T(8,128)(2,1)S(1)} %bitcast.72), channel_id=1, source_target_pairs={{0,24},{1,25},{2,26},{3,27},{4,28},{5,29},{6,30},{7,31},{8,16},{9,... | collective-permute-start | bytes 884744 | tf_op jit(solution)/shard_map/ppermute | solution.py:47
  45.4 32.7 %collective-permute-start.10 = (bf16[384,384]{1,0:T(8,128)(2,1)S(1)}, bf16[384,384]{1,0:T(8,128)(2,1)S(1)}, u32[]{:S(2)}, u32[]{:S(2)}) collective-permute-start(bf16[384,384]{1,0:T(8,128)(2,1)S(1)} %bitcast.71), channel_id=1, source_target_pairs={{0,16},{1,17},{2,18},{3,19},{4,20},{5,21},{6,22},{7,23},{8,24},{9,... | collective-permute-start | bytes 884744 | tf_op jit(solution)/shard_map/ppermute | solution.py:47
  45.6 33.7 %collective-permute-start.9 = (bf16[384,384]{1,0:T(8,128)(2,1)S(1)}, bf16[384,384]{1,0:T(8,128)(2,1)S(1)}, u32[]{:S(2)}, u32[]{:S(2)}) collective-permute-start(bf16[384,384]{1,0:T(8,128)(2,1)S(1)} %bitcast.70), channel_id=1, source_target_pairs={{0,8},{1,9},{2,10},{3,11},{4,12},{5,13},{6,14},{7,15},{8,0},{9,1},... | collective-permute-start | bytes 884744 | tf_op jit(solution)/shard_map/ppermute | solution.py:47
  51.9 8.3 %collective-permute-start.15 = (bf16[2,96,384]{2,1,0:T(8,128)(2,1)S(1)}, bf16[2,96,384]{2,1,0:T(8,128)(2,1)S(1)}, u32[]{:S(2)}, u32[]{:S(2)}) collective-permute-start(bf16[2,96,384]{2,1,0:T(8,128)(2,1)S(1)} %get-tuple-element.80), channel_id=1, source_target_pairs={{0,2},{1,3},{2,4},{3,5},{8,10},{9,11},{10,12},{11,13},{12,14},{13,... | collective-permute-start | bytes 442376 | tf_op jit(solution)/shard_map/ppermute | solution.py:47
  53.2 8.9 %collective-permute-start.17 = (bf16[2,96,384]{2,1,0:T(8,128)(2,1)S(1)}, bf16[2,96,384]{2,1,0:T(8,128)(2,1)S(1)}, u32[]{:S(2)}, u32[]{:S(2)}) collective-permute-start(bf16[2,96,384]{2,1,0:T(8,128)(2,1)S(1)} %broadcast_select_fusion.9), channel_id=1, source_target_pairs={{2,4},{3,5},{4,6},{5,7},{8,10},{9,11},{10,12},{11,13},{12,14},{13,... | collective-permute-start | bytes 442376 | tf_op jit(solution)/shard_map/ppermute | solution.py:47
  54.8 52.3 %copy-start.1 = (bf16[2,384,384]{2,1,0:T(8,128)(2,1)}, bf16[2,384,384]{2,1,0:T(8,128)(2,1)S(1)}, u32[]{:S(2)}) copy-start(bf16[2,384,384]{2,1,0:T(8,128)(2,1)S(1)} %pad_maximum_fusion.6.refs_1_) | copy-start | bytes 1769476
  54.9 39.0 %copy-start.2 = (bf16[2,384,384]{2,1,0:T(8,128)(2,1)}, bf16[2,384,384]{2,1,0:T(8,128)(2,1)S(1)}, u32[]{:S(2)}) copy-start(bf16[2,384,384]{2,1,0:T(8,128)(2,1)S(1)} %pad_maximum_fusion.5.refs_0_) | copy-start | bytes 1769476
  62.2 6.2 %collective-permute-start.18 = (bf16[2,96,384]{2,1,0:T(8,128)(2,1)S(1)}, bf16[2,96,384]{2,1,0:T(8,128)(2,1)S(1)}, u32[]{:S(2)}, u32[]{:S(2)}) collective-permute-start(bf16[2,96,384]{2,1,0:T(8,128)(2,1)S(1)} %broadcast_select_fusion.8), channel_id=1, source_target_pairs={{2,4},{3,5},{4,6},{5,7},{8,10},{9,11},{10,12},{11,13},{12,14},{13,... | collective-permute-start | bytes 442376 | tf_op jit(solution)/shard_map/ppermute | solution.py:47
  63.5 6.8 %collective-permute-start.20 = (bf16[2,96,384]{2,1,0:T(8,128)(2,1)S(1)}, bf16[2,96,384]{2,1,0:T(8,128)(2,1)S(1)}, u32[]{:S(2)}, u32[]{:S(2)}) collective-permute-start(bf16[2,96,384]{2,1,0:T(8,128)(2,1)S(1)} %broadcast_select_fusion.7), channel_id=1, source_target_pairs={{4,6},{5,7},{8,12},{9,13},{12,14},{13,15},{20,22},{21,23},{24,28},... | collective-permute-start | bytes 442376 | tf_op jit(solution)/shard_map/ppermute | solution.py:47
  68.4 9.0 %collective-permute-start.16 = (bf16[2,192,384]{2,1,0:T(8,128)(2,1)S(1)}, bf16[2,192,384]{2,1,0:T(8,128)(2,1)S(1)}, u32[]{:S(2)}, u32[]{:S(2)}) collective-permute-start(bf16[2,192,384]{2,1,0:T(8,128)(2,1)S(1)} %get-tuple-element.81), channel_id=1, source_target_pairs={{0,2},{1,3},{2,4},{3,5},{8,10},{9,11},{10,12},{11,13},{12,14},{13,... | collective-permute-start | bytes 884744 | tf_op jit(solution)/shard_map/ppermute | solution.py:47
  70.3 7.0 %collective-permute-start.27 = (bf16[2,96,384]{2,1,0:T(8,128)(2,1)S(1)}, bf16[2,96,384]{2,1,0:T(8,128)(2,1)S(1)}, u32[]{:S(2)}, u32[]{:S(2)}) collective-permute-start(bf16[2,96,384]{2,1,0:T(8,128)(2,1)S(1)} %collective-permute-done.14.refs_2_), channel_id=1, source_target_pairs={{0,8},{1,9},{2,10},{3,11},{4,12},{5,13},{6,14},{7,15},{8,0},{9,1},... | collective-permute-start | bytes 442376 | tf_op jit(solution)/shard_map/ppermute | solution.py:47
  77.4 32.9 %copy-start.3 = (bf16[2,192,384]{2,1,0:T(8,128)(2,1)}, bf16[2,192,384]{2,1,0:T(8,128)(2,1)S(1)}, u32[]{:S(2)}) copy-start(bf16[2,192,384]{2,1,0:T(8,128)(2,1)S(1)} %collective-permute-done.16.refs_4_) | copy-start | bytes 884740
  77.4 16.5 %collective-permute-start.8 = (bf16[384,768]{1,0:T(8,128)(2,1)S(1)}, bf16[384,768]{1,0:T(8,128)(2,1)S(1)}, u32[]{:S(2)}, u32[]{:S(2)}) collective-permute-start(bf16[384,768]{1,0:T(8,128)(2,1)S(1)} %get-tuple-element.129), channel_id=1, source_target_pairs={{0,8},{1,9},{2,10},{3,11},{4,12},{5,13},{6,14},{7,15},{8,0},{9,1},... | collective-permute-start | bytes 1769480 | tf_op jit(solution)/shard_map/ppermute | solution.py:47
  77.4 2.5 %collective-permute-start.28 = (bf16[2,96,384]{2,1,0:T(8,128)(2,1)S(1)}, bf16[2,96,384]{2,1,0:T(8,128)(2,1)S(1)}, u32[]{:S(2)}, u32[]{:S(2)}) collective-permute-start(bf16[2,96,384]{2,1,0:T(8,128)(2,1)S(1)} %collective-permute-done.15.refs_3_), channel_id=1, source_target_pairs={{0,8},{1,9},{2,10},{3,11},{4,12},{5,13},{6,14},{7,15},{8,0},{9,1},... | collective-permute-start | bytes 442376 | tf_op jit(solution)/shard_map/ppermute | solution.py:47
  78.0 2.1 %collective-permute-start.30 = (bf16[2,96,384]{2,1,0:T(8,128)(2,1)S(1)}, bf16[2,96,384]{2,1,0:T(8,128)(2,1)S(1)}, u32[]{:S(2)}, u32[]{:S(2)}) collective-permute-start(bf16[2,96,384]{2,1,0:T(8,128)(2,1)S(1)} %collective-permute-done.17.refs_5_), channel_id=1, source_target_pairs={{0,8},{1,9},{2,10},{3,11},{4,12},{5,13},{6,14},{7,15},{8,0},{9,1},... | collective-permute-start | bytes 442376 | tf_op jit(solution)/shard_map/ppermute | solution.py:47
  78.1 12.0 %collective-permute-start.21 = (bf16[2,96,384]{2,1,0:T(8,128)(2,1)S(1)}, bf16[2,96,384]{2,1,0:T(8,128)(2,1)S(1)}, u32[]{:S(2)}, u32[]{:S(2)}) collective-permute-start(bf16[2,96,384]{2,1,0:T(8,128)(2,1)S(1)} %broadcast_select_fusion.6), channel_id=1, source_target_pairs={{4,6},{5,7},{8,12},{9,13},{12,14},{13,15},{20,22},{21,23},{24,28},... | collective-permute-start | bytes 442376 | tf_op jit(solution)/shard_map/ppermute | solution.py:47
  79.4 11.1 %collective-permute-start.31 = (bf16[2,96,384]{2,1,0:T(8,128)(2,1)S(1)}, bf16[2,96,384]{2,1,0:T(8,128)(2,1)S(1)}, u32[]{:S(2)}, u32[]{:S(2)}) collective-permute-start(bf16[2,96,384]{2,1,0:T(8,128)(2,1)S(1)} %collective-permute-done.18.refs_6_), channel_id=1, source_target_pairs={{0,8},{1,9},{2,10},{3,11},{4,12},{5,13},{6,14},{7,15},{8,0},{9,1},... | collective-permute-start | bytes 442376 | tf_op jit(solution)/shard_map/ppermute | solution.py:47
  79.9 28.2 %copy-start.32 = (bf16[2,96,384]{2,1,0:T(8,128)(2,1)}, bf16[2,96,384]{2,1,0:T(8,128)(2,1)S(1)}, u32[]{:S(2)}) copy-start(bf16[2,96,384]{2,1,0:T(8,128)(2,1)S(1)} %collective-permute-done.28.refs_16_) | copy-start | bytes 442372
  79.9 28.2 %collective-permute-start.7 = (bf16[384,768]{1,0:T(8,128)(2,1)S(1)}, bf16[384,768]{1,0:T(8,128)(2,1)S(1)}, u32[]{:S(2)}, u32[]{:S(2)}) collective-permute-start(bf16[384,768]{1,0:T(8,128)(2,1)S(1)} %get-tuple-element.125), channel_id=1, source_target_pairs={{0,8},{1,9},{2,10},{3,11},{4,12},{5,13},{6,14},{7,15},{8,0},{9,1},... | collective-permute-start | bytes 1769480 | tf_op jit(solution)/shard_map/ppermute | solution.py:47
  80.1 28.0 %copy-start.33 = (bf16[2,96,384]{2,1,0:T(8,128)(2,1)}, bf16[2,96,384]{2,1,0:T(8,128)(2,1)S(1)}, u32[]{:S(2)}) copy-start(bf16[2,96,384]{2,1,0:T(8,128)(2,1)S(1)} %collective-permute-done.30.refs_18_) | copy-start | bytes 442372
  80.1 11.8 %collective-permute-start.33 = (bf16[2,96,384]{2,1,0:T(8,128)(2,1)S(1)}, bf16[2,96,384]{2,1,0:T(8,128)(2,1)S(1)}, u32[]{:S(2)}, u32[]{:S(2)}) collective-permute-start(bf16[2,96,384]{2,1,0:T(8,128)(2,1)S(1)} %collective-permute-done.20.refs_8_), channel_id=1, source_target_pairs={{0,8},{1,9},{2,10},{3,11},{4,12},{5,13},{6,14},{7,15},{8,0},{9,1},... | collective-permute-start | bytes 442376 | tf_op jit(solution)/shard_map/ppermute | solution.py:47
  90.0 3.1 %collective-permute-start.34 = (bf16[2,96,384]{2,1,0:T(8,128)(2,1)S(1)}, bf16[2,96,384]{2,1,0:T(8,128)(2,1)}, u32[]{:S(2)}, u32[]{:S(2)}) collective-permute-start(bf16[2,96,384]{2,1,0:T(8,128)(2,1)S(1)} %collective-permute-done.21.refs_9_), channel_id=1, source_target_pairs={{0,8},{1,9},{2,10},{3,11},{4,12},{5,13},{6,14},{7,15},{8,0},{9,1},... | collective-permute-start | bytes 442376 | tf_op jit(solution)/shard_map/ppermute | solution.py:47
  90.4 16.7 %collective-permute-start.19 = (bf16[2,192,384]{2,1,0:T(8,128)(2,1)S(1)}, bf16[2,192,384]{2,1,0:T(8,128)(2,1)S(1)}, u32[]{:S(2)}, u32[]{:S(2)}) collective-permute-start(bf16[2,192,384]{2,1,0:T(8,128)(2,1)S(1)} %broadcast_select_fusion.3), channel_id=1, source_target_pairs={{2,4},{3,5},{4,6},{5,7},{8,10},{9,11},{10,12},{11,13},{12,14},{13,... | collective-permute-start | bytes 884744 | tf_op jit(solution)/shard_map/ppermute | solution.py:47
  91.8 28.8 %copy-start.36 = (bf16[2,96,384]{2,1,0:T(8,128)(2,1)}, bf16[2,96,384]{2,1,0:T(8,128)(2,1)S(1)}, u32[]{:S(2)}) copy-start(bf16[2,96,384]{2,1,0:T(8,128)(2,1)S(1)} %collective-permute-done.33.refs_21_) | copy-start | bytes 442372
  91.9 17.8 %collective-permute-start.23 = (bf16[2,384,384]{2,1,0:T(8,128)(2,1)S(1)}, bf16[2,384,384]{2,1,0:T(8,128)(2,1)S(1)}, u32[]{:S(2)}, u32[]{:S(2)}) collective-permute-start(bf16[2,384,384]{2,1,0:T(8,128)(2,1)S(1)} %select_select_fusion), channel_id=1, source_target_pairs={{2,0},{3,1},{8,14},{9,15},{10,8},{11,9},{12,10},{13,11},{18,16},{1... | collective-permute-start | bytes 1769480 | tf_op jit(solution)/shard_map/ppermute | solution.py:47
  93.2 16.6 %collective-permute-start.24 = (bf16[2,384,384]{2,1,0:T(8,128)(2,1)S(1)}, bf16[2,384,384]{2,1,0:T(8,128)(2,1)S(1)}, u32[]{:S(2)}, u32[]{:S(2)}) collective-permute-start(bf16[2,384,384]{2,1,0:T(8,128)(2,1)S(1)} %pad_maximum_fusion.6.refs_1_), channel_id=1, source_target_pairs={{12,8},{13,9},{28,24},{29,25}} | collective-permute-start | bytes 1769480 | tf_op jit(solution)/shard_map/ppermute | solution.py:47
  93.9 16.3 %collective-permute-start.25 = (bf16[2,384,384]{2,1,0:T(8,128)(2,1)S(1)}, bf16[2,384,384]{2,1,0:T(8,128)(2,1)S(1)}, u32[]{:S(2)}, u32[]{:S(2)}) collective-permute-start(bf16[2,384,384]{2,1,0:T(8,128)(2,1)S(1)} %pad_maximum_fusion.5.refs_0_), channel_id=1, source_target_pairs={{0,8},{1,9},{2,10},{3,11},{4,12},{5,13},{6,14},{7,15},{8,0},{9,1},... | collective-permute-start | bytes 1769480 | tf_op jit(solution)/shard_map/ppermute | solution.py:47
  107.1 3.3 %collective-permute-start.26 = (bf16[2,384,384]{2,1,0:T(8,128)(2,1)S(1)}, bf16[2,384,384]{2,1,0:T(8,128)(2,1)S(1)}, u32[]{:S(2)}, u32[]{:S(2)}) collective-permute-start(bf16[2,384,384]{2,1,0:T(8,128)(2,1)S(1)} %pad_maximum_fusion.6.refs_1_), channel_id=1, source_target_pairs={{0,8},{1,9},{2,10},{3,11},{4,12},{5,13},{6,14},{7,15},{8,0},{9,1},... | collective-permute-start | bytes 1769480 | tf_op jit(solution)/shard_map/ppermute | solution.py:47
  108.2 10.5 %collective-permute-start.22 = (bf16[2,192,384]{2,1,0:T(8,128)(2,1)S(1)}, bf16[2,192,384]{2,1,0:T(8,128)(2,1)S(1)}, u32[]{:S(2)}, u32[]{:S(2)}) collective-permute-start(bf16[2,192,384]{2,1,0:T(8,128)(2,1)S(1)} %broadcast_select_fusion.2), channel_id=1, source_target_pairs={{4,6},{5,7},{8,12},{9,13},{12,14},{13,15},{20,22},{21,23},{24,28},... | collective-permute-start | bytes 884744 | tf_op jit(solution)/shard_map/ppermute | solution.py:47
  109.7 12.8 %collective-permute-start.36 = (bf16[2,384,384]{2,1,0:T(8,128)(2,1)S(1)}, bf16[2,384,384]{2,1,0:T(8,128)(2,1)S(1)}, u32[]{:S(2)}, u32[]{:S(2)}) collective-permute-start(bf16[2,384,384]{2,1,0:T(8,128)(2,1)S(1)} %collective-permute-done.23.refs_11_), channel_id=1, source_target_pairs={{0,8},{1,9},{2,10},{3,11},{4,12},{5,13},{6,14},{7,15},{8,0},{9,1},... | collective-permute-start | bytes 1769480 | tf_op jit(solution)/shard_map/ppermute | solution.py:47
  109.8 12.7 %collective-permute-start.37 = (bf16[2,384,384]{2,1,0:T(8,128)(2,1)S(1)}, bf16[2,384,384]{2,1,0:T(8,128)(2,1)S(1)}, u32[]{:S(2)}, u32[]{:S(2)}) collective-permute-start(bf16[2,384,384]{2,1,0:T(8,128)(2,1)S(1)} %collective-permute-done.24.refs_12_), channel_id=1, source_target_pairs={{0,8},{1,9},{2,10},{3,11},{4,12},{5,13},{6,14},{7,15},{8,0},{9,1},... | collective-permute-start | bytes 1769480 | tf_op jit(solution)/shard_map/ppermute | solution.py:47
  110.3 12.2 %collective-permute-start.29 = (bf16[2,192,384]{2,1,0:T(8,128)(2,1)S(1)}, bf16[2,192,384]{2,1,0:T(8,128)(2,1)S(1)}, u32[]{:S(2)}, u32[]{:S(2)}) collective-permute-start(bf16[2,192,384]{2,1,0:T(8,128)(2,1)S(1)} %collective-permute-done.16.refs_4_), channel_id=1, source_target_pairs={{0,8},{1,9},{2,10},{3,11},{4,12},{5,13},{6,14},{7,15},{8,0},{9,1},... | collective-permute-start | bytes 884744 | tf_op jit(solution)/shard_map/ppermute | solution.py:47
  110.4 12.0 %collective-permute-start.32 = (bf16[2,192,384]{2,1,0:T(8,128)(2,1)S(1)}, bf16[2,192,384]{2,1,0:T(8,128)(2,1)S(1)}, u32[]{:S(2)}, u32[]{:S(2)}) collective-permute-start(bf16[2,192,384]{2,1,0:T(8,128)(2,1)S(1)} %collective-permute-done.19.refs_7_), channel_id=1, source_target_pairs={{0,8},{1,9},{2,10},{3,11},{4,12},{5,13},{6,14},{7,15},{8,0},{9,1},... | collective-permute-start | bytes 884744 | tf_op jit(solution)/shard_map/ppermute | solution.py:47
  118.7 3.8 %collective-permute-start.35 = (bf16[2,192,384]{2,1,0:T(8,128)(2,1)S(1)}, bf16[2,192,384]{2,1,0:T(8,128)(2,1)S(1)}, u32[]{:S(2)}, u32[]{:S(2)}) collective-permute-start(bf16[2,192,384]{2,1,0:T(8,128)(2,1)S(1)} %collective-permute-done.22.refs_10_), channel_id=1, source_target_pairs={{0,8},{1,9},{2,10},{3,11},{4,12},{5,13},{6,14},{7,15},{8,0},{9,1},... | collective-permute-start | bytes 884744 | tf_op jit(solution)/shard_map/ppermute | solution.py:47
  132.8 8.7 %collective-permute-start.38 = (bf16[2,192,384]{2,1,0:T(8,128)(2,1)S(1)}, bf16[2,192,384]{2,1,0:T(8,128)(2,1)S(1)}, u32[]{:S(2)}, u32[]{:S(2)}) collective-permute-start(bf16[2,192,384]{2,1,0:T(8,128)(2,1)S(1)} %copy-done.38), channel_id=1, source_target_pairs={{0,1},{1,0},{2,3},{3,2},{4,5},{5,4},{6,7},{7,6},{8,9},{9,8},{10,11... | collective-permute-start | bytes 884744 | tf_op jit(solution)/shard_map/ppermute | solution.py:47
  134.1 11.3 %collective-permute-start.39 = (bf16[384,384]{1,0:T(8,128)(2,1)}, bf16[384,384]{1,0:T(8,128)(2,1)S(1)}, u32[]{:S(2)}, u32[]{:S(2)}) collective-permute-start(bf16[384,384]{1,0:T(8,128)(2,1)} %get-tuple-element.98), channel_id=1, source_target_pairs={{0,8},{1,9},{2,10},{3,11},{4,12},{5,13},{6,14},{7,15},{8,0},{9,1},... | collective-permute-start | bytes 884744 | tf_op jit(solution)/shard_map/ppermute | solution.py:47
  134.3 11.0 %collective-permute-start.40 = (bf16[384,384]{1,0:T(8,128)(2,1)}, bf16[384,384]{1,0:T(8,128)(2,1)S(1)}, u32[]{:S(2)}, u32[]{:S(2)}) collective-permute-start(bf16[384,384]{1,0:T(8,128)(2,1)} %get-tuple-element.99), channel_id=1, source_target_pairs={{0,16},{1,17},{2,18},{3,19},{4,20},{5,21},{6,22},{7,23},{8,24},{9,... | collective-permute-start | bytes 884744 | tf_op jit(solution)/shard_map/ppermute | solution.py:47
  136.0 13.8 %collective-permute-start.41 = (bf16[384,384]{1,0:T(8,128)(2,1)}, bf16[384,384]{1,0:T(8,128)(2,1)S(1)}, u32[]{:S(2)}, u32[]{:S(2)}) collective-permute-start(bf16[384,384]{1,0:T(8,128)(2,1)} %get-tuple-element.100), channel_id=1, source_target_pairs={{0,24},{1,25},{2,26},{3,27},{4,28},{5,29},{6,30},{7,31},{8,16},{9,... | collective-permute-start | bytes 884744 | tf_op jit(solution)/shard_map/ppermute | solution.py:47
  (33 other events, 275.0 us)

commit v10 on v9

--- a/solution.py
+++ b/solution.py
@@ -25,8 +25,7 @@
         self.width = side // self.groups
         self.subs = 2 if self.half % 32 == 0 else 1
         self.sub = self.half // self.subs
-        self.chunks = [(0, u * self.sub, self.sub) for u in range(self.subs)]
-        self.chunks += [(q, 0, self.half) for q in range(1, self.moms)]
+        self.chunks = [(q, 0, self.half) for q in range(self.moms)]
         self.starts = [0]
         for _, _, height in self.chunks:
             self.starts.append(self.starts[-1] + height)
@@ -110,7 +109,7 @@
     refs = list(refs)
     take = lambda number: [refs.pop(0) for _ in range(number)]
     lesser_in, partner_in = take(moms), take(moms)
-    before, outs = take(count - moments if u else 0), take(count)
+    before, outs = take(count if u else 0), take(count)
     lesser, partner, pairs, third, held, in_sems, out_sems, before_sems = refs
     x, y = place[0] // groups, place[2]
     height = sub // chunks
@@ -132,7 +131,7 @@
                 copies[chunk].append(copy)
     earlier = [
         pltpu.make_async_copy(
-            before[n], held.at[moments + n, :, pl.ds(0, u * sub), :], before_sems.at[n]
+            before[n], held.at[n, :, pl.ds(0, u * sub), :], before_sems.at[n]
         )
         for n in range(len(before))
     ]
@@ -166,7 +165,7 @@
                     n += 1
             for q, b in order:
                 moment = (y ^ q) * moments + (x ^ b)
-                to = rows if q == 0 else pl.ds(pl.multiple_of(u * sub + row, 16), 16)
+                to = pl.ds(pl.multiple_of(u * sub + row, 16), 16)
                 for lane in range(0, side, lanes):
                     cols = pl.ds(lane, lanes)
                     total_re = total_im = None
@@ -184,8 +183,7 @@
 
         lax.fori_loop(0, height // 16, block, 0)
         for index in range(count):
-            offset = chunk * height + (u * sub if index >= moments else 0)
-            rows = pl.ds(offset, height)
+            rows = pl.ds(u * sub + chunk * height, height)
             copy = pltpu.make_async_copy(
                 held.at[index, :, rows, :], outs[index].at[:, rows, :], out_sems.at[chunk * count + index]
             )
@@ -196,7 +194,7 @@
     for n in range(len(before)):
         rows = pl.ds(0, u * sub)
         copy = pltpu.make_async_copy(
-            held.at[moments + n, :, rows, :], outs[moments + n].at[:, rows, :], before_sems.at[n]
+            held.at[n, :, rows, :], outs[n].at[:, rows, :], before_sems.at[n]
         )
         copy.start()
         sent.append(copy)
@@ -216,11 +214,12 @@
     run_copies(copies)
 
 
-def solve_kernel(plan, sources, place, diag, right, *refs):
+def solve_kernel(plan, sources, place, *refs):
     rows, moms, groups, side = plan.rows, plan.moms, plan.groups, plan.side
     moments, half, width, keys = plan.moments, plan.half, plan.width, plan.keys
     top = moments - 1
-    sig_in, outs = refs[: -rows - 4], refs[-rows - 4 : -4]
+    diag, right = refs[:rows], refs[rows : 2 * rows]
+    sig_in, outs = refs[2 * rows : -rows - 4], refs[-rows - 4 : -4]
     sig, solved, sems, out_sems = refs[-4:]
     r, y = place[0], place[2]
     g = r % groups
@@ -244,6 +243,12 @@
 
     weight = 1.0 / math.sqrt(side * rows)
 
+    def pick(held, number):
+        value = held[0][...]
+        for n in range(1, len(held)):
+            value = jnp.where(number == n, held[n][...], value)
+        return value
+
     def turn(value):
         return jnp.concatenate([-value[:, width:], value[:, :width]], axis=1)
 
@@ -254,7 +259,7 @@
                     for _ in range(groups * 2):
                         tile = sig.at[0, :, pl.ds(0, side)]
                         pltpu.make_async_copy(tile, tile, sems.at[key[0]]).wait()
-        pending = right[r ^ row].astype(jnp.float32)
+        pending = pick(right, r ^ row).astype(jnp.float32)
         if row > 0:
             depth = 2 * side * row
             pending = pending + weight * jnp.dot(
@@ -262,7 +267,7 @@
             )
         both = jnp.concatenate([pending, turn(pending)], axis=0).astype(jnp.bfloat16)
         value = jnp.dot(
-            diag[(row // groups) * groups + (g ^ (row % groups))],
+            pick(diag[row // groups * groups :][:groups], g ^ (row % groups)),
             both,
             preferred_element_type=jnp.float32,
         )
@@ -334,15 +339,15 @@
     copies = 2 if plan.sub % 32 == 0 else 1
     came = []
     whole = []
-    rest_of = []
+    so_far = []
 
     def self_energy(u, *behind):
         height = (u + 1) * plan.sub
-        shapes = [(2, plan.sub, side)] * moments + [(2, height, side)] * (count - moments)
+        shapes = [(2, height, side)] * count
         return pl.pallas_call(
             functools.partial(sigma_kernel, plan, pair_count, u, copies),
             out_shape=[jax.ShapeDtypeStruct(shape, bf16) for shape in shapes],
-            in_specs=[smem()] * 3 + hbm(2 * moms + len(rest_of)),
+            in_specs=[smem()] * 3 + hbm(2 * moms + len(so_far)),
             out_specs=hbm(count),
             scratch_shapes=[
                 pltpu.VMEM((count, 2, plan.sub, side), bf16),
@@ -360,7 +365,7 @@
             *after((place, quads, thirds), behind),
             *([lesser] + lesser_came[u]),
             *([partner] + partner_came[u]),
-            *rest_of,
+            *so_far,
         )
 
     def to_row(value, b, q):
@@ -368,27 +373,23 @@
         return plan.send(value, goal)
 
     for u in range(plan.subs):
-        slots = list(self_energy(u, right_all, diag))
-        came = [after(tiles, rest_of, slots) for tiles in came]
-        rest_of = slots[moments:]
-        came.append(slots[:1] + [to_row(slots[b], b, 0) for b in range(1, moments)])
-        whole += slots[:moments]
+        so_far = list(self_energy(u, right_all, diag))
+    came.append(so_far[:1] + [to_row(so_far[b], b, 0) for b in range(1, moments)])
+    whole += so_far[:moments]
     late = []
     for q in range(1, moms):
-        mine = rest_of[(q - 1) * moments : q * moments]
+        mine = so_far[q * moments : (q + 1) * moments]
         came.append(
             [exchange_mom(mine[0], q)] + [to_row(mine[b], b, q) for b in range(1, moments)]
         )
         late += [(came[-1][0], None)] + [(mine[b], q) for b in range(1, moments)]
     right_all = after(right_all, came[-1])
     right_all = right_all[:1] + [exchange_row(right_all[s], s) for s in range(1, rows)]
-    right_came = jnp.stack(right_all)
     diag = after(by_block(diag), came[-1])
     diag = [jnp.concatenate([value[0], value[1]], axis=1) for value in diag]
     diag_all = [
         diag[b] if t == 0 else exchange_row(diag[b], t) for b in range(moments) for t in range(groups)
     ]
-    diag_came = jnp.stack(diag_all)
 
     def valid(key, a):
         return key[0] * groups + a % groups > key[1]
@@ -463,7 +464,7 @@
     solved = pl.pallas_call(
         functools.partial(solve_kernel, plan, sources),
         out_shape=[jax.ShapeDtypeStruct((side, 2 * width), bf16)] * rows,
-        in_specs=[smem()] + [pl.BlockSpec(memory_space=pltpu.VMEM)] * 2 + hbm(len(sig_all)),
+        in_specs=[smem()] + [pl.BlockSpec(memory_space=pltpu.VMEM)] * (2 * rows) + hbm(len(sig_all)),
         out_specs=hbm(rows),
         scratch_shapes=[
             pltpu.VMEM((rows, side, 2 * side * (cols - 1)), bf16),
@@ -473,7 +474,7 @@
         ],
         compiler_params=params,
         name="substitution",
-    )(place, diag_came, right_came, *sig_all)
+    )(place, *diag_all, *right_all, *sig_all)
 
     for value, q in late:
         whole.append(value if q is None else exchange_mom(after(value, solved), q))

time: 155 us -> 138 us (0.89)
  the two profiles are of different devices: /device:TPU:25 before, /device:TPU:0 now
where the time goes in v10:
time: 138 us
  starting transfers between devices  50.2 us (36%)
  waiting for transfers between devices  44.6 us (32%)
  Pallas kernels  20.1 us (15%)
  local copies, waits for them, and re-layouts  18.9 us (14%)
  other arithmetic  2.39 us (2%)
  between operations  1.43 us (1%)
    ppermute x35, starting transfers between devices, send(): return lax.ppermute(value, AXES, pairs)  50.2 us
    ppermute x35, waiting for transfers between devices, send(): return lax.ppermute(value, AXES, pairs)  44.6 us
    pallas_call x2, Pallas kernels, self_energy(): pl.pallas_call(functools.partial(sigma_kernel, plan, pair_count, u, copie...  9.21 us
    pallas_call x1, Pallas kernels, on_device(): pl.pallas_call(functools.partial(solve_kernel, plan, sources), out_shape=...  7.96 us
    unnamed x87, local copies, waits for them, and re-layouts  6.75 us
    dynamic_slice x5, local copies, waits for them, and re-layouts, on_device(): lax.dynamic_index_in_dim(right, r ^ s, 0, keepdims=False)  3.78 us
    dynamic_slice x2, local copies, waits for them, and re-layouts, part_of(): lax.dynamic_slice_in_dim(value, (y ^ q) * half + u * plan.sub, plan.sub, 2)  2.95 us
    pallas_call x1, Pallas kernels, on_device(): pl.pallas_call(functools.partial(place_kernel, plan), out_shape=jax.Shape...  2.95 us
  transfers between devices with their start and end apart: 35, of which 13 were waited for; matrix products, arithmetic and copies ran while one was open for 8% of the time, Pallas kernels for 5%

profile of v10, /device:TPU:0, one launch (start us, length us, event | category | flops | bytes accessed | tf_op | source)
XLA Modules:
  0.0 137.6 jit_solution(6140393266614619772)
XLA Ops:
  0.7 2.0 %constant_dynamic-slice_fusion = (bf16[2,2,96,384]{3,2,1,0:T(8,128)(2,1)}, bf16[2,2,96,384]{3,2,1,0:T(8,128)(2,1)}) fusion(bf16[2,2,384,384]{3,2,1,0:T(8,128)(2,1)} %refs_0_.3, s32[]{:T(128)S(6)} %select_n.231, s32[]{:T(128)S(6)} %select_n.223), kind=kLoop, calls=%fused_computation.33 | loop fusion | bytes 1179656 | tf_op jit(solution)/shard_map/dynamic_slice | solution.py:315
  2.7 3.0 %collective-permute-start.1 = (bf16[2,2,96,384]{3,2,1,0:T(8,128)(2,1)}, bf16[2,2,96,384]{3,2,1,0:T(8,128)(2,1)}, u32[]{:S(2)}, u32[]{:S(2)}) collective-permute-start(bf16[2,2,96,384]{3,2,1,0:T(8,128)(2,1)} %get-tuple-element.103), channel_id=1, source_target_pairs={{0,1},{1,0},{2,3},{3,2},{4,5},{5,4},{6,7},{7,6},{8,9},{9,8},{10,11... | collective-permute-start | bytes 884744 | tf_op jit(solution)/shard_map/ppermute | solution.py:46
  5.7 0.8 copy.12
  6.5 0.9 dynamic-slice_bitcast_fusion.2
  7.4 0.9 dynamic-slice_bitcast_fusion
  8.3 2.0 %collective-permute-start = (bf16[2,384,384]{2,1,0:T(8,128)(2,1)}, bf16[2,384,384]{2,1,0:T(8,128)(2,1)S(1)}, u32[]{:S(2)}, u32[]{:S(2)}) collective-permute-start(bf16[2,384,384]{2,1,0:T(8,128)(2,1)} %dynamic-slice_bitcast_fusion), channel_id=1, source_target_pairs={{0,16},{1,17},{2,18},{3,19},{4,20},{5,21},{6,22},{7,23},{8,24},{9,... | collective-permute-start | bytes 1769480 | tf_op jit(solution)/shard_map/ppermute | solution.py:46
  10.9 2.0 %copy.13 = bf16[2,384,2,384]{1,3,2,0:T(8,128)(2,1)S(1)} copy(bf16[2,384,2,384]{3,2,1,0:T(2,128)(2,1)S(1)} %copy-done.12) | data formatting | bytes 2359296 | tf_op jit(solution)/shard_map/optimization_barrier | solution.py:288
  13.8 2.1 %collective-permute-start.2 = (bf16[2,2,96,384]{3,2,1,0:T(8,128)(2,1)}, bf16[2,2,96,384]{3,2,1,0:T(8,128)(2,1)S(1)}, u32[]{:S(2)}, u32[]{:S(2)}) collective-permute-start(bf16[2,2,96,384]{3,2,1,0:T(8,128)(2,1)} %get-tuple-element.55), channel_id=1, source_target_pairs={{0,1},{1,0},{2,3},{3,2},{4,5},{5,4},{6,7},{7,6},{8,9},{9,8},{10,11... | collective-permute-start | bytes 884744 | tf_op jit(solution)/shard_map/ppermute | solution.py:46
  16.6 0.9 copy.15
  17.5 0.9 copy.16
  18.4 0.9 copy.17
  19.3 0.9 copy.18
  20.2 3.1 %collective-permute-done = bf16[2,384,384]{2,1,0:T(8,128)(2,1)S(1)} collective-permute-done((bf16[2,384,384]{2,1,0:T(8,128)(2,1)}, bf16[2,384,384]{2,1,0:T(8,128)(2,1)S(1)}, u32[]{:S(2)}, u32[]{:S(2)}) %collective-permute-start) | collective-permute-done | bytes 589856 | tf_op jit(solution)/shard_map/ppermute | solution.py:46
  23.4 4.5 %self_energy.2 = (bf16[2,96,384]{2,1,0:T(8,128)(2,1)}, bf16[2,96,384]{2,1,0:T(8,128)(2,1)}, bf16[2,96,384]{2,1,0:T(8,128)(2,1)}, bf16[2,96,384]{2,1,0:T(8,128)(2,1)}) custom-call(s32[3]{0:T(128)} %pad_add_fusion.place, s32[4,8]{1,0:T(4,128)} %fusion.1.quads, s32[4,8]{1,0:T(4,128)} %slice_bitcast_fusion.4.thirds, bf16[2,2,384,384]{3,2,1,0:T(8,128)(2,1)} %refs_0_.3, ...), custom_call_target="tpu_custom_call" | custom-call | tf_op jit(solution)/shard_map/self_energy/pallas_call | solution.py:347
  27.9 3.9 %collective-permute-done.3.refs_3_ = bf16[2,2,96,384]{3,2,1,0:T(8,128)(2,1)S(1)} collective-permute-done((bf16[2,2,96,384]{3,2,1,0:T(8,128)(2,1)}, bf16[2,2,96,384]{3,2,1,0:T(8,128)(2,1)S(1)}, u32[]{:S(2)}, u32[]{:S(2)}) %collective-permute-start.3) | collective-permute-done | bytes 294944 | tf_op jit(solution)/shard_map/ppermute | solution.py:46
  31.9 0.8 copy-done.33
  32.6 4.7 %self_energy.3 = (bf16[2,192,384]{2,1,0:T(8,128)(2,1)}, bf16[2,192,384]{2,1,0:T(8,128)(2,1)}, bf16[2,192,384]{2,1,0:T(8,128)(2,1)}, bf16[2,192,384]{2,1,0:T(8,128)(2,1)}) custom-call(s32[3]{0:T(128)} %pad_add_fusion.place, s32[4,8]{1,0:T(4,128)} %fusion.1.quads, s32[4,8]{1,0:T(4,128)} %slice_bitcast_fusion.4.thirds, bf16[2,2,384,384]{3,2,1,0:T(8,128)(2,1)} %refs_0_.3, ...), custom_call_target="tpu_custom_call" | custom-call | tf_op jit(solution)/shard_map/self_energy/pallas_call | solution.py:347
  37.4 1.4 %collective-permute-start.12 = (bf16[2,192,384]{2,1,0:T(8,128)(2,1)}, bf16[2,192,384]{2,1,0:T(8,128)(2,1)S(1)}, u32[]{:S(2)}, u32[]{:S(2)}) collective-permute-start(bf16[2,192,384]{2,1,0:T(8,128)(2,1)} %get-tuple-element.62.refs_1_), channel_id=1, source_target_pairs={{8,24},{9,25},{16,0},{17,1},{18,2},{19,3},{24,8},{25,9},{26,10},{2... | collective-permute-start | bytes 884744 | tf_op jit(solution)/shard_map/ppermute | solution.py:46
  38.8 1.8 %collective-permute-start.5 = (bf16[2,192,384]{2,1,0:T(8,128)(2,1)}, bf16[2,192,384]{2,1,0:T(8,128)(2,1)S(1)}, u32[]{:S(2)}, u32[]{:S(2)}) collective-permute-start(bf16[2,192,384]{2,1,0:T(8,128)(2,1)} %get-tuple-element.63), channel_id=1, source_target_pairs={{0,1},{1,0},{2,3},{3,2},{4,5},{5,4},{6,7},{7,6},{8,9},{9,8},{10,11... | collective-permute-start | bytes 884744 | tf_op jit(solution)/shard_map/ppermute | solution.py:46
  40.6 1.3 collective-permute-start.6
  42.0 7.6 %collective-permute-done.12 = bf16[2,192,384]{2,1,0:T(8,128)(2,1)S(1)} collective-permute-done((bf16[2,192,384]{2,1,0:T(8,128)(2,1)}, bf16[2,192,384]{2,1,0:T(8,128)(2,1)S(1)}, u32[]{:S(2)}, u32[]{:S(2)}) %collective-permute-start.12) | collective-permute-done | bytes 294944 | tf_op jit(solution)/shard_map/ppermute | solution.py:46
  49.6 3.9 %collective-permute-start.13 = (bf16[2,192,384]{2,1,0:T(8,128)(2,1)S(1)}, bf16[2,192,384]{2,1,0:T(8,128)(2,1)S(1)}, u32[]{:S(2)}, u32[]{:S(2)}) collective-permute-start(bf16[2,192,384]{2,1,0:T(8,128)(2,1)S(1)} %get-tuple-element.108), channel_id=1, source_target_pairs={{0,2},{1,3},{2,4},{3,5},{8,10},{9,11},{10,12},{11,13},{12,14},{13,... | collective-permute-start | bytes 884744 | tf_op jit(solution)/shard_map/ppermute | solution.py:46
  53.5 1.7 %collective-permute-done.5.refs_2_ = bf16[2,192,384]{2,1,0:T(8,128)(2,1)S(1)} collective-permute-done((bf16[2,192,384]{2,1,0:T(8,128)(2,1)}, bf16[2,192,384]{2,1,0:T(8,128)(2,1)S(1)}, u32[]{:S(2)}, u32[]{:S(2)}) %collective-permute-start.5) | collective-permute-done | bytes 294944 | tf_op jit(solution)/shard_map/ppermute | solution.py:46
  56.0 1.5 %collective-permute-start.11 = (bf16[384,384]{1,0:T(8,128)(2,1)S(1)}, bf16[384,384]{1,0:T(8,128)(2,1)S(1)}, u32[]{:S(2)}, u32[]{:S(2)}) collective-permute-start(bf16[384,384]{1,0:T(8,128)(2,1)S(1)} %bitcast.57), channel_id=1, source_target_pairs={{0,24},{1,25},{2,26},{3,27},{4,28},{5,29},{6,30},{7,31},{8,16},{9,... | collective-permute-start | bytes 884744 | tf_op jit(solution)/shard_map/ppermute | solution.py:46
  57.5 0.7 collective-permute-start.9
  58.4 0.7 collective-permute-start.15
  59.0 5.1 %collective-permute-start.14 = (bf16[2,192,384]{2,1,0:T(8,128)(2,1)S(1)}, bf16[2,192,384]{2,1,0:T(8,128)(2,1)S(1)}, u32[]{:S(2)}, u32[]{:S(2)}) collective-permute-start(bf16[2,192,384]{2,1,0:T(8,128)(2,1)S(1)} %get-tuple-element.71), channel_id=1, source_target_pairs={{0,2},{1,3},{2,4},{3,5},{8,10},{9,11},{10,12},{11,13},{12,14},{13,... | collective-permute-start | bytes 884744 | tf_op jit(solution)/shard_map/ppermute | solution.py:46
  64.4 6.2 %collective-permute-done.14.refs_11_ = bf16[2,192,384]{2,1,0:T(8,128)(2,1)S(1)} collective-permute-done((bf16[2,192,384]{2,1,0:T(8,128)(2,1)S(1)}, bf16[2,192,384]{2,1,0:T(8,128)(2,1)S(1)}, u32[]{:S(2)}, u32[]{:S(2)}) %collective-permute-start.14) | collective-permute-done | bytes 294944 | tf_op jit(solution)/shard_map/ppermute | solution.py:46
  70.7 0.7 collective-permute-start.17
  71.4 6.9 %collective-permute-start.8 = (bf16[384,768]{1,0:T(8,128)(2,1)S(1)}, bf16[384,768]{1,0:T(8,128)(2,1)S(1)}, u32[]{:S(2)}, u32[]{:S(2)}) collective-permute-start(bf16[384,768]{1,0:T(8,128)(2,1)S(1)} %pad_maximum_fusion.2.refs_2_), channel_id=1, source_target_pairs={{0,8},{1,9},{2,10},{3,11},{4,12},{5,13},{6,14},{7,15},{8,0},{9,1},... | collective-permute-start | bytes 1769480 | tf_op jit(solution)/shard_map/ppermute | solution.py:46
  79.2 0.7 collective-permute-start.7
  79.9 0.7 collective-permute-start.20
  80.6 1.3 collective-permute-start.19
  82.0 6.9 %collective-permute-start.23 = (bf16[2,192,384]{2,1,0:T(8,128)(2,1)S(1)}, bf16[2,192,384]{2,1,0:T(8,128)(2,1)S(1)}, u32[]{:S(2)}, u32[]{:S(2)}) collective-permute-start(bf16[2,192,384]{2,1,0:T(8,128)(2,1)S(1)} %collective-permute-done.13.refs_10_), channel_id=1, source_target_pairs={{0,8},{1,9},{2,10},{3,11},{4,12},{5,13},{6,14},{7,15},{8,0},{9,1},... | collective-permute-start | bytes 884744 | tf_op jit(solution)/shard_map/ppermute | solution.py:46
  88.9 1.1 collective-permute-done.23.refs_20_
  90.6 0.8 collective-permute-start.18
  91.5 4.1 %collective-permute-start.30 = (bf16[2,384,384]{2,1,0:T(8,128)(2,1)S(1)}, bf16[2,384,384]{2,1,0:T(8,128)(2,1)S(1)}, u32[]{:S(2)}, u32[]{:S(2)}) collective-permute-start(bf16[2,384,384]{2,1,0:T(8,128)(2,1)S(1)} %collective-permute-done.20.refs_17_), channel_id=1, source_target_pairs={{0,8},{1,9},{2,10},{3,11},{4,12},{5,13},{6,14},{7,15},{8,0},{9,1},... | collective-permute-start | bytes 1769480 | tf_op jit(solution)/shard_map/ppermute | solution.py:46
  95.6 8.6 %collective-permute-done.19.refs_16_ = bf16[2,384,384]{2,1,0:T(8,128)(2,1)S(1)} collective-permute-done((bf16[2,384,384]{2,1,0:T(8,128)(2,1)S(1)}, bf16[2,384,384]{2,1,0:T(8,128)(2,1)S(1)}, u32[]{:S(2)}, u32[]{:S(2)}) %collective-permute-start.19) | collective-permute-done | bytes 589856 | tf_op jit(solution)/shard_map/ppermute | solution.py:46
  105.3 1.4 %collective-permute-done.27.refs_24_ = bf16[2,192,384]{2,1,0:T(8,128)(2,1)S(1)} collective-permute-done((bf16[2,192,384]{2,1,0:T(8,128)(2,1)S(1)}, bf16[2,192,384]{2,1,0:T(8,128)(2,1)S(1)}, u32[]{:S(2)}, u32[]{:S(2)}) %collective-permute-start.27) | collective-permute-done | bytes 294944 | tf_op jit(solution)/shard_map/ppermute | solution.py:46
  108.5 0.8 copy-done.22
  109.3 8.0 %substitution.1 = (bf16[384,384]{1,0:T(8,128)(2,1)}, bf16[384,384]{1,0:T(8,128)(2,1)}, bf16[384,384]{1,0:T(8,128)(2,1)}, bf16[384,384]{1,0:T(8,128)(2,1)}) custom-call(s32[3]{0:T(128)} %pad_add_fusion.place, bf16[384,768]{1,0:T(8,128)(2,1)} %copy-done.4, bf16[384,768]{1,0:T(8,128)(2,1)} %copy-done.18, bf16[384,768]{1,0:T(8,128)(2,1)} %copy-done.3, ...), custom_call_target="tpu_custom_call" | custom-call | tf_op jit(solution)/shard_map/substitution/pallas_call | solution.py:464
  118.4 1.4 collective-permute-start.34
  119.7 6.7 %collective-permute-done.31.refs_3_ = bf16[2,192,384]{2,1,0:T(8,128)(2,1)S(1)} collective-permute-done((bf16[2,192,384]{2,1,0:T(8,128)(2,1)S(1)}, bf16[2,192,384]{2,1,0:T(8,128)(2,1)S(1)}, u32[]{:S(2)}, u32[]{:S(2)}) %collective-permute-start.31) | collective-permute-done | bytes 294944 | tf_op jit(solution)/shard_map/ppermute | solution.py:46
  126.4 0.7 copy-done.36
  127.2 2.9 %place_sigma.1 = bf16[2,2,384,384]{3,2,1,0:T(8,128)(2,1)} custom-call(s32[3]{0:T(128)} %pad_add_fusion.place, bf16[2,192,384]{2,1,0:T(8,128)(2,1)} %get-tuple-element.61.refs_0_, bf16[2,192,384]{2,1,0:T(8,128)(2,1)} %get-tuple-element.62.refs_1_, bf16[2,192,384]{2,1,0:T(8,128)(2,1)} %copy-done.10, bf16[2,192,384]{2,1,0:T(8,128)(2,1)} %copy-done.36), custom_call_target="tpu_custom_call" | custom-call | tf_op jit(solution)/shard_map/place_sigma/pallas_call | solution.py:481
  130.1 3.3 %collective-permute-done.34 = bf16[384,384]{1,0:T(8,128)(2,1)S(1)} collective-permute-done((bf16[384,384]{1,0:T(8,128)(2,1)}, bf16[384,384]{1,0:T(8,128)(2,1)S(1)}, u32[]{:S(2)}, u32[]{:S(2)}) %collective-permute-start.34) | collective-permute-done | bytes 294944 | tf_op jit(solution)/shard_map/ppermute | solution.py:46
  133.8 0.8 copy.21
  134.8 2.8 %copy.23 = bf16[2,384,2,384]{3,2,1,0:T(2,128)(2,1)} copy(bf16[2,384,2,384]{1,3,2,0:T(8,128)(2,1)S(1)} %bitcast.52) | data formatting | bytes 2359296
  (145 shorter events, 9.5 us)
Async XLA Ops:
  2.7 11.1 %collective-permute-start.1 = (bf16[2,2,96,384]{3,2,1,0:T(8,128)(2,1)}, bf16[2,2,96,384]{3,2,1,0:T(8,128)(2,1)}, u32[]{:S(2)}, u32[]{:S(2)}) collective-permute-start(bf16[2,2,96,384]{3,2,1,0:T(8,128)(2,1)} %get-tuple-element.103), channel_id=1, source_target_pairs={{0,1},{1,0},{2,3},{3,2},{4,5},{5,4},{6,7},{7,6},{8,9},{9,8},{10,11... | collective-permute-start | bytes 884744 | tf_op jit(solution)/shard_map/ppermute | solution.py:46
  7.4 16.0 %collective-permute-start.4 = (bf16[2,2,96,384]{3,2,1,0:T(8,128)(2,1)}, bf16[2,2,96,384]{3,2,1,0:T(8,128)(2,1)}, u32[]{:S(2)}, u32[]{:S(2)}) collective-permute-start(bf16[2,2,96,384]{3,2,1,0:T(8,128)(2,1)} %get-tuple-element.101), channel_id=1, source_target_pairs={{0,1},{1,0},{2,3},{3,2},{4,5},{5,4},{6,7},{7,6},{8,9},{9,8},{10,11... | collective-permute-start | bytes 884744 | tf_op jit(solution)/shard_map/ppermute | solution.py:46
  8.3 15.0 %collective-permute-start = (bf16[2,384,384]{2,1,0:T(8,128)(2,1)}, bf16[2,384,384]{2,1,0:T(8,128)(2,1)S(1)}, u32[]{:S(2)}, u32[]{:S(2)}) collective-permute-start(bf16[2,384,384]{2,1,0:T(8,128)(2,1)} %dynamic-slice_bitcast_fusion), channel_id=1, source_target_pairs={{0,16},{1,17},{2,18},{3,19},{4,20},{5,21},{6,22},{7,23},{8,24},{9,... | collective-permute-start | bytes 1769480 | tf_op jit(solution)/shard_map/ppermute | solution.py:46
  13.8 14.1 %collective-permute-start.2 = (bf16[2,2,96,384]{3,2,1,0:T(8,128)(2,1)}, bf16[2,2,96,384]{3,2,1,0:T(8,128)(2,1)S(1)}, u32[]{:S(2)}, u32[]{:S(2)}) collective-permute-start(bf16[2,2,96,384]{3,2,1,0:T(8,128)(2,1)} %get-tuple-element.55), channel_id=1, source_target_pairs={{0,1},{1,0},{2,3},{3,2},{4,5},{5,4},{6,7},{7,6},{8,9},{9,8},{10,11... | collective-permute-start | bytes 884744 | tf_op jit(solution)/shard_map/ppermute | solution.py:46
  15.9 16.0 %collective-permute-start.3 = (bf16[2,2,96,384]{3,2,1,0:T(8,128)(2,1)}, bf16[2,2,96,384]{3,2,1,0:T(8,128)(2,1)S(1)}, u32[]{:S(2)}, u32[]{:S(2)}) collective-permute-start(bf16[2,2,96,384]{3,2,1,0:T(8,128)(2,1)} %get-tuple-element.56), channel_id=1, source_target_pairs={{0,1},{1,0},{2,3},{3,2},{4,5},{5,4},{6,7},{7,6},{8,9},{9,8},{10,11... | collective-permute-start | bytes 884744 | tf_op jit(solution)/shard_map/ppermute | solution.py:46
  37.4 12.2 %collective-permute-start.12 = (bf16[2,192,384]{2,1,0:T(8,128)(2,1)}, bf16[2,192,384]{2,1,0:T(8,128)(2,1)S(1)}, u32[]{:S(2)}, u32[]{:S(2)}) collective-permute-start(bf16[2,192,384]{2,1,0:T(8,128)(2,1)} %get-tuple-element.62.refs_1_), channel_id=1, source_target_pairs={{8,24},{9,25},{16,0},{17,1},{18,2},{19,3},{24,8},{25,9},{26,10},{2... | collective-permute-start | bytes 884744 | tf_op jit(solution)/shard_map/ppermute | solution.py:46
  38.8 16.4 %collective-permute-start.5 = (bf16[2,192,384]{2,1,0:T(8,128)(2,1)}, bf16[2,192,384]{2,1,0:T(8,128)(2,1)S(1)}, u32[]{:S(2)}, u32[]{:S(2)}) collective-permute-start(bf16[2,192,384]{2,1,0:T(8,128)(2,1)} %get-tuple-element.63), channel_id=1, source_target_pairs={{0,1},{1,0},{2,3},{3,2},{4,5},{5,4},{6,7},{7,6},{8,9},{9,8},{10,11... | collective-permute-start | bytes 884744 | tf_op jit(solution)/shard_map/ppermute | solution.py:46
  40.6 14.6 %collective-permute-start.6 = (bf16[2,192,384]{2,1,0:T(8,128)(2,1)}, bf16[2,192,384]{2,1,0:T(8,128)(2,1)S(1)}, u32[]{:S(2)}, u32[]{:S(2)}) collective-permute-start(bf16[2,192,384]{2,1,0:T(8,128)(2,1)} %get-tuple-element.87), channel_id=1, source_target_pairs={{8,25},{9,24},{16,1},{17,0},{18,3},{19,2},{24,9},{25,8},{26,11},{2... | collective-permute-start | bytes 884744 | tf_op jit(solution)/shard_map/ppermute | solution.py:46
  49.6 8.7 %collective-permute-start.13 = (bf16[2,192,384]{2,1,0:T(8,128)(2,1)S(1)}, bf16[2,192,384]{2,1,0:T(8,128)(2,1)S(1)}, u32[]{:S(2)}, u32[]{:S(2)}) collective-permute-start(bf16[2,192,384]{2,1,0:T(8,128)(2,1)S(1)} %get-tuple-element.108), channel_id=1, source_target_pairs={{0,2},{1,3},{2,4},{3,5},{8,10},{9,11},{10,12},{11,13},{12,14},{13,... | collective-permute-start | bytes 884744 | tf_op jit(solution)/shard_map/ppermute | solution.py:46
  56.0 23.9 %copy-start.1 = (bf16[2,384,384]{2,1,0:T(8,128)(2,1)}, bf16[2,384,384]{2,1,0:T(8,128)(2,1)S(1)}, u32[]{:S(2)}) copy-start(bf16[2,384,384]{2,1,0:T(8,128)(2,1)S(1)} %pad_maximum_fusion.4.refs_9_) | copy-start | bytes 1769476
  56.0 14.6 %collective-permute-start.10 = (bf16[384,384]{1,0:T(8,128)(2,1)S(1)}, bf16[384,384]{1,0:T(8,128)(2,1)S(1)}, u32[]{:S(2)}, u32[]{:S(2)}) collective-permute-start(bf16[384,384]{1,0:T(8,128)(2,1)S(1)} %bitcast.58), channel_id=1, source_target_pairs={{0,16},{1,17},{2,18},{3,19},{4,20},{5,21},{6,22},{7,23},{8,24},{9,... | collective-permute-start | bytes 884744 | tf_op jit(solution)/shard_map/ppermute | solution.py:46
  56.0 15.4 %collective-permute-start.11 = (bf16[384,384]{1,0:T(8,128)(2,1)S(1)}, bf16[384,384]{1,0:T(8,128)(2,1)S(1)}, u32[]{:S(2)}, u32[]{:S(2)}) collective-permute-start(bf16[384,384]{1,0:T(8,128)(2,1)S(1)} %bitcast.57), channel_id=1, source_target_pairs={{0,24},{1,25},{2,26},{3,27},{4,28},{5,29},{6,30},{7,31},{8,16},{9,... | collective-permute-start | bytes 884744 | tf_op jit(solution)/shard_map/ppermute | solution.py:46
  57.5 20.9 %collective-permute-start.9 = (bf16[384,384]{1,0:T(8,128)(2,1)S(1)}, bf16[384,384]{1,0:T(8,128)(2,1)S(1)}, u32[]{:S(2)}, u32[]{:S(2)}) collective-permute-start(bf16[384,384]{1,0:T(8,128)(2,1)S(1)} %bitcast.56), channel_id=1, source_target_pairs={{0,8},{1,9},{2,10},{3,11},{4,12},{5,13},{6,14},{7,15},{8,0},{9,1},... | collective-permute-start | bytes 884744 | tf_op jit(solution)/shard_map/ppermute | solution.py:46
  58.3 23.6 %copy-start.5 = (bf16[2,192,384]{2,1,0:T(8,128)(2,1)}, bf16[2,192,384]{2,1,0:T(8,128)(2,1)S(1)}, u32[]{:S(2)}) copy-start(bf16[2,192,384]{2,1,0:T(8,128)(2,1)S(1)} %collective-permute-done.13.refs_10_) | copy-start | bytes 884740
  58.4 6.0 %collective-permute-start.15 = (bf16[2,192,384]{2,1,0:T(8,128)(2,1)S(1)}, bf16[2,192,384]{2,1,0:T(8,128)(2,1)S(1)}, u32[]{:S(2)}, u32[]{:S(2)}) collective-permute-start(bf16[2,192,384]{2,1,0:T(8,128)(2,1)S(1)} %broadcast_select_fusion.5), channel_id=1, source_target_pairs={{2,4},{3,5},{4,6},{5,7},{8,10},{9,11},{10,12},{11,13},{12,14},{13,... | collective-permute-start | bytes 884744 | tf_op jit(solution)/shard_map/ppermute | solution.py:46
  59.0 11.6 %collective-permute-start.14 = (bf16[2,192,384]{2,1,0:T(8,128)(2,1)S(1)}, bf16[2,192,384]{2,1,0:T(8,128)(2,1)S(1)}, u32[]{:S(2)}, u32[]{:S(2)}) collective-permute-start(bf16[2,192,384]{2,1,0:T(8,128)(2,1)S(1)} %get-tuple-element.71), channel_id=1, source_target_pairs={{0,2},{1,3},{2,4},{3,5},{8,10},{9,11},{10,12},{11,13},{12,14},{13,... | collective-permute-start | bytes 884744 | tf_op jit(solution)/shard_map/ppermute | solution.py:46
  64.3 25.7 %copy-start.6 = (bf16[2,192,384]{2,1,0:T(8,128)(2,1)}, bf16[2,192,384]{2,1,0:T(8,128)(2,1)S(1)}, u32[]{:S(2)}) copy-start(bf16[2,192,384]{2,1,0:T(8,128)(2,1)S(1)} %collective-permute-done.15.refs_12_) | copy-start | bytes 884740
  64.3 14.8 %collective-permute-start.22 = (bf16[2,384,384]{2,1,0:T(8,128)(2,1)S(1)}, bf16[2,384,384]{2,1,0:T(8,128)(2,1)S(1)}, u32[]{:S(2)}, u32[]{:S(2)}) collective-permute-start(bf16[2,384,384]{2,1,0:T(8,128)(2,1)S(1)} %pad_maximum_fusion.4.refs_9_), channel_id=1, source_target_pairs={{0,8},{1,9},{2,10},{3,11},{4,12},{5,13},{6,14},{7,15},{8,0},{9,1},... | collective-permute-start | bytes 1769480 | tf_op jit(solution)/shard_map/ppermute | solution.py:46
  70.6 19.8 %copy-start.7 = (bf16[2,192,384]{2,1,0:T(8,128)(2,1)}, bf16[2,192,384]{2,1,0:T(8,128)(2,1)S(1)}, u32[]{:S(2)}) copy-start(bf16[2,192,384]{2,1,0:T(8,128)(2,1)S(1)} %collective-permute-done.14.refs_11_) | copy-start | bytes 884740
  70.6 9.3 %collective-permute-start.21 = (bf16[2,384,384]{2,1,0:T(8,128)(2,1)S(1)}, bf16[2,384,384]{2,1,0:T(8,128)(2,1)S(1)}, u32[]{:S(2)}, u32[]{:S(2)}) collective-permute-start(bf16[2,384,384]{2,1,0:T(8,128)(2,1)S(1)} %pad_maximum_fusion.3.refs_8_), channel_id=1, source_target_pairs={{0,8},{1,9},{2,10},{3,11},{4,12},{5,13},{6,14},{7,15},{8,0},{9,1},... | collective-permute-start | bytes 1769480 | tf_op jit(solution)/shard_map/ppermute | solution.py:46
  70.7 9.9 %collective-permute-start.17 = (bf16[2,192,384]{2,1,0:T(8,128)(2,1)S(1)}, bf16[2,192,384]{2,1,0:T(8,128)(2,1)S(1)}, u32[]{:S(2)}, u32[]{:S(2)}) collective-permute-start(bf16[2,192,384]{2,1,0:T(8,128)(2,1)S(1)} %broadcast_select_fusion.3), channel_id=1, source_target_pairs={{4,6},{5,7},{8,12},{9,13},{12,14},{13,15},{20,22},{21,23},{24,28},... | collective-permute-start | bytes 884744 | tf_op jit(solution)/shard_map/ppermute | solution.py:46
  71.4 17.5 %copy-start.24 = (bf16[384,384]{1,0:T(8,128)(2,1)}, bf16[384,384]{1,0:T(8,128)(2,1)S(1)}, u32[]{:S(2)}) copy-start(bf16[384,384]{1,0:T(8,128)(2,1)S(1)} %collective-permute-done.11.refs_7_) | copy-start | bytes 884740
  71.4 19.0 %collective-permute-start.8 = (bf16[384,768]{1,0:T(8,128)(2,1)S(1)}, bf16[384,768]{1,0:T(8,128)(2,1)S(1)}, u32[]{:S(2)}, u32[]{:S(2)}) collective-permute-start(bf16[384,768]{1,0:T(8,128)(2,1)S(1)} %pad_maximum_fusion.2.refs_2_), channel_id=1, source_target_pairs={{0,8},{1,9},{2,10},{3,11},{4,12},{5,13},{6,14},{7,15},{8,0},{9,1},... | collective-permute-start | bytes 1769480 | tf_op jit(solution)/shard_map/ppermute | solution.py:46
  78.4 3.6 %collective-permute-start.16 = (bf16[2,192,384]{2,1,0:T(8,128)(2,1)S(1)}, bf16[2,192,384]{2,1,0:T(8,128)(2,1)S(1)}, u32[]{:S(2)}, u32[]{:S(2)}) collective-permute-start(bf16[2,192,384]{2,1,0:T(8,128)(2,1)S(1)} %broadcast_select_fusion.4), channel_id=1, source_target_pairs={{2,4},{3,5},{4,6},{5,7},{8,10},{9,11},{10,12},{11,13},{12,14},{13,... | collective-permute-start | bytes 884744 | tf_op jit(solution)/shard_map/ppermute | solution.py:46
  79.2 28.4 %copy-start.15 = (bf16[2,384,384]{2,1,0:T(8,128)(2,1)}, bf16[2,384,384]{2,1,0:T(8,128)(2,1)S(1)}, u32[]{:S(2)}) copy-start(bf16[2,384,384]{2,1,0:T(8,128)(2,1)S(1)} %collective-permute-done.22.refs_19_) | copy-start | bytes 1769476
  79.2 11.5 %collective-permute-start.7 = (bf16[384,768]{1,0:T(8,128)(2,1)S(1)}, bf16[384,768]{1,0:T(8,128)(2,1)S(1)}, u32[]{:S(2)}, u32[]{:S(2)}) collective-permute-start(bf16[384,768]{1,0:T(8,128)(2,1)S(1)} %pad_maximum_fusion.1.refs_0_), channel_id=1, source_target_pairs={{0,8},{1,9},{2,10},{3,11},{4,12},{5,13},{6,14},{7,15},{8,0},{9,1},... | collective-permute-start | bytes 1769480 | tf_op jit(solution)/shard_map/ppermute | solution.py:46
  79.9 27.7 %copy-start.16 = (bf16[2,384,384]{2,1,0:T(8,128)(2,1)}, bf16[2,384,384]{2,1,0:T(8,128)(2,1)S(1)}, u32[]{:S(2)}) copy-start(bf16[2,384,384]{2,1,0:T(8,128)(2,1)S(1)} %collective-permute-done.21.refs_18_) | copy-start | bytes 1769476
  79.9 11.6 %collective-permute-start.20 = (bf16[2,384,384]{2,1,0:T(8,128)(2,1)S(1)}, bf16[2,384,384]{2,1,0:T(8,128)(2,1)S(1)}, u32[]{:S(2)}, u32[]{:S(2)}) collective-permute-start(bf16[2,384,384]{2,1,0:T(8,128)(2,1)S(1)} %pad_maximum_fusion.4.refs_9_), channel_id=1, source_target_pairs={{12,8},{13,9},{28,24},{29,25}} | collective-permute-start | bytes 1769480 | tf_op jit(solution)/shard_map/ppermute | solution.py:46
  80.6 27.0 %copy-start.26 = (bf16[2,192,384]{2,1,0:T(8,128)(2,1)}, bf16[2,192,384]{2,1,0:T(8,128)(2,1)S(1)}, u32[]{:S(2)}) copy-start(bf16[2,192,384]{2,1,0:T(8,128)(2,1)S(1)} %collective-permute-done.17.refs_14_) | copy-start | bytes 884740
  80.6 23.6 %collective-permute-start.19 = (bf16[2,384,384]{2,1,0:T(8,128)(2,1)S(1)}, bf16[2,384,384]{2,1,0:T(8,128)(2,1)S(1)}, u32[]{:S(2)}, u32[]{:S(2)}) collective-permute-start(bf16[2,384,384]{2,1,0:T(8,128)(2,1)S(1)} %select_select_fusion), channel_id=1, source_target_pairs={{2,0},{3,1},{8,14},{9,15},{10,8},{11,9},{12,10},{13,11},{18,16},{1... | collective-permute-start | bytes 1769480 | tf_op jit(solution)/shard_map/ppermute | solution.py:46
  82.0 25.6 %copy-start.8 = (bf16[2,192,384]{2,1,0:T(8,128)(2,1)}, bf16[2,192,384]{2,1,0:T(8,128)(2,1)S(1)}, u32[]{:S(2)}) copy-start(bf16[2,192,384]{2,1,0:T(8,128)(2,1)S(1)} %collective-permute-done.16.refs_13_) | copy-start | bytes 884740
  82.0 8.1 %collective-permute-start.23 = (bf16[2,192,384]{2,1,0:T(8,128)(2,1)S(1)}, bf16[2,192,384]{2,1,0:T(8,128)(2,1)S(1)}, u32[]{:S(2)}, u32[]{:S(2)}) collective-permute-start(bf16[2,192,384]{2,1,0:T(8,128)(2,1)S(1)} %collective-permute-done.13.refs_10_), channel_id=1, source_target_pairs={{0,8},{1,9},{2,10},{3,11},{4,12},{5,13},{6,14},{7,15},{8,0},{9,1},... | collective-permute-start | bytes 884744 | tf_op jit(solution)/shard_map/ppermute | solution.py:46
  88.9 28.4 %copy-start.42 = (bf16[2,192,384]{2,1,0:T(8,128)(2,1)S(1)}, bf16[2,192,384]{2,1,0:T(8,128)(2,1)}, u32[]{:S(2)}) copy-start(bf16[2,192,384]{2,1,0:T(8,128)(2,1)} %get-tuple-element.87) | copy-start | bytes 884740
  90.1 17.5 %copy-start.27 = (bf16[2,192,384]{2,1,0:T(8,128)(2,1)}, bf16[2,192,384]{2,1,0:T(8,128)(2,1)S(1)}, u32[]{:S(2)}) copy-start(bf16[2,192,384]{2,1,0:T(8,128)(2,1)S(1)} %collective-permute-done.23.refs_20_) | copy-start | bytes 884740
  90.1 14.3 %collective-permute-start.25 = (bf16[2,192,384]{2,1,0:T(8,128)(2,1)S(1)}, bf16[2,192,384]{2,1,0:T(8,128)(2,1)S(1)}, u32[]{:S(2)}, u32[]{:S(2)}) collective-permute-start(bf16[2,192,384]{2,1,0:T(8,128)(2,1)S(1)} %collective-permute-done.15.refs_12_), channel_id=1, source_target_pairs={{0,8},{1,9},{2,10},{3,11},{4,12},{5,13},{6,14},{7,15},{8,0},{9,1},... | collective-permute-start | bytes 884744 | tf_op jit(solution)/shard_map/ppermute | solution.py:46
  90.4 17.2 %copy-start.17 = (bf16[384,768]{1,0:T(8,128)(2,1)}, bf16[384,768]{1,0:T(8,128)(2,1)S(1)}, u32[]{:S(2)}) copy-start(bf16[384,768]{1,0:T(8,128)(2,1)S(1)} %collective-permute-done.8.refs_3_) | copy-start | bytes 1769476
  90.4 14.4 %collective-permute-start.24 = (bf16[2,192,384]{2,1,0:T(8,128)(2,1)S(1)}, bf16[2,192,384]{2,1,0:T(8,128)(2,1)S(1)}, u32[]{:S(2)}, u32[]{:S(2)}) collective-permute-start(bf16[2,192,384]{2,1,0:T(8,128)(2,1)S(1)} %collective-permute-done.14.refs_11_), channel_id=1, source_target_pairs={{0,8},{1,9},{2,10},{3,11},{4,12},{5,13},{6,14},{7,15},{8,0},{9,1},... | collective-permute-start | bytes 884744 | tf_op jit(solution)/shard_map/ppermute | solution.py:46
  90.6 17.0 %copy-start.18 = (bf16[384,768]{1,0:T(8,128)(2,1)}, bf16[384,768]{1,0:T(8,128)(2,1)S(1)}, u32[]{:S(2)}) copy-start(bf16[384,768]{1,0:T(8,128)(2,1)S(1)} %collective-permute-done.7.refs_1_) | copy-start | bytes 1769476
  90.6 14.3 %collective-permute-start.18 = (bf16[2,192,384]{2,1,0:T(8,128)(2,1)S(1)}, bf16[2,192,384]{2,1,0:T(8,128)(2,1)S(1)}, u32[]{:S(2)}, u32[]{:S(2)}) collective-permute-start(bf16[2,192,384]{2,1,0:T(8,128)(2,1)S(1)} %broadcast_select_fusion.2), channel_id=1, source_target_pairs={{4,6},{5,7},{8,12},{9,13},{12,14},{13,15},{20,22},{21,23},{24,28},... | collective-permute-start | bytes 884744 | tf_op jit(solution)/shard_map/ppermute | solution.py:46
  91.5 16.0 %collective-permute-start.30 = (bf16[2,384,384]{2,1,0:T(8,128)(2,1)S(1)}, bf16[2,384,384]{2,1,0:T(8,128)(2,1)S(1)}, u32[]{:S(2)}, u32[]{:S(2)}) collective-permute-start(bf16[2,384,384]{2,1,0:T(8,128)(2,1)S(1)} %collective-permute-done.20.refs_17_), channel_id=1, source_target_pairs={{0,8},{1,9},{2,10},{3,11},{4,12},{5,13},{6,14},{7,15},{8,0},{9,1},... | collective-permute-start | bytes 1769480 | tf_op jit(solution)/shard_map/ppermute | solution.py:46
  104.3 3.3 %collective-permute-start.29 = (bf16[2,384,384]{2,1,0:T(8,128)(2,1)S(1)}, bf16[2,384,384]{2,1,0:T(8,128)(2,1)S(1)}, u32[]{:S(2)}, u32[]{:S(2)}) collective-permute-start(bf16[2,384,384]{2,1,0:T(8,128)(2,1)S(1)} %collective-permute-done.19.refs_16_), channel_id=1, source_target_pairs={{0,8},{1,9},{2,10},{3,11},{4,12},{5,13},{6,14},{7,15},{8,0},{9,1},... | collective-permute-start | bytes 1769480 | tf_op jit(solution)/shard_map/ppermute | solution.py:46
  104.4 2.3 %collective-permute-start.27 = (bf16[2,192,384]{2,1,0:T(8,128)(2,1)S(1)}, bf16[2,192,384]{2,1,0:T(8,128)(2,1)S(1)}, u32[]{:S(2)}, u32[]{:S(2)}) collective-permute-start(bf16[2,192,384]{2,1,0:T(8,128)(2,1)S(1)} %collective-permute-done.17.refs_14_), channel_id=1, source_target_pairs={{0,8},{1,9},{2,10},{3,11},{4,12},{5,13},{6,14},{7,15},{8,0},{9,1},... | collective-permute-start | bytes 884744 | tf_op jit(solution)/shard_map/ppermute | solution.py:46
  104.8 2.3 %collective-permute-start.26 = (bf16[2,192,384]{2,1,0:T(8,128)(2,1)S(1)}, bf16[2,192,384]{2,1,0:T(8,128)(2,1)S(1)}, u32[]{:S(2)}, u32[]{:S(2)}) collective-permute-start(bf16[2,192,384]{2,1,0:T(8,128)(2,1)S(1)} %collective-permute-done.16.refs_13_), channel_id=1, source_target_pairs={{0,8},{1,9},{2,10},{3,11},{4,12},{5,13},{6,14},{7,15},{8,0},{9,1},... | collective-permute-start | bytes 884744 | tf_op jit(solution)/shard_map/ppermute | solution.py:46
  104.9 2.6 %collective-permute-start.28 = (bf16[2,192,384]{2,1,0:T(8,128)(2,1)S(1)}, bf16[2,192,384]{2,1,0:T(8,128)(2,1)S(1)}, u32[]{:S(2)}, u32[]{:S(2)}) collective-permute-start(bf16[2,192,384]{2,1,0:T(8,128)(2,1)S(1)} %collective-permute-done.18.refs_15_), channel_id=1, source_target_pairs={{0,8},{1,9},{2,10},{3,11},{4,12},{5,13},{6,14},{7,15},{8,0},{9,1},... | collective-permute-start | bytes 884744 | tf_op jit(solution)/shard_map/ppermute | solution.py:46
  117.3 9.1 %collective-permute-start.31 = (bf16[2,192,384]{2,1,0:T(8,128)(2,1)S(1)}, bf16[2,192,384]{2,1,0:T(8,128)(2,1)S(1)}, u32[]{:S(2)}, u32[]{:S(2)}) collective-permute-start(bf16[2,192,384]{2,1,0:T(8,128)(2,1)S(1)} %copy-done.42), channel_id=1, source_target_pairs={{0,1},{1,0},{2,3},{3,2},{4,5},{5,4},{6,7},{7,6},{8,9},{9,8},{10,11... | collective-permute-start | bytes 884744 | tf_op jit(solution)/shard_map/ppermute | solution.py:46
  117.9 12.2 %collective-permute-start.32 = (bf16[384,384]{1,0:T(8,128)(2,1)}, bf16[384,384]{1,0:T(8,128)(2,1)S(1)}, u32[]{:S(2)}, u32[]{:S(2)}) collective-permute-start(bf16[384,384]{1,0:T(8,128)(2,1)} %get-tuple-element.84), channel_id=1, source_target_pairs={{0,8},{1,9},{2,10},{3,11},{4,12},{5,13},{6,14},{7,15},{8,0},{9,1},... | collective-permute-start | bytes 884744 | tf_op jit(solution)/shard_map/ppermute | solution.py:46
  117.9 12.3 %collective-permute-start.33 = (bf16[384,384]{1,0:T(8,128)(2,1)}, bf16[384,384]{1,0:T(8,128)(2,1)S(1)}, u32[]{:S(2)}, u32[]{:S(2)}) collective-permute-start(bf16[384,384]{1,0:T(8,128)(2,1)} %get-tuple-element.85), channel_id=1, source_target_pairs={{0,16},{1,17},{2,18},{3,19},{4,20},{5,21},{6,22},{7,23},{8,24},{9,... | collective-permute-start | bytes 884744 | tf_op jit(solution)/shard_map/ppermute | solution.py:46
  118.4 15.1 %collective-permute-start.34 = (bf16[384,384]{1,0:T(8,128)(2,1)}, bf16[384,384]{1,0:T(8,128)(2,1)S(1)}, u32[]{:S(2)}, u32[]{:S(2)}) collective-permute-start(bf16[384,384]{1,0:T(8,128)(2,1)} %get-tuple-element.86), channel_id=1, source_target_pairs={{0,24},{1,25},{2,26},{3,27},{4,28},{5,29},{6,30},{7,31},{8,16},{9,... | collective-permute-start | bytes 884744 | tf_op jit(solution)/shard_map/ppermute | solution.py:46
  (30 other events, 164.8 us)

commit v11 on v10

--- a/solution.py
+++ b/solution.py
@@ -68,8 +68,12 @@
                     break
         return sends
 
+    def left(self):
+        top = self.moments - 1
+        return {col: ((top, col), col - 1) for col in range(1, self.cols - 1)}
+
     def rest(self):
-        done = {(key, to) for key, to, _ in self.ring().values()}
+        done = {(key, to) for key, to, _ in self.ring().values()} | set(self.left().values())
         wanted = [
             (key, to)
             for key in self.keys
@@ -288,6 +292,23 @@
     return lax.optimization_barrier((value, others))[0]
 
 
+def spread_kernel(plan, place, *refs):
+    groups, width = plan.groups, plan.width
+    ins, out, held, sems = refs[:-3], refs[-3], refs[-2], refs[-1]
+    run_copies(
+        [
+            pltpu.make_async_copy(ins[s], held.at[place[0] ^ s], sems.at[s])
+            for s in range(plan.rows)
+        ]
+    )
+    for m in range(plan.moments):
+        parts = [held[m * groups + g] for g in range(groups)]
+        for p in range(2):
+            out[m, :, p, :] = jnp.concatenate(
+                [part[:, p * width : (p + 1) * width] for part in parts], axis=1
+            )
+
+
 def on_device(mesh, lesser, greater, triples, diag_inverse, right_side):
     moments, _, side, _ = lesser.shape
     plan = Plan(mesh, moments, side)
@@ -415,7 +436,7 @@
         goal = lambda a, c, m: (a, goals[c][1], m) if c in goals and valid(goals[c][0], a) else None
         return plan.send(choose(values, behind), goal)
 
-    ring, rest = plan.ring(), plan.rest()
+    top, ring, rest = moments - 1, plan.ring(), plan.rest()
     got = [[] for _ in plan.chunks]
 
     def ring_step(q, number, *behind):
@@ -429,6 +450,12 @@
         for key, to, _ in sends.values():
             found[key, to, q] = (value, 0)
 
+    def left_step(k):
+        value = shift({col: own[k][top] for col in plan.left()}, plan.left(), ())
+        for key, to in plan.left().values():
+            found[key, to, k] = (value, 0)
+        return value
+
     def rest_step(number, *behind):
         step = rest[number]
         value = shift({col: both[key[0]] for col, (key, _) in step.items()}, step, behind)
@@ -436,11 +463,14 @@
             for k in range(len(plan.chunks)):
                 found[key, to, k] = (value, plan.starts[k])
 
+    lefts = [left_step(k) for k in range(len(plan.chunks))]
     for number in range(cols - 1):
         for k in range(len(plan.chunks)):
             behind = [got[k - 1][number]] if k else []
             if number == 1 and k + 1 < len(plan.chunks):
                 behind.append(came[k + 1])
+            if number == 1:
+                behind.append(lefts[k])
             ring_step(k, number, *behind)
     for number in range(len(rest)):
         rest_step(number, got[0][1], got[-1][0], right_all)
@@ -489,9 +519,15 @@
 
     back = [solved[0]] + [exchange_row(solved[s], s) for s in range(1, rows)]
     back = after(back, sigma)
-    pieces = jnp.stack([lax.select_n(r ^ s, *back) for s in range(rows)])
-    pieces = pieces.reshape(moments, groups, side, 2, width).transpose(0, 2, 3, 1, 4)
-    return sigma, pieces.reshape(moments, side, 2, side)
+    spread = pl.pallas_call(
+        functools.partial(spread_kernel, plan),
+        out_shape=jax.ShapeDtypeStruct(right_side.shape, bf16),
+        in_specs=[smem()] + hbm(rows),
+        scratch_shapes=[pltpu.VMEM((rows, side, 2 * width), bf16), dma(rows)],
+        compiler_params=params,
+        name="place_solution",
+    )
+    return sigma, spread(place, *back)
 
 
 def solution(mesh):

time: 138 us -> 142 us (1.029)
  the two profiles are of different devices: /device:TPU:0 before, /device:TPU:25 now
where the time goes in v11:
time: 142 us; the launch traced here: 141 us
  waiting for transfers between devices  64.7 us (46%)
  starting transfers between devices  33.9 us (24%)
  Pallas kernels  24.1 us (17%)
  local copies, waits for them, and re-layouts  14.8 us (10%)
  other arithmetic  1.99 us (1%)
  between operations  1.65 us (1%)
    ppermute x37, waiting for transfers between devices, send(): return lax.ppermute(value, AXES, pairs)  64.7 us
    ppermute x37, starting transfers between devices, send(): return lax.ppermute(value, AXES, pairs)  33.9 us
    pallas_call x2, Pallas kernels, self_energy(): pl.pallas_call(functools.partial(sigma_kernel, plan, pair_count, u, copie...  9.22 us
    pallas_call x1, Pallas kernels, on_device(): pl.pallas_call(functools.partial(solve_kernel, plan, sources), out_shape=...  8.06 us
    pallas_call x1, Pallas kernels, on_device(): return (sigma, spread(place, *back))  3.89 us
    unnamed x94, local copies, waits for them, and re-layouts  3.76 us
    dynamic_slice x5, local copies, waits for them, and re-layouts, on_device(): lax.dynamic_index_in_dim(right, r ^ s, 0, keepdims=False)  3.7 us
    pallas_call x1, Pallas kernels, on_device(): pl.pallas_call(functools.partial(place_kernel, plan), out_shape=jax.Shape...  2.95 us
  transfers between devices with their start and end apart: 37, of which 12 were waited for; matrix products, arithmetic and copies ran while one was open for 8% of the time, Pallas kernels for 5%

profile of v11, /device:TPU:25, one launch (start us, length us, event | category | flops | bytes accessed | tf_op | source)
XLA Modules:
  0.0 141.2 jit_solution(6740703408488338475)
XLA Ops:
  0.7 2.0 %constant_dynamic-slice_fusion = (bf16[2,2,96,384]{3,2,1,0:T(8,128)(2,1)}, bf16[2,2,96,384]{3,2,1,0:T(8,128)(2,1)}) fusion(bf16[2,2,384,384]{3,2,1,0:T(8,128)(2,1)} %refs_0_.3, s32[]{:T(128)S(6)} %select_n.117, s32[]{:T(128)S(6)} %select_n.109), kind=kLoop, calls=%fused_computation.28 | loop fusion | bytes 1179656 | tf_op jit(solution)/shard_map/dynamic_slice | solution.py:336
  2.7 1.2 collective-permute-start.1
  3.9 0.8 copy.11
  4.8 0.9 dynamic-slice_bitcast_fusion.2
  5.9 0.9 dynamic-slice_bitcast_fusion
  6.8 1.2 collective-permute-start
  8.5 2.0 %copy.12 = bf16[2,384,2,384]{1,3,2,0:T(8,128)(2,1)S(1)} copy(bf16[2,384,2,384]{3,2,1,0:T(2,128)(2,1)S(1)} %copy-done.12) | data formatting | bytes 2359296 | tf_op jit(solution)/shard_map/optimization_barrier | solution.py:292
  11.4 1.2 collective-permute-start.2
  13.5 0.9 copy.17
  14.4 0.9 copy.16
  15.3 0.9 copy.15
  16.2 0.9 copy.14
  17.1 3.5 %collective-permute-done = bf16[2,384,384]{2,1,0:T(8,128)(2,1)S(1)} collective-permute-done((bf16[2,384,384]{2,1,0:T(8,128)(2,1)}, bf16[2,384,384]{2,1,0:T(8,128)(2,1)S(1)}, u32[]{:S(2)}, u32[]{:S(2)}) %collective-permute-start) | collective-permute-done | bytes 589856 | tf_op jit(solution)/shard_map/ppermute | solution.py:46
  20.7 4.5 %self_energy.2 = (bf16[2,96,384]{2,1,0:T(8,128)(2,1)}, bf16[2,96,384]{2,1,0:T(8,128)(2,1)}, bf16[2,96,384]{2,1,0:T(8,128)(2,1)}, bf16[2,96,384]{2,1,0:T(8,128)(2,1)}) custom-call(s32[3]{0:T(128)} %pad_add_fusion.place, s32[4,8]{1,0:T(4,128)} %fusion.1.quads, s32[4,8]{1,0:T(4,128)} %slice_bitcast_fusion.4.thirds, bf16[2,2,384,384]{3,2,1,0:T(8,128)(2,1)} %refs_0_.3, ...), custom_call_target="tpu_custom_call" | custom-call | tf_op jit(solution)/shard_map/self_energy/pallas_call | solution.py:368
  25.2 4.5 %collective-permute-done.3.refs_3_ = bf16[2,2,96,384]{3,2,1,0:T(8,128)(2,1)S(1)} collective-permute-done((bf16[2,2,96,384]{3,2,1,0:T(8,128)(2,1)}, bf16[2,2,96,384]{3,2,1,0:T(8,128)(2,1)S(1)}, u32[]{:S(2)}, u32[]{:S(2)}) %collective-permute-start.3) | collective-permute-done | bytes 294944 | tf_op jit(solution)/shard_map/ppermute | solution.py:46
  29.7 0.7 copy-done.35
  30.4 4.7 %self_energy.3 = (bf16[2,192,384]{2,1,0:T(8,128)(2,1)}, bf16[2,192,384]{2,1,0:T(8,128)(2,1)}, bf16[2,192,384]{2,1,0:T(8,128)(2,1)}, bf16[2,192,384]{2,1,0:T(8,128)(2,1)}) custom-call(s32[3]{0:T(128)} %pad_add_fusion.place, s32[4,8]{1,0:T(4,128)} %fusion.1.quads, s32[4,8]{1,0:T(4,128)} %slice_bitcast_fusion.4.thirds, bf16[2,2,384,384]{3,2,1,0:T(8,128)(2,1)} %refs_0_.3, ...), custom_call_target="tpu_custom_call" | custom-call | tf_op jit(solution)/shard_map/self_energy/pallas_call | solution.py:368
  35.2 0.8 collective-permute-start.12
  36.0 1.3 collective-permute-start.5
  38.2 1.3 collective-permute-start.15
  39.5 0.7 collective-permute-start.13
  40.2 3.1 %collective-permute-done.5.refs_2_ = bf16[2,192,384]{2,1,0:T(8,128)(2,1)S(1)} collective-permute-done((bf16[2,192,384]{2,1,0:T(8,128)(2,1)}, bf16[2,192,384]{2,1,0:T(8,128)(2,1)S(1)}, u32[]{:S(2)}, u32[]{:S(2)}) %collective-permute-start.5) | collective-permute-done | bytes 294944 | tf_op jit(solution)/shard_map/ppermute | solution.py:46
  44.2 5.4 %collective-permute-done.15.refs_12_ = bf16[2,192,384]{2,1,0:T(8,128)(2,1)S(1)} collective-permute-done((bf16[2,192,384]{2,1,0:T(8,128)(2,1)S(1)}, bf16[2,192,384]{2,1,0:T(8,128)(2,1)S(1)}, u32[]{:S(2)}, u32[]{:S(2)}) %collective-permute-start.15) | collective-permute-done | bytes 294944 | tf_op jit(solution)/shard_map/ppermute | solution.py:46
  49.6 1.3 collective-permute-start.17
  51.3 1.4 %collective-permute-start.16 = (bf16[2,192,384]{2,1,0:T(8,128)(2,1)S(1)}, bf16[2,192,384]{2,1,0:T(8,128)(2,1)S(1)}, u32[]{:S(2)}, u32[]{:S(2)}) collective-permute-start(bf16[2,192,384]{2,1,0:T(8,128)(2,1)S(1)} %get-tuple-element.70), channel_id=1, source_target_pairs={{0,2},{1,3},{2,4},{3,5},{8,10},{9,11},{10,12},{11,13},{12,14},{13,... | collective-permute-start | bytes 884744 | tf_op jit(solution)/shard_map/ppermute | solution.py:46
  52.8 9.0 %collective-permute-done.17.refs_14_ = bf16[2,192,384]{2,1,0:T(8,128)(2,1)S(1)} collective-permute-done((bf16[2,192,384]{2,1,0:T(8,128)(2,1)S(1)}, bf16[2,192,384]{2,1,0:T(8,128)(2,1)S(1)}, u32[]{:S(2)}, u32[]{:S(2)}) %collective-permute-start.17) | collective-permute-done | bytes 294944 | tf_op jit(solution)/shard_map/ppermute | solution.py:46
  61.7 0.8 collective-permute-start.11
  62.6 3.8 %collective-permute-start.26 = (bf16[2,192,384]{2,1,0:T(8,128)(2,1)S(1)}, bf16[2,192,384]{2,1,0:T(8,128)(2,1)S(1)}, u32[]{:S(2)}, u32[]{:S(2)}) collective-permute-start(bf16[2,192,384]{2,1,0:T(8,128)(2,1)S(1)} %collective-permute-done.15.refs_12_), channel_id=1, source_target_pairs={{0,8},{1,9},{2,10},{3,11},{4,12},{5,13},{6,14},{7,15},{8,0},{9,1},... | collective-permute-start | bytes 884744 | tf_op jit(solution)/shard_map/ppermute | solution.py:46
  67.3 1.3 collective-permute-start.19
  68.6 1.3 collective-permute-start.18
  70.0 3.9 %collective-permute-start.7 = (bf16[384,768]{1,0:T(8,128)(2,1)S(1)}, bf16[384,768]{1,0:T(8,128)(2,1)S(1)}, u32[]{:S(2)}, u32[]{:S(2)}) collective-permute-start(bf16[384,768]{1,0:T(8,128)(2,1)S(1)} %pad_maximum_fusion.refs_0_), channel_id=1, source_target_pairs={{0,8},{1,9},{2,10},{3,11},{4,12},{5,13},{6,14},{7,15},{8,0},{9,1},... | collective-permute-start | bytes 1769480 | tf_op jit(solution)/shard_map/ppermute | solution.py:46
  74.1 1.3 collective-permute-start.21
  75.5 8.2 %collective-permute-done.19.refs_16_ = bf16[2,192,384]{2,1,0:T(8,128)(2,1)S(1)} collective-permute-done((bf16[2,192,384]{2,1,0:T(8,128)(2,1)S(1)}, bf16[2,192,384]{2,1,0:T(8,128)(2,1)S(1)}, u32[]{:S(2)}, u32[]{:S(2)}) %collective-permute-start.19) | collective-permute-done | bytes 294944 | tf_op jit(solution)/shard_map/ppermute | solution.py:46
  84.1 12.2 %collective-permute-done.18.refs_15_ = bf16[2,192,384]{2,1,0:T(8,128)(2,1)S(1)} collective-permute-done((bf16[2,192,384]{2,1,0:T(8,128)(2,1)S(1)}, bf16[2,192,384]{2,1,0:T(8,128)(2,1)S(1)}, u32[]{:S(2)}, u32[]{:S(2)}) %collective-permute-start.18) | collective-permute-done | bytes 294944 | tf_op jit(solution)/shard_map/ppermute | solution.py:46
  97.0 1.5 %collective-permute-start.20 = (bf16[2,192,384]{2,1,0:T(8,128)(2,1)S(1)}, bf16[2,192,384]{2,1,0:T(8,128)(2,1)S(1)}, u32[]{:S(2)}, u32[]{:S(2)}) collective-permute-start(bf16[2,192,384]{2,1,0:T(8,128)(2,1)S(1)} %broadcast_select_fusion.3), channel_id=1, source_target_pairs={{4,6},{5,7},{8,12},{9,13},{12,14},{13,15},{20,22},{21,23},{24,28},... | collective-permute-start | bytes 884744 | tf_op jit(solution)/shard_map/ppermute | solution.py:46
  99.6 7.4 %collective-permute-done.20.refs_17_ = bf16[2,192,384]{2,1,0:T(8,128)(2,1)S(1)} collective-permute-done((bf16[2,192,384]{2,1,0:T(8,128)(2,1)S(1)}, bf16[2,192,384]{2,1,0:T(8,128)(2,1)S(1)}, u32[]{:S(2)}, u32[]{:S(2)}) %collective-permute-start.20) | collective-permute-done | bytes 294944 | tf_op jit(solution)/shard_map/ppermute | solution.py:46
  107.0 1.2 collective-permute-start.31
  108.3 1.2 collective-permute-done.31.refs_28_
  110.2 0.8 copy-done.20
  111.0 8.1 %substitution.1 = (bf16[384,384]{1,0:T(8,128)(2,1)}, bf16[384,384]{1,0:T(8,128)(2,1)}, bf16[384,384]{1,0:T(8,128)(2,1)}, bf16[384,384]{1,0:T(8,128)(2,1)}) custom-call(s32[3]{0:T(128)} %pad_add_fusion.place, bf16[384,768]{1,0:T(8,128)(2,1)} %copy-done.3, bf16[384,768]{1,0:T(8,128)(2,1)} %copy-done.15, bf16[384,768]{1,0:T(8,128)(2,1)} %copy-done.4, ...), custom_call_target="tpu_custom_call" | custom-call | tf_op jit(solution)/shard_map/substitution/pallas_call | solution.py:494
  119.1 1.4 %collective-permute-start.33 = (bf16[2,192,384]{2,1,0:T(8,128)(2,1)S(1)}, bf16[2,192,384]{2,1,0:T(8,128)(2,1)S(1)}, u32[]{:S(2)}, u32[]{:S(2)}) collective-permute-start(bf16[2,192,384]{2,1,0:T(8,128)(2,1)S(1)} %copy-done.46), channel_id=1, source_target_pairs={{0,1},{1,0},{2,3},{3,2},{4,5},{5,4},{6,7},{7,6},{8,9},{9,8},{10,11... | collective-permute-start | bytes 884744 | tf_op jit(solution)/shard_map/ppermute | solution.py:46
  121.6 1.2 collective-permute-start.36
  122.8 4.6 %collective-permute-done.33.refs_3_ = bf16[2,192,384]{2,1,0:T(8,128)(2,1)S(1)} collective-permute-done((bf16[2,192,384]{2,1,0:T(8,128)(2,1)S(1)}, bf16[2,192,384]{2,1,0:T(8,128)(2,1)S(1)}, u32[]{:S(2)}, u32[]{:S(2)}) %collective-permute-start.33) | collective-permute-done | bytes 294944 | tf_op jit(solution)/shard_map/ppermute | solution.py:46
  127.4 0.7 copy-done.41
  128.1 2.9 %place_sigma.1 = bf16[2,2,384,384]{3,2,1,0:T(8,128)(2,1)} custom-call(s32[3]{0:T(128)} %pad_add_fusion.place, bf16[2,192,384]{2,1,0:T(8,128)(2,1)} %get-tuple-element.60.refs_0_, bf16[2,192,384]{2,1,0:T(8,128)(2,1)} %get-tuple-element.61.refs_1_, bf16[2,192,384]{2,1,0:T(8,128)(2,1)} %copy-done.10, bf16[2,192,384]{2,1,0:T(8,128)(2,1)} %copy-done.41), custom_call_target="tpu_custom_call" | custom-call | tf_op jit(solution)/shard_map/place_sigma/pallas_call | solution.py:511
  131.1 5.3 %collective-permute-done.36.refs_3_ = bf16[384,384]{1,0:T(8,128)(2,1)S(1)} collective-permute-done((bf16[384,384]{1,0:T(8,128)(2,1)}, bf16[384,384]{1,0:T(8,128)(2,1)S(1)}, u32[]{:S(2)}, u32[]{:S(2)}) %collective-permute-start.36) | collective-permute-done | bytes 294944 | tf_op jit(solution)/shard_map/ppermute | solution.py:46
  136.4 0.8 copy-done.40
  137.2 3.9 %place_solution.1 = bf16[2,384,2,384]{3,2,1,0:T(2,128)(2,1)} custom-call(s32[3]{0:T(128)} %pad_add_fusion.place, bf16[384,384]{1,0:T(8,128)(2,1)} %get-tuple-element.86.refs_0_, bf16[384,384]{1,0:T(8,128)(2,1)} %copy-done.38, bf16[384,384]{1,0:T(8,128)(2,1)} %copy-done.39, bf16[384,384]{1,0:T(8,128)(2,1)} %copy-done.40), custom_call_target="tpu_custom_call" | custom-call | tf_op jit(solution)/shard_map/place_solution/pallas_call | solution.py:530
  (153 shorter events, 9.7 us)
Async XLA Ops:
  2.7 8.7 %collective-permute-start.1 = (bf16[2,2,96,384]{3,2,1,0:T(8,128)(2,1)}, bf16[2,2,96,384]{3,2,1,0:T(8,128)(2,1)}, u32[]{:S(2)}, u32[]{:S(2)}) collective-permute-start(bf16[2,2,96,384]{3,2,1,0:T(8,128)(2,1)} %get-tuple-element.95), channel_id=1, source_target_pairs={{0,1},{1,0},{2,3},{3,2},{4,5},{5,4},{6,7},{7,6},{8,9},{9,8},{10,11... | collective-permute-start | bytes 884744 | tf_op jit(solution)/shard_map/ppermute | solution.py:46
  5.7 15.0 %collective-permute-start.4 = (bf16[2,2,96,384]{3,2,1,0:T(8,128)(2,1)}, bf16[2,2,96,384]{3,2,1,0:T(8,128)(2,1)}, u32[]{:S(2)}, u32[]{:S(2)}) collective-permute-start(bf16[2,2,96,384]{3,2,1,0:T(8,128)(2,1)} %get-tuple-element.93), channel_id=1, source_target_pairs={{0,1},{1,0},{2,3},{3,2},{4,5},{5,4},{6,7},{7,6},{8,9},{9,8},{10,11... | collective-permute-start | bytes 884744 | tf_op jit(solution)/shard_map/ppermute | solution.py:46
  6.8 13.8 %collective-permute-start = (bf16[2,384,384]{2,1,0:T(8,128)(2,1)}, bf16[2,384,384]{2,1,0:T(8,128)(2,1)S(1)}, u32[]{:S(2)}, u32[]{:S(2)}) collective-permute-start(bf16[2,384,384]{2,1,0:T(8,128)(2,1)} %dynamic-slice_bitcast_fusion), channel_id=1, source_target_pairs={{0,16},{1,17},{2,18},{3,19},{4,20},{5,21},{6,22},{7,23},{8,24},{9,... | collective-permute-start | bytes 1769480 | tf_op jit(solution)/shard_map/ppermute | solution.py:46
  11.4 13.8 %collective-permute-start.2 = (bf16[2,2,96,384]{3,2,1,0:T(8,128)(2,1)}, bf16[2,2,96,384]{3,2,1,0:T(8,128)(2,1)S(1)}, u32[]{:S(2)}, u32[]{:S(2)}) collective-permute-start(bf16[2,2,96,384]{3,2,1,0:T(8,128)(2,1)} %get-tuple-element.54), channel_id=1, source_target_pairs={{0,1},{1,0},{2,3},{3,2},{4,5},{5,4},{6,7},{7,6},{8,9},{9,8},{10,11... | collective-permute-start | bytes 884744 | tf_op jit(solution)/shard_map/ppermute | solution.py:46
  12.6 17.1 %collective-permute-start.3 = (bf16[2,2,96,384]{3,2,1,0:T(8,128)(2,1)}, bf16[2,2,96,384]{3,2,1,0:T(8,128)(2,1)S(1)}, u32[]{:S(2)}, u32[]{:S(2)}) collective-permute-start(bf16[2,2,96,384]{3,2,1,0:T(8,128)(2,1)} %get-tuple-element.55), channel_id=1, source_target_pairs={{0,1},{1,0},{2,3},{3,2},{4,5},{5,4},{6,7},{7,6},{8,9},{9,8},{10,11... | collective-permute-start | bytes 884744 | tf_op jit(solution)/shard_map/ppermute | solution.py:46
  35.2 2.9 %collective-permute-start.12 = (bf16[2,192,384]{2,1,0:T(8,128)(2,1)}, bf16[2,192,384]{2,1,0:T(8,128)(2,1)S(1)}, u32[]{:S(2)}, u32[]{:S(2)}) collective-permute-start(bf16[2,192,384]{2,1,0:T(8,128)(2,1)} %get-tuple-element.61.refs_1_), channel_id=1, source_target_pairs={{8,24},{9,25},{16,0},{17,1},{18,2},{19,3},{24,8},{25,9},{26,10},{2... | collective-permute-start | bytes 884744 | tf_op jit(solution)/shard_map/ppermute | solution.py:46
  36.0 7.2 %collective-permute-start.5 = (bf16[2,192,384]{2,1,0:T(8,128)(2,1)}, bf16[2,192,384]{2,1,0:T(8,128)(2,1)S(1)}, u32[]{:S(2)}, u32[]{:S(2)}) collective-permute-start(bf16[2,192,384]{2,1,0:T(8,128)(2,1)} %get-tuple-element.62), channel_id=1, source_target_pairs={{0,1},{1,0},{2,3},{3,2},{4,5},{5,4},{6,7},{7,6},{8,9},{9,8},{10,11... | collective-permute-start | bytes 884744 | tf_op jit(solution)/shard_map/ppermute | solution.py:46
  37.3 5.9 %collective-permute-start.6 = (bf16[2,192,384]{2,1,0:T(8,128)(2,1)}, bf16[2,192,384]{2,1,0:T(8,128)(2,1)S(1)}, u32[]{:S(2)}, u32[]{:S(2)}) collective-permute-start(bf16[2,192,384]{2,1,0:T(8,128)(2,1)} %get-tuple-element.85), channel_id=1, source_target_pairs={{8,25},{9,24},{16,1},{17,0},{18,3},{19,2},{24,9},{25,8},{26,11},{2... | collective-permute-start | bytes 884744 | tf_op jit(solution)/shard_map/ppermute | solution.py:46
  38.2 11.4 %collective-permute-start.15 = (bf16[2,192,384]{2,1,0:T(8,128)(2,1)S(1)}, bf16[2,192,384]{2,1,0:T(8,128)(2,1)S(1)}, u32[]{:S(2)}, u32[]{:S(2)}) collective-permute-start(bf16[2,192,384]{2,1,0:T(8,128)(2,1)S(1)} %get-tuple-element.100), channel_id=1, source_target_pairs={{0,2},{1,3},{2,4},{3,5},{8,10},{9,11},{10,12},{11,13},{12,14},{13,... | collective-permute-start | bytes 884744 | tf_op jit(solution)/shard_map/ppermute | solution.py:46
  39.5 10.1 %collective-permute-start.13 = (bf16[2,192,384]{2,1,0:T(8,128)(2,1)S(1)}, bf16[2,192,384]{2,1,0:T(8,128)(2,1)S(1)}, u32[]{:S(2)}, u32[]{:S(2)}) collective-permute-start(bf16[2,192,384]{2,1,0:T(8,128)(2,1)S(1)} %get-tuple-element.100), channel_id=1, source_target_pairs={{2,0},{3,1},{10,8},{11,9},{12,10},{13,11},{18,16},{19,17},{26,24},... | collective-permute-start | bytes 884744 | tf_op jit(solution)/shard_map/ppermute | solution.py:46
  43.3 19.3 %collective-permute-start.14 = (bf16[2,192,384]{2,1,0:T(8,128)(2,1)S(1)}, bf16[2,192,384]{2,1,0:T(8,128)(2,1)S(1)}, u32[]{:S(2)}, u32[]{:S(2)}) collective-permute-start(bf16[2,192,384]{2,1,0:T(8,128)(2,1)S(1)} %get-tuple-element.70), channel_id=1, source_target_pairs={{2,0},{3,1},{10,8},{11,9},{12,10},{13,11},{18,16},{19,17},{26,24},... | collective-permute-start | bytes 884744 | tf_op jit(solution)/shard_map/ppermute | solution.py:46
  49.6 17.2 %copy-start.21 = (bf16[2,192,384]{2,1,0:T(8,128)(2,1)}, bf16[2,192,384]{2,1,0:T(8,128)(2,1)S(1)}, u32[]{:S(2)}) copy-start(bf16[2,192,384]{2,1,0:T(8,128)(2,1)S(1)} %collective-permute-done.13.refs_10_) | copy-start | bytes 884740
  49.6 12.1 %collective-permute-start.17 = (bf16[2,192,384]{2,1,0:T(8,128)(2,1)S(1)}, bf16[2,192,384]{2,1,0:T(8,128)(2,1)S(1)}, u32[]{:S(2)}, u32[]{:S(2)}) collective-permute-start(bf16[2,192,384]{2,1,0:T(8,128)(2,1)S(1)} %broadcast_select_fusion.6), channel_id=1, source_target_pairs={{2,4},{3,5},{4,6},{5,7},{8,10},{9,11},{10,12},{11,13},{12,14},{13,... | collective-permute-start | bytes 884744 | tf_op jit(solution)/shard_map/ppermute | solution.py:46
  51.0 32.7 %copy-start.1 = (bf16[2,384,384]{2,1,0:T(8,128)(2,1)}, bf16[2,384,384]{2,1,0:T(8,128)(2,1)S(1)}, u32[]{:S(2)}) copy-start(bf16[2,384,384]{2,1,0:T(8,128)(2,1)S(1)} %pad_maximum_fusion.3.refs_9_) | copy-start | bytes 1769476
  51.0 15.7 %collective-permute-start.9 = (bf16[384,384]{1,0:T(8,128)(2,1)S(1)}, bf16[384,384]{1,0:T(8,128)(2,1)S(1)}, u32[]{:S(2)}, u32[]{:S(2)}) collective-permute-start(bf16[384,384]{1,0:T(8,128)(2,1)S(1)} %bitcast.44), channel_id=1, source_target_pairs={{0,8},{1,9},{2,10},{3,11},{4,12},{5,13},{6,14},{7,15},{8,0},{9,1},... | collective-permute-start | bytes 884744 | tf_op jit(solution)/shard_map/ppermute | solution.py:46
  51.1 16.2 %collective-permute-start.10 = (bf16[384,384]{1,0:T(8,128)(2,1)S(1)}, bf16[384,384]{1,0:T(8,128)(2,1)S(1)}, u32[]{:S(2)}, u32[]{:S(2)}) collective-permute-start(bf16[384,384]{1,0:T(8,128)(2,1)S(1)} %bitcast.43), channel_id=1, source_target_pairs={{0,16},{1,17},{2,18},{3,19},{4,20},{5,21},{6,22},{7,23},{8,24},{9,... | collective-permute-start | bytes 884744 | tf_op jit(solution)/shard_map/ppermute | solution.py:46
  51.2 22.7 %copy-start.2 = (bf16[2,384,384]{2,1,0:T(8,128)(2,1)}, bf16[2,384,384]{2,1,0:T(8,128)(2,1)S(1)}, u32[]{:S(2)}) copy-start(bf16[2,384,384]{2,1,0:T(8,128)(2,1)S(1)} %pad_maximum_fusion.2.refs_8_) | copy-start | bytes 1769476
  51.3 15.5 %collective-permute-start.16 = (bf16[2,192,384]{2,1,0:T(8,128)(2,1)S(1)}, bf16[2,192,384]{2,1,0:T(8,128)(2,1)S(1)}, u32[]{:S(2)}, u32[]{:S(2)}) collective-permute-start(bf16[2,192,384]{2,1,0:T(8,128)(2,1)S(1)} %get-tuple-element.70), channel_id=1, source_target_pairs={{0,2},{1,3},{2,4},{3,5},{8,10},{9,11},{10,12},{11,13},{12,14},{13,... | collective-permute-start | bytes 884744 | tf_op jit(solution)/shard_map/ppermute | solution.py:46
  52.7 17.3 %copy-start.3 = (bf16[384,768]{1,0:T(8,128)(2,1)}, bf16[384,768]{1,0:T(8,128)(2,1)S(1)}, u32[]{:S(2)}) copy-start(bf16[384,768]{1,0:T(8,128)(2,1)S(1)} %pad_maximum_fusion.refs_0_) | copy-start | bytes 1769476
  61.7 35.0 %copy-start.6 = (bf16[2,192,384]{2,1,0:T(8,128)(2,1)}, bf16[2,192,384]{2,1,0:T(8,128)(2,1)S(1)}, u32[]{:S(2)}) copy-start(bf16[2,192,384]{2,1,0:T(8,128)(2,1)S(1)} %collective-permute-done.17.refs_14_) | copy-start | bytes 884740
  61.7 6.9 %collective-permute-start.11 = (bf16[384,384]{1,0:T(8,128)(2,1)S(1)}, bf16[384,384]{1,0:T(8,128)(2,1)S(1)}, u32[]{:S(2)}, u32[]{:S(2)}) collective-permute-start(bf16[384,384]{1,0:T(8,128)(2,1)S(1)} %bitcast.42), channel_id=1, source_target_pairs={{0,24},{1,25},{2,26},{3,27},{4,28},{5,29},{6,30},{7,31},{8,16},{9,... | collective-permute-start | bytes 884744 | tf_op jit(solution)/shard_map/ppermute | solution.py:46
  62.6 7.4 %collective-permute-start.26 = (bf16[2,192,384]{2,1,0:T(8,128)(2,1)S(1)}, bf16[2,192,384]{2,1,0:T(8,128)(2,1)S(1)}, u32[]{:S(2)}, u32[]{:S(2)}) collective-permute-start(bf16[2,192,384]{2,1,0:T(8,128)(2,1)S(1)} %collective-permute-done.15.refs_12_), channel_id=1, source_target_pairs={{0,8},{1,9},{2,10},{3,11},{4,12},{5,13},{6,14},{7,15},{8,0},{9,1},... | collective-permute-start | bytes 884744 | tf_op jit(solution)/shard_map/ppermute | solution.py:46
  66.7 32.2 %copy-start.7 = (bf16[2,192,384]{2,1,0:T(8,128)(2,1)}, bf16[2,192,384]{2,1,0:T(8,128)(2,1)S(1)}, u32[]{:S(2)}) copy-start(bf16[2,192,384]{2,1,0:T(8,128)(2,1)S(1)} %collective-permute-done.16.refs_13_) | copy-start | bytes 884740
  66.7 7.2 %collective-permute-start.24 = (bf16[2,192,384]{2,1,0:T(8,128)(2,1)S(1)}, bf16[2,192,384]{2,1,0:T(8,128)(2,1)S(1)}, u32[]{:S(2)}, u32[]{:S(2)}) collective-permute-start(bf16[2,192,384]{2,1,0:T(8,128)(2,1)S(1)} %collective-permute-done.13.refs_10_), channel_id=1, source_target_pairs={{0,8},{1,9},{2,10},{3,11},{4,12},{5,13},{6,14},{7,15},{8,0},{9,1},... | collective-permute-start | bytes 884744 | tf_op jit(solution)/shard_map/ppermute | solution.py:46
  66.7 7.3 %collective-permute-start.25 = (bf16[2,192,384]{2,1,0:T(8,128)(2,1)S(1)}, bf16[2,192,384]{2,1,0:T(8,128)(2,1)S(1)}, u32[]{:S(2)}, u32[]{:S(2)}) collective-permute-start(bf16[2,192,384]{2,1,0:T(8,128)(2,1)S(1)} %collective-permute-done.14.refs_11_), channel_id=1, source_target_pairs={{0,8},{1,9},{2,10},{3,11},{4,12},{5,13},{6,14},{7,15},{8,0},{9,1},... | collective-permute-start | bytes 884744 | tf_op jit(solution)/shard_map/ppermute | solution.py:46
  67.3 16.4 %collective-permute-start.19 = (bf16[2,192,384]{2,1,0:T(8,128)(2,1)S(1)}, bf16[2,192,384]{2,1,0:T(8,128)(2,1)S(1)}, u32[]{:S(2)}, u32[]{:S(2)}) collective-permute-start(bf16[2,192,384]{2,1,0:T(8,128)(2,1)S(1)} %broadcast_select_fusion.4), channel_id=1, source_target_pairs={{4,6},{5,7},{8,12},{9,13},{12,14},{13,15},{20,22},{21,23},{24,28},... | collective-permute-start | bytes 884744 | tf_op jit(solution)/shard_map/ppermute | solution.py:46
  68.6 27.7 %collective-permute-start.18 = (bf16[2,192,384]{2,1,0:T(8,128)(2,1)S(1)}, bf16[2,192,384]{2,1,0:T(8,128)(2,1)S(1)}, u32[]{:S(2)}, u32[]{:S(2)}) collective-permute-start(bf16[2,192,384]{2,1,0:T(8,128)(2,1)S(1)} %broadcast_select_fusion.5), channel_id=1, source_target_pairs={{2,4},{3,5},{4,6},{5,7},{8,10},{9,11},{10,12},{11,13},{12,14},{13,... | collective-permute-start | bytes 884744 | tf_op jit(solution)/shard_map/ppermute | solution.py:46
  70.0 26.7 %collective-permute-start.7 = (bf16[384,768]{1,0:T(8,128)(2,1)S(1)}, bf16[384,768]{1,0:T(8,128)(2,1)S(1)}, u32[]{:S(2)}, u32[]{:S(2)}) collective-permute-start(bf16[384,768]{1,0:T(8,128)(2,1)S(1)} %pad_maximum_fusion.refs_0_), channel_id=1, source_target_pairs={{0,8},{1,9},{2,10},{3,11},{4,12},{5,13},{6,14},{7,15},{8,0},{9,1},... | collective-permute-start | bytes 1769480 | tf_op jit(solution)/shard_map/ppermute | solution.py:46
  74.0 23.0 %collective-permute-start.22 = (bf16[2,384,384]{2,1,0:T(8,128)(2,1)S(1)}, bf16[2,384,384]{2,1,0:T(8,128)(2,1)S(1)}, u32[]{:S(2)}, u32[]{:S(2)}) collective-permute-start(bf16[2,384,384]{2,1,0:T(8,128)(2,1)S(1)} %pad_maximum_fusion.2.refs_8_), channel_id=1, source_target_pairs={{0,8},{1,9},{2,10},{3,11},{4,12},{5,13},{6,14},{7,15},{8,0},{9,1},... | collective-permute-start | bytes 1769480 | tf_op jit(solution)/shard_map/ppermute | solution.py:46
  74.1 34.2 %copy-start.28 = (bf16[2,192,384]{2,1,0:T(8,128)(2,1)}, bf16[2,192,384]{2,1,0:T(8,128)(2,1)S(1)}, u32[]{:S(2)}) copy-start(bf16[2,192,384]{2,1,0:T(8,128)(2,1)S(1)} %collective-permute-done.25.refs_22_) | copy-start | bytes 884740
  74.1 24.4 %collective-permute-start.21 = (bf16[2,384,384]{2,1,0:T(8,128)(2,1)S(1)}, bf16[2,384,384]{2,1,0:T(8,128)(2,1)S(1)}, u32[]{:S(2)}, u32[]{:S(2)}) collective-permute-start(bf16[2,384,384]{2,1,0:T(8,128)(2,1)S(1)} %broadcast_select_fusion), channel_id=1, source_target_pairs={{8,14},{9,15},{12,8},{13,9},{24,30},{25,31},{28,24},{29,25}} | collective-permute-start | bytes 1769480 | tf_op jit(solution)/shard_map/ppermute | solution.py:46
  75.4 34.0 %copy-start.4 = (bf16[384,768]{1,0:T(8,128)(2,1)}, bf16[384,768]{1,0:T(8,128)(2,1)S(1)}, u32[]{:S(2)}) copy-start(bf16[384,768]{1,0:T(8,128)(2,1)S(1)} %pad_maximum_fusion.1.refs_2_) | copy-start | bytes 1769476
  83.7 25.8 %copy-start.29 = (bf16[2,192,384]{2,1,0:T(8,128)(2,1)}, bf16[2,192,384]{2,1,0:T(8,128)(2,1)S(1)}, u32[]{:S(2)}) copy-start(bf16[2,192,384]{2,1,0:T(8,128)(2,1)S(1)} %collective-permute-done.19.refs_16_) | copy-start | bytes 884740
  83.7 15.2 %collective-permute-start.23 = (bf16[2,384,384]{2,1,0:T(8,128)(2,1)S(1)}, bf16[2,384,384]{2,1,0:T(8,128)(2,1)S(1)}, u32[]{:S(2)}, u32[]{:S(2)}) collective-permute-start(bf16[2,384,384]{2,1,0:T(8,128)(2,1)S(1)} %pad_maximum_fusion.3.refs_9_), channel_id=1, source_target_pairs={{0,8},{1,9},{2,10},{3,11},{4,12},{5,13},{6,14},{7,15},{8,0},{9,1},... | collective-permute-start | bytes 1769480 | tf_op jit(solution)/shard_map/ppermute | solution.py:46
  96.3 13.2 %copy-start.8 = (bf16[2,192,384]{2,1,0:T(8,128)(2,1)}, bf16[2,192,384]{2,1,0:T(8,128)(2,1)S(1)}, u32[]{:S(2)}) copy-start(bf16[2,192,384]{2,1,0:T(8,128)(2,1)S(1)} %collective-permute-done.18.refs_15_) | copy-start | bytes 884740
  96.3 2.8 %collective-permute-start.8 = (bf16[384,768]{1,0:T(8,128)(2,1)S(1)}, bf16[384,768]{1,0:T(8,128)(2,1)S(1)}, u32[]{:S(2)}, u32[]{:S(2)}) collective-permute-start(bf16[384,768]{1,0:T(8,128)(2,1)S(1)} %pad_maximum_fusion.1.refs_2_), channel_id=1, source_target_pairs={{0,8},{1,9},{2,10},{3,11},{4,12},{5,13},{6,14},{7,15},{8,0},{9,1},... | collective-permute-start | bytes 1769480 | tf_op jit(solution)/shard_map/ppermute | solution.py:46
  96.7 22.3 %copy-start.46 = (bf16[2,192,384]{2,1,0:T(8,128)(2,1)S(1)}, bf16[2,192,384]{2,1,0:T(8,128)(2,1)}, u32[]{:S(2)}) copy-start(bf16[2,192,384]{2,1,0:T(8,128)(2,1)} %get-tuple-element.85) | copy-start | bytes 884740
  96.8 2.7 %collective-permute-start.28 = (bf16[2,192,384]{2,1,0:T(8,128)(2,1)S(1)}, bf16[2,192,384]{2,1,0:T(8,128)(2,1)S(1)}, u32[]{:S(2)}, u32[]{:S(2)}) collective-permute-start(bf16[2,192,384]{2,1,0:T(8,128)(2,1)S(1)} %collective-permute-done.17.refs_14_), channel_id=1, source_target_pairs={{0,8},{1,9},{2,10},{3,11},{4,12},{5,13},{6,14},{7,15},{8,0},{9,1},... | collective-permute-start | bytes 884744 | tf_op jit(solution)/shard_map/ppermute | solution.py:46
  97.0 10.1 %collective-permute-start.20 = (bf16[2,192,384]{2,1,0:T(8,128)(2,1)S(1)}, bf16[2,192,384]{2,1,0:T(8,128)(2,1)S(1)}, u32[]{:S(2)}, u32[]{:S(2)}) collective-permute-start(bf16[2,192,384]{2,1,0:T(8,128)(2,1)S(1)} %broadcast_select_fusion.3), channel_id=1, source_target_pairs={{4,6},{5,7},{8,12},{9,13},{12,14},{13,15},{20,22},{21,23},{24,28},... | collective-permute-start | bytes 884744 | tf_op jit(solution)/shard_map/ppermute | solution.py:46
  98.5 11.0 %collective-permute-start.32 = (bf16[2,384,384]{2,1,0:T(8,128)(2,1)S(1)}, bf16[2,384,384]{2,1,0:T(8,128)(2,1)S(1)}, u32[]{:S(2)}, u32[]{:S(2)}) collective-permute-start(bf16[2,384,384]{2,1,0:T(8,128)(2,1)S(1)} %collective-permute-done.21.refs_18_), channel_id=1, source_target_pairs={{0,8},{1,9},{2,10},{3,11},{4,12},{5,13},{6,14},{7,15},{8,0},{9,1},... | collective-permute-start | bytes 1769480 | tf_op jit(solution)/shard_map/ppermute | solution.py:46
  98.9 9.4 %collective-permute-start.27 = (bf16[2,192,384]{2,1,0:T(8,128)(2,1)S(1)}, bf16[2,192,384]{2,1,0:T(8,128)(2,1)S(1)}, u32[]{:S(2)}, u32[]{:S(2)}) collective-permute-start(bf16[2,192,384]{2,1,0:T(8,128)(2,1)S(1)} %collective-permute-done.16.refs_13_), channel_id=1, source_target_pairs={{0,8},{1,9},{2,10},{3,11},{4,12},{5,13},{6,14},{7,15},{8,0},{9,1},... | collective-permute-start | bytes 884744 | tf_op jit(solution)/shard_map/ppermute | solution.py:46
  99.1 9.2 %collective-permute-start.30 = (bf16[2,192,384]{2,1,0:T(8,128)(2,1)S(1)}, bf16[2,192,384]{2,1,0:T(8,128)(2,1)S(1)}, u32[]{:S(2)}, u32[]{:S(2)}) collective-permute-start(bf16[2,192,384]{2,1,0:T(8,128)(2,1)S(1)} %collective-permute-done.19.refs_16_), channel_id=1, source_target_pairs={{0,8},{1,9},{2,10},{3,11},{4,12},{5,13},{6,14},{7,15},{8,0},{9,1},... | collective-permute-start | bytes 884744 | tf_op jit(solution)/shard_map/ppermute | solution.py:46
  99.5 8.8 %collective-permute-start.29 = (bf16[2,192,384]{2,1,0:T(8,128)(2,1)S(1)}, bf16[2,192,384]{2,1,0:T(8,128)(2,1)S(1)}, u32[]{:S(2)}, u32[]{:S(2)}) collective-permute-start(bf16[2,192,384]{2,1,0:T(8,128)(2,1)S(1)} %collective-permute-done.18.refs_15_), channel_id=1, source_target_pairs={{0,8},{1,9},{2,10},{3,11},{4,12},{5,13},{6,14},{7,15},{8,0},{9,1},... | collective-permute-start | bytes 884744 | tf_op jit(solution)/shard_map/ppermute | solution.py:46
  107.0 2.4 %collective-permute-start.31 = (bf16[2,192,384]{2,1,0:T(8,128)(2,1)S(1)}, bf16[2,192,384]{2,1,0:T(8,128)(2,1)S(1)}, u32[]{:S(2)}, u32[]{:S(2)}) collective-permute-start(bf16[2,192,384]{2,1,0:T(8,128)(2,1)S(1)} %collective-permute-done.20.refs_17_), channel_id=1, source_target_pairs={{0,8},{1,9},{2,10},{3,11},{4,12},{5,13},{6,14},{7,15},{8,0},{9,1},... | collective-permute-start | bytes 884744 | tf_op jit(solution)/shard_map/ppermute | solution.py:46
  119.1 8.3 %collective-permute-start.33 = (bf16[2,192,384]{2,1,0:T(8,128)(2,1)S(1)}, bf16[2,192,384]{2,1,0:T(8,128)(2,1)S(1)}, u32[]{:S(2)}, u32[]{:S(2)}) collective-permute-start(bf16[2,192,384]{2,1,0:T(8,128)(2,1)S(1)} %copy-done.46), channel_id=1, source_target_pairs={{0,1},{1,0},{2,3},{3,2},{4,5},{5,4},{6,7},{7,6},{8,9},{9,8},{10,11... | collective-permute-start | bytes 884744 | tf_op jit(solution)/shard_map/ppermute | solution.py:46
  120.5 10.6 %collective-permute-start.34 = (bf16[384,384]{1,0:T(8,128)(2,1)}, bf16[384,384]{1,0:T(8,128)(2,1)S(1)}, u32[]{:S(2)}, u32[]{:S(2)}) collective-permute-start(bf16[384,384]{1,0:T(8,128)(2,1)} %get-tuple-element.82), channel_id=1, source_target_pairs={{0,8},{1,9},{2,10},{3,11},{4,12},{5,13},{6,14},{7,15},{8,0},{9,1},... | collective-permute-start | bytes 884744 | tf_op jit(solution)/shard_map/ppermute | solution.py:46
  121.1 9.9 %collective-permute-start.35 = (bf16[384,384]{1,0:T(8,128)(2,1)}, bf16[384,384]{1,0:T(8,128)(2,1)S(1)}, u32[]{:S(2)}, u32[]{:S(2)}) collective-permute-start(bf16[384,384]{1,0:T(8,128)(2,1)} %get-tuple-element.83), channel_id=1, source_target_pairs={{0,16},{1,17},{2,18},{3,19},{4,20},{5,21},{6,22},{7,23},{8,24},{9,... | collective-permute-start | bytes 884744 | tf_op jit(solution)/shard_map/ppermute | solution.py:46
  121.6 14.8 %collective-permute-start.36 = (bf16[384,384]{1,0:T(8,128)(2,1)}, bf16[384,384]{1,0:T(8,128)(2,1)S(1)}, u32[]{:S(2)}, u32[]{:S(2)}) collective-permute-start(bf16[384,384]{1,0:T(8,128)(2,1)} %get-tuple-element.84), channel_id=1, source_target_pairs={{0,24},{1,25},{2,26},{3,27},{4,28},{5,29},{6,30},{7,31},{8,16},{9,... | collective-permute-start | bytes 884744 | tf_op jit(solution)/shard_map/ppermute | solution.py:46
  (36 other events, 187.7 us)

commit v12 on v10

--- a/solution.py
+++ b/solution.py
@@ -10,7 +10,7 @@
 from jax.sharding import PartitionSpec as P
 
 AXES = ("row", "col", "mom")
-VMEM_BYTES = 56 * 1024 * 1024
+VMEM_BYTES = 60 * 1024 * 1024
 
 
 class Plan:
@@ -79,7 +79,8 @@
         steps = []
         for key, to in sorted(wanted, key=lambda item: (item[0][0], -item[1], -item[0][1])):
             for step in steps:
-                if key[1] not in step and to not in [goal for _, goal in step.values()]:
+                free = key[1] not in step and to not in [goal for _, goal in step.values()]
+                if free and all(other[0] == key[0] for other, _ in step.values()):
                     break
             else:
                 step = {}
@@ -243,12 +244,6 @@
 
     weight = 1.0 / math.sqrt(side * rows)
 
-    def pick(held, number):
-        value = held[0][...]
-        for n in range(1, len(held)):
-            value = jnp.where(number == n, held[n][...], value)
-        return value
-
     def turn(value):
         return jnp.concatenate([-value[:, width:], value[:, :width]], axis=1)
 
@@ -286,6 +281,24 @@
 
 def after(value, *others):
     return lax.optimization_barrier((value, others))[0]
+
+
+def pick(held, number):
+    value = held[0][...]
+    for n in range(1, len(held)):
+        value = jnp.where(number == n, held[n][...], value)
+    return value
+
+
+def spread_kernel(plan, place, *refs):
+    groups, width = plan.groups, plan.width
+    ins, out = refs[:-1], refs[-1]
+    for m in range(plan.moments):
+        parts = [pick(ins, place[0] ^ (m * groups + g)) for g in range(groups)]
+        for p in range(2):
+            out[m, :, p, :] = jnp.concatenate(
+                [part[:, p * width : (p + 1) * width] for part in parts], axis=1
+            )
 
 
 def on_device(mesh, lesser, greater, triples, diag_inverse, right_side):
@@ -415,7 +428,7 @@
         goal = lambda a, c, m: (a, goals[c][1], m) if c in goals and valid(goals[c][0], a) else None
         return plan.send(choose(values, behind), goal)
 
-    ring, rest = plan.ring(), plan.rest()
+    top, ring, rest = moments - 1, plan.ring(), plan.rest()
     got = [[] for _ in plan.chunks]
 
     def ring_step(q, number, *behind):
@@ -443,7 +456,8 @@
                 behind.append(came[k + 1])
             ring_step(k, number, *behind)
     for number in range(len(rest)):
-        rest_step(number, got[0][1], got[-1][0], right_all)
+        low = any(key[0] < top for key, _ in rest[number].values())
+        rest_step(number, *([got[0][1], got[-1][0], right_all] if low else [got[0][0]]))
 
     buffers = []
 
@@ -489,9 +503,14 @@
 
     back = [solved[0]] + [exchange_row(solved[s], s) for s in range(1, rows)]
     back = after(back, sigma)
-    pieces = jnp.stack([lax.select_n(r ^ s, *back) for s in range(rows)])
-    pieces = pieces.reshape(moments, groups, side, 2, width).transpose(0, 2, 3, 1, 4)
-    return sigma, pieces.reshape(moments, side, 2, side)
+    spread = pl.pallas_call(
+        functools.partial(spread_kernel, plan),
+        out_shape=jax.ShapeDtypeStruct(right_side.shape, bf16),
+        in_specs=[smem()] + [pl.BlockSpec(memory_space=pltpu.VMEM)] * rows,
+        compiler_params=pltpu.CompilerParams(vmem_limit_bytes=VMEM_BYTES // 2),
+        name="place_solution",
+    )
+    return sigma, spread(place, *back)
 
 
 def solution(mesh):

time: 138 us -> 138 us (level)
  the two profiles are of different devices: /device:TPU:0 before, /device:TPU:25 now
where the time goes in v12:
time: 138 us; the launch traced here: 137 us
  waiting for transfers between devices  64.5 us (47%)
  starting transfers between devices  32.4 us (23%)
  Pallas kernels  23 us (17%)
  local copies, waits for them, and re-layouts  14.1 us (10%)
  other arithmetic  1.82 us (1%)
    ppermute x37, waiting for transfers between devices, send(): return lax.ppermute(value, AXES, pairs)  64.5 us
    ppermute x37, starting transfers between devices, send(): return lax.ppermute(value, AXES, pairs)  32.4 us
    pallas_call x2, Pallas kernels, self_energy(): pl.pallas_call(functools.partial(sigma_kernel, plan, pair_count, u, copie...  9.23 us
    pallas_call x1, Pallas kernels, on_device(): pl.pallas_call(functools.partial(solve_kernel, plan, sources), out_shape=...  8.12 us
    dynamic_slice x5, local copies, waits for them, and re-layouts, on_device(): lax.dynamic_index_in_dim(right, r ^ s, 0, keepdims=False)  3.05 us
    pallas_call x1, Pallas kernels, on_device(): pl.pallas_call(functools.partial(place_kernel, plan), out_shape=jax.Shape...  2.95 us
    dynamic_slice x2, local copies, waits for them, and re-layouts, part_of(): lax.dynamic_slice_in_dim(value, (y ^ q) * half + u * plan.sub, plan.sub, 2)  2.95 us
  transfers between devices with their start and end apart: 37, of which 14 were waited for; matrix products, arithmetic and copies ran while one was open for 8% of the time, Pallas kernels for 5%

profile of v12, /device:TPU:25, one launch (start us, length us, event | category | flops | bytes accessed | tf_op | source)
XLA Modules:
  0.0 137.2 jit_solution(8263562121909166153)
XLA Ops:
  0.7 2.1 %constant_dynamic-slice_fusion = (bf16[2,2,96,384]{3,2,1,0:T(8,128)(2,1)}, bf16[2,2,96,384]{3,2,1,0:T(8,128)(2,1)}) fusion(bf16[2,2,384,384]{3,2,1,0:T(8,128)(2,1)} %refs_0_.3, s32[]{:T(128)S(6)} %select_n.109, s32[]{:T(128)S(6)} %select_n.101), kind=kLoop, calls=%fused_computation.27 | loop fusion | bytes 1179656 | tf_op jit(solution)/shard_map/dynamic_slice | solution.py:328
  2.7 1.2 collective-permute-start.1
  4.0 0.8 copy.11
  4.8 0.9 dynamic-slice_bitcast_fusion.2
  5.9 1.9 %dynamic-slice_bitcast_fusion = bf16[2,384,384]{2,1,0:T(8,128)(2,1)} fusion(bf16[2,2,384,384]{3,2,1,0:T(8,128)(2,1)} %param.8, s32[]{:T(128)S(6)} %select_n.108), kind=kLoop, calls=%fused_computation.4 | loop fusion | bytes 1179652 | tf_op jit(solution)/shard_map/jit(dynamic_index_in_dim)/squeeze | solution.py:343
  7.8 1.2 collective-permute-start
  9.6 2.0 %copy.12 = bf16[2,384,2,384]{1,3,2,0:T(8,128)(2,1)S(1)} copy(bf16[2,384,2,384]{3,2,1,0:T(2,128)(2,1)S(1)} %copy-done.14) | data formatting | bytes 2359296 | tf_op jit(solution)/shard_map/optimization_barrier | solution.py:283
  12.5 1.2 collective-permute-start.2
  14.5 0.9 copy.17
  15.4 0.9 copy.16
  16.5 0.9 copy.14
  17.4 4.3 %collective-permute-done = bf16[2,384,384]{2,1,0:T(8,128)(2,1)S(1)} collective-permute-done((bf16[2,384,384]{2,1,0:T(8,128)(2,1)}, bf16[2,384,384]{2,1,0:T(8,128)(2,1)S(1)}, u32[]{:S(2)}, u32[]{:S(2)}) %collective-permute-start) | collective-permute-done | bytes 589856 | tf_op jit(solution)/shard_map/ppermute | solution.py:46
  21.9 4.5 %self_energy.2 = (bf16[2,96,384]{2,1,0:T(8,128)(2,1)}, bf16[2,96,384]{2,1,0:T(8,128)(2,1)}, bf16[2,96,384]{2,1,0:T(8,128)(2,1)}, bf16[2,96,384]{2,1,0:T(8,128)(2,1)}) custom-call(s32[3]{0:T(128)} %pad_add_fusion.place, s32[4,8]{1,0:T(4,128)} %fusion.1.quads, s32[4,8]{1,0:T(4,128)} %slice_bitcast_fusion.4.thirds, bf16[2,2,384,384]{3,2,1,0:T(8,128)(2,1)} %refs_0_.3, ...), custom_call_target="tpu_custom_call" | custom-call | tf_op jit(solution)/shard_map/self_energy/pallas_call | solution.py:360
  26.4 3.5 %collective-permute-done.3.refs_3_ = bf16[2,2,96,384]{3,2,1,0:T(8,128)(2,1)} collective-permute-done((bf16[2,2,96,384]{3,2,1,0:T(8,128)(2,1)}, bf16[2,2,96,384]{3,2,1,0:T(8,128)(2,1)}, u32[]{:S(2)}, u32[]{:S(2)}) %collective-permute-start.3) | collective-permute-done | bytes 294944 | tf_op jit(solution)/shard_map/ppermute | solution.py:46
  29.9 4.7 %self_energy.3 = (bf16[2,192,384]{2,1,0:T(8,128)(2,1)}, bf16[2,192,384]{2,1,0:T(8,128)(2,1)}, bf16[2,192,384]{2,1,0:T(8,128)(2,1)}, bf16[2,192,384]{2,1,0:T(8,128)(2,1)}) custom-call(s32[3]{0:T(128)} %pad_add_fusion.place, s32[4,8]{1,0:T(4,128)} %fusion.1.quads, s32[4,8]{1,0:T(4,128)} %slice_bitcast_fusion.4.thirds, bf16[2,2,384,384]{3,2,1,0:T(8,128)(2,1)} %refs_0_.3, ...), custom_call_target="tpu_custom_call" | custom-call | tf_op jit(solution)/shard_map/self_energy/pallas_call | solution.py:360
  34.6 0.8 collective-permute-start.12
  35.4 1.3 collective-permute-start.5
  36.7 0.8 collective-permute-start.6
  37.7 1.3 collective-permute-start.13
  39.0 3.6 %collective-permute-done.5.refs_2_ = bf16[2,192,384]{2,1,0:T(8,128)(2,1)S(1)} collective-permute-done((bf16[2,192,384]{2,1,0:T(8,128)(2,1)}, bf16[2,192,384]{2,1,0:T(8,128)(2,1)S(1)}, u32[]{:S(2)}, u32[]{:S(2)}) %collective-permute-start.5) | collective-permute-done | bytes 294944 | tf_op jit(solution)/shard_map/ppermute | solution.py:46
  42.7 2.5 %collective-permute-start.9 = (bf16[384,384]{1,0:T(8,128)(2,1)S(1)}, bf16[384,384]{1,0:T(8,128)(2,1)S(1)}, u32[]{:S(2)}, u32[]{:S(2)}) collective-permute-start(bf16[384,384]{1,0:T(8,128)(2,1)S(1)} %bitcast.44), channel_id=1, source_target_pairs={{0,8},{1,9},{2,10},{3,11},{4,12},{5,13},{6,14},{7,15},{8,0},{9,1},... | collective-permute-start | bytes 884744 | tf_op jit(solution)/shard_map/ppermute | solution.py:46
  45.1 1.2 collective-permute-start.10
  47.1 2.1 %collective-permute-done.13.refs_10_ = bf16[2,192,384]{2,1,0:T(8,128)(2,1)S(1)} collective-permute-done((bf16[2,192,384]{2,1,0:T(8,128)(2,1)S(1)}, bf16[2,192,384]{2,1,0:T(8,128)(2,1)S(1)}, u32[]{:S(2)}, u32[]{:S(2)}) %collective-permute-start.13) | collective-permute-done | bytes 294944 | tf_op jit(solution)/shard_map/ppermute | solution.py:46
  49.3 1.3 collective-permute-start.15
  50.7 1.3 collective-permute-start.14
  52.1 1.6 %collective-permute-done.10.refs_6_ = bf16[384,384]{1,0:T(8,128)(2,1)S(1)} collective-permute-done((bf16[384,384]{1,0:T(8,128)(2,1)S(1)}, bf16[384,384]{1,0:T(8,128)(2,1)S(1)}, u32[]{:S(2)}, u32[]{:S(2)}) %collective-permute-start.10) | collective-permute-done | bytes 294944 | tf_op jit(solution)/shard_map/ppermute | solution.py:46
  53.7 1.3 collective-permute-start.22
  55.1 5.4 %collective-permute-done.11.refs_7_ = bf16[384,384]{1,0:T(8,128)(2,1)} collective-permute-done((bf16[384,384]{1,0:T(8,128)(2,1)S(1)}, bf16[384,384]{1,0:T(8,128)(2,1)}, u32[]{:S(2)}, u32[]{:S(2)}) %collective-permute-start.11) | collective-permute-done | bytes 294944 | tf_op jit(solution)/shard_map/ppermute | solution.py:46
  60.6 3.6 %collective-permute-start.8 = (bf16[384,768]{1,0:T(8,128)(2,1)S(1)}, bf16[384,768]{1,0:T(8,128)(2,1)S(1)}, u32[]{:S(2)}, u32[]{:S(2)}) collective-permute-start(bf16[384,768]{1,0:T(8,128)(2,1)S(1)} %pad_maximum_fusion.1.refs_2_), channel_id=1, source_target_pairs={{0,8},{1,9},{2,10},{3,11},{4,12},{5,13},{6,14},{7,15},{8,0},{9,1},... | collective-permute-start | bytes 1769480 | tf_op jit(solution)/shard_map/ppermute | solution.py:46
  64.4 1.9 %collective-permute-done.24.refs_21_ = bf16[2,192,384]{2,1,0:T(8,128)(2,1)S(1)} collective-permute-done((bf16[2,192,384]{2,1,0:T(8,128)(2,1)S(1)}, bf16[2,192,384]{2,1,0:T(8,128)(2,1)S(1)}, u32[]{:S(2)}, u32[]{:S(2)}) %collective-permute-start.24) | collective-permute-done | bytes 294944 | tf_op jit(solution)/shard_map/ppermute | solution.py:46
  66.2 1.3 collective-permute-start.17
  67.5 1.3 collective-permute-start.16
  68.9 0.7 collective-permute-start.21
  70.3 1.3 collective-permute-start.19
  71.6 11.1 %collective-permute-done.17.refs_14_ = bf16[2,192,384]{2,1,0:T(8,128)(2,1)S(1)} collective-permute-done((bf16[2,192,384]{2,1,0:T(8,128)(2,1)S(1)}, bf16[2,192,384]{2,1,0:T(8,128)(2,1)S(1)}, u32[]{:S(2)}, u32[]{:S(2)}) %collective-permute-start.17) | collective-permute-done | bytes 294944 | tf_op jit(solution)/shard_map/ppermute | solution.py:46
  83.0 12.2 %collective-permute-done.16.refs_13_ = bf16[2,192,384]{2,1,0:T(8,128)(2,1)S(1)} collective-permute-done((bf16[2,192,384]{2,1,0:T(8,128)(2,1)S(1)}, bf16[2,192,384]{2,1,0:T(8,128)(2,1)S(1)}, u32[]{:S(2)}, u32[]{:S(2)}) %collective-permute-start.16) | collective-permute-done | bytes 294944 | tf_op jit(solution)/shard_map/ppermute | solution.py:46
  95.7 1.5 %collective-permute-start.18 = (bf16[2,192,384]{2,1,0:T(8,128)(2,1)S(1)}, bf16[2,192,384]{2,1,0:T(8,128)(2,1)S(1)}, u32[]{:S(2)}, u32[]{:S(2)}) collective-permute-start(bf16[2,192,384]{2,1,0:T(8,128)(2,1)S(1)} %broadcast_select_fusion.2), channel_id=1, source_target_pairs={{4,6},{5,7},{8,12},{9,13},{12,14},{13,15},{20,22},{21,23},{24,28},... | collective-permute-start | bytes 884744 | tf_op jit(solution)/shard_map/ppermute | solution.py:46
  99.0 7.1 %collective-permute-done.18.refs_15_ = bf16[2,192,384]{2,1,0:T(8,128)(2,1)S(1)} collective-permute-done((bf16[2,192,384]{2,1,0:T(8,128)(2,1)S(1)}, bf16[2,192,384]{2,1,0:T(8,128)(2,1)S(1)}, u32[]{:S(2)}, u32[]{:S(2)}) %collective-permute-start.18) | collective-permute-done | bytes 294944 | tf_op jit(solution)/shard_map/ppermute | solution.py:46
  106.1 0.9 collective-permute-start.29
  107.0 1.2 collective-permute-done.29.refs_26_
  109.2 0.8 copy-done.24
  110.1 8.1 %substitution.1 = (bf16[384,384]{1,0:T(8,128)(2,1)}, bf16[384,384]{1,0:T(8,128)(2,1)}, bf16[384,384]{1,0:T(8,128)(2,1)}, bf16[384,384]{1,0:T(8,128)(2,1)}) custom-call(s32[3]{0:T(128)} %pad_add_fusion.place, bf16[384,768]{1,0:T(8,128)(2,1)} %copy-done.5, bf16[384,768]{1,0:T(8,128)(2,1)} %copy-done.16, bf16[384,768]{1,0:T(8,128)(2,1)} %copy-done.6, ...), custom_call_target="tpu_custom_call" | custom-call | tf_op jit(solution)/shard_map/substitution/pallas_call | solution.py:478
  119.2 1.6 %collective-permute-start.36 = (bf16[384,384]{1,0:T(8,128)(2,1)}, bf16[384,384]{1,0:T(8,128)(2,1)S(1)}, u32[]{:S(2)}, u32[]{:S(2)}) collective-permute-start(bf16[384,384]{1,0:T(8,128)(2,1)} %get-tuple-element.84), channel_id=1, source_target_pairs={{0,24},{1,25},{2,26},{3,27},{4,28},{5,29},{6,30},{7,31},{8,16},{9,... | collective-permute-start | bytes 884744 | tf_op jit(solution)/shard_map/ppermute | solution.py:46
  120.8 5.9 %collective-permute-done.33.refs_3_ = bf16[2,192,384]{2,1,0:T(8,128)(2,1)S(1)} collective-permute-done((bf16[2,192,384]{2,1,0:T(8,128)(2,1)}, bf16[2,192,384]{2,1,0:T(8,128)(2,1)S(1)}, u32[]{:S(2)}, u32[]{:S(2)}) %collective-permute-start.33) | collective-permute-done | bytes 294944 | tf_op jit(solution)/shard_map/ppermute | solution.py:46
  126.8 0.7 copy-done.35
  127.5 2.9 %place_sigma.1 = bf16[2,2,384,384]{3,2,1,0:T(8,128)(2,1)} custom-call(s32[3]{0:T(128)} %pad_add_fusion.place, bf16[2,192,384]{2,1,0:T(8,128)(2,1)} %get-tuple-element.60.refs_0_, bf16[2,192,384]{2,1,0:T(8,128)(2,1)} %get-tuple-element.61.refs_1_, bf16[2,192,384]{2,1,0:T(8,128)(2,1)} %copy-done.12, bf16[2,192,384]{2,1,0:T(8,128)(2,1)} %copy-done.35), custom_call_target="tpu_custom_call" | custom-call | tf_op jit(solution)/shard_map/place_sigma/pallas_call | solution.py:495
  130.4 4.0 %collective-permute-done.36.refs_3_ = bf16[384,384]{1,0:T(8,128)(2,1)S(1)} collective-permute-done((bf16[384,384]{1,0:T(8,128)(2,1)}, bf16[384,384]{1,0:T(8,128)(2,1)S(1)}, u32[]{:S(2)}, u32[]{:S(2)}) %collective-permute-start.36) | collective-permute-done | bytes 294944 | tf_op jit(solution)/shard_map/ppermute | solution.py:46
  134.5 2.7 %place_solution.1 = bf16[2,384,2,384]{3,2,1,0:T(2,128)(2,1)} custom-call(s32[3]{0:T(128)S(1)} %copy-done.1, bf16[384,384]{1,0:T(8,128)(2,1)S(1)} %copy-done, bf16[384,384]{1,0:T(8,128)(2,1)S(1)} %collective-permute-done.34.refs_1_, bf16[384,384]{1,0:T(8,128)(2,1)S(1)} %collective-permute-done.35.refs_2_, bf16[384,384]{1,0:T(8,128)(2,1)S(1)} %collective-permute-done.36.refs_3_), custom_call_target="tpu_custom_call" | custom-call | tf_op jit(solution)/shard_map/place_solution/pallas_call | solution.py:513
  (136 shorter events, 9.3 us)
Async XLA Ops:
  2.7 9.8 %collective-permute-start.1 = (bf16[2,2,96,384]{3,2,1,0:T(8,128)(2,1)}, bf16[2,2,96,384]{3,2,1,0:T(8,128)(2,1)}, u32[]{:S(2)}, u32[]{:S(2)}) collective-permute-start(bf16[2,2,96,384]{3,2,1,0:T(8,128)(2,1)} %get-tuple-element.95), channel_id=1, source_target_pairs={{0,1},{1,0},{2,3},{3,2},{4,5},{5,4},{6,7},{7,6},{8,9},{9,8},{10,11... | collective-permute-start | bytes 884744 | tf_op jit(solution)/shard_map/ppermute | solution.py:46
  5.7 16.2 %collective-permute-start.4 = (bf16[2,2,96,384]{3,2,1,0:T(8,128)(2,1)}, bf16[2,2,96,384]{3,2,1,0:T(8,128)(2,1)}, u32[]{:S(2)}, u32[]{:S(2)}) collective-permute-start(bf16[2,2,96,384]{3,2,1,0:T(8,128)(2,1)} %get-tuple-element.93), channel_id=1, source_target_pairs={{0,1},{1,0},{2,3},{3,2},{4,5},{5,4},{6,7},{7,6},{8,9},{9,8},{10,11... | collective-permute-start | bytes 884744 | tf_op jit(solution)/shard_map/ppermute | solution.py:46
  7.8 13.9 %collective-permute-start = (bf16[2,384,384]{2,1,0:T(8,128)(2,1)}, bf16[2,384,384]{2,1,0:T(8,128)(2,1)S(1)}, u32[]{:S(2)}, u32[]{:S(2)}) collective-permute-start(bf16[2,384,384]{2,1,0:T(8,128)(2,1)} %dynamic-slice_bitcast_fusion), channel_id=1, source_target_pairs={{0,16},{1,17},{2,18},{3,19},{4,20},{5,21},{6,22},{7,23},{8,24},{9,... | collective-permute-start | bytes 1769480 | tf_op jit(solution)/shard_map/ppermute | solution.py:46
  12.5 13.9 %collective-permute-start.2 = (bf16[2,2,96,384]{3,2,1,0:T(8,128)(2,1)}, bf16[2,2,96,384]{3,2,1,0:T(8,128)(2,1)}, u32[]{:S(2)}, u32[]{:S(2)}) collective-permute-start(bf16[2,2,96,384]{3,2,1,0:T(8,128)(2,1)} %get-tuple-element.54), channel_id=1, source_target_pairs={{0,1},{1,0},{2,3},{3,2},{4,5},{5,4},{6,7},{7,6},{8,9},{9,8},{10,11... | collective-permute-start | bytes 884744 | tf_op jit(solution)/shard_map/ppermute | solution.py:46
  13.7 16.1 %collective-permute-start.3 = (bf16[2,2,96,384]{3,2,1,0:T(8,128)(2,1)}, bf16[2,2,96,384]{3,2,1,0:T(8,128)(2,1)}, u32[]{:S(2)}, u32[]{:S(2)}) collective-permute-start(bf16[2,2,96,384]{3,2,1,0:T(8,128)(2,1)} %get-tuple-element.55), channel_id=1, source_target_pairs={{0,1},{1,0},{2,3},{3,2},{4,5},{5,4},{6,7},{7,6},{8,9},{9,8},{10,11... | collective-permute-start | bytes 884744 | tf_op jit(solution)/shard_map/ppermute | solution.py:46
  34.6 3.0 %collective-permute-start.12 = (bf16[2,192,384]{2,1,0:T(8,128)(2,1)}, bf16[2,192,384]{2,1,0:T(8,128)(2,1)S(1)}, u32[]{:S(2)}, u32[]{:S(2)}) collective-permute-start(bf16[2,192,384]{2,1,0:T(8,128)(2,1)} %get-tuple-element.61.refs_1_), channel_id=1, source_target_pairs={{8,24},{9,25},{16,0},{17,1},{18,2},{19,3},{24,8},{25,9},{26,10},{2... | collective-permute-start | bytes 884744 | tf_op jit(solution)/shard_map/ppermute | solution.py:46
  35.4 7.2 %collective-permute-start.5 = (bf16[2,192,384]{2,1,0:T(8,128)(2,1)}, bf16[2,192,384]{2,1,0:T(8,128)(2,1)S(1)}, u32[]{:S(2)}, u32[]{:S(2)}) collective-permute-start(bf16[2,192,384]{2,1,0:T(8,128)(2,1)} %get-tuple-element.62), channel_id=1, source_target_pairs={{0,1},{1,0},{2,3},{3,2},{4,5},{5,4},{6,7},{7,6},{8,9},{9,8},{10,11... | collective-permute-start | bytes 884744 | tf_op jit(solution)/shard_map/ppermute | solution.py:46
  36.7 5.9 %collective-permute-start.6 = (bf16[2,192,384]{2,1,0:T(8,128)(2,1)}, bf16[2,192,384]{2,1,0:T(8,128)(2,1)S(1)}, u32[]{:S(2)}, u32[]{:S(2)}) collective-permute-start(bf16[2,192,384]{2,1,0:T(8,128)(2,1)} %get-tuple-element.85), channel_id=1, source_target_pairs={{8,25},{9,24},{16,1},{17,0},{18,3},{19,2},{24,9},{25,8},{26,11},{2... | collective-permute-start | bytes 884744 | tf_op jit(solution)/shard_map/ppermute | solution.py:46
  37.7 11.5 %collective-permute-start.13 = (bf16[2,192,384]{2,1,0:T(8,128)(2,1)S(1)}, bf16[2,192,384]{2,1,0:T(8,128)(2,1)S(1)}, u32[]{:S(2)}, u32[]{:S(2)}) collective-permute-start(bf16[2,192,384]{2,1,0:T(8,128)(2,1)S(1)} %get-tuple-element.100), channel_id=1, source_target_pairs={{0,2},{1,3},{2,4},{3,5},{8,10},{9,11},{10,12},{11,13},{12,14},{13,... | collective-permute-start | bytes 884744 | tf_op jit(solution)/shard_map/ppermute | solution.py:46
  42.7 9.4 %collective-permute-start.9 = (bf16[384,384]{1,0:T(8,128)(2,1)S(1)}, bf16[384,384]{1,0:T(8,128)(2,1)S(1)}, u32[]{:S(2)}, u32[]{:S(2)}) collective-permute-start(bf16[384,384]{1,0:T(8,128)(2,1)S(1)} %bitcast.44), channel_id=1, source_target_pairs={{0,8},{1,9},{2,10},{3,11},{4,12},{5,13},{6,14},{7,15},{8,0},{9,1},... | collective-permute-start | bytes 884744 | tf_op jit(solution)/shard_map/ppermute | solution.py:46
  45.1 8.6 %collective-permute-start.10 = (bf16[384,384]{1,0:T(8,128)(2,1)S(1)}, bf16[384,384]{1,0:T(8,128)(2,1)S(1)}, u32[]{:S(2)}, u32[]{:S(2)}) collective-permute-start(bf16[384,384]{1,0:T(8,128)(2,1)S(1)} %bitcast.43), channel_id=1, source_target_pairs={{0,16},{1,17},{2,18},{3,19},{4,20},{5,21},{6,22},{7,23},{8,24},{9,... | collective-permute-start | bytes 884744 | tf_op jit(solution)/shard_map/ppermute | solution.py:46
  46.4 14.1 %collective-permute-start.11 = (bf16[384,384]{1,0:T(8,128)(2,1)S(1)}, bf16[384,384]{1,0:T(8,128)(2,1)}, u32[]{:S(2)}, u32[]{:S(2)}) collective-permute-start(bf16[384,384]{1,0:T(8,128)(2,1)S(1)} %bitcast.42), channel_id=1, source_target_pairs={{0,24},{1,25},{2,26},{3,27},{4,28},{5,29},{6,30},{7,31},{8,16},{9,... | collective-permute-start | bytes 884744 | tf_op jit(solution)/shard_map/ppermute | solution.py:46
  47.0 22.6 %copy-start.3 = (bf16[2,384,384]{2,1,0:T(8,128)(2,1)}, bf16[2,384,384]{2,1,0:T(8,128)(2,1)S(1)}, u32[]{:S(2)}) copy-start(bf16[2,384,384]{2,1,0:T(8,128)(2,1)S(1)} %pad_maximum_fusion.3.refs_9_) | copy-start | bytes 1769476
  49.3 11.3 %collective-permute-start.15 = (bf16[2,192,384]{2,1,0:T(8,128)(2,1)S(1)}, bf16[2,192,384]{2,1,0:T(8,128)(2,1)S(1)}, u32[]{:S(2)}, u32[]{:S(2)}) collective-permute-start(bf16[2,192,384]{2,1,0:T(8,128)(2,1)S(1)} %broadcast_select_fusion.5), channel_id=1, source_target_pairs={{2,4},{3,5},{4,6},{5,7},{8,10},{9,11},{10,12},{11,13},{12,14},{13,... | collective-permute-start | bytes 884744 | tf_op jit(solution)/shard_map/ppermute | solution.py:46
  50.7 19.6 %copy-start.4 = (bf16[2,384,384]{2,1,0:T(8,128)(2,1)}, bf16[2,384,384]{2,1,0:T(8,128)(2,1)S(1)}, u32[]{:S(2)}) copy-start(bf16[2,384,384]{2,1,0:T(8,128)(2,1)S(1)} %pad_maximum_fusion.2.refs_8_) | copy-start | bytes 1769476
  50.7 13.5 %collective-permute-start.14 = (bf16[2,192,384]{2,1,0:T(8,128)(2,1)S(1)}, bf16[2,192,384]{2,1,0:T(8,128)(2,1)S(1)}, u32[]{:S(2)}, u32[]{:S(2)}) collective-permute-start(bf16[2,192,384]{2,1,0:T(8,128)(2,1)S(1)} %get-tuple-element.70), channel_id=1, source_target_pairs={{0,2},{1,3},{2,4},{3,5},{8,10},{9,11},{10,12},{11,13},{12,14},{13,... | collective-permute-start | bytes 884744 | tf_op jit(solution)/shard_map/ppermute | solution.py:46
  52.1 15.4 %collective-permute-start.7 = (bf16[384,768]{1,0:T(8,128)(2,1)S(1)}, bf16[384,768]{1,0:T(8,128)(2,1)S(1)}, u32[]{:S(2)}, u32[]{:S(2)}) collective-permute-start(bf16[384,768]{1,0:T(8,128)(2,1)S(1)} %pad_maximum_fusion.refs_0_), channel_id=1, source_target_pairs={{0,8},{1,9},{2,10},{3,11},{4,12},{5,13},{6,14},{7,15},{8,0},{9,1},... | collective-permute-start | bytes 1769480 | tf_op jit(solution)/shard_map/ppermute | solution.py:46
  53.7 15.1 %collective-permute-start.22 = (bf16[2,384,384]{2,1,0:T(8,128)(2,1)S(1)}, bf16[2,384,384]{2,1,0:T(8,128)(2,1)S(1)}, u32[]{:S(2)}, u32[]{:S(2)}) collective-permute-start(bf16[2,384,384]{2,1,0:T(8,128)(2,1)S(1)} %pad_maximum_fusion.2.refs_8_), channel_id=1, source_target_pairs={{0,8},{1,9},{2,10},{3,11},{4,12},{5,13},{6,14},{7,15},{8,0},{9,1},... | collective-permute-start | bytes 1769480 | tf_op jit(solution)/shard_map/ppermute | solution.py:46
  55.1 40.6 %copy-start.6 = (bf16[384,768]{1,0:T(8,128)(2,1)}, bf16[384,768]{1,0:T(8,128)(2,1)S(1)}, u32[]{:S(2)}) copy-start(bf16[384,768]{1,0:T(8,128)(2,1)S(1)} %pad_maximum_fusion.1.refs_2_) | copy-start | bytes 1769476
  60.5 9.1 %collective-permute-start.23 = (bf16[2,384,384]{2,1,0:T(8,128)(2,1)S(1)}, bf16[2,384,384]{2,1,0:T(8,128)(2,1)S(1)}, u32[]{:S(2)}, u32[]{:S(2)}) collective-permute-start(bf16[2,384,384]{2,1,0:T(8,128)(2,1)S(1)} %pad_maximum_fusion.3.refs_9_), channel_id=1, source_target_pairs={{0,8},{1,9},{2,10},{3,11},{4,12},{5,13},{6,14},{7,15},{8,0},{9,1},... | collective-permute-start | bytes 1769480 | tf_op jit(solution)/shard_map/ppermute | solution.py:46
  60.5 35.1 %copy-start.8 = (bf16[2,192,384]{2,1,0:T(8,128)(2,1)}, bf16[2,192,384]{2,1,0:T(8,128)(2,1)S(1)}, u32[]{:S(2)}) copy-start(bf16[2,192,384]{2,1,0:T(8,128)(2,1)S(1)} %collective-permute-done.15.refs_12_) | copy-start | bytes 884740
  60.6 9.7 %collective-permute-start.8 = (bf16[384,768]{1,0:T(8,128)(2,1)S(1)}, bf16[384,768]{1,0:T(8,128)(2,1)S(1)}, u32[]{:S(2)}, u32[]{:S(2)}) collective-permute-start(bf16[384,768]{1,0:T(8,128)(2,1)S(1)} %pad_maximum_fusion.1.refs_2_), channel_id=1, source_target_pairs={{0,8},{1,9},{2,10},{3,11},{4,12},{5,13},{6,14},{7,15},{8,0},{9,1},... | collective-permute-start | bytes 1769480 | tf_op jit(solution)/shard_map/ppermute | solution.py:46
  64.2 31.5 %copy-start.9 = (bf16[2,192,384]{2,1,0:T(8,128)(2,1)}, bf16[2,192,384]{2,1,0:T(8,128)(2,1)S(1)}, u32[]{:S(2)}) copy-start(bf16[2,192,384]{2,1,0:T(8,128)(2,1)S(1)} %collective-permute-done.14.refs_11_) | copy-start | bytes 884740
  64.2 2.0 %collective-permute-start.24 = (bf16[2,192,384]{2,1,0:T(8,128)(2,1)S(1)}, bf16[2,192,384]{2,1,0:T(8,128)(2,1)S(1)}, u32[]{:S(2)}, u32[]{:S(2)}) collective-permute-start(bf16[2,192,384]{2,1,0:T(8,128)(2,1)S(1)} %collective-permute-done.13.refs_10_), channel_id=1, source_target_pairs={{0,8},{1,9},{2,10},{3,11},{4,12},{5,13},{6,14},{7,15},{8,0},{9,1},... | collective-permute-start | bytes 884744 | tf_op jit(solution)/shard_map/ppermute | solution.py:46
  66.2 31.6 %copy-start.27 = (bf16[2,192,384]{2,1,0:T(8,128)(2,1)}, bf16[2,192,384]{2,1,0:T(8,128)(2,1)S(1)}, u32[]{:S(2)}) copy-start(bf16[2,192,384]{2,1,0:T(8,128)(2,1)S(1)} %collective-permute-done.24.refs_21_) | copy-start | bytes 884740
  66.2 16.5 %collective-permute-start.17 = (bf16[2,192,384]{2,1,0:T(8,128)(2,1)S(1)}, bf16[2,192,384]{2,1,0:T(8,128)(2,1)S(1)}, u32[]{:S(2)}, u32[]{:S(2)}) collective-permute-start(bf16[2,192,384]{2,1,0:T(8,128)(2,1)S(1)} %broadcast_select_fusion.3), channel_id=1, source_target_pairs={{4,6},{5,7},{8,12},{9,13},{12,14},{13,15},{20,22},{21,23},{24,28},... | collective-permute-start | bytes 884744 | tf_op jit(solution)/shard_map/ppermute | solution.py:46
  67.5 42.5 %copy-start.16 = (bf16[384,768]{1,0:T(8,128)(2,1)}, bf16[384,768]{1,0:T(8,128)(2,1)S(1)}, u32[]{:S(2)}) copy-start(bf16[384,768]{1,0:T(8,128)(2,1)S(1)} %collective-permute-done.7.refs_1_) | copy-start | bytes 1769476
  67.5 27.7 %collective-permute-start.16 = (bf16[2,192,384]{2,1,0:T(8,128)(2,1)S(1)}, bf16[2,192,384]{2,1,0:T(8,128)(2,1)S(1)}, u32[]{:S(2)}, u32[]{:S(2)}) collective-permute-start(bf16[2,192,384]{2,1,0:T(8,128)(2,1)S(1)} %broadcast_select_fusion.4), channel_id=1, source_target_pairs={{2,4},{3,5},{4,6},{5,7},{8,10},{9,11},{10,12},{11,13},{12,14},{13,... | collective-permute-start | bytes 884744 | tf_op jit(solution)/shard_map/ppermute | solution.py:46
  68.8 41.2 %copy-start.17 = (bf16[2,384,384]{2,1,0:T(8,128)(2,1)}, bf16[2,384,384]{2,1,0:T(8,128)(2,1)S(1)}, u32[]{:S(2)}) copy-start(bf16[2,384,384]{2,1,0:T(8,128)(2,1)S(1)} %collective-permute-done.22.refs_19_) | copy-start | bytes 1769476
  68.9 28.5 %collective-permute-start.21 = (bf16[2,384,384]{2,1,0:T(8,128)(2,1)S(1)}, bf16[2,384,384]{2,1,0:T(8,128)(2,1)S(1)}, u32[]{:S(2)}, u32[]{:S(2)}) collective-permute-start(bf16[2,384,384]{2,1,0:T(8,128)(2,1)S(1)} %pad_maximum_fusion.3.refs_9_), channel_id=1, source_target_pairs={{12,8},{13,9},{28,24},{29,25}} | collective-permute-start | bytes 1769480 | tf_op jit(solution)/shard_map/ppermute | solution.py:46
  69.6 40.5 %copy-start.18 = (bf16[2,384,384]{2,1,0:T(8,128)(2,1)}, bf16[2,384,384]{2,1,0:T(8,128)(2,1)S(1)}, u32[]{:S(2)}) copy-start(bf16[2,384,384]{2,1,0:T(8,128)(2,1)S(1)} %collective-permute-done.23.refs_20_) | copy-start | bytes 1769476
  69.6 28.2 %collective-permute-start.20 = (bf16[2,384,384]{2,1,0:T(8,128)(2,1)S(1)}, bf16[2,384,384]{2,1,0:T(8,128)(2,1)S(1)}, u32[]{:S(2)}, u32[]{:S(2)}) collective-permute-start(bf16[2,384,384]{2,1,0:T(8,128)(2,1)S(1)} %pad_maximum_fusion.3.refs_9_), channel_id=1, source_target_pairs={{2,0},{3,1},{10,8},{11,9},{12,10},{13,11},{18,16},{19,17},{26,24},... | collective-permute-start | bytes 1769480 | tf_op jit(solution)/shard_map/ppermute | solution.py:46
  70.3 39.7 %copy-start.19 = (bf16[384,768]{1,0:T(8,128)(2,1)}, bf16[384,768]{1,0:T(8,128)(2,1)S(1)}, u32[]{:S(2)}) copy-start(bf16[384,768]{1,0:T(8,128)(2,1)S(1)} %collective-permute-done.8.refs_3_) | copy-start | bytes 1769476
  70.3 27.6 %collective-permute-start.19 = (bf16[2,384,384]{2,1,0:T(8,128)(2,1)S(1)}, bf16[2,384,384]{2,1,0:T(8,128)(2,1)S(1)}, u32[]{:S(2)}, u32[]{:S(2)}) collective-permute-start(bf16[2,384,384]{2,1,0:T(8,128)(2,1)S(1)} %pad_maximum_fusion.2.refs_8_), channel_id=1, source_target_pairs={{8,14},{9,15},{24,30},{25,31}} | collective-permute-start | bytes 1769480 | tf_op jit(solution)/shard_map/ppermute | solution.py:46
  82.7 27.3 %copy-start.28 = (bf16[2,192,384]{2,1,0:T(8,128)(2,1)}, bf16[2,192,384]{2,1,0:T(8,128)(2,1)S(1)}, u32[]{:S(2)}) copy-start(bf16[2,192,384]{2,1,0:T(8,128)(2,1)S(1)} %collective-permute-done.17.refs_14_) | copy-start | bytes 884740
  82.7 13.0 %collective-permute-start.26 = (bf16[2,192,384]{2,1,0:T(8,128)(2,1)S(1)}, bf16[2,192,384]{2,1,0:T(8,128)(2,1)S(1)}, u32[]{:S(2)}, u32[]{:S(2)}) collective-permute-start(bf16[2,192,384]{2,1,0:T(8,128)(2,1)S(1)} %collective-permute-done.15.refs_12_), channel_id=1, source_target_pairs={{0,8},{1,9},{2,10},{3,11},{4,12},{5,13},{6,14},{7,15},{8,0},{9,1},... | collective-permute-start | bytes 884744 | tf_op jit(solution)/shard_map/ppermute | solution.py:46
  95.2 2.0 %collective-permute-start.25 = (bf16[2,192,384]{2,1,0:T(8,128)(2,1)S(1)}, bf16[2,192,384]{2,1,0:T(8,128)(2,1)S(1)}, u32[]{:S(2)}, u32[]{:S(2)}) collective-permute-start(bf16[2,192,384]{2,1,0:T(8,128)(2,1)S(1)} %collective-permute-done.14.refs_11_), channel_id=1, source_target_pairs={{0,8},{1,9},{2,10},{3,11},{4,12},{5,13},{6,14},{7,15},{8,0},{9,1},... | collective-permute-start | bytes 884744 | tf_op jit(solution)/shard_map/ppermute | solution.py:46
  95.7 10.4 %collective-permute-start.18 = (bf16[2,192,384]{2,1,0:T(8,128)(2,1)S(1)}, bf16[2,192,384]{2,1,0:T(8,128)(2,1)S(1)}, u32[]{:S(2)}, u32[]{:S(2)}) collective-permute-start(bf16[2,192,384]{2,1,0:T(8,128)(2,1)S(1)} %broadcast_select_fusion.2), channel_id=1, source_target_pairs={{4,6},{5,7},{8,12},{9,13},{12,14},{13,15},{20,22},{21,23},{24,28},... | collective-permute-start | bytes 884744 | tf_op jit(solution)/shard_map/ppermute | solution.py:46
  97.2 1.6 %collective-permute-start.28 = (bf16[2,192,384]{2,1,0:T(8,128)(2,1)S(1)}, bf16[2,192,384]{2,1,0:T(8,128)(2,1)S(1)}, u32[]{:S(2)}, u32[]{:S(2)}) collective-permute-start(bf16[2,192,384]{2,1,0:T(8,128)(2,1)S(1)} %collective-permute-done.17.refs_14_), channel_id=1, source_target_pairs={{0,8},{1,9},{2,10},{3,11},{4,12},{5,13},{6,14},{7,15},{8,0},{9,1},... | collective-permute-start | bytes 884744 | tf_op jit(solution)/shard_map/ppermute | solution.py:46
  97.4 10.8 %collective-permute-start.32 = (bf16[2,384,384]{2,1,0:T(8,128)(2,1)S(1)}, bf16[2,384,384]{2,1,0:T(8,128)(2,1)S(1)}, u32[]{:S(2)}, u32[]{:S(2)}) collective-permute-start(bf16[2,384,384]{2,1,0:T(8,128)(2,1)S(1)} %collective-permute-done.21.refs_18_), channel_id=1, source_target_pairs={{0,8},{1,9},{2,10},{3,11},{4,12},{5,13},{6,14},{7,15},{8,0},{9,1},... | collective-permute-start | bytes 1769480 | tf_op jit(solution)/shard_map/ppermute | solution.py:46
  97.8 10.4 %collective-permute-start.31 = (bf16[2,384,384]{2,1,0:T(8,128)(2,1)S(1)}, bf16[2,384,384]{2,1,0:T(8,128)(2,1)S(1)}, u32[]{:S(2)}, u32[]{:S(2)}) collective-permute-start(bf16[2,384,384]{2,1,0:T(8,128)(2,1)S(1)} %collective-permute-done.20.refs_17_), channel_id=1, source_target_pairs={{0,8},{1,9},{2,10},{3,11},{4,12},{5,13},{6,14},{7,15},{8,0},{9,1},... | collective-permute-start | bytes 1769480 | tf_op jit(solution)/shard_map/ppermute | solution.py:46
  98.0 12.1 %collective-permute-start.30 = (bf16[2,384,384]{2,1,0:T(8,128)(2,1)S(1)}, bf16[2,384,384]{2,1,0:T(8,128)(2,1)}, u32[]{:S(2)}, u32[]{:S(2)}) collective-permute-start(bf16[2,384,384]{2,1,0:T(8,128)(2,1)S(1)} %collective-permute-done.19.refs_16_), channel_id=1, source_target_pairs={{0,8},{1,9},{2,10},{3,11},{4,12},{5,13},{6,14},{7,15},{8,0},{9,1},... | collective-permute-start | bytes 1769480 | tf_op jit(solution)/shard_map/ppermute | solution.py:46
  98.9 8.2 %collective-permute-start.27 = (bf16[2,192,384]{2,1,0:T(8,128)(2,1)S(1)}, bf16[2,192,384]{2,1,0:T(8,128)(2,1)S(1)}, u32[]{:S(2)}, u32[]{:S(2)}) collective-permute-start(bf16[2,192,384]{2,1,0:T(8,128)(2,1)S(1)} %collective-permute-done.16.refs_13_), channel_id=1, source_target_pairs={{0,8},{1,9},{2,10},{3,11},{4,12},{5,13},{6,14},{7,15},{8,0},{9,1},... | collective-permute-start | bytes 884744 | tf_op jit(solution)/shard_map/ppermute | solution.py:46
  106.1 2.2 %collective-permute-start.29 = (bf16[2,192,384]{2,1,0:T(8,128)(2,1)S(1)}, bf16[2,192,384]{2,1,0:T(8,128)(2,1)S(1)}, u32[]{:S(2)}, u32[]{:S(2)}) collective-permute-start(bf16[2,192,384]{2,1,0:T(8,128)(2,1)S(1)} %collective-permute-done.18.refs_15_), channel_id=1, source_target_pairs={{0,8},{1,9},{2,10},{3,11},{4,12},{5,13},{6,14},{7,15},{8,0},{9,1},... | collective-permute-start | bytes 884744 | tf_op jit(solution)/shard_map/ppermute | solution.py:46
  118.2 8.5 %collective-permute-start.33 = (bf16[2,192,384]{2,1,0:T(8,128)(2,1)}, bf16[2,192,384]{2,1,0:T(8,128)(2,1)S(1)}, u32[]{:S(2)}, u32[]{:S(2)}) collective-permute-start(bf16[2,192,384]{2,1,0:T(8,128)(2,1)} %get-tuple-element.85), channel_id=1, source_target_pairs={{0,1},{1,0},{2,3},{3,2},{4,5},{5,4},{6,7},{7,6},{8,9},{9,8},{10,11... | collective-permute-start | bytes 884744 | tf_op jit(solution)/shard_map/ppermute | solution.py:46
  118.5 11.9 %collective-permute-start.34 = (bf16[384,384]{1,0:T(8,128)(2,1)}, bf16[384,384]{1,0:T(8,128)(2,1)S(1)}, u32[]{:S(2)}, u32[]{:S(2)}) collective-permute-start(bf16[384,384]{1,0:T(8,128)(2,1)} %get-tuple-element.82), channel_id=1, source_target_pairs={{0,8},{1,9},{2,10},{3,11},{4,12},{5,13},{6,14},{7,15},{8,0},{9,1},... | collective-permute-start | bytes 884744 | tf_op jit(solution)/shard_map/ppermute | solution.py:46
  119.2 11.2 %collective-permute-start.35 = (bf16[384,384]{1,0:T(8,128)(2,1)}, bf16[384,384]{1,0:T(8,128)(2,1)S(1)}, u32[]{:S(2)}, u32[]{:S(2)}) collective-permute-start(bf16[384,384]{1,0:T(8,128)(2,1)} %get-tuple-element.83), channel_id=1, source_target_pairs={{0,16},{1,17},{2,18},{3,19},{4,20},{5,21},{6,22},{7,23},{8,24},{9,... | collective-permute-start | bytes 884744 | tf_op jit(solution)/shard_map/ppermute | solution.py:46
  119.2 15.3 %collective-permute-start.36 = (bf16[384,384]{1,0:T(8,128)(2,1)}, bf16[384,384]{1,0:T(8,128)(2,1)S(1)}, u32[]{:S(2)}, u32[]{:S(2)}) collective-permute-start(bf16[384,384]{1,0:T(8,128)(2,1)} %get-tuple-element.84), channel_id=1, source_target_pairs={{0,24},{1,25},{2,26},{3,27},{4,28},{5,29},{6,30},{7,31},{8,16},{9,... | collective-permute-start | bytes 884744 | tf_op jit(solution)/shard_map/ppermute | solution.py:46
  (28 other events, 211.6 us)

commit v13 on v12

--- a/solution.py
+++ b/solution.py
@@ -90,7 +90,7 @@
 
 
 def hbm(count):
-    return [pl.BlockSpec(memory_space=pl.ANY)] * count
+    return [pl.BlockSpec(memory_space=pltpu.HBM)] * count
 
 
 def smem():
@@ -451,7 +451,7 @@
 
     for number in range(cols - 1):
         for k in range(len(plan.chunks)):
-            behind = [got[k - 1][number]] if k else []
+            behind = [got[k - 1][number]] if k and number else []
             if number == 1 and k + 1 < len(plan.chunks):
                 behind.append(came[k + 1])
             ring_step(k, number, *behind)

time: 138 us -> 138 us (level)
  the two profiles are of different devices: /device:TPU:25 before, /device:TPU:0 now
where the time goes in v13:
time: 138 us; the launch traced here: 137 us
  starting transfers between devices  55 us (40%)
  waiting for transfers between devices  41.6 us (30%)
  Pallas kernels  22.9 us (17%)
  local copies, waits for them, and re-layouts  14.1 us (10%)
  other arithmetic  1.87 us (1%)
  between operations  1.42 us (1%)
    ppermute x37, starting transfers between devices, send(): return lax.ppermute(value, AXES, pairs)  55 us
    ppermute x37, waiting for transfers between devices, send(): return lax.ppermute(value, AXES, pairs)  41.6 us
    pallas_call x2, Pallas kernels, self_energy(): pl.pallas_call(functools.partial(sigma_kernel, plan, pair_count, u, copie...  9.22 us
    pallas_call x1, Pallas kernels, on_device(): pl.pallas_call(functools.partial(solve_kernel, plan, sources), out_shape=...  8.06 us
    dynamic_slice x5, local copies, waits for them, and re-layouts, on_device(): lax.dynamic_index_in_dim(right, r ^ s, 0, keepdims=False)  3.03 us
    pallas_call x1, Pallas kernels, on_device(): pl.pallas_call(functools.partial(place_kernel, plan), out_shape=jax.Shape...  2.95 us
    dynamic_slice x2, local copies, waits for them, and re-layouts, part_of(): lax.dynamic_slice_in_dim(value, (y ^ q) * half + u * plan.sub, plan.sub, 2)  2.94 us
  transfers between devices with their start and end apart: 37, of which 11 were waited for; matrix products, arithmetic and copies ran while one was open for 8% of the time, Pallas kernels for 5%

profile of v13, /device:TPU:0, one launch (start us, length us, event | category | flops | bytes accessed | tf_op | source)
XLA Modules:
  0.0 136.9 jit_solution(15236454114367954955)
XLA Ops:
  0.7 2.0 %constant_dynamic-slice_fusion = (bf16[2,2,96,384]{3,2,1,0:T(8,128)(2,1)}, bf16[2,2,96,384]{3,2,1,0:T(8,128)(2,1)}) fusion(bf16[2,2,384,384]{3,2,1,0:T(8,128)(2,1)} %refs_0_.3, s32[]{:T(128)S(6)} %select_n.109, s32[]{:T(128)S(6)} %select_n.101), kind=kLoop, calls=%fused_computation.27 | loop fusion | bytes 1179656 | tf_op jit(solution)/shard_map/dynamic_slice | solution.py:328
  2.7 3.0 %collective-permute-start.1 = (bf16[2,2,96,384]{3,2,1,0:T(8,128)(2,1)}, bf16[2,2,96,384]{3,2,1,0:T(8,128)(2,1)}, u32[]{:S(2)}, u32[]{:S(2)}) collective-permute-start(bf16[2,2,96,384]{3,2,1,0:T(8,128)(2,1)} %get-tuple-element.93), channel_id=1, source_target_pairs={{0,1},{1,0},{2,3},{3,2},{4,5},{5,4},{6,7},{7,6},{8,9},{9,8},{10,11... | collective-permute-start | bytes 884744 | tf_op jit(solution)/shard_map/ppermute | solution.py:46
  5.7 0.8 copy.11
  6.5 0.9 dynamic-slice_bitcast_fusion.2
  7.4 2.0 %dynamic-slice_bitcast_fusion = bf16[2,384,384]{2,1,0:T(8,128)(2,1)} fusion(bf16[2,2,384,384]{3,2,1,0:T(8,128)(2,1)} %param.8, s32[]{:T(128)S(6)} %select_n.108), kind=kLoop, calls=%fused_computation.4 | loop fusion | bytes 1179652 | tf_op jit(solution)/shard_map/jit(dynamic_index_in_dim)/squeeze | solution.py:343
  9.4 1.9 %collective-permute-start = (bf16[2,384,384]{2,1,0:T(8,128)(2,1)}, bf16[2,384,384]{2,1,0:T(8,128)(2,1)S(1)}, u32[]{:S(2)}, u32[]{:S(2)}) collective-permute-start(bf16[2,384,384]{2,1,0:T(8,128)(2,1)} %dynamic-slice_bitcast_fusion), channel_id=1, source_target_pairs={{0,16},{1,17},{2,18},{3,19},{4,20},{5,21},{6,22},{7,23},{8,24},{9,... | collective-permute-start | bytes 1769480 | tf_op jit(solution)/shard_map/ppermute | solution.py:46
  11.9 2.0 %copy.12 = bf16[2,384,2,384]{1,3,2,0:T(8,128)(2,1)S(1)} copy(bf16[2,384,2,384]{3,2,1,0:T(2,128)(2,1)S(1)} %copy-done.14) | data formatting | bytes 2359296 | tf_op jit(solution)/shard_map/optimization_barrier | solution.py:283
  14.8 1.5 %collective-permute-start.2 = (bf16[2,2,96,384]{3,2,1,0:T(8,128)(2,1)}, bf16[2,2,96,384]{3,2,1,0:T(8,128)(2,1)}, u32[]{:S(2)}, u32[]{:S(2)}) collective-permute-start(bf16[2,2,96,384]{3,2,1,0:T(8,128)(2,1)} %get-tuple-element.53), channel_id=1, source_target_pairs={{0,1},{1,0},{2,3},{3,2},{4,5},{5,4},{6,7},{7,6},{8,9},{9,8},{10,11... | collective-permute-start | bytes 884744 | tf_op jit(solution)/shard_map/ppermute | solution.py:46
  17.4 0.9 copy.17
  18.3 0.9 copy.16
  19.4 0.9 copy.14
  20.3 4.1 %collective-permute-done = bf16[2,384,384]{2,1,0:T(8,128)(2,1)S(1)} collective-permute-done((bf16[2,384,384]{2,1,0:T(8,128)(2,1)}, bf16[2,384,384]{2,1,0:T(8,128)(2,1)S(1)}, u32[]{:S(2)}, u32[]{:S(2)}) %collective-permute-start) | collective-permute-done | bytes 589856 | tf_op jit(solution)/shard_map/ppermute | solution.py:46
  24.5 4.5 %self_energy.2 = (bf16[2,96,384]{2,1,0:T(8,128)(2,1)}, bf16[2,96,384]{2,1,0:T(8,128)(2,1)}, bf16[2,96,384]{2,1,0:T(8,128)(2,1)}, bf16[2,96,384]{2,1,0:T(8,128)(2,1)}) custom-call(s32[3]{0:T(128)} %pad_add_fusion.place, s32[4,8]{1,0:T(4,128)} %fusion.1.quads, s32[4,8]{1,0:T(4,128)} %slice_bitcast_fusion.4.thirds, bf16[2,2,384,384]{3,2,1,0:T(8,128)(2,1)} %refs_0_.3, ...), custom_call_target="tpu_custom_call" | custom-call | tf_op jit(solution)/shard_map/self_energy/pallas_call | solution.py:360
  29.0 2.9 %collective-permute-done.3.refs_3_ = bf16[2,2,96,384]{3,2,1,0:T(8,128)(2,1)} collective-permute-done((bf16[2,2,96,384]{3,2,1,0:T(8,128)(2,1)}, bf16[2,2,96,384]{3,2,1,0:T(8,128)(2,1)}, u32[]{:S(2)}, u32[]{:S(2)}) %collective-permute-start.3) | collective-permute-done | bytes 294944 | tf_op jit(solution)/shard_map/ppermute | solution.py:46
  31.9 4.7 %self_energy.3 = (bf16[2,192,384]{2,1,0:T(8,128)(2,1)}, bf16[2,192,384]{2,1,0:T(8,128)(2,1)}, bf16[2,192,384]{2,1,0:T(8,128)(2,1)}, bf16[2,192,384]{2,1,0:T(8,128)(2,1)}) custom-call(s32[3]{0:T(128)} %pad_add_fusion.place, s32[4,8]{1,0:T(4,128)} %fusion.1.quads, s32[4,8]{1,0:T(4,128)} %slice_bitcast_fusion.4.thirds, bf16[2,2,384,384]{3,2,1,0:T(8,128)(2,1)} %refs_0_.3, ...), custom_call_target="tpu_custom_call" | custom-call | tf_op jit(solution)/shard_map/self_energy/pallas_call | solution.py:360
  36.7 1.4 %collective-permute-start.12 = (bf16[2,192,384]{2,1,0:T(8,128)(2,1)}, bf16[2,192,384]{2,1,0:T(8,128)(2,1)S(1)}, u32[]{:S(2)}, u32[]{:S(2)}) collective-permute-start(bf16[2,192,384]{2,1,0:T(8,128)(2,1)} %get-tuple-element.60.refs_1_), channel_id=1, source_target_pairs={{8,24},{9,25},{16,0},{17,1},{18,2},{19,3},{24,8},{25,9},{26,10},{2... | collective-permute-start | bytes 884744 | tf_op jit(solution)/shard_map/ppermute | solution.py:46
  38.1 1.8 %collective-permute-start.5 = (bf16[2,192,384]{2,1,0:T(8,128)(2,1)}, bf16[2,192,384]{2,1,0:T(8,128)(2,1)S(1)}, u32[]{:S(2)}, u32[]{:S(2)}) collective-permute-start(bf16[2,192,384]{2,1,0:T(8,128)(2,1)} %get-tuple-element.61), channel_id=1, source_target_pairs={{0,1},{1,0},{2,3},{3,2},{4,5},{5,4},{6,7},{7,6},{8,9},{9,8},{10,11... | collective-permute-start | bytes 884744 | tf_op jit(solution)/shard_map/ppermute | solution.py:46
  39.9 1.4 %collective-permute-start.6 = (bf16[2,192,384]{2,1,0:T(8,128)(2,1)}, bf16[2,192,384]{2,1,0:T(8,128)(2,1)S(1)}, u32[]{:S(2)}, u32[]{:S(2)}) collective-permute-start(bf16[2,192,384]{2,1,0:T(8,128)(2,1)} %get-tuple-element.83), channel_id=1, source_target_pairs={{8,25},{9,24},{16,1},{17,0},{18,3},{19,2},{24,9},{25,8},{26,11},{2... | collective-permute-start | bytes 884744 | tf_op jit(solution)/shard_map/ppermute | solution.py:46
  41.4 7.4 %collective-permute-done.12 = bf16[2,192,384]{2,1,0:T(8,128)(2,1)S(1)} collective-permute-done((bf16[2,192,384]{2,1,0:T(8,128)(2,1)}, bf16[2,192,384]{2,1,0:T(8,128)(2,1)S(1)}, u32[]{:S(2)}, u32[]{:S(2)}) %collective-permute-start.12) | collective-permute-done | bytes 294944 | tf_op jit(solution)/shard_map/ppermute | solution.py:46
  48.9 3.7 %collective-permute-start.13 = (bf16[2,192,384]{2,1,0:T(8,128)(2,1)S(1)}, bf16[2,192,384]{2,1,0:T(8,128)(2,1)S(1)}, u32[]{:S(2)}, u32[]{:S(2)}) collective-permute-start(bf16[2,192,384]{2,1,0:T(8,128)(2,1)S(1)} %get-tuple-element.98), channel_id=1, source_target_pairs={{0,2},{1,3},{2,4},{3,5},{8,10},{9,11},{10,12},{11,13},{12,14},{13,... | collective-permute-start | bytes 884744 | tf_op jit(solution)/shard_map/ppermute | solution.py:46
  52.7 1.9 %collective-permute-done.5.refs_2_ = bf16[2,192,384]{2,1,0:T(8,128)(2,1)S(1)} collective-permute-done((bf16[2,192,384]{2,1,0:T(8,128)(2,1)}, bf16[2,192,384]{2,1,0:T(8,128)(2,1)S(1)}, u32[]{:S(2)}, u32[]{:S(2)}) %collective-permute-start.5) | collective-permute-done | bytes 294944 | tf_op jit(solution)/shard_map/ppermute | solution.py:46
  54.7 1.7 %collective-permute-start.11 = (bf16[384,384]{1,0:T(8,128)(2,1)S(1)}, bf16[384,384]{1,0:T(8,128)(2,1)}, u32[]{:S(2)}, u32[]{:S(2)}) collective-permute-start(bf16[384,384]{1,0:T(8,128)(2,1)S(1)} %bitcast.42), channel_id=1, source_target_pairs={{0,24},{1,25},{2,26},{3,27},{4,28},{5,29},{6,30},{7,31},{8,16},{9,... | collective-permute-start | bytes 884744 | tf_op jit(solution)/shard_map/ppermute | solution.py:46
  56.5 3.2 %collective-permute-start.14 = (bf16[2,192,384]{2,1,0:T(8,128)(2,1)S(1)}, bf16[2,192,384]{2,1,0:T(8,128)(2,1)S(1)}, u32[]{:S(2)}, u32[]{:S(2)}) collective-permute-start(bf16[2,192,384]{2,1,0:T(8,128)(2,1)S(1)} %get-tuple-element.100), channel_id=1, source_target_pairs={{0,2},{1,3},{2,4},{3,5},{8,10},{9,11},{10,12},{11,13},{12,14},{13,... | collective-permute-start | bytes 884744 | tf_op jit(solution)/shard_map/ppermute | solution.py:46
  59.9 0.7 collective-permute-start.15
  60.8 8.9 %collective-permute-start.24 = (bf16[2,192,384]{2,1,0:T(8,128)(2,1)S(1)}, bf16[2,192,384]{2,1,0:T(8,128)(2,1)S(1)}, u32[]{:S(2)}, u32[]{:S(2)}) collective-permute-start(bf16[2,192,384]{2,1,0:T(8,128)(2,1)S(1)} %collective-permute-done.13.refs_10_), channel_id=1, source_target_pairs={{0,8},{1,9},{2,10},{3,11},{4,12},{5,13},{6,14},{7,15},{8,0},{9,1},... | collective-permute-start | bytes 884744 | tf_op jit(solution)/shard_map/ppermute | solution.py:46
  71.0 0.7 collective-permute-start.17
  71.8 2.1 %collective-permute-done.25.refs_22_ = bf16[2,192,384]{2,1,0:T(8,128)(2,1)S(1)} collective-permute-done((bf16[2,192,384]{2,1,0:T(8,128)(2,1)S(1)}, bf16[2,192,384]{2,1,0:T(8,128)(2,1)S(1)}, u32[]{:S(2)}, u32[]{:S(2)}) %collective-permute-start.25) | collective-permute-done | bytes 294944 | tf_op jit(solution)/shard_map/ppermute | solution.py:46
  74.0 4.7 %collective-permute-start.8 = (bf16[384,768]{1,0:T(8,128)(2,1)S(1)}, bf16[384,768]{1,0:T(8,128)(2,1)S(1)}, u32[]{:S(2)}, u32[]{:S(2)}) collective-permute-start(bf16[384,768]{1,0:T(8,128)(2,1)S(1)} %pad_maximum_fusion.1.refs_2_), channel_id=1, source_target_pairs={{0,8},{1,9},{2,10},{3,11},{4,12},{5,13},{6,14},{7,15},{8,0},{9,1},... | collective-permute-start | bytes 1769480 | tf_op jit(solution)/shard_map/ppermute | solution.py:46
  78.6 0.7 collective-permute-start.16
  79.3 0.7 collective-permute-start.21
  80.1 1.3 collective-permute-start.20
  81.4 0.7 collective-permute-start.19
  82.1 7.0 %collective-permute-start.26 = (bf16[2,192,384]{2,1,0:T(8,128)(2,1)S(1)}, bf16[2,192,384]{2,1,0:T(8,128)(2,1)S(1)}, u32[]{:S(2)}, u32[]{:S(2)}) collective-permute-start(bf16[2,192,384]{2,1,0:T(8,128)(2,1)S(1)} %collective-permute-done.15.refs_12_), channel_id=1, source_target_pairs={{0,8},{1,9},{2,10},{3,11},{4,12},{5,13},{6,14},{7,15},{8,0},{9,1},... | collective-permute-start | bytes 884744 | tf_op jit(solution)/shard_map/ppermute | solution.py:46
  89.3 0.9 collective-permute-start.18
  90.4 3.8 %collective-permute-start.28 = (bf16[2,192,384]{2,1,0:T(8,128)(2,1)S(1)}, bf16[2,192,384]{2,1,0:T(8,128)(2,1)S(1)}, u32[]{:S(2)}, u32[]{:S(2)}) collective-permute-start(bf16[2,192,384]{2,1,0:T(8,128)(2,1)S(1)} %collective-permute-done.17.refs_14_), channel_id=1, source_target_pairs={{0,8},{1,9},{2,10},{3,11},{4,12},{5,13},{6,14},{7,15},{8,0},{9,1},... | collective-permute-start | bytes 884744 | tf_op jit(solution)/shard_map/ppermute | solution.py:46
  94.2 10.1 %collective-permute-done.20.refs_17_ = bf16[2,384,384]{2,1,0:T(8,128)(2,1)S(1)} collective-permute-done((bf16[2,384,384]{2,1,0:T(8,128)(2,1)S(1)}, bf16[2,384,384]{2,1,0:T(8,128)(2,1)S(1)}, u32[]{:S(2)}, u32[]{:S(2)}) %collective-permute-start.20) | collective-permute-done | bytes 589856 | tf_op jit(solution)/shard_map/ppermute | solution.py:46
  105.4 1.8 %collective-permute-done.27.refs_24_ = bf16[2,192,384]{2,1,0:T(8,128)(2,1)S(1)} collective-permute-done((bf16[2,192,384]{2,1,0:T(8,128)(2,1)S(1)}, bf16[2,192,384]{2,1,0:T(8,128)(2,1)S(1)}, u32[]{:S(2)}, u32[]{:S(2)}) %collective-permute-start.27) | collective-permute-done | bytes 294944 | tf_op jit(solution)/shard_map/ppermute | solution.py:46
  107.2 0.8 collective-permute-done.29.refs_26_
  108.1 0.6 copy-done.33
  109.0 0.8 copy-done.24
  109.9 8.1 %substitution.1 = (bf16[384,384]{1,0:T(8,128)(2,1)}, bf16[384,384]{1,0:T(8,128)(2,1)}, bf16[384,384]{1,0:T(8,128)(2,1)}, bf16[384,384]{1,0:T(8,128)(2,1)}) custom-call(s32[3]{0:T(128)} %pad_add_fusion.place, bf16[384,768]{1,0:T(8,128)(2,1)} %copy-done.5, bf16[384,768]{1,0:T(8,128)(2,1)} %copy-done.16, bf16[384,768]{1,0:T(8,128)(2,1)} %copy-done.6, ...), custom_call_target="tpu_custom_call" | custom-call | tf_op jit(solution)/shard_map/substitution/pallas_call | solution.py:478
  118.0 0.6 collective-permute-start.33
  118.7 1.8 %collective-permute-start.36 = (bf16[384,384]{1,0:T(8,128)(2,1)}, bf16[384,384]{1,0:T(8,128)(2,1)S(1)}, u32[]{:S(2)}, u32[]{:S(2)}) collective-permute-start(bf16[384,384]{1,0:T(8,128)(2,1)} %get-tuple-element.82), channel_id=1, source_target_pairs={{0,24},{1,25},{2,26},{3,27},{4,28},{5,29},{6,30},{7,31},{8,16},{9,... | collective-permute-start | bytes 884744 | tf_op jit(solution)/shard_map/ppermute | solution.py:46
  120.5 6.9 %collective-permute-done.33.refs_3_ = bf16[2,192,384]{2,1,0:T(8,128)(2,1)S(1)} collective-permute-done((bf16[2,192,384]{2,1,0:T(8,128)(2,1)}, bf16[2,192,384]{2,1,0:T(8,128)(2,1)S(1)}, u32[]{:S(2)}, u32[]{:S(2)}) %collective-permute-start.33) | collective-permute-done | bytes 294944 | tf_op jit(solution)/shard_map/ppermute | solution.py:46
  127.3 0.7 copy-done.34
  128.0 2.9 %place_sigma.1 = bf16[2,2,384,384]{3,2,1,0:T(8,128)(2,1)} custom-call(s32[3]{0:T(128)} %pad_add_fusion.place, bf16[2,192,384]{2,1,0:T(8,128)(2,1)} %get-tuple-element.59.refs_0_, bf16[2,192,384]{2,1,0:T(8,128)(2,1)} %get-tuple-element.60.refs_1_, bf16[2,192,384]{2,1,0:T(8,128)(2,1)} %copy-done.12, bf16[2,192,384]{2,1,0:T(8,128)(2,1)} %copy-done.34), custom_call_target="tpu_custom_call" | custom-call | tf_op jit(solution)/shard_map/place_sigma/pallas_call | solution.py:495
  131.0 3.2 %collective-permute-done.36.refs_3_ = bf16[384,384]{1,0:T(8,128)(2,1)S(1)} collective-permute-done((bf16[384,384]{1,0:T(8,128)(2,1)}, bf16[384,384]{1,0:T(8,128)(2,1)S(1)}, u32[]{:S(2)}, u32[]{:S(2)}) %collective-permute-start.36) | collective-permute-done | bytes 294944 | tf_op jit(solution)/shard_map/ppermute | solution.py:46
  134.2 2.7 %place_solution.1 = bf16[2,384,2,384]{3,2,1,0:T(2,128)(2,1)} custom-call(s32[3]{0:T(128)S(1)} %copy-done.1, bf16[384,384]{1,0:T(8,128)(2,1)S(1)} %copy-done, bf16[384,384]{1,0:T(8,128)(2,1)S(1)} %collective-permute-done.34.refs_1_, bf16[384,384]{1,0:T(8,128)(2,1)S(1)} %collective-permute-done.35.refs_2_, bf16[384,384]{1,0:T(8,128)(2,1)S(1)} %collective-permute-done.36.refs_3_), custom_call_target="tpu_custom_call" | custom-call | tf_op jit(solution)/shard_map/place_solution/pallas_call | solution.py:513
  (134 shorter events, 6.7 us)
Async XLA Ops:
  2.7 12.1 %collective-permute-start.1 = (bf16[2,2,96,384]{3,2,1,0:T(8,128)(2,1)}, bf16[2,2,96,384]{3,2,1,0:T(8,128)(2,1)}, u32[]{:S(2)}, u32[]{:S(2)}) collective-permute-start(bf16[2,2,96,384]{3,2,1,0:T(8,128)(2,1)} %get-tuple-element.93), channel_id=1, source_target_pairs={{0,1},{1,0},{2,3},{3,2},{4,5},{5,4},{6,7},{7,6},{8,9},{9,8},{10,11... | collective-permute-start | bytes 884744 | tf_op jit(solution)/shard_map/ppermute | solution.py:46
  7.4 17.1 %collective-permute-start.4 = (bf16[2,2,96,384]{3,2,1,0:T(8,128)(2,1)}, bf16[2,2,96,384]{3,2,1,0:T(8,128)(2,1)}, u32[]{:S(2)}, u32[]{:S(2)}) collective-permute-start(bf16[2,2,96,384]{3,2,1,0:T(8,128)(2,1)} %get-tuple-element.91), channel_id=1, source_target_pairs={{0,1},{1,0},{2,3},{3,2},{4,5},{5,4},{6,7},{7,6},{8,9},{9,8},{10,11... | collective-permute-start | bytes 884744 | tf_op jit(solution)/shard_map/ppermute | solution.py:46
  9.4 15.0 %collective-permute-start = (bf16[2,384,384]{2,1,0:T(8,128)(2,1)}, bf16[2,384,384]{2,1,0:T(8,128)(2,1)S(1)}, u32[]{:S(2)}, u32[]{:S(2)}) collective-permute-start(bf16[2,384,384]{2,1,0:T(8,128)(2,1)} %dynamic-slice_bitcast_fusion), channel_id=1, source_target_pairs={{0,16},{1,17},{2,18},{3,19},{4,20},{5,21},{6,22},{7,23},{8,24},{9,... | collective-permute-start | bytes 1769480 | tf_op jit(solution)/shard_map/ppermute | solution.py:46
  14.8 14.2 %collective-permute-start.2 = (bf16[2,2,96,384]{3,2,1,0:T(8,128)(2,1)}, bf16[2,2,96,384]{3,2,1,0:T(8,128)(2,1)}, u32[]{:S(2)}, u32[]{:S(2)}) collective-permute-start(bf16[2,2,96,384]{3,2,1,0:T(8,128)(2,1)} %get-tuple-element.53), channel_id=1, source_target_pairs={{0,1},{1,0},{2,3},{3,2},{4,5},{5,4},{6,7},{7,6},{8,9},{9,8},{10,11... | collective-permute-start | bytes 884744 | tf_op jit(solution)/shard_map/ppermute | solution.py:46
  16.3 15.6 %collective-permute-start.3 = (bf16[2,2,96,384]{3,2,1,0:T(8,128)(2,1)}, bf16[2,2,96,384]{3,2,1,0:T(8,128)(2,1)}, u32[]{:S(2)}, u32[]{:S(2)}) collective-permute-start(bf16[2,2,96,384]{3,2,1,0:T(8,128)(2,1)} %get-tuple-element.54), channel_id=1, source_target_pairs={{0,1},{1,0},{2,3},{3,2},{4,5},{5,4},{6,7},{7,6},{8,9},{9,8},{10,11... | collective-permute-start | bytes 884744 | tf_op jit(solution)/shard_map/ppermute | solution.py:46
  36.7 12.2 %collective-permute-start.12 = (bf16[2,192,384]{2,1,0:T(8,128)(2,1)}, bf16[2,192,384]{2,1,0:T(8,128)(2,1)S(1)}, u32[]{:S(2)}, u32[]{:S(2)}) collective-permute-start(bf16[2,192,384]{2,1,0:T(8,128)(2,1)} %get-tuple-element.60.refs_1_), channel_id=1, source_target_pairs={{8,24},{9,25},{16,0},{17,1},{18,2},{19,3},{24,8},{25,9},{26,10},{2... | collective-permute-start | bytes 884744 | tf_op jit(solution)/shard_map/ppermute | solution.py:46
  38.1 16.4 %collective-permute-start.5 = (bf16[2,192,384]{2,1,0:T(8,128)(2,1)}, bf16[2,192,384]{2,1,0:T(8,128)(2,1)S(1)}, u32[]{:S(2)}, u32[]{:S(2)}) collective-permute-start(bf16[2,192,384]{2,1,0:T(8,128)(2,1)} %get-tuple-element.61), channel_id=1, source_target_pairs={{0,1},{1,0},{2,3},{3,2},{4,5},{5,4},{6,7},{7,6},{8,9},{9,8},{10,11... | collective-permute-start | bytes 884744 | tf_op jit(solution)/shard_map/ppermute | solution.py:46
  39.9 14.6 %collective-permute-start.6 = (bf16[2,192,384]{2,1,0:T(8,128)(2,1)}, bf16[2,192,384]{2,1,0:T(8,128)(2,1)S(1)}, u32[]{:S(2)}, u32[]{:S(2)}) collective-permute-start(bf16[2,192,384]{2,1,0:T(8,128)(2,1)} %get-tuple-element.83), channel_id=1, source_target_pairs={{8,25},{9,24},{16,1},{17,0},{18,3},{19,2},{24,9},{25,8},{26,11},{2... | collective-permute-start | bytes 884744 | tf_op jit(solution)/shard_map/ppermute | solution.py:46
  48.9 10.9 %collective-permute-start.13 = (bf16[2,192,384]{2,1,0:T(8,128)(2,1)S(1)}, bf16[2,192,384]{2,1,0:T(8,128)(2,1)S(1)}, u32[]{:S(2)}, u32[]{:S(2)}) collective-permute-start(bf16[2,192,384]{2,1,0:T(8,128)(2,1)S(1)} %get-tuple-element.98), channel_id=1, source_target_pairs={{0,2},{1,3},{2,4},{3,5},{8,10},{9,11},{10,12},{11,13},{12,14},{13,... | collective-permute-start | bytes 884744 | tf_op jit(solution)/shard_map/ppermute | solution.py:46
  54.6 15.2 %collective-permute-start.9 = (bf16[384,384]{1,0:T(8,128)(2,1)S(1)}, bf16[384,384]{1,0:T(8,128)(2,1)S(1)}, u32[]{:S(2)}, u32[]{:S(2)}) collective-permute-start(bf16[384,384]{1,0:T(8,128)(2,1)S(1)} %bitcast.44), channel_id=1, source_target_pairs={{0,8},{1,9},{2,10},{3,11},{4,12},{5,13},{6,14},{7,15},{8,0},{9,1},... | collective-permute-start | bytes 884744 | tf_op jit(solution)/shard_map/ppermute | solution.py:46
  54.7 15.2 %collective-permute-start.10 = (bf16[384,384]{1,0:T(8,128)(2,1)S(1)}, bf16[384,384]{1,0:T(8,128)(2,1)}, u32[]{:S(2)}, u32[]{:S(2)}) collective-permute-start(bf16[384,384]{1,0:T(8,128)(2,1)S(1)} %bitcast.43), channel_id=1, source_target_pairs={{0,16},{1,17},{2,18},{3,19},{4,20},{5,21},{6,22},{7,23},{8,24},{9,... | collective-permute-start | bytes 884744 | tf_op jit(solution)/shard_map/ppermute | solution.py:46
  54.7 15.7 %collective-permute-start.11 = (bf16[384,384]{1,0:T(8,128)(2,1)S(1)}, bf16[384,384]{1,0:T(8,128)(2,1)}, u32[]{:S(2)}, u32[]{:S(2)}) collective-permute-start(bf16[384,384]{1,0:T(8,128)(2,1)S(1)} %bitcast.42), channel_id=1, source_target_pairs={{0,24},{1,25},{2,26},{3,27},{4,28},{5,29},{6,30},{7,31},{8,16},{9,... | collective-permute-start | bytes 884744 | tf_op jit(solution)/shard_map/ppermute | solution.py:46
  56.5 14.0 %collective-permute-start.14 = (bf16[2,192,384]{2,1,0:T(8,128)(2,1)S(1)}, bf16[2,192,384]{2,1,0:T(8,128)(2,1)S(1)}, u32[]{:S(2)}, u32[]{:S(2)}) collective-permute-start(bf16[2,192,384]{2,1,0:T(8,128)(2,1)S(1)} %get-tuple-element.100), channel_id=1, source_target_pairs={{0,2},{1,3},{2,4},{3,5},{8,10},{9,11},{10,12},{11,13},{12,14},{13,... | collective-permute-start | bytes 884744 | tf_op jit(solution)/shard_map/ppermute | solution.py:46
  59.8 20.2 %copy-start.3 = (bf16[2,384,384]{2,1,0:T(8,128)(2,1)}, bf16[2,384,384]{2,1,0:T(8,128)(2,1)S(1)}, u32[]{:S(2)}) copy-start(bf16[2,384,384]{2,1,0:T(8,128)(2,1)S(1)} %pad_maximum_fusion.3.refs_9_) | copy-start | bytes 1769476
  59.9 0.9 collective-permute-start.15
  60.8 20.6 %copy-start.4 = (bf16[2,384,384]{2,1,0:T(8,128)(2,1)}, bf16[2,384,384]{2,1,0:T(8,128)(2,1)S(1)}, u32[]{:S(2)}) copy-start(bf16[2,384,384]{2,1,0:T(8,128)(2,1)S(1)} %pad_maximum_fusion.2.refs_8_) | copy-start | bytes 1769476
  60.8 21.3 %copy-start.9 = (bf16[2,192,384]{2,1,0:T(8,128)(2,1)}, bf16[2,192,384]{2,1,0:T(8,128)(2,1)S(1)}, u32[]{:S(2)}) copy-start(bf16[2,192,384]{2,1,0:T(8,128)(2,1)S(1)} %collective-permute-done.15.refs_12_) | copy-start | bytes 884740
  60.8 10.2 %collective-permute-start.24 = (bf16[2,192,384]{2,1,0:T(8,128)(2,1)S(1)}, bf16[2,192,384]{2,1,0:T(8,128)(2,1)S(1)}, u32[]{:S(2)}, u32[]{:S(2)}) collective-permute-start(bf16[2,192,384]{2,1,0:T(8,128)(2,1)S(1)} %collective-permute-done.13.refs_10_), channel_id=1, source_target_pairs={{0,8},{1,9},{2,10},{3,11},{4,12},{5,13},{6,14},{7,15},{8,0},{9,1},... | collective-permute-start | bytes 884744 | tf_op jit(solution)/shard_map/ppermute | solution.py:46
  69.8 8.9 %collective-permute-start.7 = (bf16[384,768]{1,0:T(8,128)(2,1)S(1)}, bf16[384,768]{1,0:T(8,128)(2,1)S(1)}, u32[]{:S(2)}, u32[]{:S(2)}) collective-permute-start(bf16[384,768]{1,0:T(8,128)(2,1)S(1)} %pad_maximum_fusion.refs_0_), channel_id=1, source_target_pairs={{0,8},{1,9},{2,10},{3,11},{4,12},{5,13},{6,14},{7,15},{8,0},{9,1},... | collective-permute-start | bytes 1769480 | tf_op jit(solution)/shard_map/ppermute | solution.py:46
  69.9 9.4 %collective-permute-start.22 = (bf16[2,384,384]{2,1,0:T(8,128)(2,1)S(1)}, bf16[2,384,384]{2,1,0:T(8,128)(2,1)S(1)}, u32[]{:S(2)}, u32[]{:S(2)}) collective-permute-start(bf16[2,384,384]{2,1,0:T(8,128)(2,1)S(1)} %pad_maximum_fusion.2.refs_8_), channel_id=1, source_target_pairs={{0,8},{1,9},{2,10},{3,11},{4,12},{5,13},{6,14},{7,15},{8,0},{9,1},... | collective-permute-start | bytes 1769480 | tf_op jit(solution)/shard_map/ppermute | solution.py:46
  70.4 9.7 %collective-permute-start.23 = (bf16[2,384,384]{2,1,0:T(8,128)(2,1)S(1)}, bf16[2,384,384]{2,1,0:T(8,128)(2,1)S(1)}, u32[]{:S(2)}, u32[]{:S(2)}) collective-permute-start(bf16[2,384,384]{2,1,0:T(8,128)(2,1)S(1)} %pad_maximum_fusion.3.refs_9_), channel_id=1, source_target_pairs={{0,8},{1,9},{2,10},{3,11},{4,12},{5,13},{6,14},{7,15},{8,0},{9,1},... | collective-permute-start | bytes 1769480 | tf_op jit(solution)/shard_map/ppermute | solution.py:46
  70.5 3.4 %collective-permute-start.25 = (bf16[2,192,384]{2,1,0:T(8,128)(2,1)S(1)}, bf16[2,192,384]{2,1,0:T(8,128)(2,1)S(1)}, u32[]{:S(2)}, u32[]{:S(2)}) collective-permute-start(bf16[2,192,384]{2,1,0:T(8,128)(2,1)S(1)} %collective-permute-done.14.refs_11_), channel_id=1, source_target_pairs={{0,8},{1,9},{2,10},{3,11},{4,12},{5,13},{6,14},{7,15},{8,0},{9,1},... | collective-permute-start | bytes 884744 | tf_op jit(solution)/shard_map/ppermute | solution.py:46
  71.0 10.4 %collective-permute-start.17 = (bf16[2,192,384]{2,1,0:T(8,128)(2,1)S(1)}, bf16[2,192,384]{2,1,0:T(8,128)(2,1)S(1)}, u32[]{:S(2)}, u32[]{:S(2)}) collective-permute-start(bf16[2,192,384]{2,1,0:T(8,128)(2,1)S(1)} %broadcast_select_fusion.3), channel_id=1, source_target_pairs={{4,6},{5,7},{8,12},{9,13},{12,14},{13,15},{20,22},{21,23},{24,28},... | collective-permute-start | bytes 884744 | tf_op jit(solution)/shard_map/ppermute | solution.py:46
  71.7 38.1 %copy-start.6 = (bf16[384,768]{1,0:T(8,128)(2,1)}, bf16[384,768]{1,0:T(8,128)(2,1)S(1)}, u32[]{:S(2)}) copy-start(bf16[384,768]{1,0:T(8,128)(2,1)S(1)} %pad_maximum_fusion.1.refs_2_) | copy-start | bytes 1769476
  74.0 34.1 %copy-start.27 = (bf16[2,192,384]{2,1,0:T(8,128)(2,1)}, bf16[2,192,384]{2,1,0:T(8,128)(2,1)S(1)}, u32[]{:S(2)}) copy-start(bf16[2,192,384]{2,1,0:T(8,128)(2,1)S(1)} %collective-permute-done.25.refs_22_) | copy-start | bytes 884740
  74.0 15.3 %collective-permute-start.8 = (bf16[384,768]{1,0:T(8,128)(2,1)S(1)}, bf16[384,768]{1,0:T(8,128)(2,1)S(1)}, u32[]{:S(2)}, u32[]{:S(2)}) collective-permute-start(bf16[384,768]{1,0:T(8,128)(2,1)S(1)} %pad_maximum_fusion.1.refs_2_), channel_id=1, source_target_pairs={{0,8},{1,9},{2,10},{3,11},{4,12},{5,13},{6,14},{7,15},{8,0},{9,1},... | collective-permute-start | bytes 1769480 | tf_op jit(solution)/shard_map/ppermute | solution.py:46
  78.6 31.2 %copy-start.16 = (bf16[384,768]{1,0:T(8,128)(2,1)}, bf16[384,768]{1,0:T(8,128)(2,1)S(1)}, u32[]{:S(2)}) copy-start(bf16[384,768]{1,0:T(8,128)(2,1)S(1)} %collective-permute-done.7.refs_1_) | copy-start | bytes 1769476
  78.6 3.5 %collective-permute-start.16 = (bf16[2,192,384]{2,1,0:T(8,128)(2,1)S(1)}, bf16[2,192,384]{2,1,0:T(8,128)(2,1)S(1)}, u32[]{:S(2)}, u32[]{:S(2)}) collective-permute-start(bf16[2,192,384]{2,1,0:T(8,128)(2,1)S(1)} %broadcast_select_fusion.4), channel_id=1, source_target_pairs={{2,4},{3,5},{4,6},{5,7},{8,10},{9,11},{10,12},{11,13},{12,14},{13,... | collective-permute-start | bytes 884744 | tf_op jit(solution)/shard_map/ppermute | solution.py:46
  79.3 30.5 %copy-start.17 = (bf16[2,384,384]{2,1,0:T(8,128)(2,1)}, bf16[2,384,384]{2,1,0:T(8,128)(2,1)S(1)}, u32[]{:S(2)}) copy-start(bf16[2,384,384]{2,1,0:T(8,128)(2,1)S(1)} %collective-permute-done.22.refs_19_) | copy-start | bytes 1769476
  79.3 14.8 %collective-permute-start.21 = (bf16[2,384,384]{2,1,0:T(8,128)(2,1)S(1)}, bf16[2,384,384]{2,1,0:T(8,128)(2,1)S(1)}, u32[]{:S(2)}, u32[]{:S(2)}) collective-permute-start(bf16[2,384,384]{2,1,0:T(8,128)(2,1)S(1)} %pad_maximum_fusion.3.refs_9_), channel_id=1, source_target_pairs={{12,8},{13,9},{28,24},{29,25}} | collective-permute-start | bytes 1769480 | tf_op jit(solution)/shard_map/ppermute | solution.py:46
  80.1 29.8 %copy-start.18 = (bf16[2,384,384]{2,1,0:T(8,128)(2,1)}, bf16[2,384,384]{2,1,0:T(8,128)(2,1)S(1)}, u32[]{:S(2)}) copy-start(bf16[2,384,384]{2,1,0:T(8,128)(2,1)S(1)} %collective-permute-done.23.refs_20_) | copy-start | bytes 1769476
  80.1 24.3 %collective-permute-start.20 = (bf16[2,384,384]{2,1,0:T(8,128)(2,1)S(1)}, bf16[2,384,384]{2,1,0:T(8,128)(2,1)S(1)}, u32[]{:S(2)}, u32[]{:S(2)}) collective-permute-start(bf16[2,384,384]{2,1,0:T(8,128)(2,1)S(1)} %pad_maximum_fusion.3.refs_9_), channel_id=1, source_target_pairs={{2,0},{3,1},{10,8},{11,9},{12,10},{13,11},{18,16},{19,17},{26,24},... | collective-permute-start | bytes 1769480 | tf_op jit(solution)/shard_map/ppermute | solution.py:46
  81.4 26.7 %copy-start.28 = (bf16[2,192,384]{2,1,0:T(8,128)(2,1)}, bf16[2,192,384]{2,1,0:T(8,128)(2,1)S(1)}, u32[]{:S(2)}) copy-start(bf16[2,192,384]{2,1,0:T(8,128)(2,1)S(1)} %collective-permute-done.17.refs_14_) | copy-start | bytes 884740
  81.4 23.1 %collective-permute-start.19 = (bf16[2,384,384]{2,1,0:T(8,128)(2,1)S(1)}, bf16[2,384,384]{2,1,0:T(8,128)(2,1)S(1)}, u32[]{:S(2)}, u32[]{:S(2)}) collective-permute-start(bf16[2,384,384]{2,1,0:T(8,128)(2,1)S(1)} %pad_maximum_fusion.2.refs_8_), channel_id=1, source_target_pairs={{8,14},{9,15},{24,30},{25,31}} | collective-permute-start | bytes 1769480 | tf_op jit(solution)/shard_map/ppermute | solution.py:46
  82.1 27.7 %copy-start.10 = (bf16[2,192,384]{2,1,0:T(8,128)(2,1)}, bf16[2,192,384]{2,1,0:T(8,128)(2,1)S(1)}, u32[]{:S(2)}) copy-start(bf16[2,192,384]{2,1,0:T(8,128)(2,1)S(1)} %collective-permute-done.16.refs_13_) | copy-start | bytes 884740
  82.1 8.2 %collective-permute-start.26 = (bf16[2,192,384]{2,1,0:T(8,128)(2,1)S(1)}, bf16[2,192,384]{2,1,0:T(8,128)(2,1)S(1)}, u32[]{:S(2)}, u32[]{:S(2)}) collective-permute-start(bf16[2,192,384]{2,1,0:T(8,128)(2,1)S(1)} %collective-permute-done.15.refs_12_), channel_id=1, source_target_pairs={{0,8},{1,9},{2,10},{3,11},{4,12},{5,13},{6,14},{7,15},{8,0},{9,1},... | collective-permute-start | bytes 884744 | tf_op jit(solution)/shard_map/ppermute | solution.py:46
  89.2 20.6 %copy-start.19 = (bf16[384,768]{1,0:T(8,128)(2,1)}, bf16[384,768]{1,0:T(8,128)(2,1)S(1)}, u32[]{:S(2)}) copy-start(bf16[384,768]{1,0:T(8,128)(2,1)S(1)} %collective-permute-done.8.refs_3_) | copy-start | bytes 1769476
  89.3 15.7 %collective-permute-start.18 = (bf16[2,192,384]{2,1,0:T(8,128)(2,1)S(1)}, bf16[2,192,384]{2,1,0:T(8,128)(2,1)S(1)}, u32[]{:S(2)}, u32[]{:S(2)}) collective-permute-start(bf16[2,192,384]{2,1,0:T(8,128)(2,1)S(1)} %broadcast_select_fusion.2), channel_id=1, source_target_pairs={{4,6},{5,7},{8,12},{9,13},{12,14},{13,15},{20,22},{21,23},{24,28},... | collective-permute-start | bytes 884744 | tf_op jit(solution)/shard_map/ppermute | solution.py:46
  90.4 14.5 %collective-permute-start.28 = (bf16[2,192,384]{2,1,0:T(8,128)(2,1)S(1)}, bf16[2,192,384]{2,1,0:T(8,128)(2,1)S(1)}, u32[]{:S(2)}, u32[]{:S(2)}) collective-permute-start(bf16[2,192,384]{2,1,0:T(8,128)(2,1)S(1)} %collective-permute-done.17.refs_14_), channel_id=1, source_target_pairs={{0,8},{1,9},{2,10},{3,11},{4,12},{5,13},{6,14},{7,15},{8,0},{9,1},... | collective-permute-start | bytes 884744 | tf_op jit(solution)/shard_map/ppermute | solution.py:46
  94.1 13.9 %collective-permute-start.32 = (bf16[2,384,384]{2,1,0:T(8,128)(2,1)S(1)}, bf16[2,384,384]{2,1,0:T(8,128)(2,1)S(1)}, u32[]{:S(2)}, u32[]{:S(2)}) collective-permute-start(bf16[2,384,384]{2,1,0:T(8,128)(2,1)S(1)} %collective-permute-done.21.refs_18_), channel_id=1, source_target_pairs={{0,8},{1,9},{2,10},{3,11},{4,12},{5,13},{6,14},{7,15},{8,0},{9,1},... | collective-permute-start | bytes 1769480 | tf_op jit(solution)/shard_map/ppermute | solution.py:46
  104.3 3.7 %collective-permute-start.31 = (bf16[2,384,384]{2,1,0:T(8,128)(2,1)S(1)}, bf16[2,384,384]{2,1,0:T(8,128)(2,1)S(1)}, u32[]{:S(2)}, u32[]{:S(2)}) collective-permute-start(bf16[2,384,384]{2,1,0:T(8,128)(2,1)S(1)} %collective-permute-done.20.refs_17_), channel_id=1, source_target_pairs={{0,8},{1,9},{2,10},{3,11},{4,12},{5,13},{6,14},{7,15},{8,0},{9,1},... | collective-permute-start | bytes 1769480 | tf_op jit(solution)/shard_map/ppermute | solution.py:46
  104.5 5.4 %collective-permute-start.30 = (bf16[2,384,384]{2,1,0:T(8,128)(2,1)S(1)}, bf16[2,384,384]{2,1,0:T(8,128)(2,1)}, u32[]{:S(2)}, u32[]{:S(2)}) collective-permute-start(bf16[2,384,384]{2,1,0:T(8,128)(2,1)S(1)} %collective-permute-done.19.refs_16_), channel_id=1, source_target_pairs={{0,8},{1,9},{2,10},{3,11},{4,12},{5,13},{6,14},{7,15},{8,0},{9,1},... | collective-permute-start | bytes 1769480 | tf_op jit(solution)/shard_map/ppermute | solution.py:46
  104.9 2.3 %collective-permute-start.27 = (bf16[2,192,384]{2,1,0:T(8,128)(2,1)S(1)}, bf16[2,192,384]{2,1,0:T(8,128)(2,1)S(1)}, u32[]{:S(2)}, u32[]{:S(2)}) collective-permute-start(bf16[2,192,384]{2,1,0:T(8,128)(2,1)S(1)} %collective-permute-done.16.refs_13_), channel_id=1, source_target_pairs={{0,8},{1,9},{2,10},{3,11},{4,12},{5,13},{6,14},{7,15},{8,0},{9,1},... | collective-permute-start | bytes 884744 | tf_op jit(solution)/shard_map/ppermute | solution.py:46
  105.0 3.0 %collective-permute-start.29 = (bf16[2,192,384]{2,1,0:T(8,128)(2,1)S(1)}, bf16[2,192,384]{2,1,0:T(8,128)(2,1)S(1)}, u32[]{:S(2)}, u32[]{:S(2)}) collective-permute-start(bf16[2,192,384]{2,1,0:T(8,128)(2,1)S(1)} %collective-permute-done.18.refs_15_), channel_id=1, source_target_pairs={{0,8},{1,9},{2,10},{3,11},{4,12},{5,13},{6,14},{7,15},{8,0},{9,1},... | collective-permute-start | bytes 884744 | tf_op jit(solution)/shard_map/ppermute | solution.py:46
  118.0 9.3 %collective-permute-start.33 = (bf16[2,192,384]{2,1,0:T(8,128)(2,1)}, bf16[2,192,384]{2,1,0:T(8,128)(2,1)S(1)}, u32[]{:S(2)}, u32[]{:S(2)}) collective-permute-start(bf16[2,192,384]{2,1,0:T(8,128)(2,1)} %get-tuple-element.83), channel_id=1, source_target_pairs={{0,1},{1,0},{2,3},{3,2},{4,5},{5,4},{6,7},{7,6},{8,9},{9,8},{10,11... | collective-permute-start | bytes 884744 | tf_op jit(solution)/shard_map/ppermute | solution.py:46
  118.6 12.4 %collective-permute-start.34 = (bf16[384,384]{1,0:T(8,128)(2,1)}, bf16[384,384]{1,0:T(8,128)(2,1)S(1)}, u32[]{:S(2)}, u32[]{:S(2)}) collective-permute-start(bf16[384,384]{1,0:T(8,128)(2,1)} %get-tuple-element.80), channel_id=1, source_target_pairs={{0,8},{1,9},{2,10},{3,11},{4,12},{5,13},{6,14},{7,15},{8,0},{9,1},... | collective-permute-start | bytes 884744 | tf_op jit(solution)/shard_map/ppermute | solution.py:46
  118.6 12.4 %collective-permute-start.35 = (bf16[384,384]{1,0:T(8,128)(2,1)}, bf16[384,384]{1,0:T(8,128)(2,1)S(1)}, u32[]{:S(2)}, u32[]{:S(2)}) collective-permute-start(bf16[384,384]{1,0:T(8,128)(2,1)} %get-tuple-element.81), channel_id=1, source_target_pairs={{0,16},{1,17},{2,18},{3,19},{4,20},{5,21},{6,22},{7,23},{8,24},{9,... | collective-permute-start | bytes 884744 | tf_op jit(solution)/shard_map/ppermute | solution.py:46
  118.7 15.5 %collective-permute-start.36 = (bf16[384,384]{1,0:T(8,128)(2,1)}, bf16[384,384]{1,0:T(8,128)(2,1)S(1)}, u32[]{:S(2)}, u32[]{:S(2)}) collective-permute-start(bf16[384,384]{1,0:T(8,128)(2,1)} %get-tuple-element.82), channel_id=1, source_target_pairs={{0,24},{1,25},{2,26},{3,27},{4,28},{5,29},{6,30},{7,31},{8,16},{9,... | collective-permute-start | bytes 884744 | tf_op jit(solution)/shard_map/ppermute | solution.py:46
  (27 other events, 199.8 us)

commit v14 on v13

--- a/solution.py
+++ b/solution.py
@@ -68,8 +68,12 @@
                     break
         return sends
 
+    def left(self):
+        top = self.moments - 1
+        return {col: ((top, col), col - 1) for col in range(1, self.cols - 1)}
+
     def rest(self):
-        done = {(key, to) for key, to, _ in self.ring().values()}
+        done = {(key, to) for key, to, _ in self.ring().values()} | set(self.left().values())
         wanted = [
             (key, to)
             for key in self.keys
@@ -442,6 +446,12 @@
         for key, to, _ in sends.values():
             found[key, to, q] = (value, 0)
 
+    def left_step(k):
+        value = shift({col: own[k][top] for col in plan.left()}, plan.left(), ())
+        for key, to in plan.left().values():
+            found[key, to, k] = (value, 0)
+        return value
+
     def rest_step(number, *behind):
         step = rest[number]
         value = shift({col: both[key[0]] for col, (key, _) in step.items()}, step, behind)
@@ -449,11 +459,12 @@
             for k in range(len(plan.chunks)):
                 found[key, to, k] = (value, plan.starts[k])
 
+    lefts = [left_step(k) for k in range(len(plan.chunks))]
     for number in range(cols - 1):
         for k in range(len(plan.chunks)):
             behind = [got[k - 1][number]] if k and number else []
             if number == 1 and k + 1 < len(plan.chunks):
-                behind.append(came[k + 1])
+                behind += [came[k + 1], lefts[k]]
             ring_step(k, number, *behind)
     for number in range(len(rest)):
         low = any(key[0] < top for key, _ in rest[number].values())

time: 138 us -> 135 us (0.978)
  the two profiles are of different devices: /device:TPU:0 before, /device:TPU:25 now
where the time goes in v14:
time: 135 us; the launch traced here: 134 us
  waiting for transfers between devices  59.1 us (44%)
  starting transfers between devices  31.4 us (23%)
  Pallas kernels  22.9 us (17%)
  local copies, waits for them, and re-layouts  16.3 us (12%)
  other arithmetic  2.89 us (2%)
  between operations  1.42 us (1%)
    ppermute x39, waiting for transfers between devices, send(): return lax.ppermute(value, AXES, pairs)  59.1 us
    ppermute x39, starting transfers between devices, send(): return lax.ppermute(value, AXES, pairs)  31.4 us
    pallas_call x2, Pallas kernels, self_energy(): pl.pallas_call(functools.partial(sigma_kernel, plan, pair_count, u, copie...  9.22 us
    pallas_call x1, Pallas kernels, on_device(): pl.pallas_call(functools.partial(solve_kernel, plan, sources), out_shape=...  8.05 us
    unnamed x90, local copies, waits for them, and re-layouts  5.15 us
    dynamic_slice x5, local copies, waits for them, and re-layouts, on_device(): lax.dynamic_index_in_dim(right, r ^ s, 0, keepdims=False)  3.75 us
    dynamic_slice x2, local copies, waits for them, and re-layouts, part_of(): lax.dynamic_slice_in_dim(value, (y ^ q) * half + u * plan.sub, plan.sub, 2)  2.96 us
    pallas_call x1, Pallas kernels, on_device(): pl.pallas_call(functools.partial(place_kernel, plan), out_shape=jax.Shape...  2.95 us
  transfers between devices with their start and end apart: 39, of which 13 were waited for; matrix products, arithmetic and copies ran while one was open for 9% of the time, Pallas kernels for 6%

profile of v14, /device:TPU:25, one launch (start us, length us, event | category | flops | bytes accessed | tf_op | source)
XLA Modules:
  0.0 134.0 jit_solution(17401539258645938317)
XLA Ops:
  0.7 2.1 %constant_dynamic-slice_fusion = (bf16[2,2,96,384]{3,2,1,0:T(8,128)(2,1)}, bf16[2,2,96,384]{3,2,1,0:T(8,128)(2,1)}) fusion(bf16[2,2,384,384]{3,2,1,0:T(8,128)(2,1)} %refs_0_.3, s32[]{:T(128)S(6)} %select_n.109, s32[]{:T(128)S(6)} %select_n.101), kind=kLoop, calls=%fused_computation.27 | loop fusion | bytes 1179656 | tf_op jit(solution)/shard_map/dynamic_slice | solution.py:332
  2.7 1.2 collective-permute-start.1
  4.0 0.8 copy.11
  4.8 0.9 dynamic-slice_bitcast_fusion.2
  5.9 0.9 dynamic-slice_bitcast_fusion
  6.8 1.2 collective-permute-start
  8.6 2.0 %copy.12 = bf16[2,384,2,384]{1,3,2,0:T(8,128)(2,1)S(1)} copy(bf16[2,384,2,384]{3,2,1,0:T(2,128)(2,1)S(1)} %copy-done.13) | data formatting | bytes 2359296 | tf_op jit(solution)/shard_map/optimization_barrier | solution.py:287
  11.5 1.2 collective-permute-start.2
  13.6 0.9 copy.17
  14.5 0.9 copy.16
  15.4 0.9 copy.15
  16.3 0.9 copy.14
  17.2 3.4 %collective-permute-done = bf16[2,384,384]{2,1,0:T(8,128)(2,1)S(1)} collective-permute-done((bf16[2,384,384]{2,1,0:T(8,128)(2,1)}, bf16[2,384,384]{2,1,0:T(8,128)(2,1)S(1)}, u32[]{:S(2)}, u32[]{:S(2)}) %collective-permute-start) | collective-permute-done | bytes 589856 | tf_op jit(solution)/shard_map/ppermute | solution.py:46
  20.7 4.5 %self_energy.2 = (bf16[2,96,384]{2,1,0:T(8,128)(2,1)}, bf16[2,96,384]{2,1,0:T(8,128)(2,1)}, bf16[2,96,384]{2,1,0:T(8,128)(2,1)}, bf16[2,96,384]{2,1,0:T(8,128)(2,1)}) custom-call(s32[3]{0:T(128)} %pad_add_fusion.place, s32[4,8]{1,0:T(4,128)} %fusion.1.quads, s32[4,8]{1,0:T(4,128)} %slice_bitcast_fusion.4.thirds, bf16[2,2,384,384]{3,2,1,0:T(8,128)(2,1)} %refs_0_.3, ...), custom_call_target="tpu_custom_call" | custom-call | tf_op jit(solution)/shard_map/self_energy/pallas_call | solution.py:364
  25.2 4.6 %collective-permute-done.3.refs_3_ = bf16[2,2,96,384]{3,2,1,0:T(8,128)(2,1)S(1)} collective-permute-done((bf16[2,2,96,384]{3,2,1,0:T(8,128)(2,1)}, bf16[2,2,96,384]{3,2,1,0:T(8,128)(2,1)S(1)}, u32[]{:S(2)}, u32[]{:S(2)}) %collective-permute-start.3) | collective-permute-done | bytes 294944 | tf_op jit(solution)/shard_map/ppermute | solution.py:46
  29.8 0.7 copy-done.38
  30.5 4.8 %self_energy.3 = (bf16[2,192,384]{2,1,0:T(8,128)(2,1)}, bf16[2,192,384]{2,1,0:T(8,128)(2,1)}, bf16[2,192,384]{2,1,0:T(8,128)(2,1)}, bf16[2,192,384]{2,1,0:T(8,128)(2,1)}) custom-call(s32[3]{0:T(128)} %pad_add_fusion.place, s32[4,8]{1,0:T(4,128)} %fusion.1.quads, s32[4,8]{1,0:T(4,128)} %slice_bitcast_fusion.4.thirds, bf16[2,2,384,384]{3,2,1,0:T(8,128)(2,1)} %refs_0_.3, ...), custom_call_target="tpu_custom_call" | custom-call | tf_op jit(solution)/shard_map/self_energy/pallas_call | solution.py:364
  36.0 1.3 collective-permute-start.5
  38.0 1.0 broadcast_select_fusion.7
  39.0 1.4 %collective-permute-start.15 = (bf16[2,192,384]{2,1,0:T(8,128)(2,1)S(1)}, bf16[2,192,384]{2,1,0:T(8,128)(2,1)S(1)}, u32[]{:S(2)}, u32[]{:S(2)}) collective-permute-start(bf16[2,192,384]{2,1,0:T(8,128)(2,1)S(1)} %get-tuple-element.98), channel_id=1, source_target_pairs={{0,2},{1,3},{2,4},{3,5},{8,10},{9,11},{10,12},{11,13},{12,14},{13,... | collective-permute-start | bytes 884744 | tf_op jit(solution)/shard_map/ppermute | solution.py:46
  41.2 2.0 %collective-permute-done.5.refs_2_ = bf16[2,192,384]{2,1,0:T(8,128)(2,1)S(1)} collective-permute-done((bf16[2,192,384]{2,1,0:T(8,128)(2,1)}, bf16[2,192,384]{2,1,0:T(8,128)(2,1)S(1)}, u32[]{:S(2)}, u32[]{:S(2)}) %collective-permute-start.5) | collective-permute-done | bytes 294944 | tf_op jit(solution)/shard_map/ppermute | solution.py:46
  43.3 1.3 collective-permute-start.16
  45.3 1.9 %collective-permute-start.9 = (bf16[384,384]{1,0:T(8,128)(2,1)S(1)}, bf16[384,384]{1,0:T(8,128)(2,1)S(1)}, u32[]{:S(2)}, u32[]{:S(2)}) collective-permute-start(bf16[384,384]{1,0:T(8,128)(2,1)S(1)} %bitcast.44), channel_id=1, source_target_pairs={{0,8},{1,9},{2,10},{3,11},{4,12},{5,13},{6,14},{7,15},{8,0},{9,1},... | collective-permute-start | bytes 884744 | tf_op jit(solution)/shard_map/ppermute | solution.py:46
  47.2 3.7 %collective-permute-done.15.refs_12_ = bf16[2,192,384]{2,1,0:T(8,128)(2,1)S(1)} collective-permute-done((bf16[2,192,384]{2,1,0:T(8,128)(2,1)S(1)}, bf16[2,192,384]{2,1,0:T(8,128)(2,1)S(1)}, u32[]{:S(2)}, u32[]{:S(2)}) %collective-permute-start.15) | collective-permute-done | bytes 294944 | tf_op jit(solution)/shard_map/ppermute | solution.py:46
  51.0 1.3 collective-permute-start.17
  52.5 0.9 copy-done.41
  53.4 9.1 %collective-permute-done.17.refs_14_ = bf16[2,192,384]{2,1,0:T(8,128)(2,1)S(1)} collective-permute-done((bf16[2,192,384]{2,1,0:T(8,128)(2,1)S(1)}, bf16[2,192,384]{2,1,0:T(8,128)(2,1)S(1)}, u32[]{:S(2)}, u32[]{:S(2)}) %collective-permute-start.17) | collective-permute-done | bytes 294944 | tf_op jit(solution)/shard_map/ppermute | solution.py:46
  62.5 3.6 %collective-permute-start.27 = (bf16[2,192,384]{2,1,0:T(8,128)(2,1)S(1)}, bf16[2,192,384]{2,1,0:T(8,128)(2,1)S(1)}, u32[]{:S(2)}, u32[]{:S(2)}) collective-permute-start(bf16[2,192,384]{2,1,0:T(8,128)(2,1)S(1)} %collective-permute-done.15.refs_12_), channel_id=1, source_target_pairs={{0,8},{1,9},{2,10},{3,11},{4,12},{5,13},{6,14},{7,15},{8,0},{9,1},... | collective-permute-start | bytes 884744 | tf_op jit(solution)/shard_map/ppermute | solution.py:46
  67.4 1.3 collective-permute-start.19
  69.3 1.3 collective-permute-start.18
  71.3 0.7 collective-permute-start.22
  72.1 10.4 %collective-permute-done.19.refs_16_ = bf16[2,192,384]{2,1,0:T(8,128)(2,1)S(1)} collective-permute-done((bf16[2,192,384]{2,1,0:T(8,128)(2,1)S(1)}, bf16[2,192,384]{2,1,0:T(8,128)(2,1)S(1)}, u32[]{:S(2)}, u32[]{:S(2)}) %collective-permute-start.19) | collective-permute-done | bytes 294944 | tf_op jit(solution)/shard_map/ppermute | solution.py:46
  82.5 1.3 collective-permute-start.21
  83.9 4.6 %collective-permute-done.18.refs_15_ = bf16[2,192,384]{2,1,0:T(8,128)(2,1)S(1)} collective-permute-done((bf16[2,192,384]{2,1,0:T(8,128)(2,1)S(1)}, bf16[2,192,384]{2,1,0:T(8,128)(2,1)S(1)}, u32[]{:S(2)}, u32[]{:S(2)}) %collective-permute-start.18) | collective-permute-done | bytes 294944 | tf_op jit(solution)/shard_map/ppermute | solution.py:46
  89.1 1.5 %collective-permute-start.20 = (bf16[2,192,384]{2,1,0:T(8,128)(2,1)S(1)}, bf16[2,192,384]{2,1,0:T(8,128)(2,1)S(1)}, u32[]{:S(2)}, u32[]{:S(2)}) collective-permute-start(bf16[2,192,384]{2,1,0:T(8,128)(2,1)S(1)} %broadcast_select_fusion.2), channel_id=1, source_target_pairs={{4,6},{5,7},{8,12},{9,13},{12,14},{13,15},{20,22},{21,23},{24,28},... | collective-permute-start | bytes 884744 | tf_op jit(solution)/shard_map/ppermute | solution.py:46
  91.1 4.0 %collective-permute-done.21.refs_18_ = bf16[2,384,384]{2,1,0:T(8,128)(2,1)S(1)} collective-permute-done((bf16[2,384,384]{2,1,0:T(8,128)(2,1)S(1)}, bf16[2,384,384]{2,1,0:T(8,128)(2,1)S(1)}, u32[]{:S(2)}, u32[]{:S(2)}) %collective-permute-start.21) | collective-permute-done | bytes 589856 | tf_op jit(solution)/shard_map/ppermute | solution.py:46
  95.6 5.8 %collective-permute-done.20.refs_17_ = bf16[2,192,384]{2,1,0:T(8,128)(2,1)S(1)} collective-permute-done((bf16[2,192,384]{2,1,0:T(8,128)(2,1)S(1)}, bf16[2,192,384]{2,1,0:T(8,128)(2,1)S(1)}, u32[]{:S(2)}, u32[]{:S(2)}) %collective-permute-start.20) | collective-permute-done | bytes 294944 | tf_op jit(solution)/shard_map/ppermute | solution.py:46
  101.9 1.2 collective-permute-done.32.refs_29_
  103.9 0.8 copy-done.22
  104.7 0.8 copy-done.23
  105.5 8.1 %substitution.1 = (bf16[384,384]{1,0:T(8,128)(2,1)}, bf16[384,384]{1,0:T(8,128)(2,1)}, bf16[384,384]{1,0:T(8,128)(2,1)}, bf16[384,384]{1,0:T(8,128)(2,1)}) custom-call(s32[3]{0:T(128)} %pad_add_fusion.place, bf16[384,768]{1,0:T(8,128)(2,1)} %copy-done.4, bf16[384,768]{1,0:T(8,128)(2,1)} %copy-done.16, bf16[384,768]{1,0:T(8,128)(2,1)} %copy-done.6, ...), custom_call_target="tpu_custom_call" | custom-call | tf_op jit(solution)/shard_map/substitution/pallas_call | solution.py:489
  113.6 1.4 %collective-permute-start.35 = (bf16[2,192,384]{2,1,0:T(8,128)(2,1)}, bf16[2,192,384]{2,1,0:T(8,128)(2,1)S(1)}, u32[]{:S(2)}, u32[]{:S(2)}) collective-permute-start(bf16[2,192,384]{2,1,0:T(8,128)(2,1)} %get-tuple-element.83), channel_id=1, source_target_pairs={{0,1},{1,0},{2,3},{3,2},{4,5},{5,4},{6,7},{7,6},{8,9},{9,8},{10,11... | collective-permute-start | bytes 884744 | tf_op jit(solution)/shard_map/ppermute | solution.py:46
  115.6 1.8 %collective-permute-start.37 = (bf16[384,384]{1,0:T(8,128)(2,1)}, bf16[384,384]{1,0:T(8,128)(2,1)S(1)}, u32[]{:S(2)}, u32[]{:S(2)}) collective-permute-start(bf16[384,384]{1,0:T(8,128)(2,1)} %get-tuple-element.81), channel_id=1, source_target_pairs={{0,16},{1,17},{2,18},{3,19},{4,20},{5,21},{6,22},{7,23},{8,24},{9,... | collective-permute-start | bytes 884744 | tf_op jit(solution)/shard_map/ppermute | solution.py:46
  117.4 4.7 %collective-permute-done.35.refs_3_ = bf16[2,192,384]{2,1,0:T(8,128)(2,1)S(1)} collective-permute-done((bf16[2,192,384]{2,1,0:T(8,128)(2,1)}, bf16[2,192,384]{2,1,0:T(8,128)(2,1)S(1)}, u32[]{:S(2)}, u32[]{:S(2)}) %collective-permute-start.35) | collective-permute-done | bytes 294944 | tf_op jit(solution)/shard_map/ppermute | solution.py:46
  122.1 0.7 copy-done.40
  122.8 2.9 %place_sigma.1 = bf16[2,2,384,384]{3,2,1,0:T(8,128)(2,1)} custom-call(s32[3]{0:T(128)} %pad_add_fusion.place, bf16[2,192,384]{2,1,0:T(8,128)(2,1)} %get-tuple-element.59.refs_0_, bf16[2,192,384]{2,1,0:T(8,128)(2,1)} %get-tuple-element.60.refs_1_, bf16[2,192,384]{2,1,0:T(8,128)(2,1)} %copy-done.11, bf16[2,192,384]{2,1,0:T(8,128)(2,1)} %copy-done.40), custom_call_target="tpu_custom_call" | custom-call | tf_op jit(solution)/shard_map/place_sigma/pallas_call | solution.py:506
  125.8 5.5 %collective-permute-done.38.refs_3_ = bf16[384,384]{1,0:T(8,128)(2,1)S(1)} collective-permute-done((bf16[384,384]{1,0:T(8,128)(2,1)}, bf16[384,384]{1,0:T(8,128)(2,1)S(1)}, u32[]{:S(2)}, u32[]{:S(2)}) %collective-permute-start.38) | collective-permute-done | bytes 294944 | tf_op jit(solution)/shard_map/ppermute | solution.py:46
  131.4 2.7 %place_solution.1 = bf16[2,384,2,384]{3,2,1,0:T(2,128)(2,1)} custom-call(s32[3]{0:T(128)S(1)} %copy-done.1, bf16[384,384]{1,0:T(8,128)(2,1)S(1)} %copy-done, bf16[384,384]{1,0:T(8,128)(2,1)S(1)} %collective-permute-done.36.refs_1_, bf16[384,384]{1,0:T(8,128)(2,1)S(1)} %collective-permute-done.37.refs_2_, bf16[384,384]{1,0:T(8,128)(2,1)S(1)} %collective-permute-done.38.refs_3_), custom_call_target="tpu_custom_call" | custom-call | tf_op jit(solution)/shard_map/place_solution/pallas_call | solution.py:524
  (152 shorter events, 12.0 us)
Async XLA Ops:
  2.7 8.8 %collective-permute-start.1 = (bf16[2,2,96,384]{3,2,1,0:T(8,128)(2,1)}, bf16[2,2,96,384]{3,2,1,0:T(8,128)(2,1)}, u32[]{:S(2)}, u32[]{:S(2)}) collective-permute-start(bf16[2,2,96,384]{3,2,1,0:T(8,128)(2,1)} %get-tuple-element.93), channel_id=1, source_target_pairs={{0,1},{1,0},{2,3},{3,2},{4,5},{5,4},{6,7},{7,6},{8,9},{9,8},{10,11... | collective-permute-start | bytes 884744 | tf_op jit(solution)/shard_map/ppermute | solution.py:46
  5.7 15.0 %collective-permute-start.4 = (bf16[2,2,96,384]{3,2,1,0:T(8,128)(2,1)}, bf16[2,2,96,384]{3,2,1,0:T(8,128)(2,1)}, u32[]{:S(2)}, u32[]{:S(2)}) collective-permute-start(bf16[2,2,96,384]{3,2,1,0:T(8,128)(2,1)} %get-tuple-element.91), channel_id=1, source_target_pairs={{0,1},{1,0},{2,3},{3,2},{4,5},{5,4},{6,7},{7,6},{8,9},{9,8},{10,11... | collective-permute-start | bytes 884744 | tf_op jit(solution)/shard_map/ppermute | solution.py:46
  6.8 13.8 %collective-permute-start = (bf16[2,384,384]{2,1,0:T(8,128)(2,1)}, bf16[2,384,384]{2,1,0:T(8,128)(2,1)S(1)}, u32[]{:S(2)}, u32[]{:S(2)}) collective-permute-start(bf16[2,384,384]{2,1,0:T(8,128)(2,1)} %dynamic-slice_bitcast_fusion), channel_id=1, source_target_pairs={{0,16},{1,17},{2,18},{3,19},{4,20},{5,21},{6,22},{7,23},{8,24},{9,... | collective-permute-start | bytes 1769480 | tf_op jit(solution)/shard_map/ppermute | solution.py:46
  11.5 13.7 %collective-permute-start.2 = (bf16[2,2,96,384]{3,2,1,0:T(8,128)(2,1)}, bf16[2,2,96,384]{3,2,1,0:T(8,128)(2,1)S(1)}, u32[]{:S(2)}, u32[]{:S(2)}) collective-permute-start(bf16[2,2,96,384]{3,2,1,0:T(8,128)(2,1)} %get-tuple-element.53), channel_id=1, source_target_pairs={{0,1},{1,0},{2,3},{3,2},{4,5},{5,4},{6,7},{7,6},{8,9},{9,8},{10,11... | collective-permute-start | bytes 884744 | tf_op jit(solution)/shard_map/ppermute | solution.py:46
  12.7 17.0 %collective-permute-start.3 = (bf16[2,2,96,384]{3,2,1,0:T(8,128)(2,1)}, bf16[2,2,96,384]{3,2,1,0:T(8,128)(2,1)S(1)}, u32[]{:S(2)}, u32[]{:S(2)}) collective-permute-start(bf16[2,2,96,384]{3,2,1,0:T(8,128)(2,1)} %get-tuple-element.54), channel_id=1, source_target_pairs={{0,1},{1,0},{2,3},{3,2},{4,5},{5,4},{6,7},{7,6},{8,9},{9,8},{10,11... | collective-permute-start | bytes 884744 | tf_op jit(solution)/shard_map/ppermute | solution.py:46
  35.3 2.7 %collective-permute-start.12 = (bf16[2,192,384]{2,1,0:T(8,128)(2,1)}, bf16[2,192,384]{2,1,0:T(8,128)(2,1)S(1)}, u32[]{:S(2)}, u32[]{:S(2)}) collective-permute-start(bf16[2,192,384]{2,1,0:T(8,128)(2,1)} %get-tuple-element.60.refs_1_), channel_id=1, source_target_pairs={{8,24},{9,25},{16,0},{17,1},{18,2},{19,3},{24,8},{25,9},{26,10},{2... | collective-permute-start | bytes 884744 | tf_op jit(solution)/shard_map/ppermute | solution.py:46
  36.0 7.2 %collective-permute-start.5 = (bf16[2,192,384]{2,1,0:T(8,128)(2,1)}, bf16[2,192,384]{2,1,0:T(8,128)(2,1)S(1)}, u32[]{:S(2)}, u32[]{:S(2)}) collective-permute-start(bf16[2,192,384]{2,1,0:T(8,128)(2,1)} %get-tuple-element.61), channel_id=1, source_target_pairs={{0,1},{1,0},{2,3},{3,2},{4,5},{5,4},{6,7},{7,6},{8,9},{9,8},{10,11... | collective-permute-start | bytes 884744 | tf_op jit(solution)/shard_map/ppermute | solution.py:46
  37.3 5.9 %collective-permute-start.6 = (bf16[2,192,384]{2,1,0:T(8,128)(2,1)}, bf16[2,192,384]{2,1,0:T(8,128)(2,1)S(1)}, u32[]{:S(2)}, u32[]{:S(2)}) collective-permute-start(bf16[2,192,384]{2,1,0:T(8,128)(2,1)} %get-tuple-element.83), channel_id=1, source_target_pairs={{8,25},{9,24},{16,1},{17,0},{18,3},{19,2},{24,9},{25,8},{26,11},{2... | collective-permute-start | bytes 884744 | tf_op jit(solution)/shard_map/ppermute | solution.py:46
  39.0 11.9 %collective-permute-start.15 = (bf16[2,192,384]{2,1,0:T(8,128)(2,1)S(1)}, bf16[2,192,384]{2,1,0:T(8,128)(2,1)S(1)}, u32[]{:S(2)}, u32[]{:S(2)}) collective-permute-start(bf16[2,192,384]{2,1,0:T(8,128)(2,1)S(1)} %get-tuple-element.98), channel_id=1, source_target_pairs={{0,2},{1,3},{2,4},{3,5},{8,10},{9,11},{10,12},{11,13},{12,14},{13,... | collective-permute-start | bytes 884744 | tf_op jit(solution)/shard_map/ppermute | solution.py:46
  40.4 10.5 %collective-permute-start.13 = (bf16[2,192,384]{2,1,0:T(8,128)(2,1)S(1)}, bf16[2,192,384]{2,1,0:T(8,128)(2,1)S(1)}, u32[]{:S(2)}, u32[]{:S(2)}) collective-permute-start(bf16[2,192,384]{2,1,0:T(8,128)(2,1)S(1)} %get-tuple-element.98), channel_id=1, source_target_pairs={{2,0},{3,1},{10,8},{11,9},{12,10},{13,11},{18,16},{19,17},{26,24},... | collective-permute-start | bytes 884744 | tf_op jit(solution)/shard_map/ppermute | solution.py:46
  43.3 23.6 %collective-permute-start.16 = (bf16[2,192,384]{2,1,0:T(8,128)(2,1)S(1)}, bf16[2,192,384]{2,1,0:T(8,128)(2,1)S(1)}, u32[]{:S(2)}, u32[]{:S(2)}) collective-permute-start(bf16[2,192,384]{2,1,0:T(8,128)(2,1)S(1)} %get-tuple-element.100), channel_id=1, source_target_pairs={{0,2},{1,3},{2,4},{3,5},{8,10},{9,11},{10,12},{11,13},{12,14},{13,... | collective-permute-start | bytes 884744 | tf_op jit(solution)/shard_map/ppermute | solution.py:46
  44.6 22.4 %collective-permute-start.14 = (bf16[2,192,384]{2,1,0:T(8,128)(2,1)S(1)}, bf16[2,192,384]{2,1,0:T(8,128)(2,1)S(1)}, u32[]{:S(2)}, u32[]{:S(2)}) collective-permute-start(bf16[2,192,384]{2,1,0:T(8,128)(2,1)S(1)} %get-tuple-element.100), channel_id=1, source_target_pairs={{2,0},{3,1},{10,8},{11,9},{12,10},{13,11},{18,16},{19,17},{26,24},... | collective-permute-start | bytes 884744 | tf_op jit(solution)/shard_map/ppermute | solution.py:46
  45.3 7.2 %collective-permute-start.9 = (bf16[384,384]{1,0:T(8,128)(2,1)S(1)}, bf16[384,384]{1,0:T(8,128)(2,1)S(1)}, u32[]{:S(2)}, u32[]{:S(2)}) collective-permute-start(bf16[384,384]{1,0:T(8,128)(2,1)S(1)} %bitcast.44), channel_id=1, source_target_pairs={{0,8},{1,9},{2,10},{3,11},{4,12},{5,13},{6,14},{7,15},{8,0},{9,1},... | collective-permute-start | bytes 884744 | tf_op jit(solution)/shard_map/ppermute | solution.py:46
  50.9 15.2 %collective-permute-start.10 = (bf16[384,384]{1,0:T(8,128)(2,1)S(1)}, bf16[384,384]{1,0:T(8,128)(2,1)S(1)}, u32[]{:S(2)}, u32[]{:S(2)}) collective-permute-start(bf16[384,384]{1,0:T(8,128)(2,1)S(1)} %bitcast.43), channel_id=1, source_target_pairs={{0,16},{1,17},{2,18},{3,19},{4,20},{5,21},{6,22},{7,23},{8,24},{9,... | collective-permute-start | bytes 884744 | tf_op jit(solution)/shard_map/ppermute | solution.py:46
  51.0 11.5 %collective-permute-start.17 = (bf16[2,192,384]{2,1,0:T(8,128)(2,1)S(1)}, bf16[2,192,384]{2,1,0:T(8,128)(2,1)S(1)}, u32[]{:S(2)}, u32[]{:S(2)}) collective-permute-start(bf16[2,192,384]{2,1,0:T(8,128)(2,1)S(1)} %broadcast_select_fusion.5), channel_id=1, source_target_pairs={{2,4},{3,5},{4,6},{5,7},{8,10},{9,11},{10,12},{11,13},{12,14},{13,... | collective-permute-start | bytes 884744 | tf_op jit(solution)/shard_map/ppermute | solution.py:46
  52.5 18.8 %copy-start.3 = (bf16[2,384,384]{2,1,0:T(8,128)(2,1)}, bf16[2,384,384]{2,1,0:T(8,128)(2,1)S(1)}, u32[]{:S(2)}) copy-start(bf16[2,384,384]{2,1,0:T(8,128)(2,1)S(1)} %pad_maximum_fusion.3.refs_9_) | copy-start | bytes 1769476
  53.4 12.9 %collective-permute-start.11 = (bf16[384,384]{1,0:T(8,128)(2,1)S(1)}, bf16[384,384]{1,0:T(8,128)(2,1)S(1)}, u32[]{:S(2)}, u32[]{:S(2)}) collective-permute-start(bf16[384,384]{1,0:T(8,128)(2,1)S(1)} %bitcast.42), channel_id=1, source_target_pairs={{0,24},{1,25},{2,26},{3,27},{4,28},{5,29},{6,30},{7,31},{8,16},{9,... | collective-permute-start | bytes 884744 | tf_op jit(solution)/shard_map/ppermute | solution.py:46
  62.5 26.4 %copy-start.9 = (bf16[2,192,384]{2,1,0:T(8,128)(2,1)}, bf16[2,192,384]{2,1,0:T(8,128)(2,1)S(1)}, u32[]{:S(2)}) copy-start(bf16[2,192,384]{2,1,0:T(8,128)(2,1)S(1)} %collective-permute-done.17.refs_14_) | copy-start | bytes 884740
  62.5 4.9 %collective-permute-start.27 = (bf16[2,192,384]{2,1,0:T(8,128)(2,1)S(1)}, bf16[2,192,384]{2,1,0:T(8,128)(2,1)S(1)}, u32[]{:S(2)}, u32[]{:S(2)}) collective-permute-start(bf16[2,192,384]{2,1,0:T(8,128)(2,1)S(1)} %collective-permute-done.15.refs_12_), channel_id=1, source_target_pairs={{0,8},{1,9},{2,10},{3,11},{4,12},{5,13},{6,14},{7,15},{8,0},{9,1},... | collective-permute-start | bytes 884744 | tf_op jit(solution)/shard_map/ppermute | solution.py:46
  66.1 5.2 %collective-permute-start.7 = (bf16[384,768]{1,0:T(8,128)(2,1)S(1)}, bf16[384,768]{1,0:T(8,128)(2,1)S(1)}, u32[]{:S(2)}, u32[]{:S(2)}) collective-permute-start(bf16[384,768]{1,0:T(8,128)(2,1)S(1)} %pad_maximum_fusion.refs_0_), channel_id=1, source_target_pairs={{0,8},{1,9},{2,10},{3,11},{4,12},{5,13},{6,14},{7,15},{8,0},{9,1},... | collective-permute-start | bytes 1769480 | tf_op jit(solution)/shard_map/ppermute | solution.py:46
  66.3 2.8 %collective-permute-start.25 = (bf16[2,192,384]{2,1,0:T(8,128)(2,1)S(1)}, bf16[2,192,384]{2,1,0:T(8,128)(2,1)S(1)}, u32[]{:S(2)}, u32[]{:S(2)}) collective-permute-start(bf16[2,192,384]{2,1,0:T(8,128)(2,1)S(1)} %collective-permute-done.13.refs_10_), channel_id=1, source_target_pairs={{0,8},{1,9},{2,10},{3,11},{4,12},{5,13},{6,14},{7,15},{8,0},{9,1},... | collective-permute-start | bytes 884744 | tf_op jit(solution)/shard_map/ppermute | solution.py:46
  66.9 17.0 %copy-start.8 = (bf16[2,192,384]{2,1,0:T(8,128)(2,1)}, bf16[2,192,384]{2,1,0:T(8,128)(2,1)S(1)}, u32[]{:S(2)}) copy-start(bf16[2,192,384]{2,1,0:T(8,128)(2,1)S(1)} %collective-permute-done.16.refs_13_) | copy-start | bytes 884740
  66.9 2.5 %collective-permute-start.28 = (bf16[2,192,384]{2,1,0:T(8,128)(2,1)S(1)}, bf16[2,192,384]{2,1,0:T(8,128)(2,1)}, u32[]{:S(2)}, u32[]{:S(2)}) collective-permute-start(bf16[2,192,384]{2,1,0:T(8,128)(2,1)S(1)} %collective-permute-done.16.refs_13_), channel_id=1, source_target_pairs={{0,8},{1,9},{2,10},{3,11},{4,12},{5,13},{6,14},{7,15},{8,0},{9,1},... | collective-permute-start | bytes 884744 | tf_op jit(solution)/shard_map/ppermute | solution.py:46
  67.0 3.7 %collective-permute-start.26 = (bf16[2,192,384]{2,1,0:T(8,128)(2,1)S(1)}, bf16[2,192,384]{2,1,0:T(8,128)(2,1)S(1)}, u32[]{:S(2)}, u32[]{:S(2)}) collective-permute-start(bf16[2,192,384]{2,1,0:T(8,128)(2,1)S(1)} %collective-permute-done.14.refs_11_), channel_id=1, source_target_pairs={{0,8},{1,9},{2,10},{3,11},{4,12},{5,13},{6,14},{7,15},{8,0},{9,1},... | collective-permute-start | bytes 884744 | tf_op jit(solution)/shard_map/ppermute | solution.py:46
  67.4 15.1 %collective-permute-start.19 = (bf16[2,192,384]{2,1,0:T(8,128)(2,1)S(1)}, bf16[2,192,384]{2,1,0:T(8,128)(2,1)S(1)}, u32[]{:S(2)}, u32[]{:S(2)}) collective-permute-start(bf16[2,192,384]{2,1,0:T(8,128)(2,1)S(1)} %broadcast_select_fusion.3), channel_id=1, source_target_pairs={{4,6},{5,7},{8,12},{9,13},{12,14},{13,15},{20,22},{21,23},{24,28},... | collective-permute-start | bytes 884744 | tf_op jit(solution)/shard_map/ppermute | solution.py:46
  68.8 20.1 %copy-start.5 = (bf16[2,384,384]{2,1,0:T(8,128)(2,1)}, bf16[2,384,384]{2,1,0:T(8,128)(2,1)S(1)}, u32[]{:S(2)}) copy-start(bf16[2,384,384]{2,1,0:T(8,128)(2,1)S(1)} %pad_maximum_fusion.2.refs_8_) | copy-start | bytes 1769476
  69.1 19.8 %collective-permute-start.23 = (bf16[2,384,384]{2,1,0:T(8,128)(2,1)S(1)}, bf16[2,384,384]{2,1,0:T(8,128)(2,1)S(1)}, u32[]{:S(2)}, u32[]{:S(2)}) collective-permute-start(bf16[2,384,384]{2,1,0:T(8,128)(2,1)S(1)} %pad_maximum_fusion.2.refs_8_), channel_id=1, source_target_pairs={{0,8},{1,9},{2,10},{3,11},{4,12},{5,13},{6,14},{7,15},{8,0},{9,1},... | collective-permute-start | bytes 1769480 | tf_op jit(solution)/shard_map/ppermute | solution.py:46
  69.3 19.1 %collective-permute-start.18 = (bf16[2,192,384]{2,1,0:T(8,128)(2,1)S(1)}, bf16[2,192,384]{2,1,0:T(8,128)(2,1)S(1)}, u32[]{:S(2)}, u32[]{:S(2)}) collective-permute-start(bf16[2,192,384]{2,1,0:T(8,128)(2,1)S(1)} %broadcast_select_fusion.4), channel_id=1, source_target_pairs={{2,4},{3,5},{4,6},{5,7},{8,10},{9,11},{10,12},{11,13},{12,14},{13,... | collective-permute-start | bytes 884744 | tf_op jit(solution)/shard_map/ppermute | solution.py:46
  70.6 18.5 %collective-permute-start.24 = (bf16[2,384,384]{2,1,0:T(8,128)(2,1)S(1)}, bf16[2,384,384]{2,1,0:T(8,128)(2,1)S(1)}, u32[]{:S(2)}, u32[]{:S(2)}) collective-permute-start(bf16[2,384,384]{2,1,0:T(8,128)(2,1)S(1)} %pad_maximum_fusion.3.refs_9_), channel_id=1, source_target_pairs={{0,8},{1,9},{2,10},{3,11},{4,12},{5,13},{6,14},{7,15},{8,0},{9,1},... | collective-permute-start | bytes 1769480 | tf_op jit(solution)/shard_map/ppermute | solution.py:46
  71.3 32.5 %copy-start.16 = (bf16[384,768]{1,0:T(8,128)(2,1)}, bf16[384,768]{1,0:T(8,128)(2,1)S(1)}, u32[]{:S(2)}) copy-start(bf16[384,768]{1,0:T(8,128)(2,1)S(1)} %collective-permute-done.7.refs_1_) | copy-start | bytes 1769476
  71.3 19.2 %collective-permute-start.22 = (bf16[2,384,384]{2,1,0:T(8,128)(2,1)S(1)}, bf16[2,384,384]{2,1,0:T(8,128)(2,1)S(1)}, u32[]{:S(2)}, u32[]{:S(2)}) collective-permute-start(bf16[2,384,384]{2,1,0:T(8,128)(2,1)S(1)} %pad_maximum_fusion.3.refs_9_), channel_id=1, source_target_pairs={{12,8},{13,9},{28,24},{29,25}} | collective-permute-start | bytes 1769480 | tf_op jit(solution)/shard_map/ppermute | solution.py:46
  82.5 20.6 %copy-start.32 = (bf16[2,192,384]{2,1,0:T(8,128)(2,1)}, bf16[2,192,384]{2,1,0:T(8,128)(2,1)S(1)}, u32[]{:S(2)}) copy-start(bf16[2,192,384]{2,1,0:T(8,128)(2,1)S(1)} %collective-permute-done.19.refs_16_) | copy-start | bytes 884740
  82.5 12.5 %collective-permute-start.21 = (bf16[2,384,384]{2,1,0:T(8,128)(2,1)S(1)}, bf16[2,384,384]{2,1,0:T(8,128)(2,1)S(1)}, u32[]{:S(2)}, u32[]{:S(2)}) collective-permute-start(bf16[2,384,384]{2,1,0:T(8,128)(2,1)S(1)} %pad_maximum_fusion.2.refs_8_), channel_id=1, source_target_pairs={{8,14},{9,15},{24,30},{25,31}} | collective-permute-start | bytes 1769480 | tf_op jit(solution)/shard_map/ppermute | solution.py:46
  83.9 20.0 %copy-start.6 = (bf16[384,768]{1,0:T(8,128)(2,1)}, bf16[384,768]{1,0:T(8,128)(2,1)S(1)}, u32[]{:S(2)}) copy-start(bf16[384,768]{1,0:T(8,128)(2,1)S(1)} %pad_maximum_fusion.1.refs_2_) | copy-start | bytes 1769476
  88.4 6.6 %collective-permute-start.8 = (bf16[384,768]{1,0:T(8,128)(2,1)S(1)}, bf16[384,768]{1,0:T(8,128)(2,1)S(1)}, u32[]{:S(2)}, u32[]{:S(2)}) collective-permute-start(bf16[384,768]{1,0:T(8,128)(2,1)S(1)} %pad_maximum_fusion.1.refs_2_), channel_id=1, source_target_pairs={{0,8},{1,9},{2,10},{3,11},{4,12},{5,13},{6,14},{7,15},{8,0},{9,1},... | collective-permute-start | bytes 1769480 | tf_op jit(solution)/shard_map/ppermute | solution.py:46
  88.9 6.6 %collective-permute-start.29 = (bf16[2,192,384]{2,1,0:T(8,128)(2,1)S(1)}, bf16[2,192,384]{2,1,0:T(8,128)(2,1)S(1)}, u32[]{:S(2)}, u32[]{:S(2)}) collective-permute-start(bf16[2,192,384]{2,1,0:T(8,128)(2,1)S(1)} %collective-permute-done.17.refs_14_), channel_id=1, source_target_pairs={{0,8},{1,9},{2,10},{3,11},{4,12},{5,13},{6,14},{7,15},{8,0},{9,1},... | collective-permute-start | bytes 884744 | tf_op jit(solution)/shard_map/ppermute | solution.py:46
  89.1 12.3 %collective-permute-start.20 = (bf16[2,192,384]{2,1,0:T(8,128)(2,1)S(1)}, bf16[2,192,384]{2,1,0:T(8,128)(2,1)S(1)}, u32[]{:S(2)}, u32[]{:S(2)}) collective-permute-start(bf16[2,192,384]{2,1,0:T(8,128)(2,1)S(1)} %broadcast_select_fusion.2), channel_id=1, source_target_pairs={{4,6},{5,7},{8,12},{9,13},{12,14},{13,15},{20,22},{21,23},{24,28},... | collective-permute-start | bytes 884744 | tf_op jit(solution)/shard_map/ppermute | solution.py:46
  90.6 12.5 %collective-permute-start.34 = (bf16[2,384,384]{2,1,0:T(8,128)(2,1)S(1)}, bf16[2,384,384]{2,1,0:T(8,128)(2,1)S(1)}, u32[]{:S(2)}, u32[]{:S(2)}) collective-permute-start(bf16[2,384,384]{2,1,0:T(8,128)(2,1)S(1)} %collective-permute-done.22.refs_19_), channel_id=1, source_target_pairs={{0,8},{1,9},{2,10},{3,11},{4,12},{5,13},{6,14},{7,15},{8,0},{9,1},... | collective-permute-start | bytes 1769480 | tf_op jit(solution)/shard_map/ppermute | solution.py:46
  95.0 8.8 %collective-permute-start.33 = (bf16[2,384,384]{2,1,0:T(8,128)(2,1)S(1)}, bf16[2,384,384]{2,1,0:T(8,128)(2,1)S(1)}, u32[]{:S(2)}, u32[]{:S(2)}) collective-permute-start(bf16[2,384,384]{2,1,0:T(8,128)(2,1)S(1)} %collective-permute-done.21.refs_18_), channel_id=1, source_target_pairs={{0,8},{1,9},{2,10},{3,11},{4,12},{5,13},{6,14},{7,15},{8,0},{9,1},... | collective-permute-start | bytes 1769480 | tf_op jit(solution)/shard_map/ppermute | solution.py:46
  95.0 6.9 %collective-permute-start.31 = (bf16[2,192,384]{2,1,0:T(8,128)(2,1)S(1)}, bf16[2,192,384]{2,1,0:T(8,128)(2,1)S(1)}, u32[]{:S(2)}, u32[]{:S(2)}) collective-permute-start(bf16[2,192,384]{2,1,0:T(8,128)(2,1)S(1)} %collective-permute-done.19.refs_16_), channel_id=1, source_target_pairs={{0,8},{1,9},{2,10},{3,11},{4,12},{5,13},{6,14},{7,15},{8,0},{9,1},... | collective-permute-start | bytes 884744 | tf_op jit(solution)/shard_map/ppermute | solution.py:46
  95.5 6.4 %collective-permute-start.30 = (bf16[2,192,384]{2,1,0:T(8,128)(2,1)S(1)}, bf16[2,192,384]{2,1,0:T(8,128)(2,1)S(1)}, u32[]{:S(2)}, u32[]{:S(2)}) collective-permute-start(bf16[2,192,384]{2,1,0:T(8,128)(2,1)S(1)} %collective-permute-done.18.refs_15_), channel_id=1, source_target_pairs={{0,8},{1,9},{2,10},{3,11},{4,12},{5,13},{6,14},{7,15},{8,0},{9,1},... | collective-permute-start | bytes 884744 | tf_op jit(solution)/shard_map/ppermute | solution.py:46
  101.4 1.7 %collective-permute-start.32 = (bf16[2,192,384]{2,1,0:T(8,128)(2,1)S(1)}, bf16[2,192,384]{2,1,0:T(8,128)(2,1)S(1)}, u32[]{:S(2)}, u32[]{:S(2)}) collective-permute-start(bf16[2,192,384]{2,1,0:T(8,128)(2,1)S(1)} %collective-permute-done.20.refs_17_), channel_id=1, source_target_pairs={{0,8},{1,9},{2,10},{3,11},{4,12},{5,13},{6,14},{7,15},{8,0},{9,1},... | collective-permute-start | bytes 884744 | tf_op jit(solution)/shard_map/ppermute | solution.py:46
  113.6 17.8 %copy-start = (bf16[384,384]{1,0:T(8,128)(2,1)S(1)}, bf16[384,384]{1,0:T(8,128)(2,1)}, u32[]{:S(2)}) copy-start(bf16[384,384]{1,0:T(8,128)(2,1)} %get-tuple-element.84.refs_0_) | copy-start | bytes 884740
  113.6 17.8 %copy-start.1 = (s32[3]{0:T(128)S(1)}, s32[3]{0:T(128)}, u32[]{:S(2)}) copy-start(s32[3]{0:T(128)} %pad_add_fusion.place) | copy-start | bytes 40
  113.6 8.5 %collective-permute-start.35 = (bf16[2,192,384]{2,1,0:T(8,128)(2,1)}, bf16[2,192,384]{2,1,0:T(8,128)(2,1)S(1)}, u32[]{:S(2)}, u32[]{:S(2)}) collective-permute-start(bf16[2,192,384]{2,1,0:T(8,128)(2,1)} %get-tuple-element.83), channel_id=1, source_target_pairs={{0,1},{1,0},{2,3},{3,2},{4,5},{5,4},{6,7},{7,6},{8,9},{9,8},{10,11... | collective-permute-start | bytes 884744 | tf_op jit(solution)/shard_map/ppermute | solution.py:46
  115.0 10.8 %collective-permute-start.36 = (bf16[384,384]{1,0:T(8,128)(2,1)}, bf16[384,384]{1,0:T(8,128)(2,1)S(1)}, u32[]{:S(2)}, u32[]{:S(2)}) collective-permute-start(bf16[384,384]{1,0:T(8,128)(2,1)} %get-tuple-element.80), channel_id=1, source_target_pairs={{0,8},{1,9},{2,10},{3,11},{4,12},{5,13},{6,14},{7,15},{8,0},{9,1},... | collective-permute-start | bytes 884744 | tf_op jit(solution)/shard_map/ppermute | solution.py:46
  115.6 10.2 %collective-permute-start.37 = (bf16[384,384]{1,0:T(8,128)(2,1)}, bf16[384,384]{1,0:T(8,128)(2,1)S(1)}, u32[]{:S(2)}, u32[]{:S(2)}) collective-permute-start(bf16[384,384]{1,0:T(8,128)(2,1)} %get-tuple-element.81), channel_id=1, source_target_pairs={{0,16},{1,17},{2,18},{3,19},{4,20},{5,21},{6,22},{7,23},{8,24},{9,... | collective-permute-start | bytes 884744 | tf_op jit(solution)/shard_map/ppermute | solution.py:46
  117.4 13.9 %collective-permute-start.38 = (bf16[384,384]{1,0:T(8,128)(2,1)}, bf16[384,384]{1,0:T(8,128)(2,1)S(1)}, u32[]{:S(2)}, u32[]{:S(2)}) collective-permute-start(bf16[384,384]{1,0:T(8,128)(2,1)} %get-tuple-element.82), channel_id=1, source_target_pairs={{0,24},{1,25},{2,26},{3,27},{4,28},{5,29},{6,30},{7,31},{8,16},{9,... | collective-permute-start | bytes 884744 | tf_op jit(solution)/shard_map/ppermute | solution.py:46
  (36 other events, 217.7 us)

commit v15 on v14

--- a/solution.py
+++ b/solution.py
@@ -10,7 +10,7 @@
 from jax.sharding import PartitionSpec as P
 
 AXES = ("row", "col", "mom")
-VMEM_BYTES = 60 * 1024 * 1024
+VMEM_BYTES = 32 * 1024 * 1024
 
 
 class Plan:
@@ -224,8 +224,8 @@
     moments, half, width, keys = plan.moments, plan.half, plan.width, plan.keys
     top = moments - 1
     diag, right = refs[:rows], refs[rows : 2 * rows]
-    sig_in, outs = refs[2 * rows : -rows - 4], refs[-rows - 4 : -4]
-    sig, solved, sems, out_sems = refs[-4:]
+    sig_in, outs = refs[2 * rows : -rows - 6], refs[-rows - 6 : -6]
+    sig, solved, diag_at, right_at, sems, out_sems = refs[-6:]
     r, y = place[0], place[2]
     g = r % groups
     for key in sorted(keys, key=lambda key: key[0]):
@@ -235,16 +235,28 @@
             def _(key=key, col=col):
                 for t in range(groups):
                     row = key[0] * groups + (g ^ t)
-                    for k, (q, first, height) in enumerate(plan.chunks):
-                        index, start = sources[key, col, k, t]
-                        at = pl.ds(pl.multiple_of((y ^ q) * half + first, 16), height)
-                        for p in range(2):
-                            lane = pl.ds((2 * key[1] + p) * side, side)
-                            pltpu.make_async_copy(
-                                sig_in[index].at[p, pl.ds(start, height), :],
-                                sig.at[row, at, lane],
-                                sems.at[key[0]],
-                            ).start()
+
+                    def start(row=row, t=t):
+                        for k, (q, first, height) in enumerate(plan.chunks):
+                            index, begin = sources[key, col, k, t]
+                            at = pl.ds(pl.multiple_of((y ^ q) * half + first, 16), height)
+                            for p in range(2):
+                                lane = pl.ds((2 * key[1] + p) * side, side)
+                                pltpu.make_async_copy(
+                                    sig_in[index].at[p, pl.ds(begin, height), :],
+                                    sig.at[row, at, lane],
+                                    sems.at[key[0]],
+                                ).start()
+
+                    if key[0] * groups > key[1]:
+                        start()
+                    else:
+                        pl.when(row > key[1])(start)
+
+    for s in range(rows):
+        right_at[r ^ s] = right[s][...]
+    for n in range(rows):
+        diag_at[n // groups * groups + (g ^ (n % groups))] = diag[n][...]
 
     weight = 1.0 / math.sqrt(side * rows)
 
@@ -255,10 +267,10 @@
         if row == max(1, row // groups * groups):
             for key in keys:
                 if key[0] == row // groups:
-                    for _ in range(groups * 2):
+                    for _ in range(2 * sum(key[0] * groups + t > key[1] for t in range(groups))):
                         tile = sig.at[0, :, pl.ds(0, side)]
                         pltpu.make_async_copy(tile, tile, sems.at[key[0]]).wait()
-        pending = pick(right, r ^ row).astype(jnp.float32)
+        pending = right_at[row].astype(jnp.float32)
         if row > 0:
             depth = 2 * side * row
             pending = pending + weight * jnp.dot(
@@ -266,7 +278,7 @@
             )
         both = jnp.concatenate([pending, turn(pending)], axis=0).astype(jnp.bfloat16)
         value = jnp.dot(
-            pick(diag[row // groups * groups :][:groups], g ^ (row % groups)),
+            diag_at[row],
             both,
             preferred_element_type=jnp.float32,
         )
@@ -486,6 +498,8 @@
             sources[name + (t,)] = (len(sig_all) + number_of(value), part)
         sig_all += [exchange_row(value, t) for value in buffers]
 
+    lanes = -(-2 * width // 128) * 128
+    held = 2 * rows * side * (2 * side * (cols + 1) + 4 * lanes)
     solved = pl.pallas_call(
         functools.partial(solve_kernel, plan, sources),
         out_shape=[jax.ShapeDtypeStruct((side, 2 * width), bf16)] * rows,
@@ -494,10 +508,12 @@
         scratch_shapes=[
             pltpu.VMEM((rows, side, 2 * side * (cols - 1)), bf16),
             pltpu.VMEM((rows * 2 * side, 2 * width), bf16),
+            pltpu.VMEM((rows, side, 2 * side), bf16),
+            pltpu.VMEM((rows, side, 2 * width), bf16),
             dma(moments),
             dma(rows),
         ],
-        compiler_params=params,
+        compiler_params=pltpu.CompilerParams(vmem_limit_bytes=held + 12 * 1024 * 1024),
         name="substitution",
     )(place, *diag_all, *right_all, *sig_all)
 
@@ -518,7 +534,7 @@
         functools.partial(spread_kernel, plan),
         out_shape=jax.ShapeDtypeStruct(right_side.shape, bf16),
         in_specs=[smem()] + [pl.BlockSpec(memory_space=pltpu.VMEM)] * rows,
-        compiler_params=pltpu.CompilerParams(vmem_limit_bytes=VMEM_BYTES // 2),
+        compiler_params=params,
         name="place_solution",
     )
     return sigma, spread(place, *back)

time: 135 us -> 128 us (0.948)
  Pallas kernels: 22.9 us -> 18.2 us
  local copies, waits for them, and re-layouts: 16.3 us -> 14.9 us
    unnamed x90 -> x16, local copies, waits for them, and re-layouts: 5.15 us -> 1.23 us
    pallas_call x1, Pallas kernels: 8.05 us -> 6.23 us  [on_device(): pl.pallas_call(functools.partial(solve_kernel, plan, sources), out_shape=...]
    pallas_call x2, Pallas kernels: 9.22 us -> 7.49 us  [self_energy(): pl.pallas_call(functools.partial(sigma_kernel, plan, pair_count, u, copie...]
    optimization_barrier x2, local copies, waits for them, and re-layouts: 2.75 us -> 4.36 us  [after(): return lax.optimization_barrier((value, others))[0]]
  transfers between devices with their start and end apart: 39 -> 39, of which waited for: 13 -> 13; matrix products, arithmetic and copies ran while one was open for 9% -> 12% of each run, Pallas kernels for 6% -> 4%
where the time goes in v15:
time: 128 us
  waiting for transfers between devices  59 us (46%)
  starting transfers between devices  31.3 us (24%)
  Pallas kernels  18.2 us (14%)
  local copies, waits for them, and re-layouts  14.9 us (12%)
  other arithmetic  3.06 us (2%)
    ppermute x39, waiting for transfers between devices, send(): return lax.ppermute(value, AXES, pairs)  59 us
    ppermute x39, starting transfers between devices, send(): return lax.ppermute(value, AXES, pairs)  31.3 us
    pallas_call x2, Pallas kernels, self_energy(): pl.pallas_call(functools.partial(sigma_kernel, plan, pair_count, u, copie...  7.49 us
    pallas_call x1, Pallas kernels, on_device(): pl.pallas_call(functools.partial(solve_kernel, plan, sources), out_shape=...  6.23 us
    optimization_barrier x2, local copies, waits for them, and re-layouts, after(): return lax.optimization_barrier((value, others))[0]  4.36 us
    dynamic_slice x5, local copies, waits for them, and re-layouts, on_device(): lax.dynamic_index_in_dim(right, r ^ s, 0, keepdims=False)  3.59 us
    dynamic_slice x2, local copies, waits for them, and re-layouts, part_of(): lax.dynamic_slice_in_dim(value, (y ^ q) * half + u * plan.sub, plan.sub, 2)  2.95 us
    pallas_call x1, Pallas kernels, on_device(): return (sigma, spread(place, *back))  2.69 us
  transfers between devices with their start and end apart: 39, of which 13 were waited for; matrix products, arithmetic and copies ran while one was open for 12% of the time, Pallas kernels for 4%

profile of v15, /device:TPU:25, one launch (start us, length us, event | category | flops | bytes accessed | tf_op | source)
XLA Modules:
  0.0 127.6 jit_solution(17800164592166688670)
XLA Ops:
  0.7 2.0 %constant_dynamic-slice_fusion = (bf16[2,2,96,384]{3,2,1,0:T(8,128)(2,1)}, bf16[2,2,96,384]{3,2,1,0:T(8,128)(2,1)}) fusion(bf16[2,2,384,384]{3,2,1,0:T(8,128)(2,1)} %refs_0_.3, s32[]{:T(128)S(6)} %select_n.109, s32[]{:T(128)S(6)} %select_n.101), kind=kLoop, calls=%fused_computation.27 | loop fusion | bytes 1179656 | tf_op jit(solution)/shard_map/dynamic_slice | solution.py:344
  2.7 1.2 collective-permute-start.1
  3.9 0.8 copy.11
  4.7 0.9 dynamic-slice_bitcast_fusion.2
  6.2 0.9 dynamic-slice_bitcast_fusion
  7.1 1.2 collective-permute-start
  8.3 0.7 slice_bitcast_fusion.4.thirds
  9.0 3.6 %copy.12 = bf16[2,384,2,384]{1,3,2,0:T(8,128)(2,1)S(1)} copy(bf16[2,384,2,384]{3,2,1,0:T(2,128)(2,1)} %param.9) | data formatting | bytes 2359296 | tf_op jit(solution)/shard_map/optimization_barrier | solution.py:299
  12.5 1.1 copy.13
  13.7 1.4 %constant_dynamic-slice_fusion.1 = (bf16[1,384,384]{1,2,0:T(8,128)(2,1)S(1)}, bf16[1,384,384]{1,2,0:T(8,128)(2,1)S(1)}, bf16[1,384,384]{1,2,0:T(8,128)(2,1)S(1)}, bf16[1,384,384]{1,2,0:T(8,128)(2,1)S(1)}) fusion(bf16[4,384,384]{1,2,0:T(8,128)(2,1)} %bitcast.41, s32[]{:T(128)S(6)} %select_n.105, s32[]{:T(128)S(6)} %select_n.104, s32[]{:T(128)S(6)} %select_n.103, ...), kind=kLoop, calls=%fused_computation.28 | loop fusion | bytes 2359312 | tf_op jit(solution)/shard_map/jit(dynamic_index_in_dim)/dynamic_slice | solution.py:364
  15.1 1.0 collective-permute-start.2
  16.7 0.9 copy.17
  17.8 0.9 copy.15
  19.0 2.3 %collective-permute-done = bf16[2,384,384]{2,1,0:T(8,128)(2,1)} collective-permute-done((bf16[2,384,384]{2,1,0:T(8,128)(2,1)}, bf16[2,384,384]{2,1,0:T(8,128)(2,1)}, u32[]{:S(2)}, u32[]{:S(2)}) %collective-permute-start) | collective-permute-done | bytes 589856 | tf_op jit(solution)/shard_map/ppermute | solution.py:46
  21.3 2.4 %broadcast_select_fusion = (bf16[2,384,384]{2,1,0:T(8,128)(2,1)}, bf16[2,384,384]{2,1,0:T(8,128)(2,1)}) fusion(bf16[2,384,384]{2,1,0:T(8,128)(2,1)} %collective-permute-done, pred[]{:T(512)S(6)} %select_n.113, bf16[2,2,384,384]{3,2,1,0:T(8,128)(2,1)} %param.8, s32[]{:T(128)S(6)} %select_n.107), kind=kLoop, calls=%fused_computation.6 | loop fusion | flops 294912 | bytes 2359301 | tf_op jit(solution)/shard_map/select_n | solution.py:341
  23.6 3.3 %self_energy.2 = (bf16[2,96,384]{2,1,0:T(8,128)(2,1)S(1)}, bf16[2,96,384]{2,1,0:T(8,128)(2,1)S(1)}, bf16[2,96,384]{2,1,0:T(8,128)(2,1)S(1)}, bf16[2,96,384]{2,1,0:T(8,128)(2,1)S(1)}) custom-call(s32[3]{0:T(128)S(1)} %pad_add_fusion.place, s32[4,8]{1,0:T(4,128)S(1)} %fusion.1.quads, s32[4,8]{1,0:T(4,128)S(1)} %slice_bitcast_fusion.4.thirds, ...), custom_call_target="tpu_custom_call" | custom-call | tf_op jit(solution)/shard_map/self_energy/pallas_call | solution.py:376
  27.0 2.3 %collective-permute-done.3.refs_3_ = bf16[2,2,96,384]{3,2,1,0:T(8,128)(2,1)S(1)} collective-permute-done((bf16[2,2,96,384]{3,2,1,0:T(8,128)(2,1)}, bf16[2,2,96,384]{3,2,1,0:T(8,128)(2,1)S(1)}, u32[]{:S(2)}, u32[]{:S(2)}) %collective-permute-start.3) | collective-permute-done | bytes 294944 | tf_op jit(solution)/shard_map/ppermute | solution.py:46
  29.3 4.2 %self_energy.3 = (bf16[2,192,384]{2,1,0:T(8,128)(2,1)S(1)}, bf16[2,192,384]{2,1,0:T(8,128)(2,1)S(1)}, bf16[2,192,384]{2,1,0:T(8,128)(2,1)S(1)}, bf16[2,192,384]{2,1,0:T(8,128)(2,1)S(1)}) custom-call(s32[3]{0:T(128)S(1)} %pad_add_fusion.place, s32[4,8]{1,0:T(4,128)S(1)} %fusion.1.quads, s32[4,8]{1,0:T(4,128)S(1)} %slice_bitcast_fusion.4.thirds, ...), custom_call_target="tpu_custom_call" | custom-call | tf_op jit(solution)/shard_map/self_energy/pallas_call | solution.py:376
  33.5 0.8 collective-permute-start.12
  34.3 1.3 %collective-permute-start.5 = (bf16[2,192,384]{2,1,0:T(8,128)(2,1)S(1)}, bf16[2,192,384]{2,1,0:T(8,128)(2,1)S(1)}, u32[]{:S(2)}, u32[]{:S(2)}) collective-permute-start(bf16[2,192,384]{2,1,0:T(8,128)(2,1)S(1)} %get-tuple-element.61), channel_id=1, source_target_pairs={{0,1},{1,0},{2,3},{3,2},{4,5},{5,4},{6,7},{7,6},{8,9},{9,8},{10,11... | collective-permute-start | bytes 884744 | tf_op jit(solution)/shard_map/ppermute | solution.py:46
  36.4 1.4 %collective-permute-start.15 = (bf16[2,192,384]{2,1,0:T(8,128)(2,1)S(1)}, bf16[2,192,384]{2,1,0:T(8,128)(2,1)S(1)}, u32[]{:S(2)}, u32[]{:S(2)}) collective-permute-start(bf16[2,192,384]{2,1,0:T(8,128)(2,1)S(1)} %get-tuple-element.98), channel_id=1, source_target_pairs={{0,2},{1,3},{2,4},{3,5},{8,10},{9,11},{10,12},{11,13},{12,14},{13,... | collective-permute-start | bytes 884744 | tf_op jit(solution)/shard_map/ppermute | solution.py:46
  37.8 0.7 collective-permute-start.13
  38.7 2.2 %collective-permute-done.5.refs_2_ = bf16[2,192,384]{2,1,0:T(8,128)(2,1)S(1)} collective-permute-done((bf16[2,192,384]{2,1,0:T(8,128)(2,1)S(1)}, bf16[2,192,384]{2,1,0:T(8,128)(2,1)S(1)}, u32[]{:S(2)}, u32[]{:S(2)}) %collective-permute-start.5) | collective-permute-done | bytes 294944 | tf_op jit(solution)/shard_map/ppermute | solution.py:46
  40.9 1.3 %collective-permute-start.16 = (bf16[2,192,384]{2,1,0:T(8,128)(2,1)S(1)}, bf16[2,192,384]{2,1,0:T(8,128)(2,1)S(1)}, u32[]{:S(2)}, u32[]{:S(2)}) collective-permute-start(bf16[2,192,384]{2,1,0:T(8,128)(2,1)S(1)} %get-tuple-element.100), channel_id=1, source_target_pairs={{0,2},{1,3},{2,4},{3,5},{8,10},{9,11},{10,12},{11,13},{12,14},{13,... | collective-permute-start | bytes 884744 | tf_op jit(solution)/shard_map/ppermute | solution.py:46
  42.2 0.7 collective-permute-start.14
  42.9 2.4 %collective-permute-start.9 = (bf16[384,384]{1,0:T(8,128)(2,1)S(1)}, bf16[384,384]{1,0:T(8,128)(2,1)S(1)}, u32[]{:S(2)}, u32[]{:S(2)}) collective-permute-start(bf16[384,384]{1,0:T(8,128)(2,1)S(1)} %bitcast.44), channel_id=1, source_target_pairs={{0,8},{1,9},{2,10},{3,11},{4,12},{5,13},{6,14},{7,15},{8,0},{9,1},... | collective-permute-start | bytes 884744 | tf_op jit(solution)/shard_map/ppermute | solution.py:46
  45.3 2.4 %collective-permute-done.15.refs_12_ = bf16[2,192,384]{2,1,0:T(8,128)(2,1)S(1)} collective-permute-done((bf16[2,192,384]{2,1,0:T(8,128)(2,1)S(1)}, bf16[2,192,384]{2,1,0:T(8,128)(2,1)S(1)}, u32[]{:S(2)}, u32[]{:S(2)}) %collective-permute-start.15) | collective-permute-done | bytes 294944 | tf_op jit(solution)/shard_map/ppermute | solution.py:46
  47.8 1.3 %collective-permute-start.17 = (bf16[2,192,384]{2,1,0:T(8,128)(2,1)S(1)}, bf16[2,192,384]{2,1,0:T(8,128)(2,1)S(1)}, u32[]{:S(2)}, u32[]{:S(2)}) collective-permute-start(bf16[2,192,384]{2,1,0:T(8,128)(2,1)S(1)} %broadcast_select_fusion.5), channel_id=1, source_target_pairs={{2,4},{3,5},{4,6},{5,7},{8,10},{9,11},{10,12},{11,13},{12,14},{13,... | collective-permute-start | bytes 884744 | tf_op jit(solution)/shard_map/ppermute | solution.py:46
  49.3 0.9 copy-done.5
  50.2 10.3 %collective-permute-done.17.refs_14_ = bf16[2,192,384]{2,1,0:T(8,128)(2,1)S(1)} collective-permute-done((bf16[2,192,384]{2,1,0:T(8,128)(2,1)S(1)}, bf16[2,192,384]{2,1,0:T(8,128)(2,1)S(1)}, u32[]{:S(2)}, u32[]{:S(2)}) %collective-permute-start.17) | collective-permute-done | bytes 294944 | tf_op jit(solution)/shard_map/ppermute | solution.py:46
  60.5 3.2 %collective-permute-start.27 = (bf16[2,192,384]{2,1,0:T(8,128)(2,1)S(1)}, bf16[2,192,384]{2,1,0:T(8,128)(2,1)S(1)}, u32[]{:S(2)}, u32[]{:S(2)}) collective-permute-start(bf16[2,192,384]{2,1,0:T(8,128)(2,1)S(1)} %collective-permute-done.15.refs_12_), channel_id=1, source_target_pairs={{0,8},{1,9},{2,10},{3,11},{4,12},{5,13},{6,14},{7,15},{8,0},{9,1},... | collective-permute-start | bytes 884744 | tf_op jit(solution)/shard_map/ppermute | solution.py:46
  65.0 1.3 %collective-permute-start.19 = (bf16[2,192,384]{2,1,0:T(8,128)(2,1)S(1)}, bf16[2,192,384]{2,1,0:T(8,128)(2,1)S(1)}, u32[]{:S(2)}, u32[]{:S(2)}) collective-permute-start(bf16[2,192,384]{2,1,0:T(8,128)(2,1)S(1)} %broadcast_select_fusion.3), channel_id=1, source_target_pairs={{4,6},{5,7},{8,12},{9,13},{12,14},{13,15},{20,22},{21,23},{24,28},... | collective-permute-start | bytes 884744 | tf_op jit(solution)/shard_map/ppermute | solution.py:46
  66.8 1.3 %collective-permute-start.18 = (bf16[2,192,384]{2,1,0:T(8,128)(2,1)S(1)}, bf16[2,192,384]{2,1,0:T(8,128)(2,1)S(1)}, u32[]{:S(2)}, u32[]{:S(2)}) collective-permute-start(bf16[2,192,384]{2,1,0:T(8,128)(2,1)S(1)} %broadcast_select_fusion.4), channel_id=1, source_target_pairs={{2,4},{3,5},{4,6},{5,7},{8,10},{9,11},{10,12},{11,13},{12,14},{13,... | collective-permute-start | bytes 884744 | tf_op jit(solution)/shard_map/ppermute | solution.py:46
  68.3 0.7 collective-permute-start.22
  69.0 11.9 %collective-permute-done.19.refs_16_ = bf16[2,192,384]{2,1,0:T(8,128)(2,1)S(1)} collective-permute-done((bf16[2,192,384]{2,1,0:T(8,128)(2,1)S(1)}, bf16[2,192,384]{2,1,0:T(8,128)(2,1)S(1)}, u32[]{:S(2)}, u32[]{:S(2)}) %collective-permute-start.19) | collective-permute-done | bytes 294944 | tf_op jit(solution)/shard_map/ppermute | solution.py:46
  81.0 1.3 %collective-permute-start.21 = (bf16[2,384,384]{2,1,0:T(8,128)(2,1)S(1)}, bf16[2,384,384]{2,1,0:T(8,128)(2,1)S(1)}, u32[]{:S(2)}, u32[]{:S(2)}) collective-permute-start(bf16[2,384,384]{2,1,0:T(8,128)(2,1)S(1)} %pad_maximum_fusion.2.refs_8_), channel_id=1, source_target_pairs={{8,14},{9,15},{24,30},{25,31}} | collective-permute-start | bytes 1769480 | tf_op jit(solution)/shard_map/ppermute | solution.py:46
  82.3 4.7 %collective-permute-done.18.refs_15_ = bf16[2,192,384]{2,1,0:T(8,128)(2,1)S(1)} collective-permute-done((bf16[2,192,384]{2,1,0:T(8,128)(2,1)S(1)}, bf16[2,192,384]{2,1,0:T(8,128)(2,1)S(1)}, u32[]{:S(2)}, u32[]{:S(2)}) %collective-permute-start.18) | collective-permute-done | bytes 294944 | tf_op jit(solution)/shard_map/ppermute | solution.py:46
  87.7 1.3 %collective-permute-start.20 = (bf16[2,192,384]{2,1,0:T(8,128)(2,1)S(1)}, bf16[2,192,384]{2,1,0:T(8,128)(2,1)S(1)}, u32[]{:S(2)}, u32[]{:S(2)}) collective-permute-start(bf16[2,192,384]{2,1,0:T(8,128)(2,1)S(1)} %broadcast_select_fusion.2), channel_id=1, source_target_pairs={{4,6},{5,7},{8,12},{9,13},{12,14},{13,15},{20,22},{21,23},{24,28},... | collective-permute-start | bytes 884744 | tf_op jit(solution)/shard_map/ppermute | solution.py:46
  89.4 4.1 %collective-permute-done.21.refs_18_ = bf16[2,384,384]{2,1,0:T(8,128)(2,1)S(1)} collective-permute-done((bf16[2,384,384]{2,1,0:T(8,128)(2,1)S(1)}, bf16[2,384,384]{2,1,0:T(8,128)(2,1)S(1)}, u32[]{:S(2)}, u32[]{:S(2)}) %collective-permute-start.21) | collective-permute-done | bytes 589856 | tf_op jit(solution)/shard_map/ppermute | solution.py:46
  94.1 5.8 %collective-permute-done.20.refs_17_ = bf16[2,192,384]{2,1,0:T(8,128)(2,1)S(1)} collective-permute-done((bf16[2,192,384]{2,1,0:T(8,128)(2,1)S(1)}, bf16[2,192,384]{2,1,0:T(8,128)(2,1)S(1)}, u32[]{:S(2)}, u32[]{:S(2)}) %collective-permute-start.20) | collective-permute-done | bytes 294944 | tf_op jit(solution)/shard_map/ppermute | solution.py:46
  100.4 1.2 collective-permute-done.32.refs_29_
  101.6 6.2 %substitution.1 = (bf16[384,384]{1,0:T(8,128)(2,1)S(1)}, bf16[384,384]{1,0:T(8,128)(2,1)S(1)}, bf16[384,384]{1,0:T(8,128)(2,1)S(1)}, bf16[384,384]{1,0:T(8,128)(2,1)S(1)}) custom-call(s32[3]{0:T(128)S(1)} %pad_add_fusion.place, bf16[384,768]{1,0:T(8,128)(2,1)S(1)} %pad_maximum_fusion.refs_0_, bf16[384,768]{1,0:T(8,128)(2,1)S(1)} %collective-permute-done.7.refs_1_, ...), custom_call_target="tpu_custom_call" | custom-call | tf_op jit(solution)/shard_map/substitution/pallas_call | solution.py:503
  107.9 1.3 %collective-permute-start.35 = (bf16[2,192,384]{2,1,0:T(8,128)(2,1)S(1)}, bf16[2,192,384]{2,1,0:T(8,128)(2,1)S(1)}, u32[]{:S(2)}, u32[]{:S(2)}) collective-permute-start(bf16[2,192,384]{2,1,0:T(8,128)(2,1)S(1)} %get-tuple-element.83), channel_id=1, source_target_pairs={{0,1},{1,0},{2,3},{3,2},{4,5},{5,4},{6,7},{7,6},{8,9},{9,8},{10,11... | collective-permute-start | bytes 884744 | tf_op jit(solution)/shard_map/ppermute | solution.py:46
  109.8 1.1 collective-permute-start.37
  111.4 4.7 %collective-permute-done.35.refs_3_ = bf16[2,192,384]{2,1,0:T(8,128)(2,1)S(1)} collective-permute-done((bf16[2,192,384]{2,1,0:T(8,128)(2,1)S(1)}, bf16[2,192,384]{2,1,0:T(8,128)(2,1)S(1)}, u32[]{:S(2)}, u32[]{:S(2)}) %collective-permute-start.35) | collective-permute-done | bytes 294944 | tf_op jit(solution)/shard_map/ppermute | solution.py:46
  116.1 1.8 %place_sigma.1 = bf16[2,2,384,384]{3,2,1,0:T(8,128)(2,1)} custom-call(s32[3]{0:T(128)S(1)} %pad_add_fusion.place, bf16[2,192,384]{2,1,0:T(8,128)(2,1)S(1)} %get-tuple-element.59.refs_0_, bf16[2,192,384]{2,1,0:T(8,128)(2,1)S(1)} %get-tuple-element.60.refs_1_, bf16[2,192,384]{2,1,0:T(8,128)(2,1)S(1)} %collective-permute-done.5.refs_2_, ...), custom_call_target="tpu_custom_call" | custom-call | tf_op jit(solution)/shard_map/place_sigma/pallas_call | solution.py:522
  118.5 6.4 %collective-permute-done.38.refs_3_ = bf16[384,384]{1,0:T(8,128)(2,1)S(1)} collective-permute-done((bf16[384,384]{1,0:T(8,128)(2,1)S(1)}, bf16[384,384]{1,0:T(8,128)(2,1)S(1)}, u32[]{:S(2)}, u32[]{:S(2)}) %collective-permute-start.38) | collective-permute-done | bytes 294944 | tf_op jit(solution)/shard_map/ppermute | solution.py:46
  124.9 2.7 %place_solution.1 = bf16[2,384,2,384]{3,2,1,0:T(2,128)(2,1)} custom-call(s32[3]{0:T(128)S(1)} %pad_add_fusion.place, bf16[384,384]{1,0:T(8,128)(2,1)S(1)} %get-tuple-element.84.refs_0_, bf16[384,384]{1,0:T(8,128)(2,1)S(1)} %collective-permute-done.36.refs_1_, bf16[384,384]{1,0:T(8,128)(2,1)S(1)} %collective-permute-done.37.refs_2_, ...), custom_call_target="tpu_custom_call" | custom-call | tf_op jit(solution)/shard_map/place_solution/pallas_call | solution.py:540
  (78 shorter events, 8.7 us)
Async XLA Ops:
  0.6 3.3 %copy-start.3 = (bf16[2,2,384,384]{3,2,1,0:T(8,128)(2,1)S(1)}, bf16[2,2,384,384]{3,2,1,0:T(8,128)(2,1)}, u32[]{:S(2)}) copy-start(bf16[2,2,384,384]{3,2,1,0:T(8,128)(2,1)} %param.6) | copy-start | bytes 3538948
  2.7 12.4 %collective-permute-start.1 = (bf16[2,2,96,384]{3,2,1,0:T(8,128)(2,1)}, bf16[2,2,96,384]{3,2,1,0:T(8,128)(2,1)S(1)}, u32[]{:S(2)}, u32[]{:S(2)}) collective-permute-start(bf16[2,2,96,384]{3,2,1,0:T(8,128)(2,1)} %get-tuple-element.93), channel_id=1, source_target_pairs={{0,1},{1,0},{2,3},{3,2},{4,5},{5,4},{6,7},{7,6},{8,9},{9,8},{10,11... | collective-permute-start | bytes 884744 | tf_op jit(solution)/shard_map/ppermute | solution.py:46
  4.7 1.5 %copy-start.4 = (bf16[2,2,384,384]{3,2,1,0:T(8,128)(2,1)S(1)}, bf16[2,2,384,384]{3,2,1,0:T(8,128)(2,1)}, u32[]{:S(2)}) copy-start(bf16[2,2,384,384]{3,2,1,0:T(8,128)(2,1)} %param.8) | copy-start | bytes 3538948
  5.6 18.0 %collective-permute-start.4 = (bf16[2,2,96,384]{3,2,1,0:T(8,128)(2,1)}, bf16[2,2,96,384]{3,2,1,0:T(8,128)(2,1)S(1)}, u32[]{:S(2)}, u32[]{:S(2)}) collective-permute-start(bf16[2,2,96,384]{3,2,1,0:T(8,128)(2,1)} %get-tuple-element.91), channel_id=1, source_target_pairs={{0,1},{1,0},{2,3},{3,2},{4,5},{5,4},{6,7},{7,6},{8,9},{9,8},{10,11... | collective-permute-start | bytes 884744 | tf_op jit(solution)/shard_map/ppermute | solution.py:46
  7.1 14.2 %collective-permute-start = (bf16[2,384,384]{2,1,0:T(8,128)(2,1)}, bf16[2,384,384]{2,1,0:T(8,128)(2,1)}, u32[]{:S(2)}, u32[]{:S(2)}) collective-permute-start(bf16[2,384,384]{2,1,0:T(8,128)(2,1)} %dynamic-slice_bitcast_fusion), channel_id=1, source_target_pairs={{0,16},{1,17},{2,18},{3,19},{4,20},{5,21},{6,22},{7,23},{8,24},{9,... | collective-permute-start | bytes 1769480 | tf_op jit(solution)/shard_map/ppermute | solution.py:46
  13.7 1.4 %copy-start.7 = (s32[4,8,3]{1,0,2:T(4,128)S(1)}, s32[4,8,3]{1,0,2:T(4,128)}, u32[]{:S(2)}) copy-start(s32[4,8,3]{1,0,2:T(4,128)} %param.7) | copy-start | bytes 1156
  15.1 11.9 %collective-permute-start.2 = (bf16[2,2,96,384]{3,2,1,0:T(8,128)(2,1)}, bf16[2,2,96,384]{3,2,1,0:T(8,128)(2,1)S(1)}, u32[]{:S(2)}, u32[]{:S(2)}) collective-permute-start(bf16[2,2,96,384]{3,2,1,0:T(8,128)(2,1)} %get-tuple-element.53), channel_id=1, source_target_pairs={{0,1},{1,0},{2,3},{3,2},{4,5},{5,4},{6,7},{7,6},{8,9},{9,8},{10,11... | collective-permute-start | bytes 884744 | tf_op jit(solution)/shard_map/ppermute | solution.py:46
  16.1 13.2 %collective-permute-start.3 = (bf16[2,2,96,384]{3,2,1,0:T(8,128)(2,1)}, bf16[2,2,96,384]{3,2,1,0:T(8,128)(2,1)S(1)}, u32[]{:S(2)}, u32[]{:S(2)}) collective-permute-start(bf16[2,2,96,384]{3,2,1,0:T(8,128)(2,1)} %get-tuple-element.54), channel_id=1, source_target_pairs={{0,1},{1,0},{2,3},{3,2},{4,5},{5,4},{6,7},{7,6},{8,9},{9,8},{10,11... | collective-permute-start | bytes 884744 | tf_op jit(solution)/shard_map/ppermute | solution.py:46
  18.9 4.7 %copy-start = (bf16[2,2,384,384]{3,2,1,0:T(8,128)(2,1)S(1)}, bf16[2,2,384,384]{3,2,1,0:T(8,128)(2,1)}, u32[]{:S(2)}) copy-start(bf16[2,2,384,384]{3,2,1,0:T(8,128)(2,1)} %refs_0_.3) | copy-start | bytes 3538948
  33.5 5.1 %copy-start.2 = (bf16[2,384,384]{2,1,0:T(8,128)(2,1)S(1)}, bf16[2,384,384]{2,1,0:T(8,128)(2,1)}, u32[]{:S(2)}) copy-start(bf16[2,384,384]{2,1,0:T(8,128)(2,1)} %get-tuple-element.89) | copy-start | bytes 1769476
  33.5 2.9 %collective-permute-start.12 = (bf16[2,192,384]{2,1,0:T(8,128)(2,1)S(1)}, bf16[2,192,384]{2,1,0:T(8,128)(2,1)S(1)}, u32[]{:S(2)}, u32[]{:S(2)}) collective-permute-start(bf16[2,192,384]{2,1,0:T(8,128)(2,1)S(1)} %get-tuple-element.60.refs_1_), channel_id=1, source_target_pairs={{8,24},{9,25},{16,0},{17,1},{18,2},{19,3},{24,8},{25,9},{26,10},{2... | collective-permute-start | bytes 884744 | tf_op jit(solution)/shard_map/ppermute | solution.py:46
  34.3 6.6 %collective-permute-start.5 = (bf16[2,192,384]{2,1,0:T(8,128)(2,1)S(1)}, bf16[2,192,384]{2,1,0:T(8,128)(2,1)S(1)}, u32[]{:S(2)}, u32[]{:S(2)}) collective-permute-start(bf16[2,192,384]{2,1,0:T(8,128)(2,1)S(1)} %get-tuple-element.61), channel_id=1, source_target_pairs={{0,1},{1,0},{2,3},{3,2},{4,5},{5,4},{6,7},{7,6},{8,9},{9,8},{10,11... | collective-permute-start | bytes 884744 | tf_op jit(solution)/shard_map/ppermute | solution.py:46
  35.6 5.2 %collective-permute-start.6 = (bf16[2,192,384]{2,1,0:T(8,128)(2,1)S(1)}, bf16[2,192,384]{2,1,0:T(8,128)(2,1)S(1)}, u32[]{:S(2)}, u32[]{:S(2)}) collective-permute-start(bf16[2,192,384]{2,1,0:T(8,128)(2,1)S(1)} %get-tuple-element.83), channel_id=1, source_target_pairs={{8,25},{9,24},{16,1},{17,0},{18,3},{19,2},{24,9},{25,8},{26,11},{2... | collective-permute-start | bytes 884744 | tf_op jit(solution)/shard_map/ppermute | solution.py:46
  36.4 6.5 %copy-start.6 = (bf16[1,384,384]{2,1,0:T(8,128)(2,1)S(1)}, bf16[1,384,384]{2,1,0:T(8,128)(2,1)}, u32[]{:S(2)}) copy-start(bf16[1,384,384]{2,1,0:T(8,128)(2,1)} %copy.15) | copy-start | bytes 884740
  36.4 11.3 %collective-permute-start.15 = (bf16[2,192,384]{2,1,0:T(8,128)(2,1)S(1)}, bf16[2,192,384]{2,1,0:T(8,128)(2,1)S(1)}, u32[]{:S(2)}, u32[]{:S(2)}) collective-permute-start(bf16[2,192,384]{2,1,0:T(8,128)(2,1)S(1)} %get-tuple-element.98), channel_id=1, source_target_pairs={{0,2},{1,3},{2,4},{3,5},{8,10},{9,11},{10,12},{11,13},{12,14},{13,... | collective-permute-start | bytes 884744 | tf_op jit(solution)/shard_map/ppermute | solution.py:46
  37.8 9.9 %collective-permute-start.13 = (bf16[2,192,384]{2,1,0:T(8,128)(2,1)S(1)}, bf16[2,192,384]{2,1,0:T(8,128)(2,1)S(1)}, u32[]{:S(2)}, u32[]{:S(2)}) collective-permute-start(bf16[2,192,384]{2,1,0:T(8,128)(2,1)S(1)} %get-tuple-element.98), channel_id=1, source_target_pairs={{2,0},{3,1},{10,8},{11,9},{12,10},{13,11},{18,16},{19,17},{26,24},... | collective-permute-start | bytes 884744 | tf_op jit(solution)/shard_map/ppermute | solution.py:46
  38.7 10.4 %copy-start.1 = (bf16[2,384,384]{2,1,0:T(8,128)(2,1)S(1)}, bf16[2,384,384]{2,1,0:T(8,128)(2,1)}, u32[]{:S(2)}) copy-start(bf16[2,384,384]{2,1,0:T(8,128)(2,1)} %get-tuple-element.64) | copy-start | bytes 1769476
  40.9 23.5 %collective-permute-start.16 = (bf16[2,192,384]{2,1,0:T(8,128)(2,1)S(1)}, bf16[2,192,384]{2,1,0:T(8,128)(2,1)S(1)}, u32[]{:S(2)}, u32[]{:S(2)}) collective-permute-start(bf16[2,192,384]{2,1,0:T(8,128)(2,1)S(1)} %get-tuple-element.100), channel_id=1, source_target_pairs={{0,2},{1,3},{2,4},{3,5},{8,10},{9,11},{10,12},{11,13},{12,14},{13,... | collective-permute-start | bytes 884744 | tf_op jit(solution)/shard_map/ppermute | solution.py:46
  42.2 22.3 %collective-permute-start.14 = (bf16[2,192,384]{2,1,0:T(8,128)(2,1)S(1)}, bf16[2,192,384]{2,1,0:T(8,128)(2,1)S(1)}, u32[]{:S(2)}, u32[]{:S(2)}) collective-permute-start(bf16[2,192,384]{2,1,0:T(8,128)(2,1)S(1)} %get-tuple-element.100), channel_id=1, source_target_pairs={{2,0},{3,1},{10,8},{11,9},{12,10},{13,11},{18,16},{19,17},{26,24},... | collective-permute-start | bytes 884744 | tf_op jit(solution)/shard_map/ppermute | solution.py:46
  42.9 6.4 %collective-permute-start.9 = (bf16[384,384]{1,0:T(8,128)(2,1)S(1)}, bf16[384,384]{1,0:T(8,128)(2,1)S(1)}, u32[]{:S(2)}, u32[]{:S(2)}) collective-permute-start(bf16[384,384]{1,0:T(8,128)(2,1)S(1)} %bitcast.44), channel_id=1, source_target_pairs={{0,8},{1,9},{2,10},{3,11},{4,12},{5,13},{6,14},{7,15},{8,0},{9,1},... | collective-permute-start | bytes 884744 | tf_op jit(solution)/shard_map/ppermute | solution.py:46
  47.7 16.0 %collective-permute-start.10 = (bf16[384,384]{1,0:T(8,128)(2,1)S(1)}, bf16[384,384]{1,0:T(8,128)(2,1)S(1)}, u32[]{:S(2)}, u32[]{:S(2)}) collective-permute-start(bf16[384,384]{1,0:T(8,128)(2,1)S(1)} %bitcast.43), channel_id=1, source_target_pairs={{0,16},{1,17},{2,18},{3,19},{4,20},{5,21},{6,22},{7,23},{8,24},{9,... | collective-permute-start | bytes 884744 | tf_op jit(solution)/shard_map/ppermute | solution.py:46
  47.8 12.7 %collective-permute-start.17 = (bf16[2,192,384]{2,1,0:T(8,128)(2,1)S(1)}, bf16[2,192,384]{2,1,0:T(8,128)(2,1)S(1)}, u32[]{:S(2)}, u32[]{:S(2)}) collective-permute-start(bf16[2,192,384]{2,1,0:T(8,128)(2,1)S(1)} %broadcast_select_fusion.5), channel_id=1, source_target_pairs={{2,4},{3,5},{4,6},{5,7},{8,10},{9,11},{10,12},{11,13},{12,14},{13,... | collective-permute-start | bytes 884744 | tf_op jit(solution)/shard_map/ppermute | solution.py:46
  49.2 1.0 copy-start.5
  50.2 13.7 %collective-permute-start.11 = (bf16[384,384]{1,0:T(8,128)(2,1)S(1)}, bf16[384,384]{1,0:T(8,128)(2,1)S(1)}, u32[]{:S(2)}, u32[]{:S(2)}) collective-permute-start(bf16[384,384]{1,0:T(8,128)(2,1)S(1)} %bitcast.42), channel_id=1, source_target_pairs={{0,24},{1,25},{2,26},{3,27},{4,28},{5,29},{6,30},{7,31},{8,16},{9,... | collective-permute-start | bytes 884744 | tf_op jit(solution)/shard_map/ppermute | solution.py:46
  60.5 4.5 %collective-permute-start.27 = (bf16[2,192,384]{2,1,0:T(8,128)(2,1)S(1)}, bf16[2,192,384]{2,1,0:T(8,128)(2,1)S(1)}, u32[]{:S(2)}, u32[]{:S(2)}) collective-permute-start(bf16[2,192,384]{2,1,0:T(8,128)(2,1)S(1)} %collective-permute-done.15.refs_12_), channel_id=1, source_target_pairs={{0,8},{1,9},{2,10},{3,11},{4,12},{5,13},{6,14},{7,15},{8,0},{9,1},... | collective-permute-start | bytes 884744 | tf_op jit(solution)/shard_map/ppermute | solution.py:46
  63.8 4.6 %collective-permute-start.7 = (bf16[384,768]{1,0:T(8,128)(2,1)S(1)}, bf16[384,768]{1,0:T(8,128)(2,1)S(1)}, u32[]{:S(2)}, u32[]{:S(2)}) collective-permute-start(bf16[384,768]{1,0:T(8,128)(2,1)S(1)} %pad_maximum_fusion.refs_0_), channel_id=1, source_target_pairs={{0,8},{1,9},{2,10},{3,11},{4,12},{5,13},{6,14},{7,15},{8,0},{9,1},... | collective-permute-start | bytes 1769480 | tf_op jit(solution)/shard_map/ppermute | solution.py:46
  63.9 2.5 %collective-permute-start.25 = (bf16[2,192,384]{2,1,0:T(8,128)(2,1)S(1)}, bf16[2,192,384]{2,1,0:T(8,128)(2,1)S(1)}, u32[]{:S(2)}, u32[]{:S(2)}) collective-permute-start(bf16[2,192,384]{2,1,0:T(8,128)(2,1)S(1)} %collective-permute-done.13.refs_10_), channel_id=1, source_target_pairs={{0,8},{1,9},{2,10},{3,11},{4,12},{5,13},{6,14},{7,15},{8,0},{9,1},... | collective-permute-start | bytes 884744 | tf_op jit(solution)/shard_map/ppermute | solution.py:46
  64.5 2.3 %collective-permute-start.28 = (bf16[2,192,384]{2,1,0:T(8,128)(2,1)S(1)}, bf16[2,192,384]{2,1,0:T(8,128)(2,1)S(1)}, u32[]{:S(2)}, u32[]{:S(2)}) collective-permute-start(bf16[2,192,384]{2,1,0:T(8,128)(2,1)S(1)} %collective-permute-done.16.refs_13_), channel_id=1, source_target_pairs={{0,8},{1,9},{2,10},{3,11},{4,12},{5,13},{6,14},{7,15},{8,0},{9,1},... | collective-permute-start | bytes 884744 | tf_op jit(solution)/shard_map/ppermute | solution.py:46
  64.6 3.5 %collective-permute-start.26 = (bf16[2,192,384]{2,1,0:T(8,128)(2,1)S(1)}, bf16[2,192,384]{2,1,0:T(8,128)(2,1)S(1)}, u32[]{:S(2)}, u32[]{:S(2)}) collective-permute-start(bf16[2,192,384]{2,1,0:T(8,128)(2,1)S(1)} %collective-permute-done.14.refs_11_), channel_id=1, source_target_pairs={{0,8},{1,9},{2,10},{3,11},{4,12},{5,13},{6,14},{7,15},{8,0},{9,1},... | collective-permute-start | bytes 884744 | tf_op jit(solution)/shard_map/ppermute | solution.py:46
  65.0 16.0 %collective-permute-start.19 = (bf16[2,192,384]{2,1,0:T(8,128)(2,1)S(1)}, bf16[2,192,384]{2,1,0:T(8,128)(2,1)S(1)}, u32[]{:S(2)}, u32[]{:S(2)}) collective-permute-start(bf16[2,192,384]{2,1,0:T(8,128)(2,1)S(1)} %broadcast_select_fusion.3), channel_id=1, source_target_pairs={{4,6},{5,7},{8,12},{9,13},{12,14},{13,15},{20,22},{21,23},{24,28},... | collective-permute-start | bytes 884744 | tf_op jit(solution)/shard_map/ppermute | solution.py:46
  66.4 21.1 %collective-permute-start.23 = (bf16[2,384,384]{2,1,0:T(8,128)(2,1)S(1)}, bf16[2,384,384]{2,1,0:T(8,128)(2,1)S(1)}, u32[]{:S(2)}, u32[]{:S(2)}) collective-permute-start(bf16[2,384,384]{2,1,0:T(8,128)(2,1)S(1)} %pad_maximum_fusion.2.refs_8_), channel_id=1, source_target_pairs={{0,8},{1,9},{2,10},{3,11},{4,12},{5,13},{6,14},{7,15},{8,0},{9,1},... | collective-permute-start | bytes 1769480 | tf_op jit(solution)/shard_map/ppermute | solution.py:46
  66.8 20.3 %collective-permute-start.18 = (bf16[2,192,384]{2,1,0:T(8,128)(2,1)S(1)}, bf16[2,192,384]{2,1,0:T(8,128)(2,1)S(1)}, u32[]{:S(2)}, u32[]{:S(2)}) collective-permute-start(bf16[2,192,384]{2,1,0:T(8,128)(2,1)S(1)} %broadcast_select_fusion.4), channel_id=1, source_target_pairs={{2,4},{3,5},{4,6},{5,7},{8,10},{9,11},{10,12},{11,13},{12,14},{13,... | collective-permute-start | bytes 884744 | tf_op jit(solution)/shard_map/ppermute | solution.py:46
  68.1 19.6 %collective-permute-start.24 = (bf16[2,384,384]{2,1,0:T(8,128)(2,1)S(1)}, bf16[2,384,384]{2,1,0:T(8,128)(2,1)S(1)}, u32[]{:S(2)}, u32[]{:S(2)}) collective-permute-start(bf16[2,384,384]{2,1,0:T(8,128)(2,1)S(1)} %pad_maximum_fusion.3.refs_9_), channel_id=1, source_target_pairs={{0,8},{1,9},{2,10},{3,11},{4,12},{5,13},{6,14},{7,15},{8,0},{9,1},... | collective-permute-start | bytes 1769480 | tf_op jit(solution)/shard_map/ppermute | solution.py:46
  68.3 20.6 %collective-permute-start.22 = (bf16[2,384,384]{2,1,0:T(8,128)(2,1)S(1)}, bf16[2,384,384]{2,1,0:T(8,128)(2,1)S(1)}, u32[]{:S(2)}, u32[]{:S(2)}) collective-permute-start(bf16[2,384,384]{2,1,0:T(8,128)(2,1)S(1)} %pad_maximum_fusion.3.refs_9_), channel_id=1, source_target_pairs={{12,8},{13,9},{28,24},{29,25}} | collective-permute-start | bytes 1769480 | tf_op jit(solution)/shard_map/ppermute | solution.py:46
  81.0 12.5 %collective-permute-start.21 = (bf16[2,384,384]{2,1,0:T(8,128)(2,1)S(1)}, bf16[2,384,384]{2,1,0:T(8,128)(2,1)S(1)}, u32[]{:S(2)}, u32[]{:S(2)}) collective-permute-start(bf16[2,384,384]{2,1,0:T(8,128)(2,1)S(1)} %pad_maximum_fusion.2.refs_8_), channel_id=1, source_target_pairs={{8,14},{9,15},{24,30},{25,31}} | collective-permute-start | bytes 1769480 | tf_op jit(solution)/shard_map/ppermute | solution.py:46
  87.0 6.5 %collective-permute-start.8 = (bf16[384,768]{1,0:T(8,128)(2,1)S(1)}, bf16[384,768]{1,0:T(8,128)(2,1)S(1)}, u32[]{:S(2)}, u32[]{:S(2)}) collective-permute-start(bf16[384,768]{1,0:T(8,128)(2,1)S(1)} %pad_maximum_fusion.1.refs_2_), channel_id=1, source_target_pairs={{0,8},{1,9},{2,10},{3,11},{4,12},{5,13},{6,14},{7,15},{8,0},{9,1},... | collective-permute-start | bytes 1769480 | tf_op jit(solution)/shard_map/ppermute | solution.py:46
  87.5 6.5 %collective-permute-start.29 = (bf16[2,192,384]{2,1,0:T(8,128)(2,1)S(1)}, bf16[2,192,384]{2,1,0:T(8,128)(2,1)S(1)}, u32[]{:S(2)}, u32[]{:S(2)}) collective-permute-start(bf16[2,192,384]{2,1,0:T(8,128)(2,1)S(1)} %collective-permute-done.17.refs_14_), channel_id=1, source_target_pairs={{0,8},{1,9},{2,10},{3,11},{4,12},{5,13},{6,14},{7,15},{8,0},{9,1},... | collective-permute-start | bytes 884744 | tf_op jit(solution)/shard_map/ppermute | solution.py:46
  87.7 12.3 %collective-permute-start.20 = (bf16[2,192,384]{2,1,0:T(8,128)(2,1)S(1)}, bf16[2,192,384]{2,1,0:T(8,128)(2,1)S(1)}, u32[]{:S(2)}, u32[]{:S(2)}) collective-permute-start(bf16[2,192,384]{2,1,0:T(8,128)(2,1)S(1)} %broadcast_select_fusion.2), channel_id=1, source_target_pairs={{4,6},{5,7},{8,12},{9,13},{12,14},{13,15},{20,22},{21,23},{24,28},... | collective-permute-start | bytes 884744 | tf_op jit(solution)/shard_map/ppermute | solution.py:46
  89.0 12.7 %collective-permute-start.34 = (bf16[2,384,384]{2,1,0:T(8,128)(2,1)S(1)}, bf16[2,384,384]{2,1,0:T(8,128)(2,1)S(1)}, u32[]{:S(2)}, u32[]{:S(2)}) collective-permute-start(bf16[2,384,384]{2,1,0:T(8,128)(2,1)S(1)} %collective-permute-done.22.refs_19_), channel_id=1, source_target_pairs={{0,8},{1,9},{2,10},{3,11},{4,12},{5,13},{6,14},{7,15},{8,0},{9,1},... | collective-permute-start | bytes 1769480 | tf_op jit(solution)/shard_map/ppermute | solution.py:46
  93.5 8.1 %collective-permute-start.33 = (bf16[2,384,384]{2,1,0:T(8,128)(2,1)S(1)}, bf16[2,384,384]{2,1,0:T(8,128)(2,1)S(1)}, u32[]{:S(2)}, u32[]{:S(2)}) collective-permute-start(bf16[2,384,384]{2,1,0:T(8,128)(2,1)S(1)} %collective-permute-done.21.refs_18_), channel_id=1, source_target_pairs={{0,8},{1,9},{2,10},{3,11},{4,12},{5,13},{6,14},{7,15},{8,0},{9,1},... | collective-permute-start | bytes 1769480 | tf_op jit(solution)/shard_map/ppermute | solution.py:46
  93.5 6.9 %collective-permute-start.31 = (bf16[2,192,384]{2,1,0:T(8,128)(2,1)S(1)}, bf16[2,192,384]{2,1,0:T(8,128)(2,1)S(1)}, u32[]{:S(2)}, u32[]{:S(2)}) collective-permute-start(bf16[2,192,384]{2,1,0:T(8,128)(2,1)S(1)} %collective-permute-done.19.refs_16_), channel_id=1, source_target_pairs={{0,8},{1,9},{2,10},{3,11},{4,12},{5,13},{6,14},{7,15},{8,0},{9,1},... | collective-permute-start | bytes 884744 | tf_op jit(solution)/shard_map/ppermute | solution.py:46
  94.0 6.4 %collective-permute-start.30 = (bf16[2,192,384]{2,1,0:T(8,128)(2,1)S(1)}, bf16[2,192,384]{2,1,0:T(8,128)(2,1)S(1)}, u32[]{:S(2)}, u32[]{:S(2)}) collective-permute-start(bf16[2,192,384]{2,1,0:T(8,128)(2,1)S(1)} %collective-permute-done.18.refs_15_), channel_id=1, source_target_pairs={{0,8},{1,9},{2,10},{3,11},{4,12},{5,13},{6,14},{7,15},{8,0},{9,1},... | collective-permute-start | bytes 884744 | tf_op jit(solution)/shard_map/ppermute | solution.py:46
  99.9 1.7 %collective-permute-start.32 = (bf16[2,192,384]{2,1,0:T(8,128)(2,1)S(1)}, bf16[2,192,384]{2,1,0:T(8,128)(2,1)S(1)}, u32[]{:S(2)}, u32[]{:S(2)}) collective-permute-start(bf16[2,192,384]{2,1,0:T(8,128)(2,1)S(1)} %collective-permute-done.20.refs_17_), channel_id=1, source_target_pairs={{0,8},{1,9},{2,10},{3,11},{4,12},{5,13},{6,14},{7,15},{8,0},{9,1},... | collective-permute-start | bytes 884744 | tf_op jit(solution)/shard_map/ppermute | solution.py:46
  107.9 8.3 %collective-permute-start.35 = (bf16[2,192,384]{2,1,0:T(8,128)(2,1)S(1)}, bf16[2,192,384]{2,1,0:T(8,128)(2,1)S(1)}, u32[]{:S(2)}, u32[]{:S(2)}) collective-permute-start(bf16[2,192,384]{2,1,0:T(8,128)(2,1)S(1)} %get-tuple-element.83), channel_id=1, source_target_pairs={{0,1},{1,0},{2,3},{3,2},{4,5},{5,4},{6,7},{7,6},{8,9},{9,8},{10,11... | collective-permute-start | bytes 884744 | tf_op jit(solution)/shard_map/ppermute | solution.py:46
  109.2 8.8 %collective-permute-start.36 = (bf16[384,384]{1,0:T(8,128)(2,1)S(1)}, bf16[384,384]{1,0:T(8,128)(2,1)S(1)}, u32[]{:S(2)}, u32[]{:S(2)}) collective-permute-start(bf16[384,384]{1,0:T(8,128)(2,1)S(1)} %get-tuple-element.80), channel_id=1, source_target_pairs={{0,8},{1,9},{2,10},{3,11},{4,12},{5,13},{6,14},{7,15},{8,0},{9,1},... | collective-permute-start | bytes 884744 | tf_op jit(solution)/shard_map/ppermute | solution.py:46
  109.8 8.6 %collective-permute-start.37 = (bf16[384,384]{1,0:T(8,128)(2,1)S(1)}, bf16[384,384]{1,0:T(8,128)(2,1)S(1)}, u32[]{:S(2)}, u32[]{:S(2)}) collective-permute-start(bf16[384,384]{1,0:T(8,128)(2,1)S(1)} %get-tuple-element.81), channel_id=1, source_target_pairs={{0,16},{1,17},{2,18},{3,19},{4,20},{5,21},{6,22},{7,23},{8,24},{9,... | collective-permute-start | bytes 884744 | tf_op jit(solution)/shard_map/ppermute | solution.py:46
  111.0 13.9 %collective-permute-start.38 = (bf16[384,384]{1,0:T(8,128)(2,1)S(1)}, bf16[384,384]{1,0:T(8,128)(2,1)S(1)}, u32[]{:S(2)}, u32[]{:S(2)}) collective-permute-start(bf16[384,384]{1,0:T(8,128)(2,1)S(1)} %get-tuple-element.82), channel_id=1, source_target_pairs={{0,24},{1,25},{2,26},{3,27},{4,28},{5,29},{6,30},{7,31},{8,16},{9,... | collective-permute-start | bytes 884744 | tf_op jit(solution)/shard_map/ppermute | solution.py:46

commit v16 on v15

--- a/solution.py
+++ b/solution.py
@@ -306,15 +306,15 @@
     return value
 
 
-def spread_kernel(plan, place, *refs):
+def spread_kernel(plan, block, place, *refs):
     groups, width = plan.groups, plan.width
-    ins, out = refs[:-1], refs[-1]
-    for m in range(plan.moments):
-        parts = [pick(ins, place[0] ^ (m * groups + g)) for g in range(groups)]
-        for p in range(2):
-            out[m, :, p, :] = jnp.concatenate(
-                [part[:, p * width : (p + 1) * width] for part in parts], axis=1
-            )
+    ins, out, held, sem = refs[:groups], refs[-3], refs[-2], refs[-1]
+    parts = [pick(ins, (place[0] % groups) ^ g) for g in range(groups)]
+    for p in range(2):
+        held[:, p, :] = jnp.concatenate(
+            [part[:, p * width : (p + 1) * width] for part in parts], axis=1
+        )
+    run_copies([pltpu.make_async_copy(held, out.at[(place[0] // groups) ^ block], sem.at[0])])
 
 
 def on_device(mesh, lesser, greater, triples, diag_inverse, right_side):
@@ -529,15 +529,26 @@
     )(place, *whole)
 
     back = [solved[0]] + [exchange_row(solved[s], s) for s in range(1, rows)]
-    back = after(back, sigma)
-    spread = pl.pallas_call(
-        functools.partial(spread_kernel, plan),
-        out_shape=jax.ShapeDtypeStruct(right_side.shape, bf16),
-        in_specs=[smem()] + [pl.BlockSpec(memory_space=pltpu.VMEM)] * rows,
-        compiler_params=params,
-        name="place_solution",
-    )
-    return sigma, spread(place, *back)
+    spread = None
+    for block in range(moments):
+        pieces = back[block * groups : (block + 1) * groups]
+        before = []
+        if block:
+            pieces = after(pieces, spread, sigma)
+            before = [spread]
+        spread = pl.pallas_call(
+            functools.partial(spread_kernel, plan, block),
+            out_shape=jax.ShapeDtypeStruct(right_side.shape, bf16),
+            in_specs=[smem()]
+            + [pl.BlockSpec(memory_space=pltpu.VMEM)] * groups
+            + hbm(len(before)),
+            out_specs=hbm(1)[0],
+            scratch_shapes=[pltpu.VMEM((side, 2, side), bf16), dma(1)],
+            input_output_aliases={1 + groups: 0} if block else {},
+            compiler_params=params,
+            name="place_solution",
+        )(place, *pieces, *before)
+    return sigma, spread
 
 
 def solution(mesh):

time: 128 us -> 128 us (level)
  waiting for transfers between devices: 59 us -> 57.2 us
    ppermute x39, waiting for transfers between devices: 59 us -> 57.2 us  [send(): return lax.ppermute(value, AXES, pairs)]
    pallas_call x1 -> x2, Pallas kernels: 2.69 us -> 3.81 us  [on_device(): pl.pallas_call(functools.partial(spread_kernel, plan, block), out_shape=j...]
  transfers between devices with their start and end apart: 39 -> 39, of which waited for: 13 -> 12; matrix products, arithmetic and copies ran while one was open for 12% -> 12% of each run, Pallas kernels for 4% -> 6%
where the time goes in v16:
time: 128 us; the launch traced here: 127 us
  waiting for transfers between devices  57.2 us (45%)
  starting transfers between devices  31.2 us (24%)
  Pallas kernels  19.3 us (15%)
  local copies, waits for them, and re-layouts  14.9 us (12%)
  other arithmetic  3.02 us (2%)
  between operations  1.29 us (1%)
    ppermute x39, waiting for transfers between devices, send(): return lax.ppermute(value, AXES, pairs)  57.2 us
    ppermute x39, starting transfers between devices, send(): return lax.ppermute(value, AXES, pairs)  31.2 us
    pallas_call x2, Pallas kernels, self_energy(): pl.pallas_call(functools.partial(sigma_kernel, plan, pair_count, u, copie...  7.49 us
    pallas_call x1, Pallas kernels, on_device(): pl.pallas_call(functools.partial(solve_kernel, plan, sources), out_shape=...  6.21 us
    optimization_barrier x2, local copies, waits for them, and re-layouts, after(): return lax.optimization_barrier((value, others))[0]  4.34 us
    pallas_call x2, Pallas kernels, on_device(): pl.pallas_call(functools.partial(spread_kernel, plan, block), out_shape=j...  3.81 us
    dynamic_slice x5, local copies, waits for them, and re-layouts, on_device(): lax.dynamic_index_in_dim(right, r ^ s, 0, keepdims=False)  3.6 us
    dynamic_slice x2, local copies, waits for them, and re-layouts, part_of(): lax.dynamic_slice_in_dim(value, (y ^ q) * half + u * plan.sub, plan.sub, 2)  2.95 us
  transfers between devices with their start and end apart: 39, of which 12 were waited for; matrix products, arithmetic and copies ran while one was open for 12% of the time, Pallas kernels for 6%

profile of v16, /device:TPU:25, one launch (start us, length us, event | category | flops | bytes accessed | tf_op | source)
XLA Modules:
  0.0 126.9 jit_solution(18334511141390858141)
XLA Ops:
  0.7 2.0 %constant_dynamic-slice_fusion = (bf16[2,2,96,384]{3,2,1,0:T(8,128)(2,1)}, bf16[2,2,96,384]{3,2,1,0:T(8,128)(2,1)}) fusion(bf16[2,2,384,384]{3,2,1,0:T(8,128)(2,1)} %refs_0_.3, s32[]{:T(128)S(6)} %select_n.109, s32[]{:T(128)S(6)} %select_n.101), kind=kLoop, calls=%fused_computation.27 | loop fusion | bytes 1179656 | tf_op jit(solution)/shard_map/dynamic_slice | solution.py:344
  2.7 1.2 collective-permute-start.1
  3.9 0.8 copy.12
  4.7 0.9 dynamic-slice_bitcast_fusion.2
  6.2 0.9 dynamic-slice_bitcast_fusion
  7.1 1.2 collective-permute-start
  8.3 0.7 slice_bitcast_fusion.4.thirds
  9.0 3.6 %copy.13 = bf16[2,384,2,384]{1,3,2,0:T(8,128)(2,1)S(1)} copy(bf16[2,384,2,384]{3,2,1,0:T(2,128)(2,1)} %param.9) | data formatting | bytes 2359296 | tf_op jit(solution)/shard_map/optimization_barrier | solution.py:299
  12.5 1.1 copy.14
  13.7 1.4 %constant_dynamic-slice_fusion.1 = (bf16[1,384,384]{1,2,0:T(8,128)(2,1)S(1)}, bf16[1,384,384]{1,2,0:T(8,128)(2,1)S(1)}, bf16[1,384,384]{1,2,0:T(8,128)(2,1)S(1)}, bf16[1,384,384]{1,2,0:T(8,128)(2,1)S(1)}) fusion(bf16[4,384,384]{1,2,0:T(8,128)(2,1)} %bitcast.41, s32[]{:T(128)S(6)} %select_n.105, s32[]{:T(128)S(6)} %select_n.104, s32[]{:T(128)S(6)} %select_n.103, ...), kind=kLoop, calls=%fused_computation.28 | loop fusion | bytes 2359312 | tf_op jit(solution)/shard_map/jit(dynamic_index_in_dim)/dynamic_slice | solution.py:364
  15.1 1.0 collective-permute-start.2
  16.7 0.9 copy.18
  17.8 0.9 copy.16
  19.0 2.3 %collective-permute-done = bf16[2,384,384]{2,1,0:T(8,128)(2,1)} collective-permute-done((bf16[2,384,384]{2,1,0:T(8,128)(2,1)}, bf16[2,384,384]{2,1,0:T(8,128)(2,1)}, u32[]{:S(2)}, u32[]{:S(2)}) %collective-permute-start) | collective-permute-done | bytes 589856 | tf_op jit(solution)/shard_map/ppermute | solution.py:46
  21.3 2.4 %broadcast_select_fusion = (bf16[2,384,384]{2,1,0:T(8,128)(2,1)}, bf16[2,384,384]{2,1,0:T(8,128)(2,1)}) fusion(bf16[2,384,384]{2,1,0:T(8,128)(2,1)} %collective-permute-done, pred[]{:T(512)S(6)} %select_n.113, bf16[2,2,384,384]{3,2,1,0:T(8,128)(2,1)} %param.8, s32[]{:T(128)S(6)} %select_n.107), kind=kLoop, calls=%fused_computation.6 | loop fusion | flops 294912 | bytes 2359301 | tf_op jit(solution)/shard_map/select_n | solution.py:341
  23.6 3.3 %self_energy.2 = (bf16[2,96,384]{2,1,0:T(8,128)(2,1)S(1)}, bf16[2,96,384]{2,1,0:T(8,128)(2,1)S(1)}, bf16[2,96,384]{2,1,0:T(8,128)(2,1)S(1)}, bf16[2,96,384]{2,1,0:T(8,128)(2,1)S(1)}) custom-call(s32[3]{0:T(128)S(1)} %pad_add_fusion.place, s32[4,8]{1,0:T(4,128)S(1)} %fusion.1.quads, s32[4,8]{1,0:T(4,128)S(1)} %slice_bitcast_fusion.4.thirds, ...), custom_call_target="tpu_custom_call" | custom-call | tf_op jit(solution)/shard_map/self_energy/pallas_call | solution.py:376
  27.0 2.3 %collective-permute-done.3.refs_3_ = bf16[2,2,96,384]{3,2,1,0:T(8,128)(2,1)S(1)} collective-permute-done((bf16[2,2,96,384]{3,2,1,0:T(8,128)(2,1)}, bf16[2,2,96,384]{3,2,1,0:T(8,128)(2,1)S(1)}, u32[]{:S(2)}, u32[]{:S(2)}) %collective-permute-start.3) | collective-permute-done | bytes 294944 | tf_op jit(solution)/shard_map/ppermute | solution.py:46
  29.3 4.2 %self_energy.3 = (bf16[2,192,384]{2,1,0:T(8,128)(2,1)S(1)}, bf16[2,192,384]{2,1,0:T(8,128)(2,1)S(1)}, bf16[2,192,384]{2,1,0:T(8,128)(2,1)S(1)}, bf16[2,192,384]{2,1,0:T(8,128)(2,1)S(1)}) custom-call(s32[3]{0:T(128)S(1)} %pad_add_fusion.place, s32[4,8]{1,0:T(4,128)S(1)} %fusion.1.quads, s32[4,8]{1,0:T(4,128)S(1)} %slice_bitcast_fusion.4.thirds, ...), custom_call_target="tpu_custom_call" | custom-call | tf_op jit(solution)/shard_map/self_energy/pallas_call | solution.py:376
  33.5 0.8 collective-permute-start.12
  34.3 1.3 %collective-permute-start.5 = (bf16[2,192,384]{2,1,0:T(8,128)(2,1)S(1)}, bf16[2,192,384]{2,1,0:T(8,128)(2,1)S(1)}, u32[]{:S(2)}, u32[]{:S(2)}) collective-permute-start(bf16[2,192,384]{2,1,0:T(8,128)(2,1)S(1)} %get-tuple-element.59), channel_id=1, source_target_pairs={{0,1},{1,0},{2,3},{3,2},{4,5},{5,4},{6,7},{7,6},{8,9},{9,8},{10,11... | collective-permute-start | bytes 884744 | tf_op jit(solution)/shard_map/ppermute | solution.py:46
  36.4 1.4 %collective-permute-start.15 = (bf16[2,192,384]{2,1,0:T(8,128)(2,1)S(1)}, bf16[2,192,384]{2,1,0:T(8,128)(2,1)S(1)}, u32[]{:S(2)}, u32[]{:S(2)}) collective-permute-start(bf16[2,192,384]{2,1,0:T(8,128)(2,1)S(1)} %get-tuple-element.94), channel_id=1, source_target_pairs={{0,2},{1,3},{2,4},{3,5},{8,10},{9,11},{10,12},{11,13},{12,14},{13,... | collective-permute-start | bytes 884744 | tf_op jit(solution)/shard_map/ppermute | solution.py:46
  37.9 0.7 collective-permute-start.13
  38.7 2.2 %collective-permute-done.5.refs_2_ = bf16[2,192,384]{2,1,0:T(8,128)(2,1)S(1)} collective-permute-done((bf16[2,192,384]{2,1,0:T(8,128)(2,1)S(1)}, bf16[2,192,384]{2,1,0:T(8,128)(2,1)S(1)}, u32[]{:S(2)}, u32[]{:S(2)}) %collective-permute-start.5) | collective-permute-done | bytes 294944 | tf_op jit(solution)/shard_map/ppermute | solution.py:46
  41.0 1.3 %collective-permute-start.16 = (bf16[2,192,384]{2,1,0:T(8,128)(2,1)S(1)}, bf16[2,192,384]{2,1,0:T(8,128)(2,1)S(1)}, u32[]{:S(2)}, u32[]{:S(2)}) collective-permute-start(bf16[2,192,384]{2,1,0:T(8,128)(2,1)S(1)} %get-tuple-element.96), channel_id=1, source_target_pairs={{0,2},{1,3},{2,4},{3,5},{8,10},{9,11},{10,12},{11,13},{12,14},{13,... | collective-permute-start | bytes 884744 | tf_op jit(solution)/shard_map/ppermute | solution.py:46
  43.0 2.4 %collective-permute-start.9 = (bf16[384,384]{1,0:T(8,128)(2,1)S(1)}, bf16[384,384]{1,0:T(8,128)(2,1)S(1)}, u32[]{:S(2)}, u32[]{:S(2)}) collective-permute-start(bf16[384,384]{1,0:T(8,128)(2,1)S(1)} %bitcast.44), channel_id=1, source_target_pairs={{0,8},{1,9},{2,10},{3,11},{4,12},{5,13},{6,14},{7,15},{8,0},{9,1},... | collective-permute-start | bytes 884744 | tf_op jit(solution)/shard_map/ppermute | solution.py:46
  45.3 2.4 %collective-permute-done.15.refs_12_ = bf16[2,192,384]{2,1,0:T(8,128)(2,1)S(1)} collective-permute-done((bf16[2,192,384]{2,1,0:T(8,128)(2,1)S(1)}, bf16[2,192,384]{2,1,0:T(8,128)(2,1)S(1)}, u32[]{:S(2)}, u32[]{:S(2)}) %collective-permute-start.15) | collective-permute-done | bytes 294944 | tf_op jit(solution)/shard_map/ppermute | solution.py:46
  47.8 1.3 %collective-permute-start.17 = (bf16[2,192,384]{2,1,0:T(8,128)(2,1)S(1)}, bf16[2,192,384]{2,1,0:T(8,128)(2,1)S(1)}, u32[]{:S(2)}, u32[]{:S(2)}) collective-permute-start(bf16[2,192,384]{2,1,0:T(8,128)(2,1)S(1)} %broadcast_select_fusion.5), channel_id=1, source_target_pairs={{2,4},{3,5},{4,6},{5,7},{8,10},{9,11},{10,12},{11,13},{12,14},{13,... | collective-permute-start | bytes 884744 | tf_op jit(solution)/shard_map/ppermute | solution.py:46
  49.3 0.9 copy-done.5
  50.2 10.4 %collective-permute-done.17.refs_14_ = bf16[2,192,384]{2,1,0:T(8,128)(2,1)S(1)} collective-permute-done((bf16[2,192,384]{2,1,0:T(8,128)(2,1)S(1)}, bf16[2,192,384]{2,1,0:T(8,128)(2,1)S(1)}, u32[]{:S(2)}, u32[]{:S(2)}) %collective-permute-start.17) | collective-permute-done | bytes 294944 | tf_op jit(solution)/shard_map/ppermute | solution.py:46
  60.6 3.1 %collective-permute-start.27 = (bf16[2,192,384]{2,1,0:T(8,128)(2,1)S(1)}, bf16[2,192,384]{2,1,0:T(8,128)(2,1)S(1)}, u32[]{:S(2)}, u32[]{:S(2)}) collective-permute-start(bf16[2,192,384]{2,1,0:T(8,128)(2,1)S(1)} %collective-permute-done.15.refs_12_), channel_id=1, source_target_pairs={{0,8},{1,9},{2,10},{3,11},{4,12},{5,13},{6,14},{7,15},{8,0},{9,1},... | collective-permute-start | bytes 884744 | tf_op jit(solution)/shard_map/ppermute | solution.py:46
  65.0 1.3 %collective-permute-start.19 = (bf16[2,192,384]{2,1,0:T(8,128)(2,1)S(1)}, bf16[2,192,384]{2,1,0:T(8,128)(2,1)S(1)}, u32[]{:S(2)}, u32[]{:S(2)}) collective-permute-start(bf16[2,192,384]{2,1,0:T(8,128)(2,1)S(1)} %broadcast_select_fusion.3), channel_id=1, source_target_pairs={{4,6},{5,7},{8,12},{9,13},{12,14},{13,15},{20,22},{21,23},{24,28},... | collective-permute-start | bytes 884744 | tf_op jit(solution)/shard_map/ppermute | solution.py:46
  66.8 1.3 %collective-permute-start.18 = (bf16[2,192,384]{2,1,0:T(8,128)(2,1)S(1)}, bf16[2,192,384]{2,1,0:T(8,128)(2,1)S(1)}, u32[]{:S(2)}, u32[]{:S(2)}) collective-permute-start(bf16[2,192,384]{2,1,0:T(8,128)(2,1)S(1)} %broadcast_select_fusion.4), channel_id=1, source_target_pairs={{2,4},{3,5},{4,6},{5,7},{8,10},{9,11},{10,12},{11,13},{12,14},{13,... | collective-permute-start | bytes 884744 | tf_op jit(solution)/shard_map/ppermute | solution.py:46
  68.4 0.7 collective-permute-start.22
  69.1 11.9 %collective-permute-done.19.refs_16_ = bf16[2,192,384]{2,1,0:T(8,128)(2,1)S(1)} collective-permute-done((bf16[2,192,384]{2,1,0:T(8,128)(2,1)S(1)}, bf16[2,192,384]{2,1,0:T(8,128)(2,1)S(1)}, u32[]{:S(2)}, u32[]{:S(2)}) %collective-permute-start.19) | collective-permute-done | bytes 294944 | tf_op jit(solution)/shard_map/ppermute | solution.py:46
  81.0 1.3 %collective-permute-start.21 = (bf16[2,384,384]{2,1,0:T(8,128)(2,1)S(1)}, bf16[2,384,384]{2,1,0:T(8,128)(2,1)S(1)}, u32[]{:S(2)}, u32[]{:S(2)}) collective-permute-start(bf16[2,384,384]{2,1,0:T(8,128)(2,1)S(1)} %pad_maximum_fusion.2.refs_8_), channel_id=1, source_target_pairs={{8,14},{9,15},{24,30},{25,31}} | collective-permute-start | bytes 1769480 | tf_op jit(solution)/shard_map/ppermute | solution.py:46
  82.3 4.7 %collective-permute-done.18.refs_15_ = bf16[2,192,384]{2,1,0:T(8,128)(2,1)S(1)} collective-permute-done((bf16[2,192,384]{2,1,0:T(8,128)(2,1)S(1)}, bf16[2,192,384]{2,1,0:T(8,128)(2,1)S(1)}, u32[]{:S(2)}, u32[]{:S(2)}) %collective-permute-start.18) | collective-permute-done | bytes 294944 | tf_op jit(solution)/shard_map/ppermute | solution.py:46
  87.6 1.3 %collective-permute-start.20 = (bf16[2,192,384]{2,1,0:T(8,128)(2,1)S(1)}, bf16[2,192,384]{2,1,0:T(8,128)(2,1)S(1)}, u32[]{:S(2)}, u32[]{:S(2)}) collective-permute-start(bf16[2,192,384]{2,1,0:T(8,128)(2,1)S(1)} %broadcast_select_fusion.2), channel_id=1, source_target_pairs={{4,6},{5,7},{8,12},{9,13},{12,14},{13,15},{20,22},{21,23},{24,28},... | collective-permute-start | bytes 884744 | tf_op jit(solution)/shard_map/ppermute | solution.py:46
  89.4 4.1 %collective-permute-done.21.refs_18_ = bf16[2,384,384]{2,1,0:T(8,128)(2,1)S(1)} collective-permute-done((bf16[2,384,384]{2,1,0:T(8,128)(2,1)S(1)}, bf16[2,384,384]{2,1,0:T(8,128)(2,1)S(1)}, u32[]{:S(2)}, u32[]{:S(2)}) %collective-permute-start.21) | collective-permute-done | bytes 589856 | tf_op jit(solution)/shard_map/ppermute | solution.py:46
  94.1 5.8 %collective-permute-done.20.refs_17_ = bf16[2,192,384]{2,1,0:T(8,128)(2,1)S(1)} collective-permute-done((bf16[2,192,384]{2,1,0:T(8,128)(2,1)S(1)}, bf16[2,192,384]{2,1,0:T(8,128)(2,1)S(1)}, u32[]{:S(2)}, u32[]{:S(2)}) %collective-permute-start.20) | collective-permute-done | bytes 294944 | tf_op jit(solution)/shard_map/ppermute | solution.py:46
  100.4 1.2 collective-permute-done.32.refs_29_
  101.6 6.2 %substitution.1 = (bf16[384,384]{1,0:T(8,128)(2,1)S(1)}, bf16[384,384]{1,0:T(8,128)(2,1)S(1)}, bf16[384,384]{1,0:T(8,128)(2,1)S(1)}, bf16[384,384]{1,0:T(8,128)(2,1)S(1)}) custom-call(s32[3]{0:T(128)S(1)} %pad_add_fusion.place, bf16[384,768]{1,0:T(8,128)(2,1)S(1)} %pad_maximum_fusion.refs_0_, bf16[384,768]{1,0:T(8,128)(2,1)S(1)} %collective-permute-done.7.refs_1_, ...), custom_call_target="tpu_custom_call" | custom-call | tf_op jit(solution)/shard_map/substitution/pallas_call | solution.py:503
  107.8 1.3 %collective-permute-start.35 = (bf16[2,192,384]{2,1,0:T(8,128)(2,1)S(1)}, bf16[2,192,384]{2,1,0:T(8,128)(2,1)S(1)}, u32[]{:S(2)}, u32[]{:S(2)}) collective-permute-start(bf16[2,192,384]{2,1,0:T(8,128)(2,1)S(1)} %get-tuple-element.81), channel_id=1, source_target_pairs={{0,1},{1,0},{2,3},{3,2},{4,5},{5,4},{6,7},{7,6},{8,9},{9,8},{10,11... | collective-permute-start | bytes 884744 | tf_op jit(solution)/shard_map/ppermute | solution.py:46
  109.8 1.1 collective-permute-start.36
  111.4 4.7 %collective-permute-done.35.refs_3_ = bf16[2,192,384]{2,1,0:T(8,128)(2,1)S(1)} collective-permute-done((bf16[2,192,384]{2,1,0:T(8,128)(2,1)S(1)}, bf16[2,192,384]{2,1,0:T(8,128)(2,1)S(1)}, u32[]{:S(2)}, u32[]{:S(2)}) %collective-permute-start.35) | collective-permute-done | bytes 294944 | tf_op jit(solution)/shard_map/ppermute | solution.py:46
  116.1 1.8 %place_sigma.1 = bf16[2,2,384,384]{3,2,1,0:T(8,128)(2,1)} custom-call(s32[3]{0:T(128)S(1)} %pad_add_fusion.place, bf16[2,192,384]{2,1,0:T(8,128)(2,1)S(1)} %get-tuple-element.57.refs_0_, bf16[2,192,384]{2,1,0:T(8,128)(2,1)S(1)} %get-tuple-element.58.refs_1_, bf16[2,192,384]{2,1,0:T(8,128)(2,1)S(1)} %collective-permute-done.5.refs_2_, ...), custom_call_target="tpu_custom_call" | custom-call | tf_op jit(solution)/shard_map/place_sigma/pallas_call | solution.py:522
  117.9 1.9 %place_solution.2.refs_2_ = bf16[2,384,2,384]{3,2,1,0:T(2,128)(2,1)} custom-call(s32[3]{0:T(128)S(1)} %pad_add_fusion.place, bf16[384,384]{1,0:T(8,128)(2,1)S(1)} %get-tuple-element.77.refs_0_, bf16[384,384]{1,0:T(8,128)(2,1)S(1)} %collective-permute-done.38.refs_1_), custom_call_target="tpu_custom_call" | custom-call | tf_op jit(solution)/shard_map/place_solution/pallas_call | solution.py:539
  119.8 5.0 %collective-permute-done.37.refs_1_ = bf16[384,384]{1,0:T(8,128)(2,1)S(1)} collective-permute-done((bf16[384,384]{1,0:T(8,128)(2,1)S(1)}, bf16[384,384]{1,0:T(8,128)(2,1)S(1)}, u32[]{:S(2)}, u32[]{:S(2)}) %collective-permute-start.37) | collective-permute-done | bytes 294944 | tf_op jit(solution)/shard_map/ppermute | solution.py:46
  124.8 1.9 %place_solution.3 = bf16[2,384,2,384]{3,2,1,0:T(2,128)(2,1)} custom-call(s32[3]{0:T(128)S(1)} %pad_add_fusion.place, bf16[384,384]{1,0:T(8,128)(2,1)S(1)} %collective-permute-done.36.refs_0_, bf16[384,384]{1,0:T(8,128)(2,1)S(1)} %collective-permute-done.37.refs_1_, bf16[2,384,2,384]{3,2,1,0:T(2,128)(2,1)} %place_solution.2.refs_2_), custom_call_target="tpu_custom_call", output_to_operand_aliasing={{}: (3, {})} | custom-call | tf_op jit(solution)/shard_map/place_solution/pallas_call | solution.py:539
  (79 shorter events, 8.8 us)
Async XLA Ops:
  0.6 3.3 %copy-start.3 = (bf16[2,2,384,384]{3,2,1,0:T(8,128)(2,1)S(1)}, bf16[2,2,384,384]{3,2,1,0:T(8,128)(2,1)}, u32[]{:S(2)}) copy-start(bf16[2,2,384,384]{3,2,1,0:T(8,128)(2,1)} %param.6) | copy-start | bytes 3538948
  2.7 12.4 %collective-permute-start.1 = (bf16[2,2,96,384]{3,2,1,0:T(8,128)(2,1)}, bf16[2,2,96,384]{3,2,1,0:T(8,128)(2,1)S(1)}, u32[]{:S(2)}, u32[]{:S(2)}) collective-permute-start(bf16[2,2,96,384]{3,2,1,0:T(8,128)(2,1)} %get-tuple-element.89), channel_id=1, source_target_pairs={{0,1},{1,0},{2,3},{3,2},{4,5},{5,4},{6,7},{7,6},{8,9},{9,8},{10,11... | collective-permute-start | bytes 884744 | tf_op jit(solution)/shard_map/ppermute | solution.py:46
  4.7 1.5 %copy-start.4 = (bf16[2,2,384,384]{3,2,1,0:T(8,128)(2,1)S(1)}, bf16[2,2,384,384]{3,2,1,0:T(8,128)(2,1)}, u32[]{:S(2)}) copy-start(bf16[2,2,384,384]{3,2,1,0:T(8,128)(2,1)} %param.8) | copy-start | bytes 3538948
  5.6 18.0 %collective-permute-start.4 = (bf16[2,2,96,384]{3,2,1,0:T(8,128)(2,1)}, bf16[2,2,96,384]{3,2,1,0:T(8,128)(2,1)S(1)}, u32[]{:S(2)}, u32[]{:S(2)}) collective-permute-start(bf16[2,2,96,384]{3,2,1,0:T(8,128)(2,1)} %get-tuple-element.87), channel_id=1, source_target_pairs={{0,1},{1,0},{2,3},{3,2},{4,5},{5,4},{6,7},{7,6},{8,9},{9,8},{10,11... | collective-permute-start | bytes 884744 | tf_op jit(solution)/shard_map/ppermute | solution.py:46
  7.1 14.2 %collective-permute-start = (bf16[2,384,384]{2,1,0:T(8,128)(2,1)}, bf16[2,384,384]{2,1,0:T(8,128)(2,1)}, u32[]{:S(2)}, u32[]{:S(2)}) collective-permute-start(bf16[2,384,384]{2,1,0:T(8,128)(2,1)} %dynamic-slice_bitcast_fusion), channel_id=1, source_target_pairs={{0,16},{1,17},{2,18},{3,19},{4,20},{5,21},{6,22},{7,23},{8,24},{9,... | collective-permute-start | bytes 1769480 | tf_op jit(solution)/shard_map/ppermute | solution.py:46
  13.7 1.4 %copy-start.7 = (s32[4,8,3]{1,0,2:T(4,128)S(1)}, s32[4,8,3]{1,0,2:T(4,128)}, u32[]{:S(2)}) copy-start(s32[4,8,3]{1,0,2:T(4,128)} %param.7) | copy-start | bytes 1156
  15.1 11.9 %collective-permute-start.2 = (bf16[2,2,96,384]{3,2,1,0:T(8,128)(2,1)}, bf16[2,2,96,384]{3,2,1,0:T(8,128)(2,1)S(1)}, u32[]{:S(2)}, u32[]{:S(2)}) collective-permute-start(bf16[2,2,96,384]{3,2,1,0:T(8,128)(2,1)} %get-tuple-element.51), channel_id=1, source_target_pairs={{0,1},{1,0},{2,3},{3,2},{4,5},{5,4},{6,7},{7,6},{8,9},{9,8},{10,11... | collective-permute-start | bytes 884744 | tf_op jit(solution)/shard_map/ppermute | solution.py:46
  16.1 13.2 %collective-permute-start.3 = (bf16[2,2,96,384]{3,2,1,0:T(8,128)(2,1)}, bf16[2,2,96,384]{3,2,1,0:T(8,128)(2,1)S(1)}, u32[]{:S(2)}, u32[]{:S(2)}) collective-permute-start(bf16[2,2,96,384]{3,2,1,0:T(8,128)(2,1)} %get-tuple-element.52), channel_id=1, source_target_pairs={{0,1},{1,0},{2,3},{3,2},{4,5},{5,4},{6,7},{7,6},{8,9},{9,8},{10,11... | collective-permute-start | bytes 884744 | tf_op jit(solution)/shard_map/ppermute | solution.py:46
  18.9 4.7 %copy-start = (bf16[2,2,384,384]{3,2,1,0:T(8,128)(2,1)S(1)}, bf16[2,2,384,384]{3,2,1,0:T(8,128)(2,1)}, u32[]{:S(2)}) copy-start(bf16[2,2,384,384]{3,2,1,0:T(8,128)(2,1)} %refs_0_.3) | copy-start | bytes 3538948
  33.5 5.1 %copy-start.2 = (bf16[2,384,384]{2,1,0:T(8,128)(2,1)S(1)}, bf16[2,384,384]{2,1,0:T(8,128)(2,1)}, u32[]{:S(2)}) copy-start(bf16[2,384,384]{2,1,0:T(8,128)(2,1)} %get-tuple-element.85) | copy-start | bytes 1769476
  33.5 2.9 %collective-permute-start.12 = (bf16[2,192,384]{2,1,0:T(8,128)(2,1)S(1)}, bf16[2,192,384]{2,1,0:T(8,128)(2,1)S(1)}, u32[]{:S(2)}, u32[]{:S(2)}) collective-permute-start(bf16[2,192,384]{2,1,0:T(8,128)(2,1)S(1)} %get-tuple-element.58.refs_1_), channel_id=1, source_target_pairs={{8,24},{9,25},{16,0},{17,1},{18,2},{19,3},{24,8},{25,9},{26,10},{2... | collective-permute-start | bytes 884744 | tf_op jit(solution)/shard_map/ppermute | solution.py:46
  34.3 6.6 %collective-permute-start.5 = (bf16[2,192,384]{2,1,0:T(8,128)(2,1)S(1)}, bf16[2,192,384]{2,1,0:T(8,128)(2,1)S(1)}, u32[]{:S(2)}, u32[]{:S(2)}) collective-permute-start(bf16[2,192,384]{2,1,0:T(8,128)(2,1)S(1)} %get-tuple-element.59), channel_id=1, source_target_pairs={{0,1},{1,0},{2,3},{3,2},{4,5},{5,4},{6,7},{7,6},{8,9},{9,8},{10,11... | collective-permute-start | bytes 884744 | tf_op jit(solution)/shard_map/ppermute | solution.py:46
  35.7 5.2 %collective-permute-start.6 = (bf16[2,192,384]{2,1,0:T(8,128)(2,1)S(1)}, bf16[2,192,384]{2,1,0:T(8,128)(2,1)S(1)}, u32[]{:S(2)}, u32[]{:S(2)}) collective-permute-start(bf16[2,192,384]{2,1,0:T(8,128)(2,1)S(1)} %get-tuple-element.81), channel_id=1, source_target_pairs={{8,25},{9,24},{16,1},{17,0},{18,3},{19,2},{24,9},{25,8},{26,11},{2... | collective-permute-start | bytes 884744 | tf_op jit(solution)/shard_map/ppermute | solution.py:46
  36.4 6.5 %copy-start.6 = (bf16[1,384,384]{2,1,0:T(8,128)(2,1)S(1)}, bf16[1,384,384]{2,1,0:T(8,128)(2,1)}, u32[]{:S(2)}) copy-start(bf16[1,384,384]{2,1,0:T(8,128)(2,1)} %copy.16) | copy-start | bytes 884740
  36.4 11.3 %collective-permute-start.15 = (bf16[2,192,384]{2,1,0:T(8,128)(2,1)S(1)}, bf16[2,192,384]{2,1,0:T(8,128)(2,1)S(1)}, u32[]{:S(2)}, u32[]{:S(2)}) collective-permute-start(bf16[2,192,384]{2,1,0:T(8,128)(2,1)S(1)} %get-tuple-element.94), channel_id=1, source_target_pairs={{0,2},{1,3},{2,4},{3,5},{8,10},{9,11},{10,12},{11,13},{12,14},{13,... | collective-permute-start | bytes 884744 | tf_op jit(solution)/shard_map/ppermute | solution.py:46
  37.9 9.9 %collective-permute-start.13 = (bf16[2,192,384]{2,1,0:T(8,128)(2,1)S(1)}, bf16[2,192,384]{2,1,0:T(8,128)(2,1)S(1)}, u32[]{:S(2)}, u32[]{:S(2)}) collective-permute-start(bf16[2,192,384]{2,1,0:T(8,128)(2,1)S(1)} %get-tuple-element.94), channel_id=1, source_target_pairs={{2,0},{3,1},{10,8},{11,9},{12,10},{13,11},{18,16},{19,17},{26,24},... | collective-permute-start | bytes 884744 | tf_op jit(solution)/shard_map/ppermute | solution.py:46
  38.6 10.5 %copy-start.1 = (bf16[2,384,384]{2,1,0:T(8,128)(2,1)S(1)}, bf16[2,384,384]{2,1,0:T(8,128)(2,1)}, u32[]{:S(2)}) copy-start(bf16[2,384,384]{2,1,0:T(8,128)(2,1)} %get-tuple-element.62) | copy-start | bytes 1769476
  41.0 23.5 %collective-permute-start.16 = (bf16[2,192,384]{2,1,0:T(8,128)(2,1)S(1)}, bf16[2,192,384]{2,1,0:T(8,128)(2,1)S(1)}, u32[]{:S(2)}, u32[]{:S(2)}) collective-permute-start(bf16[2,192,384]{2,1,0:T(8,128)(2,1)S(1)} %get-tuple-element.96), channel_id=1, source_target_pairs={{0,2},{1,3},{2,4},{3,5},{8,10},{9,11},{10,12},{11,13},{12,14},{13,... | collective-permute-start | bytes 884744 | tf_op jit(solution)/shard_map/ppermute | solution.py:46
  42.3 22.3 %collective-permute-start.14 = (bf16[2,192,384]{2,1,0:T(8,128)(2,1)S(1)}, bf16[2,192,384]{2,1,0:T(8,128)(2,1)S(1)}, u32[]{:S(2)}, u32[]{:S(2)}) collective-permute-start(bf16[2,192,384]{2,1,0:T(8,128)(2,1)S(1)} %get-tuple-element.96), channel_id=1, source_target_pairs={{2,0},{3,1},{10,8},{11,9},{12,10},{13,11},{18,16},{19,17},{26,24},... | collective-permute-start | bytes 884744 | tf_op jit(solution)/shard_map/ppermute | solution.py:46
  43.0 6.4 %collective-permute-start.9 = (bf16[384,384]{1,0:T(8,128)(2,1)S(1)}, bf16[384,384]{1,0:T(8,128)(2,1)S(1)}, u32[]{:S(2)}, u32[]{:S(2)}) collective-permute-start(bf16[384,384]{1,0:T(8,128)(2,1)S(1)} %bitcast.44), channel_id=1, source_target_pairs={{0,8},{1,9},{2,10},{3,11},{4,12},{5,13},{6,14},{7,15},{8,0},{9,1},... | collective-permute-start | bytes 884744 | tf_op jit(solution)/shard_map/ppermute | solution.py:46
  47.8 16.0 %collective-permute-start.10 = (bf16[384,384]{1,0:T(8,128)(2,1)S(1)}, bf16[384,384]{1,0:T(8,128)(2,1)S(1)}, u32[]{:S(2)}, u32[]{:S(2)}) collective-permute-start(bf16[384,384]{1,0:T(8,128)(2,1)S(1)} %bitcast.43), channel_id=1, source_target_pairs={{0,16},{1,17},{2,18},{3,19},{4,20},{5,21},{6,22},{7,23},{8,24},{9,... | collective-permute-start | bytes 884744 | tf_op jit(solution)/shard_map/ppermute | solution.py:46
  47.8 12.8 %collective-permute-start.17 = (bf16[2,192,384]{2,1,0:T(8,128)(2,1)S(1)}, bf16[2,192,384]{2,1,0:T(8,128)(2,1)S(1)}, u32[]{:S(2)}, u32[]{:S(2)}) collective-permute-start(bf16[2,192,384]{2,1,0:T(8,128)(2,1)S(1)} %broadcast_select_fusion.5), channel_id=1, source_target_pairs={{2,4},{3,5},{4,6},{5,7},{8,10},{9,11},{10,12},{11,13},{12,14},{13,... | collective-permute-start | bytes 884744 | tf_op jit(solution)/shard_map/ppermute | solution.py:46
  49.3 1.0 copy-start.5
  50.2 13.7 %collective-permute-start.11 = (bf16[384,384]{1,0:T(8,128)(2,1)S(1)}, bf16[384,384]{1,0:T(8,128)(2,1)S(1)}, u32[]{:S(2)}, u32[]{:S(2)}) collective-permute-start(bf16[384,384]{1,0:T(8,128)(2,1)S(1)} %bitcast.42), channel_id=1, source_target_pairs={{0,24},{1,25},{2,26},{3,27},{4,28},{5,29},{6,30},{7,31},{8,16},{9,... | collective-permute-start | bytes 884744 | tf_op jit(solution)/shard_map/ppermute | solution.py:46
  60.6 4.4 %collective-permute-start.27 = (bf16[2,192,384]{2,1,0:T(8,128)(2,1)S(1)}, bf16[2,192,384]{2,1,0:T(8,128)(2,1)S(1)}, u32[]{:S(2)}, u32[]{:S(2)}) collective-permute-start(bf16[2,192,384]{2,1,0:T(8,128)(2,1)S(1)} %collective-permute-done.15.refs_12_), channel_id=1, source_target_pairs={{0,8},{1,9},{2,10},{3,11},{4,12},{5,13},{6,14},{7,15},{8,0},{9,1},... | collective-permute-start | bytes 884744 | tf_op jit(solution)/shard_map/ppermute | solution.py:46
  63.8 4.6 %collective-permute-start.7 = (bf16[384,768]{1,0:T(8,128)(2,1)S(1)}, bf16[384,768]{1,0:T(8,128)(2,1)S(1)}, u32[]{:S(2)}, u32[]{:S(2)}) collective-permute-start(bf16[384,768]{1,0:T(8,128)(2,1)S(1)} %pad_maximum_fusion.refs_0_), channel_id=1, source_target_pairs={{0,8},{1,9},{2,10},{3,11},{4,12},{5,13},{6,14},{7,15},{8,0},{9,1},... | collective-permute-start | bytes 1769480 | tf_op jit(solution)/shard_map/ppermute | solution.py:46
  63.9 2.5 %collective-permute-start.25 = (bf16[2,192,384]{2,1,0:T(8,128)(2,1)S(1)}, bf16[2,192,384]{2,1,0:T(8,128)(2,1)S(1)}, u32[]{:S(2)}, u32[]{:S(2)}) collective-permute-start(bf16[2,192,384]{2,1,0:T(8,128)(2,1)S(1)} %collective-permute-done.13.refs_10_), channel_id=1, source_target_pairs={{0,8},{1,9},{2,10},{3,11},{4,12},{5,13},{6,14},{7,15},{8,0},{9,1},... | collective-permute-start | bytes 884744 | tf_op jit(solution)/shard_map/ppermute | solution.py:46
  64.5 2.3 %collective-permute-start.28 = (bf16[2,192,384]{2,1,0:T(8,128)(2,1)S(1)}, bf16[2,192,384]{2,1,0:T(8,128)(2,1)S(1)}, u32[]{:S(2)}, u32[]{:S(2)}) collective-permute-start(bf16[2,192,384]{2,1,0:T(8,128)(2,1)S(1)} %collective-permute-done.16.refs_13_), channel_id=1, source_target_pairs={{0,8},{1,9},{2,10},{3,11},{4,12},{5,13},{6,14},{7,15},{8,0},{9,1},... | collective-permute-start | bytes 884744 | tf_op jit(solution)/shard_map/ppermute | solution.py:46
  64.6 3.5 %collective-permute-start.26 = (bf16[2,192,384]{2,1,0:T(8,128)(2,1)S(1)}, bf16[2,192,384]{2,1,0:T(8,128)(2,1)S(1)}, u32[]{:S(2)}, u32[]{:S(2)}) collective-permute-start(bf16[2,192,384]{2,1,0:T(8,128)(2,1)S(1)} %collective-permute-done.14.refs_11_), channel_id=1, source_target_pairs={{0,8},{1,9},{2,10},{3,11},{4,12},{5,13},{6,14},{7,15},{8,0},{9,1},... | collective-permute-start | bytes 884744 | tf_op jit(solution)/shard_map/ppermute | solution.py:46
  65.0 15.9 %collective-permute-start.19 = (bf16[2,192,384]{2,1,0:T(8,128)(2,1)S(1)}, bf16[2,192,384]{2,1,0:T(8,128)(2,1)S(1)}, u32[]{:S(2)}, u32[]{:S(2)}) collective-permute-start(bf16[2,192,384]{2,1,0:T(8,128)(2,1)S(1)} %broadcast_select_fusion.3), channel_id=1, source_target_pairs={{4,6},{5,7},{8,12},{9,13},{12,14},{13,15},{20,22},{21,23},{24,28},... | collective-permute-start | bytes 884744 | tf_op jit(solution)/shard_map/ppermute | solution.py:46
  66.4 21.0 %collective-permute-start.23 = (bf16[2,384,384]{2,1,0:T(8,128)(2,1)S(1)}, bf16[2,384,384]{2,1,0:T(8,128)(2,1)S(1)}, u32[]{:S(2)}, u32[]{:S(2)}) collective-permute-start(bf16[2,384,384]{2,1,0:T(8,128)(2,1)S(1)} %pad_maximum_fusion.2.refs_8_), channel_id=1, source_target_pairs={{0,8},{1,9},{2,10},{3,11},{4,12},{5,13},{6,14},{7,15},{8,0},{9,1},... | collective-permute-start | bytes 1769480 | tf_op jit(solution)/shard_map/ppermute | solution.py:46
  66.8 20.2 %collective-permute-start.18 = (bf16[2,192,384]{2,1,0:T(8,128)(2,1)S(1)}, bf16[2,192,384]{2,1,0:T(8,128)(2,1)S(1)}, u32[]{:S(2)}, u32[]{:S(2)}) collective-permute-start(bf16[2,192,384]{2,1,0:T(8,128)(2,1)S(1)} %broadcast_select_fusion.4), channel_id=1, source_target_pairs={{2,4},{3,5},{4,6},{5,7},{8,10},{9,11},{10,12},{11,13},{12,14},{13,... | collective-permute-start | bytes 884744 | tf_op jit(solution)/shard_map/ppermute | solution.py:46
  68.1 19.5 %collective-permute-start.24 = (bf16[2,384,384]{2,1,0:T(8,128)(2,1)S(1)}, bf16[2,384,384]{2,1,0:T(8,128)(2,1)S(1)}, u32[]{:S(2)}, u32[]{:S(2)}) collective-permute-start(bf16[2,384,384]{2,1,0:T(8,128)(2,1)S(1)} %pad_maximum_fusion.3.refs_9_), channel_id=1, source_target_pairs={{0,8},{1,9},{2,10},{3,11},{4,12},{5,13},{6,14},{7,15},{8,0},{9,1},... | collective-permute-start | bytes 1769480 | tf_op jit(solution)/shard_map/ppermute | solution.py:46
  68.4 20.5 %collective-permute-start.22 = (bf16[2,384,384]{2,1,0:T(8,128)(2,1)S(1)}, bf16[2,384,384]{2,1,0:T(8,128)(2,1)S(1)}, u32[]{:S(2)}, u32[]{:S(2)}) collective-permute-start(bf16[2,384,384]{2,1,0:T(8,128)(2,1)S(1)} %pad_maximum_fusion.3.refs_9_), channel_id=1, source_target_pairs={{12,8},{13,9},{28,24},{29,25}} | collective-permute-start | bytes 1769480 | tf_op jit(solution)/shard_map/ppermute | solution.py:46
  81.0 12.5 %collective-permute-start.21 = (bf16[2,384,384]{2,1,0:T(8,128)(2,1)S(1)}, bf16[2,384,384]{2,1,0:T(8,128)(2,1)S(1)}, u32[]{:S(2)}, u32[]{:S(2)}) collective-permute-start(bf16[2,384,384]{2,1,0:T(8,128)(2,1)S(1)} %pad_maximum_fusion.2.refs_8_), channel_id=1, source_target_pairs={{8,14},{9,15},{24,30},{25,31}} | collective-permute-start | bytes 1769480 | tf_op jit(solution)/shard_map/ppermute | solution.py:46
  87.0 6.5 %collective-permute-start.8 = (bf16[384,768]{1,0:T(8,128)(2,1)S(1)}, bf16[384,768]{1,0:T(8,128)(2,1)S(1)}, u32[]{:S(2)}, u32[]{:S(2)}) collective-permute-start(bf16[384,768]{1,0:T(8,128)(2,1)S(1)} %pad_maximum_fusion.1.refs_2_), channel_id=1, source_target_pairs={{0,8},{1,9},{2,10},{3,11},{4,12},{5,13},{6,14},{7,15},{8,0},{9,1},... | collective-permute-start | bytes 1769480 | tf_op jit(solution)/shard_map/ppermute | solution.py:46
  87.4 6.5 %collective-permute-start.29 = (bf16[2,192,384]{2,1,0:T(8,128)(2,1)S(1)}, bf16[2,192,384]{2,1,0:T(8,128)(2,1)S(1)}, u32[]{:S(2)}, u32[]{:S(2)}) collective-permute-start(bf16[2,192,384]{2,1,0:T(8,128)(2,1)S(1)} %collective-permute-done.17.refs_14_), channel_id=1, source_target_pairs={{0,8},{1,9},{2,10},{3,11},{4,12},{5,13},{6,14},{7,15},{8,0},{9,1},... | collective-permute-start | bytes 884744 | tf_op jit(solution)/shard_map/ppermute | solution.py:46
  87.6 12.3 %collective-permute-start.20 = (bf16[2,192,384]{2,1,0:T(8,128)(2,1)S(1)}, bf16[2,192,384]{2,1,0:T(8,128)(2,1)S(1)}, u32[]{:S(2)}, u32[]{:S(2)}) collective-permute-start(bf16[2,192,384]{2,1,0:T(8,128)(2,1)S(1)} %broadcast_select_fusion.2), channel_id=1, source_target_pairs={{4,6},{5,7},{8,12},{9,13},{12,14},{13,15},{20,22},{21,23},{24,28},... | collective-permute-start | bytes 884744 | tf_op jit(solution)/shard_map/ppermute | solution.py:46
  88.9 12.7 %collective-permute-start.34 = (bf16[2,384,384]{2,1,0:T(8,128)(2,1)S(1)}, bf16[2,384,384]{2,1,0:T(8,128)(2,1)S(1)}, u32[]{:S(2)}, u32[]{:S(2)}) collective-permute-start(bf16[2,384,384]{2,1,0:T(8,128)(2,1)S(1)} %collective-permute-done.22.refs_19_), channel_id=1, source_target_pairs={{0,8},{1,9},{2,10},{3,11},{4,12},{5,13},{6,14},{7,15},{8,0},{9,1},... | collective-permute-start | bytes 1769480 | tf_op jit(solution)/shard_map/ppermute | solution.py:46
  93.5 8.1 %collective-permute-start.33 = (bf16[2,384,384]{2,1,0:T(8,128)(2,1)S(1)}, bf16[2,384,384]{2,1,0:T(8,128)(2,1)S(1)}, u32[]{:S(2)}, u32[]{:S(2)}) collective-permute-start(bf16[2,384,384]{2,1,0:T(8,128)(2,1)S(1)} %collective-permute-done.21.refs_18_), channel_id=1, source_target_pairs={{0,8},{1,9},{2,10},{3,11},{4,12},{5,13},{6,14},{7,15},{8,0},{9,1},... | collective-permute-start | bytes 1769480 | tf_op jit(solution)/shard_map/ppermute | solution.py:46
  93.5 6.9 %collective-permute-start.31 = (bf16[2,192,384]{2,1,0:T(8,128)(2,1)S(1)}, bf16[2,192,384]{2,1,0:T(8,128)(2,1)S(1)}, u32[]{:S(2)}, u32[]{:S(2)}) collective-permute-start(bf16[2,192,384]{2,1,0:T(8,128)(2,1)S(1)} %collective-permute-done.19.refs_16_), channel_id=1, source_target_pairs={{0,8},{1,9},{2,10},{3,11},{4,12},{5,13},{6,14},{7,15},{8,0},{9,1},... | collective-permute-start | bytes 884744 | tf_op jit(solution)/shard_map/ppermute | solution.py:46
  94.0 6.4 %collective-permute-start.30 = (bf16[2,192,384]{2,1,0:T(8,128)(2,1)S(1)}, bf16[2,192,384]{2,1,0:T(8,128)(2,1)S(1)}, u32[]{:S(2)}, u32[]{:S(2)}) collective-permute-start(bf16[2,192,384]{2,1,0:T(8,128)(2,1)S(1)} %collective-permute-done.18.refs_15_), channel_id=1, source_target_pairs={{0,8},{1,9},{2,10},{3,11},{4,12},{5,13},{6,14},{7,15},{8,0},{9,1},... | collective-permute-start | bytes 884744 | tf_op jit(solution)/shard_map/ppermute | solution.py:46
  99.9 1.7 %collective-permute-start.32 = (bf16[2,192,384]{2,1,0:T(8,128)(2,1)S(1)}, bf16[2,192,384]{2,1,0:T(8,128)(2,1)S(1)}, u32[]{:S(2)}, u32[]{:S(2)}) collective-permute-start(bf16[2,192,384]{2,1,0:T(8,128)(2,1)S(1)} %collective-permute-done.20.refs_17_), channel_id=1, source_target_pairs={{0,8},{1,9},{2,10},{3,11},{4,12},{5,13},{6,14},{7,15},{8,0},{9,1},... | collective-permute-start | bytes 884744 | tf_op jit(solution)/shard_map/ppermute | solution.py:46
  107.8 8.3 %collective-permute-start.35 = (bf16[2,192,384]{2,1,0:T(8,128)(2,1)S(1)}, bf16[2,192,384]{2,1,0:T(8,128)(2,1)S(1)}, u32[]{:S(2)}, u32[]{:S(2)}) collective-permute-start(bf16[2,192,384]{2,1,0:T(8,128)(2,1)S(1)} %get-tuple-element.81), channel_id=1, source_target_pairs={{0,1},{1,0},{2,3},{3,2},{4,5},{5,4},{6,7},{7,6},{8,9},{9,8},{10,11... | collective-permute-start | bytes 884744 | tf_op jit(solution)/shard_map/ppermute | solution.py:46
  109.1 8.8 %collective-permute-start.38 = (bf16[384,384]{1,0:T(8,128)(2,1)S(1)}, bf16[384,384]{1,0:T(8,128)(2,1)S(1)}, u32[]{:S(2)}, u32[]{:S(2)}) collective-permute-start(bf16[384,384]{1,0:T(8,128)(2,1)S(1)} %get-tuple-element.78), channel_id=1, source_target_pairs={{0,8},{1,9},{2,10},{3,11},{4,12},{5,13},{6,14},{7,15},{8,0},{9,1},... | collective-permute-start | bytes 884744 | tf_op jit(solution)/shard_map/ppermute | solution.py:46
  109.8 10.0 %collective-permute-start.36 = (bf16[384,384]{1,0:T(8,128)(2,1)S(1)}, bf16[384,384]{1,0:T(8,128)(2,1)S(1)}, u32[]{:S(2)}, u32[]{:S(2)}) collective-permute-start(bf16[384,384]{1,0:T(8,128)(2,1)S(1)} %get-tuple-element.79), channel_id=1, source_target_pairs={{0,16},{1,17},{2,18},{3,19},{4,20},{5,21},{6,22},{7,23},{8,24},{9,... | collective-permute-start | bytes 884744 | tf_op jit(solution)/shard_map/ppermute | solution.py:46
  110.9 13.9 %collective-permute-start.37 = (bf16[384,384]{1,0:T(8,128)(2,1)S(1)}, bf16[384,384]{1,0:T(8,128)(2,1)S(1)}, u32[]{:S(2)}, u32[]{:S(2)}) collective-permute-start(bf16[384,384]{1,0:T(8,128)(2,1)S(1)} %get-tuple-element.80), channel_id=1, source_target_pairs={{0,24},{1,25},{2,26},{3,27},{4,28},{5,29},{6,30},{7,31},{8,16},{9,... | collective-permute-start | bytes 884744 | tf_op jit(solution)/shard_map/ppermute | solution.py:46
